TPU v7x, 128 devices: a whole 4x4x4 slice. The times are simulated.
128 devices in a mesh: gx: 8 (over x, core), gy: 4 (over y), gz: 4 (over z).
Axes of the slice: x: 4, y: 4, z: 4, core: 2. Of those that a mesh axis runs over, the one named last changes fastest.
Arguments:
- normals: bfloat16 [2, 512, 512, 512], P(None, 'gx', 'gy', 'gz'), may hold values from -6 to 6
- spectrum: float32 [512, 512, 512], P('gx', 'gy', 'gz'), may hold values from 1e-05 to 0.0001
- block_owner: int32 [131072, 1], P(('gx', 'gy', 'gz')), may hold values from 0 to 127; in each aligned block of 1024 rows (0 to 1023, 1024 to 2047, ...) at most 16 rows name the same one
Outputs:
- owned: float32 [128, 128, 16, 2, 128], P(('gx', 'gy', 'gz'))
Inputs may be any that keep to these rules, and one draw needn't show every extreme that they name: `block_owner`: among the 1024 blocks of one source device no owner is named more than 16 times, and in every draw some owner is named exactly 16 times by some device.
All inputs are finite; a program needn't handle non-finite values.
Results may differ from a plain program's by a relative error of at most 0.0003.
Values sent between devices are 32-bit elements; how exact they have to be, the bound alone decides.
No kernel may reach another device: no remote copies, remote signals or barrier semaphores. Data moves between devices by JAX's collectives and lax.ppermute only.
A program may use at most 128 MiB of HBM per device.

v0:
```python
import math

import jax
import jax.numpy as jnp
from jax import lax
from jax.sharding import PartitionSpec as P

EX = 512
EY = 512
EZ = 512
BW = 128


def dft_tables(length, positions):
    kept_index = jnp.arange(length // 2, dtype=jnp.int32)
    phase_index = positions[:, None] * kept_index[None, :] % length
    angles = phase_index.astype(jnp.float32) * (2.0 * math.pi / length)
    return (jnp.cos(angles), jnp.sin(angles))


def transform(field_pair, form, cosine, sine_table):

    def contract(operand, matrix):
        return jnp.einsum(form, operand, matrix, precision=lax.Precision.HIGHEST)

    real_out = contract(field_pair[0], cosine) + contract(field_pair[1], sine_table)
    imag_out = contract(field_pair[1], cosine) - contract(field_pair[0], sine_table)
    return jnp.stack([real_out, imag_out])


def per_device(normals, spectrum, block_owner):
    real_part = spectrum * normals[0].astype(jnp.float32)
    imag_part = spectrum * normals[1].astype(jnp.float32)
    field_pair = jnp.stack([real_part, imag_part])
    cos_y, sin_y = dft_tables(EY, jnp.arange(EY, dtype=jnp.int32))
    cos_z, sin_z = dft_tables(EZ, jnp.arange(EZ, dtype=jnp.int32))
    field_pair = lax.all_to_all(
        lax.all_to_all(field_pair, "gy", split_axis=1, concat_axis=2, tiled=True),
        "gz",
        split_axis=1,
        concat_axis=3,
        tiled=True,
    )
    field_pair = transform(
        transform(field_pair, "xyz,zk->xyk", cos_z, sin_z), "xyz,yk->xkz", cos_y, sin_y
    )
    count_x = lax.axis_size("gx")
    count_yz = lax.axis_size("gy") * lax.axis_size("gz")
    devices_all = count_x * count_yz
    cos_x, sin_x = dft_tables(EX, jnp.arange(EX, dtype=jnp.int32))
    field_pair = transform(
        lax.all_to_all(field_pair, ("gx", "gy", "gz"), split_axis=2, concat_axis=1, tiled=True),
        "xyz,xk->kyz",
        cos_x,
        sin_x,
    )
    coefficient = jnp.exp(field_pair)
    planes, rows_x, rows_y, depth = coefficient.shape
    blocks = coefficient.reshape(planes, rows_x, rows_y, depth // BW, BW)
    blocks = blocks.transpose(1, 2, 3, 0, 4).reshape(rows_x * rows_y * (depth // BW), planes, BW)
    capacity = max(2, 2 * blocks.shape[0] // devices_all)
    destination = block_owner[:, 0]
    one_hot = (destination[:, None] == jnp.arange(devices_all, dtype=jnp.int32)[None, :]).astype(
        jnp.int32
    )
    earlier = jnp.cumsum(one_hot, axis=0) - one_hot
    slot_index = jnp.sum(earlier * one_hot, axis=1)
    outgoing = jnp.zeros((devices_all, capacity, planes, BW), jnp.float32)
    outgoing = outgoing.at[destination, slot_index].set(blocks)
    arrived = lax.all_to_all(
        outgoing[:, None], ("gx", "gy", "gz"), split_axis=0, concat_axis=1, tiled=True
    )
    return arrived


def solution(mesh):
    placed = (P(None, "gx", "gy", "gz"), P("gx", "gy", "gz"), P(("gx", "gy", "gz"), None))
    return jax.shard_map(
        per_device,
        mesh=mesh,
        in_specs=placed,
        out_specs=P(("gx", "gy", "gz"), None, None, None, None),
        check_vma=False,
    )
```

profile of v0, /device:TPU:1, one launch (start us, length us, event | category | flops | bytes accessed | tf_op | source)
XLA Modules:
  0.0 393.9 jit_solution(8522990174895532905)
XLA Ops:
  0.0 4.7 %fusion.1 = (f32[1,64,128,128]{3,2,0,1:T(8,128)S(1)}, f32[1,64,128,128]{3,2,0,1:T(8,128)S(1)}) fusion(f32[64,128,128]{2,1,0:T(8,128)} %param.4, bf16[2,64,128,128]{3,2,1,0:T(8,128)(2,1)} %param.3), kind=kLoop, calls=%fused_computation.5 | loop fusion | flops 4194304 | bytes 16777216 | tf_op jit(solution)/shard_map/stack | solution.py:34
  4.7 1.1 pad_maximum_fusion
  5.8 97.6 %all_to_all.60 = f32[2,64,128,128]{3,2,0,1:T(8,128)S(1)} all-to-all(f32[2,64,128,128]{3,2,0,1:T(8,128)S(1)} %pad_maximum_fusion), channel_id=1, replica_groups=mesh['gx'=8,'gy'=4,'gz'=4] {'gy'}, dimensions={1} | all-to-all | bytes 16777216 | tf_op jit(solution)/shard_map/all_to_all | solution.py:38
  103.5 1.1 copy.46
  104.6 0.9 copy.47
  105.5 96.2 %all_to_all.61 = f32[2,16,512,128]{3,2,0,1:T(8,128)S(1)} all-to-all(f32[2,16,512,128]{3,2,0,1:T(8,128)S(1)} %copy.47), channel_id=1, replica_groups=mesh['gx'=8,'gy'=4,'gz'=4] {'gz'}, dimensions={1} | all-to-all | bytes 16777216 | tf_op jit(solution)/shard_map/all_to_all | solution.py:37
  201.6 0.9 copy.48
  202.6 2.7 fusion.95
  205.2 4.7 %copy.49 = f32[1,4,512,4,128]{4,3,2,1,0:T(4,128)} copy(f32[1,4,512,4,128]{4,2,1,3,0:T(8,128)S(1)} %get-tuple-element.5) | data formatting | bytes 8388608 | tf_op jit(solution)/shard_map/slice | solution.py:26
  209.9 5.9 %squeeze.8 = f32[4,512,512]{2,1,0:T(8,128)} reshape(f32[1,4,512,4,128]{4,3,2,1,0:T(4,128)} %copy.49) | data formatting | bytes 8388608 | tf_op jit(solution)/shard_map/squeeze | solution.py:26
  215.8 7.7 %fusion.25 = f32[4,512,256]{2,1,0:T(8,128)S(1)} fusion(f32[4,512,512]{2,1,0:T(8,128)} %squeeze.8), kind=kOutput, calls=%fused_computation.42 | convolution fusion | flops 3223060480 | bytes 6291456 | tf_op jit(solution)/shard_map/xyz,zk->xyk/dot_general | solution.py:24
  223.6 4.7 %copy.50 = f32[1,4,512,4,128]{4,3,2,1,0:T(4,128)} copy(f32[1,4,512,4,128]{4,2,1,3,0:T(8,128)S(1)} %copy-done.2) | data formatting | bytes 8388608 | tf_op jit(solution)/shard_map/slice | solution.py:26
  228.2 5.6 %squeeze.9 = f32[4,512,512]{2,1,0:T(8,128)} reshape(f32[1,4,512,4,128]{4,3,2,1,0:T(4,128)} %copy.50) | data formatting | bytes 8388608 | tf_op jit(solution)/shard_map/squeeze | solution.py:26
  233.8 7.9 %fusion.23 = f32[4,512,256]{2,1,0:T(8,128)S(1)} fusion(f32[4,512,512]{2,1,0:T(8,128)} %squeeze.9), kind=kOutput, calls=%fused_computation.40 | convolution fusion | flops 3223060480 | bytes 6291456 | tf_op jit(solution)/shard_map/xyz,zk->xyk/dot_general | solution.py:24
  241.8 5.6 %convolution_add_fusion = f32[4,512,256]{2,1,0:T(8,128)S(1)} fusion(f32[4,512,256]{2,1,0:T(8,128)S(1)} %fusion.25, f32[4,512,512]{2,1,0:T(8,128)S(1)} %copy-done.1), kind=kOutput, calls=%fused_computation.9 | convolution fusion | flops 3223584768 | bytes 8388608 | tf_op jit(solution)/shard_map/xyz,zk->xyk/dot_general | solution.py:24
  247.4 4.2 %fusion.17 = f32[256,4,256]{2,0,1:T(8,128)S(1)} fusion(f32[4,512,256]{2,1,0:T(8,128)S(1)} %convolution_add_fusion), kind=kOutput, calls=%fused_computation.34 | convolution fusion | flops 1612447744 | bytes 3145728 | tf_op jit(solution)/shard_map/xyz,yk->xkz/dot_general | solution.py:24
  251.6 5.6 %convolution_subtract_fusion = f32[4,512,256]{2,1,0:T(8,128)S(1)} fusion(f32[4,512,256]{2,1,0:T(8,128)S(1)} %fusion.23, f32[4,512,512]{2,1,0:T(8,128)S(1)} %copy-done), kind=kOutput, calls=%fused_computation.8 | convolution fusion | flops 3223584768 | bytes 8388608 | tf_op jit(solution)/shard_map/xyz,zk->xyk/dot_general | solution.py:24
  257.2 3.8 fusion.15
  261.1 4.0 %fusion.3 = f32[1,4,256,256]{3,2,1,0:T(8,128)S(1)} fusion(f32[256,4,256]{2,0,1:T(8,128)S(1)} %fusion.17, f32[4,512,256]{2,1,0:T(8,128)S(1)} %convolution_subtract_fusion), kind=kOutput, calls=%fused_computation.13 | convolution fusion | flops 1612709888 | bytes 4194304 | tf_op jit(solution)/shard_map/xyz,yk->xkz/dot_general | solution.py:24
  265.1 3.8 fusion.2
  268.9 0.1 pad_maximum_fusion.1
  269.1 0.0 copy-start.3
  269.1 2.7 copy.55
  271.8 8.4 %all-to-all-start.2 = ((f32[2,4,256,256]{3,1,0,2:T(4,128)}), f32[2,4,256,256]{3,1,0,2:T(4,128)S(1)}, u32[]{:S(2)}, u32[]{:S(2)}) async-start(f32[2,4,256,256]{3,1,0,2:T(4,128)} %copy.55), calls=%async_computation.2 | async-start | bytes 4194304 | tf_op jit(solution)/shard_map/all_to_all | solution.py:52
  280.2 0.1 copy.43
  280.3 0.2 fusion.29
  280.6 0.1 copy.44
  280.7 0.4 fusion.8
  281.1 0.0 copy-done.5
  281.1 0.1 multiply_reduce_fusion
  281.2 0.1 and_reduce_fusion
  281.3 28.4 %all-to-all-done.2 = f32[2,4,256,256]{3,1,0,2:T(4,128)S(1)} async-done(((f32[2,4,256,256]{3,1,0,2:T(4,128)}), f32[2,4,256,256]{3,1,0,2:T(4,128)S(1)}, u32[]{:S(2)}, u32[]{:S(2)}) %all-to-all-start.2) | async-done | bytes 2097184 | tf_op jit(solution)/shard_map/all_to_all | solution.py:52
  309.7 1.1 copy.75
  310.8 0.7 fusion.96
  311.5 0.8 copy.57
  312.3 3.7 fusion.21
  316.0 1.0 copy.58
  317.1 3.7 fusion.19
  320.7 4.0 %convolution_add_fusion.2 = f32[256,2,256]{0,2,1:T(8,128)S(1)} fusion(f32[256,2,256]{0,2,1:T(8,128)} %fusion.21, f32[512,2,256]{0,2,1:T(8,128)S(1)} %copy.58), kind=kOutput, calls=%fused_computation.15 | convolution fusion | flops 807272448 | bytes 2097152 | tf_op jit(solution)/shard_map/xyz,xk->kyz/dot_general | solution.py:24
  324.7 0.3 copy.61
  325.0 4.0 %convolution_subtract_fusion.2 = f32[256,2,256]{0,2,1:T(8,128)S(1)} fusion(f32[256,2,256]{0,2,1:T(8,128)} %fusion.19, f32[512,2,256]{0,2,1:T(8,128)S(1)} %copy.57), kind=kOutput, calls=%fused_computation.14 | convolution fusion | flops 807272448 | bytes 2097152 | tf_op jit(solution)/shard_map/xyz,xk->kyz/dot_general | solution.py:24
  329.0 0.3 copy.62
  329.3 0.6 maximum_exponential_fusion
  330.0 0.8 copy.63
  330.8 0.6 broadcast.54
  331.4 26.6 %scatter_fusion = f32[2048,2,128]{2,1,0:T(2,128)S(1)} fusion(f32[2048,2,128]{2,1,0:T(2,128)S(1)} %broadcast.54, s32[1024]{0:T(1024)S(1)} %broadcast_select_fusion, f32[1024,2,128]{2,1,0:T(2,128)S(1)} %copy.63), kind=kCustom, calls=%fused_computation | custom fusion | bytes 3149824
  358.0 34.2 %all_to_all.62 = f32[128,1,16,2,128]{4,3,2,1,0:T(2,128)S(1)} all-to-all(f32[128,1,16,2,128]{4,3,2,1,0:T(2,128)S(1)} %bitcast.98), channel_id=1, replica_groups=mesh['gx'=8,'gy'=4,'gz'=4] {'gx','gy','gz'}, dimensions={0} | all-to-all | bytes 4194304 | tf_op jit(solution)/shard_map/all_to_all | solution.py:70
  392.2 1.3 copy.78
  (16 shorter events, 0.1 us)
Async XLA Ops:
  215.8 7.7 %copy-start.2 = (f32[1,4,512,4,128]{4,2,1,3,0:T(8,128)S(1)}, f32[1,4,512,4,128]{4,2,1,3,0:T(8,128)}, u32[]{:S(2)}) copy-start(f32[1,4,512,4,128]{4,2,1,3,0:T(8,128)} %get-tuple-element.6) | copy-start | bytes 12582916
  233.8 7.9 %copy-start.1 = (f32[4,512,512]{2,1,0:T(8,128)S(1)}, f32[4,512,512]{2,1,0:T(8,128)}, u32[]{:S(2)}) copy-start(f32[4,512,512]{2,1,0:T(8,128)} %squeeze.9) | copy-start | bytes 12582916
  241.8 9.9 %copy-start = (f32[4,512,512]{2,1,0:T(8,128)S(1)}, f32[4,512,512]{2,1,0:T(8,128)}, u32[]{:S(2)}) copy-start(f32[4,512,512]{2,1,0:T(8,128)} %squeeze.8) | copy-start | bytes 12582916
  269.1 11.1 %copy-start.3 = (s32[1024,1]{0,1:T(1,128)S(1)}, s32[1024,1]{0,1:T(1,128)}, u32[]{:S(2)}) copy-start(s32[1024,1]{0,1:T(1,128)} %param.5) | copy-start | bytes 12292
  271.8 9.4 %copy-start.5 = (s32[2]{0:T(128)S(1)}, s32[2]{0:T(128)}, u32[]{:S(2)}) copy-start(s32[2]{0:T(128)} %constant.35) | copy-start | bytes 28
  271.8 9.5 %copy-start.4 = (s32[2]{0:T(128)S(1)}, s32[2]{0:T(128)}, u32[]{:S(2)}) copy-start(s32[2]{0:T(128)} %constant.38) | copy-start | bytes 28
  271.8 37.9 %all-to-all-start.2 = ((f32[2,4,256,256]{3,1,0,2:T(4,128)}), f32[2,4,256,256]{3,1,0,2:T(4,128)S(1)}, u32[]{:S(2)}, u32[]{:S(2)}) async-start(f32[2,4,256,256]{3,1,0,2:T(4,128)} %copy.55), calls=%async_computation.2 | async-start | bytes 4194304 | tf_op jit(solution)/shard_map/all_to_all | solution.py:52
where the time goes:
time: 400 us; the launch traced here: 394 us
  blocking collectives  228 us (57%)
  local copies, waits for them, and re-layouts  62.9 us (16%)
  matrix products  58 us (14%)
  waiting for transfers between devices  28.4 us (7%)
  starting transfers between devices  8.44 us (2%)
  other arithmetic  7.39 us (2%)
    all_to_all x1, blocking collectives, per_device(): lax.all_to_all(field_pair, 'gy', split_axis=1, concat_axis=2, tiled=True)  97.6 us
    all_to_all x1, blocking collectives, per_device(): lax.all_to_all(lax.all_to_all(field_pair, 'gy', split_axis=1, concat_axis...  96.2 us
    dot_general x12, matrix products, contract(): return jnp.einsum(form, operand, matrix, precision=lax.Precision.HIGHEST)  58 us
    all_to_all x1, blocking collectives, per_device(): lax.all_to_all(outgoing[:, None], ('gx', 'gy', 'gz'), split_axis=0, conca...  34.2 us
    unnamed x15, local copies, waits for them, and re-layouts  28.5 us
    all_to_all x1, waiting for transfers between devices, per_device(): lax.all_to_all(field_pair, ('gx', 'gy', 'gz'), split_axis=2, concat_axis=...  28.4 us
    all_to_all x1, starting transfers between devices, per_device(): lax.all_to_all(field_pair, ('gx', 'gy', 'gz'), split_axis=2, concat_axis=...  8.44 us
    slice x3, local copies, waits for them, and re-layouts, transform(): field_pair[0]  8.08 us
  transfers between devices with their start and end apart: 1, of which 1 were waited for; matrix products, arithmetic and copies ran while one was open for 0% of the time, Pallas kernels for 0%

commit v1 on v0

v1 whole, which is shorter than its diff:
```python
import functools

import jax
import jax.numpy as jnp
import ml_dtypes
import numpy as np
from jax import lax
from jax.experimental import pallas as pl
from jax.experimental.pallas import tpu as pltpu
from jax.sharding import PartitionSpec as P

N = 512
KEPT = 256
BW = 128
CAP = 16
ALL = ("gx", "gy", "gz")
MIB = 1 << 20


def split_table(table):
    high = table.astype(np.float32).astype(ml_dtypes.bfloat16)
    low = (table - high.astype(np.float64)).astype(np.float32).astype(ml_dtypes.bfloat16)
    return np.stack([high, low])


def cos_sin(positions, kept):
    angles = (positions[:, None] * kept[None, :] % N) * (2.0 * np.pi / N)
    return np.cos(angles), np.sin(angles)


@functools.cache
def tables():
    cosine, sine = cos_sin(np.arange(N), np.arange(KEPT))
    real_rows = np.concatenate([cosine, -sine], 1).reshape(4, 1, 128, 2 * KEPT)
    imag_rows = np.concatenate([sine, cosine], 1).reshape(4, 1, 128, 2 * KEPT)
    table_z = np.concatenate([real_rows, imag_rows], 1).reshape(4, 256, 2 * KEPT)
    order = np.arange(KEPT).reshape(KEPT // 2, 2).T.reshape(-1)
    cosine, sine = cos_sin(np.arange(N), order)
    cosine, sine = cosine.reshape(4, 128, KEPT), sine.reshape(4, 128, KEPT)
    top = np.concatenate([cosine, sine], 1)
    bottom = np.concatenate([-sine, cosine], 1)
    table_y = np.concatenate([top, bottom], 2).transpose(0, 2, 1)
    gx, gy, gz = np.meshgrid(np.arange(8), np.arange(4), np.arange(4), indexing="ij")
    first = 64 * gx + 8 * gz + 2 * gy
    second = 64 * gx + 32 + 8 * gy + 2 * gz
    cells = np.stack([first, first + 1, second, second + 1], -1).reshape(128, 4)
    cosine, sine = cos_sin(cells.reshape(-1), np.arange(KEPT))
    cosine = cosine.T.reshape(KEPT, 128, 1, 4)
    sine = sine.T.reshape(KEPT, 128, 1, 4)
    top = np.concatenate([cosine, sine], 2).reshape(KEPT, 1024)
    bottom = np.concatenate([-sine, cosine], 2).reshape(KEPT, 1024)
    table_x = np.concatenate([top, bottom], 0)
    return split_table(table_x), split_table(table_y), split_table(table_z)


def halves(values):
    high = values.astype(jnp.bfloat16)
    low = (values - high.astype(jnp.float32)).astype(jnp.bfloat16)
    return high, low


def product(left, right):
    def dot(a, b):
        return jnp.dot(a, b, preferred_element_type=jnp.float32)

    return dot(left[0], right[0]) + (dot(left[0], right[1]) + dot(left[1], right[0]))


def params(mib):
    return pltpu.CompilerParams(vmem_limit_bytes=mib * MIB)


def cost(multiplies, moved):
    return pl.CostEstimate(flops=6 * multiplies, bytes_accessed=moved, transcendentals=0)


def first_z_kernel(place_ref, in_ref, table_ref, out_ref):
    total = None
    for g in range(4):
        rows = jnp.concatenate(
            [in_ref[g, plane].reshape(256, 128) for plane in range(2)], axis=1
        )
        term = product(halves(rows), (table_ref[0, g], table_ref[1, g]))
        total = term if total is None else total + term
    for plane in range(2):
        out_ref[plane] = total[:, plane * KEPT : (plane + 1) * KEPT].reshape(2, 128, KEPT)


def first_z(place, arrived, table_z):
    return pl.pallas_call(
        first_z_kernel,
        grid_spec=pltpu.PrefetchScalarGridSpec(
            num_scalar_prefetch=1,
            grid=(1,),
            in_specs=[
                pl.BlockSpec((4, 2, 2, 128, 128), lambda i, place: (0, 0, place[0], 0, 0)),
                pl.BlockSpec((2, 4, 256, 512), lambda i, place: (0, 0, 0, 0)),
            ],
            out_specs=pl.BlockSpec((2, 2, 128, KEPT), lambda i, place: (0, 0, 0, 0)),
        ),
        out_shape=jax.ShapeDtypeStruct((2, 2, 128, KEPT), jnp.float32),
        compiler_params=params(24),
        cost_estimate=cost(256 * 1024 * 512, 4 * MIB),
        name="first_z",
    )(place, arrived, table_z)


def first_y_kernel(place_ref, p0, p1, p2, p3, table_ref, out_ref):
    total = None
    for shift, piece in enumerate((p0, p1, p2, p3)):
        g = lax.rem(place_ref[0] + (4 - shift), 4)
        columns = jnp.concatenate([piece[:, x].reshape(256, 128) for x in range(2)], axis=1)
        term = product((table_ref[0, g], table_ref[1, g]), halves(columns))
        total = term if total is None else total + term
    for plane in range(2):
        for x in range(2):
            out_ref[0, plane, x] = total[
                plane * KEPT : (plane + 1) * KEPT, x * 128 : (x + 1) * 128
            ]


def first_y(place, pieces, table_y):
    return pl.pallas_call(
        first_y_kernel,
        grid_spec=pltpu.PrefetchScalarGridSpec(
            num_scalar_prefetch=1,
            grid=(4,),
            in_specs=[pl.BlockSpec((2, 2, 128, 128), lambda i, place: (0, i, 0, 0))] * 4
            + [pl.BlockSpec((2, 4, 512, 256), lambda i, place: (0, 0, 0, 0))],
            out_specs=pl.BlockSpec((1, 2, 2, KEPT, 128), lambda i, place: (i, 0, 0, 0, 0)),
        ),
        out_shape=jax.ShapeDtypeStruct((4, 2, 2, KEPT, 128), jnp.float32),
        compiler_params=params(24),
        cost_estimate=cost(1024 * 1024 * 512, 8 * MIB),
        name="first_y",
    )(place, *pieces, table_y)


def second_kernel(place_ref, p0, p1, p2, p3, b_ref, table_y_ref, table_z_ref, out_ref):
    def put(values, row):
        for parity in range(2):
            for half in range(2):
                out_ref[pl.ds(parity * 16 + half * 8 + row, 128, stride=32), :] = values[
                    parity * 128 : (parity + 1) * 128, half * 128 : (half + 1) * 128
                ]

    for x in range(2):
        total = None
        for shift, piece in enumerate((p0, p1, p2, p3)):
            g = lax.rem(place_ref[0] + (4 - shift), 4)
            columns = piece[:, x].reshape(256, KEPT)
            term = product((table_y_ref[0, g], table_y_ref[1, g]), halves(columns))
            total = term if total is None else total + term
        for plane in range(2):
            put(total[plane * KEPT : (plane + 1) * KEPT], plane * 4 + x)
    for x in range(2):
        total = None
        for g in range(4):
            rows = jnp.concatenate([b_ref[g, plane, x] for plane in range(2)], axis=1)
            term = product(halves(rows), (table_z_ref[0, g], table_z_ref[1, g]))
            total = term if total is None else total + term
        for plane in range(2):
            put(total[:, plane * KEPT : (plane + 1) * KEPT], plane * 4 + 2 + x)


def second(place, pieces, arrived, table_y, table_z):
    whole = pl.BlockSpec(memory_space=pltpu.VMEM)
    return pl.pallas_call(
        second_kernel,
        in_specs=[pl.BlockSpec(memory_space=pltpu.SMEM)] + [whole] * 7,
        out_specs=whole,
        out_shape=jax.ShapeDtypeStruct((4096, 128), jnp.float32),
        compiler_params=params(40),
        cost_estimate=cost(1024 * 1024 * 512, 10 * MIB),
        name="second",
    )(place, *pieces, arrived, table_y, table_z)


def third_kernel(slot_ref, in_ref, table_ref, out_ref, held):
    parity = pl.program_id(0)

    @pl.when(parity == 0)
    def _():
        out_ref[...] = jnp.zeros_like(out_ref)

    columns = jnp.concatenate(
        [in_ref[:, 0, half].reshape(1024, 128) for half in range(2)], axis=1
    )
    values = jnp.exp(product((table_ref[0], table_ref[1]), halves(columns)))
    for plane in range(2):
        for half in range(2):
            held[plane, half] = values[
                plane * KEPT : (plane + 1) * KEPT, half * 128 : (half + 1) * 128
            ]

    def place_rows(group, carry):
        for offset in range(8):
            x = group * 8 + offset
            for half in range(2):
                slot = slot_ref[x * 4 + parity * 2 + half]
                for plane in range(2):
                    out_ref[pl.ds(slot * 2 + plane, 1), :] = held[plane, half, pl.ds(x, 1), :]
        return carry

    lax.fori_loop(0, KEPT // 8, place_rows, 0)


def third(slots, arrived, table_x):
    return pl.pallas_call(
        third_kernel,
        grid_spec=pltpu.PrefetchScalarGridSpec(
            num_scalar_prefetch=1,
            grid=(2,),
            in_specs=[
                pl.BlockSpec((128, 1, 2, 8, 128), lambda i, slots: (0, i, 0, 0, 0)),
                pl.BlockSpec((2, 512, 1024), lambda i, slots: (0, 0, 0)),
            ],
            out_specs=pl.BlockSpec((4096, 128), lambda i, slots: (0, 0)),
            scratch_shapes=[pltpu.VMEM((2, 2, KEPT, 128), jnp.float32)],
        ),
        out_shape=jax.ShapeDtypeStruct((4096, 128), jnp.float32),
        compiler_params=params(32),
        cost_estimate=cost(512 * 1024 * 512, 6 * MIB),
        name="third",
    )(slots, arrived, table_x)


def shifted(piece, axis, shift):
    size = lax.axis_size(axis)
    return lax.ppermute(piece, axis, [(i, (i + shift) % size) for i in range(size)])


def exchange(pieces, axis):
    return [pieces[0]] + [shifted(pieces[s], axis, s) for s in range(1, 4)]


def slots_of(block_owner):
    destination = block_owner[:, 0]
    one_hot = (destination[:, None] == jnp.arange(128, dtype=jnp.int32)[None, :]).astype(jnp.int32)
    earlier = jnp.cumsum(one_hot, axis=0) - one_hot
    return destination * CAP + jnp.sum(earlier * one_hot, axis=1)


def per_device(normals, spectrum, block_owner):
    table_x, table_y, table_z = (jnp.asarray(table) for table in tables())
    gy = lax.axis_index("gy").astype(jnp.int32)
    place = gy.reshape(1)

    first = spectrum[:32].reshape(4, 1, 8, 128, 128) * normals[:, :32].astype(
        jnp.float32
    ).reshape(2, 4, 8, 128, 128).transpose(1, 0, 2, 3, 4)
    arrived_a = lax.all_to_all(first, "gz", split_axis=0, concat_axis=0, tiled=True)

    def chunk_b(shift):
        start = 32 + 8 * lax.rem(gy + shift, 4)
        return lax.dynamic_slice_in_dim(spectrum, start, 8, 0)[None] * lax.dynamic_slice_in_dim(
            normals, start, 8, 1
        ).astype(jnp.float32)

    pieces_b = exchange([chunk_b(s) for s in range(4)], "gy")

    pieces_a = exchange(
        [first_z(lax.rem(place + s, 4), arrived_a, table_z) for s in range(4)], "gy"
    )
    sent_b = first_y(place, pieces_b, table_y)
    arrived_b = lax.all_to_all(sent_b, "gz", split_axis=0, concat_axis=0, tiled=True)

    planes = second(place, pieces_a, arrived_b, table_y, table_z)
    lines = lax.all_to_all(
        planes.reshape(128, 2, 2, 8, 128), ALL, split_axis=0, concat_axis=0, tiled=True
    )
    outgoing = third(slots_of(block_owner), lines, table_x)
    return lax.all_to_all(
        outgoing.reshape(128, 1, CAP, 2, BW), ALL, split_axis=0, concat_axis=1, tiled=True
    )


def solution(mesh):
    placed = (P(None, "gx", "gy", "gz"), P("gx", "gy", "gz"), P(ALL, None))
    return jax.shard_map(
        per_device,
        mesh=mesh,
        in_specs=placed,
        out_specs=P(ALL, None, None, None, None),
        check_vma=False,
    )
```

time: 400 us -> 197 us (0.49); the launches traced: 394 us -> 197 us
  blocking collectives: 228 us -> 34.2 us
  waiting for transfers between devices: 28.4 us -> 88.3 us
  matrix products: 58 us -> 0 us
  local copies, waits for them, and re-layouts: 62.9 us -> 14.2 us
  Pallas kernels: 0 us -> 25 us
  starting transfers between devices: 8.44 us -> 30.9 us
    all_to_all x3 -> x1, blocking collectives: 228 us -> 34.2 us  [per_device(): lax.all_to_all(outgoing.reshape(128, 1, CAP, 2, BW), ALL, split_axis=0, c...]
    dot_general x12 -> x0, matrix products: 58 us -> none  [contract(): return jnp.einsum(form, operand, matrix, precision=lax.Precision.HIGHEST)]
    ppermute x0 -> x6, waiting for transfers between devices: none -> 49.7 us  [shifted(): lax.ppermute(piece, axis, [(i, (i + shift) % size) for i in range(size)])]
    pallas_call x0 -> x7, Pallas kernels: none -> 25 us  [the longest x4 9.61 us: first_z(): pl.pallas_call(first_z_kernel, grid_spec=pltpu.PrefetchScalarGridSpec(num...]
    unnamed x15 -> x21, local copies, waits for them, and re-layouts: 28.5 us -> 9.9 us
    squeeze x4 -> x0, local copies, waits for them, and re-layouts: 13.3 us -> none  [the longest x2 6.71 us: transform(): field_pair[0]]
    all_to_all x1 -> x3, starting transfers between devices: 8.44 us -> 21.6 us  [the longest x1 10.4 us: per_device(): lax.all_to_all(planes.reshape(128, 2, 2, 8, 128), ALL, split_axis=0, conc...]
    slice x4, local copies, waits for them, and re-layouts: 12.7 us -> 2.22 us  [the longest x2 1.59 us: per_device(): spectrum[:32].reshape(4, 1, 8, 128, 128)]
  transfers between devices with their start and end apart: 1 -> 9, of which waited for: 1 -> 6; matrix products, arithmetic and copies ran while one was open for 0% -> 2% of each run, Pallas kernels for 0% -> 7%
where the time goes in v1:
time: 197 us
  waiting for transfers between devices  88.3 us (45%)
  blocking collectives  34.2 us (17%)
  starting transfers between devices  30.9 us (16%)
  Pallas kernels  25 us (13%)
  local copies, waits for them, and re-layouts  14.2 us (7%)
  other arithmetic  3.89 us (2%)
    ppermute x6, waiting for transfers between devices, shifted(): lax.ppermute(piece, axis, [(i, (i + shift) % size) for i in range(size)])  49.7 us
    all_to_all x1, blocking collectives, per_device(): lax.all_to_all(outgoing.reshape(128, 1, CAP, 2, BW), ALL, split_axis=0, c...  34.2 us
    all_to_all x1, waiting for transfers between devices, per_device(): lax.all_to_all(planes.reshape(128, 2, 2, 8, 128), ALL, split_axis=0, conc...  28.6 us
    all_to_all x1, starting transfers between devices, per_device(): lax.all_to_all(planes.reshape(128, 2, 2, 8, 128), ALL, split_axis=0, conc...  10.4 us
    all_to_all x1, waiting for transfers between devices, per_device(): lax.all_to_all(sent_b, 'gz', split_axis=0, concat_axis=0, tiled=True)  9.98 us
    unnamed x21, local copies, waits for them, and re-layouts  9.9 us
    pallas_call x4, Pallas kernels, first_z(): pl.pallas_call(first_z_kernel, grid_spec=pltpu.PrefetchScalarGridSpec(num...  9.61 us
    ppermute x6, starting transfers between devices, shifted(): lax.ppermute(piece, axis, [(i, (i + shift) % size) for i in range(size)])  9.32 us
  transfers between devices with their start and end apart: 9, of which 6 were waited for; matrix products, arithmetic and copies ran while one was open for 2% of the time, Pallas kernels for 7%

profile of v1, /device:TPU:1, one launch (start us, length us, event | category | flops | bytes accessed | tf_op | source)
XLA Modules:
  0.0 196.7 jit_solution(865115187501745716)
XLA Ops:
  0.0 1.6 slice-done
  1.6 0.6 slice-done.1
  2.2 2.6 %fusion = f32[4,2,8,128,128]{4,3,2,1,0:T(8,128)} fusion(f32[4,8,128,128]{3,2,1,0:T(8,128)S(1)} %bitcast.26, bf16[2,4,8,128,128]{4,3,2,1,0:T(8,128)(2,1)S(1)} %bitcast.27), kind=kLoop, calls=%fused_computation.1 | loop fusion | flops 2097152 | bytes 8388608 | tf_op jit(solution)/shard_map/mul | solution.py:249
  4.8 5.9 %all-to-all-start = ((f32[4,2,8,128,128]{4,3,2,1,0:T(8,128)}), f32[4,2,8,128,128]{4,3,2,1,0:T(8,128)}, u32[]{:S(2)}, u32[]{:S(2)}) async-start(f32[4,2,8,128,128]{4,3,2,1,0:T(8,128)} %fusion), calls=%async_computation | async-start | bytes 8388608 | tf_op jit(solution)/shard_map/all_to_all | solution.py:252
  10.6 1.9 constant_dynamic-slice_fusion
  12.5 0.9 copy-done.8
  13.5 0.7 convert_multiply_fusion
  14.2 1.4 collective-permute-start.3
  15.5 2.6 %collective-permute-start.4 = (f32[2,8,128,128]{3,2,1,0:T(8,128)S(1)}, f32[2,8,128,128]{3,2,1,0:T(8,128)S(1)}, u32[]{:S(2)}, u32[]{:S(2)}) collective-permute-start(f32[2,8,128,128]{3,2,1,0:T(8,128)S(1)} %get-tuple-element.8), channel_id=1, source_target_pairs={{0,8},{4,12},{8,0},{12,4},{1,9},{5,13},{9,1},{13,5},{2,10},{6,14},... | collective-permute-start | bytes 3145736 | tf_op jit(solution)/shard_map/ppermute | solution.py:230
  18.2 1.1 collective-permute-start.5
  19.2 20.2 %collective-permute-done.3.p1 = f32[2,8,128,128]{3,2,1,0:T(8,128)S(1)} collective-permute-done((f32[2,8,128,128]{3,2,1,0:T(8,128)S(1)}, f32[2,8,128,128]{3,2,1,0:T(8,128)S(1)}, u32[]{:S(2)}, u32[]{:S(2)}) %collective-permute-start.3) | collective-permute-done | bytes 1048608 | tf_op jit(solution)/shard_map/ppermute | solution.py:230
  39.4 23.5 %collective-permute-done.4.p2 = f32[2,8,128,128]{3,2,1,0:T(8,128)S(1)} collective-permute-done((f32[2,8,128,128]{3,2,1,0:T(8,128)S(1)}, f32[2,8,128,128]{3,2,1,0:T(8,128)S(1)}, u32[]{:S(2)}, u32[]{:S(2)}) %collective-permute-start.4) | collective-permute-done | bytes 1048608 | tf_op jit(solution)/shard_map/ppermute | solution.py:230
  62.9 0.0 collective-permute-done.5.p3
  62.9 0.0 copy-done.6
  62.9 4.3 %first_y.1 = f32[4,2,2,256,128]{4,3,2,1,0:T(8,128)S(1)} custom-call(s32[1]{0:T(128)} %bitcast.5.place_ref, f32[2,8,128,128]{3,2,1,0:T(8,128)S(1)} %get-tuple-element.7.p0, f32[2,8,128,128]{3,2,1,0:T(8,128)S(1)} %collective-permute-done.3.p1, f32[2,8,128,128]{3,2,1,0:T(8,128)S(1)} %collective-permute-done.4.p2, ...), custom_call_target="tpu_custom_call" | custom-call | flops 3221225472 | bytes 8388608 | tf_op jit(solution)/shard_map/first_y/pallas_call | solution.py:123
  67.2 0.0 copy-start.1
  67.2 1.3 copy-done.1
  68.5 0.0 all-to-all-done.in_ref
  68.5 5.3 %all-to-all-start.1 = ((f32[4,2,2,256,128]{4,3,2,1,0:T(8,128)}), f32[4,2,2,256,128]{4,3,2,1,0:T(8,128)}, u32[]{:S(2)}, u32[]{:S(2)}) async-start(f32[4,2,2,256,128]{4,3,2,1,0:T(8,128)} %copy-done.1), calls=%async_computation.1 | async-start | bytes 4194304 | tf_op jit(solution)/shard_map/all_to_all | solution.py:266
  73.9 0.0 copy-done
  73.9 2.2 %first_z.5 = f32[2,2,128,256]{3,2,1,0:T(8,128)S(1)} custom-call(s32[1]{0:T(128)S(6)} %rem.115.place_ref, f32[4,2,8,128,128]{4,3,2,1,0:T(8,128)} %all-to-all-done.in_ref, bf16[2,4,256,512]{3,2,1,0:T(8,128)(2,1)S(1)} %copy-done), custom_call_target="tpu_custom_call" | custom-call | flops 805306368 | bytes 4194304 | tf_op jit(solution)/shard_map/first_z/pallas_call | solution.py:90
  76.1 1.3 collective-permute-start
  77.4 2.2 %first_z.6 = f32[2,2,128,256]{3,2,1,0:T(8,128)S(1)} custom-call(s32[1]{0:T(128)S(6)} %rem.121.place_ref, f32[4,2,8,128,128]{4,3,2,1,0:T(8,128)} %all-to-all-done.in_ref, bf16[2,4,256,512]{3,2,1,0:T(8,128)(2,1)S(1)} %copy-done), custom_call_target="tpu_custom_call" | custom-call | flops 805306368 | bytes 4194304 | tf_op jit(solution)/shard_map/first_z/pallas_call | solution.py:90
  79.6 3.0 %collective-permute-start.1 = (f32[2,2,128,256]{3,2,1,0:T(8,128)S(1)}, f32[2,2,128,256]{3,2,1,0:T(8,128)}, u32[]{:S(2)}, u32[]{:S(2)}) collective-permute-start(f32[2,2,128,256]{3,2,1,0:T(8,128)S(1)} %first_z.6), channel_id=1, source_target_pairs={{0,8},{4,12},{8,0},{12,4},{1,9},{5,13},{9,1},{13,5},{2,10},{6,14},... | collective-permute-start | bytes 1572872 | tf_op jit(solution)/shard_map/ppermute | solution.py:230
  82.5 3.0 %first_z.7 = f32[2,2,128,256]{3,2,1,0:T(8,128)} custom-call(s32[1]{0:T(128)S(6)} %rem.127.place_ref, f32[4,2,8,128,128]{4,3,2,1,0:T(8,128)} %all-to-all-done.in_ref, bf16[2,4,256,512]{3,2,1,0:T(8,128)(2,1)S(1)} %copy-done), custom_call_target="tpu_custom_call" | custom-call | flops 805306368 | bytes 4194304 | tf_op jit(solution)/shard_map/first_z/pallas_call | solution.py:90
  85.6 0.0 collective-permute-start.2
  85.6 2.2 %first_z.4.p0 = f32[2,2,128,256]{3,2,1,0:T(8,128)S(1)} custom-call(s32[1]{0:T(128)S(6)} %rem.109.place_ref, f32[4,2,8,128,128]{4,3,2,1,0:T(8,128)} %all-to-all-done.in_ref, bf16[2,4,256,512]{3,2,1,0:T(8,128)(2,1)S(1)} %copy-done), custom_call_target="tpu_custom_call" | custom-call | flops 805306368 | bytes 4194304 | tf_op jit(solution)/shard_map/first_z/pallas_call | solution.py:90
  87.8 0.0 copy-start.4
  87.8 0.8 copy-done.4
  88.6 10.0 %all-to-all-done.1.b_ref = f32[4,2,2,256,128]{4,3,2,1,0:T(8,128)} async-done(((f32[4,2,2,256,128]{4,3,2,1,0:T(8,128)}), f32[4,2,2,256,128]{4,3,2,1,0:T(8,128)}, u32[]{:S(2)}, u32[]{:S(2)}) %all-to-all-start.1) | async-done | bytes 2097184 | tf_op jit(solution)/shard_map/all_to_all | solution.py:266
  98.6 0.0 collective-permute-done.p1
  98.6 4.2 %collective-permute-done.1.p2 = f32[2,2,128,256]{3,2,1,0:T(8,128)} collective-permute-done((f32[2,2,128,256]{3,2,1,0:T(8,128)S(1)}, f32[2,2,128,256]{3,2,1,0:T(8,128)}, u32[]{:S(2)}, u32[]{:S(2)}) %collective-permute-start.1) | collective-permute-done | bytes 524320 | tf_op jit(solution)/shard_map/ppermute | solution.py:230
  102.8 1.9 collective-permute-done.2.p3
  104.6 1.0 copy-done.5
  105.7 1.6 copy-done.7
  107.3 6.5 %second.1 = f32[4096,128]{1,0:T(8,128)S(1)} custom-call(s32[1]{0:T(128)} %bitcast.5.place_ref, f32[2,2,128,256]{3,2,1,0:T(8,128)S(1)} %copy-done.5, f32[2,2,128,256]{3,2,1,0:T(8,128)} %collective-permute-done.p1, f32[2,2,128,256]{3,2,1,0:T(8,128)} %collective-permute-done.1.p2, f32[2,2,128,256]{3,2,1,0:T(8,128)} %collective-permute-done.2.p3, ...), custom_call_target="tpu_custom_call" | custom-call | flops 3221225472 | bytes 10485760 | tf_op jit(solution)/shard_map/second/pallas_call | solution.py:168
  113.8 0.0 copy-start.2
  113.8 1.3 copy-done.2
  115.1 10.4 %all-to-all-start.2 = ((f32[128,2,2,8,128]{4,3,2,1,0:T(8,128)}), f32[128,2,2,8,128]{4,3,2,1,0:T(8,128)S(1)}, u32[]{:S(2)}, u32[]{:S(2)}) async-start(f32[128,2,2,8,128]{4,3,2,1,0:T(8,128)} %bitcast.24), calls=%async_computation.2 | async-start | bytes 4194304 | tf_op jit(solution)/shard_map/all_to_all | solution.py:269
  125.6 0.1 copy.11
  125.7 0.2 fusion.3
  126.0 0.1 copy.12
  126.1 0.4 fusion.2
  126.4 28.6 %all-to-all-done.2.in_ref = f32[128,2,2,8,128]{4,3,2,1,0:T(8,128)S(1)} async-done(((f32[128,2,2,8,128]{4,3,2,1,0:T(8,128)}), f32[128,2,2,8,128]{4,3,2,1,0:T(8,128)S(1)}, u32[]{:S(2)}, u32[]{:S(2)}) %all-to-all-start.2) | async-done | bytes 2097184 | tf_op jit(solution)/shard_map/all_to_all | solution.py:269
  155.0 1.6 copy-done.3
  156.6 4.5 %third.1 = f32[4096,128]{1,0:T(8,128)S(1)} custom-call(s32[1024]{0:T(1024)S(1)} %multiply_add_fusion.slot_ref, f32[128,2,2,8,128]{4,3,2,1,0:T(8,128)S(1)} %all-to-all-done.2.in_ref, bf16[2,512,1024]{2,1,0:T(8,128)(2,1)S(1)} %copy-done.3), custom_call_target="tpu_custom_call" | custom-call | flops 1610612736 | bytes 6291456 | tf_op jit(solution)/shard_map/third/pallas_call | solution.py:209
  161.2 34.2 %all_to_all.27 = f32[128,1,16,2,128]{4,3,2,1,0:T(2,128)S(1)} all-to-all(f32[128,1,16,2,128]{4,3,2,1,0:T(2,128)S(1)} %bitcast.23), channel_id=1, replica_groups=mesh['gx'=8,'gy'=4,'gz'=4] {'gx','gy','gz'}, dimensions={0} | all-to-all | bytes 4194304 | tf_op jit(solution)/shard_map/all_to_all | solution.py:273
  195.4 1.3 copy.19
  (15 shorter events, 0.1 us)
Async XLA Ops:
  0.0 1.6 slice-start
  0.0 2.2 %slice-start.1 = ((bf16[2,64,128,128]{3,2,1,0:T(8,128)(2,1)}), bf16[2,32,128,128]{3,2,1,0:T(8,128)(2,1)S(1)}, s32[]{:S(2)}) async-start(bf16[2,64,128,128]{3,2,1,0:T(8,128)(2,1)} %param.6), calls=%async_computation.5 | async-start | bytes 4194304 | tf_op jit(solution)/shard_map/slice | solution.py:249
  4.8 63.8 %all-to-all-start = ((f32[4,2,8,128,128]{4,3,2,1,0:T(8,128)}), f32[4,2,8,128,128]{4,3,2,1,0:T(8,128)}, u32[]{:S(2)}, u32[]{:S(2)}) async-start(f32[4,2,8,128,128]{4,3,2,1,0:T(8,128)} %fusion), calls=%async_computation | async-start | bytes 8388608 | tf_op jit(solution)/shard_map/all_to_all | solution.py:252
  10.6 2.8 %copy-start.8 = (bf16[2,64,128,128]{3,2,1,0:T(8,128)(2,1)S(1)}, bf16[2,64,128,128]{3,2,1,0:T(8,128)(2,1)}, u32[]{:S(2)}) copy-start(bf16[2,64,128,128]{3,2,1,0:T(8,128)(2,1)} %param.6) | copy-start | bytes 12582916
  13.5 49.4 %copy-start.6 = (bf16[2,4,512,256]{3,2,1,0:T(8,128)(2,1)S(1)}, bf16[2,4,512,256]{3,2,1,0:T(8,128)(2,1)}, u32[]{:S(2)}) copy-start(bf16[2,4,512,256]{3,2,1,0:T(8,128)(2,1)} %constant.69.clone.table_ref.table_y_ref) | copy-start | bytes 6291460
  14.2 25.2 %collective-permute-start.3 = (f32[2,8,128,128]{3,2,1,0:T(8,128)S(1)}, f32[2,8,128,128]{3,2,1,0:T(8,128)S(1)}, u32[]{:S(2)}, u32[]{:S(2)}) collective-permute-start(f32[2,8,128,128]{3,2,1,0:T(8,128)S(1)} %get-tuple-element.6), channel_id=1, source_target_pairs={{0,4},{4,8},{8,12},{12,0},{1,5},{5,9},{9,13},{13,1},{2,6},{6,10},{... | collective-permute-start | bytes 3145736 | tf_op jit(solution)/shard_map/ppermute | solution.py:230
  15.5 47.3 %collective-permute-start.4 = (f32[2,8,128,128]{3,2,1,0:T(8,128)S(1)}, f32[2,8,128,128]{3,2,1,0:T(8,128)S(1)}, u32[]{:S(2)}, u32[]{:S(2)}) collective-permute-start(f32[2,8,128,128]{3,2,1,0:T(8,128)S(1)} %get-tuple-element.8), channel_id=1, source_target_pairs={{0,8},{4,12},{8,0},{12,4},{1,9},{5,13},{9,1},{13,5},{2,10},{6,14},... | collective-permute-start | bytes 3145736 | tf_op jit(solution)/shard_map/ppermute | solution.py:230
  18.2 44.7 %collective-permute-start.5 = (f32[2,8,128,128]{3,2,1,0:T(8,128)S(1)}, f32[2,8,128,128]{3,2,1,0:T(8,128)S(1)}, u32[]{:S(2)}, u32[]{:S(2)}) collective-permute-start(f32[2,8,128,128]{3,2,1,0:T(8,128)S(1)} %get-tuple-element.5), channel_id=1, source_target_pairs={{0,12},{4,0},{8,4},{12,8},{1,13},{5,1},{9,5},{13,9},{2,14},{6,2},{... | collective-permute-start | bytes 3145736 | tf_op jit(solution)/shard_map/ppermute | solution.py:230
  67.2 1.3 copy-start.1
  68.5 5.3 %copy-start = (bf16[2,4,256,512]{3,2,1,0:T(8,128)(2,1)S(1)}, bf16[2,4,256,512]{3,2,1,0:T(8,128)(2,1)}, u32[]{:S(2)}) copy-start(bf16[2,4,256,512]{3,2,1,0:T(8,128)(2,1)} %constant.70.clone.table_ref.table_z_ref) | copy-start | bytes 6291460
  68.5 30.0 %all-to-all-start.1 = ((f32[4,2,2,256,128]{4,3,2,1,0:T(8,128)}), f32[4,2,2,256,128]{4,3,2,1,0:T(8,128)}, u32[]{:S(2)}, u32[]{:S(2)}) async-start(f32[4,2,2,256,128]{4,3,2,1,0:T(8,128)} %copy-done.1), calls=%async_computation.1 | async-start | bytes 4194304 | tf_op jit(solution)/shard_map/all_to_all | solution.py:266
  76.1 22.5 %collective-permute-start = (f32[2,2,128,256]{3,2,1,0:T(8,128)S(1)}, f32[2,2,128,256]{3,2,1,0:T(8,128)}, u32[]{:S(2)}, u32[]{:S(2)}) collective-permute-start(f32[2,2,128,256]{3,2,1,0:T(8,128)S(1)} %first_z.5), channel_id=1, source_target_pairs={{0,4},{4,8},{8,12},{12,0},{1,5},{5,9},{9,13},{13,1},{2,6},{6,10},{... | collective-permute-start | bytes 1572872 | tf_op jit(solution)/shard_map/ppermute | solution.py:230
  79.6 23.2 %collective-permute-start.1 = (f32[2,2,128,256]{3,2,1,0:T(8,128)S(1)}, f32[2,2,128,256]{3,2,1,0:T(8,128)}, u32[]{:S(2)}, u32[]{:S(2)}) collective-permute-start(f32[2,2,128,256]{3,2,1,0:T(8,128)S(1)} %first_z.6), channel_id=1, source_target_pairs={{0,8},{4,12},{8,0},{12,4},{1,9},{5,13},{9,1},{13,5},{2,10},{6,14},... | collective-permute-start | bytes 1572872 | tf_op jit(solution)/shard_map/ppermute | solution.py:230
  85.6 19.1 %collective-permute-start.2 = (f32[2,2,128,256]{3,2,1,0:T(8,128)}, f32[2,2,128,256]{3,2,1,0:T(8,128)}, u32[]{:S(2)}, u32[]{:S(2)}) collective-permute-start(f32[2,2,128,256]{3,2,1,0:T(8,128)} %first_z.7), channel_id=1, source_target_pairs={{0,12},{4,0},{8,4},{12,8},{1,13},{5,1},{9,5},{13,9},{2,14},{6,2},{... | collective-permute-start | bytes 1572872 | tf_op jit(solution)/shard_map/ppermute | solution.py:230
  87.8 0.8 copy-start.4
  104.6 1.0 copy-start.5
  105.7 1.6 copy-start.7
  113.8 1.3 copy-start.2
  115.1 10.5 %copy-start.9 = (s32[1024,1]{0,1:T(1,128)S(1)}, s32[1024,1]{0,1:T(1,128)}, u32[]{:S(2)}) copy-start(s32[1024,1]{0,1:T(1,128)} %param.8) | copy-start | bytes 12292
  115.1 39.9 %all-to-all-start.2 = ((f32[128,2,2,8,128]{4,3,2,1,0:T(8,128)}), f32[128,2,2,8,128]{4,3,2,1,0:T(8,128)S(1)}, u32[]{:S(2)}, u32[]{:S(2)}) async-start(f32[128,2,2,8,128]{4,3,2,1,0:T(8,128)} %bitcast.24), calls=%async_computation.2 | async-start | bytes 4194304 | tf_op jit(solution)/shard_map/all_to_all | solution.py:269
  155.0 1.6 copy-start.3

commit v2 on v1

v2 whole, which is shorter than its diff:
```python
import functools

import jax
import jax.numpy as jnp
import ml_dtypes
import numpy as np
from jax import lax
from jax.experimental import pallas as pl
from jax.experimental.pallas import tpu as pltpu
from jax.sharding import PartitionSpec as P

N = 512
KEPT = 256
BW = 128
CAP = 16
ALL = ("gx", "gy", "gz")
MIB = 1 << 20
VMEM = 40


def split_table(table):
    high = table.astype(np.float32).astype(ml_dtypes.bfloat16)
    low = (table - high.astype(np.float64)).astype(np.float32).astype(ml_dtypes.bfloat16)
    return np.stack([high, low])


def cos_sin(positions, kept):
    angles = (positions[:, None] * kept[None, :] % N) * (2.0 * np.pi / N)
    return np.cos(angles), np.sin(angles)


@functools.cache
def tables():
    cosine, sine = cos_sin(np.arange(N), np.arange(KEPT))
    real_rows = np.concatenate([cosine, -sine], 1).reshape(4, 1, 128, 2 * KEPT)
    imag_rows = np.concatenate([sine, cosine], 1).reshape(4, 1, 128, 2 * KEPT)
    table_z = np.concatenate([real_rows, imag_rows], 1).reshape(4, 256, 2 * KEPT)
    order = np.arange(KEPT).reshape(KEPT // 2, 2).T.reshape(-1)
    cosine, sine = cos_sin(np.arange(N), order)
    cosine, sine = cosine.reshape(4, 128, KEPT), sine.reshape(4, 128, KEPT)
    top = np.concatenate([cosine, sine], 1)
    bottom = np.concatenate([-sine, cosine], 1)
    table_y = np.concatenate([top, bottom], 2).transpose(0, 2, 1)
    gx, gy, gz = np.meshgrid(np.arange(8), np.arange(4), np.arange(4), indexing="ij")
    first = 64 * gx + 8 * gz + 2 * gy
    second = 64 * gx + 32 + 8 * gy + 2 * gz
    cells = np.stack([first, first + 1, second, second + 1], -1).reshape(128, 4)
    cosine, sine = cos_sin(cells.reshape(-1), np.arange(KEPT))
    cosine = cosine.T.reshape(KEPT, 128, 1, 4)
    sine = sine.T.reshape(KEPT, 128, 1, 4)
    top = np.concatenate([cosine, sine], 2).reshape(KEPT, 1024)
    bottom = np.concatenate([-sine, cosine], 2).reshape(KEPT, 1024)
    table_x = np.concatenate([top, bottom], 0)
    return split_table(table_x), split_table(table_y), split_table(table_z)


def halves(values):
    high = values.astype(jnp.bfloat16)
    low = (values - high.astype(jnp.float32)).astype(jnp.bfloat16)
    return high, low


def product(left, right):
    def dot(a, b):
        return jnp.dot(a, b, preferred_element_type=jnp.float32)

    return dot(left[0], right[0]) + (dot(left[0], right[1]) + dot(left[1], right[0]))


def params(mib):
    return pltpu.CompilerParams(vmem_limit_bytes=mib * MIB)


def cost(multiplies, moved):
    return pl.CostEstimate(flops=6 * multiplies, bytes_accessed=moved, transcendentals=0)


def scale_kernel(place_ref, normals_ref, spectrum_ref, out_ref):
    out_ref[...] = normals_ref[...].astype(jnp.float32) * spectrum_ref[...][None]


def scale(chunk, normals, spectrum):
    return pl.pallas_call(
        scale_kernel,
        grid_spec=pltpu.PrefetchScalarGridSpec(
            num_scalar_prefetch=1,
            grid=(2,),
            in_specs=[
                pl.BlockSpec((2, 4, 128, 128), lambda i, chunk: (0, 2 * chunk[0] + i, 0, 0)),
                pl.BlockSpec((4, 128, 128), lambda i, chunk: (2 * chunk[0] + i, 0, 0)),
            ],
            out_specs=pl.BlockSpec((2, 4, 128, 128), lambda i, chunk: (0, i, 0, 0)),
        ),
        out_shape=jax.ShapeDtypeStruct((2, 8, 128, 128), jnp.float32),
        compiler_params=params(VMEM),
        cost_estimate=cost(1 << 18, 2 * MIB),
        name="scale",
    )(chunk, normals, spectrum)


def rows_z(piece):
    return halves(jnp.concatenate([piece[plane].reshape(-1, 128) for plane in range(2)], axis=1))


def columns_y(piece):
    planes, cells = piece.shape[:2]
    return halves(
        jnp.concatenate([piece[:, x].reshape(256, piece.shape[3]) for x in range(cells)], axis=1)
    )


def source(place, shift):
    return lax.rem(place + (4 - shift), 4)


def first_part_kernel(along_z, place_ref, p0, p1, p3, table_ref, out_ref):
    total = None
    for shift, piece in ((0, p0), (1, p1), (3, p3)):
        g = source(place_ref[0], shift)
        table = (table_ref[0, g], table_ref[1, g])
        if along_z:
            term = product(rows_z(piece[...]), table)
        else:
            term = product(table, columns_y(piece[...]))
        total = term if total is None else total + term
    out_ref[0] = total


def first_part(along_z, place, pieces, table):
    shape = (256, 512) if along_z else (512, 256)
    return pl.pallas_call(
        functools.partial(first_part_kernel, along_z),
        grid_spec=pltpu.PrefetchScalarGridSpec(
            num_scalar_prefetch=1,
            grid=(4,),
            in_specs=[pl.BlockSpec((2, 2, 128, 128), lambda i, place: (0, i, 0, 0))] * 3
            + [pl.BlockSpec((2, 4) + table.shape[2:], lambda i, place: (0, 0, 0, 0))],
            out_specs=pl.BlockSpec((1,) + shape, lambda i, place: (i, 0, 0)),
        ),
        out_shape=jax.ShapeDtypeStruct((4,) + shape, jnp.float32),
        compiler_params=params(VMEM),
        cost_estimate=cost(768 * 1024 * 512, 8 * MIB),
        name="first_part_z" if along_z else "first_part_y",
    )(place, *pieces, table)


def first_last_kernel(along_z, shifts, place_ref, to_ref, part_ref, p2, table_ref, *out_refs):
    table = (table_ref[0, 0], table_ref[1, 0])
    if along_z:
        total = part_ref[0] + product(rows_z(p2[...]), table)
    else:
        total = part_ref[0] + product(table, columns_y(p2[...]))
    for step, out_ref in enumerate(out_refs):

        @pl.when(pl.program_id(0) == step)
        def _():
            for plane in range(2):
                if along_z:
                    out_ref[plane] = total[:, plane * KEPT : (plane + 1) * KEPT].reshape(
                        2, 128, KEPT
                    )
                else:
                    for x in range(2):
                        out_ref[plane, x] = total[
                            plane * KEPT : (plane + 1) * KEPT, x * 128 : (x + 1) * 128
                        ]


def first_last(along_z, shifts, place, to, part, piece, table):
    def pair(i, to):
        shift = shifts[0]
        for step in range(1, len(shifts)):
            shift = jnp.where(i == step, shifts[step], shift)
        return lax.rem(to[0] + shift, 4)

    shape = (2, 2, 128, KEPT) if along_z else (2, 2, KEPT, 128)
    return pl.pallas_call(
        functools.partial(first_last_kernel, along_z, shifts),
        grid_spec=pltpu.PrefetchScalarGridSpec(
            num_scalar_prefetch=2,
            grid=(len(shifts),),
            in_specs=[
                pl.BlockSpec((1,) + part.shape[1:], lambda i, place, to: (pair(i, to), 0, 0)),
                pl.BlockSpec((2, 2, 128, 128), lambda i, place, to: (0, pair(i, to), 0, 0)),
                pl.BlockSpec(
                    (2, 1) + table.shape[2:],
                    lambda i, place, to: (0, lax.rem(place[0] + 2, 4), 0, 0),
                ),
            ],
            out_specs=[pl.BlockSpec(shape, lambda i, place, to: (0, 0, 0, 0))] * len(shifts),
        ),
        out_shape=[jax.ShapeDtypeStruct(shape, jnp.float32)] * len(shifts),
        compiler_params=params(VMEM),
        cost_estimate=cost(len(shifts) * 256 * 256 * 512, 2 * len(shifts) * MIB),
        name="first_last_z" if along_z else "first_last_y",
    )(place, to, part, piece, table)


def second_part_kernel(along_z, place_ref, p0, p1, p3, table_ref, out_ref):
    total = None
    for shift, piece in ((0, p0), (1, p1), (3, p3)):
        g = source(place_ref[0], shift)
        table = (table_ref[0, g], table_ref[1, g])
        if along_z:
            term = product(rows_z(piece[...]), table)
        else:
            term = product(table, columns_y(piece[...]))
        total = term if total is None else total + term
    out_ref[0] = total


def second_part(along_z, place, pieces, table):
    shape = (256, 512) if along_z else (512, 256)
    return pl.pallas_call(
        functools.partial(second_part_kernel, along_z),
        grid_spec=pltpu.PrefetchScalarGridSpec(
            num_scalar_prefetch=1,
            grid=(2,),
            in_specs=[
                pl.BlockSpec((2, 1) + pieces[0].shape[2:], lambda i, place: (0, i, 0, 0))
            ]
            * 3
            + [pl.BlockSpec((2, 4) + table.shape[2:], lambda i, place: (0, 0, 0, 0))],
            out_specs=pl.BlockSpec((1,) + shape, lambda i, place: (i, 0, 0)),
        ),
        out_shape=jax.ShapeDtypeStruct((2,) + shape, jnp.float32),
        compiler_params=params(VMEM),
        cost_estimate=cost(384 * 1024 * 512, 5 * MIB),
        name="second_part_z" if along_z else "second_part_y",
    )(place, *pieces, table)


def second_last_kernel(
    gy_ref, gz_ref, part_y, last_y, table_y_ref, part_z, last_z, table_z_ref, out_ref, held
):
    def put(values, row):
        for half in range(2):
            held[pl.ds(half * 8 + row, 128, stride=16), :] = values[
                :, half * 128 : (half + 1) * 128
            ]

    table = tuple(table_y_ref[i, 0].reshape(256, 256) for i in range(2))
    for x in range(2):
        total = part_y[x].reshape(256, KEPT) + product(table, columns_y(last_y[:, x : x + 1]))
        for plane in range(2):
            put(total[plane * 128 : (plane + 1) * 128], plane * 4 + x)
    table = (table_z_ref[0, 0], table_z_ref[1, 0])
    total = part_z[...].reshape(256, 512) + product(rows_z(last_z[...]), table)
    for x in range(2):
        for plane in range(2):
            put(
                total[x * 128 : (x + 1) * 128, plane * KEPT : (plane + 1) * KEPT],
                plane * 4 + 2 + x,
            )
    out_ref[...] = held[...].reshape(128, 1, 2, 8, 128)


def second_last(gy, gz, part_y, last_y, table_y, part_z, last_z, table_z):
    return pl.pallas_call(
        second_last_kernel,
        grid_spec=pltpu.PrefetchScalarGridSpec(
            num_scalar_prefetch=2,
            grid=(2,),
            in_specs=[
                pl.BlockSpec((2, 2, 128, KEPT), lambda i, gy, gz: (0, 0, i, 0)),
                pl.BlockSpec((2, 2, 128, KEPT), lambda i, gy, gz: (0, 0, 0, 0)),
                pl.BlockSpec(
                    (2, 1, 2, 128, 256), lambda i, gy, gz: (0, lax.rem(gy[0] + 2, 4), 0, i, 0)
                ),
                pl.BlockSpec((2, 128, 512), lambda i, gy, gz: (0, i, 0)),
                pl.BlockSpec((2, 2, 128, 128), lambda i, gy, gz: (0, 0, i, 0)),
                pl.BlockSpec(
                    (2, 1, 256, 512), lambda i, gy, gz: (0, lax.rem(gz[0] + 2, 4), 0, 0)
                ),
            ],
            out_specs=pl.BlockSpec((128, 1, 2, 8, 128), lambda i, gy, gz: (0, i, 0, 0, 0)),
            scratch_shapes=[pltpu.VMEM((2048, 128), jnp.float32)],
        ),
        out_shape=jax.ShapeDtypeStruct((128, 2, 2, 8, 128), jnp.float32),
        compiler_params=params(VMEM),
        cost_estimate=cost(256 * 1024 * 512, 6 * MIB),
        name="second_last",
    )(
        gy,
        gz,
        part_y.reshape(2, 2, KEPT, KEPT),
        last_y,
        table_y.reshape(2, 4, 2, KEPT, 256),
        part_z,
        last_z,
        table_z,
    )


def third_kernel(slot_ref, in_ref, table_ref, out_ref, held):
    parity = pl.program_id(0)

    @pl.when(parity == 0)
    def _():
        out_ref[...] = jnp.zeros_like(out_ref)

    columns = jnp.concatenate(
        [in_ref[:, 0, half].reshape(1024, 128) for half in range(2)], axis=1
    )
    values = jnp.exp(product((table_ref[0], table_ref[1]), halves(columns)))
    for plane in range(2):
        for half in range(2):
            held[plane, half] = values[
                plane * KEPT : (plane + 1) * KEPT, half * 128 : (half + 1) * 128
            ]

    def place_rows(group, carry):
        for offset in range(8):
            x = group * 8 + offset
            for half in range(2):
                slot = slot_ref[x * 4 + parity * 2 + half]
                for plane in range(2):
                    out_ref[pl.ds(slot * 2 + plane, 1), :] = held[plane, half, pl.ds(x, 1), :]
        return carry

    lax.fori_loop(0, KEPT // 8, place_rows, 0)


def third(slots, arrived, table_x):
    return pl.pallas_call(
        third_kernel,
        grid_spec=pltpu.PrefetchScalarGridSpec(
            num_scalar_prefetch=1,
            grid=(2,),
            in_specs=[
                pl.BlockSpec((128, 1, 2, 8, 128), lambda i, slots: (0, i, 0, 0, 0)),
                pl.BlockSpec((2, 512, 1024), lambda i, slots: (0, 0, 0)),
            ],
            out_specs=pl.BlockSpec((4096, 128), lambda i, slots: (0, 0)),
            scratch_shapes=[pltpu.VMEM((2, 2, KEPT, 128), jnp.float32)],
        ),
        out_shape=jax.ShapeDtypeStruct((4096, 128), jnp.float32),
        compiler_params=params(VMEM),
        cost_estimate=cost(512 * 1024 * 512, 6 * MIB),
        name="third",
    )(slots, arrived, table_x)


def shifted(piece, axis, shift):
    size = lax.axis_size(axis)
    return lax.ppermute(piece, axis, [(i, (i + shift) % size) for i in range(size)])


def slots_of(block_owner):
    destination = block_owner[:, 0]
    one_hot = (destination[:, None] == jnp.arange(128, dtype=jnp.int32)[None, :]).astype(jnp.int32)
    earlier = jnp.cumsum(one_hot, axis=0) - one_hot
    return destination * CAP + jnp.sum(earlier * one_hot, axis=1)


def per_device(normals, spectrum, block_owner):
    table_x, table_y, table_z = (jnp.asarray(table) for table in tables())
    gy = lax.axis_index("gy").astype(jnp.int32).reshape(1)
    gz = lax.axis_index("gz").astype(jnp.int32).reshape(1)

    a, b = {}, {}
    for s in (1, 3, 2):
        a[s] = shifted(scale(lax.rem(gz + s, 4), normals, spectrum), "gz", s)
        b[s] = shifted(scale(4 + lax.rem(gy + s, 4), normals, spectrum), "gy", s)
    a[0] = scale(gz, normals, spectrum)
    b[0] = scale(4 + gy, normals, spectrum)

    part_a = first_part(True, gz, (a[0], a[1], a[3]), table_z)
    part_b = first_part(False, gy, (b[0], b[1], b[3]), table_y)
    a1, a3 = first_last(True, (1, 3), gz, gy, part_a, a[2], table_z)
    b1, b3 = first_last(False, (1, 3), gy, gz, part_b, b[2], table_y)
    a2, a0 = first_last(True, (2, 0), gz, gy, part_a, a[2], table_z)
    b2, b0 = first_last(False, (2, 0), gy, gz, part_b, b[2], table_y)
    a1, b1 = shifted(a1, "gy", 1), shifted(b1, "gz", 1)
    a3, b3 = shifted(a3, "gy", 3), shifted(b3, "gz", 3)
    a2, b2 = shifted(a2, "gy", 2), shifted(b2, "gz", 2)

    part_a = second_part(False, gy, (a0, a1, a3), table_y)
    part_b = second_part(True, gz, (b0, b1, b3), table_z)
    planes = second_last(gy, gz, part_a, a2, table_y, part_b, b2, table_z)
    planes, slots = lax.optimization_barrier((planes, slots_of(block_owner)))
    lines = lax.all_to_all(planes, ALL, split_axis=0, concat_axis=0, tiled=True)
    outgoing = third(slots, lines, table_x)
    return lax.all_to_all(
        outgoing.reshape(128, 1, CAP, 2, BW), ALL, split_axis=0, concat_axis=1, tiled=True
    )


def solution(mesh):
    placed = (P(None, "gx", "gy", "gz"), P("gx", "gy", "gz"), P(ALL, None))
    return jax.shard_map(
        per_device,
        mesh=mesh,
        in_specs=placed,
        out_specs=P(ALL, None, None, None, None),
        check_vma=False,
    )
```

time: 197 us -> 185 us (0.939)
  waiting for transfers between devices: 88.3 us -> 22 us
  blocking collectives: 34.2 us -> 76.9 us
  local copies, waits for them, and re-layouts: 14.2 us -> 23.6 us
  Pallas kernels: 25 us -> 33.1 us
  starting transfers between devices: 30.9 us -> 27.4 us
  other arithmetic: 3.89 us -> 0.63 us
    all_to_all x0 -> x1, blocking collectives: none -> 42.7 us  [per_device(): lines = lax.all_to_all(planes, ALL, split_axis=0, concat_axis=0, tiled=True)]
    all_to_all x3 -> x0, waiting for transfers between devices: 38.6 us -> none  [the longest x1 28.6 us: per_device(): lax.all_to_all(planes.reshape(128, 2, 2, 8, 128), ALL, split_axis=0, conc...]
    ppermute x6 -> x12, waiting for transfers between devices: 49.7 us -> 22 us  [shifted(): lax.ppermute(piece, axis, [(i, (i + shift) % size) for i in range(size)])]
    all_to_all x3 -> x0, starting transfers between devices: 21.6 us -> none  [the longest x1 10.4 us: per_device(): lax.all_to_all(planes.reshape(128, 2, 2, 8, 128), ALL, split_axis=0, conc...]
    ppermute x6 -> x12, starting transfers between devices: 9.32 us -> 27.4 us  [shifted(): lax.ppermute(piece, axis, [(i, (i + shift) % size) for i in range(size)])]
    unnamed x21 -> x41, local copies, waits for them, and re-layouts: 9.9 us -> 23.3 us
    pallas_call x6 -> x17, Pallas kernels: 20.4 us -> 28.5 us  [the longest x2 9.19 us: first_part(): pl.pallas_call(functools.partial(first_part_kernel, along_z), grid_spec=p...]
    mul x2 -> x0, other arithmetic: 3.26 us -> none  [the longest x1 2.56 us: per_device(): spectrum[:32].reshape(4, 1, 8, 128, 128)]
  transfers between devices with their start and end apart: 9 -> 12, of which waited for: 6 -> 4; matrix products, arithmetic and copies ran while one was open for 2% -> 0% of each run, Pallas kernels for 7% -> 14%
where the time goes in v2:
time: 185 us; the launch traced here: 184 us
  blocking collectives  76.9 us (42%)
  Pallas kernels  33.1 us (18%)
  starting transfers between devices  27.4 us (15%)
  local copies, waits for them, and re-layouts  23.6 us (13%)
  waiting for transfers between devices  22 us (12%)
    all_to_all x1, blocking collectives, per_device(): lines = lax.all_to_all(planes, ALL, split_axis=0, concat_axis=0, tiled=True)  42.7 us
    all_to_all x1, blocking collectives, per_device(): lax.all_to_all(outgoing.reshape(128, 1, CAP, 2, BW), ALL, split_axis=0, c...  34.2 us
    ppermute x12, starting transfers between devices, shifted(): lax.ppermute(piece, axis, [(i, (i + shift) % size) for i in range(size)])  27.4 us
    unnamed x41, local copies, waits for them, and re-layouts  23.3 us
    ppermute x12, waiting for transfers between devices, shifted(): lax.ppermute(piece, axis, [(i, (i + shift) % size) for i in range(size)])  22 us
    pallas_call x2, Pallas kernels, first_part(): pl.pallas_call(functools.partial(first_part_kernel, along_z), grid_spec=p...  9.19 us
    pallas_call x4, Pallas kernels, first_last(): pl.pallas_call(functools.partial(first_last_kernel, along_z, shifts), gri...  8.2 us
    pallas_call x8, Pallas kernels, scale(): pl.pallas_call(scale_kernel, grid_spec=pltpu.PrefetchScalarGridSpec(num_s...  5.49 us
  transfers between devices with their start and end apart: 12, of which 4 were waited for; matrix products, arithmetic and copies ran while one was open for 0% of the time, Pallas kernels for 14%

profile of v2, /device:TPU:1, one launch (start us, length us, event | category | flops | bytes accessed | tf_op | source)
XLA Modules:
  0.0 183.9 jit_solution(14623360106625724399)
XLA Ops:
  0.0 2.2 %copy-done = bf16[2,64,128,128]{3,2,1,0:T(8,128)(2,1)S(1)} copy-done((bf16[2,64,128,128]{3,2,1,0:T(8,128)(2,1)S(1)}, bf16[2,64,128,128]{3,2,1,0:T(8,128)(2,1)}, u32[]{:S(2)}) %copy-start) | copy-done | bytes 4194328
  2.2 2.2 %copy-done.5 = f32[64,128,128]{2,1,0:T(8,128)S(1)} copy-done((f32[64,128,128]{2,1,0:T(8,128)S(1)}, f32[64,128,128]{2,1,0:T(8,128)}, u32[]{:S(2)}) %copy-start.5) | copy-done | bytes 4194328
  4.4 0.3 scale.13
  4.6 2.2 %collective-permute-start.6 = (f32[2,8,128,128]{3,2,1,0:T(8,128)S(1)}, f32[2,8,128,128]{3,2,1,0:T(8,128)S(1)}, u32[]{:S(2)}, u32[]{:S(2)}) collective-permute-start(f32[2,8,128,128]{3,2,1,0:T(8,128)S(1)} %scale.13), channel_id=1, source_target_pairs={{0,4},{4,8},{8,12},{12,0},{1,5},{5,9},{9,13},{13,1},{2,6},{6,10},{... | collective-permute-start | bytes 3145736 | tf_op jit(solution)/shard_map/ppermute | solution.py:346
  6.8 0.3 scale.14
  7.1 1.5 collective-permute-start.7
  8.7 1.2 scale.15
  9.8 1.6 collective-permute-start.8
  11.5 2.2 %copy-done.1 = bf16[2,64,128,128]{3,2,1,0:T(8,128)(2,1)S(1)} copy-done((bf16[2,64,128,128]{3,2,1,0:T(8,128)(2,1)S(1)}, bf16[2,64,128,128]{3,2,1,0:T(8,128)(2,1)}, u32[]{:S(2)}) %copy-start.1) | copy-done | bytes 4194328
  13.6 2.2 %copy-done.6 = f32[64,128,128]{2,1,0:T(8,128)S(1)} copy-done((f32[64,128,128]{2,1,0:T(8,128)S(1)}, f32[64,128,128]{2,1,0:T(8,128)}, u32[]{:S(2)}) %copy-start.6) | copy-done | bytes 4194328
  15.8 1.1 scale.9
  16.9 1.6 collective-permute-start
  18.5 1.1 scale.10
  19.6 2.1 %collective-permute-start.1 = (f32[2,8,128,128]{3,2,1,0:T(8,128)}, f32[2,8,128,128]{3,2,1,0:T(8,128)}, u32[]{:S(2)}, u32[]{:S(2)}) collective-permute-start(f32[2,8,128,128]{3,2,1,0:T(8,128)} %scale.10), channel_id=1, source_target_pairs={{0,3},{1,0},{2,1},{3,2},{4,7},{5,4},{6,5},{7,6},{8,11},{9,8},{10,9... | collective-permute-start | bytes 3145736 | tf_op jit(solution)/shard_map/ppermute | solution.py:346
  21.9 2.2 %copy-done.2 = bf16[2,64,128,128]{3,2,1,0:T(8,128)(2,1)S(1)} copy-done((bf16[2,64,128,128]{3,2,1,0:T(8,128)(2,1)S(1)}, bf16[2,64,128,128]{3,2,1,0:T(8,128)(2,1)}, u32[]{:S(2)}) %copy-start.2) | copy-done | bytes 4194328
  24.1 2.2 %copy-done.7 = f32[64,128,128]{2,1,0:T(8,128)S(1)} copy-done((f32[64,128,128]{2,1,0:T(8,128)S(1)}, f32[64,128,128]{2,1,0:T(8,128)}, u32[]{:S(2)}) %copy-start.7) | copy-done | bytes 4194328
  26.2 1.1 scale.11
  27.3 3.8 %collective-permute-done.6.p1 = f32[2,8,128,128]{3,2,1,0:T(8,128)S(1)} collective-permute-done((f32[2,8,128,128]{3,2,1,0:T(8,128)S(1)}, f32[2,8,128,128]{3,2,1,0:T(8,128)S(1)}, u32[]{:S(2)}, u32[]{:S(2)}) %collective-permute-start.6) | collective-permute-done | bytes 1048608 | tf_op jit(solution)/shard_map/ppermute | solution.py:346
  31.1 3.4 %collective-permute-start.2 = (f32[2,8,128,128]{3,2,1,0:T(8,128)}, f32[2,8,128,128]{3,2,1,0:T(8,128)}, u32[]{:S(2)}, u32[]{:S(2)}) collective-permute-start(f32[2,8,128,128]{3,2,1,0:T(8,128)} %scale.11), channel_id=1, source_target_pairs={{0,2},{1,3},{2,0},{3,1},{4,6},{5,7},{6,4},{7,5},{8,10},{9,11},{10,... | collective-permute-start | bytes 3145736 | tf_op jit(solution)/shard_map/ppermute | solution.py:346
  34.7 0.8 copy-done.16
  35.6 2.2 %copy-done.3 = bf16[2,64,128,128]{3,2,1,0:T(8,128)(2,1)S(1)} copy-done((bf16[2,64,128,128]{3,2,1,0:T(8,128)(2,1)S(1)}, bf16[2,64,128,128]{3,2,1,0:T(8,128)(2,1)}, u32[]{:S(2)}) %copy-start.3) | copy-done | bytes 4194328
  37.7 2.2 %copy-done.8 = f32[64,128,128]{2,1,0:T(8,128)S(1)} copy-done((f32[64,128,128]{2,1,0:T(8,128)S(1)}, f32[64,128,128]{2,1,0:T(8,128)}, u32[]{:S(2)}) %copy-start.8) | copy-done | bytes 4194328
  39.9 0.3 scale.12.p0
  40.2 1.3 copy-done.11
  41.5 1.2 copy-done.15
  42.7 4.6 %first_part_y.1.part_ref = f32[4,512,256]{2,1,0:T(8,128)S(1)} custom-call(s32[1]{0:T(128)} %bitcast.to_ref.place_ref.gy_ref, f32[2,8,128,128]{3,2,1,0:T(8,128)S(1)} %scale.12.p0, f32[2,8,128,128]{3,2,1,0:T(8,128)S(1)} %copy-done.15, f32[2,8,128,128]{3,2,1,0:T(8,128)} %collective-permute-done.7.p3, bf16[2,4,512,256]{3,2,1,0:T(8,128)(2,1)S(1)} %copy-done.11), custom_call_target="tpu_custom_call" | custom-call | flops 2415919104 | bytes 8388608 | tf_op jit(solution)/shard_map/first_part_y/pallas_call | solution.py:131
  47.4 7.2 %collective-permute-done.8.p2 = f32[2,8,128,128]{3,2,1,0:T(8,128)} collective-permute-done((f32[2,8,128,128]{3,2,1,0:T(8,128)}, f32[2,8,128,128]{3,2,1,0:T(8,128)}, u32[]{:S(2)}, u32[]{:S(2)}) %collective-permute-start.8) | collective-permute-done | bytes 1048608 | tf_op jit(solution)/shard_map/ppermute | solution.py:346
  54.6 2.7 %first_last_y.3 = (f32[2,2,256,128]{3,2,1,0:T(8,128)S(1)}, f32[2,2,256,128]{3,2,1,0:T(8,128)}) custom-call(s32[1]{0:T(128)} %bitcast.to_ref.place_ref.gy_ref, s32[1]{0:T(128)} %bitcast.1.place_ref.to_ref.gz_ref, f32[4,512,256]{2,1,0:T(8,128)S(1)} %first_part_y.1.part_ref, f32[2,8,128,128]{3,2,1,0:T(8,128)} %collective-permute-done.8.p2, ...), custom_call_target="tpu_custom_call" | custom-call | flops 402653184 | bytes 4194304 | tf_op jit(solution)/shard_map/first_last_y/pallas_call | solution.py:177
  57.3 3.8 %collective-permute-start.10 = (f32[2,2,256,128]{3,2,1,0:T(8,128)}, f32[2,2,256,128]{3,2,1,0:T(8,128)S(1)}, u32[]{:S(2)}, u32[]{:S(2)}) collective-permute-start(f32[2,2,256,128]{3,2,1,0:T(8,128)} %get-tuple-element.21), channel_id=1, source_target_pairs={{0,3},{1,0},{2,1},{3,2},{4,7},{5,4},{6,5},{7,6},{8,11},{9,8},{10,9... | collective-permute-start | bytes 1572872 | tf_op jit(solution)/shard_map/ppermute | solution.py:346
  61.3 0.3 scale.8.p0
  61.7 1.2 copy-done.10
  62.9 4.6 %first_part_z.1.part_ref = f32[4,256,512]{2,1,0:T(8,128)S(1)} custom-call(s32[1]{0:T(128)} %bitcast.1.place_ref.to_ref.gz_ref, f32[2,8,128,128]{3,2,1,0:T(8,128)S(1)} %scale.8.p0, f32[2,8,128,128]{3,2,1,0:T(8,128)} %collective-permute-done.p1, f32[2,8,128,128]{3,2,1,0:T(8,128)} %collective-permute-done.1.p3, bf16[2,4,256,512]{3,2,1,0:T(8,128)(2,1)S(1)} %copy-done.10), custom_call_target="tpu_custom_call" | custom-call | flops 2415919104 | bytes 8388608 | tf_op jit(solution)/shard_map/first_part_z/pallas_call | solution.py:131
  67.5 1.8 first_last_z.3
  69.3 0.9 collective-permute-start.3
  70.2 1.8 collective-permute-start.4
  72.0 1.8 first_last_y.2
  74.1 1.8 first_last_z.2
  75.9 2.5 %collective-permute-done.10.p3 = f32[2,2,256,128]{3,2,1,0:T(8,128)S(1)} collective-permute-done((f32[2,2,256,128]{3,2,1,0:T(8,128)}, f32[2,2,256,128]{3,2,1,0:T(8,128)S(1)}, u32[]{:S(2)}, u32[]{:S(2)}) %collective-permute-start.10) | collective-permute-done | bytes 524320 | tf_op jit(solution)/shard_map/ppermute | solution.py:346
  78.3 8.1 %collective-permute-start.5 = (f32[2,2,128,256]{3,2,1,0:T(8,128)S(1)}, f32[2,2,128,256]{3,2,1,0:T(8,128)S(1)}, u32[]{:S(2)}, u32[]{:S(2)}) collective-permute-start(f32[2,2,128,256]{3,2,1,0:T(8,128)S(1)} %get-tuple-element.18), channel_id=1, source_target_pairs={{0,8},{4,12},{8,0},{12,4},{1,9},{5,13},{9,1},{13,5},{2,10},{6,14},... | collective-permute-start | bytes 1572872 | tf_op jit(solution)/shard_map/ppermute | solution.py:346
  86.5 0.4 fusion.1
  86.9 1.7 second_part_z.1.part_z
  88.6 1.8 second_part_y.1
  90.4 8.6 %collective-permute-done.5.last_y = f32[2,2,128,256]{3,2,1,0:T(8,128)S(1)} collective-permute-done((f32[2,2,128,256]{3,2,1,0:T(8,128)S(1)}, f32[2,2,128,256]{3,2,1,0:T(8,128)S(1)}, u32[]{:S(2)}, u32[]{:S(2)}) %collective-permute-start.5) | collective-permute-done | bytes 524320 | tf_op jit(solution)/shard_map/ppermute | solution.py:346
  99.0 2.1 %second_last.1 = f32[128,2,2,8,128]{4,3,2,1,0:T(8,128)S(1)} custom-call(s32[1]{0:T(128)} %bitcast.to_ref.place_ref.gy_ref, s32[1]{0:T(128)} %bitcast.1.place_ref.to_ref.gz_ref, f32[2,2,256,256]{3,2,1,0:T(8,128)S(1)} %bitcast.20, f32[2,2,128,256]{3,2,1,0:T(8,128)S(1)} %collective-permute-done.5.last_y, bf16[2,4,2,256,256]{4,3,2,1,0:T(8,128)(2,1)S(1)} %copy-done.12, ...), custom_call_target="tpu_custom_call" | custom-call | flops 805306368 | bytes 6291456 | tf_op jit(solution)/shard_map/second_last/pallas_call | solution.py:259
  101.1 42.7 %all_to_all.17.in_ref = f32[128,2,2,8,128]{4,3,2,1,0:T(8,128)S(1)} all-to-all(f32[128,2,2,8,128]{4,3,2,1,0:T(8,128)S(1)} %second_last.1), channel_id=1, replica_groups=mesh['gx'=8,'gy'=4,'gz'=4] {'gx','gy','gz'}, dimensions={0} | all-to-all | bytes 4194304 | tf_op jit(solution)/shard_map/all_to_all | solution.py:382
  143.8 4.6 %third.1 = f32[4096,128]{1,0:T(8,128)S(1)} custom-call(s32[1024]{0:T(1024)S(1)} %multiply_add_fusion.slot_ref, f32[128,2,2,8,128]{4,3,2,1,0:T(8,128)S(1)} %all_to_all.17.in_ref, bf16[2,512,1024]{2,1,0:T(8,128)(2,1)S(1)} %copy-done.13), custom_call_target="tpu_custom_call" | custom-call | flops 1610612736 | bytes 6291456 | tf_op jit(solution)/shard_map/third/pallas_call | solution.py:325
  148.4 34.2 %all_to_all.18 = f32[128,1,16,2,128]{4,3,2,1,0:T(2,128)S(1)} all-to-all(f32[128,1,16,2,128]{4,3,2,1,0:T(2,128)S(1)} %bitcast.19), channel_id=1, replica_groups=mesh['gx'=8,'gy'=4,'gz'=4] {'gx','gy','gz'}, dimensions={0} | all-to-all | bytes 4194304 | tf_op jit(solution)/shard_map/all_to_all | solution.py:384
  182.6 1.3 copy.14
  (47 shorter events, 0.8 us)
Async XLA Ops:
  0.0 2.2 %copy-start = (bf16[2,64,128,128]{3,2,1,0:T(8,128)(2,1)S(1)}, bf16[2,64,128,128]{3,2,1,0:T(8,128)(2,1)}, u32[]{:S(2)}) copy-start(bf16[2,64,128,128]{3,2,1,0:T(8,128)(2,1)} %normals_ref.15) | copy-start | bytes 12582916
  2.2 2.2 %copy-start.5 = (f32[64,128,128]{2,1,0:T(8,128)S(1)}, f32[64,128,128]{2,1,0:T(8,128)}, u32[]{:S(2)}) copy-start(f32[64,128,128]{2,1,0:T(8,128)} %spectrum_ref.15) | copy-start | bytes 12582916
  4.6 26.5 %collective-permute-start.6 = (f32[2,8,128,128]{3,2,1,0:T(8,128)S(1)}, f32[2,8,128,128]{3,2,1,0:T(8,128)S(1)}, u32[]{:S(2)}, u32[]{:S(2)}) collective-permute-start(f32[2,8,128,128]{3,2,1,0:T(8,128)S(1)} %scale.13), channel_id=1, source_target_pairs={{0,4},{4,8},{8,12},{12,0},{1,5},{5,9},{9,13},{13,1},{2,6},{6,10},{... | collective-permute-start | bytes 3145736 | tf_op jit(solution)/shard_map/ppermute | solution.py:346
  7.1 33.1 %collective-permute-start.7 = (f32[2,8,128,128]{3,2,1,0:T(8,128)S(1)}, f32[2,8,128,128]{3,2,1,0:T(8,128)}, u32[]{:S(2)}, u32[]{:S(2)}) collective-permute-start(f32[2,8,128,128]{3,2,1,0:T(8,128)S(1)} %scale.14), channel_id=1, source_target_pairs={{0,12},{4,0},{8,4},{12,8},{1,13},{5,1},{9,5},{13,9},{2,14},{6,2},{... | collective-permute-start | bytes 3145736 | tf_op jit(solution)/shard_map/ppermute | solution.py:346
  9.8 44.8 %collective-permute-start.8 = (f32[2,8,128,128]{3,2,1,0:T(8,128)}, f32[2,8,128,128]{3,2,1,0:T(8,128)}, u32[]{:S(2)}, u32[]{:S(2)}) collective-permute-start(f32[2,8,128,128]{3,2,1,0:T(8,128)} %scale.15), channel_id=1, source_target_pairs={{0,8},{4,12},{8,0},{12,4},{1,9},{5,13},{9,1},{13,5},{2,10},{6,14},... | collective-permute-start | bytes 3145736 | tf_op jit(solution)/shard_map/ppermute | solution.py:346
  11.5 2.2 %copy-start.1 = (bf16[2,64,128,128]{3,2,1,0:T(8,128)(2,1)S(1)}, bf16[2,64,128,128]{3,2,1,0:T(8,128)(2,1)}, u32[]{:S(2)}) copy-start(bf16[2,64,128,128]{3,2,1,0:T(8,128)(2,1)} %normals_ref.15) | copy-start | bytes 12582916
  13.6 2.2 %copy-start.6 = (f32[64,128,128]{2,1,0:T(8,128)S(1)}, f32[64,128,128]{2,1,0:T(8,128)}, u32[]{:S(2)}) copy-start(f32[64,128,128]{2,1,0:T(8,128)} %spectrum_ref.15) | copy-start | bytes 12582916
  16.9 44.8 %collective-permute-start = (f32[2,8,128,128]{3,2,1,0:T(8,128)}, f32[2,8,128,128]{3,2,1,0:T(8,128)}, u32[]{:S(2)}, u32[]{:S(2)}) collective-permute-start(f32[2,8,128,128]{3,2,1,0:T(8,128)} %scale.9), channel_id=1, source_target_pairs={{0,1},{1,2},{2,3},{3,0},{4,5},{5,6},{6,7},{7,4},{8,9},{9,10},{10,1... | collective-permute-start | bytes 3145736 | tf_op jit(solution)/shard_map/ppermute | solution.py:346
  18.5 3.2 %copy-start.18 = (s32[1024,1]{0,1:T(1,128)S(1)}, s32[1024,1]{0,1:T(1,128)}, u32[]{:S(2)}) copy-start(s32[1024,1]{0,1:T(1,128)} %param.8) | copy-start | bytes 12292
  19.6 42.0 %collective-permute-start.1 = (f32[2,8,128,128]{3,2,1,0:T(8,128)}, f32[2,8,128,128]{3,2,1,0:T(8,128)}, u32[]{:S(2)}, u32[]{:S(2)}) collective-permute-start(f32[2,8,128,128]{3,2,1,0:T(8,128)} %scale.10), channel_id=1, source_target_pairs={{0,3},{1,0},{2,1},{3,2},{4,7},{5,4},{6,5},{7,6},{8,11},{9,8},{10,9... | collective-permute-start | bytes 3145736 | tf_op jit(solution)/shard_map/ppermute | solution.py:346
  21.9 2.2 %copy-start.2 = (bf16[2,64,128,128]{3,2,1,0:T(8,128)(2,1)S(1)}, bf16[2,64,128,128]{3,2,1,0:T(8,128)(2,1)}, u32[]{:S(2)}) copy-start(bf16[2,64,128,128]{3,2,1,0:T(8,128)(2,1)} %normals_ref.15) | copy-start | bytes 12582916
  24.1 2.2 %copy-start.7 = (f32[64,128,128]{2,1,0:T(8,128)S(1)}, f32[64,128,128]{2,1,0:T(8,128)}, u32[]{:S(2)}) copy-start(f32[64,128,128]{2,1,0:T(8,128)} %spectrum_ref.15) | copy-start | bytes 12582916
  31.1 9.1 %copy-start.14 = (f32[2,8,128,128]{3,2,1,0:T(8,128)}, f32[2,8,128,128]{3,2,1,0:T(8,128)S(1)}, u32[]{:S(2)}) copy-start(f32[2,8,128,128]{3,2,1,0:T(8,128)S(1)} %collective-permute-done.6.p1) | copy-start | bytes 3145732
  31.1 36.3 %collective-permute-start.2 = (f32[2,8,128,128]{3,2,1,0:T(8,128)}, f32[2,8,128,128]{3,2,1,0:T(8,128)}, u32[]{:S(2)}, u32[]{:S(2)}) collective-permute-start(f32[2,8,128,128]{3,2,1,0:T(8,128)} %scale.11), channel_id=1, source_target_pairs={{0,2},{1,3},{2,0},{3,1},{4,6},{5,7},{6,4},{7,5},{8,10},{9,11},{10,... | collective-permute-start | bytes 3145736 | tf_op jit(solution)/shard_map/ppermute | solution.py:346
  34.7 0.8 copy-start.16
  35.5 4.7 %copy-start.19 = (s32[128,9]{0,1:T(8,128)}, s32[128,9]{0,1:T(8,128)S(1)}, u32[]{:S(2)}) copy-start(s32[128,9]{0,1:T(8,128)S(1)} %reduce-window.9) | copy-start | bytes 13828
  35.5 2.2 %copy-start.3 = (bf16[2,64,128,128]{3,2,1,0:T(8,128)(2,1)S(1)}, bf16[2,64,128,128]{3,2,1,0:T(8,128)(2,1)}, u32[]{:S(2)}) copy-start(bf16[2,64,128,128]{3,2,1,0:T(8,128)(2,1)} %normals_ref.15) | copy-start | bytes 12582916
  37.7 2.2 %copy-start.8 = (f32[64,128,128]{2,1,0:T(8,128)S(1)}, f32[64,128,128]{2,1,0:T(8,128)}, u32[]{:S(2)}) copy-start(f32[64,128,128]{2,1,0:T(8,128)} %spectrum_ref.15) | copy-start | bytes 12582916
  39.9 1.6 copy-start.11
  41.5 1.2 copy-start.15
  42.7 18.5 %copy-start.9 = (f32[64,128,128]{2,1,0:T(8,128)S(1)}, f32[64,128,128]{2,1,0:T(8,128)}, u32[]{:S(2)}) copy-start(f32[64,128,128]{2,1,0:T(8,128)} %spectrum_ref.15) | copy-start | bytes 12582916
  47.4 13.7 %copy-start.17 = (s32[128,8,128]{0,1,2:T(8,128)S(1)}, s32[128,8,128]{0,1,2:T(8,128)}, u32[]{:S(2)}) copy-start(s32[128,8,128]{0,1,2:T(8,128)} %copy-done.16) | copy-start | bytes 1572868
  47.4 13.7 %slice-start = ((s32[128,9]{0,1:T(8,128)}), s32[128,8]{0,1:T(8,128)S(1)}, s32[]{:S(2)}) async-start(s32[128,9]{0,1:T(8,128)} %copy-done.19), calls=%async_computation.2 | async-start | bytes 8192 | tf_op jit(solution)/shard_map/slice.1
  54.6 6.7 %copy-start.4 = (bf16[2,64,128,128]{3,2,1,0:T(8,128)(2,1)S(1)}, bf16[2,64,128,128]{3,2,1,0:T(8,128)(2,1)}, u32[]{:S(2)}) copy-start(bf16[2,64,128,128]{3,2,1,0:T(8,128)(2,1)} %normals_ref.15) | copy-start | bytes 12582916
  57.3 21.0 %collective-permute-start.10 = (f32[2,2,256,128]{3,2,1,0:T(8,128)}, f32[2,2,256,128]{3,2,1,0:T(8,128)S(1)}, u32[]{:S(2)}, u32[]{:S(2)}) collective-permute-start(f32[2,2,256,128]{3,2,1,0:T(8,128)} %get-tuple-element.21), channel_id=1, source_target_pairs={{0,3},{1,0},{2,1},{3,2},{4,7},{5,4},{6,5},{7,6},{8,11},{9,8},{10,9... | collective-permute-start | bytes 1572872 | tf_op jit(solution)/shard_map/ppermute | solution.py:346
  61.3 1.6 copy-start.10
  61.6 25.3 %collective-permute-start.9 = (f32[2,2,256,128]{3,2,1,0:T(8,128)S(1)}, f32[2,2,256,128]{3,2,1,0:T(8,128)S(1)}, u32[]{:S(2)}, u32[]{:S(2)}) collective-permute-start(f32[2,2,256,128]{3,2,1,0:T(8,128)S(1)} %get-tuple-element.20), channel_id=1, source_target_pairs={{0,1},{1,2},{2,3},{3,0},{4,5},{5,6},{6,7},{7,4},{8,9},{9,10},{10,1... | collective-permute-start | bytes 1572872 | tf_op jit(solution)/shard_map/ppermute | solution.py:346
  69.3 19.3 %collective-permute-start.3 = (f32[2,2,128,256]{3,2,1,0:T(8,128)S(1)}, f32[2,2,128,256]{3,2,1,0:T(8,128)S(1)}, u32[]{:S(2)}, u32[]{:S(2)}) collective-permute-start(f32[2,2,128,256]{3,2,1,0:T(8,128)S(1)} %get-tuple-element.16), channel_id=1, source_target_pairs={{0,4},{4,8},{8,12},{12,0},{1,5},{5,9},{9,13},{13,1},{2,6},{6,10},{... | collective-permute-start | bytes 1572872 | tf_op jit(solution)/shard_map/ppermute | solution.py:346
  70.2 18.4 %collective-permute-start.4 = (f32[2,2,128,256]{3,2,1,0:T(8,128)S(1)}, f32[2,2,128,256]{3,2,1,0:T(8,128)S(1)}, u32[]{:S(2)}, u32[]{:S(2)}) collective-permute-start(f32[2,2,128,256]{3,2,1,0:T(8,128)S(1)} %get-tuple-element.17), channel_id=1, source_target_pairs={{0,12},{4,0},{8,4},{12,8},{1,13},{5,1},{9,5},{13,9},{2,14},{6,2},{... | collective-permute-start | bytes 1572872 | tf_op jit(solution)/shard_map/ppermute | solution.py:346
  73.9 16.5 %collective-permute-start.11 = (f32[2,2,256,128]{3,2,1,0:T(8,128)S(1)}, f32[2,2,256,128]{3,2,1,0:T(8,128)S(1)}, u32[]{:S(2)}, u32[]{:S(2)}) collective-permute-start(f32[2,2,256,128]{3,2,1,0:T(8,128)S(1)} %get-tuple-element.22), channel_id=1, source_target_pairs={{0,2},{1,3},{2,0},{3,1},{4,6},{5,7},{6,4},{7,5},{8,10},{9,11},{10,... | collective-permute-start | bytes 1572872 | tf_op jit(solution)/shard_map/ppermute | solution.py:346
  78.3 20.6 %collective-permute-start.5 = (f32[2,2,128,256]{3,2,1,0:T(8,128)S(1)}, f32[2,2,128,256]{3,2,1,0:T(8,128)S(1)}, u32[]{:S(2)}, u32[]{:S(2)}) collective-permute-start(f32[2,2,128,256]{3,2,1,0:T(8,128)S(1)} %get-tuple-element.18), channel_id=1, source_target_pairs={{0,8},{4,12},{8,0},{12,4},{1,9},{5,13},{9,1},{13,5},{2,10},{6,14},... | collective-permute-start | bytes 1572872 | tf_op jit(solution)/shard_map/ppermute | solution.py:346
  88.6 10.4 %copy-start.12 = (bf16[2,4,2,256,256]{4,3,2,1,0:T(8,128)(2,1)S(1)}, bf16[2,4,2,256,256]{4,3,2,1,0:T(8,128)(2,1)}, u32[]{:S(2)}) copy-start(bf16[2,4,2,256,256]{4,3,2,1,0:T(8,128)(2,1)} %constant.57.table_y_ref) | copy-start | bytes 6291460
  101.1 42.7 %copy-start.13 = (bf16[2,512,1024]{2,1,0:T(8,128)(2,1)S(1)}, bf16[2,512,1024]{2,1,0:T(8,128)(2,1)}, u32[]{:S(2)}) copy-start(bf16[2,512,1024]{2,1,0:T(8,128)(2,1)} %constant.54.clone.table_ref) | copy-start | bytes 6291460

commit v3 on v2

--- a/solution.py
+++ b/solution.py
@@ -15,7 +15,7 @@
 CAP = 16
 ALL = ("gx", "gy", "gz")
 MIB = 1 << 20
-VMEM = 40
+VMEM = 60
 
 
 def split_table(table):
@@ -367,6 +367,7 @@
 
     part_a = first_part(True, gz, (a[0], a[1], a[3]), table_z)
     part_b = first_part(False, gy, (b[0], b[1], b[3]), table_y)
+    part_a, part_b = lax.optimization_barrier((part_a, part_b))
     a1, a3 = first_last(True, (1, 3), gz, gy, part_a, a[2], table_z)
     b1, b3 = first_last(False, (1, 3), gy, gz, part_b, b[2], table_y)
     a2, a0 = first_last(True, (2, 0), gz, gy, part_a, a[2], table_z)

time: 185 us -> 192 us (1.038)
  Pallas kernels: 33.1 us -> 62.6 us
  local copies, waits for them, and re-layouts: 23.6 us -> 6.21 us
  waiting for transfers between devices: 22 us -> 9.73 us
  blocking collectives: 76.9 us -> 81.6 us
  starting transfers between devices: 27.4 us -> 29.8 us
    unnamed x41 -> x19, local copies, waits for them, and re-layouts: 23.3 us -> 6 us
    ppermute x12, waiting for transfers between devices: 22 us -> 9.73 us  [shifted(): lax.ppermute(piece, axis, [(i, (i + shift) % size) for i in range(size)])]
    pallas_call x8, Pallas kernels: 5.49 us -> 16.6 us  [scale(): pl.pallas_call(scale_kernel, grid_spec=pltpu.PrefetchScalarGridSpec(num_s...]
    pallas_call x2, Pallas kernels: 3.49 us -> 8.51 us  [second_part(): pl.pallas_call(functools.partial(second_part_kernel, along_z), grid_spec=...]
    all_to_all x1, blocking collectives: 42.7 us -> 47 us  [per_device(): lines = lax.all_to_all(planes, ALL, split_axis=0, concat_axis=0, tiled=True)]
    pallas_call x4, Pallas kernels: 8.2 us -> 12.5 us  [first_last(): pl.pallas_call(functools.partial(first_last_kernel, along_z, shifts), gri...]
    pallas_call x2, Pallas kernels: 9.19 us -> 12.9 us  [first_part(): pl.pallas_call(functools.partial(first_part_kernel, along_z), grid_spec=p...]
    pallas_call x1, Pallas kernels: 4.56 us -> 7.74 us  [third(): pl.pallas_call(third_kernel, grid_spec=pltpu.PrefetchScalarGridSpec(num_s...]
  transfers between devices with their start and end apart: 12 -> 12, of which waited for: 4 -> 2; matrix products, arithmetic and copies ran while one was open for 0% -> 1% of each run, Pallas kernels for 14% -> 25%
where the time goes in v3:
time: 192 us; the launch traced here: 191 us
  blocking collectives  81.6 us (42%)
  Pallas kernels  62.6 us (33%)
  starting transfers between devices  29.8 us (16%)
  waiting for transfers between devices  9.73 us (5%)
  local copies, waits for them, and re-layouts  6.21 us (3%)
    all_to_all x1, blocking collectives, per_device(): lines = lax.all_to_all(planes, ALL, split_axis=0, concat_axis=0, tiled=True)  47 us
    all_to_all x1, blocking collectives, per_device(): lax.all_to_all(outgoing.reshape(128, 1, CAP, 2, BW), ALL, split_axis=0, c...  34.6 us
    ppermute x12, starting transfers between devices, shifted(): lax.ppermute(piece, axis, [(i, (i + shift) % size) for i in range(size)])  29.8 us
    pallas_call x8, Pallas kernels, scale(): pl.pallas_call(scale_kernel, grid_spec=pltpu.PrefetchScalarGridSpec(num_s...  16.6 us
    pallas_call x2, Pallas kernels, first_part(): pl.pallas_call(functools.partial(first_part_kernel, along_z), grid_spec=p...  12.9 us
    pallas_call x4, Pallas kernels, first_last(): pl.pallas_call(functools.partial(first_last_kernel, along_z, shifts), gri...  12.5 us
    ppermute x12, waiting for transfers between devices, shifted(): lax.ppermute(piece, axis, [(i, (i + shift) % size) for i in range(size)])  9.73 us
    pallas_call x2, Pallas kernels, second_part(): pl.pallas_call(functools.partial(second_part_kernel, along_z), grid_spec=...  8.51 us
  transfers between devices with their start and end apart: 12, of which 2 were waited for; matrix products, arithmetic and copies ran while one was open for 1% of the time, Pallas kernels for 25%

profile of v3, /device:TPU:1, one launch (start us, length us, event | category | flops | bytes accessed | tf_op | source)
XLA Modules:
  0.0 191.4 jit_solution(13470624277992893066)
XLA Ops:
  0.0 2.1 %scale.12 = f32[2,8,128,128]{3,2,1,0:T(8,128)} custom-call(s32[1]{0:T(128)S(6)} %add.37.place_ref, bf16[2,64,128,128]{3,2,1,0:T(8,128)(2,1)} %normals_ref.15, f32[64,128,128]{2,1,0:T(8,128)} %spectrum_ref.15), custom_call_target="tpu_custom_call" | custom-call | flops 1572864 | bytes 2097152 | tf_op jit(solution)/shard_map/scale/pallas_call | solution.py:83
  2.1 2.1 %collective-permute-start.2 = (f32[2,8,128,128]{3,2,1,0:T(8,128)}, f32[2,8,128,128]{3,2,1,0:T(8,128)}, u32[]{:S(2)}, u32[]{:S(2)}) collective-permute-start(f32[2,8,128,128]{3,2,1,0:T(8,128)} %scale.12), channel_id=1, source_target_pairs={{0,4},{4,8},{8,12},{12,0},{1,5},{5,9},{9,13},{13,1},{2,6},{6,10},{... | collective-permute-start | bytes 3145736 | tf_op jit(solution)/shard_map/ppermute | solution.py:346
  4.2 2.1 %scale.13 = f32[2,8,128,128]{3,2,1,0:T(8,128)} custom-call(s32[1]{0:T(128)S(6)} %add.39.place_ref, bf16[2,64,128,128]{3,2,1,0:T(8,128)(2,1)} %normals_ref.15, f32[64,128,128]{2,1,0:T(8,128)} %spectrum_ref.15), custom_call_target="tpu_custom_call" | custom-call | flops 1572864 | bytes 2097152 | tf_op jit(solution)/shard_map/scale/pallas_call | solution.py:83
  6.3 1.5 collective-permute-start.3
  7.7 2.0 %scale.9 = f32[2,8,128,128]{3,2,1,0:T(8,128)} custom-call(s32[1]{0:T(128)S(6)} %rem.83.place_ref, bf16[2,64,128,128]{3,2,1,0:T(8,128)(2,1)} %normals_ref.15, f32[64,128,128]{2,1,0:T(8,128)} %spectrum_ref.15), custom_call_target="tpu_custom_call" | custom-call | flops 1572864 | bytes 2097152 | tf_op jit(solution)/shard_map/scale/pallas_call | solution.py:83
  9.8 1.6 collective-permute-start
  11.4 2.1 %scale.10 = f32[2,8,128,128]{3,2,1,0:T(8,128)} custom-call(s32[1]{0:T(128)S(6)} %rem.89.place_ref, bf16[2,64,128,128]{3,2,1,0:T(8,128)(2,1)} %normals_ref.15, f32[64,128,128]{2,1,0:T(8,128)} %spectrum_ref.15), custom_call_target="tpu_custom_call" | custom-call | flops 1572864 | bytes 2097152 | tf_op jit(solution)/shard_map/scale/pallas_call | solution.py:83
  13.6 2.1 %collective-permute-start.1 = (f32[2,8,128,128]{3,2,1,0:T(8,128)}, f32[2,8,128,128]{3,2,1,0:T(8,128)}, u32[]{:S(2)}, u32[]{:S(2)}) collective-permute-start(f32[2,8,128,128]{3,2,1,0:T(8,128)} %scale.10), channel_id=1, source_target_pairs={{0,3},{1,0},{2,1},{3,2},{4,7},{5,4},{6,5},{7,6},{8,11},{9,8},{10,9... | collective-permute-start | bytes 3145736 | tf_op jit(solution)/shard_map/ppermute | solution.py:346
  15.7 2.1 %scale.15 = f32[2,8,128,128]{3,2,1,0:T(8,128)} custom-call(s32[1]{0:T(128)S(6)} %add.42.place_ref, bf16[2,64,128,128]{3,2,1,0:T(8,128)(2,1)} %normals_ref.15, f32[64,128,128]{2,1,0:T(8,128)} %spectrum_ref.15), custom_call_target="tpu_custom_call" | custom-call | flops 1572864 | bytes 2097152 | tf_op jit(solution)/shard_map/scale/pallas_call | solution.py:83
  17.8 1.6 collective-permute-start.8
  19.4 0.1 copy.10
  19.5 2.1 %scale.14 = f32[2,8,128,128]{3,2,1,0:T(8,128)} custom-call(s32[1]{0:T(128)S(6)} %rem.107.place_ref, bf16[2,64,128,128]{3,2,1,0:T(8,128)(2,1)} %normals_ref.15, f32[64,128,128]{2,1,0:T(8,128)} %spectrum_ref.15), custom_call_target="tpu_custom_call" | custom-call | flops 1572864 | bytes 2097152 | tf_op jit(solution)/shard_map/scale/pallas_call | solution.py:83
  21.6 7.1 %collective-permute-done.2.p1 = f32[2,8,128,128]{3,2,1,0:T(8,128)} collective-permute-done((f32[2,8,128,128]{3,2,1,0:T(8,128)}, f32[2,8,128,128]{3,2,1,0:T(8,128)}, u32[]{:S(2)}, u32[]{:S(2)}) %collective-permute-start.2) | collective-permute-done | bytes 1048608 | tf_op jit(solution)/shard_map/ppermute | solution.py:346
  28.7 3.5 %collective-permute-start.4 = (f32[2,8,128,128]{3,2,1,0:T(8,128)}, f32[2,8,128,128]{3,2,1,0:T(8,128)S(1)}, u32[]{:S(2)}, u32[]{:S(2)}) collective-permute-start(f32[2,8,128,128]{3,2,1,0:T(8,128)} %scale.14), channel_id=1, source_target_pairs={{0,2},{1,3},{2,0},{3,1},{4,6},{5,7},{6,4},{7,5},{8,10},{9,11},{10,... | collective-permute-start | bytes 3145736 | tf_op jit(solution)/shard_map/ppermute | solution.py:346
  32.2 0.2 fusion.2
  32.4 2.1 %scale.8.p0 = f32[2,8,128,128]{3,2,1,0:T(8,128)} custom-call(s32[1]{0:T(128)} %bitcast.1.place_ref.to_ref.gz_ref, bf16[2,64,128,128]{3,2,1,0:T(8,128)(2,1)} %normals_ref.15, f32[64,128,128]{2,1,0:T(8,128)} %spectrum_ref.15), custom_call_target="tpu_custom_call" | custom-call | flops 1572864 | bytes 2097152 | tf_op jit(solution)/shard_map/scale/pallas_call | solution.py:83
  34.5 2.1 %scale.11.p0 = f32[2,8,128,128]{3,2,1,0:T(8,128)} custom-call(s32[1]{0:T(128)S(6)} %add.35.place_ref, bf16[2,64,128,128]{3,2,1,0:T(8,128)(2,1)} %normals_ref.15, f32[64,128,128]{2,1,0:T(8,128)} %spectrum_ref.15), custom_call_target="tpu_custom_call" | custom-call | flops 1572864 | bytes 2097152 | tf_op jit(solution)/shard_map/scale/pallas_call | solution.py:83
  36.6 0.0 collective-permute-done.3.p3
  36.6 6.5 %first_part_y.1.part_ref = f32[4,512,256]{2,1,0:T(8,128)} custom-call(s32[1]{0:T(128)} %bitcast.place_ref.to_ref.gy_ref, f32[2,8,128,128]{3,2,1,0:T(8,128)} %scale.11.p0, f32[2,8,128,128]{3,2,1,0:T(8,128)} %collective-permute-done.2.p1, f32[2,8,128,128]{3,2,1,0:T(8,128)} %collective-permute-done.3.p3, bf16[2,4,512,256]{3,2,1,0:T(8,128)(2,1)} %constant.55.clone.table_ref), custom_call_target="tpu_custom_call" | custom-call | flops 2415919104 | bytes 8388608 | tf_op jit(solution)/shard_map/first_part_y/pallas_call | solution.py:131
  43.0 6.4 %first_part_z.1.part_ref = f32[4,256,512]{2,1,0:T(8,128)} custom-call(s32[1]{0:T(128)} %bitcast.1.place_ref.to_ref.gz_ref, f32[2,8,128,128]{3,2,1,0:T(8,128)} %scale.8.p0, f32[2,8,128,128]{3,2,1,0:T(8,128)} %collective-permute-done.p1, f32[2,8,128,128]{3,2,1,0:T(8,128)} %collective-permute-done.1.p3, ...), custom_call_target="tpu_custom_call" | custom-call | flops 2415919104 | bytes 8388608 | tf_op jit(solution)/shard_map/first_part_z/pallas_call | solution.py:131
  49.5 2.6 %collective-permute-done.8.p2 = f32[2,8,128,128]{3,2,1,0:T(8,128)S(1)} collective-permute-done((f32[2,8,128,128]{3,2,1,0:T(8,128)}, f32[2,8,128,128]{3,2,1,0:T(8,128)S(1)}, u32[]{:S(2)}, u32[]{:S(2)}) %collective-permute-start.8) | collective-permute-done | bytes 1048608 | tf_op jit(solution)/shard_map/ppermute | solution.py:346
  52.1 1.0 copy-done
  53.1 3.1 %first_last_y.3 = (f32[2,2,256,128]{3,2,1,0:T(8,128)}, f32[2,2,256,128]{3,2,1,0:T(8,128)}) custom-call(s32[1]{0:T(128)} %bitcast.place_ref.to_ref.gy_ref, s32[1]{0:T(128)} %bitcast.1.place_ref.to_ref.gz_ref, f32[4,512,256]{2,1,0:T(8,128)} %first_part_y.1.part_ref, f32[2,8,128,128]{3,2,1,0:T(8,128)} %copy-done, bf16[2,4,512,256]{3,2,1,0:T(8,128)(2,1)} %constant.55.clone.table_ref), custom_call_target="tpu_custom_call" | custom-call | flops 402653184 | bytes 4194304 | tf_op jit(solution)/shard_map/first_last_y/pallas_call | solution.py:177
  56.2 3.8 %collective-permute-start.10 = (f32[2,2,256,128]{3,2,1,0:T(8,128)}, f32[2,2,256,128]{3,2,1,0:T(8,128)S(1)}, u32[]{:S(2)}, u32[]{:S(2)}) collective-permute-start(f32[2,2,256,128]{3,2,1,0:T(8,128)} %get-tuple-element.25), channel_id=1, source_target_pairs={{0,3},{1,0},{2,1},{3,2},{4,7},{5,4},{6,5},{7,6},{8,11},{9,8},{10,9... | collective-permute-start | bytes 1572872 | tf_op jit(solution)/shard_map/ppermute | solution.py:346
  60.0 0.1 collective-permute-start.9
  60.1 0.1 copy.11
  60.2 1.0 copy-done.1
  61.2 3.1 %first_last_z.3 = (f32[2,2,128,256]{3,2,1,0:T(8,128)}, f32[2,2,128,256]{3,2,1,0:T(8,128)}) custom-call(s32[1]{0:T(128)} %bitcast.1.place_ref.to_ref.gz_ref, s32[1]{0:T(128)} %bitcast.place_ref.to_ref.gy_ref, f32[4,256,512]{2,1,0:T(8,128)} %first_part_z.1.part_ref, f32[2,8,128,128]{3,2,1,0:T(8,128)} %copy-done.1, ...), custom_call_target="tpu_custom_call" | custom-call | flops 402653184 | bytes 4194304 | tf_op jit(solution)/shard_map/first_last_z/pallas_call | solution.py:177
  64.3 2.7 %collective-permute-start.5 = (f32[2,2,128,256]{3,2,1,0:T(8,128)}, f32[2,2,128,256]{3,2,1,0:T(8,128)S(1)}, u32[]{:S(2)}, u32[]{:S(2)}) collective-permute-start(f32[2,2,128,256]{3,2,1,0:T(8,128)} %get-tuple-element.19), channel_id=1, source_target_pairs={{0,4},{4,8},{8,12},{12,0},{1,5},{5,9},{9,13},{13,1},{2,6},{6,10},{... | collective-permute-start | bytes 1572872 | tf_op jit(solution)/shard_map/ppermute | solution.py:346
  67.0 0.3 collective-permute-start.6
  67.4 3.1 %first_last_y.2 = (f32[2,2,256,128]{3,2,1,0:T(8,128)}, f32[2,2,256,128]{3,2,1,0:T(8,128)}) custom-call(s32[1]{0:T(128)} %bitcast.place_ref.to_ref.gy_ref, s32[1]{0:T(128)} %bitcast.1.place_ref.to_ref.gz_ref, f32[4,512,256]{2,1,0:T(8,128)} %first_part_y.1.part_ref, f32[2,8,128,128]{3,2,1,0:T(8,128)} %copy-done, bf16[2,4,512,256]{3,2,1,0:T(8,128)(2,1)} %constant.55.clone.table_ref), custom_call_target="tpu_custom_call" | custom-call | flops 402653184 | bytes 4194304 | tf_op jit(solution)/shard_map/first_last_y/pallas_call | solution.py:177
  70.5 1.3 collective-permute-start.11
  71.8 3.1 %first_last_z.2 = (f32[2,2,128,256]{3,2,1,0:T(8,128)}, f32[2,2,128,256]{3,2,1,0:T(8,128)}) custom-call(s32[1]{0:T(128)} %bitcast.1.place_ref.to_ref.gz_ref, s32[1]{0:T(128)} %bitcast.place_ref.to_ref.gy_ref, f32[4,256,512]{2,1,0:T(8,128)} %first_part_z.1.part_ref, f32[2,8,128,128]{3,2,1,0:T(8,128)} %copy-done.1, ...), custom_call_target="tpu_custom_call" | custom-call | flops 402653184 | bytes 4194304 | tf_op jit(solution)/shard_map/first_last_z/pallas_call | solution.py:177
  74.9 9.2 %collective-permute-start.7 = (f32[2,2,128,256]{3,2,1,0:T(8,128)}, f32[2,2,128,256]{3,2,1,0:T(8,128)S(1)}, u32[]{:S(2)}, u32[]{:S(2)}) collective-permute-start(f32[2,2,128,256]{3,2,1,0:T(8,128)} %get-tuple-element.21), channel_id=1, source_target_pairs={{0,8},{4,12},{8,0},{12,4},{1,9},{5,13},{9,1},{13,5},{2,10},{6,14},... | collective-permute-start | bytes 1572872 | tf_op jit(solution)/shard_map/ppermute | solution.py:346
  84.1 0.4 fusion.1
  84.5 0.6 multiply_add_fusion.slot_ref
  85.1 0.8 copy-done.3
  85.9 4.2 %second_part_z.1.part_z = f32[2,256,512]{2,1,0:T(8,128)} custom-call(s32[1]{0:T(128)} %bitcast.1.place_ref.to_ref.gz_ref, f32[2,2,256,128]{3,2,1,0:T(8,128)} %get-tuple-element.23.p0, f32[2,2,256,128]{3,2,1,0:T(8,128)} %copy-done.3, f32[2,2,256,128]{3,2,1,0:T(8,128)} %copy-done.2, bf16[2,4,256,512]{3,2,1,0:T(8,128)(2,1)} %constant.56.clone.table_ref.table_z_ref), custom_call_target="tpu_custom_call" | custom-call | flops 1207959552 | bytes 5242880 | tf_op jit(solution)/shard_map/second_part_z/pallas_call | solution.py:214
  90.1 0.8 copy-done.5
  90.9 0.2 copy-done.6
  91.1 4.3 %second_part_y.1 = f32[2,512,256]{2,1,0:T(8,128)} custom-call(s32[1]{0:T(128)} %bitcast.place_ref.to_ref.gy_ref, f32[2,2,128,256]{3,2,1,0:T(8,128)} %get-tuple-element.18.p0, f32[2,2,128,256]{3,2,1,0:T(8,128)} %copy-done.5, f32[2,2,128,256]{3,2,1,0:T(8,128)} %copy-done.6, bf16[2,4,512,256]{3,2,1,0:T(8,128)(2,1)} %constant.55.clone.table_ref), custom_call_target="tpu_custom_call" | custom-call | flops 1207959552 | bytes 5242880 | tf_op jit(solution)/shard_map/second_part_y/pallas_call | solution.py:214
  95.4 0.8 copy-done.4
  96.2 0.1 copy-done.7
  96.4 4.3 %second_last.1 = f32[128,2,2,8,128]{4,3,2,1,0:T(8,128)} custom-call(s32[1]{0:T(128)} %bitcast.place_ref.to_ref.gy_ref, s32[1]{0:T(128)} %bitcast.1.place_ref.to_ref.gz_ref, f32[2,2,256,256]{3,2,1,0:T(8,128)} %bitcast.21, f32[2,2,128,256]{3,2,1,0:T(8,128)} %copy-done.7, bf16[2,4,2,256,256]{4,3,2,1,0:T(8,128)(2,1)} %constant.57.table_y_ref, ...), custom_call_target="tpu_custom_call" | custom-call | flops 805306368 | bytes 6291456 | tf_op jit(solution)/shard_map/second_last/pallas_call | solution.py:259
  100.7 47.0 %all_to_all.17.in_ref = f32[128,2,2,8,128]{4,3,2,1,0:T(8,128)} all-to-all(f32[128,2,2,8,128]{4,3,2,1,0:T(8,128)} %second_last.1), channel_id=1, replica_groups=mesh['gx'=8,'gy'=4,'gz'=4] {'gx','gy','gz'}, dimensions={0} | all-to-all | bytes 4194304 | tf_op jit(solution)/shard_map/all_to_all | solution.py:383
  147.7 7.7 %third.1 = f32[4096,128]{1,0:T(8,128)} custom-call(s32[1024]{0:T(1024)} %multiply_add_fusion.slot_ref, f32[128,2,2,8,128]{4,3,2,1,0:T(8,128)} %all_to_all.17.in_ref, bf16[2,512,1024]{2,1,0:T(8,128)(2,1)} %constant.54.clone.table_ref), custom_call_target="tpu_custom_call" | custom-call | flops 1610612736 | bytes 6291456 | tf_op jit(solution)/shard_map/third/pallas_call | solution.py:325
  155.5 34.6 %all_to_all.18 = f32[128,1,16,2,128]{4,3,2,1,0:T(2,128)S(1)} all-to-all(f32[128,1,16,2,128]{4,3,2,1,0:T(2,128)} %bitcast.20), channel_id=1, replica_groups=mesh['gx'=8,'gy'=4,'gz'=4] {'gx','gy','gz'}, dimensions={0} | all-to-all | bytes 4194304 | tf_op jit(solution)/shard_map/all_to_all | solution.py:385
  190.0 1.3 copy.14
  (24 shorter events, 0.1 us)
Async XLA Ops:
  2.1 26.6 %collective-permute-start.2 = (f32[2,8,128,128]{3,2,1,0:T(8,128)}, f32[2,8,128,128]{3,2,1,0:T(8,128)}, u32[]{:S(2)}, u32[]{:S(2)}) collective-permute-start(f32[2,8,128,128]{3,2,1,0:T(8,128)} %scale.12), channel_id=1, source_target_pairs={{0,4},{4,8},{8,12},{12,0},{1,5},{5,9},{9,13},{13,1},{2,6},{6,10},{... | collective-permute-start | bytes 3145736 | tf_op jit(solution)/shard_map/ppermute | solution.py:346
  6.3 30.3 %collective-permute-start.3 = (f32[2,8,128,128]{3,2,1,0:T(8,128)}, f32[2,8,128,128]{3,2,1,0:T(8,128)}, u32[]{:S(2)}, u32[]{:S(2)}) collective-permute-start(f32[2,8,128,128]{3,2,1,0:T(8,128)} %scale.13), channel_id=1, source_target_pairs={{0,12},{4,0},{8,4},{12,8},{1,13},{5,1},{9,5},{13,9},{2,14},{6,2},{... | collective-permute-start | bytes 3145736 | tf_op jit(solution)/shard_map/ppermute | solution.py:346
  9.8 33.3 %collective-permute-start = (f32[2,8,128,128]{3,2,1,0:T(8,128)}, f32[2,8,128,128]{3,2,1,0:T(8,128)}, u32[]{:S(2)}, u32[]{:S(2)}) collective-permute-start(f32[2,8,128,128]{3,2,1,0:T(8,128)} %scale.9), channel_id=1, source_target_pairs={{0,1},{1,2},{2,3},{3,0},{4,5},{5,6},{6,7},{7,4},{8,9},{9,10},{10,1... | collective-permute-start | bytes 3145736 | tf_op jit(solution)/shard_map/ppermute | solution.py:346
  13.6 29.5 %collective-permute-start.1 = (f32[2,8,128,128]{3,2,1,0:T(8,128)}, f32[2,8,128,128]{3,2,1,0:T(8,128)}, u32[]{:S(2)}, u32[]{:S(2)}) collective-permute-start(f32[2,8,128,128]{3,2,1,0:T(8,128)} %scale.10), channel_id=1, source_target_pairs={{0,3},{1,0},{2,1},{3,2},{4,7},{5,4},{6,5},{7,6},{8,11},{9,8},{10,9... | collective-permute-start | bytes 3145736 | tf_op jit(solution)/shard_map/ppermute | solution.py:346
  15.7 3.7 %copy-start.8 = (s32[1024,1]{0,1:T(1,128)S(1)}, s32[1024,1]{0,1:T(1,128)}, u32[]{:S(2)}) copy-start(s32[1024,1]{0,1:T(1,128)} %param.8) | copy-start | bytes 12292
  17.8 34.3 %collective-permute-start.8 = (f32[2,8,128,128]{3,2,1,0:T(8,128)}, f32[2,8,128,128]{3,2,1,0:T(8,128)S(1)}, u32[]{:S(2)}, u32[]{:S(2)}) collective-permute-start(f32[2,8,128,128]{3,2,1,0:T(8,128)} %scale.15), channel_id=1, source_target_pairs={{0,8},{4,12},{8,0},{12,4},{1,9},{5,13},{9,1},{13,5},{2,10},{6,14},... | collective-permute-start | bytes 3145736 | tf_op jit(solution)/shard_map/ppermute | solution.py:346
  28.7 31.5 %collective-permute-start.4 = (f32[2,8,128,128]{3,2,1,0:T(8,128)}, f32[2,8,128,128]{3,2,1,0:T(8,128)S(1)}, u32[]{:S(2)}, u32[]{:S(2)}) collective-permute-start(f32[2,8,128,128]{3,2,1,0:T(8,128)} %scale.14), channel_id=1, source_target_pairs={{0,2},{1,3},{2,0},{3,1},{4,6},{5,7},{6,4},{7,5},{8,10},{9,11},{10,... | collective-permute-start | bytes 3145736 | tf_op jit(solution)/shard_map/ppermute | solution.py:346
  52.1 1.0 copy-start
  56.2 18.7 %collective-permute-start.10 = (f32[2,2,256,128]{3,2,1,0:T(8,128)}, f32[2,2,256,128]{3,2,1,0:T(8,128)S(1)}, u32[]{:S(2)}, u32[]{:S(2)}) collective-permute-start(f32[2,2,256,128]{3,2,1,0:T(8,128)} %get-tuple-element.25), channel_id=1, source_target_pairs={{0,3},{1,0},{2,1},{3,2},{4,7},{5,4},{6,5},{7,6},{8,11},{9,8},{10,9... | collective-permute-start | bytes 1572872 | tf_op jit(solution)/shard_map/ppermute | solution.py:346
  60.0 25.1 %collective-permute-start.9 = (f32[2,2,256,128]{3,2,1,0:T(8,128)}, f32[2,2,256,128]{3,2,1,0:T(8,128)S(1)}, u32[]{:S(2)}, u32[]{:S(2)}) collective-permute-start(f32[2,2,256,128]{3,2,1,0:T(8,128)} %get-tuple-element.24), channel_id=1, source_target_pairs={{0,1},{1,2},{2,3},{3,0},{4,5},{5,6},{6,7},{7,4},{8,9},{9,10},{10,1... | collective-permute-start | bytes 1572872 | tf_op jit(solution)/shard_map/ppermute | solution.py:346
  60.2 1.0 copy-start.1
  64.3 25.8 %collective-permute-start.5 = (f32[2,2,128,256]{3,2,1,0:T(8,128)}, f32[2,2,128,256]{3,2,1,0:T(8,128)S(1)}, u32[]{:S(2)}, u32[]{:S(2)}) collective-permute-start(f32[2,2,128,256]{3,2,1,0:T(8,128)} %get-tuple-element.19), channel_id=1, source_target_pairs={{0,4},{4,8},{8,12},{12,0},{1,5},{5,9},{9,13},{13,1},{2,6},{6,10},{... | collective-permute-start | bytes 1572872 | tf_op jit(solution)/shard_map/ppermute | solution.py:346
  67.0 23.1 %collective-permute-start.6 = (f32[2,2,128,256]{3,2,1,0:T(8,128)}, f32[2,2,128,256]{3,2,1,0:T(8,128)S(1)}, u32[]{:S(2)}, u32[]{:S(2)}) collective-permute-start(f32[2,2,128,256]{3,2,1,0:T(8,128)} %get-tuple-element.20), channel_id=1, source_target_pairs={{0,12},{4,0},{8,4},{12,8},{1,13},{5,1},{9,5},{13,9},{2,14},{6,2},{... | collective-permute-start | bytes 1572872 | tf_op jit(solution)/shard_map/ppermute | solution.py:346
  70.5 24.9 %collective-permute-start.11 = (f32[2,2,256,128]{3,2,1,0:T(8,128)}, f32[2,2,256,128]{3,2,1,0:T(8,128)S(1)}, u32[]{:S(2)}, u32[]{:S(2)}) collective-permute-start(f32[2,2,256,128]{3,2,1,0:T(8,128)} %get-tuple-element.26), channel_id=1, source_target_pairs={{0,2},{1,3},{2,0},{3,1},{4,6},{5,7},{6,4},{7,5},{8,10},{9,11},{10,... | collective-permute-start | bytes 1572872 | tf_op jit(solution)/shard_map/ppermute | solution.py:346
  74.9 10.2 %copy-start.2 = (f32[2,2,256,128]{3,2,1,0:T(8,128)}, f32[2,2,256,128]{3,2,1,0:T(8,128)S(1)}, u32[]{:S(2)}) copy-start(f32[2,2,256,128]{3,2,1,0:T(8,128)S(1)} %collective-permute-done.10.p3) | copy-start | bytes 1572868
  74.9 20.5 %collective-permute-start.7 = (f32[2,2,128,256]{3,2,1,0:T(8,128)}, f32[2,2,128,256]{3,2,1,0:T(8,128)S(1)}, u32[]{:S(2)}, u32[]{:S(2)}) collective-permute-start(f32[2,2,128,256]{3,2,1,0:T(8,128)} %get-tuple-element.21), channel_id=1, source_target_pairs={{0,8},{4,12},{8,0},{12,4},{1,9},{5,13},{9,1},{13,5},{2,10},{6,14},... | collective-permute-start | bytes 1572872 | tf_op jit(solution)/shard_map/ppermute | solution.py:346
  85.1 0.8 copy-start.3
  90.1 0.8 copy-start.5
  90.1 1.0 copy-start.6
  95.4 0.8 copy-start.4
  95.4 1.0 copy-start.7

commit v4 on v2

v4 whole, which is shorter than its diff:
```python
import functools

import jax
import jax.numpy as jnp
import ml_dtypes
import numpy as np
from jax import lax
from jax.experimental import pallas as pl
from jax.experimental.pallas import tpu as pltpu
from jax.sharding import PartitionSpec as P

N = 512
KEPT = 256
BW = 128
CAP = 16
ALL = ("gx", "gy", "gz")
MIB = 1 << 20
VMEM = 40


def split_table(table):
    high = table.astype(np.float32).astype(ml_dtypes.bfloat16)
    low = (table - high.astype(np.float64)).astype(np.float32).astype(ml_dtypes.bfloat16)
    return np.stack([high, low])


def cos_sin(positions, kept):
    angles = (positions[:, None] * kept[None, :] % N) * (2.0 * np.pi / N)
    return np.cos(angles), np.sin(angles)


@functools.cache
def tables():
    cosine, sine = cos_sin(np.arange(N), np.arange(KEPT))
    real_rows = np.concatenate([cosine, -sine], 1).reshape(4, 1, 128, 2 * KEPT)
    imag_rows = np.concatenate([sine, cosine], 1).reshape(4, 1, 128, 2 * KEPT)
    table_z = np.concatenate([real_rows, imag_rows], 1).reshape(4, 256, 2 * KEPT)
    order = np.arange(KEPT).reshape(KEPT // 2, 2).T.reshape(-1)
    cosine, sine = cos_sin(np.arange(N), order)
    cosine, sine = cosine.reshape(4, 128, KEPT), sine.reshape(4, 128, KEPT)
    top = np.concatenate([cosine, sine], 1)
    bottom = np.concatenate([-sine, cosine], 1)
    table_y = np.concatenate([top, bottom], 2).transpose(0, 2, 1)
    gx, gy, gz = np.meshgrid(np.arange(8), np.arange(4), np.arange(4), indexing="ij")
    first = 64 * gx + 8 * gz + 2 * gy
    second = 64 * gx + 32 + 8 * gy + 2 * gz
    cells = np.stack([first, first + 1, second, second + 1], -1).reshape(128, 4)
    cosine, sine = cos_sin(cells.reshape(-1), np.arange(KEPT))
    cosine = cosine.T.reshape(KEPT, 128, 1, 4)
    sine = sine.T.reshape(KEPT, 128, 1, 4)
    top = np.concatenate([cosine, sine], 2).reshape(KEPT, 1024)
    bottom = np.concatenate([-sine, cosine], 2).reshape(KEPT, 1024)
    table_x = np.concatenate([top, bottom], 0)
    return split_table(table_x), split_table(table_y), split_table(table_z)


def halves(values):
    high = values.astype(jnp.bfloat16)
    low = (values - high.astype(jnp.float32)).astype(jnp.bfloat16)
    return high, low


def product(left, right):
    def dot(a, b):
        return jnp.dot(a, b, preferred_element_type=jnp.float32)

    return dot(left[0], right[0]) + (dot(left[0], right[1]) + dot(left[1], right[0]))


def params(mib):
    return pltpu.CompilerParams(vmem_limit_bytes=mib * MIB)


def cost(multiplies, moved):
    return pl.CostEstimate(flops=6 * multiplies, bytes_accessed=moved, transcendentals=0)


def scale_kernel(rotated, place_ref, normals_ref, spectrum_ref, *out_refs):
    for shift, out_ref in enumerate(out_refs if rotated else range(4)):
        chunk = lax.rem(place_ref[0] + shift, 4) if rotated else shift
        values = normals_ref[:, chunk].astype(jnp.float32) * spectrum_ref[chunk][None]
        if rotated:
            out_ref[...] = values
        else:
            out_refs[0][shift] = values


def scale(half, rotated, place, normals, spectrum):
    if rotated:
        out_specs = [pl.BlockSpec((2, 1, 128, 128), lambda i, place: (0, i, 0, 0))] * 4
        out_shape = [jax.ShapeDtypeStruct((2, 8, 128, 128), jnp.float32)] * 4
    else:
        out_specs = pl.BlockSpec((4, 2, 1, 128, 128), lambda i, place: (0, 0, i, 0, 0))
        out_shape = jax.ShapeDtypeStruct((4, 2, 8, 128, 128), jnp.float32)
    return pl.pallas_call(
        functools.partial(scale_kernel, rotated),
        grid_spec=pltpu.PrefetchScalarGridSpec(
            num_scalar_prefetch=1,
            grid=(8,),
            in_specs=[
                pl.BlockSpec((2, 4, 1, 128, 128), lambda i, place: (0, half, i, 0, 0)),
                pl.BlockSpec((4, 1, 128, 128), lambda i, place: (half, i, 0, 0)),
            ],
            out_specs=out_specs,
        ),
        out_shape=out_shape,
        compiler_params=params(60),
        cost_estimate=cost(1 << 20, 8 * MIB),
        name="scale_b" if rotated else "scale_a",
    )(place, normals.reshape(2, 8, 8, 128, 128), spectrum.reshape(8, 8, 128, 128))


def rows_z(piece):
    return halves(jnp.concatenate([piece[plane].reshape(-1, 128) for plane in range(2)], axis=1))


def columns_y(piece):
    planes, cells = piece.shape[:2]
    return halves(
        jnp.concatenate([piece[:, x].reshape(256, piece.shape[3]) for x in range(cells)], axis=1)
    )


def source(place, shift):
    return lax.rem(place + (4 - shift), 4)


def part_kernel(place_ref, p0, p1, p3, table_ref, out_ref):
    total = None
    for shift, piece in ((0, p0), (1, p1), (3, p3)):
        g = source(place_ref[0], shift)
        term = product((table_ref[0, g], table_ref[1, g]), columns_y(piece[...]))
        total = term if total is None else total + term
    out_ref[0] = total


def part_y(place, pieces, cells, table):
    count, columns = pieces[0].shape[1], pieces[0].shape[3]
    return pl.pallas_call(
        part_kernel,
        grid_spec=pltpu.PrefetchScalarGridSpec(
            num_scalar_prefetch=1,
            grid=(count // cells,),
            in_specs=[
                pl.BlockSpec((2, cells, 128, columns), lambda i, place: (0, i, 0, 0))
            ]
            * 3
            + [pl.BlockSpec((2, 4, 512, 256), lambda i, place: (0, 0, 0, 0))],
            out_specs=pl.BlockSpec((1, 512, cells * columns), lambda i, place: (i, 0, 0)),
        ),
        out_shape=jax.ShapeDtypeStruct((count // cells, 512, cells * columns), jnp.float32),
        compiler_params=params(VMEM),
        cost_estimate=cost(count * columns * 768 * 512, 8 * MIB),
        name="part_y",
    )(place, *pieces, table)


def first_y_kernel(place_ref, part_ref, p2, table_ref, out_ref):
    table = (table_ref[0, 0], table_ref[1, 0])
    total = part_ref[0] + product(table, columns_y(p2[...]))
    for plane in range(2):
        for x in range(2):
            out_ref[0, plane, x] = total[
                plane * KEPT : (plane + 1) * KEPT, x * 128 : (x + 1) * 128
            ]


def first_y(place, part, piece, table):
    return pl.pallas_call(
        first_y_kernel,
        grid_spec=pltpu.PrefetchScalarGridSpec(
            num_scalar_prefetch=1,
            grid=(4,),
            in_specs=[
                pl.BlockSpec((1, 512, 256), lambda i, place: (i, 0, 0)),
                pl.BlockSpec((2, 2, 128, 128), lambda i, place: (0, i, 0, 0)),
                pl.BlockSpec(
                    (2, 1, 512, 256), lambda i, place: (0, lax.rem(place[0] + 2, 4), 0, 0)
                ),
            ],
            out_specs=pl.BlockSpec((1, 2, 2, KEPT, 128), lambda i, place: (i, 0, 0, 0, 0)),
        ),
        out_shape=jax.ShapeDtypeStruct((4, 2, 2, KEPT, 128), jnp.float32),
        compiler_params=params(VMEM),
        cost_estimate=cost(1024 * 256 * 512, 6 * MIB),
        name="first_y",
    )(place, part, piece, table)


def first_z_kernel(to_ref, in_ref, table_ref, *out_refs):
    total = None
    for g in range(4):
        term = product(rows_z(in_ref[g]), (table_ref[0, g], table_ref[1, g]))
        total = term if total is None else total + term
    for step, out_ref in enumerate(out_refs):

        @pl.when(pl.program_id(0) == step)
        def _():
            for plane in range(2):
                out_ref[plane] = total[:, plane * KEPT : (plane + 1) * KEPT].reshape(2, 128, KEPT)


def first_z(shifts, to, arrived, table):
    def pair(i, to):
        shift = shifts[0]
        for step in range(1, len(shifts)):
            shift = jnp.where(i == step, shifts[step], shift)
        return lax.rem(to[0] + shift, 4)

    shape = (2, 2, 128, KEPT)
    return pl.pallas_call(
        first_z_kernel,
        grid_spec=pltpu.PrefetchScalarGridSpec(
            num_scalar_prefetch=1,
            grid=(len(shifts),),
            in_specs=[
                pl.BlockSpec((4, 2, 2, 128, 128), lambda i, to: (0, 0, pair(i, to), 0, 0)),
                pl.BlockSpec((2, 4, 256, 512), lambda i, to: (0, 0, 0, 0)),
            ],
            out_specs=[pl.BlockSpec(shape, lambda i, to: (0, 0, 0, 0))] * len(shifts),
        ),
        out_shape=[jax.ShapeDtypeStruct(shape, jnp.float32)] * len(shifts),
        compiler_params=params(VMEM),
        cost_estimate=cost(len(shifts) * 256 * 1024 * 512, 2 * len(shifts) * MIB),
        name="first_z",
    )(to, arrived, table)


def second_kernel(gy_ref, part_ref, last_y, table_y_ref, in_z, table_z_ref, out_ref, held):
    def put(values, row):
        for half in range(2):
            held[pl.ds(half * 8 + row, 128, stride=16), :] = values[
                :, half * 128 : (half + 1) * 128
            ]

    total = None
    for g in range(4):
        term = product(rows_z(in_z[g]), (table_z_ref[0, g], table_z_ref[1, g]))
        total = term if total is None else total + term
    for x in range(2):
        for plane in range(2):
            put(
                total[x * 128 : (x + 1) * 128, plane * KEPT : (plane + 1) * KEPT],
                plane * 4 + 2 + x,
            )
    table = tuple(table_y_ref[i, 0].reshape(256, 256) for i in range(2))
    for x in range(2):
        total = part_ref[x].reshape(256, KEPT) + product(table, columns_y(last_y[:, x : x + 1]))
        for plane in range(2):
            put(total[plane * 128 : (plane + 1) * 128], plane * 4 + x)
    out_ref[...] = held[...].reshape(128, 1, 2, 8, 128)


def second(gy, part, last_y, table_y, arrived, table_z):
    return pl.pallas_call(
        second_kernel,
        grid_spec=pltpu.PrefetchScalarGridSpec(
            num_scalar_prefetch=1,
            grid=(2,),
            in_specs=[
                pl.BlockSpec((2, 2, 128, KEPT), lambda i, gy: (0, 0, i, 0)),
                pl.BlockSpec((2, 2, 128, KEPT), lambda i, gy: (0, 0, 0, 0)),
                pl.BlockSpec(
                    (2, 1, 2, 128, 256), lambda i, gy: (0, lax.rem(gy[0] + 2, 4), 0, i, 0)
                ),
                pl.BlockSpec((4, 2, 2, 128, 128), lambda i, gy: (0, 0, 0, i, 0)),
                pl.BlockSpec((2, 4, 256, 512), lambda i, gy: (0, 0, 0, 0)),
            ],
            out_specs=pl.BlockSpec((128, 1, 2, 8, 128), lambda i, gy: (0, i, 0, 0, 0)),
            scratch_shapes=[pltpu.VMEM((2048, 128), jnp.float32)],
        ),
        out_shape=jax.ShapeDtypeStruct((128, 2, 2, 8, 128), jnp.float32),
        compiler_params=params(VMEM),
        cost_estimate=cost(640 * 1024 * 512, 8 * MIB),
        name="second",
    )(
        gy,
        part.reshape(2, 2, KEPT, KEPT),
        last_y,
        table_y.reshape(2, 4, 2, KEPT, 256),
        arrived,
        table_z,
    )


def third_kernel(slot_ref, in_ref, table_ref, out_ref, held):
    parity = pl.program_id(0)

    @pl.when(parity == 0)
    def _():
        out_ref[...] = jnp.zeros_like(out_ref)

    columns = jnp.concatenate(
        [in_ref[:, 0, half].reshape(1024, 128) for half in range(2)], axis=1
    )
    values = jnp.exp(product((table_ref[0], table_ref[1]), halves(columns)))
    for plane in range(2):
        for half in range(2):
            held[plane, half] = values[
                plane * KEPT : (plane + 1) * KEPT, half * 128 : (half + 1) * 128
            ]

    def place_rows(group, carry):
        for offset in range(8):
            x = group * 8 + offset
            for half in range(2):
                slot = slot_ref[x * 4 + parity * 2 + half]
                for plane in range(2):
                    out_ref[pl.ds(slot * 2 + plane, 1), :] = held[plane, half, pl.ds(x, 1), :]
        return carry

    lax.fori_loop(0, KEPT // 8, place_rows, 0)


def third(slots, arrived, table_x):
    return pl.pallas_call(
        third_kernel,
        grid_spec=pltpu.PrefetchScalarGridSpec(
            num_scalar_prefetch=1,
            grid=(2,),
            in_specs=[
                pl.BlockSpec((128, 1, 2, 8, 128), lambda i, slots: (0, i, 0, 0, 0)),
                pl.BlockSpec((2, 512, 1024), lambda i, slots: (0, 0, 0)),
            ],
            out_specs=pl.BlockSpec((4096, 128), lambda i, slots: (0, 0)),
            scratch_shapes=[pltpu.VMEM((2, 2, KEPT, 128), jnp.float32)],
        ),
        out_shape=jax.ShapeDtypeStruct((4096, 128), jnp.float32),
        compiler_params=params(VMEM),
        cost_estimate=cost(512 * 1024 * 512, 6 * MIB),
        name="third",
    )(slots, arrived, table_x)


def shifted(piece, axis, shift):
    size = lax.axis_size(axis)
    return lax.ppermute(piece, axis, [(i, (i + shift) % size) for i in range(size)])


def slots_of(block_owner):
    destination = block_owner[:, 0]
    one_hot = (destination[:, None] == jnp.arange(128, dtype=jnp.int32)[None, :]).astype(jnp.int32)
    earlier = jnp.cumsum(one_hot, axis=0) - one_hot
    return destination * CAP + jnp.sum(earlier * one_hot, axis=1)


def per_device(normals, spectrum, block_owner):
    table_x, table_y, table_z = (jnp.asarray(table) for table in tables())
    gy = lax.axis_index("gy").astype(jnp.int32).reshape(1)
    gz = lax.axis_index("gz").astype(jnp.int32).reshape(1)

    a = scale(0, False, gz, normals, spectrum)
    a = lax.all_to_all(a, "gz", split_axis=0, concat_axis=0, tiled=True)
    b0, b1, b2, b3 = scale(1, True, gy, normals, spectrum)
    b1, b3, b2 = shifted(b1, "gy", 1), shifted(b3, "gy", 3), shifted(b2, "gy", 2)

    part_b = part_y(gy, (b0, b1, b3), 2, table_y)
    b = first_y(gy, part_b, b2, table_y)
    b = lax.all_to_all(b, "gz", split_axis=0, concat_axis=0, tiled=True)
    a1, a3 = first_z((1, 3), gy, a, table_z)
    a2, a0 = first_z((2, 0), gy, a, table_z)
    a1, a3, a2 = shifted(a1, "gy", 1), shifted(a3, "gy", 3), shifted(a2, "gy", 2)

    part_a = part_y(gy, (a0, a1, a3), 1, table_y)
    planes = second(gy, part_a, a2, table_y, b, table_z)
    planes, slots = lax.optimization_barrier((planes, slots_of(block_owner)))
    lines = lax.all_to_all(planes, ALL, split_axis=0, concat_axis=0, tiled=True)
    outgoing = third(slots, lines, table_x)
    return lax.all_to_all(
        outgoing.reshape(128, 1, CAP, 2, BW), ALL, split_axis=0, concat_axis=1, tiled=True
    )


def solution(mesh):
    placed = (P(None, "gx", "gy", "gz"), P("gx", "gy", "gz"), P(ALL, None))
    return jax.shard_map(
        per_device,
        mesh=mesh,
        in_specs=placed,
        out_specs=P(ALL, None, None, None, None),
        check_vma=False,
    )
```

time: 185 us -> 194 us (1.049)
  waiting for transfers between devices: 22 us -> 53.2 us
  local copies, waits for them, and re-layouts: 23.6 us -> 5.68 us
  starting transfers between devices: 27.4 us -> 18.3 us
  Pallas kernels: 33.1 us -> 36.5 us
    ppermute x12 -> x6, waiting for transfers between devices: 22 us -> 46.7 us  [shifted(): lax.ppermute(piece, axis, [(i, (i + shift) % size) for i in range(size)])]
    ppermute x12 -> x6, starting transfers between devices: 27.4 us -> 7.13 us  [shifted(): lax.ppermute(piece, axis, [(i, (i + shift) % size) for i in range(size)])]
    unnamed x41 -> x19, local copies, waits for them, and re-layouts: 23.3 us -> 5.47 us
    all_to_all x0 -> x2, starting transfers between devices: none -> 11.2 us  [the longest x1 5.86 us: per_device(): a = lax.all_to_all(a, 'gz', split_axis=0, concat_axis=0, tiled=True)]
    all_to_all x0 -> x2, waiting for transfers between devices: none -> 6.49 us  [the longest x1 6.49 us: per_device(): b = lax.all_to_all(b, 'gz', split_axis=0, concat_axis=0, tiled=True)]
    pallas_call x17 -> x8, Pallas kernels: 28.5 us -> 31.9 us  [the longest x2 13.2 us: scale(): pl.pallas_call(functools.partial(scale_kernel, rotated), grid_spec=pltpu....]
  transfers between devices with their start and end apart: 12 -> 8, of which waited for: 4 -> 5; matrix products, arithmetic and copies ran while one was open for 0% -> 0% of each run, Pallas kernels for 14% -> 11%
where the time goes in v4:
time: 194 us; the launch traced here: 193 us
  blocking collectives  78.8 us (41%)
  waiting for transfers between devices  53.2 us (27%)
  Pallas kernels  36.5 us (19%)
  starting transfers between devices  18.3 us (9%)
  local copies, waits for them, and re-layouts  5.68 us (3%)
    ppermute x6, waiting for transfers between devices, shifted(): lax.ppermute(piece, axis, [(i, (i + shift) % size) for i in range(size)])  46.7 us
    all_to_all x1, blocking collectives, per_device(): lines = lax.all_to_all(planes, ALL, split_axis=0, concat_axis=0, tiled=True)  44.5 us
    all_to_all x1, blocking collectives, per_device(): lax.all_to_all(outgoing.reshape(128, 1, CAP, 2, BW), ALL, split_axis=0, c...  34.2 us
    pallas_call x2, Pallas kernels, scale(): pl.pallas_call(functools.partial(scale_kernel, rotated), grid_spec=pltpu....  13.2 us
    pallas_call x2, Pallas kernels, first_z(): pl.pallas_call(first_z_kernel, grid_spec=pltpu.PrefetchScalarGridSpec(num...  7.36 us
    ppermute x6, starting transfers between devices, shifted(): lax.ppermute(piece, axis, [(i, (i + shift) % size) for i in range(size)])  7.13 us
    all_to_all x1, waiting for transfers between devices, per_device(): b = lax.all_to_all(b, 'gz', split_axis=0, concat_axis=0, tiled=True)  6.49 us
    all_to_all x1, starting transfers between devices, per_device(): a = lax.all_to_all(a, 'gz', split_axis=0, concat_axis=0, tiled=True)  5.86 us
  transfers between devices with their start and end apart: 8, of which 5 were waited for; matrix products, arithmetic and copies ran while one was open for 0% of the time, Pallas kernels for 11%

profile of v4, /device:TPU:1, one launch (start us, length us, event | category | flops | bytes accessed | tf_op | source)
XLA Modules:
  0.0 193.3 jit_solution(14201001315277930436)
XLA Ops:
  0.0 6.6 %scale_a.1 = f32[4,2,8,128,128]{4,3,2,1,0:T(8,128)} custom-call(s32[1]{0:T(128)} %bitcast.1.place_ref, bf16[2,8,8,128,128]{4,3,2,1,0:T(8,128)(2,1)} %bitcast.23, f32[8,8,128,128]{3,2,1,0:T(8,128)} %bitcast.25), custom_call_target="tpu_custom_call" | custom-call | flops 6291456 | bytes 8388608 | tf_op jit(solution)/shard_map/scale_a/pallas_call | solution.py:95
  6.6 5.9 %all-to-all-start = ((f32[4,2,8,128,128]{4,3,2,1,0:T(8,128)}), f32[4,2,8,128,128]{4,3,2,1,0:T(8,128)}, u32[]{:S(2)}, u32[]{:S(2)}) async-start(f32[4,2,8,128,128]{4,3,2,1,0:T(8,128)} %scale_a.1), calls=%async_computation | async-start | bytes 8388608 | tf_op jit(solution)/shard_map/all_to_all | solution.py:353
  12.4 0.0 copy-start.1
  12.4 6.7 %scale_b.1 = (f32[2,8,128,128]{3,2,1,0:T(8,128)}, f32[2,8,128,128]{3,2,1,0:T(8,128)}, f32[2,8,128,128]{3,2,1,0:T(8,128)}, f32[2,8,128,128]{3,2,1,0:T(8,128)}) custom-call(s32[1]{0:T(128)} %bitcast.to_ref.place_ref.gy_ref, bf16[2,8,8,128,128]{4,3,2,1,0:T(8,128)(2,1)} %bitcast.24, f32[8,8,128,128]{3,2,1,0:T(8,128)} %bitcast.26), custom_call_target="tpu_custom_call" | custom-call | flops 6291456 | bytes 8388608 | tf_op jit(solution)/shard_map/scale_b/pallas_call | solution.py:95
  19.1 1.3 collective-permute-start.3
  20.4 1.5 collective-permute-start.4
  21.9 1.6 collective-permute-start.5
  23.5 21.0 %collective-permute-done.3.p1 = f32[2,8,128,128]{3,2,1,0:T(8,128)S(1)} collective-permute-done((f32[2,8,128,128]{3,2,1,0:T(8,128)}, f32[2,8,128,128]{3,2,1,0:T(8,128)S(1)}, u32[]{:S(2)}, u32[]{:S(2)}) %collective-permute-start.3) | collective-permute-done | bytes 1048608 | tf_op jit(solution)/shard_map/ppermute | solution.py:337
  44.5 0.0 collective-permute-done.4.p3
  44.5 0.0 copy-done.1
  44.5 0.0 copy-start.6
  44.5 1.2 copy-done.6
  45.7 3.5 %part_y.3.part_ref = f32[4,512,256]{2,1,0:T(8,128)S(1)} custom-call(s32[1]{0:T(128)} %bitcast.to_ref.place_ref.gy_ref, f32[2,8,128,128]{3,2,1,0:T(8,128)S(1)} %copy-done.6, f32[2,8,128,128]{3,2,1,0:T(8,128)S(1)} %collective-permute-done.3.p1, f32[2,8,128,128]{3,2,1,0:T(8,128)S(1)} %collective-permute-done.4.p3, bf16[2,4,512,256]{3,2,1,0:T(8,128)(2,1)S(1)} %copy-done.1), custom_call_target="tpu_custom_call" | custom-call | flops 2415919104 | bytes 8388608 | tf_op jit(solution)/shard_map/part_y/pallas_call | solution.py:139
  49.2 18.8 %collective-permute-done.5.p2 = f32[2,8,128,128]{3,2,1,0:T(8,128)S(1)} collective-permute-done((f32[2,8,128,128]{3,2,1,0:T(8,128)}, f32[2,8,128,128]{3,2,1,0:T(8,128)S(1)}, u32[]{:S(2)}, u32[]{:S(2)}) %collective-permute-start.5) | collective-permute-done | bytes 1048608 | tf_op jit(solution)/shard_map/ppermute | solution.py:337
  67.9 1.7 first_y.1
  69.7 0.0 copy-start.3
  69.7 1.3 copy-done.3
  71.0 0.0 copy-start.7
  71.0 0.0 copy-start
  71.0 0.0 all-to-all-done.in_ref
  71.0 5.3 %all-to-all-start.1 = ((f32[4,2,2,256,128]{4,3,2,1,0:T(8,128)}), f32[4,2,2,256,128]{4,3,2,1,0:T(8,128)}, u32[]{:S(2)}, u32[]{:S(2)}) async-start(f32[4,2,2,256,128]{4,3,2,1,0:T(8,128)} %copy-done.3), calls=%async_computation.1 | async-start | bytes 4194304 | tf_op jit(solution)/shard_map/all_to_all | solution.py:359
  76.3 0.0 copy-done.7
  76.3 0.1 copy.10
  76.4 0.2 fusion.2
  76.7 0.0 copy-done
  76.7 3.3 %first_z.3 = (f32[2,2,128,256]{3,2,1,0:T(8,128)S(1)}, f32[2,2,128,256]{3,2,1,0:T(8,128)S(1)}) custom-call(s32[1]{0:T(128)} %bitcast.to_ref.place_ref.gy_ref, f32[4,2,8,128,128]{4,3,2,1,0:T(8,128)} %all-to-all-done.in_ref, bf16[2,4,256,512]{3,2,1,0:T(8,128)(2,1)S(1)} %copy-done), custom_call_target="tpu_custom_call" | custom-call | flops 1610612736 | bytes 4194304 | tf_op jit(solution)/shard_map/first_z/pallas_call | solution.py:211
  80.0 0.0 copy-done.8
  80.0 0.6 collective-permute-start
  80.6 2.1 %collective-permute-start.1 = (f32[2,2,128,256]{3,2,1,0:T(8,128)S(1)}, f32[2,2,128,256]{3,2,1,0:T(8,128)S(1)}, u32[]{:S(2)}, u32[]{:S(2)}) collective-permute-start(f32[2,2,128,256]{3,2,1,0:T(8,128)S(1)} %get-tuple-element.17), channel_id=1, source_target_pairs={{0,12},{4,0},{8,4},{12,8},{1,13},{5,1},{9,5},{13,9},{2,14},{6,2},{... | collective-permute-start | bytes 1572872 | tf_op jit(solution)/shard_map/ppermute | solution.py:337
  82.8 4.1 %first_z.2 = (f32[2,2,128,256]{3,2,1,0:T(8,128)}, f32[2,2,128,256]{3,2,1,0:T(8,128)S(1)}) custom-call(s32[1]{0:T(128)} %bitcast.to_ref.place_ref.gy_ref, f32[4,2,8,128,128]{4,3,2,1,0:T(8,128)} %all-to-all-done.in_ref, bf16[2,4,256,512]{3,2,1,0:T(8,128)(2,1)S(1)} %copy-done), custom_call_target="tpu_custom_call" | custom-call | flops 1610612736 | bytes 4194304 | tf_op jit(solution)/shard_map/first_z/pallas_call | solution.py:211
  86.8 0.0 collective-permute-start.2
  86.8 0.0 slice-done
  86.9 0.1 copy.11
  87.0 0.4 fusion.1
  87.4 2.4 %collective-permute-done.p1 = f32[2,2,128,256]{3,2,1,0:T(8,128)S(1)} collective-permute-done((f32[2,2,128,256]{3,2,1,0:T(8,128)S(1)}, f32[2,2,128,256]{3,2,1,0:T(8,128)S(1)}, u32[]{:S(2)}, u32[]{:S(2)}) %collective-permute-start) | collective-permute-done | bytes 524320 | tf_op jit(solution)/shard_map/ppermute | solution.py:337
  89.7 0.0 collective-permute-done.1.p3
  89.7 0.0 copy-done.2
  89.7 1.7 part_y.2
  91.5 6.5 %all-to-all-done.1.in_z = f32[4,2,2,256,128]{4,3,2,1,0:T(8,128)} async-done(((f32[4,2,2,256,128]{4,3,2,1,0:T(8,128)}), f32[4,2,2,256,128]{4,3,2,1,0:T(8,128)}, u32[]{:S(2)}, u32[]{:S(2)}) %all-to-all-start.1) | async-done | bytes 2097184 | tf_op jit(solution)/shard_map/all_to_all | solution.py:359
  98.0 4.6 %collective-permute-done.2.last_y = f32[2,2,128,256]{3,2,1,0:T(8,128)} collective-permute-done((f32[2,2,128,256]{3,2,1,0:T(8,128)}, f32[2,2,128,256]{3,2,1,0:T(8,128)}, u32[]{:S(2)}, u32[]{:S(2)}) %collective-permute-start.2) | collective-permute-done | bytes 524320 | tf_op jit(solution)/shard_map/ppermute | solution.py:337
  102.6 1.6 copy-done.4
  104.2 4.4 %second.1 = f32[128,2,2,8,128]{4,3,2,1,0:T(8,128)S(1)} custom-call(s32[1]{0:T(128)} %bitcast.to_ref.place_ref.gy_ref, f32[2,2,256,256]{3,2,1,0:T(8,128)S(1)} %bitcast.22, f32[2,2,128,256]{3,2,1,0:T(8,128)} %collective-permute-done.2.last_y, bf16[2,4,2,256,256]{4,3,2,1,0:T(8,128)(2,1)S(1)} %copy-done.4, f32[4,2,2,256,128]{4,3,2,1,0:T(8,128)} %all-to-all-done.1.in_z, ...), custom_call_target="tpu_custom_call" | custom-call | flops 2013265920 | bytes 8388608 | tf_op jit(solution)/shard_map/second/pallas_call | solution.py:255
  108.6 0.0 copy-start.5
  108.6 44.5 %all_to_all.27.in_ref = f32[128,2,2,8,128]{4,3,2,1,0:T(8,128)S(1)} all-to-all(f32[128,2,2,8,128]{4,3,2,1,0:T(8,128)S(1)} %second.1), channel_id=1, replica_groups=mesh['gx'=8,'gy'=4,'gz'=4] {'gx','gy','gz'}, dimensions={0} | all-to-all | bytes 4194304 | tf_op jit(solution)/shard_map/all_to_all | solution.py:367
  153.2 0.0 copy-done.5
  153.2 4.5 %third.1 = f32[4096,128]{1,0:T(8,128)S(1)} custom-call(s32[1024]{0:T(1024)S(1)} %multiply_add_fusion.slot_ref, f32[128,2,2,8,128]{4,3,2,1,0:T(8,128)S(1)} %all_to_all.27.in_ref, bf16[2,512,1024]{2,1,0:T(8,128)(2,1)S(1)} %copy-done.5), custom_call_target="tpu_custom_call" | custom-call | flops 1610612736 | bytes 6291456 | tf_op jit(solution)/shard_map/third/pallas_call | solution.py:316
  157.7 34.2 %all_to_all.28 = f32[128,1,16,2,128]{4,3,2,1,0:T(2,128)S(1)} all-to-all(f32[128,1,16,2,128]{4,3,2,1,0:T(2,128)S(1)} %bitcast.21), channel_id=1, replica_groups=mesh['gx'=8,'gy'=4,'gz'=4] {'gx','gy','gz'}, dimensions={0} | all-to-all | bytes 4194304 | tf_op jit(solution)/shard_map/all_to_all | solution.py:369
  191.9 1.3 copy.14
  (8 shorter events, 0.1 us)
Async XLA Ops:
  6.6 64.4 %all-to-all-start = ((f32[4,2,8,128,128]{4,3,2,1,0:T(8,128)}), f32[4,2,8,128,128]{4,3,2,1,0:T(8,128)}, u32[]{:S(2)}, u32[]{:S(2)}) async-start(f32[4,2,8,128,128]{4,3,2,1,0:T(8,128)} %scale_a.1), calls=%async_computation | async-start | bytes 8388608 | tf_op jit(solution)/shard_map/all_to_all | solution.py:353
  12.4 32.1 %copy-start.1 = (bf16[2,4,512,256]{3,2,1,0:T(8,128)(2,1)S(1)}, bf16[2,4,512,256]{3,2,1,0:T(8,128)(2,1)}, u32[]{:S(2)}) copy-start(bf16[2,4,512,256]{3,2,1,0:T(8,128)(2,1)} %constant.22.clone.table_ref) | copy-start | bytes 6291460
  19.1 25.4 %collective-permute-start.3 = (f32[2,8,128,128]{3,2,1,0:T(8,128)}, f32[2,8,128,128]{3,2,1,0:T(8,128)S(1)}, u32[]{:S(2)}, u32[]{:S(2)}) collective-permute-start(f32[2,8,128,128]{3,2,1,0:T(8,128)} %get-tuple-element.20), channel_id=1, source_target_pairs={{0,4},{4,8},{8,12},{12,0},{1,5},{5,9},{9,13},{13,1},{2,6},{6,10},{... | collective-permute-start | bytes 3145736 | tf_op jit(solution)/shard_map/ppermute | solution.py:337
  20.4 24.1 %collective-permute-start.4 = (f32[2,8,128,128]{3,2,1,0:T(8,128)}, f32[2,8,128,128]{3,2,1,0:T(8,128)S(1)}, u32[]{:S(2)}, u32[]{:S(2)}) collective-permute-start(f32[2,8,128,128]{3,2,1,0:T(8,128)} %get-tuple-element.21), channel_id=1, source_target_pairs={{0,12},{4,0},{8,4},{12,8},{1,13},{5,1},{9,5},{13,9},{2,14},{6,2},{... | collective-permute-start | bytes 3145736 | tf_op jit(solution)/shard_map/ppermute | solution.py:337
  21.9 46.0 %collective-permute-start.5 = (f32[2,8,128,128]{3,2,1,0:T(8,128)}, f32[2,8,128,128]{3,2,1,0:T(8,128)S(1)}, u32[]{:S(2)}, u32[]{:S(2)}) collective-permute-start(f32[2,8,128,128]{3,2,1,0:T(8,128)} %get-tuple-element.22), channel_id=1, source_target_pairs={{0,8},{4,12},{8,0},{12,4},{1,9},{5,13},{9,1},{13,5},{2,10},{6,14},... | collective-permute-start | bytes 3145736 | tf_op jit(solution)/shard_map/ppermute | solution.py:337
  44.5 1.2 copy-start.6
  69.7 1.3 copy-start.3
  71.0 5.3 %copy-start.7 = (s32[1024,1]{0,1:T(1,128)S(1)}, s32[1024,1]{0,1:T(1,128)}, u32[]{:S(2)}) copy-start(s32[1024,1]{0,1:T(1,128)} %param.8) | copy-start | bytes 12292
  71.0 5.7 %copy-start = (bf16[2,4,256,512]{3,2,1,0:T(8,128)(2,1)S(1)}, bf16[2,4,256,512]{3,2,1,0:T(8,128)(2,1)}, u32[]{:S(2)}) copy-start(bf16[2,4,256,512]{3,2,1,0:T(8,128)(2,1)} %constant.23.clone.table_ref.table_z_ref) | copy-start | bytes 6291460
  71.0 27.0 %all-to-all-start.1 = ((f32[4,2,2,256,128]{4,3,2,1,0:T(8,128)}), f32[4,2,2,256,128]{4,3,2,1,0:T(8,128)}, u32[]{:S(2)}, u32[]{:S(2)}) async-start(f32[4,2,2,256,128]{4,3,2,1,0:T(8,128)} %copy-done.3), calls=%async_computation.1 | async-start | bytes 4194304 | tf_op jit(solution)/shard_map/all_to_all | solution.py:359
  76.7 3.3 %copy-start.8 = (s32[128,9]{0,1:T(8,128)}, s32[128,9]{0,1:T(8,128)S(1)}, u32[]{:S(2)}) copy-start(s32[128,9]{0,1:T(8,128)S(1)} %reduce-window.9) | copy-start | bytes 13828
  80.0 9.7 %collective-permute-start = (f32[2,2,128,256]{3,2,1,0:T(8,128)S(1)}, f32[2,2,128,256]{3,2,1,0:T(8,128)S(1)}, u32[]{:S(2)}, u32[]{:S(2)}) collective-permute-start(f32[2,2,128,256]{3,2,1,0:T(8,128)S(1)} %get-tuple-element.16), channel_id=1, source_target_pairs={{0,4},{4,8},{8,12},{12,0},{1,5},{5,9},{9,13},{13,1},{2,6},{6,10},{... | collective-permute-start | bytes 1572872 | tf_op jit(solution)/shard_map/ppermute | solution.py:337
  80.6 6.2 %slice-start = ((s32[128,9]{0,1:T(8,128)}), s32[128,8]{0,1:T(8,128)S(1)}, s32[]{:S(2)}) async-start(s32[128,9]{0,1:T(8,128)} %copy-done.8), calls=%async_computation.4 | async-start | bytes 8192 | tf_op jit(solution)/shard_map/slice.1
  80.6 9.1 %collective-permute-start.1 = (f32[2,2,128,256]{3,2,1,0:T(8,128)S(1)}, f32[2,2,128,256]{3,2,1,0:T(8,128)S(1)}, u32[]{:S(2)}, u32[]{:S(2)}) collective-permute-start(f32[2,2,128,256]{3,2,1,0:T(8,128)S(1)} %get-tuple-element.17), channel_id=1, source_target_pairs={{0,12},{4,0},{8,4},{12,8},{1,13},{5,1},{9,5},{13,9},{2,14},{6,2},{... | collective-permute-start | bytes 1572872 | tf_op jit(solution)/shard_map/ppermute | solution.py:337
  86.8 2.9 %copy-start.2 = (bf16[2,4,512,256]{3,2,1,0:T(8,128)(2,1)S(1)}, bf16[2,4,512,256]{3,2,1,0:T(8,128)(2,1)}, u32[]{:S(2)}) copy-start(bf16[2,4,512,256]{3,2,1,0:T(8,128)(2,1)} %constant.22.clone.table_ref) | copy-start | bytes 6291460
  86.8 15.8 %collective-permute-start.2 = (f32[2,2,128,256]{3,2,1,0:T(8,128)}, f32[2,2,128,256]{3,2,1,0:T(8,128)}, u32[]{:S(2)}, u32[]{:S(2)}) collective-permute-start(f32[2,2,128,256]{3,2,1,0:T(8,128)} %get-tuple-element.18), channel_id=1, source_target_pairs={{0,8},{4,12},{8,0},{12,4},{1,9},{5,13},{9,1},{13,5},{2,10},{6,14},... | collective-permute-start | bytes 1572872 | tf_op jit(solution)/shard_map/ppermute | solution.py:337
  102.6 1.6 copy-start.4
  108.6 44.6 %copy-start.5 = (bf16[2,512,1024]{2,1,0:T(8,128)(2,1)S(1)}, bf16[2,512,1024]{2,1,0:T(8,128)(2,1)}, u32[]{:S(2)}) copy-start(bf16[2,512,1024]{2,1,0:T(8,128)(2,1)} %constant.21.clone.table_ref) | copy-start | bytes 6291460

commit v5 on v4

--- a/solution.py
+++ b/solution.py
@@ -75,41 +75,6 @@
     return pl.CostEstimate(flops=6 * multiplies, bytes_accessed=moved, transcendentals=0)
 
 
-def scale_kernel(rotated, place_ref, normals_ref, spectrum_ref, *out_refs):
-    for shift, out_ref in enumerate(out_refs if rotated else range(4)):
-        chunk = lax.rem(place_ref[0] + shift, 4) if rotated else shift
-        values = normals_ref[:, chunk].astype(jnp.float32) * spectrum_ref[chunk][None]
-        if rotated:
-            out_ref[...] = values
-        else:
-            out_refs[0][shift] = values
-
-
-def scale(half, rotated, place, normals, spectrum):
-    if rotated:
-        out_specs = [pl.BlockSpec((2, 1, 128, 128), lambda i, place: (0, i, 0, 0))] * 4
-        out_shape = [jax.ShapeDtypeStruct((2, 8, 128, 128), jnp.float32)] * 4
-    else:
-        out_specs = pl.BlockSpec((4, 2, 1, 128, 128), lambda i, place: (0, 0, i, 0, 0))
-        out_shape = jax.ShapeDtypeStruct((4, 2, 8, 128, 128), jnp.float32)
-    return pl.pallas_call(
-        functools.partial(scale_kernel, rotated),
-        grid_spec=pltpu.PrefetchScalarGridSpec(
-            num_scalar_prefetch=1,
-            grid=(8,),
-            in_specs=[
-                pl.BlockSpec((2, 4, 1, 128, 128), lambda i, place: (0, half, i, 0, 0)),
-                pl.BlockSpec((4, 1, 128, 128), lambda i, place: (half, i, 0, 0)),
-            ],
-            out_specs=out_specs,
-        ),
-        out_shape=out_shape,
-        compiler_params=params(60),
-        cost_estimate=cost(1 << 20, 8 * MIB),
-        name="scale_b" if rotated else "scale_a",
-    )(place, normals.reshape(2, 8, 8, 128, 128), spectrum.reshape(8, 8, 128, 128))
-
-
 def rows_z(piece):
     return halves(jnp.concatenate([piece[plane].reshape(-1, 128) for plane in range(2)], axis=1))
 
@@ -180,7 +145,7 @@
             ],
             out_specs=pl.BlockSpec((1, 2, 2, KEPT, 128), lambda i, place: (i, 0, 0, 0, 0)),
         ),
-        out_shape=jax.ShapeDtypeStruct((4, 2, 2, KEPT, 128), jnp.float32),
+        out_shape=pltpu.HBM((4, 2, 2, KEPT, 128), jnp.float32),
         compiler_params=params(VMEM),
         cost_estimate=cost(1024 * 256 * 512, 6 * MIB),
         name="first_y",
@@ -226,23 +191,40 @@
     )(to, arrived, table)
 
 
-def second_kernel(gy_ref, part_ref, last_y, table_y_ref, in_z, table_z_ref, out_ref, held):
+def second_z_kernel(in_ref, table_ref, out_ref):
+    total = None
+    for g in range(4):
+        term = product(rows_z(in_ref[g]), (table_ref[0, g], table_ref[1, g]))
+        total = term if total is None else total + term
+    out_ref[0] = total
+
+
+def second_z(arrived, table):
+    return pl.pallas_call(
+        second_z_kernel,
+        grid=(2,),
+        in_specs=[
+            pl.BlockSpec((4, 2, 1, KEPT, 128), lambda i: (0, 0, i, 0, 0)),
+            pl.BlockSpec((2, 4, 256, 512), lambda i: (0, 0, 0, 0)),
+        ],
+        out_specs=pl.BlockSpec((1, KEPT, 512), lambda i: (i, 0, 0)),
+        out_shape=jax.ShapeDtypeStruct((2, KEPT, 512), jnp.float32),
+        compiler_params=params(VMEM),
+        cost_estimate=cost(512 * 1024 * 512, 5 * MIB),
+        name="second_z",
+    )(arrived, table)
+
+
+def second_kernel(gy_ref, part_ref, last_y, table_y_ref, in_z, out_ref, held):
     def put(values, row):
         for half in range(2):
             held[pl.ds(half * 8 + row, 128, stride=16), :] = values[
                 :, half * 128 : (half + 1) * 128
             ]
 
-    total = None
-    for g in range(4):
-        term = product(rows_z(in_z[g]), (table_z_ref[0, g], table_z_ref[1, g]))
-        total = term if total is None else total + term
     for x in range(2):
         for plane in range(2):
-            put(
-                total[x * 128 : (x + 1) * 128, plane * KEPT : (plane + 1) * KEPT],
-                plane * 4 + 2 + x,
-            )
+            put(in_z[x, :, plane * KEPT : (plane + 1) * KEPT], plane * 4 + 2 + x)
     table = tuple(table_y_ref[i, 0].reshape(256, 256) for i in range(2))
     for x in range(2):
         total = part_ref[x].reshape(256, KEPT) + product(table, columns_y(last_y[:, x : x + 1]))
@@ -251,7 +233,7 @@
     out_ref[...] = held[...].reshape(128, 1, 2, 8, 128)
 
 
-def second(gy, part, last_y, table_y, arrived, table_z):
+def second(gy, part, last_y, table_y, done_z):
     return pl.pallas_call(
         second_kernel,
         grid_spec=pltpu.PrefetchScalarGridSpec(
@@ -263,24 +245,16 @@
                 pl.BlockSpec(
                     (2, 1, 2, 128, 256), lambda i, gy: (0, lax.rem(gy[0] + 2, 4), 0, i, 0)
                 ),
-                pl.BlockSpec((4, 2, 2, 128, 128), lambda i, gy: (0, 0, 0, i, 0)),
-                pl.BlockSpec((2, 4, 256, 512), lambda i, gy: (0, 0, 0, 0)),
+                pl.BlockSpec((2, 128, 512), lambda i, gy: (0, i, 0)),
             ],
             out_specs=pl.BlockSpec((128, 1, 2, 8, 128), lambda i, gy: (0, i, 0, 0, 0)),
             scratch_shapes=[pltpu.VMEM((2048, 128), jnp.float32)],
         ),
-        out_shape=jax.ShapeDtypeStruct((128, 2, 2, 8, 128), jnp.float32),
-        compiler_params=params(VMEM),
-        cost_estimate=cost(640 * 1024 * 512, 8 * MIB),
+        out_shape=pltpu.HBM((128, 2, 2, 8, 128), jnp.float32),
+        compiler_params=params(VMEM),
+        cost_estimate=cost(128 * 1024 * 512, 8 * MIB),
         name="second",
-    )(
-        gy,
-        part.reshape(2, 2, KEPT, KEPT),
-        last_y,
-        table_y.reshape(2, 4, 2, KEPT, 256),
-        arrived,
-        table_z,
-    )
+    )(gy, part.reshape(2, 2, KEPT, KEPT), last_y, table_y.reshape(2, 4, 2, KEPT, 256), done_z)
 
 
 def third_kernel(slot_ref, in_ref, table_ref, out_ref, held):
@@ -325,7 +299,7 @@
             out_specs=pl.BlockSpec((4096, 128), lambda i, slots: (0, 0)),
             scratch_shapes=[pltpu.VMEM((2, 2, KEPT, 128), jnp.float32)],
         ),
-        out_shape=jax.ShapeDtypeStruct((4096, 128), jnp.float32),
+        out_shape=pltpu.HBM((4096, 128), jnp.float32),
         compiler_params=params(VMEM),
         cost_estimate=cost(512 * 1024 * 512, 6 * MIB),
         name="third",
@@ -349,10 +323,21 @@
     gy = lax.axis_index("gy").astype(jnp.int32).reshape(1)
     gz = lax.axis_index("gz").astype(jnp.int32).reshape(1)
 
-    a = scale(0, False, gz, normals, spectrum)
+    def chunk_b(shift):
+        start = 32 + 8 * lax.rem(gy[0] + shift, 4)
+        return lax.dynamic_slice_in_dim(spectrum, start, 8, 0)[None] * lax.dynamic_slice_in_dim(
+            normals, start, 8, 1
+        ).astype(jnp.float32)
+
+    b1, b3 = chunk_b(1), chunk_b(3)
+    b1, b3, normals, spectrum = lax.optimization_barrier((b1, b3, normals, spectrum))
+    b1, b3 = shifted(b1, "gy", 1), shifted(b3, "gy", 3)
+    a = spectrum[:32].reshape(4, 1, 8, 128, 128) * normals[:, :32].astype(jnp.float32).reshape(
+        2, 4, 8, 128, 128
+    ).transpose(1, 0, 2, 3, 4)
+    a, normals, spectrum = lax.optimization_barrier((a, normals, spectrum))
     a = lax.all_to_all(a, "gz", split_axis=0, concat_axis=0, tiled=True)
-    b0, b1, b2, b3 = scale(1, True, gy, normals, spectrum)
-    b1, b3, b2 = shifted(b1, "gy", 1), shifted(b3, "gy", 3), shifted(b2, "gy", 2)
+    b2, b0 = shifted(chunk_b(2), "gy", 2), chunk_b(0)
 
     part_b = part_y(gy, (b0, b1, b3), 2, table_y)
     b = first_y(gy, part_b, b2, table_y)
@@ -362,7 +347,9 @@
     a1, a3, a2 = shifted(a1, "gy", 1), shifted(a3, "gy", 3), shifted(a2, "gy", 2)
 
     part_a = part_y(gy, (a0, a1, a3), 1, table_y)
-    planes = second(gy, part_a, a2, table_y, b, table_z)
+    done_b = second_z(b, table_z)
+    done_b, part_a, a2 = lax.optimization_barrier((done_b, part_a, a2))
+    planes = second(gy, part_a, a2, table_y, done_b)
     planes, slots = lax.optimization_barrier((planes, slots_of(block_owner)))
     lines = lax.all_to_all(planes, ALL, split_axis=0, concat_axis=0, tiled=True)
     outgoing = third(slots, lines, table_x)

time: 194 us -> 191 us (0.985)
  Pallas kernels: 36.5 us -> 28.8 us
  other arithmetic: 0.63 us -> 7.33 us
  waiting for transfers between devices: 53.2 us -> 48.4 us
  local copies, waits for them, and re-layouts: 5.68 us -> 8.22 us
    pallas_call x2 -> x1, Pallas kernels: 13.2 us -> 3.35 us  [second_z(): pl.pallas_call(second_z_kernel, grid=(2,), in_specs=[pl.BlockSpec((4, 2,...]
    ppermute x6, waiting for transfers between devices: 46.7 us -> 39 us  [shifted(): lax.ppermute(piece, axis, [(i, (i + shift) % size) for i in range(size)])]
    mul x0 -> x3, other arithmetic: none -> 6.7 us  [the longest x2 4.01 us: chunk_b(): lax.dynamic_slice_in_dim(spectrum, start, 8, 0)[None]]
    all_to_all x1, waiting for transfers between devices: 6.49 us -> 9.46 us  [per_device(): b = lax.all_to_all(b, 'gz', split_axis=0, concat_axis=0, tiled=True)]
    dynamic_slice x0 -> x2, local copies, waits for them, and re-layouts: none -> 2.56 us  [chunk_b(): lax.dynamic_slice_in_dim(spectrum, start, 8, 0)[None]]
    unnamed x19 -> x17, local copies, waits for them, and re-layouts: 5.47 us -> 3.22 us
    slice x0 -> x4, local copies, waits for them, and re-layouts: none -> 2.22 us  [the longest x2 1.59 us: per_device(): spectrum[:32].reshape(4, 1, 8, 128, 128)]
  transfers between devices with their start and end apart: 8 -> 8, of which waited for: 5 -> 4; matrix products, arithmetic and copies ran while one was open for 0% -> 2% of each run, Pallas kernels for 11% -> 10%
where the time goes in v5:
time: 191 us; the launch traced here: 190 us
  blocking collectives  78.7 us (41%)
  waiting for transfers between devices  48.4 us (25%)
  Pallas kernels  28.8 us (15%)
  starting transfers between devices  18.3 us (10%)
  local copies, waits for them, and re-layouts  8.22 us (4%)
  other arithmetic  7.33 us (4%)
    all_to_all x1, blocking collectives, per_device(): lines = lax.all_to_all(planes, ALL, split_axis=0, concat_axis=0, tiled=True)  44.1 us
    ppermute x6, waiting for transfers between devices, shifted(): lax.ppermute(piece, axis, [(i, (i + shift) % size) for i in range(size)])  39 us
    all_to_all x1, blocking collectives, per_device(): lax.all_to_all(outgoing.reshape(128, 1, CAP, 2, BW), ALL, split_axis=0, c...  34.6 us
    all_to_all x1, waiting for transfers between devices, per_device(): b = lax.all_to_all(b, 'gz', split_axis=0, concat_axis=0, tiled=True)  9.46 us
    pallas_call x2, Pallas kernels, first_z(): pl.pallas_call(first_z_kernel, grid_spec=pltpu.PrefetchScalarGridSpec(num...  8.3 us
    ppermute x6, starting transfers between devices, shifted(): lax.ppermute(piece, axis, [(i, (i + shift) % size) for i in range(size)])  7.14 us
    all_to_all x1, starting transfers between devices, per_device(): a = lax.all_to_all(a, 'gz', split_axis=0, concat_axis=0, tiled=True)  5.86 us
    pallas_call x1, Pallas kernels, third(): pl.pallas_call(third_kernel, grid_spec=pltpu.PrefetchScalarGridSpec(num_s...  5.84 us
  transfers between devices with their start and end apart: 8, of which 4 were waited for; matrix products, arithmetic and copies ran while one was open for 2% of the time, Pallas kernels for 10%

profile of v5, /device:TPU:1, one launch (start us, length us, event | category | flops | bytes accessed | tf_op | source)
XLA Modules:
  0.0 189.9 jit_solution(10749533719045652004)
XLA Ops:
  0.0 1.3 constant_dynamic-slice_fusion.2
  1.3 2.4 %convert_multiply_fusion.2 = (f32[2,8,128,128]{3,2,1,0:T(8,128)S(1)}, f32[2,8,128,128]{3,2,1,0:T(8,128)}) fusion(bf16[2,64,128,128]{3,2,1,0:T(8,128)(2,1)} %param.6, s32[]{:T(128)S(6)} %select_n.17, f32[8,128,128]{2,1,0:T(8,128)S(1)} %get-tuple-element.43, s32[]{:T(128)S(6)} %select_n.16, f32[8,128,128]{2,1,0:T(8,128)S(1)} %get-tuple-element.44), kind=kLoop, calls=%fused_computation.4 | loop fusion | flops 1048576 | bytes 4194312 | tf_op jit(solution)/shard_map/mul | solution.py:328
  3.7 1.6 slice-done
  5.3 0.6 slice-done.1
  5.9 2.7 %fusion = f32[4,2,8,128,128]{4,3,2,1,0:T(8,128)} fusion(f32[4,8,128,128]{3,2,1,0:T(8,128)S(1)} %bitcast.26, bf16[2,4,8,128,128]{4,3,2,1,0:T(8,128)(2,1)S(1)} %bitcast.27), kind=kLoop, calls=%fused_computation.1 | loop fusion | flops 2097152 | bytes 8388608 | tf_op jit(solution)/shard_map/mul | solution.py:335
  8.6 5.9 %all-to-all-start.1 = ((f32[4,2,8,128,128]{4,3,2,1,0:T(8,128)}), f32[4,2,8,128,128]{4,3,2,1,0:T(8,128)}, u32[]{:S(2)}, u32[]{:S(2)}) async-start(f32[4,2,8,128,128]{4,3,2,1,0:T(8,128)} %fusion), calls=%async_computation.1 | async-start | bytes 8388608 | tf_op jit(solution)/shard_map/all_to_all | solution.py:339
  14.5 1.3 collective-permute-start
  15.8 1.4 collective-permute-start.1
  17.2 1.3 constant_dynamic-slice_fusion
  18.5 0.0 copy-start.1
  18.5 1.6 convert_multiply_fusion
  20.1 1.7 collective-permute-start.2
  21.8 18.0 %collective-permute-done.p1 = f32[2,8,128,128]{3,2,1,0:T(8,128)S(1)} collective-permute-done((f32[2,8,128,128]{3,2,1,0:T(8,128)}, f32[2,8,128,128]{3,2,1,0:T(8,128)S(1)}, u32[]{:S(2)}, u32[]{:S(2)}) %collective-permute-start) | collective-permute-done | bytes 1048608 | tf_op jit(solution)/shard_map/ppermute | solution.py:311
  39.9 0.0 collective-permute-done.1.p3
  39.9 0.0 copy-done.1
  39.9 3.5 %part_y.2.part_ref = f32[4,512,256]{2,1,0:T(8,128)S(1)} custom-call(s32[1]{0:T(128)} %bitcast.place_ref.to_ref.gy_ref, f32[2,8,128,128]{3,2,1,0:T(8,128)S(1)} %get-tuple-element.38.p0, f32[2,8,128,128]{3,2,1,0:T(8,128)S(1)} %collective-permute-done.p1, f32[2,8,128,128]{3,2,1,0:T(8,128)S(1)} %collective-permute-done.1.p3, bf16[2,4,512,256]{3,2,1,0:T(8,128)(2,1)S(1)} %copy-done.1), custom_call_target="tpu_custom_call" | custom-call | flops 2415919104 | bytes 8388608 | tf_op jit(solution)/shard_map/part_y/pallas_call | solution.py:104
  43.3 20.1 %collective-permute-done.2.p2 = f32[2,8,128,128]{3,2,1,0:T(8,128)S(1)} collective-permute-done((f32[2,8,128,128]{3,2,1,0:T(8,128)S(1)}, f32[2,8,128,128]{3,2,1,0:T(8,128)S(1)}, u32[]{:S(2)}, u32[]{:S(2)}) %collective-permute-start.2) | collective-permute-done | bytes 1048608 | tf_op jit(solution)/shard_map/ppermute | solution.py:311
  63.4 2.8 %first_y.1 = f32[4,2,2,256,128]{4,3,2,1,0:T(8,128)} custom-call(s32[1]{0:T(128)} %bitcast.place_ref.to_ref.gy_ref, f32[4,512,256]{2,1,0:T(8,128)S(1)} %part_y.2.part_ref, f32[2,8,128,128]{3,2,1,0:T(8,128)S(1)} %collective-permute-done.2.p2, bf16[2,4,512,256]{3,2,1,0:T(8,128)(2,1)S(1)} %copy-done.1), custom_call_target="tpu_custom_call" | custom-call | flops 805306368 | bytes 6291456 | tf_op jit(solution)/shard_map/first_y/pallas_call | solution.py:134
  66.3 0.0 all-to-all-done.1.in_ref
  66.3 5.3 %all-to-all-start = ((f32[4,2,2,256,128]{4,3,2,1,0:T(8,128)}), f32[4,2,2,256,128]{4,3,2,1,0:T(8,128)}, u32[]{:S(2)}, u32[]{:S(2)}) async-start(f32[4,2,2,256,128]{4,3,2,1,0:T(8,128)} %first_y.1), calls=%async_computation | async-start | bytes 4194304 | tf_op jit(solution)/shard_map/all_to_all | solution.py:344
  71.6 0.0 copy-done.7
  71.6 0.1 copy.12
  71.7 0.2 fusion.3
  72.0 0.1 copy.13
  72.1 1.1 copy-done
  73.2 4.2 %first_z.3 = (f32[2,2,128,256]{3,2,1,0:T(8,128)}, f32[2,2,128,256]{3,2,1,0:T(8,128)}) custom-call(s32[1]{0:T(128)} %bitcast.place_ref.to_ref.gy_ref, f32[4,2,8,128,128]{4,3,2,1,0:T(8,128)} %all-to-all-done.1.in_ref, bf16[2,4,256,512]{3,2,1,0:T(8,128)(2,1)S(1)} %copy-done), custom_call_target="tpu_custom_call" | custom-call | flops 1610612736 | bytes 4194304 | tf_op jit(solution)/shard_map/first_z/pallas_call | solution.py:176
  77.4 0.3 collective-permute-start.3
  77.7 2.3 %collective-permute-start.4 = (f32[2,2,128,256]{3,2,1,0:T(8,128)}, f32[2,2,128,256]{3,2,1,0:T(8,128)S(1)}, u32[]{:S(2)}, u32[]{:S(2)}) collective-permute-start(f32[2,2,128,256]{3,2,1,0:T(8,128)} %get-tuple-element.30), channel_id=1, source_target_pairs={{0,12},{4,0},{8,4},{12,8},{1,13},{5,1},{9,5},{13,9},{2,14},{6,2},{... | collective-permute-start | bytes 1572872 | tf_op jit(solution)/shard_map/ppermute | solution.py:311
  80.1 4.1 %first_z.2 = (f32[2,2,128,256]{3,2,1,0:T(8,128)}, f32[2,2,128,256]{3,2,1,0:T(8,128)S(1)}) custom-call(s32[1]{0:T(128)} %bitcast.place_ref.to_ref.gy_ref, f32[4,2,8,128,128]{4,3,2,1,0:T(8,128)} %all-to-all-done.1.in_ref, bf16[2,4,256,512]{3,2,1,0:T(8,128)(2,1)S(1)} %copy-done), custom_call_target="tpu_custom_call" | custom-call | flops 1610612736 | bytes 4194304 | tf_op jit(solution)/shard_map/first_z/pallas_call | solution.py:176
  84.1 0.8 copy-done.5
  84.9 0.0 collective-permute-start.5
  84.9 0.4 fusion.2
  85.3 9.5 %all-to-all-done.in_ref = f32[4,2,2,256,128]{4,3,2,1,0:T(8,128)} async-done(((f32[4,2,2,256,128]{4,3,2,1,0:T(8,128)}), f32[4,2,2,256,128]{4,3,2,1,0:T(8,128)}, u32[]{:S(2)}, u32[]{:S(2)}) %all-to-all-start) | async-done | bytes 2097184 | tf_op jit(solution)/shard_map/all_to_all | solution.py:344
  94.8 3.4 %second_z.1.in_z = f32[2,256,512]{2,1,0:T(8,128)S(1)} custom-call(f32[4,2,2,256,128]{4,3,2,1,0:T(8,128)} %all-to-all-done.in_ref, bf16[2,4,256,512]{3,2,1,0:T(8,128)(2,1)S(1)} %copy-done), custom_call_target="tpu_custom_call" | custom-call | flops 1610612736 | bytes 5242880 | tf_op jit(solution)/shard_map/second_z/pallas_call | solution.py:203
  98.1 0.0 collective-permute-done.3.p1
  98.1 0.0 collective-permute-done.4.p3
  98.2 0.0 copy-done.2
  98.2 0.0 copy-done.6
  98.2 0.0 copy-start.3
  98.2 1.8 part_y.3
  99.9 0.8 collective-permute-done.5.last_y
  100.8 0.0 copy-done.3
  100.8 3.3 %second.1 = f32[128,2,2,8,128]{4,3,2,1,0:T(8,128)} custom-call(s32[1]{0:T(128)} %bitcast.place_ref.to_ref.gy_ref, f32[2,2,256,256]{3,2,1,0:T(8,128)S(1)} %bitcast.23, f32[2,2,128,256]{3,2,1,0:T(8,128)} %collective-permute-done.5.last_y, bf16[2,4,2,256,256]{4,3,2,1,0:T(8,128)(2,1)S(1)} %copy-done.3, f32[2,256,512]{2,1,0:T(8,128)S(1)} %second_z.1.in_z), custom_call_target="tpu_custom_call" | custom-call | flops 402653184 | bytes 8388608 | tf_op jit(solution)/shard_map/second/pallas_call | solution.py:237
  104.0 44.1 %all_to_all.27.in_ref = f32[128,2,2,8,128]{4,3,2,1,0:T(8,128)S(1)} all-to-all(f32[128,2,2,8,128]{4,3,2,1,0:T(8,128)} %second.1), channel_id=1, replica_groups=mesh['gx'=8,'gy'=4,'gz'=4] {'gx','gy','gz'}, dimensions={0} | all-to-all | bytes 4194304 | tf_op jit(solution)/shard_map/all_to_all | solution.py:354
  148.2 0.0 copy-done.4
  148.2 5.8 %third.1 = f32[4096,128]{1,0:T(8,128)} custom-call(s32[1024]{0:T(1024)S(1)} %multiply_add_fusion.slot_ref, f32[128,2,2,8,128]{4,3,2,1,0:T(8,128)S(1)} %all_to_all.27.in_ref, bf16[2,512,1024]{2,1,0:T(8,128)(2,1)S(1)} %copy-done.4), custom_call_target="tpu_custom_call" | custom-call | flops 1610612736 | bytes 6291456 | tf_op jit(solution)/shard_map/third/pallas_call | solution.py:290
  154.0 34.6 %all_to_all.28 = f32[128,1,16,2,128]{4,3,2,1,0:T(2,128)S(1)} all-to-all(f32[128,1,16,2,128]{4,3,2,1,0:T(2,128)} %bitcast.25), channel_id=1, replica_groups=mesh['gx'=8,'gy'=4,'gz'=4] {'gx','gy','gz'}, dimensions={0} | all-to-all | bytes 4194304 | tf_op jit(solution)/shard_map/all_to_all | solution.py:356
  188.6 1.3 copy.19
  (13 shorter events, 0.1 us)
Async XLA Ops:
  3.7 1.6 slice-start
  3.7 2.2 %slice-start.1 = ((bf16[2,64,128,128]{3,2,1,0:T(8,128)(2,1)}), bf16[2,32,128,128]{3,2,1,0:T(8,128)(2,1)S(1)}, s32[]{:S(2)}) async-start(bf16[2,64,128,128]{3,2,1,0:T(8,128)(2,1)} %param.6), calls=%async_computation.5 | async-start | bytes 4194304 | tf_op jit(solution)/shard_map/slice | solution.py:335
  8.6 57.7 %all-to-all-start.1 = ((f32[4,2,8,128,128]{4,3,2,1,0:T(8,128)}), f32[4,2,8,128,128]{4,3,2,1,0:T(8,128)}, u32[]{:S(2)}, u32[]{:S(2)}) async-start(f32[4,2,8,128,128]{4,3,2,1,0:T(8,128)} %fusion), calls=%async_computation.1 | async-start | bytes 8388608 | tf_op jit(solution)/shard_map/all_to_all | solution.py:339
  14.5 25.4 %collective-permute-start = (f32[2,8,128,128]{3,2,1,0:T(8,128)}, f32[2,8,128,128]{3,2,1,0:T(8,128)S(1)}, u32[]{:S(2)}, u32[]{:S(2)}) collective-permute-start(f32[2,8,128,128]{3,2,1,0:T(8,128)} %get-tuple-element.25), channel_id=1, source_target_pairs={{0,4},{4,8},{8,12},{12,0},{1,5},{5,9},{9,13},{13,1},{2,6},{6,10},{... | collective-permute-start | bytes 3145736 | tf_op jit(solution)/shard_map/ppermute | solution.py:311
  15.8 24.1 %collective-permute-start.1 = (f32[2,8,128,128]{3,2,1,0:T(8,128)S(1)}, f32[2,8,128,128]{3,2,1,0:T(8,128)S(1)}, u32[]{:S(2)}, u32[]{:S(2)}) collective-permute-start(f32[2,8,128,128]{3,2,1,0:T(8,128)S(1)} %get-tuple-element.26), channel_id=1, source_target_pairs={{0,12},{4,0},{8,4},{12,8},{1,13},{5,1},{9,5},{13,9},{2,14},{6,2},{... | collective-permute-start | bytes 3145736 | tf_op jit(solution)/shard_map/ppermute | solution.py:311
  18.5 21.3 %copy-start.1 = (bf16[2,4,512,256]{3,2,1,0:T(8,128)(2,1)S(1)}, bf16[2,4,512,256]{3,2,1,0:T(8,128)(2,1)}, u32[]{:S(2)}) copy-start(bf16[2,4,512,256]{3,2,1,0:T(8,128)(2,1)} %constant.45.clone.table_ref) | copy-start | bytes 6291460
  20.1 43.3 %collective-permute-start.2 = (f32[2,8,128,128]{3,2,1,0:T(8,128)S(1)}, f32[2,8,128,128]{3,2,1,0:T(8,128)S(1)}, u32[]{:S(2)}, u32[]{:S(2)}) collective-permute-start(f32[2,8,128,128]{3,2,1,0:T(8,128)S(1)} %get-tuple-element.37), channel_id=1, source_target_pairs={{0,8},{4,12},{8,0},{12,4},{1,9},{5,13},{9,1},{13,5},{2,10},{6,14},... | collective-permute-start | bytes 3145736 | tf_op jit(solution)/shard_map/ppermute | solution.py:311
  66.3 5.3 %copy-start.7 = (s32[1024,1]{0,1:T(1,128)S(1)}, s32[1024,1]{0,1:T(1,128)}, u32[]{:S(2)}) copy-start(s32[1024,1]{0,1:T(1,128)} %param.8) | copy-start | bytes 12292
  66.3 28.5 %all-to-all-start = ((f32[4,2,2,256,128]{4,3,2,1,0:T(8,128)}), f32[4,2,2,256,128]{4,3,2,1,0:T(8,128)}, u32[]{:S(2)}, u32[]{:S(2)}) async-start(f32[4,2,2,256,128]{4,3,2,1,0:T(8,128)} %first_y.1), calls=%async_computation | async-start | bytes 4194304 | tf_op jit(solution)/shard_map/all_to_all | solution.py:344
  71.6 1.6 copy-start
  77.4 20.7 %collective-permute-start.3 = (f32[2,2,128,256]{3,2,1,0:T(8,128)}, f32[2,2,128,256]{3,2,1,0:T(8,128)S(1)}, u32[]{:S(2)}, u32[]{:S(2)}) collective-permute-start(f32[2,2,128,256]{3,2,1,0:T(8,128)} %get-tuple-element.29), channel_id=1, source_target_pairs={{0,4},{4,8},{8,12},{12,0},{1,5},{5,9},{9,13},{13,1},{2,6},{6,10},{... | collective-permute-start | bytes 1572872 | tf_op jit(solution)/shard_map/ppermute | solution.py:311
  77.7 20.4 %collective-permute-start.4 = (f32[2,2,128,256]{3,2,1,0:T(8,128)}, f32[2,2,128,256]{3,2,1,0:T(8,128)S(1)}, u32[]{:S(2)}, u32[]{:S(2)}) collective-permute-start(f32[2,2,128,256]{3,2,1,0:T(8,128)} %get-tuple-element.30), channel_id=1, source_target_pairs={{0,12},{4,0},{8,4},{12,8},{1,13},{5,1},{9,5},{13,9},{2,14},{6,2},{... | collective-permute-start | bytes 1572872 | tf_op jit(solution)/shard_map/ppermute | solution.py:311
  84.1 0.8 copy-start.5
  84.9 15.8 %collective-permute-start.5 = (f32[2,2,128,256]{3,2,1,0:T(8,128)}, f32[2,2,128,256]{3,2,1,0:T(8,128)}, u32[]{:S(2)}, u32[]{:S(2)}) collective-permute-start(f32[2,2,128,256]{3,2,1,0:T(8,128)} %get-tuple-element.31), channel_id=1, source_target_pairs={{0,8},{4,12},{8,0},{12,4},{1,9},{5,13},{9,1},{13,5},{2,10},{6,14},... | collective-permute-start | bytes 1572872 | tf_op jit(solution)/shard_map/ppermute | solution.py:311
  94.8 3.4 %copy-start.2 = (bf16[2,4,512,256]{3,2,1,0:T(8,128)(2,1)S(1)}, bf16[2,4,512,256]{3,2,1,0:T(8,128)(2,1)}, u32[]{:S(2)}) copy-start(bf16[2,4,512,256]{3,2,1,0:T(8,128)(2,1)} %constant.45.clone.table_ref) | copy-start | bytes 6291460
  94.8 3.4 %copy-start.6 = (f32[2,2,128,256]{3,2,1,0:T(8,128)S(1)}, f32[2,2,128,256]{3,2,1,0:T(8,128)}, u32[]{:S(2)}) copy-start(f32[2,2,128,256]{3,2,1,0:T(8,128)} %copy-done.5) | copy-start | bytes 1572868
  98.2 2.6 %copy-start.3 = (bf16[2,4,2,256,256]{4,3,2,1,0:T(8,128)(2,1)S(1)}, bf16[2,4,2,256,256]{4,3,2,1,0:T(8,128)(2,1)}, u32[]{:S(2)}) copy-start(bf16[2,4,2,256,256]{4,3,2,1,0:T(8,128)(2,1)} %constant.47.table_y_ref) | copy-start | bytes 6291460
  104.0 44.1 %copy-start.4 = (bf16[2,512,1024]{2,1,0:T(8,128)(2,1)S(1)}, bf16[2,512,1024]{2,1,0:T(8,128)(2,1)}, u32[]{:S(2)}) copy-start(bf16[2,512,1024]{2,1,0:T(8,128)(2,1)} %constant.44.clone.table_ref) | copy-start | bytes 6291460

commit v6 on v5

v6 whole, which is shorter than its diff:
```python
import functools

import jax
import jax.numpy as jnp
import ml_dtypes
import numpy as np
from jax import lax
from jax.experimental import pallas as pl
from jax.experimental.pallas import tpu as pltpu
from jax.sharding import PartitionSpec as P

N = 512
KEPT = 256
BW = 128
CAP = 16
ALL = ("gx", "gy", "gz")
MIB = 1 << 20
VMEM = 40


def split_table(table):
    high = table.astype(np.float32).astype(ml_dtypes.bfloat16)
    low = (table - high.astype(np.float64)).astype(np.float32).astype(ml_dtypes.bfloat16)
    return np.stack([high, low])


def cos_sin(positions, kept):
    angles = (positions[:, None] * kept[None, :] % N) * (2.0 * np.pi / N)
    return np.cos(angles), np.sin(angles)


@functools.cache
def tables():
    cosine, sine = cos_sin(np.arange(N), np.arange(KEPT))
    real_rows = np.concatenate([cosine, -sine], 1).reshape(4, 1, 128, 2 * KEPT)
    imag_rows = np.concatenate([sine, cosine], 1).reshape(4, 1, 128, 2 * KEPT)
    table_z = np.concatenate([real_rows, imag_rows], 1).reshape(4, 256, 2 * KEPT)
    order = np.arange(KEPT).reshape(KEPT // 2, 2).T.reshape(-1)
    cosine, sine = cos_sin(np.arange(N), order)
    cosine, sine = cosine.reshape(4, 128, KEPT), sine.reshape(4, 128, KEPT)
    top = np.concatenate([cosine, sine], 1)
    bottom = np.concatenate([-sine, cosine], 1)
    table_y = np.concatenate([top, bottom], 2).transpose(0, 2, 1)
    gx, gy, gz = np.meshgrid(np.arange(8), np.arange(4), np.arange(4), indexing="ij")
    first = 64 * gx + 8 * gz + 2 * gy
    second = 64 * gx + 32 + 8 * gy + 2 * gz
    cells = np.stack([first, first + 1, second, second + 1], -1).reshape(128, 4)
    cosine, sine = cos_sin(cells.reshape(-1), np.arange(KEPT))
    cosine = cosine.T.reshape(KEPT, 128, 1, 4)
    sine = sine.T.reshape(KEPT, 128, 1, 4)
    top = np.concatenate([cosine, sine], 2).reshape(KEPT, 1024)
    bottom = np.concatenate([-sine, cosine], 2).reshape(KEPT, 1024)
    table_x = np.concatenate([top, bottom], 0)
    return split_table(table_x), split_table(table_y), split_table(table_z)


def halves(values):
    high = values.astype(jnp.bfloat16)
    low = (values - high.astype(jnp.float32)).astype(jnp.bfloat16)
    return high, low


def product(left, right):
    def dot(a, b):
        return jnp.dot(a, b, preferred_element_type=jnp.float32)

    return dot(left[0], right[0]) + (dot(left[0], right[1]) + dot(left[1], right[0]))


def params(mib):
    return pltpu.CompilerParams(vmem_limit_bytes=mib * MIB)


def cost(multiplies, moved):
    return pl.CostEstimate(flops=6 * multiplies, bytes_accessed=moved, transcendentals=0)


def rows_z(piece):
    return halves(jnp.concatenate([piece[plane].reshape(-1, 128) for plane in range(2)], axis=1))


def columns_y(piece):
    planes, cells = piece.shape[:2]
    return halves(
        jnp.concatenate([piece[:, x].reshape(256, piece.shape[3]) for x in range(cells)], axis=1)
    )


def term_of(along_z, piece, table_ref, g):
    table = (table_ref[0, g], table_ref[1, g])
    if along_z:
        return product(rows_z(piece), table)
    return product(table, columns_y(piece))


def sum_kernel(along_z, place_ref, *refs):
    *pieces, table_ref, out_ref = refs
    total = None
    for shift, piece in zip((0, 1, 3), pieces):
        g = lax.rem(place_ref[0] + (4 - shift), 4)
        term = term_of(along_z, piece[...], table_ref, g)
        total = term if total is None else total + term
    out_ref[0] = total


def part_sum(along_z, place, pieces, cells, table):
    _, count, lines, columns = pieces[0].shape
    shape = (cells * lines, 512) if along_z else (512, cells * columns)
    return pl.pallas_call(
        functools.partial(sum_kernel, along_z),
        grid_spec=pltpu.PrefetchScalarGridSpec(
            num_scalar_prefetch=1,
            grid=(count // cells,),
            in_specs=[
                pl.BlockSpec((2, cells, lines, columns), lambda i, place: (0, i, 0, 0))
            ]
            * 3
            + [pl.BlockSpec(table.shape, lambda i, place: (0, 0, 0, 0))],
            out_specs=pl.BlockSpec((1,) + shape, lambda i, place: (i, 0, 0)),
        ),
        out_shape=jax.ShapeDtypeStruct((count // cells,) + shape, jnp.float32),
        compiler_params=params(VMEM),
        cost_estimate=cost(count // cells * shape[0] * shape[1] * 768, 8 * MIB),
        name="part_z" if along_z else "part_y",
    )(place, *pieces, table)


def first_y_kernel(place_ref, to_ref, part_ref, p2, table_ref, *out_refs):
    total = part_ref[0] + term_of(False, p2[...], table_ref, 0)
    for step, out_ref in enumerate(out_refs):

        @pl.when(pl.program_id(0) == step)
        def _():
            for plane in range(2):
                for x in range(2):
                    out_ref[plane, x] = total[
                        plane * KEPT : (plane + 1) * KEPT, x * 128 : (x + 1) * 128
                    ]


def first_y(shifts, place, to, part, piece, table):
    def pair(i, to):
        return lax.rem(to[0] + jnp.where(i == 0, shifts[0], shifts[1]), 4)

    shape = (2, 2, KEPT, 128)
    return pl.pallas_call(
        first_y_kernel,
        grid_spec=pltpu.PrefetchScalarGridSpec(
            num_scalar_prefetch=2,
            grid=(2,),
            in_specs=[
                pl.BlockSpec((1, 512, 256), lambda i, place, to: (pair(i, to), 0, 0)),
                pl.BlockSpec((2, 2, 128, 128), lambda i, place, to: (0, pair(i, to), 0, 0)),
                pl.BlockSpec(
                    (2, 1, 512, 256), lambda i, place, to: (0, lax.rem(place[0] + 2, 4), 0, 0)
                ),
            ],
            out_specs=[pl.BlockSpec(shape, lambda i, place, to: (0, 0, 0, 0))] * 2,
        ),
        out_shape=[jax.ShapeDtypeStruct(shape, jnp.float32)] * 2,
        compiler_params=params(VMEM),
        cost_estimate=cost(512 * 256 * 512, 4 * MIB),
        name="first_y",
    )(place, to, part, piece, table)


def first_z_kernel(in_ref, table_ref, out_ref):
    total = None
    for g in range(4):
        term = term_of(True, in_ref[g], table_ref, g)
        total = term if total is None else total + term
    for plane in range(2):
        out_ref[0, plane] = total[:, plane * KEPT : (plane + 1) * KEPT].reshape(2, 128, KEPT)


def first_z(arrived, table):
    return pl.pallas_call(
        first_z_kernel,
        grid=(4,),
        in_specs=[
            pl.BlockSpec((4, 2, 2, 128, 128), lambda i: (0, 0, i, 0, 0)),
            pl.BlockSpec((2, 4, 256, 512), lambda i: (0, 0, 0, 0)),
        ],
        out_specs=pl.BlockSpec((1, 2, 2, 128, KEPT), lambda i: (i, 0, 0, 0, 0)),
        out_shape=pltpu.HBM((4, 2, 2, 128, KEPT), jnp.float32),
        compiler_params=params(VMEM),
        cost_estimate=cost(1024 * 1024 * 512, 8 * MIB),
        name="first_z",
    )(arrived, table)


def second_y_kernel(in_ref, table_ref, out_ref):
    total = None
    for g in range(4):
        term = term_of(False, in_ref[g], table_ref, g)
        total = term if total is None else total + term
    out_ref[0] = total


def second_y(arrived, table):
    return pl.pallas_call(
        second_y_kernel,
        grid=(2,),
        in_specs=[
            pl.BlockSpec((4, 2, 1, 128, KEPT), lambda i: (0, 0, i, 0, 0)),
            pl.BlockSpec((2, 4, 512, 256), lambda i: (0, 0, 0, 0)),
        ],
        out_specs=pl.BlockSpec((1, 512, KEPT), lambda i: (i, 0, 0)),
        out_shape=jax.ShapeDtypeStruct((2, 512, KEPT), jnp.float32),
        compiler_params=params(VMEM),
        cost_estimate=cost(512 * 1024 * 512, 5 * MIB),
        name="second_y",
    )(arrived, table)


def second_kernel(gz_ref, done_y, part_ref, last_z, table_ref, out_ref, held):
    def put(values, row):
        for half in range(2):
            held[pl.ds(half * 8 + row, 128, stride=16), :] = values[
                :, half * 128 : (half + 1) * 128
            ]

    for x in range(2):
        for plane in range(2):
            put(done_y[x, plane], plane * 4 + x)
    total = part_ref[...].reshape(256, 512) + term_of(True, last_z[...], table_ref, 0)
    for x in range(2):
        for plane in range(2):
            put(
                total[x * 128 : (x + 1) * 128, plane * KEPT : (plane + 1) * KEPT],
                plane * 4 + 2 + x,
            )
    out_ref[...] = held[...].reshape(128, 1, 2, 8, 128)


def second(gz, done_y, part, last_z, table):
    return pl.pallas_call(
        second_kernel,
        grid_spec=pltpu.PrefetchScalarGridSpec(
            num_scalar_prefetch=1,
            grid=(2,),
            in_specs=[
                pl.BlockSpec((2, 2, 128, KEPT), lambda i, gz: (0, 0, i, 0)),
                pl.BlockSpec((2, 128, 512), lambda i, gz: (0, i, 0)),
                pl.BlockSpec((2, 2, 128, 128), lambda i, gz: (0, 0, i, 0)),
                pl.BlockSpec((2, 1, 256, 512), lambda i, gz: (0, lax.rem(gz[0] + 2, 4), 0, 0)),
            ],
            out_specs=pl.BlockSpec((128, 1, 2, 8, 128), lambda i, gz: (0, i, 0, 0, 0)),
            scratch_shapes=[pltpu.VMEM((2048, 128), jnp.float32)],
        ),
        out_shape=jax.ShapeDtypeStruct((128, 2, 2, 8, 128), jnp.float32),
        compiler_params=params(VMEM),
        cost_estimate=cost(128 * 1024 * 512, 8 * MIB),
        name="second",
    )(gz, done_y.reshape(2, 2, KEPT, KEPT), part, last_z, table)


def third_kernel(slot_ref, in_ref, table_ref, out_ref, held):
    parity = pl.program_id(0)

    @pl.when(parity == 0)
    def _():
        out_ref[...] = jnp.zeros_like(out_ref)

    columns = jnp.concatenate(
        [in_ref[:, 0, half].reshape(1024, 128) for half in range(2)], axis=1
    )
    values = jnp.exp(product((table_ref[0], table_ref[1]), halves(columns)))
    for plane in range(2):
        for half in range(2):
            held[plane, half] = values[
                plane * KEPT : (plane + 1) * KEPT, half * 128 : (half + 1) * 128
            ]

    def place_rows(group, carry):
        for offset in range(8):
            x = group * 8 + offset
            for half in range(2):
                slot = slot_ref[x * 4 + parity * 2 + half]
                for plane in range(2):
                    out_ref[pl.ds(slot * 2 + plane, 1), :] = held[plane, half, pl.ds(x, 1), :]
        return carry

    lax.fori_loop(0, KEPT // 8, place_rows, 0)


def third(slots, arrived, table_x):
    return pl.pallas_call(
        third_kernel,
        grid_spec=pltpu.PrefetchScalarGridSpec(
            num_scalar_prefetch=1,
            grid=(2,),
            in_specs=[
                pl.BlockSpec((128, 1, 2, 8, 128), lambda i, slots: (0, i, 0, 0, 0)),
                pl.BlockSpec((2, 512, 1024), lambda i, slots: (0, 0, 0)),
            ],
            out_specs=pl.BlockSpec((4096, 128), lambda i, slots: (0, 0)),
            scratch_shapes=[pltpu.VMEM((2, 2, KEPT, 128), jnp.float32)],
        ),
        out_shape=jax.ShapeDtypeStruct((4096, 128), jnp.float32),
        compiler_params=params(VMEM),
        cost_estimate=cost(512 * 1024 * 512, 6 * MIB),
        name="third",
    )(slots, arrived, table_x)


def shifted(piece, axis, shift):
    size = lax.axis_size(axis)
    return lax.ppermute(piece, axis, [(i, (i + shift) % size) for i in range(size)])


def slots_of(block_owner):
    destination = block_owner[:, 0]
    one_hot = (destination[:, None] == jnp.arange(128, dtype=jnp.int32)[None, :]).astype(jnp.int32)
    earlier = jnp.cumsum(one_hot, axis=0) - one_hot
    return destination * CAP + jnp.sum(earlier * one_hot, axis=1)


def per_device(normals, spectrum, block_owner):
    table_x, table_y, table_z = (jnp.asarray(table) for table in tables())
    gy = lax.axis_index("gy").astype(jnp.int32).reshape(1)
    gz = lax.axis_index("gz").astype(jnp.int32).reshape(1)

    def chunk_b(shift):
        start = 32 + 8 * lax.rem(gy[0] + shift, 4)
        return lax.dynamic_slice_in_dim(spectrum, start, 8, 0)[None] * lax.dynamic_slice_in_dim(
            normals, start, 8, 1
        ).astype(jnp.float32)

    a = spectrum[:32].reshape(4, 1, 8, 128, 128) * normals[:, :32].astype(jnp.float32).reshape(
        2, 4, 8, 128, 128
    ).transpose(1, 0, 2, 3, 4)
    a, normals, spectrum = lax.optimization_barrier((a, normals, spectrum))
    a = lax.all_to_all(a, "gz", split_axis=0, concat_axis=0, tiled=True)
    b1, b3, b2 = shifted(chunk_b(1), "gy", 1), shifted(chunk_b(3), "gy", 3), shifted(chunk_b(2), "gy", 2)
    b0 = chunk_b(0)

    part_b = part_sum(False, gy, (b0, b1, b3), 2, table_y)
    a = first_z(a, table_z)
    a, part_b, b2 = lax.optimization_barrier((a, part_b, b2))
    a = lax.all_to_all(a, "gy", split_axis=0, concat_axis=0, tiled=True)
    b1, b3 = first_y((1, 3), gy, gz, part_b, b2, table_y)
    b1, b3 = shifted(b1, "gz", 1), shifted(b3, "gz", 3)
    b2, b0 = first_y((2, 0), gy, gz, part_b, b2, table_y)
    b2 = shifted(b2, "gz", 2)

    part_b = part_sum(True, gz, (b0, b1, b3), 1, table_z)
    a = second_y(a, table_y)
    a, part_b, b2 = lax.optimization_barrier((a, part_b, b2))
    planes = second(gz, a, part_b, b2, table_z)
    planes, slots = lax.optimization_barrier((planes, slots_of(block_owner)))
    lines = lax.all_to_all(planes, ALL, split_axis=0, concat_axis=0, tiled=True)
    outgoing = third(slots, lines, table_x)
    return lax.all_to_all(
        outgoing.reshape(128, 1, CAP, 2, BW), ALL, split_axis=0, concat_axis=1, tiled=True
    )


def solution(mesh):
    placed = (P(None, "gx", "gy", "gz"), P("gx", "gy", "gz"), P(ALL, None))
    return jax.shard_map(
        per_device,
        mesh=mesh,
        in_specs=placed,
        out_specs=P(ALL, None, None, None, None),
        check_vma=False,
    )
```

time: 191 us -> 191 us (level)
  blocking collectives: 78.7 us -> 84.9 us
  local copies, waits for them, and re-layouts: 8.22 us -> 13.5 us
  Pallas kernels: 28.8 us -> 24.5 us
  waiting for transfers between devices: 48.4 us -> 44.5 us
  other arithmetic: 7.33 us -> 4.88 us
    all_to_all x1, waiting for transfers between devices: 0.01 us -> 14.4 us  [per_device(): a = lax.all_to_all(a, 'gz', split_axis=0, concat_axis=0, tiled=True)]
    all_to_all x1, waiting for transfers between devices: 9.46 us -> 0.01 us  [per_device(): a = lax.all_to_all(a, 'gy', split_axis=0, concat_axis=0, tiled=True)]
    ppermute x6, waiting for transfers between devices: 39 us -> 30.1 us  [shifted(): lax.ppermute(piece, axis, [(i, (i + shift) % size) for i in range(size)])]
    all_to_all x1, blocking collectives: 44.1 us -> 50.7 us  [per_device(): lines = lax.all_to_all(planes, ALL, split_axis=0, concat_axis=0, tiled=True)]
    unnamed x17 -> x23, local copies, waits for them, and re-layouts: 3.22 us -> 9.2 us
    mul x2 -> x1, other arithmetic: 4.01 us -> 1.69 us  [chunk_b(): lax.dynamic_slice_in_dim(spectrum, start, 8, 0)[None]]
    pallas_call x5 -> x4, Pallas kernels: 16.9 us -> 14.9 us  [the longest x1 6.47 us: first_z(): pl.pallas_call(first_z_kernel, grid=(4,), in_specs=[pl.BlockSpec((4, 2, 2...]
  transfers between devices with their start and end apart: 8 -> 8, of which waited for: 4 -> 4; matrix products, arithmetic and copies ran while one was open for 2% -> 2% of each run, Pallas kernels for 10% -> 9%
where the time goes in v6:
time: 191 us; the launch traced here: 190 us
  blocking collectives  84.9 us (44%)
  waiting for transfers between devices  44.5 us (23%)
  Pallas kernels  24.5 us (13%)
  starting transfers between devices  17.6 us (9%)
  local copies, waits for them, and re-layouts  13.5 us (7%)
  other arithmetic  4.88 us (3%)
    all_to_all x1, blocking collectives, per_device(): lines = lax.all_to_all(planes, ALL, split_axis=0, concat_axis=0, tiled=True)  50.7 us
    all_to_all x1, blocking collectives, per_device(): lax.all_to_all(outgoing.reshape(128, 1, CAP, 2, BW), ALL, split_axis=0, c...  34.2 us
    ppermute x6, waiting for transfers between devices, shifted(): lax.ppermute(piece, axis, [(i, (i + shift) % size) for i in range(size)])  30.1 us
    all_to_all x1, waiting for transfers between devices, per_device(): a = lax.all_to_all(a, 'gz', split_axis=0, concat_axis=0, tiled=True)  14.4 us
    unnamed x23, local copies, waits for them, and re-layouts  9.2 us
    ppermute x6, starting transfers between devices, shifted(): lax.ppermute(piece, axis, [(i, (i + shift) % size) for i in range(size)])  7.2 us
    pallas_call x1, Pallas kernels, first_z(): pl.pallas_call(first_z_kernel, grid=(4,), in_specs=[pl.BlockSpec((4, 2, 2...  6.47 us
    all_to_all x1, starting transfers between devices, per_device(): a = lax.all_to_all(a, 'gz', split_axis=0, concat_axis=0, tiled=True)  5.86 us
  transfers between devices with their start and end apart: 8, of which 4 were waited for; matrix products, arithmetic and copies ran while one was open for 2% of the time, Pallas kernels for 9%

profile of v6, /device:TPU:1, one launch (start us, length us, event | category | flops | bytes accessed | tf_op | source)
XLA Modules:
  0.0 190.1 jit_solution(4930330010202654732)
XLA Ops:
  0.0 1.6 slice-done
  1.6 0.6 slice-done.1
  2.2 2.6 %fusion = f32[4,2,8,128,128]{4,3,2,1,0:T(8,128)} fusion(f32[4,8,128,128]{3,2,1,0:T(8,128)S(1)} %bitcast.27, bf16[2,4,8,128,128]{4,3,2,1,0:T(8,128)(2,1)S(1)} %bitcast.28), kind=kLoop, calls=%fused_computation.1 | loop fusion | flops 2097152 | bytes 8388608 | tf_op jit(solution)/shard_map/mul | solution.py:330
  4.8 5.9 %all-to-all-start = ((f32[4,2,8,128,128]{4,3,2,1,0:T(8,128)}), f32[4,2,8,128,128]{4,3,2,1,0:T(8,128)}, u32[]{:S(2)}, u32[]{:S(2)}) async-start(f32[4,2,8,128,128]{4,3,2,1,0:T(8,128)} %fusion), calls=%async_computation | async-start | bytes 8388608 | tf_op jit(solution)/shard_map/all_to_all | solution.py:334
  10.6 1.9 constant_dynamic-slice_fusion
  12.5 0.9 copy-done.7
  13.5 1.7 convert_multiply_fusion
  15.1 1.3 collective-permute-start
  16.4 1.4 collective-permute-start.1
  17.9 1.6 collective-permute-start.2
  19.5 20.8 %collective-permute-done.refs_1_ = f32[2,8,128,128]{3,2,1,0:T(8,128)S(1)} collective-permute-done((f32[2,8,128,128]{3,2,1,0:T(8,128)S(1)}, f32[2,8,128,128]{3,2,1,0:T(8,128)S(1)}, u32[]{:S(2)}, u32[]{:S(2)}) %collective-permute-start) | collective-permute-done | bytes 1048608 | tf_op jit(solution)/shard_map/ppermute | solution.py:309
  40.3 0.0 collective-permute-done.1.refs_2_
  40.3 0.0 copy-done.1
  40.3 3.5 %part_y.1.part_ref = f32[4,512,256]{2,1,0:T(8,128)S(1)} custom-call(s32[1]{0:T(128)} %bitcast.4.place_ref, f32[2,8,128,128]{3,2,1,0:T(8,128)S(1)} %get-tuple-element.38.refs_0_, f32[2,8,128,128]{3,2,1,0:T(8,128)S(1)} %collective-permute-done.refs_1_, f32[2,8,128,128]{3,2,1,0:T(8,128)S(1)} %collective-permute-done.1.refs_2_, ...), custom_call_target="tpu_custom_call" | custom-call | flops 2415919104 | bytes 8388608 | tf_op jit(solution)/shard_map/part_y/pallas_call | solution.py:109
  43.8 0.0 copy-start.4
  43.8 1.4 copy-done.4
  45.2 14.4 %all-to-all-done.in_ref = f32[4,2,8,128,128]{4,3,2,1,0:T(8,128)} async-done(((f32[4,2,8,128,128]{4,3,2,1,0:T(8,128)}), f32[4,2,8,128,128]{4,3,2,1,0:T(8,128)}, u32[]{:S(2)}, u32[]{:S(2)}) %all-to-all-start) | async-done | bytes 4194336 | tf_op jit(solution)/shard_map/all_to_all | solution.py:334
  59.6 0.0 copy-done
  59.6 6.5 %first_z.1 = f32[4,2,2,128,256]{4,3,2,1,0:T(8,128)} custom-call(f32[4,2,8,128,128]{4,3,2,1,0:T(8,128)} %all-to-all-done.in_ref, bf16[2,4,256,512]{3,2,1,0:T(8,128)(2,1)S(1)} %copy-done), custom_call_target="tpu_custom_call" | custom-call | flops 3221225472 | bytes 8388608 | tf_op jit(solution)/shard_map/first_z/pallas_call | solution.py:177
  66.0 0.0 collective-permute-done.2.p2
  66.0 4.6 %all-to-all-start.1 = ((f32[4,2,2,128,256]{4,3,2,1,0:T(8,128)}), f32[4,2,2,128,256]{4,3,2,1,0:T(8,128)}, u32[]{:S(2)}, u32[]{:S(2)}) async-start(f32[4,2,2,128,256]{4,3,2,1,0:T(8,128)} %first_z.1), calls=%async_computation.1 | async-start | bytes 4194304 | tf_op jit(solution)/shard_map/all_to_all | solution.py:341
  70.6 0.0 copy-done.10
  70.6 0.1 copy.12
  70.7 0.2 fusion.3
  71.0 0.8 copy-done.8
  71.8 1.6 copy-done.2
  73.4 1.6 copy-done.5
  75.0 1.0 first_y.3
  75.9 1.0 collective-permute-start.3
  76.9 1.8 collective-permute-start.4
  78.7 0.1 copy.13
  78.8 1.8 first_y.2
  80.6 0.1 collective-permute-start.5
  80.7 0.4 fusion.2
  81.1 4.6 %collective-permute-done.3.refs_1_ = f32[2,2,256,128]{3,2,1,0:T(8,128)S(1)} collective-permute-done((f32[2,2,256,128]{3,2,1,0:T(8,128)S(1)}, f32[2,2,256,128]{3,2,1,0:T(8,128)S(1)}, u32[]{:S(2)}, u32[]{:S(2)}) %collective-permute-start.3) | collective-permute-done | bytes 524320 | tf_op jit(solution)/shard_map/ppermute | solution.py:309
  85.6 4.8 %collective-permute-done.4.refs_2_ = f32[2,2,256,128]{3,2,1,0:T(8,128)S(1)} collective-permute-done((f32[2,2,256,128]{3,2,1,0:T(8,128)S(1)}, f32[2,2,256,128]{3,2,1,0:T(8,128)S(1)}, u32[]{:S(2)}, u32[]{:S(2)}) %collective-permute-start.4) | collective-permute-done | bytes 524320 | tf_op jit(solution)/shard_map/ppermute | solution.py:309
  90.4 1.7 part_z.1.part_ref
  92.1 0.0 all-to-all-done.1.in_ref
  92.1 0.0 copy-start.3
  92.2 1.6 copy-done.3
  93.7 3.2 %second_y.1 = f32[2,512,256]{2,1,0:T(8,128)S(1)} custom-call(f32[4,2,2,128,256]{4,3,2,1,0:T(8,128)} %all-to-all-done.1.in_ref, bf16[2,4,512,256]{3,2,1,0:T(8,128)(2,1)S(1)} %copy-done.3), custom_call_target="tpu_custom_call" | custom-call | flops 1610612736 | bytes 5242880 | tf_op jit(solution)/shard_map/second_y/pallas_call | solution.py:201
  97.0 0.0 collective-permute-done.5.last_z
  97.0 2.3 %second.1 = f32[128,2,2,8,128]{4,3,2,1,0:T(8,128)S(1)} custom-call(s32[1]{0:T(128)} %bitcast.to_ref.place_ref.gz_ref, f32[2,2,256,256]{3,2,1,0:T(8,128)S(1)} %bitcast.25, f32[2,256,512]{2,1,0:T(8,128)S(1)} %part_z.1.part_ref, f32[2,2,256,128]{3,2,1,0:T(8,128)} %collective-permute-done.5.last_z, bf16[2,4,256,512]{3,2,1,0:T(8,128)(2,1)S(1)} %copy-done), custom_call_target="tpu_custom_call" | custom-call | flops 402653184 | bytes 8388608 | tf_op jit(solution)/shard_map/second/pallas_call | solution.py:237
  99.3 0.0 copy-start.6
  99.3 50.7 %all_to_all.27.in_ref = f32[128,2,2,8,128]{4,3,2,1,0:T(8,128)S(1)} all-to-all(f32[128,2,2,8,128]{4,3,2,1,0:T(8,128)S(1)} %second.1), channel_id=1, replica_groups=mesh['gx'=8,'gy'=4,'gz'=4] {'gx','gy','gz'}, dimensions={0} | all-to-all | bytes 4194304 | tf_op jit(solution)/shard_map/all_to_all | solution.py:352
  150.0 4.5 %third.1 = f32[4096,128]{1,0:T(8,128)S(1)} custom-call(s32[1024]{0:T(1024)S(1)} %multiply_add_fusion.slot_ref, f32[128,2,2,8,128]{4,3,2,1,0:T(8,128)S(1)} %all_to_all.27.in_ref, bf16[2,512,1024]{2,1,0:T(8,128)(2,1)S(1)} %copy-done.6), custom_call_target="tpu_custom_call" | custom-call | flops 1610612736 | bytes 6291456 | tf_op jit(solution)/shard_map/third/pallas_call | solution.py:288
  154.6 34.2 %all_to_all.28 = f32[128,1,16,2,128]{4,3,2,1,0:T(2,128)S(1)} all-to-all(f32[128,1,16,2,128]{4,3,2,1,0:T(2,128)S(1)} %bitcast.24), channel_id=1, replica_groups=mesh['gx'=8,'gy'=4,'gz'=4] {'gx','gy','gz'}, dimensions={0} | all-to-all | bytes 4194304 | tf_op jit(solution)/shard_map/all_to_all | solution.py:354
  188.8 1.3 copy.19
  (17 shorter events, 0.1 us)
Async XLA Ops:
  0.0 1.6 slice-start
  0.0 2.2 %slice-start.1 = ((bf16[2,64,128,128]{3,2,1,0:T(8,128)(2,1)}), bf16[2,32,128,128]{3,2,1,0:T(8,128)(2,1)S(1)}, s32[]{:S(2)}) async-start(bf16[2,64,128,128]{3,2,1,0:T(8,128)(2,1)} %param.6), calls=%async_computation.5 | async-start | bytes 4194304 | tf_op jit(solution)/shard_map/slice | solution.py:330
  4.8 54.8 %all-to-all-start = ((f32[4,2,8,128,128]{4,3,2,1,0:T(8,128)}), f32[4,2,8,128,128]{4,3,2,1,0:T(8,128)}, u32[]{:S(2)}, u32[]{:S(2)}) async-start(f32[4,2,8,128,128]{4,3,2,1,0:T(8,128)} %fusion), calls=%async_computation | async-start | bytes 8388608 | tf_op jit(solution)/shard_map/all_to_all | solution.py:334
  10.6 2.8 %copy-start.7 = (bf16[2,64,128,128]{3,2,1,0:T(8,128)(2,1)S(1)}, bf16[2,64,128,128]{3,2,1,0:T(8,128)(2,1)}, u32[]{:S(2)}) copy-start(bf16[2,64,128,128]{3,2,1,0:T(8,128)(2,1)} %param.6) | copy-start | bytes 12582916
  13.5 26.8 %copy-start.1 = (bf16[2,4,512,256]{3,2,1,0:T(8,128)(2,1)S(1)}, bf16[2,4,512,256]{3,2,1,0:T(8,128)(2,1)}, u32[]{:S(2)}) copy-start(bf16[2,4,512,256]{3,2,1,0:T(8,128)(2,1)} %constant.47.clone.refs_3_.table_ref) | copy-start | bytes 6291460
  15.1 25.2 %collective-permute-start = (f32[2,8,128,128]{3,2,1,0:T(8,128)S(1)}, f32[2,8,128,128]{3,2,1,0:T(8,128)S(1)}, u32[]{:S(2)}, u32[]{:S(2)}) collective-permute-start(f32[2,8,128,128]{3,2,1,0:T(8,128)S(1)} %get-tuple-element.37), channel_id=1, source_target_pairs={{0,4},{4,8},{8,12},{12,0},{1,5},{5,9},{9,13},{13,1},{2,6},{6,10},{... | collective-permute-start | bytes 3145736 | tf_op jit(solution)/shard_map/ppermute | solution.py:309
  16.4 23.9 %collective-permute-start.1 = (f32[2,8,128,128]{3,2,1,0:T(8,128)S(1)}, f32[2,8,128,128]{3,2,1,0:T(8,128)S(1)}, u32[]{:S(2)}, u32[]{:S(2)}) collective-permute-start(f32[2,8,128,128]{3,2,1,0:T(8,128)S(1)} %get-tuple-element.36), channel_id=1, source_target_pairs={{0,12},{4,0},{8,4},{12,8},{1,13},{5,1},{9,5},{13,9},{2,14},{6,2},{... | collective-permute-start | bytes 3145736 | tf_op jit(solution)/shard_map/ppermute | solution.py:309
  17.9 48.2 %collective-permute-start.2 = (f32[2,8,128,128]{3,2,1,0:T(8,128)}, f32[2,8,128,128]{3,2,1,0:T(8,128)S(1)}, u32[]{:S(2)}, u32[]{:S(2)}) collective-permute-start(f32[2,8,128,128]{3,2,1,0:T(8,128)} %get-tuple-element.35), channel_id=1, source_target_pairs={{0,8},{4,12},{8,0},{12,4},{1,9},{5,13},{9,1},{13,5},{2,10},{6,14},... | collective-permute-start | bytes 3145736 | tf_op jit(solution)/shard_map/ppermute | solution.py:309
  40.3 19.3 %copy-start = (bf16[2,4,256,512]{3,2,1,0:T(8,128)(2,1)S(1)}, bf16[2,4,256,512]{3,2,1,0:T(8,128)(2,1)}, u32[]{:S(2)}) copy-start(bf16[2,4,256,512]{3,2,1,0:T(8,128)(2,1)} %constant.48.clone.table_ref.refs_3_) | copy-start | bytes 6291460
  43.8 1.4 copy-start.4
  66.0 4.6 %copy-start.10 = (s32[1024,1]{0,1:T(1,128)S(1)}, s32[1024,1]{0,1:T(1,128)}, u32[]{:S(2)}) copy-start(s32[1024,1]{0,1:T(1,128)} %param.8) | copy-start | bytes 12292
  66.0 26.1 %all-to-all-start.1 = ((f32[4,2,2,128,256]{4,3,2,1,0:T(8,128)}), f32[4,2,2,128,256]{4,3,2,1,0:T(8,128)}, u32[]{:S(2)}, u32[]{:S(2)}) async-start(f32[4,2,2,128,256]{4,3,2,1,0:T(8,128)} %first_z.1), calls=%async_computation.1 | async-start | bytes 4194304 | tf_op jit(solution)/shard_map/all_to_all | solution.py:341
  70.9 0.8 copy-start.8
  71.8 1.6 copy-start.2
  73.4 1.6 copy-start.5
  75.0 3.7 %copy-start.9 = (s32[128,8,128]{0,1,2:T(8,128)S(1)}, s32[128,8,128]{0,1,2:T(8,128)}, u32[]{:S(2)}) copy-start(s32[128,8,128]{0,1,2:T(8,128)} %copy-done.8) | copy-start | bytes 1572868
  75.9 9.7 %collective-permute-start.3 = (f32[2,2,256,128]{3,2,1,0:T(8,128)S(1)}, f32[2,2,256,128]{3,2,1,0:T(8,128)S(1)}, u32[]{:S(2)}, u32[]{:S(2)}) collective-permute-start(f32[2,2,256,128]{3,2,1,0:T(8,128)S(1)} %get-tuple-element.27), channel_id=1, source_target_pairs={{0,1},{1,2},{2,3},{3,0},{4,5},{5,6},{6,7},{7,4},{8,9},{9,10},{10,1... | collective-permute-start | bytes 1572872 | tf_op jit(solution)/shard_map/ppermute | solution.py:309
  76.9 13.5 %collective-permute-start.4 = (f32[2,2,256,128]{3,2,1,0:T(8,128)S(1)}, f32[2,2,256,128]{3,2,1,0:T(8,128)S(1)}, u32[]{:S(2)}, u32[]{:S(2)}) collective-permute-start(f32[2,2,256,128]{3,2,1,0:T(8,128)S(1)} %get-tuple-element.28), channel_id=1, source_target_pairs={{0,3},{1,0},{2,1},{3,2},{4,7},{5,4},{6,5},{7,6},{8,11},{9,8},{10,9... | collective-permute-start | bytes 1572872 | tf_op jit(solution)/shard_map/ppermute | solution.py:309
  80.6 16.4 %collective-permute-start.5 = (f32[2,2,256,128]{3,2,1,0:T(8,128)}, f32[2,2,256,128]{3,2,1,0:T(8,128)}, u32[]{:S(2)}, u32[]{:S(2)}) collective-permute-start(f32[2,2,256,128]{3,2,1,0:T(8,128)} %get-tuple-element.29), channel_id=1, source_target_pairs={{0,2},{1,3},{2,0},{3,1},{4,6},{5,7},{6,4},{7,5},{8,10},{9,11},{10,... | collective-permute-start | bytes 1572872 | tf_op jit(solution)/shard_map/ppermute | solution.py:309
  92.1 1.6 copy-start.3
  99.3 50.7 %copy-start.6 = (bf16[2,512,1024]{2,1,0:T(8,128)(2,1)S(1)}, bf16[2,512,1024]{2,1,0:T(8,128)(2,1)}, u32[]{:S(2)}) copy-start(bf16[2,512,1024]{2,1,0:T(8,128)(2,1)} %constant.46.clone.table_ref) | copy-start | bytes 6291460

commit v7 on v6

--- a/solution.py
+++ b/solution.py
@@ -15,7 +15,7 @@
 CAP = 16
 ALL = ("gx", "gy", "gz")
 MIB = 1 << 20
-VMEM = 40
+VMEM = 24
 
 
 def split_table(table):
@@ -125,8 +125,12 @@
     )(place, *pieces, table)
 
 
-def first_y_kernel(place_ref, to_ref, part_ref, p2, table_ref, *out_refs):
-    total = part_ref[0] + term_of(False, p2[...], table_ref, 0)
+def first_y_kernel(place_ref, to_ref, p0, p1, p2, p3, table_ref, *out_refs):
+    total = None
+    for shift, piece in enumerate((p0, p1, p2, p3)):
+        g = lax.rem(place_ref[0] + (4 - shift), 4)
+        term = term_of(False, piece[...], table_ref, g)
+        total = term if total is None else total + term
     for step, out_ref in enumerate(out_refs):
 
         @pl.when(pl.program_id(0) == step)
@@ -138,7 +142,7 @@
                     ]
 
 
-def first_y(shifts, place, to, part, piece, table):
+def first_y(shifts, place, to, pieces, table):
     def pair(i, to):
         return lax.rem(to[0] + jnp.where(i == 0, shifts[0], shifts[1]), 4)
 
@@ -149,68 +153,73 @@
             num_scalar_prefetch=2,
             grid=(2,),
             in_specs=[
-                pl.BlockSpec((1, 512, 256), lambda i, place, to: (pair(i, to), 0, 0)),
-                pl.BlockSpec((2, 2, 128, 128), lambda i, place, to: (0, pair(i, to), 0, 0)),
-                pl.BlockSpec(
-                    (2, 1, 512, 256), lambda i, place, to: (0, lax.rem(place[0] + 2, 4), 0, 0)
-                ),
-            ],
+                pl.BlockSpec((2, 2, 128, 128), lambda i, place, to: (0, pair(i, to), 0, 0))
+            ]
+            * 4
+            + [pl.BlockSpec((2, 4, 512, 256), lambda i, place, to: (0, 0, 0, 0))],
             out_specs=[pl.BlockSpec(shape, lambda i, place, to: (0, 0, 0, 0))] * 2,
         ),
         out_shape=[jax.ShapeDtypeStruct(shape, jnp.float32)] * 2,
         compiler_params=params(VMEM),
-        cost_estimate=cost(512 * 256 * 512, 4 * MIB),
+        cost_estimate=cost(512 * 1024 * 512, 4 * MIB),
         name="first_y",
-    )(place, to, part, piece, table)
-
-
-def first_z_kernel(in_ref, table_ref, out_ref):
-    total = None
-    for g in range(4):
-        term = term_of(True, in_ref[g], table_ref, g)
-        total = term if total is None else total + term
-    for plane in range(2):
-        out_ref[0, plane] = total[:, plane * KEPT : (plane + 1) * KEPT].reshape(2, 128, KEPT)
+    )(place, to, *pieces, table)
+
+
+def first_z_kernel(p0, p1, p2, p3, table_ref, out_ref):
+    rows = jnp.concatenate(
+        [piece[0, plane].reshape(512, 128) for piece in (p0, p1, p2, p3) for plane in range(2)],
+        axis=1,
+    )
+    table = tuple(table_ref[i].reshape(1024, 512) for i in range(2))
+    total = product(halves(rows), table)
+    for pair in range(2):
+        for plane in range(2):
+            out_ref[pair, plane] = total[
+                pair * 256 : (pair + 1) * 256, plane * KEPT : (plane + 1) * KEPT
+            ].reshape(2, 128, KEPT)
 
 
 def first_z(arrived, table):
+    def from_device(g):
+        return pl.BlockSpec((1, 2, 4, 128, 128), lambda i: (g, 0, i, 0, 0))
+
     return pl.pallas_call(
         first_z_kernel,
-        grid=(4,),
-        in_specs=[
-            pl.BlockSpec((4, 2, 2, 128, 128), lambda i: (0, 0, i, 0, 0)),
-            pl.BlockSpec((2, 4, 256, 512), lambda i: (0, 0, 0, 0)),
-        ],
-        out_specs=pl.BlockSpec((1, 2, 2, 128, KEPT), lambda i: (i, 0, 0, 0, 0)),
+        grid=(2,),
+        in_specs=[from_device(g) for g in range(4)]
+        + [pl.BlockSpec((2, 4, 256, 512), lambda i: (0, 0, 0, 0))],
+        out_specs=pl.BlockSpec((2, 2, 2, 128, KEPT), lambda i: (i, 0, 0, 0, 0)),
         out_shape=pltpu.HBM((4, 2, 2, 128, KEPT), jnp.float32),
         compiler_params=params(VMEM),
         cost_estimate=cost(1024 * 1024 * 512, 8 * MIB),
         name="first_z",
-    )(arrived, table)
-
-
-def second_y_kernel(in_ref, table_ref, out_ref):
+    )(arrived, arrived, arrived, arrived, table)
+
+
+def second_y_kernel(p0, p1, p2, p3, table_ref, out_ref):
     total = None
-    for g in range(4):
-        term = term_of(False, in_ref[g], table_ref, g)
+    for g, piece in enumerate((p0, p1, p2, p3)):
+        term = term_of(False, piece[0], table_ref, g)
         total = term if total is None else total + term
     out_ref[0] = total
 
 
 def second_y(arrived, table):
+    def from_device(g):
+        return pl.BlockSpec((1, 2, 1, 128, KEPT), lambda i: (g, 0, i, 0, 0))
+
     return pl.pallas_call(
         second_y_kernel,
         grid=(2,),
-        in_specs=[
-            pl.BlockSpec((4, 2, 1, 128, KEPT), lambda i: (0, 0, i, 0, 0)),
-            pl.BlockSpec((2, 4, 512, 256), lambda i: (0, 0, 0, 0)),
-        ],
+        in_specs=[from_device(g) for g in range(4)]
+        + [pl.BlockSpec((2, 4, 512, 256), lambda i: (0, 0, 0, 0))],
         out_specs=pl.BlockSpec((1, 512, KEPT), lambda i: (i, 0, 0)),
         out_shape=jax.ShapeDtypeStruct((2, 512, KEPT), jnp.float32),
         compiler_params=params(VMEM),
         cost_estimate=cost(512 * 1024 * 512, 5 * MIB),
         name="second_y",
-    )(arrived, table)
+    )(arrived, arrived, arrived, arrived, table)
 
 
 def second_kernel(gz_ref, done_y, part_ref, last_z, table_ref, out_ref, held):
@@ -327,7 +336,10 @@
             normals, start, 8, 1
         ).astype(jnp.float32)
 
-    a = spectrum[:32].reshape(4, 1, 8, 128, 128) * normals[:, :32].astype(jnp.float32).reshape(
+    zero = lax.optimization_barrier(jnp.int32(0))
+    a = lax.dynamic_slice_in_dim(spectrum, zero, 32, 0).reshape(
+        4, 1, 8, 128, 128
+    ) * lax.dynamic_slice_in_dim(normals, zero, 32, 1).astype(jnp.float32).reshape(
         2, 4, 8, 128, 128
     ).transpose(1, 0, 2, 3, 4)
     a, normals, spectrum = lax.optimization_barrier((a, normals, spectrum))
@@ -335,20 +347,21 @@
     b1, b3, b2 = shifted(chunk_b(1), "gy", 1), shifted(chunk_b(3), "gy", 3), shifted(chunk_b(2), "gy", 2)
     b0 = chunk_b(0)
 
-    part_b = part_sum(False, gy, (b0, b1, b3), 2, table_y)
+    a, slots = lax.optimization_barrier((a, slots_of(block_owner)))
     a = first_z(a, table_z)
-    a, part_b, b2 = lax.optimization_barrier((a, part_b, b2))
+    b0, b1, b2, b3, _ = lax.optimization_barrier((b0, b1, b2, b3, a))
     a = lax.all_to_all(a, "gy", split_axis=0, concat_axis=0, tiled=True)
-    b1, b3 = first_y((1, 3), gy, gz, part_b, b2, table_y)
+    pieces = b0, b1, b2, b3
+    b1, b3 = first_y((1, 3), gy, gz, pieces, table_y)
     b1, b3 = shifted(b1, "gz", 1), shifted(b3, "gz", 3)
-    b2, b0 = first_y((2, 0), gy, gz, part_b, b2, table_y)
+    b2, b0 = first_y((2, 0), gy, gz, pieces, table_y)
     b2 = shifted(b2, "gz", 2)
 
+    a = second_y(a, table_y)
+    a, b1, b3 = lax.optimization_barrier((a, b1, b3))
     part_b = part_sum(True, gz, (b0, b1, b3), 1, table_z)
-    a = second_y(a, table_y)
-    a, part_b, b2 = lax.optimization_barrier((a, part_b, b2))
+    part_b, b2 = lax.optimization_barrier((part_b, b2))
     planes = second(gz, a, part_b, b2, table_z)
-    planes, slots = lax.optimization_barrier((planes, slots_of(block_owner)))
     lines = lax.all_to_all(planes, ALL, split_axis=0, concat_axis=0, tiled=True)
     outgoing = third(slots, lines, table_x)
     return lax.all_to_all(

time: 191 us -> 187 us (0.979)
  blocking collectives: 84.9 us -> 77 us
  waiting for transfers between devices: 44.5 us -> 48.9 us
    ppermute x6, waiting for transfers between devices: 30.1 us -> 0.02 us  [shifted(): lax.ppermute(piece, axis, [(i, (i + shift) % size) for i in range(size)])]
    all_to_all x1, waiting for transfers between devices: 14.4 us -> 37.7 us  [per_device(): a = lax.all_to_all(a, 'gz', split_axis=0, concat_axis=0, tiled=True)]
    all_to_all x1, waiting for transfers between devices: 0.01 us -> 11.2 us  [per_device(): a = lax.all_to_all(a, 'gy', split_axis=0, concat_axis=0, tiled=True)]
    all_to_all x1, blocking collectives: 50.7 us -> 42.8 us  [per_device(): lines = lax.all_to_all(planes, ALL, split_axis=0, concat_axis=0, tiled=True)]
    pallas_call x2, Pallas kernels: 2.73 us -> 8.24 us  [first_y(): pl.pallas_call(first_y_kernel, grid_spec=pltpu.PrefetchScalarGridSpec(num...]
    pallas_call x2 -> x1, Pallas kernels: 5.17 us -> 2.65 us  [part_sum(): pl.pallas_call(functools.partial(sum_kernel, along_z), grid_spec=pltpu.Pr...]
    slice x4 -> x0, local copies, waits for them, and re-layouts: 2.22 us -> none  [the longest x2 1.59 us: per_device(): spectrum[:32].reshape(4, 1, 8, 128, 128)]
    dynamic_slice x0 -> x2, local copies, waits for them, and re-layouts: none -> 2.11 us  [the longest x1 1.98 us: per_device(): lax.dynamic_slice_in_dim(normals, zero, 32, 1).astype(jnp.float32)]
  transfers between devices with their start and end apart: 8 -> 8, of which waited for: 4 -> 2; matrix products, arithmetic and copies ran while one was open for 2% -> 3% of each run, Pallas kernels for 9% -> 10%
where the time goes in v7:
time: 187 us; the launch traced here: 186 us
  blocking collectives  77 us (41%)
  waiting for transfers between devices  48.9 us (26%)
  Pallas kernels  25.3 us (14%)
  starting transfers between devices  16.5 us (9%)
  local copies, waits for them, and re-layouts  12.1 us (6%)
  other arithmetic  6.28 us (3%)
    all_to_all x1, blocking collectives, per_device(): lines = lax.all_to_all(planes, ALL, split_axis=0, concat_axis=0, tiled=True)  42.8 us
    all_to_all x1, waiting for transfers between devices, per_device(): a = lax.all_to_all(a, 'gz', split_axis=0, concat_axis=0, tiled=True)  37.7 us
    all_to_all x1, blocking collectives, per_device(): lax.all_to_all(outgoing.reshape(128, 1, CAP, 2, BW), ALL, split_axis=0, c...  34.2 us
    all_to_all x1, waiting for transfers between devices, per_device(): a = lax.all_to_all(a, 'gy', split_axis=0, concat_axis=0, tiled=True)  11.2 us
    pallas_call x2, Pallas kernels, first_y(): pl.pallas_call(first_y_kernel, grid_spec=pltpu.PrefetchScalarGridSpec(num...  8.24 us
    unnamed x23, local copies, waits for them, and re-layouts  7.88 us
    ppermute x6, starting transfers between devices, shifted(): lax.ppermute(piece, axis, [(i, (i + shift) % size) for i in range(size)])  6.46 us
    pallas_call x1, Pallas kernels, first_z(): pl.pallas_call(first_z_kernel, grid=(2,), in_specs=[from_device(g) for g...  6.16 us
  transfers between devices with their start and end apart: 8, of which 2 were waited for; matrix products, arithmetic and copies ran while one was open for 3% of the time, Pallas kernels for 10%

profile of v7, /device:TPU:1, one launch (start us, length us, event | category | flops | bytes accessed | tf_op | source)
XLA Modules:
  0.0 186.3 jit_solution(14002782062114362491)
XLA Ops:
  0.0 2.0 %constant_dynamic-slice_fusion.4 = bf16[2,32,128,128]{3,2,1,0:T(8,128)(2,1)S(1)} fusion(bf16[2,64,128,128]{3,2,1,0:T(8,128)(2,1)} %param.6, s32[]{:T(128)S(6)} %select_n.20), kind=kLoop, calls=%fused_computation.21 | loop fusion | bytes 4194308 | tf_op jit(solution)/shard_map/dynamic_slice | solution.py:342
  2.0 0.8 copy-done.8
  2.8 0.1 constant_dynamic-slice_fusion.5
  3.0 2.7 %fusion = f32[4,2,8,128,128]{4,3,2,1,0:T(8,128)} fusion(f32[4,8,128,128]{3,2,1,0:T(8,128)S(1)} %bitcast.28, bf16[2,4,8,128,128]{4,3,2,1,0:T(8,128)(2,1)S(1)} %bitcast.27), kind=kLoop, calls=%fused_computation.1 | loop fusion | flops 2097152 | bytes 8388608 | tf_op jit(solution)/shard_map/mul | solution.py:340
  5.7 5.9 %all-to-all-start = ((f32[4,2,8,128,128]{4,3,2,1,0:T(8,128)}), f32[4,2,8,128,128]{4,3,2,1,0:T(8,128)}, u32[]{:S(2)}, u32[]{:S(2)}) async-start(f32[4,2,8,128,128]{4,3,2,1,0:T(8,128)} %fusion), calls=%async_computation | async-start | bytes 8388608 | tf_op jit(solution)/shard_map/all_to_all | solution.py:346
  11.5 1.9 %constant_dynamic-slice_fusion = (f32[8,128,128]{2,1,0:T(8,128)S(1)}, f32[8,128,128]{2,1,0:T(8,128)S(1)}, f32[8,128,128]{2,1,0:T(8,128)S(1)}, f32[8,128,128]{2,1,0:T(8,128)S(1)}) fusion(f32[64,128,128]{2,1,0:T(8,128)} %param.7, s32[]{:T(128)S(6)} %select_n.24, s32[]{:T(128)S(6)} %select_n.23, s32[]{:T(128)S(6)} %select_n.22, s32[]{:T(128)S(6)} %select_n.21), kind=kLoop, calls=%fused_computation.17 | loop fusion | bytes 4194320 | tf_op jit(solution)/shard_map/dynamic_slice | solution.py:335
  13.4 0.9 copy-done.7
  14.3 1.9 %convert_multiply_fusion = (f32[2,8,128,128]{3,2,1,0:T(8,128)}, f32[2,8,128,128]{3,2,1,0:T(8,128)}, f32[2,8,128,128]{3,2,1,0:T(8,128)}, f32[2,8,128,128]{3,2,1,0:T(8,128)S(1)}) fusion(bf16[2,64,128,128]{3,2,1,0:T(8,128)(2,1)S(1)} %copy-done.7, s32[]{:T(128)S(6)} %select_n.24, f32[8,128,128]{2,1,0:T(8,128)S(1)} %get-tuple-element.45, s32[]{:T(128)S(6)} %select_n.23, ...), kind=kLoop, calls=%fused_computation.2 | loop fusion | flops 2097152 | bytes 8388624 | tf_op jit(solution)/shard_map/mul | solution.py:335
  16.3 2.7 %collective-permute-start.2 = (f32[2,8,128,128]{3,2,1,0:T(8,128)}, f32[2,8,128,128]{3,2,1,0:T(8,128)}, u32[]{:S(2)}, u32[]{:S(2)}) collective-permute-start(f32[2,8,128,128]{3,2,1,0:T(8,128)} %get-tuple-element.41), channel_id=1, source_target_pairs={{0,12},{4,0},{8,4},{12,8},{1,13},{5,1},{9,5},{13,9},{2,14},{6,2},{... | collective-permute-start | bytes 3145736 | tf_op jit(solution)/shard_map/ppermute | solution.py:318
  19.0 0.3 collective-permute-start.1
  19.3 0.7 collective-permute-start
  20.0 0.0 copy-done.10
  20.0 0.1 copy.12
  20.1 0.2 fusion.3
  20.3 0.0 copy-start.9
  20.4 0.8 copy-done.9
  21.2 1.1 broadcast_add_fusion
  22.3 0.1 copy.13
  22.4 0.4 fusion.2
  22.7 37.7 %all-to-all-done.p0.p1.p2.p3 = f32[4,2,8,128,128]{4,3,2,1,0:T(8,128)} async-done(((f32[4,2,8,128,128]{4,3,2,1,0:T(8,128)}), f32[4,2,8,128,128]{4,3,2,1,0:T(8,128)}, u32[]{:S(2)}, u32[]{:S(2)}) %all-to-all-start) | async-done | bytes 4194336 | tf_op jit(solution)/shard_map/all_to_all | solution.py:346
  60.4 6.2 %first_z.1 = f32[4,2,2,128,256]{4,3,2,1,0:T(8,128)} custom-call(f32[4,2,8,128,128]{4,3,2,1,0:T(8,128)} %all-to-all-done.p0.p1.p2.p3, f32[4,2,8,128,128]{4,3,2,1,0:T(8,128)} %all-to-all-done.p0.p1.p2.p3, f32[4,2,8,128,128]{4,3,2,1,0:T(8,128)} %all-to-all-done.p0.p1.p2.p3, f32[4,2,8,128,128]{4,3,2,1,0:T(8,128)} %all-to-all-done.p0.p1.p2.p3, ...), custom_call_target="tpu_custom_call" | custom-call | flops 3221225472 | bytes 8388608 | tf_op jit(solution)/shard_map/first_z/pallas_call | solution.py:187
  66.6 4.2 %all-to-all-start.1 = ((f32[4,2,2,128,256]{4,3,2,1,0:T(8,128)}), f32[4,2,2,128,256]{4,3,2,1,0:T(8,128)S(1)}, u32[]{:S(2)}, u32[]{:S(2)}) async-start(f32[4,2,2,128,256]{4,3,2,1,0:T(8,128)} %first_z.1), calls=%async_computation.1 | async-start | bytes 4194304 | tf_op jit(solution)/shard_map/all_to_all | solution.py:353
  70.8 0.0 collective-permute-done.2.p3
  70.8 0.0 collective-permute-done.1.p2
  70.8 0.0 collective-permute-done.p1
  70.8 0.0 copy-start.2
  70.8 1.6 copy-done.2
  72.4 4.2 %first_y.2 = (f32[2,2,256,128]{3,2,1,0:T(8,128)}, f32[2,2,256,128]{3,2,1,0:T(8,128)}) custom-call(s32[1]{0:T(128)} %bitcast.9.place_ref, s32[1]{0:T(128)} %bitcast.8.to_ref.place_ref.gz_ref, f32[2,8,128,128]{3,2,1,0:T(8,128)S(1)} %get-tuple-element.28.p0, f32[2,8,128,128]{3,2,1,0:T(8,128)} %collective-permute-done.p1, ...), custom_call_target="tpu_custom_call" | custom-call | flops 1610612736 | bytes 4194304 | tf_op jit(solution)/shard_map/first_y/pallas_call | solution.py:150
  76.6 0.9 collective-permute-start.3
  77.5 1.8 collective-permute-start.4
  79.3 4.0 %first_y.3 = (f32[2,2,256,128]{3,2,1,0:T(8,128)}, f32[2,2,256,128]{3,2,1,0:T(8,128)S(1)}) custom-call(s32[1]{0:T(128)} %bitcast.9.place_ref, s32[1]{0:T(128)} %bitcast.8.to_ref.place_ref.gz_ref, f32[2,8,128,128]{3,2,1,0:T(8,128)S(1)} %get-tuple-element.28.p0, f32[2,8,128,128]{3,2,1,0:T(8,128)} %collective-permute-done.p1, ...), custom_call_target="tpu_custom_call" | custom-call | flops 1610612736 | bytes 4194304 | tf_op jit(solution)/shard_map/first_y/pallas_call | solution.py:150
  83.3 0.8 copy-done.5
  84.1 0.0 collective-permute-start.5
  84.1 11.2 %all-to-all-done.1.p0.p1.p2.p3 = f32[4,2,2,128,256]{4,3,2,1,0:T(8,128)S(1)} async-done(((f32[4,2,2,128,256]{4,3,2,1,0:T(8,128)}), f32[4,2,2,128,256]{4,3,2,1,0:T(8,128)S(1)}, u32[]{:S(2)}, u32[]{:S(2)}) %all-to-all-start.1) | async-done | bytes 2097184 | tf_op jit(solution)/shard_map/all_to_all | solution.py:353
  95.3 1.6 copy-done.3
  96.9 2.2 %second_y.1 = f32[2,512,256]{2,1,0:T(8,128)S(1)} custom-call(f32[4,2,2,128,256]{4,3,2,1,0:T(8,128)S(1)} %all-to-all-done.1.p0.p1.p2.p3, f32[4,2,2,128,256]{4,3,2,1,0:T(8,128)S(1)} %all-to-all-done.1.p0.p1.p2.p3, f32[4,2,2,128,256]{4,3,2,1,0:T(8,128)S(1)} %all-to-all-done.1.p0.p1.p2.p3, f32[4,2,2,128,256]{4,3,2,1,0:T(8,128)S(1)} %all-to-all-done.1.p0.p1.p2.p3, ...), custom_call_target="tpu_custom_call" | custom-call | flops 1610612736 | bytes 5242880 | tf_op jit(solution)/shard_map/second_y/pallas_call | solution.py:212
  99.1 0.0 collective-permute-done.3.refs_1_
  99.1 0.0 collective-permute-done.4.refs_2_
  99.1 0.0 copy-done.1
  99.1 0.0 copy-done.6
  99.1 2.7 %part_z.1.part_ref = f32[2,256,512]{2,1,0:T(8,128)S(1)} custom-call(s32[1]{0:T(128)} %bitcast.8.to_ref.place_ref.gz_ref, f32[2,2,256,128]{3,2,1,0:T(8,128)S(1)} %copy-done.6, f32[2,2,256,128]{3,2,1,0:T(8,128)} %collective-permute-done.3.refs_1_, f32[2,2,256,128]{3,2,1,0:T(8,128)} %collective-permute-done.4.refs_2_, bf16[2,4,256,512]{3,2,1,0:T(8,128)(2,1)S(1)} %copy-done.1), custom_call_target="tpu_custom_call" | custom-call | flops 1207959552 | bytes 8388608 | tf_op jit(solution)/shard_map/part_z/pallas_call | solution.py:109
  101.8 0.0 collective-permute-done.5.last_z
  101.8 1.5 second.1
  103.3 0.0 copy-start.4
  103.4 42.8 %all_to_all.27.in_ref = f32[128,2,2,8,128]{4,3,2,1,0:T(8,128)S(1)} all-to-all(f32[128,2,2,8,128]{4,3,2,1,0:T(8,128)S(1)} %second.1), channel_id=1, replica_groups=mesh['gx'=8,'gy'=4,'gz'=4] {'gx','gy','gz'}, dimensions={0} | all-to-all | bytes 4194304 | tf_op jit(solution)/shard_map/all_to_all | solution.py:365
  146.2 4.5 %third.1 = f32[4096,128]{1,0:T(8,128)S(1)} custom-call(s32[1024]{0:T(1024)S(1)} %multiply_add_fusion.slot_ref, f32[128,2,2,8,128]{4,3,2,1,0:T(8,128)S(1)} %all_to_all.27.in_ref, bf16[2,512,1024]{2,1,0:T(8,128)(2,1)S(1)} %copy-done.4), custom_call_target="tpu_custom_call" | custom-call | flops 1610612736 | bytes 6291456 | tf_op jit(solution)/shard_map/third/pallas_call | solution.py:297
  150.7 34.2 %all_to_all.28 = f32[128,1,16,2,128]{4,3,2,1,0:T(2,128)S(1)} all-to-all(f32[128,1,16,2,128]{4,3,2,1,0:T(2,128)S(1)} %bitcast.24), channel_id=1, replica_groups=mesh['gx'=8,'gy'=4,'gz'=4] {'gx','gy','gz'}, dimensions={0} | all-to-all | bytes 4194304 | tf_op jit(solution)/shard_map/all_to_all | solution.py:367
  184.9 1.3 copy.19
  (14 shorter events, 0.1 us)
Async XLA Ops:
  0.0 2.8 %copy-start.8 = (f32[64,128,128]{2,1,0:T(8,128)S(1)}, f32[64,128,128]{2,1,0:T(8,128)}, u32[]{:S(2)}) copy-start(f32[64,128,128]{2,1,0:T(8,128)} %param.7) | copy-start | bytes 12582916
  5.7 54.8 %all-to-all-start = ((f32[4,2,8,128,128]{4,3,2,1,0:T(8,128)}), f32[4,2,8,128,128]{4,3,2,1,0:T(8,128)}, u32[]{:S(2)}, u32[]{:S(2)}) async-start(f32[4,2,8,128,128]{4,3,2,1,0:T(8,128)} %fusion), calls=%async_computation | async-start | bytes 8388608 | tf_op jit(solution)/shard_map/all_to_all | solution.py:346
  11.5 2.8 %copy-start.7 = (bf16[2,64,128,128]{3,2,1,0:T(8,128)(2,1)S(1)}, bf16[2,64,128,128]{3,2,1,0:T(8,128)(2,1)}, u32[]{:S(2)}) copy-start(bf16[2,64,128,128]{3,2,1,0:T(8,128)(2,1)} %param.6) | copy-start | bytes 12582916
  14.3 5.7 %copy-start.10 = (s32[1024,1]{0,1:T(1,128)S(1)}, s32[1024,1]{0,1:T(1,128)}, u32[]{:S(2)}) copy-start(s32[1024,1]{0,1:T(1,128)} %param.8) | copy-start | bytes 12292
  16.2 44.2 %copy-start = (bf16[2,4,256,512]{3,2,1,0:T(8,128)(2,1)S(1)}, bf16[2,4,256,512]{3,2,1,0:T(8,128)(2,1)}, u32[]{:S(2)}) copy-start(bf16[2,4,256,512]{3,2,1,0:T(8,128)(2,1)} %constant.49.clone.table_ref.refs_3_) | copy-start | bytes 6291460
  16.3 54.5 %collective-permute-start.2 = (f32[2,8,128,128]{3,2,1,0:T(8,128)}, f32[2,8,128,128]{3,2,1,0:T(8,128)}, u32[]{:S(2)}, u32[]{:S(2)}) collective-permute-start(f32[2,8,128,128]{3,2,1,0:T(8,128)} %get-tuple-element.41), channel_id=1, source_target_pairs={{0,12},{4,0},{8,4},{12,8},{1,13},{5,1},{9,5},{13,9},{2,14},{6,2},{... | collective-permute-start | bytes 3145736 | tf_op jit(solution)/shard_map/ppermute | solution.py:318
  19.0 51.8 %collective-permute-start.1 = (f32[2,8,128,128]{3,2,1,0:T(8,128)}, f32[2,8,128,128]{3,2,1,0:T(8,128)}, u32[]{:S(2)}, u32[]{:S(2)}) collective-permute-start(f32[2,8,128,128]{3,2,1,0:T(8,128)} %get-tuple-element.42), channel_id=1, source_target_pairs={{0,8},{4,12},{8,0},{12,4},{1,9},{5,13},{9,1},{13,5},{2,10},{6,14},... | collective-permute-start | bytes 3145736 | tf_op jit(solution)/shard_map/ppermute | solution.py:318
  19.3 51.4 %collective-permute-start = (f32[2,8,128,128]{3,2,1,0:T(8,128)}, f32[2,8,128,128]{3,2,1,0:T(8,128)}, u32[]{:S(2)}, u32[]{:S(2)}) collective-permute-start(f32[2,8,128,128]{3,2,1,0:T(8,128)} %get-tuple-element.43), channel_id=1, source_target_pairs={{0,4},{4,8},{8,12},{12,0},{1,5},{5,9},{9,13},{13,1},{2,6},{6,10},{... | collective-permute-start | bytes 3145736 | tf_op jit(solution)/shard_map/ppermute | solution.py:318
  20.3 0.8 copy-start.9
  66.6 28.7 %all-to-all-start.1 = ((f32[4,2,2,128,256]{4,3,2,1,0:T(8,128)}), f32[4,2,2,128,256]{4,3,2,1,0:T(8,128)S(1)}, u32[]{:S(2)}, u32[]{:S(2)}) async-start(f32[4,2,2,128,256]{4,3,2,1,0:T(8,128)} %first_z.1), calls=%async_computation.1 | async-start | bytes 4194304 | tf_op jit(solution)/shard_map/all_to_all | solution.py:353
  70.8 1.6 copy-start.2
  76.6 22.5 %collective-permute-start.3 = (f32[2,2,256,128]{3,2,1,0:T(8,128)}, f32[2,2,256,128]{3,2,1,0:T(8,128)}, u32[]{:S(2)}, u32[]{:S(2)}) collective-permute-start(f32[2,2,256,128]{3,2,1,0:T(8,128)} %get-tuple-element.32), channel_id=1, source_target_pairs={{0,1},{1,2},{2,3},{3,0},{4,5},{5,6},{6,7},{7,4},{8,9},{9,10},{10,1... | collective-permute-start | bytes 1572872 | tf_op jit(solution)/shard_map/ppermute | solution.py:318
  77.5 21.6 %collective-permute-start.4 = (f32[2,2,256,128]{3,2,1,0:T(8,128)}, f32[2,2,256,128]{3,2,1,0:T(8,128)}, u32[]{:S(2)}, u32[]{:S(2)}) collective-permute-start(f32[2,2,256,128]{3,2,1,0:T(8,128)} %get-tuple-element.33), channel_id=1, source_target_pairs={{0,3},{1,0},{2,1},{3,2},{4,7},{5,4},{6,5},{7,6},{8,11},{9,8},{10,9... | collective-permute-start | bytes 1572872 | tf_op jit(solution)/shard_map/ppermute | solution.py:318
  83.3 0.8 copy-start.5
  84.1 17.7 %collective-permute-start.5 = (f32[2,2,256,128]{3,2,1,0:T(8,128)}, f32[2,2,256,128]{3,2,1,0:T(8,128)S(1)}, u32[]{:S(2)}, u32[]{:S(2)}) collective-permute-start(f32[2,2,256,128]{3,2,1,0:T(8,128)} %get-tuple-element.38), channel_id=1, source_target_pairs={{0,2},{1,3},{2,0},{3,1},{4,6},{5,7},{6,4},{7,5},{8,10},{9,11},{10,... | collective-permute-start | bytes 1572872 | tf_op jit(solution)/shard_map/ppermute | solution.py:318
  95.3 1.6 copy-start.3
  96.9 2.2 %copy-start.1 = (bf16[2,4,256,512]{3,2,1,0:T(8,128)(2,1)S(1)}, bf16[2,4,256,512]{3,2,1,0:T(8,128)(2,1)}, u32[]{:S(2)}) copy-start(bf16[2,4,256,512]{3,2,1,0:T(8,128)(2,1)} %constant.49.clone.table_ref.refs_3_) | copy-start | bytes 6291460
  96.9 2.2 %copy-start.6 = (f32[2,2,256,128]{3,2,1,0:T(8,128)S(1)}, f32[2,2,256,128]{3,2,1,0:T(8,128)}, u32[]{:S(2)}) copy-start(f32[2,2,256,128]{3,2,1,0:T(8,128)} %copy-done.5) | copy-start | bytes 1572868
  103.3 42.8 %copy-start.4 = (bf16[2,512,1024]{2,1,0:T(8,128)(2,1)S(1)}, bf16[2,512,1024]{2,1,0:T(8,128)(2,1)}, u32[]{:S(2)}) copy-start(bf16[2,512,1024]{2,1,0:T(8,128)(2,1)} %constant.47.clone.table_ref) | copy-start | bytes 6291460

commit v8 on v7

--- a/solution.py
+++ b/solution.py
@@ -36,11 +36,11 @@
     imag_rows = np.concatenate([sine, cosine], 1).reshape(4, 1, 128, 2 * KEPT)
     table_z = np.concatenate([real_rows, imag_rows], 1).reshape(4, 256, 2 * KEPT)
     order = np.arange(KEPT).reshape(KEPT // 2, 2).T.reshape(-1)
-    cosine, sine = cos_sin(np.arange(N), order)
-    cosine, sine = cosine.reshape(4, 128, KEPT), sine.reshape(4, 128, KEPT)
-    top = np.concatenate([cosine, sine], 1)
-    bottom = np.concatenate([-sine, cosine], 1)
-    table_y = np.concatenate([top, bottom], 2).transpose(0, 2, 1)
+    cosine, sine = cos_sin(np.arange(N // 2), order)
+    cosine, sine = (t.T.reshape(2, 128, 2, 128).transpose(2, 0, 1, 3) for t in (cosine, sine))
+    top = np.concatenate([cosine, sine], 3)
+    bottom = np.concatenate([-sine, cosine], 3)
+    table_y = np.concatenate([top, bottom], 2)
     gx, gy, gz = np.meshgrid(np.arange(8), np.arange(4), np.arange(4), indexing="ij")
     first = 64 * gx + 8 * gz + 2 * gy
     second = 64 * gx + 32 + 8 * gy + 2 * gz
@@ -86,60 +86,114 @@
     )
 
 
-def term_of(along_z, piece, table_ref, g):
-    table = (table_ref[0, g], table_ref[1, g])
-    if along_z:
-        return product(rows_z(piece), table)
-    return product(table, columns_y(piece))
-
-
-def sum_kernel(along_z, place_ref, *refs):
-    *pieces, table_ref, out_ref = refs
+def scale_kernel(half, rotated, place_ref, normals_ref, spectrum_ref, *refs):
+    *out_refs, held_n, held_s, semaphores = refs
+
+    def copies(shift):
+        chunk = 4 * half + (lax.rem(place_ref[0] + shift, 4) if rotated else shift)
+        return (
+            pltpu.make_async_copy(
+                normals_ref.at[:, chunk], held_n.at[shift], semaphores.at[shift, 0]
+            ),
+            pltpu.make_async_copy(
+                spectrum_ref.at[chunk], held_s.at[shift], semaphores.at[shift, 1]
+            ),
+        )
+
+    for shift in (1, 3, 2, 0):
+        for copy in copies(shift):
+            copy.start()
+    for shift in (1, 3, 2, 0):
+        for copy in copies(shift):
+            copy.wait()
+        for plane in range(2):
+            values = held_n[shift, plane].astype(jnp.float32) * held_s[shift]
+            if rotated:
+                out_refs[shift][plane] = values
+            else:
+                out_refs[0][shift, plane] = values
+
+
+def scale(half, rotated, place, normals, spectrum):
+    if rotated:
+        out_shape = [jax.ShapeDtypeStruct((2, 8, 128, 128), jnp.float32)] * 4
+    else:
+        out_shape = [jax.ShapeDtypeStruct((4, 2, 8, 128, 128), jnp.float32)]
+    return pl.pallas_call(
+        functools.partial(scale_kernel, half, rotated),
+        in_specs=[pl.BlockSpec(memory_space=pltpu.SMEM)]
+        + [pl.BlockSpec(memory_space=pltpu.HBM)] * 2,
+        out_specs=[pl.BlockSpec(memory_space=pltpu.VMEM)] * len(out_shape),
+        out_shape=out_shape,
+        scratch_shapes=[
+            pltpu.VMEM((4, 2, 8, 128, 128), jnp.bfloat16),
+            pltpu.VMEM((4, 8, 128, 128), jnp.float32),
+            pltpu.SemaphoreType.DMA((4, 2)),
+        ],
+        compiler_params=params(VMEM),
+        cost_estimate=cost(1 << 20, 8 * MIB),
+        name="scale_b" if rotated else "scale_a",
+    )(place, normals.reshape(2, 8, 8, 128, 128), spectrum.reshape(8, 8, 128, 128))
+
+
+def term_of(piece, table_ref, g):
+    return product(rows_z(piece), (table_ref[0, g], table_ref[1, g]))
+
+
+def transform_y(pairs, table_ref):
+    even = odd = None
+    for first, second, g in pairs:
+        base = lax.rem(g, 2)
+        sign = jnp.where(g < 2, 1.0, -1.0).astype(jnp.float32)
+        term = product((table_ref[0, base, 0], table_ref[1, base, 0]), columns_y(first + second))
+        even = term if even is None else even + term
+        term = product(
+            (table_ref[0, base, 1], table_ref[1, base, 1]), columns_y((first - second) * sign)
+        )
+        odd = term if odd is None else odd + term
+    return even, odd
+
+
+def part_z_kernel(place_ref, p0, p1, p3, table_ref, out_ref):
     total = None
-    for shift, piece in zip((0, 1, 3), pieces):
-        g = lax.rem(place_ref[0] + (4 - shift), 4)
-        term = term_of(along_z, piece[...], table_ref, g)
+    for shift, piece in ((0, p0), (1, p1), (3, p3)):
+        term = term_of(piece[...], table_ref, lax.rem(place_ref[0] + (4 - shift), 4))
         total = term if total is None else total + term
     out_ref[0] = total
 
 
-def part_sum(along_z, place, pieces, cells, table):
-    _, count, lines, columns = pieces[0].shape
-    shape = (cells * lines, 512) if along_z else (512, cells * columns)
-    return pl.pallas_call(
-        functools.partial(sum_kernel, along_z),
+def part_z(place, pieces, table):
+    return pl.pallas_call(
+        part_z_kernel,
         grid_spec=pltpu.PrefetchScalarGridSpec(
             num_scalar_prefetch=1,
-            grid=(count // cells,),
-            in_specs=[
-                pl.BlockSpec((2, cells, lines, columns), lambda i, place: (0, i, 0, 0))
-            ]
-            * 3
+            grid=(2,),
+            in_specs=[pl.BlockSpec((2, 1, KEPT, 128), lambda i, place: (0, i, 0, 0))] * 3
             + [pl.BlockSpec(table.shape, lambda i, place: (0, 0, 0, 0))],
-            out_specs=pl.BlockSpec((1,) + shape, lambda i, place: (i, 0, 0)),
+            out_specs=pl.BlockSpec((1, KEPT, 512), lambda i, place: (i, 0, 0)),
         ),
-        out_shape=jax.ShapeDtypeStruct((count // cells,) + shape, jnp.float32),
-        compiler_params=params(VMEM),
-        cost_estimate=cost(count // cells * shape[0] * shape[1] * 768, 8 * MIB),
-        name="part_z" if along_z else "part_y",
+        out_shape=jax.ShapeDtypeStruct((2, KEPT, 512), jnp.float32),
+        compiler_params=params(VMEM),
+        cost_estimate=cost(512 * 512 * 768, 5 * MIB),
+        name="part_z",
     )(place, *pieces, table)
 
 
 def first_y_kernel(place_ref, to_ref, p0, p1, p2, p3, table_ref, *out_refs):
-    total = None
-    for shift, piece in enumerate((p0, p1, p2, p3)):
-        g = lax.rem(place_ref[0] + (4 - shift), 4)
-        term = term_of(False, piece[...], table_ref, g)
-        total = term if total is None else total + term
+    g = place_ref[0]
+    parts = transform_y(
+        [(p0[...], p2[...], g), (p1[...], p3[...], lax.rem(g + 3, 4))], table_ref
+    )
     for step, out_ref in enumerate(out_refs):
 
         @pl.when(pl.program_id(0) == step)
         def _():
-            for plane in range(2):
-                for x in range(2):
-                    out_ref[plane, x] = total[
-                        plane * KEPT : (plane + 1) * KEPT, x * 128 : (x + 1) * 128
-                    ]
+            for parity, values in enumerate(parts):
+                for plane in range(2):
+                    for x in range(2):
+                        out_ref[plane, x, parity * 128 : (parity + 1) * 128] = values[
+                            plane * 128 : (plane + 1) * 128, x * 128 : (x + 1) * 128
+                        ]
 
 
 def first_y(shifts, place, to, pieces, table):
@@ -156,12 +210,12 @@
                 pl.BlockSpec((2, 2, 128, 128), lambda i, place, to: (0, pair(i, to), 0, 0))
             ]
             * 4
-            + [pl.BlockSpec((2, 4, 512, 256), lambda i, place, to: (0, 0, 0, 0))],
+            + [pl.BlockSpec(table.shape, lambda i, place, to: (0, 0, 0, 0, 0))],
             out_specs=[pl.BlockSpec(shape, lambda i, place, to: (0, 0, 0, 0))] * 2,
         ),
         out_shape=[jax.ShapeDtypeStruct(shape, jnp.float32)] * 2,
         compiler_params=params(VMEM),
-        cost_estimate=cost(512 * 1024 * 512, 4 * MIB),
+        cost_estimate=cost(512 * 512 * 512, 4 * MIB),
         name="first_y",
     )(place, to, *pieces, table)
 
@@ -198,11 +252,12 @@
 
 
 def second_y_kernel(p0, p1, p2, p3, table_ref, out_ref):
-    total = None
-    for g, piece in enumerate((p0, p1, p2, p3)):
-        term = term_of(False, piece[0], table_ref, g)
-        total = term if total is None else total + term
-    out_ref[0] = total
+    parts = transform_y([(p0[0], p2[0], 0), (p1[0], p3[0], 1)], table_ref)
+    for parity, values in enumerate(parts):
+        for plane in range(2):
+            out_ref[0, plane, parity * 128 : (parity + 1) * 128] = values[
+                plane * 128 : (plane + 1) * 128
+            ]
 
 
 def second_y(arrived, table):
@@ -213,11 +268,11 @@
         second_y_kernel,
         grid=(2,),
         in_specs=[from_device(g) for g in range(4)]
-        + [pl.BlockSpec((2, 4, 512, 256), lambda i: (0, 0, 0, 0))],
-        out_specs=pl.BlockSpec((1, 512, KEPT), lambda i: (i, 0, 0)),
-        out_shape=jax.ShapeDtypeStruct((2, 512, KEPT), jnp.float32),
-        compiler_params=params(VMEM),
-        cost_estimate=cost(512 * 1024 * 512, 5 * MIB),
+        + [pl.BlockSpec(table.shape, lambda i: (0, 0, 0, 0, 0))],
+        out_specs=pl.BlockSpec((1, 2, KEPT, KEPT), lambda i: (i, 0, 0, 0)),
+        out_shape=jax.ShapeDtypeStruct((2, 2, KEPT, KEPT), jnp.float32),
+        compiler_params=params(VMEM),
+        cost_estimate=cost(512 * 512 * 512, 5 * MIB),
         name="second_y",
     )(arrived, arrived, arrived, arrived, table)
 
@@ -232,7 +287,7 @@
     for x in range(2):
         for plane in range(2):
             put(done_y[x, plane], plane * 4 + x)
-    total = part_ref[...].reshape(256, 512) + term_of(True, last_z[...], table_ref, 0)
+    total = part_ref[...].reshape(256, 512) + term_of(last_z[...], table_ref, 0)
     for x in range(2):
         for plane in range(2):
             put(
@@ -261,7 +316,7 @@
         compiler_params=params(VMEM),
         cost_estimate=cost(128 * 1024 * 512, 8 * MIB),
         name="second",
-    )(gz, done_y.reshape(2, 2, KEPT, KEPT), part, last_z, table)
+    )(gz, done_y, part, last_z, table)
 
 
 def third_kernel(slot_ref, in_ref, table_ref, out_ref, held):
@@ -330,22 +385,11 @@
     gy = lax.axis_index("gy").astype(jnp.int32).reshape(1)
     gz = lax.axis_index("gz").astype(jnp.int32).reshape(1)
 
-    def chunk_b(shift):
-        start = 32 + 8 * lax.rem(gy[0] + shift, 4)
-        return lax.dynamic_slice_in_dim(spectrum, start, 8, 0)[None] * lax.dynamic_slice_in_dim(
-            normals, start, 8, 1
-        ).astype(jnp.float32)
-
-    zero = lax.optimization_barrier(jnp.int32(0))
-    a = lax.dynamic_slice_in_dim(spectrum, zero, 32, 0).reshape(
-        4, 1, 8, 128, 128
-    ) * lax.dynamic_slice_in_dim(normals, zero, 32, 1).astype(jnp.float32).reshape(
-        2, 4, 8, 128, 128
-    ).transpose(1, 0, 2, 3, 4)
-    a, normals, spectrum = lax.optimization_barrier((a, normals, spectrum))
+    (a,) = scale(0, False, gz, normals, spectrum)
+    a, place = lax.optimization_barrier((a, gy))
     a = lax.all_to_all(a, "gz", split_axis=0, concat_axis=0, tiled=True)
-    b1, b3, b2 = shifted(chunk_b(1), "gy", 1), shifted(chunk_b(3), "gy", 3), shifted(chunk_b(2), "gy", 2)
-    b0 = chunk_b(0)
+    b0, b1, b2, b3 = scale(1, True, place, normals, spectrum)
+    b1, b3, b2 = shifted(b1, "gy", 1), shifted(b3, "gy", 3), shifted(b2, "gy", 2)
 
     a, slots = lax.optimization_barrier((a, slots_of(block_owner)))
     a = first_z(a, table_z)
@@ -359,7 +403,7 @@
 
     a = second_y(a, table_y)
     a, b1, b3 = lax.optimization_barrier((a, b1, b3))
-    part_b = part_sum(True, gz, (b0, b1, b3), 1, table_z)
+    part_b = part_z(gz, (b0, b1, b3), table_z)
     part_b, b2 = lax.optimization_barrier((part_b, b2))
     planes = second(gz, a, part_b, b2, table_z)
     lines = lax.all_to_all(planes, ALL, split_axis=0, concat_axis=0, tiled=True)

time: 187 us -> 188 us (level)
  other arithmetic: 6.28 us -> 0.63 us
  local copies, waits for them, and re-layouts: 12.1 us -> 15.5 us
    unnamed x23 -> x29, local copies, waits for them, and re-layouts: 7.88 us -> 15.3 us
    mul x2 -> x0, other arithmetic: 4.61 us -> none  [the longest x1 2.69 us: per_device(): lax.dynamic_slice_in_dim(spectrum, zero, 32, 0).reshape(4, 1, 8, 128, 128)]
    dynamic_slice x3 -> x0, local copies, waits for them, and re-layouts: 3.99 us -> none  [the longest x1 1.98 us: per_device(): lax.dynamic_slice_in_dim(normals, zero, 32, 1).astype(jnp.float32)]
    pallas_call x1 -> x3, Pallas kernels: 2.65 us -> 5.73 us  [the longest x2 3.1 us: scale(): pl.pallas_call(functools.partial(scale_kernel, half, rotated), in_specs=[...]
    all_to_all x1, waiting for transfers between devices: 37.7 us -> 35.3 us  [per_device(): a = lax.all_to_all(a, 'gz', split_axis=0, concat_axis=0, tiled=True)]
    all_to_all x1, waiting for transfers between devices: 11.2 us -> 13.2 us  [per_device(): a = lax.all_to_all(a, 'gy', split_axis=0, concat_axis=0, tiled=True)]
  transfers between devices with their start and end apart: 8 -> 8, of which waited for: 2 -> 3; matrix products, arithmetic and copies ran while one was open for 3% -> 0% of each run, Pallas kernels for 10% -> 10%
where the time goes in v8:
time: 188 us
  blocking collectives  77.8 us (41%)
  waiting for transfers between devices  48.6 us (26%)
  Pallas kernels  26.9 us (14%)
  starting transfers between devices  17.9 us (10%)
  local copies, waits for them, and re-layouts  15.5 us (8%)
    all_to_all x1, blocking collectives, per_device(): lines = lax.all_to_all(planes, ALL, split_axis=0, concat_axis=0, tiled=True)  43.6 us
    all_to_all x1, waiting for transfers between devices, per_device(): a = lax.all_to_all(a, 'gz', split_axis=0, concat_axis=0, tiled=True)  35.3 us
    all_to_all x1, blocking collectives, per_device(): lax.all_to_all(outgoing.reshape(128, 1, CAP, 2, BW), ALL, split_axis=0, c...  34.2 us
    unnamed x29, local copies, waits for them, and re-layouts  15.3 us
    all_to_all x1, waiting for transfers between devices, per_device(): a = lax.all_to_all(a, 'gy', split_axis=0, concat_axis=0, tiled=True)  13.2 us
    ppermute x6, starting transfers between devices, shifted(): lax.ppermute(piece, axis, [(i, (i + shift) % size) for i in range(size)])  7.68 us
    pallas_call x2, Pallas kernels, first_y(): pl.pallas_call(first_y_kernel, grid_spec=pltpu.PrefetchScalarGridSpec(num...  6.73 us
    pallas_call x1, Pallas kernels, first_z(): pl.pallas_call(first_z_kernel, grid=(2,), in_specs=[from_device(g) for g...  6.16 us
  transfers between devices with their start and end apart: 8, of which 3 were waited for; matrix products, arithmetic and copies ran while one was open for 0% of the time, Pallas kernels for 10%

profile of v8, /device:TPU:1, one launch (start us, length us, event | category | flops | bytes accessed | tf_op | source)
XLA Modules:
  0.0 187.5 jit_solution(10547421583089498071)
XLA Ops:
  0.0 2.2 %copy-done.2 = bf16[2,64,128,128]{3,2,1,0:T(8,128)(2,1)S(1)} copy-done((bf16[2,64,128,128]{3,2,1,0:T(8,128)(2,1)S(1)}, bf16[2,64,128,128]{3,2,1,0:T(8,128)(2,1)}, u32[]{:S(2)}) %copy-start.2) | copy-done | bytes 4194328
  2.2 2.2 %copy-done.4 = f32[64,128,128]{2,1,0:T(8,128)S(1)} copy-done((f32[64,128,128]{2,1,0:T(8,128)S(1)}, f32[64,128,128]{2,1,0:T(8,128)}, u32[]{:S(2)}) %copy-start.4) | copy-done | bytes 4194328
  4.4 0.7 scale_a.1
  5.1 0.0 copy-start.6
  5.1 2.0 %copy-done.6 = f32[4,2,8,128,128]{4,3,2,1,0:T(8,128)} copy-done((f32[4,2,8,128,128]{4,3,2,1,0:T(8,128)}, f32[4,2,8,128,128]{4,3,2,1,0:T(8,128)S(1)}, u32[]{:S(2)}) %copy-start.6) | copy-done | bytes 4194328
  7.1 5.9 %all-to-all-start = ((f32[4,2,8,128,128]{4,3,2,1,0:T(8,128)}), f32[4,2,8,128,128]{4,3,2,1,0:T(8,128)}, u32[]{:S(2)}, u32[]{:S(2)}) async-start(f32[4,2,8,128,128]{4,3,2,1,0:T(8,128)} %copy-done.6), calls=%async_computation | async-start | bytes 8388608 | tf_op jit(solution)/shard_map/all_to_all | solution.py:390
  12.9 2.2 %copy-done.3 = bf16[2,64,128,128]{3,2,1,0:T(8,128)(2,1)S(1)} copy-done((bf16[2,64,128,128]{3,2,1,0:T(8,128)(2,1)S(1)}, bf16[2,64,128,128]{3,2,1,0:T(8,128)(2,1)}, u32[]{:S(2)}) %copy-start.3) | copy-done | bytes 4194328
  15.1 2.2 %copy-done.5 = f32[64,128,128]{2,1,0:T(8,128)S(1)} copy-done((f32[64,128,128]{2,1,0:T(8,128)S(1)}, f32[64,128,128]{2,1,0:T(8,128)}, u32[]{:S(2)}) %copy-start.5) | copy-done | bytes 4194328
  17.3 2.4 %scale_b.1 = (f32[2,8,128,128]{3,2,1,0:T(8,128)S(1)}, f32[2,8,128,128]{3,2,1,0:T(8,128)}, f32[2,8,128,128]{3,2,1,0:T(8,128)}, f32[2,8,128,128]{3,2,1,0:T(8,128)}) custom-call(s32[1]{0:T(128)} %bitcast.3.place_ref, bf16[2,8,8,128,128]{4,3,2,1,0:T(8,128)(2,1)S(1)} %bitcast.21, f32[8,8,128,128]{3,2,1,0:T(8,128)S(1)} %bitcast.23), custom_call_target="tpu_custom_call" | custom-call | flops 6291456 | bytes 8388608 | tf_op jit(solution)/shard_map/scale_b/pallas_call | solution.py:122
  19.7 0.0 copy-start.8
  19.7 1.0 copy-done.8
  20.7 1.3 collective-permute-start
  22.0 2.6 %collective-permute-start.1 = (f32[2,8,128,128]{3,2,1,0:T(8,128)}, f32[2,8,128,128]{3,2,1,0:T(8,128)}, u32[]{:S(2)}, u32[]{:S(2)}) collective-permute-start(f32[2,8,128,128]{3,2,1,0:T(8,128)} %get-tuple-element.32), channel_id=1, source_target_pairs={{0,8},{4,12},{8,0},{12,4},{1,9},{5,13},{9,1},{13,5},{2,10},{6,14},... | collective-permute-start | bytes 3145736 | tf_op jit(solution)/shard_map/ppermute | solution.py:373
  24.6 1.1 collective-permute-start.2
  25.7 0.0 copy-done.13
  25.7 0.1 copy.10
  25.8 0.2 fusion.2
  26.1 0.1 copy.11
  26.2 0.4 fusion.1
  26.6 35.3 %all-to-all-done.p0.p1.p2.p3 = f32[4,2,8,128,128]{4,3,2,1,0:T(8,128)} async-done(((f32[4,2,8,128,128]{4,3,2,1,0:T(8,128)}), f32[4,2,8,128,128]{4,3,2,1,0:T(8,128)}, u32[]{:S(2)}, u32[]{:S(2)}) %all-to-all-start) | async-done | bytes 4194336 | tf_op jit(solution)/shard_map/all_to_all | solution.py:390
  61.8 0.0 copy-done
  61.9 6.2 %first_z.1 = f32[4,2,2,128,256]{4,3,2,1,0:T(8,128)} custom-call(f32[4,2,8,128,128]{4,3,2,1,0:T(8,128)} %all-to-all-done.p0.p1.p2.p3, f32[4,2,8,128,128]{4,3,2,1,0:T(8,128)} %all-to-all-done.p0.p1.p2.p3, f32[4,2,8,128,128]{4,3,2,1,0:T(8,128)} %all-to-all-done.p0.p1.p2.p3, f32[4,2,8,128,128]{4,3,2,1,0:T(8,128)} %all-to-all-done.p0.p1.p2.p3, ...), custom_call_target="tpu_custom_call" | custom-call | flops 3221225472 | bytes 8388608 | tf_op jit(solution)/shard_map/first_z/pallas_call | solution.py:241
  68.0 4.3 %all-to-all-start.1 = ((f32[4,2,2,128,256]{4,3,2,1,0:T(8,128)}), f32[4,2,2,128,256]{4,3,2,1,0:T(8,128)S(1)}, u32[]{:S(2)}, u32[]{:S(2)}) async-start(f32[4,2,2,128,256]{4,3,2,1,0:T(8,128)} %first_z.1), calls=%async_computation.1 | async-start | bytes 4194304 | tf_op jit(solution)/shard_map/all_to_all | solution.py:397
  72.3 0.0 collective-permute-done.p1
  72.3 0.0 collective-permute-done.1.p2
  72.3 0.0 collective-permute-done.2.p3
  72.4 1.2 copy-done.9
  73.6 3.5 %first_y.2 = (f32[2,2,256,128]{3,2,1,0:T(8,128)}, f32[2,2,256,128]{3,2,1,0:T(8,128)}) custom-call(s32[1]{0:T(128)} %bitcast.3.place_ref, s32[1]{0:T(128)} %bitcast.place_ref.to_ref.gz_ref, f32[2,8,128,128]{3,2,1,0:T(8,128)S(1)} %copy-done.9, f32[2,8,128,128]{3,2,1,0:T(8,128)} %collective-permute-done.p1, f32[2,8,128,128]{3,2,1,0:T(8,128)} %collective-permute-done.1.p2, ...), custom_call_target="tpu_custom_call" | custom-call | flops 805306368 | bytes 4194304 | tf_op jit(solution)/shard_map/first_y/pallas_call | solution.py:204
  77.1 0.9 collective-permute-start.3
  78.0 1.8 collective-permute-start.4
  79.7 3.3 %first_y.3 = (f32[2,2,256,128]{3,2,1,0:T(8,128)}, f32[2,2,256,128]{3,2,1,0:T(8,128)S(1)}) custom-call(s32[1]{0:T(128)} %bitcast.3.place_ref, s32[1]{0:T(128)} %bitcast.place_ref.to_ref.gz_ref, f32[2,8,128,128]{3,2,1,0:T(8,128)S(1)} %copy-done.9, f32[2,8,128,128]{3,2,1,0:T(8,128)} %collective-permute-done.p1, f32[2,8,128,128]{3,2,1,0:T(8,128)} %collective-permute-done.1.p2, ...), custom_call_target="tpu_custom_call" | custom-call | flops 805306368 | bytes 4194304 | tf_op jit(solution)/shard_map/first_y/pallas_call | solution.py:204
  83.0 0.8 copy-done.11
  83.8 0.0 collective-permute-start.5
  83.8 13.2 %all-to-all-done.1.p0.p1.p2.p3 = f32[4,2,2,128,256]{4,3,2,1,0:T(8,128)S(1)} async-done(((f32[4,2,2,128,256]{4,3,2,1,0:T(8,128)}), f32[4,2,2,128,256]{4,3,2,1,0:T(8,128)S(1)}, u32[]{:S(2)}, u32[]{:S(2)}) %all-to-all-start.1) | async-done | bytes 2097184 | tf_op jit(solution)/shard_map/all_to_all | solution.py:397
  97.0 1.4 second_y.1.done_y
  98.4 0.0 collective-permute-done.3.p1
  98.4 0.0 collective-permute-done.4.p3
  98.4 0.1 copy-done.1
  98.6 0.1 copy-done.12
  98.6 2.6 %part_z.1.part_ref = f32[2,256,512]{2,1,0:T(8,128)S(1)} custom-call(s32[1]{0:T(128)} %bitcast.place_ref.to_ref.gz_ref, f32[2,2,256,128]{3,2,1,0:T(8,128)S(1)} %copy-done.12, f32[2,2,256,128]{3,2,1,0:T(8,128)} %collective-permute-done.3.p1, f32[2,2,256,128]{3,2,1,0:T(8,128)} %collective-permute-done.4.p3, bf16[2,4,256,512]{3,2,1,0:T(8,128)(2,1)S(1)} %copy-done.1), custom_call_target="tpu_custom_call" | custom-call | flops 1207959552 | bytes 5242880 | tf_op jit(solution)/shard_map/part_z/pallas_call | solution.py:166
  101.3 0.2 collective-permute-done.5.last_z
  101.4 2.3 %second.1 = f32[128,2,2,8,128]{4,3,2,1,0:T(8,128)S(1)} custom-call(s32[1]{0:T(128)} %bitcast.place_ref.to_ref.gz_ref, f32[2,2,256,256]{3,2,1,0:T(8,128)S(1)} %second_y.1.done_y, f32[2,256,512]{2,1,0:T(8,128)S(1)} %part_z.1.part_ref, f32[2,2,256,128]{3,2,1,0:T(8,128)} %collective-permute-done.5.last_z, bf16[2,4,256,512]{3,2,1,0:T(8,128)(2,1)S(1)} %copy-done.1), custom_call_target="tpu_custom_call" | custom-call | flops 402653184 | bytes 8388608 | tf_op jit(solution)/shard_map/second/pallas_call | solution.py:301
  103.8 0.0 copy-start.10
  103.8 43.6 %all_to_all.27.in_ref = f32[128,2,2,8,128]{4,3,2,1,0:T(8,128)S(1)} all-to-all(f32[128,2,2,8,128]{4,3,2,1,0:T(8,128)S(1)} %second.1), channel_id=1, replica_groups=mesh['gx'=8,'gy'=4,'gz'=4] {'gx','gy','gz'}, dimensions={0} | all-to-all | bytes 4194304 | tf_op jit(solution)/shard_map/all_to_all | solution.py:409
  147.4 0.0 copy-done.10
  147.4 4.5 %third.1 = f32[4096,128]{1,0:T(8,128)S(1)} custom-call(s32[1024]{0:T(1024)S(1)} %multiply_add_fusion.slot_ref, f32[128,2,2,8,128]{4,3,2,1,0:T(8,128)S(1)} %all_to_all.27.in_ref, bf16[2,512,1024]{2,1,0:T(8,128)(2,1)S(1)} %copy-done.10), custom_call_target="tpu_custom_call" | custom-call | flops 1610612736 | bytes 6291456 | tf_op jit(solution)/shard_map/third/pallas_call | solution.py:352
  152.0 34.2 %all_to_all.28 = f32[128,1,16,2,128]{4,3,2,1,0:T(2,128)S(1)} all-to-all(f32[128,1,16,2,128]{4,3,2,1,0:T(2,128)S(1)} %bitcast.24), channel_id=1, replica_groups=mesh['gx'=8,'gy'=4,'gz'=4] {'gx','gy','gz'}, dimensions={0} | all-to-all | bytes 4194304 | tf_op jit(solution)/shard_map/all_to_all | solution.py:411
  186.2 1.3 copy.14
  (17 shorter events, 0.1 us)
Async XLA Ops:
  0.0 2.2 %copy-start.2 = (bf16[2,64,128,128]{3,2,1,0:T(8,128)(2,1)S(1)}, bf16[2,64,128,128]{3,2,1,0:T(8,128)(2,1)}, u32[]{:S(2)}) copy-start(bf16[2,64,128,128]{3,2,1,0:T(8,128)(2,1)} %param.6) | copy-start | bytes 12582916
  2.2 2.2 %copy-start.4 = (f32[64,128,128]{2,1,0:T(8,128)S(1)}, f32[64,128,128]{2,1,0:T(8,128)}, u32[]{:S(2)}) copy-start(f32[64,128,128]{2,1,0:T(8,128)} %param.7) | copy-start | bytes 12582916
  5.1 2.0 %copy-start.6 = (f32[4,2,8,128,128]{4,3,2,1,0:T(8,128)}, f32[4,2,8,128,128]{4,3,2,1,0:T(8,128)S(1)}, u32[]{:S(2)}) copy-start(f32[4,2,8,128,128]{4,3,2,1,0:T(8,128)S(1)} %scale_a.1) | copy-start | bytes 12582916
  7.1 54.8 %all-to-all-start = ((f32[4,2,8,128,128]{4,3,2,1,0:T(8,128)}), f32[4,2,8,128,128]{4,3,2,1,0:T(8,128)}, u32[]{:S(2)}, u32[]{:S(2)}) async-start(f32[4,2,8,128,128]{4,3,2,1,0:T(8,128)} %copy-done.6), calls=%async_computation | async-start | bytes 8388608 | tf_op jit(solution)/shard_map/all_to_all | solution.py:390
  12.9 2.2 %copy-start.3 = (bf16[2,64,128,128]{3,2,1,0:T(8,128)(2,1)S(1)}, bf16[2,64,128,128]{3,2,1,0:T(8,128)(2,1)}, u32[]{:S(2)}) copy-start(bf16[2,64,128,128]{3,2,1,0:T(8,128)(2,1)} %param.6) | copy-start | bytes 12582916
  15.1 2.2 %copy-start.5 = (f32[64,128,128]{2,1,0:T(8,128)S(1)}, f32[64,128,128]{2,1,0:T(8,128)}, u32[]{:S(2)}) copy-start(f32[64,128,128]{2,1,0:T(8,128)} %param.7) | copy-start | bytes 12582916
  17.3 8.4 %copy-start.13 = (s32[1024,1]{0,1:T(1,128)S(1)}, s32[1024,1]{0,1:T(1,128)}, u32[]{:S(2)}) copy-start(s32[1024,1]{0,1:T(1,128)} %param.8) | copy-start | bytes 12292
  19.7 1.0 copy-start.8
  20.7 41.1 %copy-start = (bf16[2,4,256,512]{3,2,1,0:T(8,128)(2,1)S(1)}, bf16[2,4,256,512]{3,2,1,0:T(8,128)(2,1)}, u32[]{:S(2)}) copy-start(bf16[2,4,256,512]{3,2,1,0:T(8,128)(2,1)} %constant.23.clone.table_ref) | copy-start | bytes 6291460
  20.7 51.6 %collective-permute-start = (f32[2,8,128,128]{3,2,1,0:T(8,128)}, f32[2,8,128,128]{3,2,1,0:T(8,128)}, u32[]{:S(2)}, u32[]{:S(2)}) collective-permute-start(f32[2,8,128,128]{3,2,1,0:T(8,128)} %get-tuple-element.31), channel_id=1, source_target_pairs={{0,4},{4,8},{8,12},{12,0},{1,5},{5,9},{9,13},{13,1},{2,6},{6,10},{... | collective-permute-start | bytes 3145736 | tf_op jit(solution)/shard_map/ppermute | solution.py:373
  22.0 50.3 %collective-permute-start.1 = (f32[2,8,128,128]{3,2,1,0:T(8,128)}, f32[2,8,128,128]{3,2,1,0:T(8,128)}, u32[]{:S(2)}, u32[]{:S(2)}) collective-permute-start(f32[2,8,128,128]{3,2,1,0:T(8,128)} %get-tuple-element.32), channel_id=1, source_target_pairs={{0,8},{4,12},{8,0},{12,4},{1,9},{5,13},{9,1},{13,5},{2,10},{6,14},... | collective-permute-start | bytes 3145736 | tf_op jit(solution)/shard_map/ppermute | solution.py:373
  24.6 47.7 %collective-permute-start.2 = (f32[2,8,128,128]{3,2,1,0:T(8,128)}, f32[2,8,128,128]{3,2,1,0:T(8,128)}, u32[]{:S(2)}, u32[]{:S(2)}) collective-permute-start(f32[2,8,128,128]{3,2,1,0:T(8,128)} %get-tuple-element.33), channel_id=1, source_target_pairs={{0,12},{4,0},{8,4},{12,8},{1,13},{5,1},{9,5},{13,9},{2,14},{6,2},{... | collective-permute-start | bytes 3145736 | tf_op jit(solution)/shard_map/ppermute | solution.py:373
  68.0 4.3 %copy-start.7 = (bf16[2,2,2,256,256]{4,3,2,1,0:T(8,128)(2,1)S(1)}, bf16[2,2,2,256,256]{4,3,2,1,0:T(8,128)(2,1)}, u32[]{:S(2)}) copy-start(bf16[2,2,2,256,256]{4,3,2,1,0:T(8,128)(2,1)} %constant.22.clone.table_ref) | copy-start | bytes 3145732
  68.0 29.0 %all-to-all-start.1 = ((f32[4,2,2,128,256]{4,3,2,1,0:T(8,128)}), f32[4,2,2,128,256]{4,3,2,1,0:T(8,128)S(1)}, u32[]{:S(2)}, u32[]{:S(2)}) async-start(f32[4,2,2,128,256]{4,3,2,1,0:T(8,128)} %first_z.1), calls=%async_computation.1 | async-start | bytes 4194304 | tf_op jit(solution)/shard_map/all_to_all | solution.py:397
  72.4 1.2 copy-start.9
  77.1 21.4 %collective-permute-start.3 = (f32[2,2,256,128]{3,2,1,0:T(8,128)}, f32[2,2,256,128]{3,2,1,0:T(8,128)}, u32[]{:S(2)}, u32[]{:S(2)}) collective-permute-start(f32[2,2,256,128]{3,2,1,0:T(8,128)} %get-tuple-element.38), channel_id=1, source_target_pairs={{0,1},{1,2},{2,3},{3,0},{4,5},{5,6},{6,7},{7,4},{8,9},{9,10},{10,1... | collective-permute-start | bytes 1572872 | tf_op jit(solution)/shard_map/ppermute | solution.py:373
  78.0 20.5 %collective-permute-start.4 = (f32[2,2,256,128]{3,2,1,0:T(8,128)}, f32[2,2,256,128]{3,2,1,0:T(8,128)}, u32[]{:S(2)}, u32[]{:S(2)}) collective-permute-start(f32[2,2,256,128]{3,2,1,0:T(8,128)} %get-tuple-element.39), channel_id=1, source_target_pairs={{0,3},{1,0},{2,1},{3,2},{4,7},{5,4},{6,5},{7,6},{8,11},{9,8},{10,9... | collective-permute-start | bytes 1572872 | tf_op jit(solution)/shard_map/ppermute | solution.py:373
  83.0 0.8 copy-start.11
  83.8 17.6 %collective-permute-start.5 = (f32[2,2,256,128]{3,2,1,0:T(8,128)}, f32[2,2,256,128]{3,2,1,0:T(8,128)}, u32[]{:S(2)}, u32[]{:S(2)}) collective-permute-start(f32[2,2,256,128]{3,2,1,0:T(8,128)} %get-tuple-element.44), channel_id=1, source_target_pairs={{0,2},{1,3},{2,0},{3,1},{4,6},{5,7},{6,4},{7,5},{8,10},{9,11},{10,... | collective-permute-start | bytes 1572872 | tf_op jit(solution)/shard_map/ppermute | solution.py:373
  97.0 1.6 copy-start.1
  97.0 1.7 copy-start.12
  103.8 43.6 %copy-start.10 = (bf16[2,512,1024]{2,1,0:T(8,128)(2,1)S(1)}, bf16[2,512,1024]{2,1,0:T(8,128)(2,1)}, u32[]{:S(2)}) copy-start(bf16[2,512,1024]{2,1,0:T(8,128)(2,1)} %constant.21.clone.table_ref) | copy-start | bytes 6291460

commit v9 on v8

--- a/solution.py
+++ b/solution.py
@@ -87,7 +87,7 @@
 
 
 def scale_kernel(half, rotated, place_ref, normals_ref, spectrum_ref, *refs):
-    *out_refs, held_n, held_s, semaphores = refs
+    *out_refs, held_n, held_s, held_out, semaphores = refs
 
     def copies(shift):
         chunk = 4 * half + (lax.rem(place_ref[0] + shift, 4) if rotated else shift)
@@ -100,6 +100,10 @@
             ),
         )
 
+    def result(shift):
+        target = out_refs[shift] if rotated else out_refs[0].at[shift]
+        return pltpu.make_async_copy(held_out.at[shift], target, semaphores.at[shift, 2])
+
     for shift in (1, 3, 2, 0):
         for copy in copies(shift):
             copy.start()
@@ -107,30 +111,30 @@
         for copy in copies(shift):
             copy.wait()
         for plane in range(2):
-            values = held_n[shift, plane].astype(jnp.float32) * held_s[shift]
-            if rotated:
-                out_refs[shift][plane] = values
-            else:
-                out_refs[0][shift, plane] = values
+            held_out[shift, plane] = held_n[shift, plane].astype(jnp.float32) * held_s[shift]
+        result(shift).start()
+    for shift in (1, 3, 2, 0):
+        result(shift).wait()
 
 
 def scale(half, rotated, place, normals, spectrum):
     if rotated:
-        out_shape = [jax.ShapeDtypeStruct((2, 8, 128, 128), jnp.float32)] * 4
+        out_shape = [pltpu.HBM((2, 8, 128, 128), jnp.float32)] * 4
     else:
-        out_shape = [jax.ShapeDtypeStruct((4, 2, 8, 128, 128), jnp.float32)]
+        out_shape = [pltpu.HBM((4, 2, 8, 128, 128), jnp.float32)]
     return pl.pallas_call(
         functools.partial(scale_kernel, half, rotated),
         in_specs=[pl.BlockSpec(memory_space=pltpu.SMEM)]
         + [pl.BlockSpec(memory_space=pltpu.HBM)] * 2,
-        out_specs=[pl.BlockSpec(memory_space=pltpu.VMEM)] * len(out_shape),
+        out_specs=[pl.BlockSpec(memory_space=pltpu.HBM)] * len(out_shape),
         out_shape=out_shape,
         scratch_shapes=[
             pltpu.VMEM((4, 2, 8, 128, 128), jnp.bfloat16),
             pltpu.VMEM((4, 8, 128, 128), jnp.float32),
-            pltpu.SemaphoreType.DMA((4, 2)),
+            pltpu.VMEM((4, 2, 8, 128, 128), jnp.float32),
+            pltpu.SemaphoreType.DMA((4, 3)),
         ],
-        compiler_params=params(VMEM),
+        compiler_params=params(60),
         cost_estimate=cost(1 << 20, 8 * MIB),
         name="scale_b" if rotated else "scale_a",
     )(place, normals.reshape(2, 8, 8, 128, 128), spectrum.reshape(8, 8, 128, 128))
@@ -213,7 +217,7 @@
             + [pl.BlockSpec(table.shape, lambda i, place, to: (0, 0, 0, 0, 0))],
             out_specs=[pl.BlockSpec(shape, lambda i, place, to: (0, 0, 0, 0))] * 2,
         ),
-        out_shape=[jax.ShapeDtypeStruct(shape, jnp.float32)] * 2,
+        out_shape=[pltpu.HBM(shape, jnp.float32)] * 2,
         compiler_params=params(VMEM),
         cost_estimate=cost(512 * 512 * 512, 4 * MIB),
         name="first_y",

time: 188 us -> 184 us (0.979)
  local copies, waits for them, and re-layouts: 15.5 us -> 2.98 us
  waiting for transfers between devices: 48.6 us -> 53.4 us
  Pallas kernels: 26.9 us -> 30.8 us
    unnamed x29 -> x15, local copies, waits for them, and re-layouts: 15.3 us -> 2.77 us
    all_to_all x1, waiting for transfers between devices: 35.3 us -> 39.6 us  [per_device(): a = lax.all_to_all(a, 'gz', split_axis=0, concat_axis=0, tiled=True)]
    pallas_call x2, Pallas kernels: 3.1 us -> 6.83 us  [scale(): pl.pallas_call(functools.partial(scale_kernel, half, rotated), in_specs=[...]
  transfers between devices with their start and end apart: 8 -> 8, of which waited for: 3 -> 2; matrix products, arithmetic and copies ran while one was open for 0% -> 0% of each run, Pallas kernels for 10% -> 11%
where the time goes in v9:
time: 184 us
  blocking collectives  78 us (42%)
  waiting for transfers between devices  53.4 us (29%)
  Pallas kernels  30.8 us (17%)
  starting transfers between devices  17.9 us (10%)
  local copies, waits for them, and re-layouts  2.98 us (2%)
    all_to_all x1, blocking collectives, per_device(): lines = lax.all_to_all(planes, ALL, split_axis=0, concat_axis=0, tiled=True)  43.7 us
    all_to_all x1, waiting for transfers between devices, per_device(): a = lax.all_to_all(a, 'gz', split_axis=0, concat_axis=0, tiled=True)  39.6 us
    all_to_all x1, blocking collectives, per_device(): lax.all_to_all(outgoing.reshape(128, 1, CAP, 2, BW), ALL, split_axis=0, c...  34.2 us
    all_to_all x1, waiting for transfers between devices, per_device(): a = lax.all_to_all(a, 'gy', split_axis=0, concat_axis=0, tiled=True)  13.8 us
    ppermute x6, starting transfers between devices, shifted(): lax.ppermute(piece, axis, [(i, (i + shift) % size) for i in range(size)])  7.75 us
    pallas_call x2, Pallas kernels, first_y(): pl.pallas_call(first_y_kernel, grid_spec=pltpu.PrefetchScalarGridSpec(num...  6.89 us
    pallas_call x2, Pallas kernels, scale(): pl.pallas_call(functools.partial(scale_kernel, half, rotated), in_specs=[...  6.83 us
    pallas_call x1, Pallas kernels, first_z(): pl.pallas_call(first_z_kernel, grid=(2,), in_specs=[from_device(g) for g...  6.17 us
  transfers between devices with their start and end apart: 8, of which 2 were waited for; matrix products, arithmetic and copies ran while one was open for 0% of the time, Pallas kernels for 11%

profile of v9, /device:TPU:1, one launch (start us, length us, event | category | flops | bytes accessed | tf_op | source)
XLA Modules:
  0.0 183.9 jit_solution(4700293737152171211)
XLA Ops:
  0.0 3.4 %scale_a.1 = f32[4,2,8,128,128]{4,3,2,1,0:T(8,128)} custom-call(s32[1]{0:T(128)} %bitcast.place_ref.to_ref.gz_ref, bf16[2,8,8,128,128]{4,3,2,1,0:T(8,128)(2,1)} %bitcast.21, f32[8,8,128,128]{3,2,1,0:T(8,128)} %bitcast.23), custom_call_target="tpu_custom_call" | custom-call | flops 6291456 | bytes 8388608 | tf_op jit(solution)/shard_map/scale_a/pallas_call | solution.py:125
  3.4 5.9 %all-to-all-start = ((f32[4,2,8,128,128]{4,3,2,1,0:T(8,128)}), f32[4,2,8,128,128]{4,3,2,1,0:T(8,128)}, u32[]{:S(2)}, u32[]{:S(2)}) async-start(f32[4,2,8,128,128]{4,3,2,1,0:T(8,128)} %scale_a.1), calls=%async_computation | async-start | bytes 8388608 | tf_op jit(solution)/shard_map/all_to_all | solution.py:394
  9.3 0.0 copy-start.6
  9.3 3.4 %scale_b.1 = (f32[2,8,128,128]{3,2,1,0:T(8,128)}, f32[2,8,128,128]{3,2,1,0:T(8,128)}, f32[2,8,128,128]{3,2,1,0:T(8,128)}, f32[2,8,128,128]{3,2,1,0:T(8,128)}) custom-call(s32[1]{0:T(128)} %bitcast.3.place_ref, bf16[2,8,8,128,128]{4,3,2,1,0:T(8,128)(2,1)} %bitcast.22, f32[8,8,128,128]{3,2,1,0:T(8,128)} %bitcast.24), custom_call_target="tpu_custom_call" | custom-call | flops 6291456 | bytes 8388608 | tf_op jit(solution)/shard_map/scale_b/pallas_call | solution.py:125
  12.7 0.0 copy-start
  12.7 1.4 collective-permute-start
  14.1 2.6 %collective-permute-start.1 = (f32[2,8,128,128]{3,2,1,0:T(8,128)}, f32[2,8,128,128]{3,2,1,0:T(8,128)}, u32[]{:S(2)}, u32[]{:S(2)}) collective-permute-start(f32[2,8,128,128]{3,2,1,0:T(8,128)} %get-tuple-element.32), channel_id=1, source_target_pairs={{0,8},{4,12},{8,0},{12,4},{1,9},{5,13},{9,1},{13,5},{2,10},{6,14},... | collective-permute-start | bytes 3145736 | tf_op jit(solution)/shard_map/ppermute | solution.py:377
  16.7 1.1 collective-permute-start.2
  17.8 0.0 copy-done.6
  17.8 0.1 copy.10
  17.9 0.2 fusion.2
  18.2 0.1 copy.11
  18.3 0.4 fusion.1
  18.7 39.6 %all-to-all-done.p0.p1.p2.p3 = f32[4,2,8,128,128]{4,3,2,1,0:T(8,128)} async-done(((f32[4,2,8,128,128]{4,3,2,1,0:T(8,128)}), f32[4,2,8,128,128]{4,3,2,1,0:T(8,128)}, u32[]{:S(2)}, u32[]{:S(2)}) %all-to-all-start) | async-done | bytes 4194336 | tf_op jit(solution)/shard_map/all_to_all | solution.py:394
  58.2 0.0 copy-done
  58.2 6.2 %first_z.1 = f32[4,2,2,128,256]{4,3,2,1,0:T(8,128)} custom-call(f32[4,2,8,128,128]{4,3,2,1,0:T(8,128)} %all-to-all-done.p0.p1.p2.p3, f32[4,2,8,128,128]{4,3,2,1,0:T(8,128)} %all-to-all-done.p0.p1.p2.p3, f32[4,2,8,128,128]{4,3,2,1,0:T(8,128)} %all-to-all-done.p0.p1.p2.p3, f32[4,2,8,128,128]{4,3,2,1,0:T(8,128)} %all-to-all-done.p0.p1.p2.p3, ...), custom_call_target="tpu_custom_call" | custom-call | flops 3221225472 | bytes 8388608 | tf_op jit(solution)/shard_map/first_z/pallas_call | solution.py:245
  64.4 0.0 copy-start.2
  64.4 4.3 %all-to-all-start.1 = ((f32[4,2,2,128,256]{4,3,2,1,0:T(8,128)}), f32[4,2,2,128,256]{4,3,2,1,0:T(8,128)S(1)}, u32[]{:S(2)}, u32[]{:S(2)}) async-start(f32[4,2,2,128,256]{4,3,2,1,0:T(8,128)} %first_z.1), calls=%async_computation.1 | async-start | bytes 4194304 | tf_op jit(solution)/shard_map/all_to_all | solution.py:401
  68.7 0.0 collective-permute-done.p1
  68.7 0.0 collective-permute-done.1.p2
  68.7 0.0 collective-permute-done.2.p3
  68.7 0.0 copy-done.2
  68.7 0.0 copy-start.3
  68.7 1.2 copy-done.3
  69.9 3.4 %first_y.2 = (f32[2,2,256,128]{3,2,1,0:T(8,128)}, f32[2,2,256,128]{3,2,1,0:T(8,128)}) custom-call(s32[1]{0:T(128)} %bitcast.3.place_ref, s32[1]{0:T(128)} %bitcast.place_ref.to_ref.gz_ref, f32[2,8,128,128]{3,2,1,0:T(8,128)S(1)} %copy-done.3, f32[2,8,128,128]{3,2,1,0:T(8,128)} %collective-permute-done.p1, f32[2,8,128,128]{3,2,1,0:T(8,128)} %collective-permute-done.1.p2, ...), custom_call_target="tpu_custom_call" | custom-call | flops 805306368 | bytes 4194304 | tf_op jit(solution)/shard_map/first_y/pallas_call | solution.py:208
  73.4 0.9 collective-permute-start.3
  74.3 1.8 collective-permute-start.4
  76.0 3.4 %first_y.3 = (f32[2,2,256,128]{3,2,1,0:T(8,128)}, f32[2,2,256,128]{3,2,1,0:T(8,128)}) custom-call(s32[1]{0:T(128)} %bitcast.3.place_ref, s32[1]{0:T(128)} %bitcast.place_ref.to_ref.gz_ref, f32[2,8,128,128]{3,2,1,0:T(8,128)S(1)} %copy-done.3, f32[2,8,128,128]{3,2,1,0:T(8,128)} %collective-permute-done.p1, f32[2,8,128,128]{3,2,1,0:T(8,128)} %collective-permute-done.1.p2, ...), custom_call_target="tpu_custom_call" | custom-call | flops 805306368 | bytes 4194304 | tf_op jit(solution)/shard_map/first_y/pallas_call | solution.py:208
  79.5 0.0 collective-permute-start.5
  79.5 13.8 %all-to-all-done.1.p0.p1.p2.p3 = f32[4,2,2,128,256]{4,3,2,1,0:T(8,128)S(1)} async-done(((f32[4,2,2,128,256]{4,3,2,1,0:T(8,128)}), f32[4,2,2,128,256]{4,3,2,1,0:T(8,128)S(1)}, u32[]{:S(2)}, u32[]{:S(2)}) %all-to-all-start.1) | async-done | bytes 2097184 | tf_op jit(solution)/shard_map/all_to_all | solution.py:401
  93.4 0.0 copy-start.1
  93.4 0.0 copy-start.5
  93.4 1.4 second_y.1.done_y
  94.8 0.0 collective-permute-done.3.p1
  94.8 0.0 collective-permute-done.4.p3
  94.8 0.1 copy-done.1
  95.0 0.1 copy-done.5
  95.0 2.6 %part_z.1.part_ref = f32[2,256,512]{2,1,0:T(8,128)S(1)} custom-call(s32[1]{0:T(128)} %bitcast.place_ref.to_ref.gz_ref, f32[2,2,256,128]{3,2,1,0:T(8,128)S(1)} %copy-done.5, f32[2,2,256,128]{3,2,1,0:T(8,128)} %collective-permute-done.3.p1, f32[2,2,256,128]{3,2,1,0:T(8,128)} %collective-permute-done.4.p3, bf16[2,4,256,512]{3,2,1,0:T(8,128)(2,1)S(1)} %copy-done.1), custom_call_target="tpu_custom_call" | custom-call | flops 1207959552 | bytes 5242880 | tf_op jit(solution)/shard_map/part_z/pallas_call | solution.py:170
  97.7 0.0 collective-permute-done.5.last_z
  97.7 2.3 %second.1 = f32[128,2,2,8,128]{4,3,2,1,0:T(8,128)S(1)} custom-call(s32[1]{0:T(128)} %bitcast.place_ref.to_ref.gz_ref, f32[2,2,256,256]{3,2,1,0:T(8,128)S(1)} %second_y.1.done_y, f32[2,256,512]{2,1,0:T(8,128)S(1)} %part_z.1.part_ref, f32[2,2,256,128]{3,2,1,0:T(8,128)} %collective-permute-done.5.last_z, bf16[2,4,256,512]{3,2,1,0:T(8,128)(2,1)S(1)} %copy-done.1), custom_call_target="tpu_custom_call" | custom-call | flops 402653184 | bytes 8388608 | tf_op jit(solution)/shard_map/second/pallas_call | solution.py:305
  100.0 0.0 copy-start.4
  100.0 43.7 %all_to_all.27.in_ref = f32[128,2,2,8,128]{4,3,2,1,0:T(8,128)S(1)} all-to-all(f32[128,2,2,8,128]{4,3,2,1,0:T(8,128)S(1)} %second.1), channel_id=1, replica_groups=mesh['gx'=8,'gy'=4,'gz'=4] {'gx','gy','gz'}, dimensions={0} | all-to-all | bytes 4194304 | tf_op jit(solution)/shard_map/all_to_all | solution.py:413
  143.8 0.0 copy-done.4
  143.8 4.5 %third.1 = f32[4096,128]{1,0:T(8,128)S(1)} custom-call(s32[1024]{0:T(1024)S(1)} %multiply_add_fusion.slot_ref, f32[128,2,2,8,128]{4,3,2,1,0:T(8,128)S(1)} %all_to_all.27.in_ref, bf16[2,512,1024]{2,1,0:T(8,128)(2,1)S(1)} %copy-done.4), custom_call_target="tpu_custom_call" | custom-call | flops 1610612736 | bytes 6291456 | tf_op jit(solution)/shard_map/third/pallas_call | solution.py:356
  148.3 34.2 %all_to_all.28 = f32[128,1,16,2,128]{4,3,2,1,0:T(2,128)S(1)} all-to-all(f32[128,1,16,2,128]{4,3,2,1,0:T(2,128)S(1)} %bitcast.20), channel_id=1, replica_groups=mesh['gx'=8,'gy'=4,'gz'=4] {'gx','gy','gz'}, dimensions={0} | all-to-all | bytes 4194304 | tf_op jit(solution)/shard_map/all_to_all | solution.py:415
  182.6 1.3 copy.14
  (5 shorter events, 0.1 us)
Async XLA Ops:
  3.4 54.8 %all-to-all-start = ((f32[4,2,8,128,128]{4,3,2,1,0:T(8,128)}), f32[4,2,8,128,128]{4,3,2,1,0:T(8,128)}, u32[]{:S(2)}, u32[]{:S(2)}) async-start(f32[4,2,8,128,128]{4,3,2,1,0:T(8,128)} %scale_a.1), calls=%async_computation | async-start | bytes 8388608 | tf_op jit(solution)/shard_map/all_to_all | solution.py:394
  9.3 8.5 %copy-start.6 = (s32[1024,1]{0,1:T(1,128)S(1)}, s32[1024,1]{0,1:T(1,128)}, u32[]{:S(2)}) copy-start(s32[1024,1]{0,1:T(1,128)} %param.8) | copy-start | bytes 12292
  12.7 45.5 %copy-start = (bf16[2,4,256,512]{3,2,1,0:T(8,128)(2,1)S(1)}, bf16[2,4,256,512]{3,2,1,0:T(8,128)(2,1)}, u32[]{:S(2)}) copy-start(bf16[2,4,256,512]{3,2,1,0:T(8,128)(2,1)} %constant.23.clone.table_ref) | copy-start | bytes 6291460
  12.7 56.0 %collective-permute-start = (f32[2,8,128,128]{3,2,1,0:T(8,128)}, f32[2,8,128,128]{3,2,1,0:T(8,128)}, u32[]{:S(2)}, u32[]{:S(2)}) collective-permute-start(f32[2,8,128,128]{3,2,1,0:T(8,128)} %get-tuple-element.31), channel_id=1, source_target_pairs={{0,4},{4,8},{8,12},{12,0},{1,5},{5,9},{9,13},{13,1},{2,6},{6,10},{... | collective-permute-start | bytes 3145736 | tf_op jit(solution)/shard_map/ppermute | solution.py:377
  14.1 54.6 %collective-permute-start.1 = (f32[2,8,128,128]{3,2,1,0:T(8,128)}, f32[2,8,128,128]{3,2,1,0:T(8,128)}, u32[]{:S(2)}, u32[]{:S(2)}) collective-permute-start(f32[2,8,128,128]{3,2,1,0:T(8,128)} %get-tuple-element.32), channel_id=1, source_target_pairs={{0,8},{4,12},{8,0},{12,4},{1,9},{5,13},{9,1},{13,5},{2,10},{6,14},... | collective-permute-start | bytes 3145736 | tf_op jit(solution)/shard_map/ppermute | solution.py:377
  16.7 52.0 %collective-permute-start.2 = (f32[2,8,128,128]{3,2,1,0:T(8,128)}, f32[2,8,128,128]{3,2,1,0:T(8,128)}, u32[]{:S(2)}, u32[]{:S(2)}) collective-permute-start(f32[2,8,128,128]{3,2,1,0:T(8,128)} %get-tuple-element.33), channel_id=1, source_target_pairs={{0,12},{4,0},{8,4},{12,8},{1,13},{5,1},{9,5},{13,9},{2,14},{6,2},{... | collective-permute-start | bytes 3145736 | tf_op jit(solution)/shard_map/ppermute | solution.py:377
  64.4 4.3 %copy-start.2 = (bf16[2,2,2,256,256]{4,3,2,1,0:T(8,128)(2,1)S(1)}, bf16[2,2,2,256,256]{4,3,2,1,0:T(8,128)(2,1)}, u32[]{:S(2)}) copy-start(bf16[2,2,2,256,256]{4,3,2,1,0:T(8,128)(2,1)} %constant.22.clone.table_ref) | copy-start | bytes 3145732
  64.4 29.0 %all-to-all-start.1 = ((f32[4,2,2,128,256]{4,3,2,1,0:T(8,128)}), f32[4,2,2,128,256]{4,3,2,1,0:T(8,128)S(1)}, u32[]{:S(2)}, u32[]{:S(2)}) async-start(f32[4,2,2,128,256]{4,3,2,1,0:T(8,128)} %first_z.1), calls=%async_computation.1 | async-start | bytes 4194304 | tf_op jit(solution)/shard_map/all_to_all | solution.py:401
  68.7 1.2 copy-start.3
  73.4 21.4 %collective-permute-start.3 = (f32[2,2,256,128]{3,2,1,0:T(8,128)}, f32[2,2,256,128]{3,2,1,0:T(8,128)}, u32[]{:S(2)}, u32[]{:S(2)}) collective-permute-start(f32[2,2,256,128]{3,2,1,0:T(8,128)} %get-tuple-element.38), channel_id=1, source_target_pairs={{0,1},{1,2},{2,3},{3,0},{4,5},{5,6},{6,7},{7,4},{8,9},{9,10},{10,1... | collective-permute-start | bytes 1572872 | tf_op jit(solution)/shard_map/ppermute | solution.py:377
  74.3 20.5 %collective-permute-start.4 = (f32[2,2,256,128]{3,2,1,0:T(8,128)}, f32[2,2,256,128]{3,2,1,0:T(8,128)}, u32[]{:S(2)}, u32[]{:S(2)}) collective-permute-start(f32[2,2,256,128]{3,2,1,0:T(8,128)} %get-tuple-element.39), channel_id=1, source_target_pairs={{0,3},{1,0},{2,1},{3,2},{4,7},{5,4},{6,5},{7,6},{8,11},{9,8},{10,9... | collective-permute-start | bytes 1572872 | tf_op jit(solution)/shard_map/ppermute | solution.py:377
  79.5 18.2 %collective-permute-start.5 = (f32[2,2,256,128]{3,2,1,0:T(8,128)}, f32[2,2,256,128]{3,2,1,0:T(8,128)}, u32[]{:S(2)}, u32[]{:S(2)}) collective-permute-start(f32[2,2,256,128]{3,2,1,0:T(8,128)} %get-tuple-element.44), channel_id=1, source_target_pairs={{0,2},{1,3},{2,0},{3,1},{4,6},{5,7},{6,4},{7,5},{8,10},{9,11},{10,... | collective-permute-start | bytes 1572872 | tf_op jit(solution)/shard_map/ppermute | solution.py:377
  93.4 1.6 copy-start.1
  93.4 1.7 copy-start.5
  100.0 43.7 %copy-start.4 = (bf16[2,512,1024]{2,1,0:T(8,128)(2,1)S(1)}, bf16[2,512,1024]{2,1,0:T(8,128)(2,1)}, u32[]{:S(2)}) copy-start(bf16[2,512,1024]{2,1,0:T(8,128)(2,1)} %constant.21.clone.table_ref) | copy-start | bytes 6291460

commit v10 on v9

--- a/solution.py
+++ b/solution.py
@@ -45,12 +45,14 @@
     first = 64 * gx + 8 * gz + 2 * gy
     second = 64 * gx + 32 + 8 * gy + 2 * gz
     cells = np.stack([first, first + 1, second, second + 1], -1).reshape(128, 4)
-    cosine, sine = cos_sin(cells.reshape(-1), np.arange(KEPT))
-    cosine = cosine.T.reshape(KEPT, 128, 1, 4)
-    sine = sine.T.reshape(KEPT, 128, 1, 4)
-    top = np.concatenate([cosine, sine], 2).reshape(KEPT, 1024)
-    bottom = np.concatenate([-sine, cosine], 2).reshape(KEPT, 1024)
-    table_x = np.concatenate([top, bottom], 0)
+    order = np.arange(KEPT).reshape(KEPT // 2, 2).T.reshape(-1)
+    cosine, sine = cos_sin(cells[:64].reshape(-1), order)
+    cosine, sine = (
+        t.T.reshape(2, KEPT // 2, 64, 1, 4) for t in (cosine, sine)
+    )
+    top = np.concatenate([cosine, sine], 3).reshape(2, KEPT // 2, 512)
+    bottom = np.concatenate([-sine, cosine], 3).reshape(2, KEPT // 2, 512)
+    table_x = np.concatenate([top, bottom], 1)
     return split_table(table_x), split_table(table_y), split_table(table_z)
 
 
@@ -183,76 +185,128 @@
     )(place, *pieces, table)
 
 
-def first_y_kernel(place_ref, to_ref, p0, p1, p2, p3, table_ref, *out_refs):
+def first_y_kernel(shifts, place_ref, to_ref, p0, p1, p2, p3, table_ref, *refs):
+    *out_refs, pieces, table, held_out, semaphores = refs
+    get_table = pltpu.make_async_copy(table_ref, table, semaphores.at[2, 0])
+
+    def gets(step):
+        pair = lax.rem(to_ref[0] + shifts[step], 4)
+        return [
+            pltpu.make_async_copy(
+                piece.at[:, pl.ds(2 * pair, 2)], pieces.at[step, shift], semaphores.at[step, shift]
+            )
+            for shift, piece in enumerate((p0, p1, p2, p3))
+        ]
+
+    def put(step):
+        return pltpu.make_async_copy(
+            held_out.at[step], out_refs[step], semaphores.at[2, 1 + step]
+        )
+
+    get_table.start()
+    for step in range(2):
+        for copy in gets(step):
+            copy.start()
+    get_table.wait()
     g = place_ref[0]
-    parts = transform_y(
-        [(p0[...], p2[...], g), (p1[...], p3[...], lax.rem(g + 3, 4))], table_ref
-    )
-    for step, out_ref in enumerate(out_refs):
-
-        @pl.when(pl.program_id(0) == step)
-        def _():
-            for parity, values in enumerate(parts):
-                for plane in range(2):
-                    for x in range(2):
-                        out_ref[plane, x, parity * 128 : (parity + 1) * 128] = values[
-                            plane * 128 : (plane + 1) * 128, x * 128 : (x + 1) * 128
-                        ]
+    for step in range(2):
+        for copy in gets(step):
+            copy.wait()
+        parts = transform_y(
+            [
+                (pieces[step, 0], pieces[step, 2], g),
+                (pieces[step, 1], pieces[step, 3], lax.rem(g + 3, 4)),
+            ],
+            table,
+        )
+        for parity, values in enumerate(parts):
+            for plane in range(2):
+                for x in range(2):
+                    held_out[step, plane, x, parity * 128 : (parity + 1) * 128] = values[
+                        plane * 128 : (plane + 1) * 128, x * 128 : (x + 1) * 128
+                    ]
+        put(step).start()
+    for step in range(2):
+        put(step).wait()
 
 
 def first_y(shifts, place, to, pieces, table):
-    def pair(i, to):
-        return lax.rem(to[0] + jnp.where(i == 0, shifts[0], shifts[1]), 4)
-
+    hbm = pl.BlockSpec(memory_space=pltpu.HBM)
     shape = (2, 2, KEPT, 128)
     return pl.pallas_call(
-        first_y_kernel,
-        grid_spec=pltpu.PrefetchScalarGridSpec(
-            num_scalar_prefetch=2,
-            grid=(2,),
-            in_specs=[
-                pl.BlockSpec((2, 2, 128, 128), lambda i, place, to: (0, pair(i, to), 0, 0))
-            ]
-            * 4
-            + [pl.BlockSpec(table.shape, lambda i, place, to: (0, 0, 0, 0, 0))],
-            out_specs=[pl.BlockSpec(shape, lambda i, place, to: (0, 0, 0, 0))] * 2,
-        ),
+        functools.partial(first_y_kernel, shifts),
+        in_specs=[pl.BlockSpec(memory_space=pltpu.SMEM)] * 2 + [hbm] * 5,
+        out_specs=[hbm] * 2,
         out_shape=[pltpu.HBM(shape, jnp.float32)] * 2,
-        compiler_params=params(VMEM),
+        scratch_shapes=[
+            pltpu.VMEM((2, 4, 2, 2, 128, 128), jnp.float32),
+            pltpu.VMEM(table.shape, table.dtype),
+            pltpu.VMEM((2,) + shape, jnp.float32),
+            pltpu.SemaphoreType.DMA((3, 4)),
+        ],
+        compiler_params=params(60),
         cost_estimate=cost(512 * 512 * 512, 4 * MIB),
         name="first_y",
     )(place, to, *pieces, table)
 
 
-def first_z_kernel(p0, p1, p2, p3, table_ref, out_ref):
-    rows = jnp.concatenate(
-        [piece[0, plane].reshape(512, 128) for piece in (p0, p1, p2, p3) for plane in range(2)],
-        axis=1,
-    )
-    table = tuple(table_ref[i].reshape(1024, 512) for i in range(2))
-    total = product(halves(rows), table)
-    for pair in range(2):
-        for plane in range(2):
-            out_ref[pair, plane] = total[
-                pair * 256 : (pair + 1) * 256, plane * KEPT : (plane + 1) * KEPT
-            ].reshape(2, 128, KEPT)
+def first_z_kernel(in_ref, table_ref, out_ref, pieces, table, held_out, semaphores):
+    get_table = pltpu.make_async_copy(table_ref, table, semaphores.at[2, 0])
+
+    def get(pair):
+        return pltpu.make_async_copy(
+            in_ref.at[:, :, pl.ds(2 * pair, 2)], pieces.at[pair], semaphores.at[0, pair]
+        )
+
+    def put(pair):
+        return pltpu.make_async_copy(
+            held_out.at[pair], out_ref.at[pair], semaphores.at[1, pair]
+        )
+
+    get(0).start()
+    get_table.start()
+    for pair in range(1, 4):
+        get(pair).start()
+    for pair in range(4):
+        get(pair).wait()
+        if pair == 0:
+            get_table.wait()
+        rows = jnp.concatenate(
+            [
+                pieces[pair, g, plane].reshape(256, 128)
+                for g in range(4)
+                for plane in range(2)
+            ],
+            axis=1,
+        )
+        total = product(halves(rows), tuple(table[i].reshape(1024, 512) for i in range(2)))
+        for plane in range(2):
+            held_out[pair, plane] = total[:, plane * KEPT : (plane + 1) * KEPT].reshape(
+                2, 128, KEPT
+            )
+        put(pair).start()
+    for pair in range(4):
+        put(pair).wait()
 
 
 def first_z(arrived, table):
-    def from_device(g):
-        return pl.BlockSpec((1, 2, 4, 128, 128), lambda i: (g, 0, i, 0, 0))
-
+    hbm = pl.BlockSpec(memory_space=pltpu.HBM)
+    shape = (4, 2, 2, 128, KEPT)
     return pl.pallas_call(
         first_z_kernel,
-        grid=(2,),
-        in_specs=[from_device(g) for g in range(4)]
-        + [pl.BlockSpec((2, 4, 256, 512), lambda i: (0, 0, 0, 0))],
-        out_specs=pl.BlockSpec((2, 2, 2, 128, KEPT), lambda i: (i, 0, 0, 0, 0)),
-        out_shape=pltpu.HBM((4, 2, 2, 128, KEPT), jnp.float32),
-        compiler_params=params(VMEM),
+        in_specs=[hbm] * 2,
+        out_specs=hbm,
+        out_shape=pltpu.HBM(shape, jnp.float32),
+        scratch_shapes=[
+            pltpu.VMEM((4, 4, 2, 2, 128, 128), jnp.float32),
+            pltpu.VMEM(table.shape, table.dtype),
+            pltpu.VMEM(shape, jnp.float32),
+            pltpu.SemaphoreType.DMA((3, 4)),
+        ],
+        compiler_params=params(60),
         cost_estimate=cost(1024 * 1024 * 512, 8 * MIB),
         name="first_z",
-    )(arrived, arrived, arrived, arrived, table)
+    )(arrived, table)
 
 
 def second_y_kernel(p0, p1, p2, p3, table_ref, out_ref):
@@ -333,20 +387,23 @@
     columns = jnp.concatenate(
         [in_ref[:, 0, half].reshape(1024, 128) for half in range(2)], axis=1
     )
-    values = jnp.exp(product((table_ref[0], table_ref[1]), halves(columns)))
-    for plane in range(2):
-        for half in range(2):
-            held[plane, half] = values[
-                plane * KEPT : (plane + 1) * KEPT, half * 128 : (half + 1) * 128
-            ]
+    first, second = columns[:512], columns[512:]
+    for odd, sides in enumerate((first + second, first - second)):
+        values = jnp.exp(product((table_ref[0, odd], table_ref[1, odd]), halves(sides)))
+        for plane in range(2):
+            for half in range(2):
+                held[plane, half, odd * 128 : (odd + 1) * 128] = values[
+                    plane * 128 : (plane + 1) * 128, half * 128 : (half + 1) * 128
+                ]
 
     def place_rows(group, carry):
         for offset in range(8):
-            x = group * 8 + offset
+            x = 2 * (group * 4 + offset // 2) + offset % 2
+            row = group * 4 + offset // 2 + 128 * (offset % 2)
             for half in range(2):
                 slot = slot_ref[x * 4 + parity * 2 + half]
                 for plane in range(2):
-                    out_ref[pl.ds(slot * 2 + plane, 1), :] = held[plane, half, pl.ds(x, 1), :]
+                    out_ref[pl.ds(slot * 2 + plane, 1), :] = held[plane, half, pl.ds(row, 1), :]
         return carry
 
     lax.fori_loop(0, KEPT // 8, place_rows, 0)
@@ -360,14 +417,14 @@
             grid=(2,),
             in_specs=[
                 pl.BlockSpec((128, 1, 2, 8, 128), lambda i, slots: (0, i, 0, 0, 0)),
-                pl.BlockSpec((2, 512, 1024), lambda i, slots: (0, 0, 0)),
+                pl.BlockSpec((2, 2, 256, 512), lambda i, slots: (0, 0, 0, 0)),
             ],
             out_specs=pl.BlockSpec((4096, 128), lambda i, slots: (0, 0)),
             scratch_shapes=[pltpu.VMEM((2, 2, KEPT, 128), jnp.float32)],
         ),
         out_shape=jax.ShapeDtypeStruct((4096, 128), jnp.float32),
         compiler_params=params(VMEM),
-        cost_estimate=cost(512 * 1024 * 512, 6 * MIB),
+        cost_estimate=cost(512 * 512 * 512, 6 * MIB),
         name="third",
     )(slots, arrived, table_x)
 

time: 184 us -> 184 us (level)
  transfers between devices with their start and end apart: 8 -> 8, of which waited for: 2 -> 2; matrix products, arithmetic and copies ran while one was open for 0% -> 0% of each run, Pallas kernels for 11% -> 12%
where the time goes in v10:
time: 184 us
  blocking collectives  77.9 us (42%)
  waiting for transfers between devices  53.2 us (29%)
  Pallas kernels  30.9 us (17%)
  starting transfers between devices  18 us (10%)
  local copies, waits for them, and re-layouts  2.71 us (1%)
    all_to_all x1, blocking collectives, per_device(): lines = lax.all_to_all(planes, ALL, split_axis=0, concat_axis=0, tiled=True)  43.7 us
    all_to_all x1, waiting for transfers between devices, per_device(): a = lax.all_to_all(a, 'gz', split_axis=0, concat_axis=0, tiled=True)  39.6 us
    all_to_all x1, blocking collectives, per_device(): lax.all_to_all(outgoing.reshape(128, 1, CAP, 2, BW), ALL, split_axis=0, c...  34.2 us
    all_to_all x1, waiting for transfers between devices, per_device(): a = lax.all_to_all(a, 'gy', split_axis=0, concat_axis=0, tiled=True)  13.6 us
    ppermute x6, starting transfers between devices, shifted(): lax.ppermute(piece, axis, [(i, (i + shift) % size) for i in range(size)])  7.93 us
    pallas_call x2, Pallas kernels, first_y(): pl.pallas_call(functools.partial(first_y_kernel, shifts), in_specs=[pl.Bl...  7.2 us
    pallas_call x2, Pallas kernels, scale(): pl.pallas_call(functools.partial(scale_kernel, half, rotated), in_specs=[...  6.81 us
    pallas_call x1, Pallas kernels, first_z(): pl.pallas_call(first_z_kernel, in_specs=[hbm] * 2, out_specs=hbm, out_sha...  6.75 us
  transfers between devices with their start and end apart: 8, of which 2 were waited for; matrix products, arithmetic and copies ran while one was open for 0% of the time, Pallas kernels for 12%

profile of v10, /device:TPU:1, one launch (start us, length us, event | category | flops | bytes accessed | tf_op | source)
XLA Modules:
  0.0 183.5 jit_solution(10724216293662250254)
XLA Ops:
  0.0 3.4 %scale_a.1 = f32[4,2,8,128,128]{4,3,2,1,0:T(8,128)} custom-call(s32[1]{0:T(128)} %bitcast.place_ref.to_ref.gz_ref, bf16[2,8,8,128,128]{4,3,2,1,0:T(8,128)(2,1)} %bitcast.21, f32[8,8,128,128]{3,2,1,0:T(8,128)} %bitcast.23), custom_call_target="tpu_custom_call" | custom-call | flops 6291456 | bytes 8388608 | tf_op jit(solution)/shard_map/scale_a/pallas_call | solution.py:127
  3.4 5.9 %all-to-all-start = ((f32[4,2,8,128,128]{4,3,2,1,0:T(8,128)}), f32[4,2,8,128,128]{4,3,2,1,0:T(8,128)}, u32[]{:S(2)}, u32[]{:S(2)}) async-start(f32[4,2,8,128,128]{4,3,2,1,0:T(8,128)} %scale_a.1), calls=%async_computation | async-start | bytes 8388608 | tf_op jit(solution)/shard_map/all_to_all | solution.py:451
  9.3 0.0 copy-start.5
  9.3 3.4 %scale_b.1 = (f32[2,8,128,128]{3,2,1,0:T(8,128)}, f32[2,8,128,128]{3,2,1,0:T(8,128)}, f32[2,8,128,128]{3,2,1,0:T(8,128)}, f32[2,8,128,128]{3,2,1,0:T(8,128)}) custom-call(s32[1]{0:T(128)} %bitcast.3.place_ref, bf16[2,8,8,128,128]{4,3,2,1,0:T(8,128)(2,1)} %bitcast.22, f32[8,8,128,128]{3,2,1,0:T(8,128)} %bitcast.24), custom_call_target="tpu_custom_call" | custom-call | flops 6291456 | bytes 8388608 | tf_op jit(solution)/shard_map/scale_b/pallas_call | solution.py:127
  12.7 1.4 collective-permute-start
  14.1 2.6 %collective-permute-start.1 = (f32[2,8,128,128]{3,2,1,0:T(8,128)}, f32[2,8,128,128]{3,2,1,0:T(8,128)}, u32[]{:S(2)}, u32[]{:S(2)}) collective-permute-start(f32[2,8,128,128]{3,2,1,0:T(8,128)} %get-tuple-element.32), channel_id=1, source_target_pairs={{0,8},{4,12},{8,0},{12,4},{1,9},{5,13},{9,1},{13,5},{2,10},{6,14},... | collective-permute-start | bytes 3145736 | tf_op jit(solution)/shard_map/ppermute | solution.py:434
  16.7 1.1 collective-permute-start.2
  17.8 0.0 copy-done.5
  17.8 0.1 copy.10
  17.9 0.2 fusion.2
  18.2 0.1 copy.11
  18.3 0.4 fusion.1
  18.6 39.6 %all-to-all-done.in_ref = f32[4,2,8,128,128]{4,3,2,1,0:T(8,128)} async-done(((f32[4,2,8,128,128]{4,3,2,1,0:T(8,128)}), f32[4,2,8,128,128]{4,3,2,1,0:T(8,128)}, u32[]{:S(2)}, u32[]{:S(2)}) %all-to-all-start) | async-done | bytes 4194336 | tf_op jit(solution)/shard_map/all_to_all | solution.py:451
  58.2 6.7 %first_z.1 = f32[4,2,2,128,256]{4,3,2,1,0:T(8,128)} custom-call(f32[4,2,8,128,128]{4,3,2,1,0:T(8,128)} %all-to-all-done.in_ref, bf16[2,4,256,512]{3,2,1,0:T(8,128)(2,1)} %constant.23.clone.table_ref), custom_call_target="tpu_custom_call" | custom-call | flops 3221225472 | bytes 8388608 | tf_op jit(solution)/shard_map/first_z/pallas_call | solution.py:295
  65.0 4.2 %all-to-all-start.1 = ((f32[4,2,2,128,256]{4,3,2,1,0:T(8,128)}), f32[4,2,2,128,256]{4,3,2,1,0:T(8,128)S(1)}, u32[]{:S(2)}, u32[]{:S(2)}) async-start(f32[4,2,2,128,256]{4,3,2,1,0:T(8,128)} %first_z.1), calls=%async_computation.1 | async-start | bytes 4194304 | tf_op jit(solution)/shard_map/all_to_all | solution.py:458
  69.2 0.0 collective-permute-done.p1
  69.2 0.0 copy-start.4
  69.2 0.0 collective-permute-done.1.p2
  69.2 0.0 collective-permute-done.2.p3
  69.2 1.0 copy-done.4
  70.2 3.6 %first_y.2 = (f32[2,2,256,128]{3,2,1,0:T(8,128)}, f32[2,2,256,128]{3,2,1,0:T(8,128)}) custom-call(s32[1]{0:T(128)} %bitcast.3.place_ref, s32[1]{0:T(128)} %bitcast.place_ref.to_ref.gz_ref, f32[2,8,128,128]{3,2,1,0:T(8,128)} %get-tuple-element.34.p0, f32[2,8,128,128]{3,2,1,0:T(8,128)} %copy-done.4, f32[2,8,128,128]{3,2,1,0:T(8,128)} %collective-permute-done.1.p2, ...), custom_call_target="tpu_custom_call" | custom-call | flops 805306368 | bytes 4194304 | tf_op jit(solution)/shard_map/first_y/pallas_call | solution.py:236
  73.8 0.9 collective-permute-start.3
  74.7 0.0 copy-start
  74.7 1.8 collective-permute-start.4
  76.5 3.6 %first_y.3 = (f32[2,2,256,128]{3,2,1,0:T(8,128)}, f32[2,2,256,128]{3,2,1,0:T(8,128)}) custom-call(s32[1]{0:T(128)} %bitcast.3.place_ref, s32[1]{0:T(128)} %bitcast.place_ref.to_ref.gz_ref, f32[2,8,128,128]{3,2,1,0:T(8,128)} %get-tuple-element.34.p0, f32[2,8,128,128]{3,2,1,0:T(8,128)} %copy-done.4, f32[2,8,128,128]{3,2,1,0:T(8,128)} %collective-permute-done.1.p2, ...), custom_call_target="tpu_custom_call" | custom-call | flops 805306368 | bytes 4194304 | tf_op jit(solution)/shard_map/first_y/pallas_call | solution.py:236
  80.1 0.1 collective-permute-start.5
  80.3 13.6 %all-to-all-done.1.p0.p1.p2.p3 = f32[4,2,2,128,256]{4,3,2,1,0:T(8,128)S(1)} async-done(((f32[4,2,2,128,256]{4,3,2,1,0:T(8,128)}), f32[4,2,2,128,256]{4,3,2,1,0:T(8,128)S(1)}, u32[]{:S(2)}, u32[]{:S(2)}) %all-to-all-start.1) | async-done | bytes 2097184 | tf_op jit(solution)/shard_map/all_to_all | solution.py:458
  93.9 0.0 copy-done
  93.9 0.0 copy-start.1
  93.9 0.0 copy-start.3
  93.9 1.4 second_y.1.done_y
  95.3 0.0 collective-permute-done.3.p1
  95.3 0.0 collective-permute-done.4.p3
  95.3 0.1 copy-done.1
  95.5 0.1 copy-done.3
  95.6 2.6 %part_z.1.part_ref = f32[2,256,512]{2,1,0:T(8,128)S(1)} custom-call(s32[1]{0:T(128)} %bitcast.place_ref.to_ref.gz_ref, f32[2,2,256,128]{3,2,1,0:T(8,128)S(1)} %copy-done.3, f32[2,2,256,128]{3,2,1,0:T(8,128)} %collective-permute-done.3.p1, f32[2,2,256,128]{3,2,1,0:T(8,128)} %collective-permute-done.4.p3, bf16[2,4,256,512]{3,2,1,0:T(8,128)(2,1)S(1)} %copy-done.1), custom_call_target="tpu_custom_call" | custom-call | flops 1207959552 | bytes 5242880 | tf_op jit(solution)/shard_map/part_z/pallas_call | solution.py:172
  98.2 0.0 collective-permute-done.5.last_z
  98.2 2.3 %second.1 = f32[128,2,2,8,128]{4,3,2,1,0:T(8,128)S(1)} custom-call(s32[1]{0:T(128)} %bitcast.place_ref.to_ref.gz_ref, f32[2,2,256,256]{3,2,1,0:T(8,128)S(1)} %second_y.1.done_y, f32[2,256,512]{2,1,0:T(8,128)S(1)} %part_z.1.part_ref, f32[2,2,256,128]{3,2,1,0:T(8,128)} %collective-permute-done.5.last_z, bf16[2,4,256,512]{3,2,1,0:T(8,128)(2,1)S(1)} %copy-done.1), custom_call_target="tpu_custom_call" | custom-call | flops 402653184 | bytes 8388608 | tf_op jit(solution)/shard_map/second/pallas_call | solution.py:359
  100.6 0.0 copy-start.2
  100.6 43.7 %all_to_all.27.in_ref = f32[128,2,2,8,128]{4,3,2,1,0:T(8,128)S(1)} all-to-all(f32[128,2,2,8,128]{4,3,2,1,0:T(8,128)S(1)} %second.1), channel_id=1, replica_groups=mesh['gx'=8,'gy'=4,'gz'=4] {'gx','gy','gz'}, dimensions={0} | all-to-all | bytes 4194304 | tf_op jit(solution)/shard_map/all_to_all | solution.py:470
  144.2 0.0 copy-done.2
  144.2 3.8 %third.1 = f32[4096,128]{1,0:T(8,128)S(1)} custom-call(s32[1024]{0:T(1024)S(1)} %multiply_add_fusion.slot_ref, f32[128,2,2,8,128]{4,3,2,1,0:T(8,128)S(1)} %all_to_all.27.in_ref, bf16[2,2,256,512]{3,2,1,0:T(8,128)(2,1)S(1)} %copy-done.2), custom_call_target="tpu_custom_call" | custom-call | flops 805306368 | bytes 6291456 | tf_op jit(solution)/shard_map/third/pallas_call | solution.py:413
  148.0 34.2 %all_to_all.28 = f32[128,1,16,2,128]{4,3,2,1,0:T(2,128)S(1)} all-to-all(f32[128,1,16,2,128]{4,3,2,1,0:T(2,128)S(1)} %bitcast.20), channel_id=1, replica_groups=mesh['gx'=8,'gy'=4,'gz'=4] {'gx','gy','gz'}, dimensions={0} | all-to-all | bytes 4194304 | tf_op jit(solution)/shard_map/all_to_all | solution.py:472
  182.2 1.3 copy.14
  (5 shorter events, 0.1 us)
Async XLA Ops:
  3.4 54.8 %all-to-all-start = ((f32[4,2,8,128,128]{4,3,2,1,0:T(8,128)}), f32[4,2,8,128,128]{4,3,2,1,0:T(8,128)}, u32[]{:S(2)}, u32[]{:S(2)}) async-start(f32[4,2,8,128,128]{4,3,2,1,0:T(8,128)} %scale_a.1), calls=%async_computation | async-start | bytes 8388608 | tf_op jit(solution)/shard_map/all_to_all | solution.py:451
  9.3 8.5 %copy-start.5 = (s32[1024,1]{0,1:T(1,128)S(1)}, s32[1024,1]{0,1:T(1,128)}, u32[]{:S(2)}) copy-start(s32[1024,1]{0,1:T(1,128)} %param.8) | copy-start | bytes 12292
  12.7 56.5 %collective-permute-start = (f32[2,8,128,128]{3,2,1,0:T(8,128)}, f32[2,8,128,128]{3,2,1,0:T(8,128)S(1)}, u32[]{:S(2)}, u32[]{:S(2)}) collective-permute-start(f32[2,8,128,128]{3,2,1,0:T(8,128)} %get-tuple-element.31), channel_id=1, source_target_pairs={{0,4},{4,8},{8,12},{12,0},{1,5},{5,9},{9,13},{13,1},{2,6},{6,10},{... | collective-permute-start | bytes 3145736 | tf_op jit(solution)/shard_map/ppermute | solution.py:434
  14.1 55.1 %collective-permute-start.1 = (f32[2,8,128,128]{3,2,1,0:T(8,128)}, f32[2,8,128,128]{3,2,1,0:T(8,128)}, u32[]{:S(2)}, u32[]{:S(2)}) collective-permute-start(f32[2,8,128,128]{3,2,1,0:T(8,128)} %get-tuple-element.32), channel_id=1, source_target_pairs={{0,8},{4,12},{8,0},{12,4},{1,9},{5,13},{9,1},{13,5},{2,10},{6,14},... | collective-permute-start | bytes 3145736 | tf_op jit(solution)/shard_map/ppermute | solution.py:434
  16.7 52.5 %collective-permute-start.2 = (f32[2,8,128,128]{3,2,1,0:T(8,128)}, f32[2,8,128,128]{3,2,1,0:T(8,128)}, u32[]{:S(2)}, u32[]{:S(2)}) collective-permute-start(f32[2,8,128,128]{3,2,1,0:T(8,128)} %get-tuple-element.33), channel_id=1, source_target_pairs={{0,12},{4,0},{8,4},{12,8},{1,13},{5,1},{9,5},{13,9},{2,14},{6,2},{... | collective-permute-start | bytes 3145736 | tf_op jit(solution)/shard_map/ppermute | solution.py:434
  65.0 28.9 %all-to-all-start.1 = ((f32[4,2,2,128,256]{4,3,2,1,0:T(8,128)}), f32[4,2,2,128,256]{4,3,2,1,0:T(8,128)S(1)}, u32[]{:S(2)}, u32[]{:S(2)}) async-start(f32[4,2,2,128,256]{4,3,2,1,0:T(8,128)} %first_z.1), calls=%async_computation.1 | async-start | bytes 4194304 | tf_op jit(solution)/shard_map/all_to_all | solution.py:458
  69.2 1.0 copy-start.4
  73.8 21.6 %collective-permute-start.3 = (f32[2,2,256,128]{3,2,1,0:T(8,128)}, f32[2,2,256,128]{3,2,1,0:T(8,128)}, u32[]{:S(2)}, u32[]{:S(2)}) collective-permute-start(f32[2,2,256,128]{3,2,1,0:T(8,128)} %get-tuple-element.38), channel_id=1, source_target_pairs={{0,1},{1,2},{2,3},{3,0},{4,5},{5,6},{6,7},{7,4},{8,9},{9,10},{10,1... | collective-permute-start | bytes 1572872 | tf_op jit(solution)/shard_map/ppermute | solution.py:434
  74.7 19.2 %copy-start = (bf16[2,2,2,256,256]{4,3,2,1,0:T(8,128)(2,1)S(1)}, bf16[2,2,2,256,256]{4,3,2,1,0:T(8,128)(2,1)}, u32[]{:S(2)}) copy-start(bf16[2,2,2,256,256]{4,3,2,1,0:T(8,128)(2,1)} %constant.22.clone.table_ref) | copy-start | bytes 3145732
  74.7 20.6 %collective-permute-start.4 = (f32[2,2,256,128]{3,2,1,0:T(8,128)}, f32[2,2,256,128]{3,2,1,0:T(8,128)}, u32[]{:S(2)}, u32[]{:S(2)}) collective-permute-start(f32[2,2,256,128]{3,2,1,0:T(8,128)} %get-tuple-element.39), channel_id=1, source_target_pairs={{0,3},{1,0},{2,1},{3,2},{4,7},{5,4},{6,5},{7,6},{8,11},{9,8},{10,9... | collective-permute-start | bytes 1572872 | tf_op jit(solution)/shard_map/ppermute | solution.py:434
  80.1 18.1 %collective-permute-start.5 = (f32[2,2,256,128]{3,2,1,0:T(8,128)}, f32[2,2,256,128]{3,2,1,0:T(8,128)}, u32[]{:S(2)}, u32[]{:S(2)}) collective-permute-start(f32[2,2,256,128]{3,2,1,0:T(8,128)} %get-tuple-element.44), channel_id=1, source_target_pairs={{0,2},{1,3},{2,0},{3,1},{4,6},{5,7},{6,4},{7,5},{8,10},{9,11},{10,... | collective-permute-start | bytes 1572872 | tf_op jit(solution)/shard_map/ppermute | solution.py:434
  93.9 1.6 copy-start.1
  93.9 1.7 copy-start.3
  100.6 43.7 %copy-start.2 = (bf16[2,2,256,512]{3,2,1,0:T(8,128)(2,1)S(1)}, bf16[2,2,256,512]{3,2,1,0:T(8,128)(2,1)}, u32[]{:S(2)}) copy-start(bf16[2,2,256,512]{3,2,1,0:T(8,128)(2,1)} %constant.21.clone.table_ref) | copy-start | bytes 3145732

commit v11 on v8

v11 whole, which is shorter than its diff:
```python
import functools

import jax
import jax.numpy as jnp
import ml_dtypes
import numpy as np
from jax import lax
from jax.experimental import pallas as pl
from jax.experimental.pallas import tpu as pltpu
from jax.sharding import PartitionSpec as P

N = 512
KEPT = 256
BW = 128
CAP = 16
ALL = ("gx", "gy", "gz")
MIB = 1 << 20
VMEM = 16


def split_table(table):
    high = table.astype(np.float32).astype(ml_dtypes.bfloat16)
    low = (table - high.astype(np.float64)).astype(np.float32).astype(ml_dtypes.bfloat16)
    return np.stack([high, low])


def cos_sin(positions, kept):
    angles = (positions[:, None] * kept[None, :] % N) * (2.0 * np.pi / N)
    return np.cos(angles), np.sin(angles)


@functools.cache
def tables():
    cosine, sine = cos_sin(np.arange(N), np.arange(KEPT))
    real_rows = np.concatenate([cosine, -sine], 1).reshape(4, 1, 128, 2 * KEPT)
    imag_rows = np.concatenate([sine, cosine], 1).reshape(4, 1, 128, 2 * KEPT)
    table_z = np.concatenate([real_rows, imag_rows], 1).reshape(4, 256, 2 * KEPT)
    order = np.arange(KEPT).reshape(KEPT // 2, 2).T.reshape(-1)
    cosine, sine = cos_sin(np.arange(N // 2), order)
    cosine, sine = (t.T.reshape(2, 128, 2, 128).transpose(2, 0, 1, 3) for t in (cosine, sine))
    top = np.concatenate([cosine, sine], 3)
    bottom = np.concatenate([-sine, cosine], 3)
    table_y = np.concatenate([top, bottom], 2)
    gx, gy, gz = np.meshgrid(np.arange(8), np.arange(4), np.arange(4), indexing="ij")
    first = 64 * gx + 8 * gz + 2 * gy
    second = 64 * gx + 32 + 8 * gy + 2 * gz
    cells = np.stack([first, first + 1, second, second + 1], -1).reshape(128, 4)
    order = np.arange(KEPT).reshape(KEPT // 2, 2).T.reshape(-1)
    cosine, sine = cos_sin(cells[:64].reshape(-1), order)
    cosine, sine = (
        t.T.reshape(2, KEPT // 2, 64, 1, 4) for t in (cosine, sine)
    )
    top = np.concatenate([cosine, sine], 3).reshape(2, KEPT // 2, 512)
    bottom = np.concatenate([-sine, cosine], 3).reshape(2, KEPT // 2, 512)
    table_x = np.concatenate([top, bottom], 1)
    return split_table(table_x), split_table(table_y), split_table(table_z)


def halves(values):
    high = values.astype(jnp.bfloat16)
    low = (values - high.astype(jnp.float32)).astype(jnp.bfloat16)
    return high, low


def product(left, right):
    def dot(a, b):
        return jnp.dot(a, b, preferred_element_type=jnp.float32)

    return dot(left[0], right[0]) + (dot(left[0], right[1]) + dot(left[1], right[0]))


def params(mib):
    return pltpu.CompilerParams(vmem_limit_bytes=mib * MIB)


def cost(multiplies, moved):
    return pl.CostEstimate(flops=6 * multiplies, bytes_accessed=moved, transcendentals=0)


def rows_z(piece):
    return halves(jnp.concatenate([piece[plane].reshape(-1, 128) for plane in range(2)], axis=1))


def columns_y(piece):
    planes, cells = piece.shape[:2]
    return halves(
        jnp.concatenate([piece[:, x].reshape(256, piece.shape[3]) for x in range(cells)], axis=1)
    )


def scale_kernel(half, rotated, place_ref, normals_ref, spectrum_ref, *refs):
    if rotated:
        *out_refs, held_n, held_s, semaphores = refs
    else:
        out_ref, held_out, held_n, held_s, semaphores = refs
    order = (1, 3, 2, 0)

    def gets(shift):
        chunk = 4 * half + (lax.rem(place_ref[0] + shift, 4) if rotated else shift)
        return (
            pltpu.make_async_copy(
                normals_ref.at[:, chunk], held_n.at[shift], semaphores.at[shift, 0]
            ),
            pltpu.make_async_copy(
                spectrum_ref.at[chunk], held_s.at[shift], semaphores.at[shift, 1]
            ),
        )

    def put(shift):
        return pltpu.make_async_copy(
            held_out.at[shift], out_ref.at[shift], semaphores.at[shift, 2]
        )

    for shift in order:
        for copy in gets(shift):
            copy.start()
    for shift in order:
        for copy in gets(shift):
            copy.wait()
        target = out_refs[shift] if rotated else held_out.at[shift]
        for plane in range(2):
            target[plane] = held_n[shift, plane].astype(jnp.float32) * held_s[shift]
        if not rotated:
            put(shift).start()
    if not rotated:
        for shift in order:
            put(shift).wait()


def scale(half, rotated, place, normals, spectrum):
    chunks = (4, 2, 8, 128, 128)
    if rotated:
        out_specs = [pl.BlockSpec(memory_space=pltpu.VMEM)] * 4
        out_shape = [pltpu.VMEM(chunks[1:], jnp.float32)] * 4
        scratch = []
    else:
        out_specs = pl.BlockSpec(memory_space=pltpu.HBM)
        out_shape = pltpu.HBM(chunks, jnp.float32)
        scratch = [pltpu.VMEM(chunks, jnp.float32)]
    return pl.pallas_call(
        functools.partial(scale_kernel, half, rotated),
        in_specs=[pl.BlockSpec(memory_space=pltpu.SMEM)]
        + [pl.BlockSpec(memory_space=pltpu.HBM)] * 2,
        out_specs=out_specs,
        out_shape=out_shape,
        scratch_shapes=scratch
        + [
            pltpu.VMEM(chunks, jnp.bfloat16),
            pltpu.VMEM((4, 8, 128, 128), jnp.float32),
            pltpu.SemaphoreType.DMA((4, 3)),
        ],
        compiler_params=params(VMEM),
        cost_estimate=cost(1 << 20, 8 * MIB),
        name="scale_b" if rotated else "scale_a",
    )(
        place,
        pltpu.with_memory_space_constraint(normals.reshape(2, 8, 8, 128, 128), pltpu.HBM),
        pltpu.with_memory_space_constraint(spectrum.reshape(8, 8, 128, 128), pltpu.HBM),
    )


def term_of(piece, table_ref, g):
    return product(rows_z(piece), (table_ref[0, g], table_ref[1, g]))


def transform_y(pairs, table_ref):
    even = odd = None
    for first, second, g in pairs:
        base = lax.rem(g, 2)
        sign = jnp.where(g < 2, 1.0, -1.0).astype(jnp.float32)
        term = product((table_ref[0, base, 0], table_ref[1, base, 0]), columns_y(first + second))
        even = term if even is None else even + term
        term = product(
            (table_ref[0, base, 1], table_ref[1, base, 1]), columns_y((first - second) * sign)
        )
        odd = term if odd is None else odd + term
    return even, odd


def in_vmem(kernel, name, multiplies, out_shape, scalars, operands, scratch=(), hbm=False):
    space = pltpu.HBM if hbm else pltpu.VMEM
    several = isinstance(out_shape, list)
    shapes = out_shape if several else [out_shape]
    specs = [pl.BlockSpec(memory_space=space) for _ in shapes]
    results = [space(shape, jnp.float32) for shape in shapes]
    return pl.pallas_call(
        kernel,
        in_specs=[pl.BlockSpec(memory_space=pltpu.SMEM)] * len(scalars)
        + [pl.BlockSpec(memory_space=pltpu.VMEM)] * len(operands),
        out_specs=specs if several else specs[0],
        out_shape=results if several else results[0],
        scratch_shapes=list(scratch),
        compiler_params=params(VMEM),
        cost_estimate=cost(multiplies, 4 * MIB),
        name=name,
    )(*scalars, *[pltpu.with_memory_space_constraint(x, pltpu.VMEM) for x in operands])


def first_z_kernel(in_ref, table_ref, out_ref, held, semaphores):
    def put(pair):
        return pltpu.make_async_copy(held.at[pair], out_ref.at[pair], semaphores.at[pair])

    table = tuple(table_ref[i].reshape(1024, 512) for i in range(2))
    for pair in range(4):
        rows = jnp.concatenate(
            [
                in_ref[g, plane, 2 * pair : 2 * pair + 2].reshape(256, 128)
                for g in range(4)
                for plane in range(2)
            ],
            axis=1,
        )
        total = product(halves(rows), table)
        for plane in range(2):
            held[pair, plane] = total[:, plane * KEPT : (plane + 1) * KEPT].reshape(2, 128, KEPT)
        put(pair).start()
    for pair in range(4):
        put(pair).wait()


def first_z(arrived, table):
    shape = (4, 2, 2, 128, KEPT)
    scratch = [pltpu.VMEM(shape, jnp.float32), pltpu.SemaphoreType.DMA((4,))]
    return in_vmem(
        first_z_kernel,
        "first_z",
        1024 * 1024 * 512,
        shape,
        [],
        [arrived, table],
        scratch,
        hbm=True,
    )


def first_y_kernel(shifts, place_ref, to_ref, p0, p1, p2, p3, table_ref, *out_refs):
    g = place_ref[0]
    for shift, out_ref in zip(shifts, out_refs):
        cells = pl.ds(2 * lax.rem(to_ref[0] + shift, 4), 2)
        parts = transform_y(
            [(p0[:, cells], p2[:, cells], g), (p1[:, cells], p3[:, cells], lax.rem(g + 3, 4))],
            table_ref,
        )
        for parity, values in enumerate(parts):
            for plane in range(2):
                for x in range(2):
                    out_ref[plane, x, parity * 128 : (parity + 1) * 128] = values[
                        plane * 128 : (plane + 1) * 128, x * 128 : (x + 1) * 128
                    ]


def first_y(shifts, place, to, pieces, table):
    return in_vmem(
        functools.partial(first_y_kernel, shifts),
        "first_y",
        512 * 512 * 512,
        [(2, 2, KEPT, 128)] * 2,
        [place, to],
        [*pieces, table],
    )


def part_z_kernel(place_ref, p0, p1, p3, table_ref, out_ref):
    total = None
    for shift, piece in ((0, p0), (1, p1), (3, p3)):
        term = term_of(piece[...], table_ref, lax.rem(place_ref[0] + (4 - shift), 4))
        total = term if total is None else total + term
    out_ref[...] = total.reshape(2, KEPT, 512)


def part_z(place, pieces, table):
    return in_vmem(
        part_z_kernel, "part_z", 512 * 512 * 768, (2, KEPT, 512), [place], [*pieces, table]
    )


def second_y_kernel(in_ref, table_ref, out_ref):
    parts = transform_y([(in_ref[0], in_ref[2], 0), (in_ref[1], in_ref[3], 1)], table_ref)
    for parity, values in enumerate(parts):
        for x in range(2):
            for plane in range(2):
                out_ref[x, plane, parity * 128 : (parity + 1) * 128] = values[
                    plane * 128 : (plane + 1) * 128, x * KEPT : (x + 1) * KEPT
                ]


def second_y(arrived, table):
    return in_vmem(
        second_y_kernel, "second_y", 512 * 512 * 512, (2, 2, KEPT, KEPT), [], [arrived, table]
    )


def second_kernel(gz_ref, done_y, part_ref, last_z, table_ref, out_ref):
    def put(values, parity, row):
        for half in range(2):
            out_ref[pl.ds(parity * 16 + half * 8 + row, 128, stride=32), :] = values[
                :, half * 128 : (half + 1) * 128
            ]

    total = part_ref[...].reshape(512, 512) + term_of(
        last_z[...], table_ref, lax.rem(gz_ref[0] + 2, 4)
    )
    for parity in range(2):
        for x in range(2):
            start = x * KEPT + parity * 128
            for plane in range(2):
                put(
                    done_y[x, plane, parity * 128 : (parity + 1) * 128], parity, plane * 4 + x
                )
                put(
                    total[start : start + 128, plane * KEPT : (plane + 1) * KEPT],
                    parity,
                    plane * 4 + 2 + x,
                )


def second(gz, done_y, part, last_z, table):
    return in_vmem(
        second_kernel,
        "second",
        512 * 512 * 256,
        (4096, 128),
        [gz],
        [done_y, part, last_z, table],
    )


def third_kernel(slot_ref, in_ref, table_ref, out_ref, held):
    out_ref[...] = jnp.zeros_like(out_ref)
    for parity in range(2):
        columns = jnp.concatenate(
            [in_ref[:, parity, half].reshape(1024, 128) for half in range(2)], axis=1
        )
        first, last = columns[:512], columns[512:]
        for odd, sides in enumerate((first + last, first - last)):
            values = jnp.exp(product((table_ref[0, odd], table_ref[1, odd]), halves(sides)))
            for plane in range(2):
                for half in range(2):
                    held[parity, plane, half, odd * 128 : (odd + 1) * 128] = values[
                        plane * 128 : (plane + 1) * 128, half * 128 : (half + 1) * 128
                    ]

    def place_rows(group, carry):
        for offset in range(4):
            x = group * 4 + offset
            row = group * 2 + offset // 2 + 128 * (offset % 2)
            for parity in range(2):
                for half in range(2):
                    slot = slot_ref[x * 4 + parity * 2 + half]
                    for plane in range(2):
                        out_ref[pl.ds(slot * 2 + plane, 1), :] = held[
                            parity, plane, half, pl.ds(row, 1), :
                        ]
        return carry

    lax.fori_loop(0, KEPT // 4, place_rows, 0)


def third(slots, arrived, table_x):
    scratch = [pltpu.VMEM((2, 2, 2, KEPT, 128), jnp.float32)]
    return in_vmem(
        third_kernel,
        "third",
        512 * 512 * 512,
        (4096, 128),
        [slots],
        [arrived, table_x],
        scratch,
    )


def shifted(piece, axis, shift):
    size = lax.axis_size(axis)
    return lax.ppermute(piece, axis, [(i, (i + shift) % size) for i in range(size)])


def slots_of(block_owner):
    destination = block_owner[:, 0]
    one_hot = (destination[:, None] == jnp.arange(128, dtype=jnp.int32)[None, :]).astype(jnp.int32)
    earlier = jnp.cumsum(one_hot, axis=0) - one_hot
    return destination * CAP + jnp.sum(earlier * one_hot, axis=1)


def per_device(normals, spectrum, block_owner):
    table_x, table_y, table_z = (jnp.asarray(table) for table in tables())
    gy = lax.axis_index("gy").astype(jnp.int32).reshape(1)
    gz = lax.axis_index("gz").astype(jnp.int32).reshape(1)

    a = scale(0, False, gz, normals, spectrum)
    a, place = lax.optimization_barrier((a, gy))
    a = lax.all_to_all(a, "gz", split_axis=0, concat_axis=0, tiled=True)
    b0, b1, b2, b3 = scale(1, True, place, normals, spectrum)
    b1, b3, b2 = shifted(b1, "gy", 1), shifted(b3, "gy", 3), shifted(b2, "gy", 2)

    a, slots = lax.optimization_barrier((a, slots_of(block_owner)))
    a = first_z(a, table_z)
    b0, b1, b2, b3, _ = lax.optimization_barrier((b0, b1, b2, b3, a))
    a = lax.all_to_all(a, "gy", split_axis=0, concat_axis=0, tiled=True)
    pieces = b0, b1, b2, b3
    b1, b3 = first_y((1, 3), gy, gz, pieces, table_y)
    b1, b3 = shifted(b1, "gz", 1), shifted(b3, "gz", 3)
    b2, b0 = first_y((2, 0), gy, gz, pieces, table_y)
    b2 = shifted(b2, "gz", 2)

    a = second_y(a, table_y)
    a, b1, b3 = lax.optimization_barrier((a, b1, b3))
    part_b = part_z(gz, (b0, b1, b3), table_z)
    part_b, b2 = lax.optimization_barrier((part_b, b2))
    planes = second(gz, a, part_b, b2, table_z)
    lines = lax.all_to_all(
        planes.reshape(128, 2, 2, 8, 128), ALL, split_axis=0, concat_axis=0, tiled=True)
    outgoing = third(slots, lines, table_x)
    return lax.all_to_all(
        outgoing.reshape(128, 1, CAP, 2, BW), ALL, split_axis=0, concat_axis=1, tiled=True
    )


def solution(mesh):
    placed = (P(None, "gx", "gy", "gz"), P("gx", "gy", "gz"), P(ALL, None))
    return jax.shard_map(
        per_device,
        mesh=mesh,
        in_specs=placed,
        out_specs=P(ALL, None, None, None, None),
        check_vma=False,
    )
```

time: 188 us -> 184 us (0.979)
  local copies, waits for them, and re-layouts: 15.5 us -> 4.6 us
  Pallas kernels: 26.9 us -> 32.4 us
  waiting for transfers between devices: 48.6 us -> 51 us
    unnamed x29 -> x17, local copies, waits for them, and re-layouts: 15.3 us -> 4.39 us
    pallas_call x2, Pallas kernels: 3.1 us -> 7.33 us  [scale(): pl.pallas_call(functools.partial(scale_kernel, half, rotated), in_specs=[...]
    all_to_all x1, waiting for transfers between devices: 35.3 us -> 38.1 us  [per_device(): a = lax.all_to_all(a, 'gz', split_axis=0, concat_axis=0, tiled=True)]
  transfers between devices with their start and end apart: 8 -> 8, of which waited for: 3 -> 2; matrix products, arithmetic and copies ran while one was open for 0% -> 0% of each run, Pallas kernels for 10% -> 12%
where the time goes in v11:
time: 184 us
  blocking collectives  76.9 us (42%)
  waiting for transfers between devices  51 us (28%)
  Pallas kernels  32.4 us (18%)
  starting transfers between devices  18.1 us (10%)
  local copies, waits for them, and re-layouts  4.6 us (2%)
    all_to_all x1, blocking collectives, per_device(): lax.all_to_all(planes.reshape(128, 2, 2, 8, 128), ALL, split_axis=0, conc...  42.7 us
    all_to_all x1, waiting for transfers between devices, per_device(): a = lax.all_to_all(a, 'gz', split_axis=0, concat_axis=0, tiled=True)  38.1 us
    all_to_all x1, blocking collectives, per_device(): lax.all_to_all(outgoing.reshape(128, 1, CAP, 2, BW), ALL, split_axis=0, c...  34.2 us
    pallas_call x7, Pallas kernels, in_vmem(): pl.pallas_call(kernel, in_specs=[pl.BlockSpec(memory_space=pltpu.SMEM)] *...  25.1 us
    all_to_all x1, waiting for transfers between devices, per_device(): a = lax.all_to_all(a, 'gy', split_axis=0, concat_axis=0, tiled=True)  12.9 us
    ppermute x6, starting transfers between devices, shifted(): lax.ppermute(piece, axis, [(i, (i + shift) % size) for i in range(size)])  7.67 us
    pallas_call x2, Pallas kernels, scale(): pl.pallas_call(functools.partial(scale_kernel, half, rotated), in_specs=[...  7.33 us
    all_to_all x1, starting transfers between devices, per_device(): a = lax.all_to_all(a, 'gz', split_axis=0, concat_axis=0, tiled=True)  5.87 us
  transfers between devices with their start and end apart: 8, of which 2 were waited for; matrix products, arithmetic and copies ran while one was open for 0% of the time, Pallas kernels for 12%

profile of v11, /device:TPU:1, one launch (start us, length us, event | category | flops | bytes accessed | tf_op | source)
XLA Modules:
  0.0 183.9 jit_solution(18312181422906882192)
XLA Ops:
  0.0 3.4 %scale_a.1 = f32[4,2,8,128,128]{4,3,2,1,0:T(8,128)} custom-call(s32[1]{0:T(128)} %bitcast.place_ref.to_ref.gz_ref, bf16[2,8,8,128,128]{4,3,2,1,0:T(8,128)(2,1)} %bitcast.23, f32[8,8,128,128]{3,2,1,0:T(8,128)} %bitcast.25), custom_call_target="tpu_custom_call" | custom-call | flops 6291456 | bytes 8388608 | tf_op jit(solution)/shard_map/scale_a/pallas_call | solution.py:140
  3.4 5.9 %all-to-all-start = ((f32[4,2,8,128,128]{4,3,2,1,0:T(8,128)}), f32[4,2,8,128,128]{4,3,2,1,0:T(8,128)}, u32[]{:S(2)}, u32[]{:S(2)}) async-start(f32[4,2,8,128,128]{4,3,2,1,0:T(8,128)} %scale_a.1), calls=%async_computation | async-start | bytes 8388608 | tf_op jit(solution)/shard_map/all_to_all | solution.py:391
  9.2 0.0 copy-start.7
  9.2 4.0 %scale_b.1 = (f32[2,8,128,128]{3,2,1,0:T(8,128)S(1)}, f32[2,8,128,128]{3,2,1,0:T(8,128)}, f32[2,8,128,128]{3,2,1,0:T(8,128)}, f32[2,8,128,128]{3,2,1,0:T(8,128)}) custom-call(s32[1]{0:T(128)} %bitcast.3.place_ref, bf16[2,8,8,128,128]{4,3,2,1,0:T(8,128)(2,1)} %bitcast.24, f32[8,8,128,128]{3,2,1,0:T(8,128)} %bitcast.26), custom_call_target="tpu_custom_call" | custom-call | flops 6291456 | bytes 8388608 | tf_op jit(solution)/shard_map/scale_b/pallas_call | solution.py:140
  13.2 0.0 copy-start.2
  13.2 1.0 copy-done.2
  14.2 0.0 copy-start.1
  14.2 1.3 collective-permute-start
  15.5 2.6 %collective-permute-start.1 = (f32[2,8,128,128]{3,2,1,0:T(8,128)}, f32[2,8,128,128]{3,2,1,0:T(8,128)}, u32[]{:S(2)}, u32[]{:S(2)}) collective-permute-start(f32[2,8,128,128]{3,2,1,0:T(8,128)} %get-tuple-element.32), channel_id=1, source_target_pairs={{0,8},{4,12},{8,0},{12,4},{1,9},{5,13},{9,1},{13,5},{2,10},{6,14},... | collective-permute-start | bytes 3145736 | tf_op jit(solution)/shard_map/ppermute | solution.py:374
  18.1 1.1 collective-permute-start.2
  19.2 0.0 copy-done.7
  19.2 0.1 copy.10
  19.3 0.2 fusion.2
  19.6 0.1 copy.11
  19.7 0.4 fusion.1
  20.1 38.1 %all-to-all-done.in_ref = f32[4,2,8,128,128]{4,3,2,1,0:T(8,128)} async-done(((f32[4,2,8,128,128]{4,3,2,1,0:T(8,128)}), f32[4,2,8,128,128]{4,3,2,1,0:T(8,128)}, u32[]{:S(2)}, u32[]{:S(2)}) %all-to-all-start) | async-done | bytes 4194336 | tf_op jit(solution)/shard_map/all_to_all | solution.py:391
  58.1 0.0 copy-done.1
  58.1 6.4 %first_z.1 = f32[4,2,2,128,256]{4,3,2,1,0:T(8,128)} custom-call(f32[4,2,8,128,128]{4,3,2,1,0:T(8,128)} %all-to-all-done.in_ref, bf16[2,4,256,512]{3,2,1,0:T(8,128)(2,1)S(1)} %copy-done.1), custom_call_target="tpu_custom_call" | custom-call | flops 3221225472 | bytes 4194304 | tf_op jit(solution)/shard_map/first_z/pallas_call | solution.py:186
  64.6 0.0 copy-start
  64.6 4.6 %all-to-all-start.1 = ((f32[4,2,2,128,256]{4,3,2,1,0:T(8,128)}), f32[4,2,2,128,256]{4,3,2,1,0:T(8,128)}, u32[]{:S(2)}, u32[]{:S(2)}) async-start(f32[4,2,2,128,256]{4,3,2,1,0:T(8,128)} %first_z.1), calls=%async_computation.1 | async-start | bytes 4194304 | tf_op jit(solution)/shard_map/all_to_all | solution.py:398
  69.2 0.0 collective-permute-done.p1
  69.2 0.0 collective-permute-done.1.p2
  69.2 0.0 collective-permute-done.2.p3
  69.2 0.0 copy-done
  69.2 0.0 copy-start.3
  69.3 1.2 copy-done.3
  70.5 3.7 %first_y.2 = (f32[2,2,256,128]{3,2,1,0:T(8,128)}, f32[2,2,256,128]{3,2,1,0:T(8,128)}) custom-call(s32[1]{0:T(128)} %bitcast.3.place_ref, s32[1]{0:T(128)} %bitcast.place_ref.to_ref.gz_ref, f32[2,8,128,128]{3,2,1,0:T(8,128)S(1)} %copy-done.3, f32[2,8,128,128]{3,2,1,0:T(8,128)} %collective-permute-done.p1, f32[2,8,128,128]{3,2,1,0:T(8,128)} %collective-permute-done.1.p2, ...), custom_call_target="tpu_custom_call" | custom-call | flops 805306368 | bytes 4194304 | tf_op jit(solution)/shard_map/first_y/pallas_call | solution.py:186
  74.2 0.9 collective-permute-start.3
  75.1 1.8 collective-permute-start.4
  76.9 3.4 %first_y.3 = (f32[2,2,256,128]{3,2,1,0:T(8,128)}, f32[2,2,256,128]{3,2,1,0:T(8,128)S(1)}) custom-call(s32[1]{0:T(128)} %bitcast.3.place_ref, s32[1]{0:T(128)} %bitcast.place_ref.to_ref.gz_ref, f32[2,8,128,128]{3,2,1,0:T(8,128)S(1)} %copy-done.3, f32[2,8,128,128]{3,2,1,0:T(8,128)} %collective-permute-done.p1, f32[2,8,128,128]{3,2,1,0:T(8,128)} %collective-permute-done.1.p2, ...), custom_call_target="tpu_custom_call" | custom-call | flops 805306368 | bytes 4194304 | tf_op jit(solution)/shard_map/first_y/pallas_call | solution.py:186
  80.2 0.0 copy-start.5
  80.3 0.8 copy-done.5
  81.1 0.0 collective-permute-start.5
  81.1 12.9 %all-to-all-done.1.in_ref = f32[4,2,2,128,256]{4,3,2,1,0:T(8,128)} async-done(((f32[4,2,2,128,256]{4,3,2,1,0:T(8,128)}), f32[4,2,2,128,256]{4,3,2,1,0:T(8,128)}, u32[]{:S(2)}, u32[]{:S(2)}) %all-to-all-start.1) | async-done | bytes 2097184 | tf_op jit(solution)/shard_map/all_to_all | solution.py:398
  94.0 0.0 copy-start.6
  94.0 2.7 %second_y.1.done_y = f32[2,2,256,256]{3,2,1,0:T(8,128)S(1)} custom-call(f32[4,2,2,128,256]{4,3,2,1,0:T(8,128)} %all-to-all-done.1.in_ref, bf16[2,2,2,256,256]{4,3,2,1,0:T(8,128)(2,1)S(1)} %copy-done), custom_call_target="tpu_custom_call" | custom-call | flops 805306368 | bytes 4194304 | tf_op jit(solution)/shard_map/second_y/pallas_call | solution.py:186
  96.8 0.0 collective-permute-done.3.p1
  96.8 0.0 collective-permute-done.4.p3
  96.8 0.0 copy-done.6
  96.8 2.6 %part_z.1.part_ref = f32[2,256,512]{2,1,0:T(8,128)S(1)} custom-call(s32[1]{0:T(128)} %bitcast.place_ref.to_ref.gz_ref, f32[2,2,256,128]{3,2,1,0:T(8,128)S(1)} %copy-done.6, f32[2,2,256,128]{3,2,1,0:T(8,128)} %collective-permute-done.3.p1, f32[2,2,256,128]{3,2,1,0:T(8,128)} %collective-permute-done.4.p3, bf16[2,4,256,512]{3,2,1,0:T(8,128)(2,1)S(1)} %copy-done.1), custom_call_target="tpu_custom_call" | custom-call | flops 1207959552 | bytes 4194304 | tf_op jit(solution)/shard_map/part_z/pallas_call | solution.py:186
  99.4 0.0 collective-permute-done.5.last_z
  99.4 3.0 %second.1 = f32[4096,128]{1,0:T(8,128)S(1)} custom-call(s32[1]{0:T(128)} %bitcast.place_ref.to_ref.gz_ref, f32[2,2,256,256]{3,2,1,0:T(8,128)S(1)} %second_y.1.done_y, f32[2,256,512]{2,1,0:T(8,128)S(1)} %part_z.1.part_ref, f32[2,2,256,128]{3,2,1,0:T(8,128)} %collective-permute-done.5.last_z, bf16[2,4,256,512]{3,2,1,0:T(8,128)(2,1)S(1)} %copy-done.1), custom_call_target="tpu_custom_call" | custom-call | flops 402653184 | bytes 4194304 | tf_op jit(solution)/shard_map/second/pallas_call | solution.py:186
  102.4 0.0 copy-start.4
  102.4 42.7 %all_to_all.27.in_ref = f32[128,2,2,8,128]{4,3,2,1,0:T(8,128)S(1)} all-to-all(f32[128,2,2,8,128]{4,3,2,1,0:T(8,128)S(1)} %bitcast.21), channel_id=1, replica_groups=mesh['gx'=8,'gy'=4,'gz'=4] {'gx','gy','gz'}, dimensions={0} | all-to-all | bytes 4194304 | tf_op jit(solution)/shard_map/all_to_all | solution.py:410
  145.2 0.0 copy-done.4
  145.2 3.2 %third.1 = f32[4096,128]{1,0:T(8,128)S(1)} custom-call(s32[1024]{0:T(1024)S(1)} %multiply_add_fusion.slot_ref, f32[128,2,2,8,128]{4,3,2,1,0:T(8,128)S(1)} %all_to_all.27.in_ref, bf16[2,2,256,512]{3,2,1,0:T(8,128)(2,1)S(1)} %copy-done.4), custom_call_target="tpu_custom_call" | custom-call | flops 805306368 | bytes 4194304 | tf_op jit(solution)/shard_map/third/pallas_call | solution.py:186
  148.4 34.2 %all_to_all.28 = f32[128,1,16,2,128]{4,3,2,1,0:T(2,128)S(1)} all-to-all(f32[128,1,16,2,128]{4,3,2,1,0:T(2,128)S(1)} %bitcast.22), channel_id=1, replica_groups=mesh['gx'=8,'gy'=4,'gz'=4] {'gx','gy','gz'}, dimensions={0} | all-to-all | bytes 4194304 | tf_op jit(solution)/shard_map/all_to_all | solution.py:413
  182.6 1.3 copy.14
  (5 shorter events, 0.1 us)
Async XLA Ops:
  3.4 54.8 %all-to-all-start = ((f32[4,2,8,128,128]{4,3,2,1,0:T(8,128)}), f32[4,2,8,128,128]{4,3,2,1,0:T(8,128)}, u32[]{:S(2)}, u32[]{:S(2)}) async-start(f32[4,2,8,128,128]{4,3,2,1,0:T(8,128)} %scale_a.1), calls=%async_computation | async-start | bytes 8388608 | tf_op jit(solution)/shard_map/all_to_all | solution.py:391
  9.2 10.0 %copy-start.7 = (s32[1024,1]{0,1:T(1,128)S(1)}, s32[1024,1]{0,1:T(1,128)}, u32[]{:S(2)}) copy-start(s32[1024,1]{0,1:T(1,128)} %param.8) | copy-start | bytes 12292
  13.2 1.0 copy-start.2
  14.2 43.9 %copy-start.1 = (bf16[2,4,256,512]{3,2,1,0:T(8,128)(2,1)S(1)}, bf16[2,4,256,512]{3,2,1,0:T(8,128)(2,1)}, u32[]{:S(2)}) copy-start(bf16[2,4,256,512]{3,2,1,0:T(8,128)(2,1)} %constant.23.clone.table_ref) | copy-start | bytes 6291460
  14.2 55.0 %collective-permute-start = (f32[2,8,128,128]{3,2,1,0:T(8,128)}, f32[2,8,128,128]{3,2,1,0:T(8,128)}, u32[]{:S(2)}, u32[]{:S(2)}) collective-permute-start(f32[2,8,128,128]{3,2,1,0:T(8,128)} %get-tuple-element.31), channel_id=1, source_target_pairs={{0,4},{4,8},{8,12},{12,0},{1,5},{5,9},{9,13},{13,1},{2,6},{6,10},{... | collective-permute-start | bytes 3145736 | tf_op jit(solution)/shard_map/ppermute | solution.py:374
  15.5 53.7 %collective-permute-start.1 = (f32[2,8,128,128]{3,2,1,0:T(8,128)}, f32[2,8,128,128]{3,2,1,0:T(8,128)}, u32[]{:S(2)}, u32[]{:S(2)}) collective-permute-start(f32[2,8,128,128]{3,2,1,0:T(8,128)} %get-tuple-element.32), channel_id=1, source_target_pairs={{0,8},{4,12},{8,0},{12,4},{1,9},{5,13},{9,1},{13,5},{2,10},{6,14},... | collective-permute-start | bytes 3145736 | tf_op jit(solution)/shard_map/ppermute | solution.py:374
  18.1 51.1 %collective-permute-start.2 = (f32[2,8,128,128]{3,2,1,0:T(8,128)}, f32[2,8,128,128]{3,2,1,0:T(8,128)}, u32[]{:S(2)}, u32[]{:S(2)}) collective-permute-start(f32[2,8,128,128]{3,2,1,0:T(8,128)} %get-tuple-element.33), channel_id=1, source_target_pairs={{0,12},{4,0},{8,4},{12,8},{1,13},{5,1},{9,5},{13,9},{2,14},{6,2},{... | collective-permute-start | bytes 3145736 | tf_op jit(solution)/shard_map/ppermute | solution.py:374
  64.6 4.7 %copy-start = (bf16[2,2,2,256,256]{4,3,2,1,0:T(8,128)(2,1)S(1)}, bf16[2,2,2,256,256]{4,3,2,1,0:T(8,128)(2,1)}, u32[]{:S(2)}) copy-start(bf16[2,2,2,256,256]{4,3,2,1,0:T(8,128)(2,1)} %constant.22.clone.table_ref) | copy-start | bytes 3145732
  64.6 29.4 %all-to-all-start.1 = ((f32[4,2,2,128,256]{4,3,2,1,0:T(8,128)}), f32[4,2,2,128,256]{4,3,2,1,0:T(8,128)}, u32[]{:S(2)}, u32[]{:S(2)}) async-start(f32[4,2,2,128,256]{4,3,2,1,0:T(8,128)} %first_z.1), calls=%async_computation.1 | async-start | bytes 4194304 | tf_op jit(solution)/shard_map/all_to_all | solution.py:398
  69.2 1.2 copy-start.3
  74.2 22.6 %collective-permute-start.3 = (f32[2,2,256,128]{3,2,1,0:T(8,128)}, f32[2,2,256,128]{3,2,1,0:T(8,128)}, u32[]{:S(2)}, u32[]{:S(2)}) collective-permute-start(f32[2,2,256,128]{3,2,1,0:T(8,128)} %get-tuple-element.38), channel_id=1, source_target_pairs={{0,1},{1,2},{2,3},{3,0},{4,5},{5,6},{6,7},{7,4},{8,9},{9,10},{10,1... | collective-permute-start | bytes 1572872 | tf_op jit(solution)/shard_map/ppermute | solution.py:374
  75.1 21.7 %collective-permute-start.4 = (f32[2,2,256,128]{3,2,1,0:T(8,128)}, f32[2,2,256,128]{3,2,1,0:T(8,128)}, u32[]{:S(2)}, u32[]{:S(2)}) collective-permute-start(f32[2,2,256,128]{3,2,1,0:T(8,128)} %get-tuple-element.39), channel_id=1, source_target_pairs={{0,3},{1,0},{2,1},{3,2},{4,7},{5,4},{6,5},{7,6},{8,11},{9,8},{10,9... | collective-permute-start | bytes 1572872 | tf_op jit(solution)/shard_map/ppermute | solution.py:374
  80.2 0.8 copy-start.5
  81.1 18.3 %collective-permute-start.5 = (f32[2,2,256,128]{3,2,1,0:T(8,128)}, f32[2,2,256,128]{3,2,1,0:T(8,128)}, u32[]{:S(2)}, u32[]{:S(2)}) collective-permute-start(f32[2,2,256,128]{3,2,1,0:T(8,128)} %get-tuple-element.44), channel_id=1, source_target_pairs={{0,2},{1,3},{2,0},{3,1},{4,6},{5,7},{6,4},{7,5},{8,10},{9,11},{10,... | collective-permute-start | bytes 1572872 | tf_op jit(solution)/shard_map/ppermute | solution.py:374
  94.0 2.7 %copy-start.6 = (f32[2,2,256,128]{3,2,1,0:T(8,128)S(1)}, f32[2,2,256,128]{3,2,1,0:T(8,128)}, u32[]{:S(2)}) copy-start(f32[2,2,256,128]{3,2,1,0:T(8,128)} %copy-done.5) | copy-start | bytes 1572868
  102.4 42.7 %copy-start.4 = (bf16[2,2,256,512]{3,2,1,0:T(8,128)(2,1)S(1)}, bf16[2,2,256,512]{3,2,1,0:T(8,128)(2,1)}, u32[]{:S(2)}) copy-start(bf16[2,2,256,512]{3,2,1,0:T(8,128)(2,1)} %constant.21.clone.table_ref) | copy-start | bytes 3145732

commit v12 on v0

v12 whole, which is shorter than its diff:
```python
import functools

import jax
import jax.numpy as jnp
import ml_dtypes
import numpy as np
from jax import lax
from jax.experimental import pallas as pl
from jax.experimental.pallas import tpu as pltpu
from jax.sharding import PartitionSpec as P

N = 512
KEPT = 256
BW = 128
CAP = 16
ALL = ("gx", "gy", "gz")
MIB = 1 << 20
VMEM = 24


def split_table(table):
    high = table.astype(np.float32).astype(ml_dtypes.bfloat16)
    low = (table - high.astype(np.float64)).astype(np.float32).astype(ml_dtypes.bfloat16)
    return np.stack([high, low])


def cos_sin(positions, kept):
    angles = (positions[:, None] * kept[None, :] % N) * (2.0 * np.pi / N)
    return np.cos(angles), np.sin(angles)


@functools.cache
def tables():
    order = np.arange(KEPT).reshape(KEPT // 2, 2).T.reshape(-1)
    cosine, sine = cos_sin(np.arange(N // 2), order)
    cosine, sine = (t.reshape(2, 128, 2, 128).transpose(0, 2, 1, 3) for t in (cosine, sine))
    real_rows = np.concatenate([cosine, -sine], 3)
    imag_rows = np.concatenate([sine, cosine], 3)
    table_z = np.concatenate([real_rows, imag_rows], 2)
    cosine, sine = cos_sin(np.arange(N // 2), order)
    cosine, sine = (t.T.reshape(2, 128, 2, 128).transpose(2, 0, 1, 3) for t in (cosine, sine))
    top = np.concatenate([cosine, sine], 3)
    bottom = np.concatenate([-sine, cosine], 3)
    table_y = np.concatenate([top, bottom], 2)
    gx, gy, gz = np.meshgrid(np.arange(8), np.arange(4), np.arange(4), indexing="ij")
    first = 64 * gx + 8 * gz + 2 * gy
    second = 64 * gx + 32 + 8 * gy + 2 * gz
    cells = np.stack([first, first + 1, second, second + 1], -1).reshape(128, 4)
    cosine, sine = cos_sin(cells[:64].reshape(-1), order)
    cosine, sine = (
        t.T.reshape(2, KEPT // 2, 64, 1, 4) for t in (cosine, sine)
    )
    top = np.concatenate([cosine, sine], 3).reshape(2, KEPT // 2, 512)
    bottom = np.concatenate([-sine, cosine], 3).reshape(2, KEPT // 2, 512)
    table_x = np.concatenate([top, bottom], 1)
    ordering = np.zeros((KEPT, KEPT), ml_dtypes.bfloat16)
    ordering[np.arange(KEPT), order] = 1
    return split_table(table_x), split_table(table_y), split_table(table_z), ordering


def halves(values):
    high = values.astype(jnp.bfloat16)
    low = (values - high.astype(jnp.float32)).astype(jnp.bfloat16)
    return high, low


def product(left, right):
    def dot(a, b):
        return jnp.dot(a, b, preferred_element_type=jnp.float32)

    return dot(left[0], right[0]) + (dot(left[0], right[1]) + dot(left[1], right[0]))


def params(mib):
    return pltpu.CompilerParams(vmem_limit_bytes=mib * MIB)


def cost(multiplies, moved):
    return pl.CostEstimate(flops=6 * multiplies, bytes_accessed=moved, transcendentals=0)


def rows_z(piece):
    return halves(jnp.concatenate([piece[plane].reshape(-1, 128) for plane in range(2)], axis=1))


def columns_y(piece):
    planes, cells = piece.shape[:2]
    return halves(
        jnp.concatenate([piece[:, x].reshape(256, piece.shape[3]) for x in range(cells)], axis=1)
    )


def in_hbm(*arrays):
    return [pltpu.with_memory_space_constraint(x, pltpu.HBM) for x in arrays]


def scale_kernel(half, shifts, rotated, place_ref, normals_ref, spectrum_ref, *refs):
    *out_refs, held_out, held_n, held_s, semaphores = refs

    def gets(i):
        chunk = 4 * half + (lax.rem(place_ref[0] + shifts[i], 4) if rotated else shifts[i])
        return (
            pltpu.make_async_copy(normals_ref.at[:, chunk], held_n.at[i], semaphores.at[i, 0]),
            pltpu.make_async_copy(spectrum_ref.at[chunk], held_s.at[i], semaphores.at[i, 1]),
        )

    def put(i):
        target = out_refs[i] if rotated else out_refs[0].at[shifts[i]]
        return pltpu.make_async_copy(held_out.at[i], target, semaphores.at[i, 2])

    steps = range(len(shifts))
    for i in steps:
        for copy in gets(i):
            copy.start()
    for i in steps:
        for copy in gets(i):
            copy.wait()
        for plane in range(2):
            held_out[i, plane] = held_n[i, plane].astype(jnp.float32) * held_s[i]
        put(i).start()
    for i in steps:
        put(i).wait()


def scale(half, shifts, rotated, place, normals, spectrum):
    chunk = (2, 8, 128, 128)
    count = len(shifts)
    shapes = [chunk] * count if rotated else [(count,) + chunk]
    hbm = pl.BlockSpec(memory_space=pltpu.HBM)
    return pl.pallas_call(
        functools.partial(scale_kernel, half, shifts, rotated),
        in_specs=[pl.BlockSpec(memory_space=pltpu.SMEM)] + [hbm] * 2,
        out_specs=[hbm] * len(shapes),
        out_shape=[pltpu.HBM(shape, jnp.float32) for shape in shapes],
        scratch_shapes=[
            pltpu.VMEM((count,) + chunk, jnp.float32),
            pltpu.VMEM((count,) + chunk, jnp.bfloat16),
            pltpu.VMEM((count,) + chunk[1:], jnp.float32),
            pltpu.SemaphoreType.DMA((count, 3)),
        ],
        compiler_params=params(VMEM),
        cost_estimate=cost(count << 18, 2 * count * MIB),
        name="scale_b" if rotated else "scale_a",
    )(place, *in_hbm(normals.reshape(2, 8, 8, 128, 128), spectrum.reshape(8, 8, 128, 128)))


def transform(along_z, pairs, table_ref):
    parts = []
    for odd in range(2):
        total = None
        for first, second, g in pairs:
            base = lax.rem(g, 2)
            table = (table_ref[0, base, odd], table_ref[1, base, odd])
            if odd:
                sides = (first - second) * jnp.where(g < 2, 1.0, -1.0).astype(jnp.float32)
            else:
                sides = first + second
            if along_z:
                term = product(rows_z(sides), table)
            else:
                term = product(table, columns_y(sides))
            total = term if total is None else total + term
        parts.append(total)
    return parts


def first_kernel(along_z, shifts, dynamic, place_ref, to_ref, *refs):
    in_refs, refs = (refs[:4], refs[4:]) if dynamic else (refs[:1], refs[1:])
    table_ref, *out_refs, pieces, held_out, semaphores = refs

    def gets(i):
        cells = pl.ds(2 * lax.rem(to_ref[0] + shifts[i], 4), 2)
        if not dynamic:
            source = in_refs[0].at[:, :, cells]
            return [pltpu.make_async_copy(source, pieces.at[i], semaphores.at[i, 0])]
        return [
            pltpu.make_async_copy(ref.at[:, cells], pieces.at[i, s], semaphores.at[i, s])
            for s, ref in enumerate(in_refs)
        ]

    def put(i):
        return pltpu.make_async_copy(held_out.at[i], out_refs[i], semaphores.at[i, 4])

    steps = range(len(shifts))
    for i in steps:
        for copy in gets(i):
            copy.start()
    for i in steps:
        for copy in gets(i):
            copy.wait()
        if dynamic:
            g, h = place_ref[0], lax.rem(place_ref[0] + 3, 4)
        else:
            g, h = 0, 1
        pairs = [(pieces[i, 0], pieces[i, 2], g), (pieces[i, 1], pieces[i, 3], h)]
        for odd, values in enumerate(transform(along_z, pairs, table_ref)):
            half = slice(odd * 128, (odd + 1) * 128)
            for plane in range(2):
                part = slice(plane * 128, (plane + 1) * 128)
                for x in range(2):
                    cell = slice(x * 128, (x + 1) * 128)
                    if along_z:
                        held_out[i, plane, x, :, half] = values[cell, part]
                    else:
                        held_out[i, plane, x, half] = values[part, cell]
        put(i).start()
    for i in steps:
        put(i).wait()


def first(along_z, shifts, place, to, arrived, table):
    dynamic = isinstance(arrived, list)
    operands = arrived if dynamic else [arrived]
    shape = (2, 2, 128, KEPT) if along_z else (2, 2, KEPT, 128)
    hbm = pl.BlockSpec(memory_space=pltpu.HBM)
    count = len(shifts)
    return pl.pallas_call(
        functools.partial(first_kernel, along_z, shifts, dynamic),
        in_specs=[pl.BlockSpec(memory_space=pltpu.SMEM)] * 2
        + [hbm] * len(operands)
        + [pl.BlockSpec(memory_space=pltpu.VMEM)],
        out_specs=[hbm] * count,
        out_shape=[pltpu.HBM(shape, jnp.float32)] * count,
        scratch_shapes=[
            pltpu.VMEM((count, 4, 2, 2, 128, 128), jnp.float32),
            pltpu.VMEM((count,) + shape, jnp.float32),
            pltpu.SemaphoreType.DMA((count, 5)),
        ],
        compiler_params=params(VMEM),
        cost_estimate=cost(count * 256 * 512 * 512, 2 * count * MIB),
        name="first_z" if along_z else "first_y",
    )(place, to, *in_hbm(*operands), table)


def second_y_kernel(place_ref, p0, p1, p2, p3, table_ref, out_ref):
    g, h = place_ref[0], lax.rem(place_ref[0] + 3, 4)
    pairs = [(p0[...], p2[...], g), (p1[...], p3[...], h)]
    for odd, values in enumerate(transform(False, pairs, table_ref)):
        for plane in range(2):
            out_ref[0, plane, odd * 128 : (odd + 1) * 128] = values[
                plane * 128 : (plane + 1) * 128
            ]


def second_y(place, pieces, table):
    return pl.pallas_call(
        second_y_kernel,
        grid_spec=pltpu.PrefetchScalarGridSpec(
            num_scalar_prefetch=1,
            grid=(2,),
            in_specs=[pl.BlockSpec((2, 1, 128, KEPT), lambda i, place: (0, i, 0, 0))] * 4
            + [pl.BlockSpec(table.shape, lambda i, place: (0, 0, 0, 0, 0))],
            out_specs=pl.BlockSpec((1, 2, KEPT, KEPT), lambda i, place: (i, 0, 0, 0)),
        ),
        out_shape=jax.ShapeDtypeStruct((2, 2, KEPT, KEPT), jnp.float32),
        compiler_params=params(VMEM),
        cost_estimate=cost(512 * 512 * 512, 5 * MIB),
        name="second_y",
    )(place, *pieces, table)


def part_z_kernel(place_ref, p1, p3, table_ref, out_ref):
    pairs = [(p1[...], p3[...], lax.rem(place_ref[0] + 3, 4))]
    for odd, values in enumerate(transform(True, pairs, table_ref)):
        out_ref[0, :, odd * 256 : (odd + 1) * 256] = values


def part_z(place, pieces, table):
    return pl.pallas_call(
        part_z_kernel,
        grid_spec=pltpu.PrefetchScalarGridSpec(
            num_scalar_prefetch=1,
            grid=(2,),
            in_specs=[pl.BlockSpec((2, 1, KEPT, 128), lambda i, place: (0, i, 0, 0))] * 2
            + [pl.BlockSpec(table.shape, lambda i, place: (0, 0, 0, 0, 0))],
            out_specs=pl.BlockSpec((1, KEPT, 512), lambda i, place: (i, 0, 0)),
        ),
        out_shape=jax.ShapeDtypeStruct((2, KEPT, 512), jnp.float32),
        compiler_params=params(VMEM),
        cost_estimate=cost(512 * 512 * 256, 4 * MIB),
        name="part_z",
    )(place, *pieces, table)


def second_kernel(place_ref, done_y, part_ref, p0, p2, table_ref, out_ref, held):
    def put(values, half, row):
        held[pl.ds(half * 8 + row, 128, stride=16), :] = values

    parts = transform(True, [(p0[...], p2[...], place_ref[0])], table_ref)
    for half, values in enumerate(parts):
        values = values + part_ref[:, :, half * 256 : (half + 1) * 256].reshape(256, 256)
        for x in range(2):
            for plane in range(2):
                put(done_y[x, plane, :, half * 128 : (half + 1) * 128], half, plane * 4 + x)
                put(
                    values[x * 128 : (x + 1) * 128, plane * 128 : (plane + 1) * 128],
                    half,
                    plane * 4 + 2 + x,
                )
    out_ref[...] = held[...].reshape(128, 1, 2, 8, 128)


def second(place, done_y, part, pieces, table):
    return pl.pallas_call(
        second_kernel,
        grid_spec=pltpu.PrefetchScalarGridSpec(
            num_scalar_prefetch=1,
            grid=(2,),
            in_specs=[
                pl.BlockSpec((2, 2, 128, KEPT), lambda i, place: (0, 0, i, 0)),
                pl.BlockSpec((2, 128, 512), lambda i, place: (0, i, 0)),
            ]
            + [pl.BlockSpec((2, 2, 128, 128), lambda i, place: (0, 0, i, 0))] * 2
            + [pl.BlockSpec(table.shape, lambda i, place: (0, 0, 0, 0, 0))],
            out_specs=pl.BlockSpec((128, 1, 2, 8, 128), lambda i, place: (0, i, 0, 0, 0)),
            scratch_shapes=[pltpu.VMEM((2048, 128), jnp.float32)],
        ),
        out_shape=jax.ShapeDtypeStruct((128, 2, 2, 8, 128), jnp.float32),
        compiler_params=params(VMEM),
        cost_estimate=cost(512 * 512 * 256, 6 * MIB),
        name="second",
    )(place, done_y, part, *pieces, table)


def third_kernel(slot_ref, in_ref, table_ref, ordering_ref, out_ref, held):
    out_ref[...] = jnp.zeros_like(out_ref)
    for parity in range(2):
        columns = jnp.concatenate(
            [in_ref[:, parity, half].reshape(1024, 128) for half in range(2)], axis=1
        )
        first, last = columns[:512], columns[512:]
        for odd, sides in enumerate((first + last, first - last)):
            sides = tuple(
                jnp.dot(
                    part, ordering_ref[...], preferred_element_type=jnp.float32
                ).astype(jnp.bfloat16)
                for part in halves(sides)
            )
            values = jnp.exp(product((table_ref[0, odd], table_ref[1, odd]), sides))
            for plane in range(2):
                for half in range(2):
                    held[parity, plane, half, odd * 128 : (odd + 1) * 128] = values[
                        plane * 128 : (plane + 1) * 128, half * 128 : (half + 1) * 128
                    ]

    def place_rows(group, carry):
        for offset in range(4):
            x = group * 4 + offset
            row = group * 2 + offset // 2 + 128 * (offset % 2)
            for parity in range(2):
                for half in range(2):
                    slot = slot_ref[x * 4 + parity * 2 + half]
                    for plane in range(2):
                        out_ref[pl.ds(slot * 2 + plane, 1), :] = held[
                            parity, plane, half, pl.ds(row, 1), :
                        ]
        return carry

    lax.fori_loop(0, KEPT // 4, place_rows, 0)


def third(slots, arrived, table_x, ordering):
    vmem = pl.BlockSpec(memory_space=pltpu.VMEM)
    return pl.pallas_call(
        third_kernel,
        in_specs=[pl.BlockSpec(memory_space=pltpu.SMEM)] + [vmem] * 3,
        out_specs=vmem,
        out_shape=jax.ShapeDtypeStruct((4096, 128), jnp.float32),
        scratch_shapes=[pltpu.VMEM((2, 2, 2, KEPT, 128), jnp.float32)],
        compiler_params=params(VMEM),
        cost_estimate=cost(768 * 512 * 512, 6 * MIB),
        name="third",
    )(slots, arrived, table_x, ordering)


def shifted(piece, axis, shift):
    size = lax.axis_size(axis)
    return lax.ppermute(piece, axis, [(i, (i + shift) % size) for i in range(size)])


def slots_of(block_owner):
    destination = block_owner[:, 0]
    one_hot = (destination[:, None] == jnp.arange(128, dtype=jnp.int32)[None, :]).astype(jnp.int32)
    earlier = jnp.cumsum(one_hot, axis=0) - one_hot
    return destination * CAP + jnp.sum(earlier * one_hot, axis=1)


def per_device(normals, spectrum, block_owner):
    table_x, table_y, table_z, ordering = (jnp.asarray(table) for table in tables())
    gy = lax.axis_index("gy").astype(jnp.int32).reshape(1)
    gz = lax.axis_index("gz").astype(jnp.int32).reshape(1)

    (a,) = scale(0, (0, 1, 2, 3), False, gz, normals, spectrum)
    a, place = lax.optimization_barrier((a, gy))
    a = lax.all_to_all(a, "gz", split_axis=0, concat_axis=0, tiled=True)
    b1, b3, b2 = scale(1, (1, 3, 2), True, place, normals, spectrum)
    place, b1, b3, b2 = lax.optimization_barrier((place, b1, b3, b2))
    b1, b3, b2 = shifted(b1, "gy", 1), shifted(b3, "gy", 3), shifted(b2, "gy", 2)
    (b0,) = scale(1, (0,), True, place, normals, spectrum)

    a, slots, b0 = lax.optimization_barrier((a, slots_of(block_owner), b0))
    a1, a3, a2, a0 = first(True, (1, 3, 2, 0), gz, gy, a, table_z)
    b1, b2, b3, _ = lax.optimization_barrier((b1, b2, b3, a1))
    pieces = [b0, b1, b2, b3]
    a1, a3 = shifted(a1, "gy", 1), shifted(a3, "gy", 3)
    b1, b3 = first(False, (1, 3), gy, gz, pieces, table_y)
    a2, b1, b3 = lax.optimization_barrier((a2, b1, b3))
    b1, b3, a2 = shifted(b1, "gz", 1), shifted(b3, "gz", 3), shifted(a2, "gy", 2)
    b2, b0 = first(False, (2, 0), gy, gz, pieces, table_y)
    b2 = shifted(b2, "gz", 2)

    part_b = part_z(gz, (b1, b3), table_z)
    done_a = second_y(gy, (a0, a1, a2, a3), table_y)
    done_a, part_b, b2 = lax.optimization_barrier((done_a, part_b, b2))
    planes = second(gz, done_a, part_b, (b0, b2), table_z)
    lines = lax.all_to_all(planes, ALL, split_axis=0, concat_axis=0, tiled=True)
    outgoing = third(slots, lines, table_x, ordering)
    return lax.all_to_all(
        outgoing.reshape(128, 1, CAP, 2, BW), ALL, split_axis=0, concat_axis=1, tiled=True
    )


def solution(mesh):
    placed = (P(None, "gx", "gy", "gz"), P("gx", "gy", "gz"), P(ALL, None))
    return jax.shard_map(
        per_device,
        mesh=mesh,
        in_specs=placed,
        out_specs=P(ALL, None, None, None, None),
        check_vma=False,
    )
```

time: 400 us -> 176 us (0.44); the launches traced: 394 us -> 176 us
  blocking collectives: 228 us -> 72.8 us
  local copies, waits for them, and re-layouts: 62.9 us -> 2.54 us
  matrix products: 58 us -> 0 us
  Pallas kernels: 0 us -> 27.8 us
  waiting for transfers between devices: 28.4 us -> 53.7 us
  starting transfers between devices: 8.44 us -> 18 us
  other arithmetic: 7.39 us -> 0.63 us
    all_to_all x3 -> x2, blocking collectives: 228 us -> 72.8 us  [the longest x1 38.5 us: per_device(): lines = lax.all_to_all(planes, ALL, split_axis=0, concat_axis=0, tiled=True)]
    dot_general x12 -> x0, matrix products: 58 us -> none  [contract(): return jnp.einsum(form, operand, matrix, precision=lax.Precision.HIGHEST)]
    pallas_call x0 -> x10, Pallas kernels: none -> 27.8 us  [the longest x3 11.3 us: first(): pl.pallas_call(functools.partial(first_kernel, along_z, shifts, dynamic),...]
    unnamed x15 -> x23, local copies, waits for them, and re-layouts: 28.5 us -> 2.33 us
    ppermute x0 -> x9, waiting for transfers between devices: none -> 16.3 us  [shifted(): lax.ppermute(piece, axis, [(i, (i + shift) % size) for i in range(size)])]
    squeeze x4 -> x0, local copies, waits for them, and re-layouts: 13.3 us -> none  [the longest x2 6.71 us: transform(): field_pair[0]]
    slice x4 -> x0, local copies, waits for them, and re-layouts: 12.7 us -> none  [the longest x3 8.08 us: transform(): field_pair[0]]
    ppermute x0 -> x9, starting transfers between devices: none -> 12.2 us  [shifted(): lax.ppermute(piece, axis, [(i, (i + shift) % size) for i in range(size)])]
  transfers between devices with their start and end apart: 1 -> 10, of which waited for: 1 -> 5; matrix products, arithmetic and copies ran while one was open for 0% -> 0% of each run, Pallas kernels for 0% -> 9%
where the time goes in v12:
time: 176 us
  blocking collectives  72.8 us (41%)
  waiting for transfers between devices  53.7 us (31%)
  Pallas kernels  27.8 us (16%)
  starting transfers between devices  18 us (10%)
  local copies, waits for them, and re-layouts  2.54 us (1%)
    all_to_all x1, blocking collectives, per_device(): lines = lax.all_to_all(planes, ALL, split_axis=0, concat_axis=0, tiled=True)  38.5 us
    all_to_all x1, waiting for transfers between devices, per_device(): a = lax.all_to_all(a, 'gz', split_axis=0, concat_axis=0, tiled=True)  37.4 us
    all_to_all x1, blocking collectives, per_device(): lax.all_to_all(outgoing.reshape(128, 1, CAP, 2, BW), ALL, split_axis=0, c...  34.2 us
    ppermute x9, waiting for transfers between devices, shifted(): lax.ppermute(piece, axis, [(i, (i + shift) % size) for i in range(size)])  16.3 us
    ppermute x9, starting transfers between devices, shifted(): lax.ppermute(piece, axis, [(i, (i + shift) % size) for i in range(size)])  12.2 us
    pallas_call x3, Pallas kernels, first(): pl.pallas_call(functools.partial(first_kernel, along_z, shifts, dynamic),...  11.3 us
    pallas_call x3, Pallas kernels, scale(): pl.pallas_call(functools.partial(scale_kernel, half, shifts, rotated), in...  8.86 us
    all_to_all x1, starting transfers between devices, per_device(): a = lax.all_to_all(a, 'gz', split_axis=0, concat_axis=0, tiled=True)  5.87 us
  transfers between devices with their start and end apart: 10, of which 5 were waited for; matrix products, arithmetic and copies ran while one was open for 0% of the time, Pallas kernels for 9%

profile of v12, /device:TPU:1, one launch (start us, length us, event | category | flops | bytes accessed | tf_op | source)
XLA Modules:
  0.0 175.7 jit_solution(8006011841777836619)
XLA Ops:
  0.0 3.4 %scale_a.1 = f32[4,2,8,128,128]{4,3,2,1,0:T(8,128)} custom-call(s32[1]{0:T(128)} %bitcast.place_ref.to_ref, bf16[2,8,8,128,128]{4,3,2,1,0:T(8,128)(2,1)} %bitcast.21, f32[8,8,128,128]{3,2,1,0:T(8,128)} %bitcast.24), custom_call_target="tpu_custom_call" | custom-call | flops 6291456 | bytes 8388608 | tf_op jit(solution)/shard_map/scale_a/pallas_call | solution.py:130
  3.4 5.9 %all-to-all-start = ((f32[4,2,8,128,128]{4,3,2,1,0:T(8,128)}), f32[4,2,8,128,128]{4,3,2,1,0:T(8,128)}, u32[]{:S(2)}, u32[]{:S(2)}) async-start(f32[4,2,8,128,128]{4,3,2,1,0:T(8,128)} %scale_a.1), calls=%async_computation | async-start | bytes 8388608 | tf_op jit(solution)/shard_map/all_to_all | solution.py:395
  9.2 3.1 %scale_b.2 = (f32[2,8,128,128]{3,2,1,0:T(8,128)}, f32[2,8,128,128]{3,2,1,0:T(8,128)}, f32[2,8,128,128]{3,2,1,0:T(8,128)}) custom-call(s32[1]{0:T(128)} %bitcast.3.place_ref.to_ref, bf16[2,8,8,128,128]{4,3,2,1,0:T(8,128)(2,1)} %bitcast.22, f32[8,8,128,128]{3,2,1,0:T(8,128)} %bitcast.25), custom_call_target="tpu_custom_call" | custom-call | flops 4718592 | bytes 6291456 | tf_op jit(solution)/shard_map/scale_b/pallas_call | solution.py:130
  12.4 1.4 collective-permute-start.1
  13.7 2.6 %collective-permute-start.2 = (f32[2,8,128,128]{3,2,1,0:T(8,128)}, f32[2,8,128,128]{3,2,1,0:T(8,128)}, u32[]{:S(2)}, u32[]{:S(2)}) collective-permute-start(f32[2,8,128,128]{3,2,1,0:T(8,128)} %get-tuple-element.47), channel_id=1, source_target_pairs={{0,8},{4,12},{8,0},{12,4},{1,9},{5,13},{9,1},{13,5},{2,10},{6,14},... | collective-permute-start | bytes 3145736 | tf_op jit(solution)/shard_map/ppermute | solution.py:378
  16.4 1.1 collective-permute-start.3
  17.4 0.0 copy-done.7
  17.4 0.1 copy.11
  17.5 0.2 fusion.2
  17.8 0.1 copy.12
  17.9 0.0 copy-start.1
  18.0 2.4 %scale_b.3.refs_0_ = f32[2,8,128,128]{3,2,1,0:T(8,128)} custom-call(s32[1]{0:T(128)} %bitcast.3.place_ref.to_ref, bf16[2,8,8,128,128]{4,3,2,1,0:T(8,128)(2,1)} %bitcast.23, f32[8,8,128,128]{3,2,1,0:T(8,128)} %bitcast.26), custom_call_target="tpu_custom_call" | custom-call | flops 1572864 | bytes 2097152 | tf_op jit(solution)/shard_map/scale_b/pallas_call | solution.py:130
  20.3 0.4 fusion.1
  20.7 0.0 copy-start
  20.7 37.4 %all-to-all-done.refs_0_ = f32[4,2,8,128,128]{4,3,2,1,0:T(8,128)} async-done(((f32[4,2,8,128,128]{4,3,2,1,0:T(8,128)}), f32[4,2,8,128,128]{4,3,2,1,0:T(8,128)}, u32[]{:S(2)}, u32[]{:S(2)}) %all-to-all-start) | async-done | bytes 4194336 | tf_op jit(solution)/shard_map/all_to_all | solution.py:395
  58.1 0.0 copy-done.1
  58.1 4.5 %first_z.1 = (f32[2,2,128,256]{3,2,1,0:T(8,128)}, f32[2,2,128,256]{3,2,1,0:T(8,128)}, f32[2,2,128,256]{3,2,1,0:T(8,128)}, f32[2,2,128,256]{3,2,1,0:T(8,128)}) custom-call(s32[1]{0:T(128)} %bitcast.place_ref.to_ref, s32[1]{0:T(128)} %bitcast.3.place_ref.to_ref, f32[4,2,8,128,128]{4,3,2,1,0:T(8,128)} %all-to-all-done.refs_0_, ...), custom_call_target="tpu_custom_call" | custom-call | flops 1610612736 | bytes 8388608 | tf_op jit(solution)/shard_map/first_z/pallas_call | solution.py:217
  62.7 0.0 collective-permute-done.1.refs_1_
  62.7 0.0 copy-start.6
  62.7 0.0 collective-permute-done.2.refs_2_
  62.7 0.0 collective-permute-done.3.refs_3_
  62.7 1.0 copy-done.6
  63.7 0.0 copy-done
  63.7 3.4 %first_y.2 = (f32[2,2,256,128]{3,2,1,0:T(8,128)}, f32[2,2,256,128]{3,2,1,0:T(8,128)}) custom-call(s32[1]{0:T(128)} %bitcast.3.place_ref.to_ref, s32[1]{0:T(128)} %bitcast.place_ref.to_ref, f32[2,8,128,128]{3,2,1,0:T(8,128)} %scale_b.3.refs_0_, f32[2,8,128,128]{3,2,1,0:T(8,128)} %copy-done.6, f32[2,8,128,128]{3,2,1,0:T(8,128)} %collective-permute-done.2.refs_2_, ...), custom_call_target="tpu_custom_call" | custom-call | flops 805306368 | bytes 4194304 | tf_op jit(solution)/shard_map/first_y/pallas_call | solution.py:217
  67.1 1.0 collective-permute-start.6
  68.1 1.7 collective-permute-start.7
  69.9 0.0 copy-done.9
  69.9 1.3 collective-permute-start
  71.2 1.5 collective-permute-start.5
  72.7 1.6 collective-permute-start.4
  74.2 3.4 %first_y.3 = (f32[2,2,256,128]{3,2,1,0:T(8,128)}, f32[2,2,256,128]{3,2,1,0:T(8,128)}) custom-call(s32[1]{0:T(128)} %bitcast.3.place_ref.to_ref, s32[1]{0:T(128)} %bitcast.place_ref.to_ref, f32[2,8,128,128]{3,2,1,0:T(8,128)} %scale_b.3.refs_0_, f32[2,8,128,128]{3,2,1,0:T(8,128)} %copy-done.6, f32[2,8,128,128]{3,2,1,0:T(8,128)} %collective-permute-done.2.refs_2_, ...), custom_call_target="tpu_custom_call" | custom-call | flops 805306368 | bytes 4194304 | tf_op jit(solution)/shard_map/first_y/pallas_call | solution.py:217
  77.6 2.8 %collective-permute-done.6.p1 = f32[2,2,256,128]{3,2,1,0:T(8,128)S(1)} collective-permute-done((f32[2,2,256,128]{3,2,1,0:T(8,128)}, f32[2,2,256,128]{3,2,1,0:T(8,128)S(1)}, u32[]{:S(2)}, u32[]{:S(2)}) %collective-permute-start.6) | collective-permute-done | bytes 524320 | tf_op jit(solution)/shard_map/ppermute | solution.py:378
  80.4 0.0 collective-permute-start.8
  80.4 0.0 collective-permute-done.7.p3
  80.4 0.9 part_z.1.part_ref
  81.3 0.8 collective-permute-done.5.p3
  82.2 0.3 collective-permute-done.p1
  82.5 12.4 %collective-permute-done.4.p2 = f32[2,2,128,256]{3,2,1,0:T(8,128)S(1)} collective-permute-done((f32[2,2,128,256]{3,2,1,0:T(8,128)S(1)}, f32[2,2,128,256]{3,2,1,0:T(8,128)S(1)}, u32[]{:S(2)}, u32[]{:S(2)}) %collective-permute-start.4) | collective-permute-done | bytes 524320 | tf_op jit(solution)/shard_map/ppermute | solution.py:378
  94.8 1.4 second_y.1.done_y
  96.3 0.0 collective-permute-done.8.p2
  96.3 0.0 copy-done.4
  96.3 1.6 second.1
  97.9 0.0 copy-start.2
  97.9 0.0 copy-start.5
  97.9 38.5 %all_to_all.22.in_ref = f32[128,2,2,8,128]{4,3,2,1,0:T(8,128)S(1)} all-to-all(f32[128,2,2,8,128]{4,3,2,1,0:T(8,128)S(1)} %second.1), channel_id=1, replica_groups=mesh['gx'=8,'gy'=4,'gz'=4] {'gx','gy','gz'}, dimensions={0} | all-to-all | bytes 4194304 | tf_op jit(solution)/shard_map/all_to_all | solution.py:416
  136.4 3.7 %third.1 = f32[4096,128]{1,0:T(8,128)S(1)} custom-call(s32[1024]{0:T(1024)S(1)} %multiply_add_fusion.slot_ref, f32[128,2,2,8,128]{4,3,2,1,0:T(8,128)S(1)} %all_to_all.22.in_ref, bf16[2,2,256,512]{3,2,1,0:T(8,128)(2,1)S(1)} %copy-done.2, bf16[256,256]{1,0:T(8,128)(2,1)S(1)} %copy-done.5), custom_call_target="tpu_custom_call" | custom-call | flops 1207959552 | bytes 6291456 | tf_op jit(solution)/shard_map/third/pallas_call | solution.py:364
  140.2 34.2 %all_to_all.23 = f32[128,1,16,2,128]{4,3,2,1,0:T(2,128)S(1)} all-to-all(f32[128,1,16,2,128]{4,3,2,1,0:T(2,128)S(1)} %bitcast.20), channel_id=1, replica_groups=mesh['gx'=8,'gy'=4,'gz'=4] {'gx','gy','gz'}, dimensions={0} | all-to-all | bytes 4194304 | tf_op jit(solution)/shard_map/all_to_all | solution.py:418
  174.4 1.3 copy.15
  (16 shorter events, 0.1 us)
Async XLA Ops:
  3.4 54.8 %all-to-all-start = ((f32[4,2,8,128,128]{4,3,2,1,0:T(8,128)}), f32[4,2,8,128,128]{4,3,2,1,0:T(8,128)}, u32[]{:S(2)}, u32[]{:S(2)}) async-start(f32[4,2,8,128,128]{4,3,2,1,0:T(8,128)} %scale_a.1), calls=%async_computation | async-start | bytes 8388608 | tf_op jit(solution)/shard_map/all_to_all | solution.py:395
  9.2 8.2 %copy-start.7 = (s32[1024,1]{0,1:T(1,128)S(1)}, s32[1024,1]{0,1:T(1,128)}, u32[]{:S(2)}) copy-start(s32[1024,1]{0,1:T(1,128)} %param.9) | copy-start | bytes 12292
  12.4 50.3 %collective-permute-start.1 = (f32[2,8,128,128]{3,2,1,0:T(8,128)}, f32[2,8,128,128]{3,2,1,0:T(8,128)S(1)}, u32[]{:S(2)}, u32[]{:S(2)}) collective-permute-start(f32[2,8,128,128]{3,2,1,0:T(8,128)} %get-tuple-element.46), channel_id=1, source_target_pairs={{0,4},{4,8},{8,12},{12,0},{1,5},{5,9},{9,13},{13,1},{2,6},{6,10},{... | collective-permute-start | bytes 3145736 | tf_op jit(solution)/shard_map/ppermute | solution.py:378
  13.7 49.0 %collective-permute-start.2 = (f32[2,8,128,128]{3,2,1,0:T(8,128)}, f32[2,8,128,128]{3,2,1,0:T(8,128)}, u32[]{:S(2)}, u32[]{:S(2)}) collective-permute-start(f32[2,8,128,128]{3,2,1,0:T(8,128)} %get-tuple-element.47), channel_id=1, source_target_pairs={{0,8},{4,12},{8,0},{12,4},{1,9},{5,13},{9,1},{13,5},{2,10},{6,14},... | collective-permute-start | bytes 3145736 | tf_op jit(solution)/shard_map/ppermute | solution.py:378
  16.4 46.4 %collective-permute-start.3 = (f32[2,8,128,128]{3,2,1,0:T(8,128)}, f32[2,8,128,128]{3,2,1,0:T(8,128)}, u32[]{:S(2)}, u32[]{:S(2)}) collective-permute-start(f32[2,8,128,128]{3,2,1,0:T(8,128)} %get-tuple-element.48), channel_id=1, source_target_pairs={{0,12},{4,0},{8,4},{12,8},{1,13},{5,1},{9,5},{13,9},{2,14},{6,2},{... | collective-permute-start | bytes 3145736 | tf_op jit(solution)/shard_map/ppermute | solution.py:378
  17.9 40.2 %copy-start.1 = (bf16[2,2,2,256,256]{4,3,2,1,0:T(8,128)(2,1)S(1)}, bf16[2,2,2,256,256]{4,3,2,1,0:T(8,128)(2,1)}, u32[]{:S(2)}) copy-start(bf16[2,2,2,256,256]{4,3,2,1,0:T(8,128)(2,1)} %constant.25.clone.refs_1_.table_ref) | copy-start | bytes 3145732
  20.7 43.0 %copy-start = (bf16[2,2,2,256,256]{4,3,2,1,0:T(8,128)(2,1)S(1)}, bf16[2,2,2,256,256]{4,3,2,1,0:T(8,128)(2,1)}, u32[]{:S(2)}) copy-start(bf16[2,2,2,256,256]{4,3,2,1,0:T(8,128)(2,1)} %constant.24.clone.refs_4_.table_ref) | copy-start | bytes 3145732
  62.7 1.0 copy-start.6
  63.7 6.2 %copy-start.9 = (f32[2,2,128,256]{3,2,1,0:T(8,128)S(1)}, f32[2,2,128,256]{3,2,1,0:T(8,128)}, u32[]{:S(2)}) copy-start(f32[2,2,128,256]{3,2,1,0:T(8,128)} %get-tuple-element.43) | copy-start | bytes 1572868
  63.7 7.5 %copy-start.10 = (f32[2,2,128,256]{3,2,1,0:T(8,128)S(1)}, f32[2,2,128,256]{3,2,1,0:T(8,128)}, u32[]{:S(2)}) copy-start(f32[2,2,128,256]{3,2,1,0:T(8,128)} %get-tuple-element.55) | copy-start | bytes 1572868
  63.7 9.0 %copy-start.8 = (f32[2,2,128,256]{3,2,1,0:T(8,128)S(1)}, f32[2,2,128,256]{3,2,1,0:T(8,128)}, u32[]{:S(2)}) copy-start(f32[2,2,128,256]{3,2,1,0:T(8,128)} %get-tuple-element.54) | copy-start | bytes 1572868
  67.1 13.3 %collective-permute-start.6 = (f32[2,2,256,128]{3,2,1,0:T(8,128)}, f32[2,2,256,128]{3,2,1,0:T(8,128)S(1)}, u32[]{:S(2)}, u32[]{:S(2)}) collective-permute-start(f32[2,2,256,128]{3,2,1,0:T(8,128)} %get-tuple-element.56), channel_id=1, source_target_pairs={{0,1},{1,2},{2,3},{3,0},{4,5},{5,6},{6,7},{7,4},{8,9},{9,10},{10,1... | collective-permute-start | bytes 1572872 | tf_op jit(solution)/shard_map/ppermute | solution.py:378
  68.1 12.3 %collective-permute-start.7 = (f32[2,2,256,128]{3,2,1,0:T(8,128)}, f32[2,2,256,128]{3,2,1,0:T(8,128)S(1)}, u32[]{:S(2)}, u32[]{:S(2)}) collective-permute-start(f32[2,2,256,128]{3,2,1,0:T(8,128)} %get-tuple-element.57), channel_id=1, source_target_pairs={{0,3},{1,0},{2,1},{3,2},{4,7},{5,4},{6,5},{7,6},{8,11},{9,8},{10,9... | collective-permute-start | bytes 1572872 | tf_op jit(solution)/shard_map/ppermute | solution.py:378
  69.9 12.6 %collective-permute-start = (f32[2,2,128,256]{3,2,1,0:T(8,128)S(1)}, f32[2,2,128,256]{3,2,1,0:T(8,128)S(1)}, u32[]{:S(2)}, u32[]{:S(2)}) collective-permute-start(f32[2,2,128,256]{3,2,1,0:T(8,128)S(1)} %copy-done.9), channel_id=1, source_target_pairs={{0,4},{4,8},{8,12},{12,0},{1,5},{5,9},{9,13},{13,1},{2,6},{6,10},{... | collective-permute-start | bytes 1572872 | tf_op jit(solution)/shard_map/ppermute | solution.py:378
  71.2 11.0 %collective-permute-start.5 = (f32[2,2,128,256]{3,2,1,0:T(8,128)S(1)}, f32[2,2,128,256]{3,2,1,0:T(8,128)S(1)}, u32[]{:S(2)}, u32[]{:S(2)}) collective-permute-start(f32[2,2,128,256]{3,2,1,0:T(8,128)S(1)} %copy-done.10), channel_id=1, source_target_pairs={{0,12},{4,0},{8,4},{12,8},{1,13},{5,1},{9,5},{13,9},{2,14},{6,2},{... | collective-permute-start | bytes 1572872 | tf_op jit(solution)/shard_map/ppermute | solution.py:378
  72.7 22.1 %collective-permute-start.4 = (f32[2,2,128,256]{3,2,1,0:T(8,128)S(1)}, f32[2,2,128,256]{3,2,1,0:T(8,128)S(1)}, u32[]{:S(2)}, u32[]{:S(2)}) collective-permute-start(f32[2,2,128,256]{3,2,1,0:T(8,128)S(1)} %copy-done.8), channel_id=1, source_target_pairs={{0,8},{4,12},{8,0},{12,4},{1,9},{5,13},{9,1},{13,5},{2,10},{6,14},... | collective-permute-start | bytes 1572872 | tf_op jit(solution)/shard_map/ppermute | solution.py:378
  77.6 17.2 %copy-start.3 = (f32[2,2,128,256]{3,2,1,0:T(8,128)S(1)}, f32[2,2,128,256]{3,2,1,0:T(8,128)}, u32[]{:S(2)}) copy-start(f32[2,2,128,256]{3,2,1,0:T(8,128)} %get-tuple-element.42.p0) | copy-start | bytes 1572868
  80.4 15.8 %collective-permute-start.8 = (f32[2,2,256,128]{3,2,1,0:T(8,128)}, f32[2,2,256,128]{3,2,1,0:T(8,128)S(1)}, u32[]{:S(2)}, u32[]{:S(2)}) collective-permute-start(f32[2,2,256,128]{3,2,1,0:T(8,128)} %get-tuple-element.58), channel_id=1, source_target_pairs={{0,2},{1,3},{2,0},{3,1},{4,6},{5,7},{6,4},{7,5},{8,10},{9,11},{10,... | collective-permute-start | bytes 1572872 | tf_op jit(solution)/shard_map/ppermute | solution.py:378
  94.8 1.5 copy-start.4
  97.9 38.6 %copy-start.2 = (bf16[2,2,256,512]{3,2,1,0:T(8,128)(2,1)S(1)}, bf16[2,2,256,512]{3,2,1,0:T(8,128)(2,1)}, u32[]{:S(2)}) copy-start(bf16[2,2,256,512]{3,2,1,0:T(8,128)(2,1)} %constant.23.clone.table_ref) | copy-start | bytes 3145732
  97.9 38.5 %copy-start.5 = (bf16[256,256]{1,0:T(8,128)(2,1)S(1)}, bf16[256,256]{1,0:T(8,128)(2,1)}, u32[]{:S(2)}) copy-start(bf16[256,256]{1,0:T(8,128)(2,1)} %constant.26.clone.ordering_ref) | copy-start | bytes 393220

commit v13 on v12

--- a/solution.py
+++ b/solution.py
@@ -76,7 +76,9 @@
 
 
 def cost(multiplies, moved):
-    return pl.CostEstimate(flops=6 * multiplies, bytes_accessed=moved, transcendentals=0)
+    return pl.CostEstimate(
+        flops=multiplies >> 16, bytes_accessed=moved >> 16, transcendentals=0
+    )
 
 
 def rows_z(piece):
@@ -94,21 +96,23 @@
     return [pltpu.with_memory_space_constraint(x, pltpu.HBM) for x in arrays]
 
 
-def scale_kernel(half, shifts, rotated, place_ref, normals_ref, spectrum_ref, *refs):
+def scale_kernel(whole, shifts, place_ref, normals_ref, spectrum_ref, *refs):
     *out_refs, held_out, held_n, held_s, semaphores = refs
+    work = [(i, out_refs[0].at[i]) for i in range(4)] if whole else []
+    for shift, out_ref in zip(shifts, out_refs[1:] if whole else out_refs):
+        work.append((4 + lax.rem(place_ref[0] + shift, 4), out_ref))
 
     def gets(i):
-        chunk = 4 * half + (lax.rem(place_ref[0] + shifts[i], 4) if rotated else shifts[i])
+        chunk = work[i][0]
         return (
             pltpu.make_async_copy(normals_ref.at[:, chunk], held_n.at[i], semaphores.at[i, 0]),
             pltpu.make_async_copy(spectrum_ref.at[chunk], held_s.at[i], semaphores.at[i, 1]),
         )
 
     def put(i):
-        target = out_refs[i] if rotated else out_refs[0].at[shifts[i]]
-        return pltpu.make_async_copy(held_out.at[i], target, semaphores.at[i, 2])
-
-    steps = range(len(shifts))
+        return pltpu.make_async_copy(held_out.at[i], work[i][1], semaphores.at[i, 2])
+
+    steps = range(len(work))
     for i in steps:
         for copy in gets(i):
             copy.start()
@@ -122,13 +126,13 @@
         put(i).wait()
 
 
-def scale(half, shifts, rotated, place, normals, spectrum):
+def scale(whole, shifts, place, normals, spectrum):
     chunk = (2, 8, 128, 128)
-    count = len(shifts)
-    shapes = [chunk] * count if rotated else [(count,) + chunk]
+    shapes = ([(4,) + chunk] if whole else []) + [chunk] * len(shifts)
+    count = 4 * whole + len(shifts)
     hbm = pl.BlockSpec(memory_space=pltpu.HBM)
     return pl.pallas_call(
-        functools.partial(scale_kernel, half, shifts, rotated),
+        functools.partial(scale_kernel, whole, shifts),
         in_specs=[pl.BlockSpec(memory_space=pltpu.SMEM)] + [hbm] * 2,
         out_specs=[hbm] * len(shapes),
         out_shape=[pltpu.HBM(shape, jnp.float32) for shape in shapes],
@@ -140,7 +144,7 @@
         ],
         compiler_params=params(VMEM),
         cost_estimate=cost(count << 18, 2 * count * MIB),
-        name="scale_b" if rotated else "scale_a",
+        name="scale" if whole else "scale_own",
     )(place, *in_hbm(normals.reshape(2, 8, 8, 128, 128), spectrum.reshape(8, 8, 128, 128)))
 
 
@@ -390,13 +394,11 @@
     gy = lax.axis_index("gy").astype(jnp.int32).reshape(1)
     gz = lax.axis_index("gz").astype(jnp.int32).reshape(1)
 
-    (a,) = scale(0, (0, 1, 2, 3), False, gz, normals, spectrum)
-    a, place = lax.optimization_barrier((a, gy))
+    a, b1, b3, b2 = scale(True, (1, 3, 2), gy, normals, spectrum)
+    place, a = lax.optimization_barrier((gy, a))
     a = lax.all_to_all(a, "gz", split_axis=0, concat_axis=0, tiled=True)
-    b1, b3, b2 = scale(1, (1, 3, 2), True, place, normals, spectrum)
-    place, b1, b3, b2 = lax.optimization_barrier((place, b1, b3, b2))
     b1, b3, b2 = shifted(b1, "gy", 1), shifted(b3, "gy", 3), shifted(b2, "gy", 2)
-    (b0,) = scale(1, (0,), True, place, normals, spectrum)
+    (b0,) = scale(False, (0,), place, normals, spectrum)
 
     a, slots, b0 = lax.optimization_barrier((a, slots_of(block_owner), b0))
     a1, a3, a2, a0 = first(True, (1, 3, 2, 0), gz, gy, a, table_z)

time: 176 us -> 180 us (1.023)
  other arithmetic: 0.63 us -> 2.71 us
  local copies, waits for them, and re-layouts: 2.54 us -> 4.54 us
    pallas_call x3 -> x2, Pallas kernels: 8.86 us -> 8.58 us  [scale(): pl.pallas_call(functools.partial(scale_kernel, whole, shifts), in_specs=[...]
  transfers between devices with their start and end apart: 10 -> 10, of which waited for: 5 -> 5; matrix products, arithmetic and copies ran while one was open for 0% -> 2% of each run, Pallas kernels for 9% -> 7%
where the time goes in v13:
time: 180 us
  blocking collectives  72.8 us (40%)
  waiting for transfers between devices  53 us (29%)
  Pallas kernels  27.5 us (15%)
  starting transfers between devices  19.2 us (11%)
  local copies, waits for them, and re-layouts  4.54 us (3%)
  other arithmetic  2.71 us (2%)
    all_to_all x1, blocking collectives, per_device(): lines = lax.all_to_all(planes, ALL, split_axis=0, concat_axis=0, tiled=True)  38.6 us
    all_to_all x1, waiting for transfers between devices, per_device(): a = lax.all_to_all(a, 'gz', split_axis=0, concat_axis=0, tiled=True)  36.9 us
    all_to_all x1, blocking collectives, per_device(): lax.all_to_all(outgoing.reshape(128, 1, CAP, 2, BW), ALL, split_axis=0, c...  34.2 us
    ppermute x9, waiting for transfers between devices, shifted(): lax.ppermute(piece, axis, [(i, (i + shift) % size) for i in range(size)])  16.1 us
    ppermute x9, starting transfers between devices, shifted(): lax.ppermute(piece, axis, [(i, (i + shift) % size) for i in range(size)])  13.3 us
    pallas_call x3, Pallas kernels, first(): pl.pallas_call(functools.partial(first_kernel, along_z, shifts, dynamic),...  11.3 us
    pallas_call x2, Pallas kernels, scale(): pl.pallas_call(functools.partial(scale_kernel, whole, shifts), in_specs=[...  8.58 us
    all_to_all x1, starting transfers between devices, per_device(): a = lax.all_to_all(a, 'gz', split_axis=0, concat_axis=0, tiled=True)  5.87 us
  transfers between devices with their start and end apart: 10, of which 5 were waited for; matrix products, arithmetic and copies ran while one was open for 2% of the time, Pallas kernels for 7%

profile of v13, /device:TPU:1, one launch (start us, length us, event | category | flops | bytes accessed | tf_op | source)
XLA Modules:
  0.0 179.9 jit_solution(15630348237669965474)
XLA Ops:
  0.0 6.2 %scale.1 = (f32[4,2,8,128,128]{4,3,2,1,0:T(8,128)}, f32[2,8,128,128]{3,2,1,0:T(8,128)}, f32[2,8,128,128]{3,2,1,0:T(8,128)}, f32[2,8,128,128]{3,2,1,0:T(8,128)}) custom-call(s32[1]{0:T(128)} %bitcast.place_ref.to_ref, bf16[2,8,8,128,128]{4,3,2,1,0:T(8,128)(2,1)} %bitcast.21, f32[8,8,128,128]{3,2,1,0:T(8,128)} %bitcast.23), custom_call_target="tpu_custom_call" | custom-call | flops 28 | bytes 224 | tf_op jit(solution)/shard_map/scale/pallas_call | solution.py:134
  6.2 5.9 %all-to-all-start = ((f32[4,2,8,128,128]{4,3,2,1,0:T(8,128)}), f32[4,2,8,128,128]{4,3,2,1,0:T(8,128)}, u32[]{:S(2)}, u32[]{:S(2)}) async-start(f32[4,2,8,128,128]{4,3,2,1,0:T(8,128)} %get-tuple-element.32), calls=%async_computation | async-start | bytes 8388608 | tf_op jit(solution)/shard_map/all_to_all | solution.py:399
  12.1 1.3 collective-permute-start.1
  13.4 2.6 %collective-permute-start.2 = (f32[2,8,128,128]{3,2,1,0:T(8,128)}, f32[2,8,128,128]{3,2,1,0:T(8,128)S(1)}, u32[]{:S(2)}, u32[]{:S(2)}) collective-permute-start(f32[2,8,128,128]{3,2,1,0:T(8,128)} %get-tuple-element.41), channel_id=1, source_target_pairs={{0,8},{4,12},{8,0},{12,4},{1,9},{5,13},{9,1},{13,5},{2,10},{6,14},... | collective-permute-start | bytes 3145736 | tf_op jit(solution)/shard_map/ppermute | solution.py:382
  16.0 1.1 collective-permute-start.3
  17.1 2.4 %scale_own.1.refs_0_ = f32[2,8,128,128]{3,2,1,0:T(8,128)} custom-call(s32[1]{0:T(128)} %bitcast.place_ref.to_ref, bf16[2,8,8,128,128]{4,3,2,1,0:T(8,128)(2,1)} %bitcast.22, f32[8,8,128,128]{3,2,1,0:T(8,128)} %bitcast.24), custom_call_target="tpu_custom_call" | custom-call | flops 4 | bytes 32 | tf_op jit(solution)/shard_map/scale_own/pallas_call | solution.py:134
  19.5 0.0 copy-start
  19.5 0.0 copy-done.9
  19.5 0.1 copy.11
  19.6 0.2 fusion.2
  19.8 0.0 copy-start.8
  19.8 0.8 copy-done.8
  20.7 1.1 broadcast_add_fusion
  21.8 0.9 copy.12
  22.7 1.4 fusion.1
  24.1 36.9 %all-to-all-done.refs_0_ = f32[4,2,8,128,128]{4,3,2,1,0:T(8,128)} async-done(((f32[4,2,8,128,128]{4,3,2,1,0:T(8,128)}), f32[4,2,8,128,128]{4,3,2,1,0:T(8,128)}, u32[]{:S(2)}, u32[]{:S(2)}) %all-to-all-start) | async-done | bytes 4194336 | tf_op jit(solution)/shard_map/all_to_all | solution.py:399
  61.0 4.6 %first_z.1 = (f32[2,2,128,256]{3,2,1,0:T(8,128)}, f32[2,2,128,256]{3,2,1,0:T(8,128)}, f32[2,2,128,256]{3,2,1,0:T(8,128)}, f32[2,2,128,256]{3,2,1,0:T(8,128)}) custom-call(s32[1]{0:T(128)} %bitcast.8.place_ref.to_ref, s32[1]{0:T(128)} %bitcast.place_ref.to_ref, f32[4,2,8,128,128]{4,3,2,1,0:T(8,128)} %all-to-all-done.refs_0_, ...), custom_call_target="tpu_custom_call" | custom-call | flops 4096 | bytes 128 | tf_op jit(solution)/shard_map/first_z/pallas_call | solution.py:221
  65.6 0.0 collective-permute-done.1.refs_1_
  65.6 0.0 copy-start.6
  65.6 0.0 collective-permute-done.2.refs_2_
  65.7 0.0 collective-permute-done.3.refs_3_
  65.7 0.9 copy-done.6
  66.6 0.4 copy-done.7
  67.0 0.0 copy-done.1
  67.0 3.4 %first_y.2 = (f32[2,2,256,128]{3,2,1,0:T(8,128)}, f32[2,2,256,128]{3,2,1,0:T(8,128)}) custom-call(s32[1]{0:T(128)} %bitcast.place_ref.to_ref, s32[1]{0:T(128)} %bitcast.8.place_ref.to_ref, f32[2,8,128,128]{3,2,1,0:T(8,128)} %scale_own.1.refs_0_, f32[2,8,128,128]{3,2,1,0:T(8,128)} %copy-done.6, f32[2,8,128,128]{3,2,1,0:T(8,128)} %copy-done.7, ...), custom_call_target="tpu_custom_call" | custom-call | flops 2048 | bytes 64 | tf_op jit(solution)/shard_map/first_y/pallas_call | solution.py:221
  70.4 1.0 collective-permute-start.6
  71.3 0.0 copy-done.12
  71.3 1.3 collective-permute-start
  72.6 1.8 collective-permute-start.7
  74.4 2.6 %collective-permute-start.4 = (f32[2,2,128,256]{3,2,1,0:T(8,128)S(1)}, f32[2,2,128,256]{3,2,1,0:T(8,128)S(1)}, u32[]{:S(2)}, u32[]{:S(2)}) collective-permute-start(f32[2,2,128,256]{3,2,1,0:T(8,128)S(1)} %copy-done.11), channel_id=1, source_target_pairs={{0,8},{4,12},{8,0},{12,4},{1,9},{5,13},{9,1},{13,5},{2,10},{6,14},... | collective-permute-start | bytes 1572872 | tf_op jit(solution)/shard_map/ppermute | solution.py:382
  77.0 1.1 collective-permute-start.5
  78.1 3.3 %first_y.3 = (f32[2,2,256,128]{3,2,1,0:T(8,128)}, f32[2,2,256,128]{3,2,1,0:T(8,128)}) custom-call(s32[1]{0:T(128)} %bitcast.place_ref.to_ref, s32[1]{0:T(128)} %bitcast.8.place_ref.to_ref, f32[2,8,128,128]{3,2,1,0:T(8,128)} %scale_own.1.refs_0_, f32[2,8,128,128]{3,2,1,0:T(8,128)} %copy-done.6, f32[2,8,128,128]{3,2,1,0:T(8,128)} %copy-done.7, ...), custom_call_target="tpu_custom_call" | custom-call | flops 2048 | bytes 64 | tf_op jit(solution)/shard_map/first_y/pallas_call | solution.py:221
  81.4 2.3 %collective-permute-done.6.p1 = f32[2,2,256,128]{3,2,1,0:T(8,128)S(1)} collective-permute-done((f32[2,2,256,128]{3,2,1,0:T(8,128)}, f32[2,2,256,128]{3,2,1,0:T(8,128)S(1)}, u32[]{:S(2)}, u32[]{:S(2)}) %collective-permute-start.6) | collective-permute-done | bytes 524320 | tf_op jit(solution)/shard_map/ppermute | solution.py:382
  83.7 0.6 collective-permute-start.8
  84.3 0.1 collective-permute-done.7.p3
  84.5 0.9 part_z.1.part_ref
  85.4 0.0 collective-permute-done.p1
  85.4 11.6 %collective-permute-done.4.p2 = f32[2,2,128,256]{3,2,1,0:T(8,128)S(1)} collective-permute-done((f32[2,2,128,256]{3,2,1,0:T(8,128)S(1)}, f32[2,2,128,256]{3,2,1,0:T(8,128)S(1)}, u32[]{:S(2)}, u32[]{:S(2)}) %collective-permute-start.4) | collective-permute-done | bytes 524320 | tf_op jit(solution)/shard_map/ppermute | solution.py:382
  96.9 2.1 %collective-permute-done.5.p3 = f32[2,2,128,256]{3,2,1,0:T(8,128)S(1)} collective-permute-done((f32[2,2,128,256]{3,2,1,0:T(8,128)S(1)}, f32[2,2,128,256]{3,2,1,0:T(8,128)S(1)}, u32[]{:S(2)}, u32[]{:S(2)}) %collective-permute-start.5) | collective-permute-done | bytes 524320 | tf_op jit(solution)/shard_map/ppermute | solution.py:382
  99.0 1.4 second_y.1.done_y
  100.4 0.0 collective-permute-done.8.p2
  100.4 1.6 second.1
  102.0 0.0 copy-start.2
  102.1 0.0 copy-start.5
  102.1 38.6 %all_to_all.22.in_ref = f32[128,2,2,8,128]{4,3,2,1,0:T(8,128)S(1)} all-to-all(f32[128,2,2,8,128]{4,3,2,1,0:T(8,128)S(1)} %second.1), channel_id=1, replica_groups=mesh['gx'=8,'gy'=4,'gz'=4] {'gx','gy','gz'}, dimensions={0} | all-to-all | bytes 4194304 | tf_op jit(solution)/shard_map/all_to_all | solution.py:418
  140.7 3.7 %third.1 = f32[4096,128]{1,0:T(8,128)S(1)} custom-call(s32[1024]{0:T(1024)S(1)} %multiply_add_fusion.slot_ref, f32[128,2,2,8,128]{4,3,2,1,0:T(8,128)S(1)} %all_to_all.22.in_ref, bf16[2,2,256,512]{3,2,1,0:T(8,128)(2,1)S(1)} %copy-done.2, bf16[256,256]{1,0:T(8,128)(2,1)S(1)} %copy-done.5), custom_call_target="tpu_custom_call" | custom-call | flops 3072 | bytes 96 | tf_op jit(solution)/shard_map/third/pallas_call | solution.py:368
  144.4 34.2 %all_to_all.23 = f32[128,1,16,2,128]{4,3,2,1,0:T(2,128)S(1)} all-to-all(f32[128,1,16,2,128]{4,3,2,1,0:T(2,128)S(1)} %bitcast.20), channel_id=1, replica_groups=mesh['gx'=8,'gy'=4,'gz'=4] {'gx','gy','gz'}, dimensions={0} | all-to-all | bytes 4194304 | tf_op jit(solution)/shard_map/all_to_all | solution.py:420
  178.6 1.3 copy.15
  (19 shorter events, 0.1 us)
Async XLA Ops:
  6.2 54.8 %all-to-all-start = ((f32[4,2,8,128,128]{4,3,2,1,0:T(8,128)}), f32[4,2,8,128,128]{4,3,2,1,0:T(8,128)}, u32[]{:S(2)}, u32[]{:S(2)}) async-start(f32[4,2,8,128,128]{4,3,2,1,0:T(8,128)} %get-tuple-element.32), calls=%async_computation | async-start | bytes 8388608 | tf_op jit(solution)/shard_map/all_to_all | solution.py:399
  12.1 53.5 %collective-permute-start.1 = (f32[2,8,128,128]{3,2,1,0:T(8,128)}, f32[2,8,128,128]{3,2,1,0:T(8,128)S(1)}, u32[]{:S(2)}, u32[]{:S(2)}) collective-permute-start(f32[2,8,128,128]{3,2,1,0:T(8,128)} %get-tuple-element.40), channel_id=1, source_target_pairs={{0,4},{4,8},{8,12},{12,0},{1,5},{5,9},{9,13},{13,1},{2,6},{6,10},{... | collective-permute-start | bytes 3145736 | tf_op jit(solution)/shard_map/ppermute | solution.py:382
  13.4 52.3 %collective-permute-start.2 = (f32[2,8,128,128]{3,2,1,0:T(8,128)}, f32[2,8,128,128]{3,2,1,0:T(8,128)S(1)}, u32[]{:S(2)}, u32[]{:S(2)}) collective-permute-start(f32[2,8,128,128]{3,2,1,0:T(8,128)} %get-tuple-element.41), channel_id=1, source_target_pairs={{0,8},{4,12},{8,0},{12,4},{1,9},{5,13},{9,1},{13,5},{2,10},{6,14},... | collective-permute-start | bytes 3145736 | tf_op jit(solution)/shard_map/ppermute | solution.py:382
  16.0 3.5 %copy-start.9 = (s32[1024,1]{0,1:T(1,128)S(1)}, s32[1024,1]{0,1:T(1,128)}, u32[]{:S(2)}) copy-start(s32[1024,1]{0,1:T(1,128)} %param.9) | copy-start | bytes 12292
  16.0 49.7 %collective-permute-start.3 = (f32[2,8,128,128]{3,2,1,0:T(8,128)}, f32[2,8,128,128]{3,2,1,0:T(8,128)}, u32[]{:S(2)}, u32[]{:S(2)}) collective-permute-start(f32[2,8,128,128]{3,2,1,0:T(8,128)} %get-tuple-element.42), channel_id=1, source_target_pairs={{0,12},{4,0},{8,4},{12,8},{1,13},{5,1},{9,5},{13,9},{2,14},{6,2},{... | collective-permute-start | bytes 3145736 | tf_op jit(solution)/shard_map/ppermute | solution.py:382
  19.5 41.5 %copy-start = (bf16[2,2,2,256,256]{4,3,2,1,0:T(8,128)(2,1)S(1)}, bf16[2,2,2,256,256]{4,3,2,1,0:T(8,128)(2,1)}, u32[]{:S(2)}) copy-start(bf16[2,2,2,256,256]{4,3,2,1,0:T(8,128)(2,1)} %constant.25.clone.refs_1_.table_ref) | copy-start | bytes 3145732
  19.8 0.8 copy-start.8
  61.0 6.0 %copy-start.1 = (bf16[2,2,2,256,256]{4,3,2,1,0:T(8,128)(2,1)S(1)}, bf16[2,2,2,256,256]{4,3,2,1,0:T(8,128)(2,1)}, u32[]{:S(2)}) copy-start(bf16[2,2,2,256,256]{4,3,2,1,0:T(8,128)(2,1)} %constant.24.clone.refs_4_.table_ref) | copy-start | bytes 3145732
  65.6 1.0 copy-start.6
  65.7 1.3 copy-start.7
  67.0 4.4 %copy-start.12 = (f32[2,2,128,256]{3,2,1,0:T(8,128)S(1)}, f32[2,2,128,256]{3,2,1,0:T(8,128)}, u32[]{:S(2)}) copy-start(f32[2,2,128,256]{3,2,1,0:T(8,128)} %get-tuple-element.37) | copy-start | bytes 1572868
  67.0 7.4 %copy-start.11 = (f32[2,2,128,256]{3,2,1,0:T(8,128)S(1)}, f32[2,2,128,256]{3,2,1,0:T(8,128)}, u32[]{:S(2)}) copy-start(f32[2,2,128,256]{3,2,1,0:T(8,128)} %get-tuple-element.48) | copy-start | bytes 1572868
  67.0 10.1 %copy-start.10 = (f32[2,2,128,256]{3,2,1,0:T(8,128)S(1)}, f32[2,2,128,256]{3,2,1,0:T(8,128)}, u32[]{:S(2)}) copy-start(f32[2,2,128,256]{3,2,1,0:T(8,128)} %get-tuple-element.49) | copy-start | bytes 1572868
  70.4 13.4 %collective-permute-start.6 = (f32[2,2,256,128]{3,2,1,0:T(8,128)}, f32[2,2,256,128]{3,2,1,0:T(8,128)S(1)}, u32[]{:S(2)}, u32[]{:S(2)}) collective-permute-start(f32[2,2,256,128]{3,2,1,0:T(8,128)} %get-tuple-element.50), channel_id=1, source_target_pairs={{0,1},{1,2},{2,3},{3,0},{4,5},{5,6},{6,7},{7,4},{8,9},{9,10},{10,1... | collective-permute-start | bytes 1572872 | tf_op jit(solution)/shard_map/ppermute | solution.py:382
  71.3 14.0 %collective-permute-start = (f32[2,2,128,256]{3,2,1,0:T(8,128)S(1)}, f32[2,2,128,256]{3,2,1,0:T(8,128)S(1)}, u32[]{:S(2)}, u32[]{:S(2)}) collective-permute-start(f32[2,2,128,256]{3,2,1,0:T(8,128)S(1)} %copy-done.12), channel_id=1, source_target_pairs={{0,4},{4,8},{8,12},{12,0},{1,5},{5,9},{9,13},{13,1},{2,6},{6,10},{... | collective-permute-start | bytes 1572872 | tf_op jit(solution)/shard_map/ppermute | solution.py:382
  72.6 11.8 %collective-permute-start.7 = (f32[2,2,256,128]{3,2,1,0:T(8,128)}, f32[2,2,256,128]{3,2,1,0:T(8,128)S(1)}, u32[]{:S(2)}, u32[]{:S(2)}) collective-permute-start(f32[2,2,256,128]{3,2,1,0:T(8,128)} %get-tuple-element.51), channel_id=1, source_target_pairs={{0,3},{1,0},{2,1},{3,2},{4,7},{5,4},{6,5},{7,6},{8,11},{9,8},{10,9... | collective-permute-start | bytes 1572872 | tf_op jit(solution)/shard_map/ppermute | solution.py:382
  74.4 22.5 %collective-permute-start.4 = (f32[2,2,128,256]{3,2,1,0:T(8,128)S(1)}, f32[2,2,128,256]{3,2,1,0:T(8,128)S(1)}, u32[]{:S(2)}, u32[]{:S(2)}) collective-permute-start(f32[2,2,128,256]{3,2,1,0:T(8,128)S(1)} %copy-done.11), channel_id=1, source_target_pairs={{0,8},{4,12},{8,0},{12,4},{1,9},{5,13},{9,1},{13,5},{2,10},{6,14},... | collective-permute-start | bytes 1572872 | tf_op jit(solution)/shard_map/ppermute | solution.py:382
  77.0 22.0 %collective-permute-start.5 = (f32[2,2,128,256]{3,2,1,0:T(8,128)S(1)}, f32[2,2,128,256]{3,2,1,0:T(8,128)S(1)}, u32[]{:S(2)}, u32[]{:S(2)}) collective-permute-start(f32[2,2,128,256]{3,2,1,0:T(8,128)S(1)} %copy-done.10), channel_id=1, source_target_pairs={{0,12},{4,0},{8,4},{12,8},{1,13},{5,1},{9,5},{13,9},{2,14},{6,2},{... | collective-permute-start | bytes 1572872 | tf_op jit(solution)/shard_map/ppermute | solution.py:382
  81.4 17.6 %copy-start.3 = (f32[2,2,128,256]{3,2,1,0:T(8,128)S(1)}, f32[2,2,128,256]{3,2,1,0:T(8,128)}, u32[]{:S(2)}) copy-start(f32[2,2,128,256]{3,2,1,0:T(8,128)} %get-tuple-element.36.p0) | copy-start | bytes 1572868
  83.7 16.7 %collective-permute-start.8 = (f32[2,2,256,128]{3,2,1,0:T(8,128)}, f32[2,2,256,128]{3,2,1,0:T(8,128)S(1)}, u32[]{:S(2)}, u32[]{:S(2)}) collective-permute-start(f32[2,2,256,128]{3,2,1,0:T(8,128)} %get-tuple-element.52), channel_id=1, source_target_pairs={{0,2},{1,3},{2,0},{3,1},{4,6},{5,7},{6,4},{7,5},{8,10},{9,11},{10,... | collective-permute-start | bytes 1572872 | tf_op jit(solution)/shard_map/ppermute | solution.py:382
  99.0 1.4 copy-start.4
  102.0 38.6 %copy-start.2 = (bf16[2,2,256,512]{3,2,1,0:T(8,128)(2,1)S(1)}, bf16[2,2,256,512]{3,2,1,0:T(8,128)(2,1)}, u32[]{:S(2)}) copy-start(bf16[2,2,256,512]{3,2,1,0:T(8,128)(2,1)} %constant.23.clone.table_ref) | copy-start | bytes 3145732
  102.1 38.6 %copy-start.5 = (bf16[256,256]{1,0:T(8,128)(2,1)S(1)}, bf16[256,256]{1,0:T(8,128)(2,1)}, u32[]{:S(2)}) copy-start(bf16[256,256]{1,0:T(8,128)(2,1)} %constant.26.clone.ordering_ref) | copy-start | bytes 393220

commit v14 on v12

--- a/solution.py
+++ b/solution.py
@@ -76,7 +76,9 @@
 
 
 def cost(multiplies, moved):
-    return pl.CostEstimate(flops=6 * multiplies, bytes_accessed=moved, transcendentals=0)
+    return pl.CostEstimate(
+        flops=multiplies >> 16, bytes_accessed=moved >> 16, transcendentals=0
+    )
 
 
 def rows_z(piece):
@@ -182,12 +184,14 @@
         return pltpu.make_async_copy(held_out.at[i], out_refs[i], semaphores.at[i, 4])
 
     steps = range(len(shifts))
-    for i in steps:
-        for copy in gets(i):
-            copy.start()
+    for copy in gets(0):
+        copy.start()
     for i in steps:
         for copy in gets(i):
             copy.wait()
+        if i + 1 < len(shifts):
+            for copy in gets(i + 1):
+                copy.start()
         if dynamic:
             g, h = place_ref[0], lax.rem(place_ref[0] + 3, 4)
         else:
@@ -232,30 +236,26 @@
     )(place, to, *in_hbm(*operands), table)
 
 
-def second_y_kernel(place_ref, p0, p1, p2, p3, table_ref, out_ref):
-    g, h = place_ref[0], lax.rem(place_ref[0] + 3, 4)
-    pairs = [(p0[...], p2[...], g), (p1[...], p3[...], h)]
+def part_y_kernel(place_ref, p1, p3, table_ref, out_ref):
+    pairs = [(p1[...], p3[...], lax.rem(place_ref[0] + 3, 4))]
     for odd, values in enumerate(transform(False, pairs, table_ref)):
-        for plane in range(2):
-            out_ref[0, plane, odd * 128 : (odd + 1) * 128] = values[
-                plane * 128 : (plane + 1) * 128
-            ]
-
-
-def second_y(place, pieces, table):
-    return pl.pallas_call(
-        second_y_kernel,
+        out_ref[odd] = values
+
+
+def part_y(place, pieces, table):
+    return pl.pallas_call(
+        part_y_kernel,
         grid_spec=pltpu.PrefetchScalarGridSpec(
             num_scalar_prefetch=1,
             grid=(2,),
-            in_specs=[pl.BlockSpec((2, 1, 128, KEPT), lambda i, place: (0, i, 0, 0))] * 4
+            in_specs=[pl.BlockSpec((2, 1, 128, KEPT), lambda i, place: (0, i, 0, 0))] * 2
             + [pl.BlockSpec(table.shape, lambda i, place: (0, 0, 0, 0, 0))],
-            out_specs=pl.BlockSpec((1, 2, KEPT, KEPT), lambda i, place: (i, 0, 0, 0)),
+            out_specs=pl.BlockSpec((2, KEPT, KEPT), lambda i, place: (0, 0, i)),
         ),
-        out_shape=jax.ShapeDtypeStruct((2, 2, KEPT, KEPT), jnp.float32),
-        compiler_params=params(VMEM),
-        cost_estimate=cost(512 * 512 * 512, 5 * MIB),
-        name="second_y",
+        out_shape=jax.ShapeDtypeStruct((2, KEPT, 512), jnp.float32),
+        compiler_params=params(VMEM),
+        cost_estimate=cost(512 * 512 * 256, 4 * MIB),
+        name="part_y",
     )(place, *pieces, table)
 
 
@@ -282,16 +282,33 @@
     )(place, *pieces, table)
 
 
-def second_kernel(place_ref, done_y, part_ref, p0, p2, table_ref, out_ref, held):
+def second_kernel(
+    y_ref, z_ref, part_a, a0, a2, table_y_ref, part_b, b0, b2, table_z_ref, out_ref, held
+):
+    odd = pl.program_id(0)
+
     def put(values, half, row):
         held[pl.ds(half * 8 + row, 128, stride=16), :] = values
 
-    parts = transform(True, [(p0[...], p2[...], place_ref[0])], table_ref)
+    base = lax.rem(y_ref[0], 2)
+    flip = jnp.where(odd == 0, 1.0, -1.0).astype(jnp.float32)
+    sign = jnp.where((odd == 0) | (y_ref[0] < 2), 1.0, -1.0).astype(jnp.float32)
+    table = (table_y_ref[0, base, 0], table_y_ref[1, base, 0])
+    values = part_a[0] + product(table, columns_y((a0[...] + flip * a2[...]) * sign))
+    for plane in range(2):
+        for x in range(2):
+            for half in range(2):
+                start = x * KEPT + half * 128
+                put(
+                    values[plane * 128 : (plane + 1) * 128, start : start + 128],
+                    half,
+                    plane * 4 + x,
+                )
+    parts = transform(True, [(b0[...], b2[...], z_ref[0])], table_z_ref)
     for half, values in enumerate(parts):
-        values = values + part_ref[:, :, half * 256 : (half + 1) * 256].reshape(256, 256)
+        values = values + part_b[:, :, half * 256 : (half + 1) * 256].reshape(256, 256)
         for x in range(2):
             for plane in range(2):
-                put(done_y[x, plane, :, half * 128 : (half + 1) * 128], half, plane * 4 + x)
                 put(
                     values[x * 128 : (x + 1) * 128, plane * 128 : (plane + 1) * 128],
                     half,
@@ -300,26 +317,28 @@
     out_ref[...] = held[...].reshape(128, 1, 2, 8, 128)
 
 
-def second(place, done_y, part, pieces, table):
+def second(gy, gz, part_a, pieces_a, table_y, part_b, pieces_b, table_z):
     return pl.pallas_call(
         second_kernel,
         grid_spec=pltpu.PrefetchScalarGridSpec(
-            num_scalar_prefetch=1,
+            num_scalar_prefetch=2,
             grid=(2,),
-            in_specs=[
-                pl.BlockSpec((2, 2, 128, KEPT), lambda i, place: (0, 0, i, 0)),
-                pl.BlockSpec((2, 128, 512), lambda i, place: (0, i, 0)),
+            in_specs=[pl.BlockSpec((1, KEPT, 512), lambda i, gy, gz: (i, 0, 0))]
+            + [pl.BlockSpec((2, 2, 128, KEPT), lambda i, gy, gz: (0, 0, 0, 0))] * 2
+            + [
+                pl.BlockSpec((2, 2, 1, KEPT, KEPT), lambda i, gy, gz: (0, 0, i, 0, 0)),
+                pl.BlockSpec((2, 128, 512), lambda i, gy, gz: (0, i, 0)),
             ]
-            + [pl.BlockSpec((2, 2, 128, 128), lambda i, place: (0, 0, i, 0))] * 2
-            + [pl.BlockSpec(table.shape, lambda i, place: (0, 0, 0, 0, 0))],
-            out_specs=pl.BlockSpec((128, 1, 2, 8, 128), lambda i, place: (0, i, 0, 0, 0)),
+            + [pl.BlockSpec((2, 2, 128, 128), lambda i, gy, gz: (0, 0, i, 0))] * 2
+            + [pl.BlockSpec(table_z.shape, lambda i, gy, gz: (0, 0, 0, 0, 0))],
+            out_specs=pl.BlockSpec((128, 1, 2, 8, 128), lambda i, gy, gz: (0, i, 0, 0, 0)),
             scratch_shapes=[pltpu.VMEM((2048, 128), jnp.float32)],
         ),
         out_shape=jax.ShapeDtypeStruct((128, 2, 2, 8, 128), jnp.float32),
         compiler_params=params(VMEM),
-        cost_estimate=cost(512 * 512 * 256, 6 * MIB),
+        cost_estimate=cost(512 * 512 * 512, 8 * MIB),
         name="second",
-    )(place, done_y, part, *pieces, table)
+    )(gy, gz, part_a, *pieces_a, table_y, part_b, *pieces_b, table_z)
 
 
 def third_kernel(slot_ref, in_ref, table_ref, ordering_ref, out_ref, held):
@@ -409,10 +428,11 @@
     b2, b0 = first(False, (2, 0), gy, gz, pieces, table_y)
     b2 = shifted(b2, "gz", 2)
 
+    part_a = part_y(gy, (a1, a3), table_y)
+    part_a, b1, b3 = lax.optimization_barrier((part_a, b1, b3))
     part_b = part_z(gz, (b1, b3), table_z)
-    done_a = second_y(gy, (a0, a1, a2, a3), table_y)
-    done_a, part_b, b2 = lax.optimization_barrier((done_a, part_b, b2))
-    planes = second(gz, done_a, part_b, (b0, b2), table_z)
+    part_b, a2, b2 = lax.optimization_barrier((part_b, a2, b2))
+    planes = second(gy, gz, part_a, (a0, a2), table_y, part_b, (b0, b2), table_z)
     lines = lax.all_to_all(planes, ALL, split_axis=0, concat_axis=0, tiled=True)
     outgoing = third(slots, lines, table_x, ordering)
     return lax.all_to_all(

time: 176 us -> 180 us (1.023)
  blocking collectives: 72.8 us -> 77.3 us
  waiting for transfers between devices: 53.7 us -> 50.1 us
  Pallas kernels: 27.8 us -> 30.7 us
    all_to_all x1, blocking collectives: 38.5 us -> 43.1 us  [per_device(): lines = lax.all_to_all(planes, ALL, split_axis=0, concat_axis=0, tiled=True)]
    ppermute x9, waiting for transfers between devices: 16.3 us -> 12.6 us  [shifted(): lax.ppermute(piece, axis, [(i, (i + shift) % size) for i in range(size)])]
    pallas_call x3, Pallas kernels: 11.3 us -> 14.2 us  [first(): pl.pallas_call(functools.partial(first_kernel, along_z, shifts, dynamic),...]
  transfers between devices with their start and end apart: 10 -> 10, of which waited for: 5 -> 4; matrix products, arithmetic and copies ran while one was open for 0% -> 0% of each run, Pallas kernels for 9% -> 12%
where the time goes in v14:
time: 180 us
  blocking collectives  77.3 us (43%)
  waiting for transfers between devices  50.1 us (28%)
  Pallas kernels  30.7 us (17%)
  starting transfers between devices  18.3 us (10%)
  local copies, waits for them, and re-layouts  2.53 us (1%)
    all_to_all x1, blocking collectives, per_device(): lines = lax.all_to_all(planes, ALL, split_axis=0, concat_axis=0, tiled=True)  43.1 us
    all_to_all x1, waiting for transfers between devices, per_device(): a = lax.all_to_all(a, 'gz', split_axis=0, concat_axis=0, tiled=True)  37.5 us
    all_to_all x1, blocking collectives, per_device(): lax.all_to_all(outgoing.reshape(128, 1, CAP, 2, BW), ALL, split_axis=0, c...  34.2 us
    pallas_call x3, Pallas kernels, first(): pl.pallas_call(functools.partial(first_kernel, along_z, shifts, dynamic),...  14.2 us
    ppermute x9, waiting for transfers between devices, shifted(): lax.ppermute(piece, axis, [(i, (i + shift) % size) for i in range(size)])  12.6 us
    ppermute x9, starting transfers between devices, shifted(): lax.ppermute(piece, axis, [(i, (i + shift) % size) for i in range(size)])  12.4 us
    pallas_call x3, Pallas kernels, scale(): pl.pallas_call(functools.partial(scale_kernel, half, shifts, rotated), in...  8.73 us
    all_to_all x1, starting transfers between devices, per_device(): a = lax.all_to_all(a, 'gz', split_axis=0, concat_axis=0, tiled=True)  5.87 us
  transfers between devices with their start and end apart: 10, of which 4 were waited for; matrix products, arithmetic and copies ran while one was open for 0% of the time, Pallas kernels for 12%

profile of v14, /device:TPU:1, one launch (start us, length us, event | category | flops | bytes accessed | tf_op | source)
XLA Modules:
  0.0 179.8 jit_solution(1281943721450597288)
XLA Ops:
  0.0 3.4 %scale_a.1 = f32[4,2,8,128,128]{4,3,2,1,0:T(8,128)} custom-call(s32[1]{0:T(128)} %bitcast.place_ref.to_ref.z_ref, bf16[2,8,8,128,128]{4,3,2,1,0:T(8,128)(2,1)} %bitcast.21, f32[8,8,128,128]{3,2,1,0:T(8,128)} %bitcast.24), custom_call_target="tpu_custom_call" | custom-call | flops 16 | bytes 128 | tf_op jit(solution)/shard_map/scale_a/pallas_call | solution.py:132
  3.4 5.9 %all-to-all-start = ((f32[4,2,8,128,128]{4,3,2,1,0:T(8,128)}), f32[4,2,8,128,128]{4,3,2,1,0:T(8,128)}, u32[]{:S(2)}, u32[]{:S(2)}) async-start(f32[4,2,8,128,128]{4,3,2,1,0:T(8,128)} %scale_a.1), calls=%async_computation | async-start | bytes 8388608 | tf_op jit(solution)/shard_map/all_to_all | solution.py:414
  9.2 3.1 %scale_b.2 = (f32[2,8,128,128]{3,2,1,0:T(8,128)}, f32[2,8,128,128]{3,2,1,0:T(8,128)}, f32[2,8,128,128]{3,2,1,0:T(8,128)}) custom-call(s32[1]{0:T(128)} %bitcast.3.place_ref.to_ref.y_ref, bf16[2,8,8,128,128]{4,3,2,1,0:T(8,128)(2,1)} %bitcast.22, f32[8,8,128,128]{3,2,1,0:T(8,128)} %bitcast.25), custom_call_target="tpu_custom_call" | custom-call | flops 12 | bytes 96 | tf_op jit(solution)/shard_map/scale_b/pallas_call | solution.py:132
  12.3 0.0 copy-start.7
  12.3 1.4 collective-permute-start.2
  13.7 2.6 %collective-permute-start.3 = (f32[2,8,128,128]{3,2,1,0:T(8,128)}, f32[2,8,128,128]{3,2,1,0:T(8,128)}, u32[]{:S(2)}, u32[]{:S(2)}) collective-permute-start(f32[2,8,128,128]{3,2,1,0:T(8,128)} %get-tuple-element.50), channel_id=1, source_target_pairs={{0,8},{4,12},{8,0},{12,4},{1,9},{5,13},{9,1},{13,5},{2,10},{6,14},... | collective-permute-start | bytes 3145736 | tf_op jit(solution)/shard_map/ppermute | solution.py:397
  16.3 1.1 collective-permute-start.4
  17.4 2.3 %scale_b.3.refs_0_ = f32[2,8,128,128]{3,2,1,0:T(8,128)} custom-call(s32[1]{0:T(128)} %bitcast.3.place_ref.to_ref.y_ref, bf16[2,8,8,128,128]{4,3,2,1,0:T(8,128)(2,1)} %bitcast.23, f32[8,8,128,128]{3,2,1,0:T(8,128)} %bitcast.26), custom_call_target="tpu_custom_call" | custom-call | flops 4 | bytes 32 | tf_op jit(solution)/shard_map/scale_b/pallas_call | solution.py:132
  19.7 0.0 copy-start.1
  19.7 0.0 copy-done.7
  19.7 0.1 copy.11
  19.8 0.2 fusion.2
  20.1 0.1 copy.12
  20.2 0.4 fusion.1
  20.6 0.0 copy-start
  20.6 37.5 %all-to-all-done.refs_0_ = f32[4,2,8,128,128]{4,3,2,1,0:T(8,128)} async-done(((f32[4,2,8,128,128]{4,3,2,1,0:T(8,128)}), f32[4,2,8,128,128]{4,3,2,1,0:T(8,128)}, u32[]{:S(2)}, u32[]{:S(2)}) %all-to-all-start) | async-done | bytes 4194336 | tf_op jit(solution)/shard_map/all_to_all | solution.py:414
  58.1 0.0 copy-done.1
  58.1 6.5 %first_z.1 = (f32[2,2,128,256]{3,2,1,0:T(8,128)}, f32[2,2,128,256]{3,2,1,0:T(8,128)}, f32[2,2,128,256]{3,2,1,0:T(8,128)}, f32[2,2,128,256]{3,2,1,0:T(8,128)}) custom-call(s32[1]{0:T(128)} %bitcast.place_ref.to_ref.z_ref, s32[1]{0:T(128)} %bitcast.3.place_ref.to_ref.y_ref, f32[4,2,8,128,128]{4,3,2,1,0:T(8,128)} %all-to-all-done.refs_0_, ...), custom_call_target="tpu_custom_call" | custom-call | flops 4096 | bytes 128 | tf_op jit(solution)/shard_map/first_z/pallas_call | solution.py:221
  64.6 2.8 %collective-permute-start.1 = (f32[2,2,128,256]{3,2,1,0:T(8,128)}, f32[2,2,128,256]{3,2,1,0:T(8,128)S(1)}, u32[]{:S(2)}, u32[]{:S(2)}) collective-permute-start(f32[2,2,128,256]{3,2,1,0:T(8,128)} %get-tuple-element.46), channel_id=1, source_target_pairs={{0,12},{4,0},{8,4},{12,8},{1,13},{5,1},{9,5},{13,9},{2,14},{6,2},{... | collective-permute-start | bytes 1572872 | tf_op jit(solution)/shard_map/ppermute | solution.py:397
  67.4 0.0 collective-permute-start
  67.4 0.0 collective-permute-done.2.refs_1_
  67.4 0.0 collective-permute-done.3.refs_2_
  67.5 0.0 collective-permute-done.4.refs_3_
  67.5 1.0 copy-done.6
  68.4 0.0 copy-done
  68.4 3.9 %first_y.2 = (f32[2,2,256,128]{3,2,1,0:T(8,128)}, f32[2,2,256,128]{3,2,1,0:T(8,128)}) custom-call(s32[1]{0:T(128)} %bitcast.3.place_ref.to_ref.y_ref, s32[1]{0:T(128)} %bitcast.place_ref.to_ref.z_ref, f32[2,8,128,128]{3,2,1,0:T(8,128)} %scale_b.3.refs_0_, f32[2,8,128,128]{3,2,1,0:T(8,128)} %copy-done.6, f32[2,8,128,128]{3,2,1,0:T(8,128)} %collective-permute-done.3.refs_2_, ...), custom_call_target="tpu_custom_call" | custom-call | flops 2048 | bytes 64 | tf_op jit(solution)/shard_map/first_y/pallas_call | solution.py:221
  72.3 0.0 copy-start.8
  72.3 1.0 collective-permute-start.5
  73.3 1.8 collective-permute-start.6
  75.0 3.9 %first_y.3 = (f32[2,2,256,128]{3,2,1,0:T(8,128)}, f32[2,2,256,128]{3,2,1,0:T(8,128)}) custom-call(s32[1]{0:T(128)} %bitcast.3.place_ref.to_ref.y_ref, s32[1]{0:T(128)} %bitcast.place_ref.to_ref.z_ref, f32[2,8,128,128]{3,2,1,0:T(8,128)} %scale_b.3.refs_0_, f32[2,8,128,128]{3,2,1,0:T(8,128)} %copy-done.6, f32[2,8,128,128]{3,2,1,0:T(8,128)} %collective-permute-done.3.refs_2_, ...), custom_call_target="tpu_custom_call" | custom-call | flops 2048 | bytes 64 | tf_op jit(solution)/shard_map/first_y/pallas_call | solution.py:221
  78.9 0.0 copy-done.8
  78.9 1.7 collective-permute-start.7
  80.7 0.0 collective-permute-done.1.p3
  80.7 0.1 collective-permute-start.8
  80.8 0.0 collective-permute-done.p1
  80.8 0.9 part_y.1.part_a
  81.7 3.9 %collective-permute-done.5.p1 = f32[2,2,256,128]{3,2,1,0:T(8,128)S(1)} collective-permute-done((f32[2,2,256,128]{3,2,1,0:T(8,128)}, f32[2,2,256,128]{3,2,1,0:T(8,128)S(1)}, u32[]{:S(2)}, u32[]{:S(2)}) %collective-permute-start.5) | collective-permute-done | bytes 524320 | tf_op jit(solution)/shard_map/ppermute | solution.py:397
  85.6 0.0 collective-permute-done.6.p3
  85.6 0.9 part_z.1.part_b
  86.5 5.1 %collective-permute-done.7.a2 = f32[2,2,128,256]{3,2,1,0:T(8,128)S(1)} collective-permute-done((f32[2,2,128,256]{3,2,1,0:T(8,128)S(1)}, f32[2,2,128,256]{3,2,1,0:T(8,128)S(1)}, u32[]{:S(2)}, u32[]{:S(2)}) %collective-permute-start.7) | collective-permute-done | bytes 524320 | tf_op jit(solution)/shard_map/ppermute | solution.py:397
  91.5 3.6 %collective-permute-done.8.b2 = f32[2,2,256,128]{3,2,1,0:T(8,128)S(1)} collective-permute-done((f32[2,2,256,128]{3,2,1,0:T(8,128)}, f32[2,2,256,128]{3,2,1,0:T(8,128)S(1)}, u32[]{:S(2)}, u32[]{:S(2)}) %collective-permute-start.8) | collective-permute-done | bytes 524320 | tf_op jit(solution)/shard_map/ppermute | solution.py:397
  95.2 2.2 %second.1 = f32[128,2,2,8,128]{4,3,2,1,0:T(8,128)S(1)} custom-call(s32[1]{0:T(128)} %bitcast.3.place_ref.to_ref.y_ref, s32[1]{0:T(128)} %bitcast.place_ref.to_ref.z_ref, f32[2,256,512]{2,1,0:T(8,128)S(1)} %part_y.1.part_a, f32[2,2,128,256]{3,2,1,0:T(8,128)S(1)} %copy-done.3, f32[2,2,128,256]{3,2,1,0:T(8,128)S(1)} %collective-permute-done.7.a2, ...), custom_call_target="tpu_custom_call" | custom-call | flops 2048 | bytes 128 | tf_op jit(solution)/shard_map/second/pallas_call | solution.py:321
  97.4 0.0 copy-start.2
  97.4 0.0 copy-start.5
  97.4 43.1 %all_to_all.22.in_ref = f32[128,2,2,8,128]{4,3,2,1,0:T(8,128)S(1)} all-to-all(f32[128,2,2,8,128]{4,3,2,1,0:T(8,128)S(1)} %second.1), channel_id=1, replica_groups=mesh['gx'=8,'gy'=4,'gz'=4] {'gx','gy','gz'}, dimensions={0} | all-to-all | bytes 4194304 | tf_op jit(solution)/shard_map/all_to_all | solution.py:436
  140.5 3.7 %third.1 = f32[4096,128]{1,0:T(8,128)S(1)} custom-call(s32[1024]{0:T(1024)S(1)} %multiply_add_fusion.slot_ref, f32[128,2,2,8,128]{4,3,2,1,0:T(8,128)S(1)} %all_to_all.22.in_ref, bf16[2,2,256,512]{3,2,1,0:T(8,128)(2,1)S(1)} %copy-done.2, bf16[256,256]{1,0:T(8,128)(2,1)S(1)} %copy-done.5), custom_call_target="tpu_custom_call" | custom-call | flops 3072 | bytes 96 | tf_op jit(solution)/shard_map/third/pallas_call | solution.py:383
  144.2 34.2 %all_to_all.23 = f32[128,1,16,2,128]{4,3,2,1,0:T(2,128)S(1)} all-to-all(f32[128,1,16,2,128]{4,3,2,1,0:T(2,128)S(1)} %bitcast.20), channel_id=1, replica_groups=mesh['gx'=8,'gy'=4,'gz'=4] {'gx','gy','gz'}, dimensions={0} | all-to-all | bytes 4194304 | tf_op jit(solution)/shard_map/all_to_all | solution.py:438
  178.5 1.3 copy.15
  (12 shorter events, 0.1 us)
Async XLA Ops:
  3.4 54.8 %all-to-all-start = ((f32[4,2,8,128,128]{4,3,2,1,0:T(8,128)}), f32[4,2,8,128,128]{4,3,2,1,0:T(8,128)}, u32[]{:S(2)}, u32[]{:S(2)}) async-start(f32[4,2,8,128,128]{4,3,2,1,0:T(8,128)} %scale_a.1), calls=%async_computation | async-start | bytes 8388608 | tf_op jit(solution)/shard_map/all_to_all | solution.py:414
  12.3 7.4 %copy-start.7 = (s32[1024,1]{0,1:T(1,128)S(1)}, s32[1024,1]{0,1:T(1,128)}, u32[]{:S(2)}) copy-start(s32[1024,1]{0,1:T(1,128)} %param.9) | copy-start | bytes 12292
  12.3 55.1 %collective-permute-start.2 = (f32[2,8,128,128]{3,2,1,0:T(8,128)}, f32[2,8,128,128]{3,2,1,0:T(8,128)S(1)}, u32[]{:S(2)}, u32[]{:S(2)}) collective-permute-start(f32[2,8,128,128]{3,2,1,0:T(8,128)} %get-tuple-element.49), channel_id=1, source_target_pairs={{0,4},{4,8},{8,12},{12,0},{1,5},{5,9},{9,13},{13,1},{2,6},{6,10},{... | collective-permute-start | bytes 3145736 | tf_op jit(solution)/shard_map/ppermute | solution.py:397
  13.7 53.7 %collective-permute-start.3 = (f32[2,8,128,128]{3,2,1,0:T(8,128)}, f32[2,8,128,128]{3,2,1,0:T(8,128)}, u32[]{:S(2)}, u32[]{:S(2)}) collective-permute-start(f32[2,8,128,128]{3,2,1,0:T(8,128)} %get-tuple-element.50), channel_id=1, source_target_pairs={{0,8},{4,12},{8,0},{12,4},{1,9},{5,13},{9,1},{13,5},{2,10},{6,14},... | collective-permute-start | bytes 3145736 | tf_op jit(solution)/shard_map/ppermute | solution.py:397
  16.3 51.1 %collective-permute-start.4 = (f32[2,8,128,128]{3,2,1,0:T(8,128)}, f32[2,8,128,128]{3,2,1,0:T(8,128)}, u32[]{:S(2)}, u32[]{:S(2)}) collective-permute-start(f32[2,8,128,128]{3,2,1,0:T(8,128)} %get-tuple-element.51), channel_id=1, source_target_pairs={{0,12},{4,0},{8,4},{12,8},{1,13},{5,1},{9,5},{13,9},{2,14},{6,2},{... | collective-permute-start | bytes 3145736 | tf_op jit(solution)/shard_map/ppermute | solution.py:397
  19.7 38.5 %copy-start.1 = (bf16[2,2,2,256,256]{4,3,2,1,0:T(8,128)(2,1)S(1)}, bf16[2,2,2,256,256]{4,3,2,1,0:T(8,128)(2,1)}, u32[]{:S(2)}) copy-start(bf16[2,2,2,256,256]{4,3,2,1,0:T(8,128)(2,1)} %constant.25.clone.refs_1_.table_ref.table_z_ref) | copy-start | bytes 3145732
  20.6 47.8 %copy-start = (bf16[2,2,2,256,256]{4,3,2,1,0:T(8,128)(2,1)S(1)}, bf16[2,2,2,256,256]{4,3,2,1,0:T(8,128)(2,1)}, u32[]{:S(2)}) copy-start(bf16[2,2,2,256,256]{4,3,2,1,0:T(8,128)(2,1)} %constant.24.clone.table_ref.refs_4_.table_y_ref) | copy-start | bytes 3145732
  64.6 16.0 %collective-permute-start.1 = (f32[2,2,128,256]{3,2,1,0:T(8,128)}, f32[2,2,128,256]{3,2,1,0:T(8,128)S(1)}, u32[]{:S(2)}, u32[]{:S(2)}) collective-permute-start(f32[2,2,128,256]{3,2,1,0:T(8,128)} %get-tuple-element.46), channel_id=1, source_target_pairs={{0,12},{4,0},{8,4},{12,8},{1,13},{5,1},{9,5},{13,9},{2,14},{6,2},{... | collective-permute-start | bytes 1572872 | tf_op jit(solution)/shard_map/ppermute | solution.py:397
  67.4 13.3 %collective-permute-start = (f32[2,2,128,256]{3,2,1,0:T(8,128)}, f32[2,2,128,256]{3,2,1,0:T(8,128)S(1)}, u32[]{:S(2)}, u32[]{:S(2)}) collective-permute-start(f32[2,2,128,256]{3,2,1,0:T(8,128)} %get-tuple-element.45), channel_id=1, source_target_pairs={{0,4},{4,8},{8,12},{12,0},{1,5},{5,9},{9,13},{13,1},{2,6},{6,10},{... | collective-permute-start | bytes 1572872 | tf_op jit(solution)/shard_map/ppermute | solution.py:397
  67.4 1.0 copy-start.6
  72.3 6.6 %copy-start.8 = (f32[2,2,128,256]{3,2,1,0:T(8,128)S(1)}, f32[2,2,128,256]{3,2,1,0:T(8,128)}, u32[]{:S(2)}) copy-start(f32[2,2,128,256]{3,2,1,0:T(8,128)} %get-tuple-element.63) | copy-start | bytes 1572868
  72.3 13.3 %collective-permute-start.5 = (f32[2,2,256,128]{3,2,1,0:T(8,128)}, f32[2,2,256,128]{3,2,1,0:T(8,128)S(1)}, u32[]{:S(2)}, u32[]{:S(2)}) collective-permute-start(f32[2,2,256,128]{3,2,1,0:T(8,128)} %get-tuple-element.57), channel_id=1, source_target_pairs={{0,1},{1,2},{2,3},{3,0},{4,5},{5,6},{6,7},{7,4},{8,9},{9,10},{10,1... | collective-permute-start | bytes 1572872 | tf_op jit(solution)/shard_map/ppermute | solution.py:397
  73.3 12.3 %collective-permute-start.6 = (f32[2,2,256,128]{3,2,1,0:T(8,128)}, f32[2,2,256,128]{3,2,1,0:T(8,128)S(1)}, u32[]{:S(2)}, u32[]{:S(2)}) collective-permute-start(f32[2,2,256,128]{3,2,1,0:T(8,128)} %get-tuple-element.58), channel_id=1, source_target_pairs={{0,3},{1,0},{2,1},{3,2},{4,7},{5,4},{6,5},{7,6},{8,11},{9,8},{10,9... | collective-permute-start | bytes 1572872 | tf_op jit(solution)/shard_map/ppermute | solution.py:397
  78.9 12.6 %collective-permute-start.7 = (f32[2,2,128,256]{3,2,1,0:T(8,128)S(1)}, f32[2,2,128,256]{3,2,1,0:T(8,128)S(1)}, u32[]{:S(2)}, u32[]{:S(2)}) collective-permute-start(f32[2,2,128,256]{3,2,1,0:T(8,128)S(1)} %copy-done.8), channel_id=1, source_target_pairs={{0,8},{4,12},{8,0},{12,4},{1,9},{5,13},{9,1},{13,5},{2,10},{6,14},... | collective-permute-start | bytes 1572872 | tf_op jit(solution)/shard_map/ppermute | solution.py:397
  80.7 14.5 %collective-permute-start.8 = (f32[2,2,256,128]{3,2,1,0:T(8,128)}, f32[2,2,256,128]{3,2,1,0:T(8,128)S(1)}, u32[]{:S(2)}, u32[]{:S(2)}) collective-permute-start(f32[2,2,256,128]{3,2,1,0:T(8,128)} %get-tuple-element.64), channel_id=1, source_target_pairs={{0,2},{1,3},{2,0},{3,1},{4,6},{5,7},{6,4},{7,5},{8,10},{9,11},{10,... | collective-permute-start | bytes 1572872 | tf_op jit(solution)/shard_map/ppermute | solution.py:397
  81.7 13.5 %copy-start.3 = (f32[2,2,128,256]{3,2,1,0:T(8,128)S(1)}, f32[2,2,128,256]{3,2,1,0:T(8,128)}, u32[]{:S(2)}) copy-start(f32[2,2,128,256]{3,2,1,0:T(8,128)} %get-tuple-element.60.a0) | copy-start | bytes 1572868
  81.7 13.5 %copy-start.4 = (f32[2,2,256,128]{3,2,1,0:T(8,128)S(1)}, f32[2,2,256,128]{3,2,1,0:T(8,128)}, u32[]{:S(2)}) copy-start(f32[2,2,256,128]{3,2,1,0:T(8,128)} %get-tuple-element.67.b0) | copy-start | bytes 1572868
  97.4 43.1 %copy-start.2 = (bf16[2,2,256,512]{3,2,1,0:T(8,128)(2,1)S(1)}, bf16[2,2,256,512]{3,2,1,0:T(8,128)(2,1)}, u32[]{:S(2)}) copy-start(bf16[2,2,256,512]{3,2,1,0:T(8,128)(2,1)} %constant.23.clone.table_ref) | copy-start | bytes 3145732
  97.4 43.1 %copy-start.5 = (bf16[256,256]{1,0:T(8,128)(2,1)S(1)}, bf16[256,256]{1,0:T(8,128)(2,1)}, u32[]{:S(2)}) copy-start(bf16[256,256]{1,0:T(8,128)(2,1)} %constant.26.clone.ordering_ref) | copy-start | bytes 393220

commit v15 on v14

--- a/solution.py
+++ b/solution.py
@@ -184,14 +184,12 @@
         return pltpu.make_async_copy(held_out.at[i], out_refs[i], semaphores.at[i, 4])
 
     steps = range(len(shifts))
-    for copy in gets(0):
-        copy.start()
+    for i in steps:
+        for copy in gets(i):
+            copy.start()
     for i in steps:
         for copy in gets(i):
             copy.wait()
-        if i + 1 < len(shifts):
-            for copy in gets(i + 1):
-                copy.start()
         if dynamic:
             g, h = place_ref[0], lax.rem(place_ref[0] + 3, 4)
         else:
@@ -259,8 +257,8 @@
     )(place, *pieces, table)
 
 
-def part_z_kernel(place_ref, p1, p3, table_ref, out_ref):
-    pairs = [(p1[...], p3[...], lax.rem(place_ref[0] + 3, 4))]
+def part_z_kernel(place_ref, p0, p2, table_ref, out_ref):
+    pairs = [(p0[...], p2[...], place_ref[0])]
     for odd, values in enumerate(transform(True, pairs, table_ref)):
         out_ref[0, :, odd * 256 : (odd + 1) * 256] = values
 
@@ -283,7 +281,7 @@
 
 
 def second_kernel(
-    y_ref, z_ref, part_a, a0, a2, table_y_ref, part_b, b0, b2, table_z_ref, out_ref, held
+    y_ref, z_ref, part_a, a0, a2, table_y_ref, part_b, b1, b3, table_z_ref, out_ref, held
 ):
     odd = pl.program_id(0)
 
@@ -304,7 +302,7 @@
                     half,
                     plane * 4 + x,
                 )
-    parts = transform(True, [(b0[...], b2[...], z_ref[0])], table_z_ref)
+    parts = transform(True, [(b1[...], b3[...], lax.rem(z_ref[0] + 3, 4))], table_z_ref)
     for half, values in enumerate(parts):
         values = values + part_b[:, :, half * 256 : (half + 1) * 256].reshape(256, 256)
         for x in range(2):
@@ -422,17 +420,17 @@
     b1, b2, b3, _ = lax.optimization_barrier((b1, b2, b3, a1))
     pieces = [b0, b1, b2, b3]
     a1, a3 = shifted(a1, "gy", 1), shifted(a3, "gy", 3)
-    b1, b3 = first(False, (1, 3), gy, gz, pieces, table_y)
-    a2, b1, b3 = lax.optimization_barrier((a2, b1, b3))
-    b1, b3, a2 = shifted(b1, "gz", 1), shifted(b3, "gz", 3), shifted(a2, "gy", 2)
-    b2, b0 = first(False, (2, 0), gy, gz, pieces, table_y)
-    b2 = shifted(b2, "gz", 2)
+    b2, b1 = first(False, (2, 1), gy, gz, pieces, table_y)
+    a2, b2, b1 = lax.optimization_barrier((a2, b2, b1))
+    b2, b1, a2 = shifted(b2, "gz", 2), shifted(b1, "gz", 1), shifted(a2, "gy", 2)
+    b3, b0 = first(False, (3, 0), gy, gz, pieces, table_y)
+    b3 = shifted(b3, "gz", 3)
 
     part_a = part_y(gy, (a1, a3), table_y)
-    part_a, b1, b3 = lax.optimization_barrier((part_a, b1, b3))
-    part_b = part_z(gz, (b1, b3), table_z)
-    part_b, a2, b2 = lax.optimization_barrier((part_b, a2, b2))
-    planes = second(gy, gz, part_a, (a0, a2), table_y, part_b, (b0, b2), table_z)
+    part_a, b2 = lax.optimization_barrier((part_a, b2))
+    part_b = part_z(gz, (b0, b2), table_z)
+    part_b, a2, b1, b3 = lax.optimization_barrier((part_b, a2, b1, b3))
+    planes = second(gy, gz, part_a, (a0, a2), table_y, part_b, (b1, b3), table_z)
     lines = lax.all_to_all(planes, ALL, split_axis=0, concat_axis=0, tiled=True)
     outgoing = third(slots, lines, table_x, ordering)
     return lax.all_to_all(

time: 180 us -> 177 us (0.983)
  blocking collectives: 77.3 us -> 72.9 us
  waiting for transfers between devices: 50.1 us -> 54 us
  Pallas kernels: 30.7 us -> 27.7 us
    all_to_all x1, blocking collectives: 43.1 us -> 38.7 us  [per_device(): lines = lax.all_to_all(planes, ALL, split_axis=0, concat_axis=0, tiled=True)]
    ppermute x9, waiting for transfers between devices: 12.6 us -> 16.5 us  [shifted(): lax.ppermute(piece, axis, [(i, (i + shift) % size) for i in range(size)])]
    pallas_call x3, Pallas kernels: 14.2 us -> 11.3 us  [first(): pl.pallas_call(functools.partial(first_kernel, along_z, shifts, dynamic),...]
  transfers between devices with their start and end apart: 10 -> 10, of which waited for: 4 -> 5; matrix products, arithmetic and copies ran while one was open for 0% -> 0% of each run, Pallas kernels for 12% -> 10%
where the time goes in v15:
time: 177 us
  blocking collectives  72.9 us (41%)
  waiting for transfers between devices  54 us (31%)
  Pallas kernels  27.7 us (16%)
  starting transfers between devices  18.8 us (11%)
  local copies, waits for them, and re-layouts  2.53 us (1%)
    all_to_all x1, blocking collectives, per_device(): lines = lax.all_to_all(planes, ALL, split_axis=0, concat_axis=0, tiled=True)  38.7 us
    all_to_all x1, waiting for transfers between devices, per_device(): a = lax.all_to_all(a, 'gz', split_axis=0, concat_axis=0, tiled=True)  37.5 us
    all_to_all x1, blocking collectives, per_device(): lax.all_to_all(outgoing.reshape(128, 1, CAP, 2, BW), ALL, split_axis=0, c...  34.2 us
    ppermute x9, waiting for transfers between devices, shifted(): lax.ppermute(piece, axis, [(i, (i + shift) % size) for i in range(size)])  16.5 us
    ppermute x9, starting transfers between devices, shifted(): lax.ppermute(piece, axis, [(i, (i + shift) % size) for i in range(size)])  13 us
    pallas_call x3, Pallas kernels, first(): pl.pallas_call(functools.partial(first_kernel, along_z, shifts, dynamic),...  11.3 us
    pallas_call x3, Pallas kernels, scale(): pl.pallas_call(functools.partial(scale_kernel, half, shifts, rotated), in...  8.75 us
    all_to_all x1, starting transfers between devices, per_device(): a = lax.all_to_all(a, 'gz', split_axis=0, concat_axis=0, tiled=True)  5.87 us
  transfers between devices with their start and end apart: 10, of which 5 were waited for; matrix products, arithmetic and copies ran while one was open for 0% of the time, Pallas kernels for 10%

profile of v15, /device:TPU:1, one launch (start us, length us, event | category | flops | bytes accessed | tf_op | source)
XLA Modules:
  0.0 176.9 jit_solution(5715170381302002631)
XLA Ops:
  0.0 3.4 %scale_a.1 = f32[4,2,8,128,128]{4,3,2,1,0:T(8,128)} custom-call(s32[1]{0:T(128)} %bitcast.place_ref.to_ref.z_ref, bf16[2,8,8,128,128]{4,3,2,1,0:T(8,128)(2,1)} %bitcast.21, f32[8,8,128,128]{3,2,1,0:T(8,128)} %bitcast.24), custom_call_target="tpu_custom_call" | custom-call | flops 16 | bytes 128 | tf_op jit(solution)/shard_map/scale_a/pallas_call | solution.py:132
  3.4 5.9 %all-to-all-start = ((f32[4,2,8,128,128]{4,3,2,1,0:T(8,128)}), f32[4,2,8,128,128]{4,3,2,1,0:T(8,128)}, u32[]{:S(2)}, u32[]{:S(2)}) async-start(f32[4,2,8,128,128]{4,3,2,1,0:T(8,128)} %scale_a.1), calls=%async_computation | async-start | bytes 8388608 | tf_op jit(solution)/shard_map/all_to_all | solution.py:412
  9.3 3.1 %scale_b.2 = (f32[2,8,128,128]{3,2,1,0:T(8,128)}, f32[2,8,128,128]{3,2,1,0:T(8,128)}, f32[2,8,128,128]{3,2,1,0:T(8,128)}) custom-call(s32[1]{0:T(128)} %bitcast.3.place_ref.to_ref.y_ref, bf16[2,8,8,128,128]{4,3,2,1,0:T(8,128)(2,1)} %bitcast.22, f32[8,8,128,128]{3,2,1,0:T(8,128)} %bitcast.25), custom_call_target="tpu_custom_call" | custom-call | flops 12 | bytes 96 | tf_op jit(solution)/shard_map/scale_b/pallas_call | solution.py:132
  12.4 0.0 copy-start.7
  12.4 1.4 collective-permute-start.2
  13.7 2.6 %collective-permute-start.3 = (f32[2,8,128,128]{3,2,1,0:T(8,128)}, f32[2,8,128,128]{3,2,1,0:T(8,128)}, u32[]{:S(2)}, u32[]{:S(2)}) collective-permute-start(f32[2,8,128,128]{3,2,1,0:T(8,128)} %get-tuple-element.50), channel_id=1, source_target_pairs={{0,8},{4,12},{8,0},{12,4},{1,9},{5,13},{9,1},{13,5},{2,10},{6,14},... | collective-permute-start | bytes 3145736 | tf_op jit(solution)/shard_map/ppermute | solution.py:395
  16.4 1.1 collective-permute-start.4
  17.4 2.3 %scale_b.3.refs_0_ = f32[2,8,128,128]{3,2,1,0:T(8,128)} custom-call(s32[1]{0:T(128)} %bitcast.3.place_ref.to_ref.y_ref, bf16[2,8,8,128,128]{4,3,2,1,0:T(8,128)(2,1)} %bitcast.23, f32[8,8,128,128]{3,2,1,0:T(8,128)} %bitcast.26), custom_call_target="tpu_custom_call" | custom-call | flops 4 | bytes 32 | tf_op jit(solution)/shard_map/scale_b/pallas_call | solution.py:132
  19.7 0.0 copy-start.1
  19.7 0.0 copy-done.7
  19.7 0.1 copy.11
  19.8 0.2 fusion.2
  20.1 0.1 copy.12
  20.2 0.4 fusion.1
  20.6 0.0 copy-start
  20.6 37.5 %all-to-all-done.refs_0_ = f32[4,2,8,128,128]{4,3,2,1,0:T(8,128)} async-done(((f32[4,2,8,128,128]{4,3,2,1,0:T(8,128)}), f32[4,2,8,128,128]{4,3,2,1,0:T(8,128)}, u32[]{:S(2)}, u32[]{:S(2)}) %all-to-all-start) | async-done | bytes 4194336 | tf_op jit(solution)/shard_map/all_to_all | solution.py:412
  58.2 0.0 copy-done.1
  58.2 4.5 %first_z.1 = (f32[2,2,128,256]{3,2,1,0:T(8,128)}, f32[2,2,128,256]{3,2,1,0:T(8,128)}, f32[2,2,128,256]{3,2,1,0:T(8,128)}, f32[2,2,128,256]{3,2,1,0:T(8,128)}) custom-call(s32[1]{0:T(128)} %bitcast.place_ref.to_ref.z_ref, s32[1]{0:T(128)} %bitcast.3.place_ref.to_ref.y_ref, f32[4,2,8,128,128]{4,3,2,1,0:T(8,128)} %all-to-all-done.refs_0_, ...), custom_call_target="tpu_custom_call" | custom-call | flops 4096 | bytes 128 | tf_op jit(solution)/shard_map/first_z/pallas_call | solution.py:219
  62.7 2.8 %collective-permute-start.1 = (f32[2,2,128,256]{3,2,1,0:T(8,128)}, f32[2,2,128,256]{3,2,1,0:T(8,128)S(1)}, u32[]{:S(2)}, u32[]{:S(2)}) collective-permute-start(f32[2,2,128,256]{3,2,1,0:T(8,128)} %get-tuple-element.46), channel_id=1, source_target_pairs={{0,12},{4,0},{8,4},{12,8},{1,13},{5,1},{9,5},{13,9},{2,14},{6,2},{... | collective-permute-start | bytes 1572872 | tf_op jit(solution)/shard_map/ppermute | solution.py:395
  65.5 0.0 collective-permute-start
  65.5 0.0 collective-permute-done.2.refs_1_
  65.5 0.0 collective-permute-done.3.refs_2_
  65.5 0.0 collective-permute-done.4.refs_3_
  65.5 1.0 copy-done.6
  66.5 0.0 copy-done
  66.5 3.4 %first_y.2 = (f32[2,2,256,128]{3,2,1,0:T(8,128)}, f32[2,2,256,128]{3,2,1,0:T(8,128)}) custom-call(s32[1]{0:T(128)} %bitcast.3.place_ref.to_ref.y_ref, s32[1]{0:T(128)} %bitcast.place_ref.to_ref.z_ref, f32[2,8,128,128]{3,2,1,0:T(8,128)} %scale_b.3.refs_0_, f32[2,8,128,128]{3,2,1,0:T(8,128)} %copy-done.6, f32[2,8,128,128]{3,2,1,0:T(8,128)} %collective-permute-done.3.refs_2_, ...), custom_call_target="tpu_custom_call" | custom-call | flops 2048 | bytes 64 | tf_op jit(solution)/shard_map/first_y/pallas_call | solution.py:219
  69.9 0.1 collective-permute-start.5
  70.0 3.4 %first_y.3 = (f32[2,2,256,128]{3,2,1,0:T(8,128)}, f32[2,2,256,128]{3,2,1,0:T(8,128)}) custom-call(s32[1]{0:T(128)} %bitcast.3.place_ref.to_ref.y_ref, s32[1]{0:T(128)} %bitcast.place_ref.to_ref.z_ref, f32[2,8,128,128]{3,2,1,0:T(8,128)} %scale_b.3.refs_0_, f32[2,8,128,128]{3,2,1,0:T(8,128)} %copy-done.6, f32[2,8,128,128]{3,2,1,0:T(8,128)} %collective-permute-done.3.refs_2_, ...), custom_call_target="tpu_custom_call" | custom-call | flops 2048 | bytes 64 | tf_op jit(solution)/shard_map/first_y/pallas_call | solution.py:219
  73.4 1.7 collective-permute-start.6
  75.1 0.9 collective-permute-start.7
  76.0 0.0 collective-permute-done.1.p3
  76.0 2.4 %collective-permute-start.8 = (f32[2,2,256,128]{3,2,1,0:T(8,128)}, f32[2,2,256,128]{3,2,1,0:T(8,128)S(1)}, u32[]{:S(2)}, u32[]{:S(2)}) collective-permute-start(f32[2,2,256,128]{3,2,1,0:T(8,128)} %get-tuple-element.64), channel_id=1, source_target_pairs={{0,3},{1,0},{2,1},{3,2},{4,7},{5,4},{6,5},{7,6},{8,11},{9,8},{10,9... | collective-permute-start | bytes 1572872 | tf_op jit(solution)/shard_map/ppermute | solution.py:395
  78.4 0.9 collective-permute-done.p1
  79.3 0.9 part_y.1.part_a
  80.2 3.1 %collective-permute-done.5.p2 = f32[2,2,256,128]{3,2,1,0:T(8,128)S(1)} collective-permute-done((f32[2,2,256,128]{3,2,1,0:T(8,128)}, f32[2,2,256,128]{3,2,1,0:T(8,128)S(1)}, u32[]{:S(2)}, u32[]{:S(2)}) %collective-permute-start.5) | collective-permute-done | bytes 524320 | tf_op jit(solution)/shard_map/ppermute | solution.py:395
  83.3 0.9 part_z.1.part_b
  84.2 4.8 %collective-permute-done.6.a2 = f32[2,2,128,256]{3,2,1,0:T(8,128)S(1)} collective-permute-done((f32[2,2,128,256]{3,2,1,0:T(8,128)S(1)}, f32[2,2,128,256]{3,2,1,0:T(8,128)S(1)}, u32[]{:S(2)}, u32[]{:S(2)}) %collective-permute-start.6) | collective-permute-done | bytes 524320 | tf_op jit(solution)/shard_map/ppermute | solution.py:395
  89.0 7.8 %collective-permute-done.7.b1 = f32[2,2,256,128]{3,2,1,0:T(8,128)S(1)} collective-permute-done((f32[2,2,256,128]{3,2,1,0:T(8,128)S(1)}, f32[2,2,256,128]{3,2,1,0:T(8,128)S(1)}, u32[]{:S(2)}, u32[]{:S(2)}) %collective-permute-start.7) | collective-permute-done | bytes 524320 | tf_op jit(solution)/shard_map/ppermute | solution.py:395
  96.8 0.0 collective-permute-done.8.b3
  96.8 0.0 copy-done.3
  96.8 2.2 %second.1 = f32[128,2,2,8,128]{4,3,2,1,0:T(8,128)S(1)} custom-call(s32[1]{0:T(128)} %bitcast.3.place_ref.to_ref.y_ref, s32[1]{0:T(128)} %bitcast.place_ref.to_ref.z_ref, f32[2,256,512]{2,1,0:T(8,128)S(1)} %part_y.1.part_a, f32[2,2,128,256]{3,2,1,0:T(8,128)S(1)} %copy-done.3, f32[2,2,128,256]{3,2,1,0:T(8,128)S(1)} %collective-permute-done.6.a2, ...), custom_call_target="tpu_custom_call" | custom-call | flops 2048 | bytes 128 | tf_op jit(solution)/shard_map/second/pallas_call | solution.py:319
  99.0 0.0 copy-start.2
  99.0 0.0 copy-start.5
  99.0 38.7 %all_to_all.22.in_ref = f32[128,2,2,8,128]{4,3,2,1,0:T(8,128)S(1)} all-to-all(f32[128,2,2,8,128]{4,3,2,1,0:T(8,128)S(1)} %second.1), channel_id=1, replica_groups=mesh['gx'=8,'gy'=4,'gz'=4] {'gx','gy','gz'}, dimensions={0} | all-to-all | bytes 4194304 | tf_op jit(solution)/shard_map/all_to_all | solution.py:434
  137.7 0.0 copy-done.5
  137.7 3.7 %third.1 = f32[4096,128]{1,0:T(8,128)S(1)} custom-call(s32[1024]{0:T(1024)S(1)} %multiply_add_fusion.slot_ref, f32[128,2,2,8,128]{4,3,2,1,0:T(8,128)S(1)} %all_to_all.22.in_ref, bf16[2,2,256,512]{3,2,1,0:T(8,128)(2,1)S(1)} %copy-done.2, bf16[256,256]{1,0:T(8,128)(2,1)S(1)} %copy-done.5), custom_call_target="tpu_custom_call" | custom-call | flops 3072 | bytes 96 | tf_op jit(solution)/shard_map/third/pallas_call | solution.py:381
  141.4 34.2 %all_to_all.23 = f32[128,1,16,2,128]{4,3,2,1,0:T(2,128)S(1)} all-to-all(f32[128,1,16,2,128]{4,3,2,1,0:T(2,128)S(1)} %bitcast.20), channel_id=1, replica_groups=mesh['gx'=8,'gy'=4,'gz'=4] {'gx','gy','gz'}, dimensions={0} | all-to-all | bytes 4194304 | tf_op jit(solution)/shard_map/all_to_all | solution.py:436
  175.6 1.3 copy.15
  (14 shorter events, 0.1 us)
Async XLA Ops:
  3.4 54.8 %all-to-all-start = ((f32[4,2,8,128,128]{4,3,2,1,0:T(8,128)}), f32[4,2,8,128,128]{4,3,2,1,0:T(8,128)}, u32[]{:S(2)}, u32[]{:S(2)}) async-start(f32[4,2,8,128,128]{4,3,2,1,0:T(8,128)} %scale_a.1), calls=%async_computation | async-start | bytes 8388608 | tf_op jit(solution)/shard_map/all_to_all | solution.py:412
  12.4 7.4 %copy-start.7 = (s32[1024,1]{0,1:T(1,128)S(1)}, s32[1024,1]{0,1:T(1,128)}, u32[]{:S(2)}) copy-start(s32[1024,1]{0,1:T(1,128)} %param.9) | copy-start | bytes 12292
  12.4 53.2 %collective-permute-start.2 = (f32[2,8,128,128]{3,2,1,0:T(8,128)}, f32[2,8,128,128]{3,2,1,0:T(8,128)S(1)}, u32[]{:S(2)}, u32[]{:S(2)}) collective-permute-start(f32[2,8,128,128]{3,2,1,0:T(8,128)} %get-tuple-element.49), channel_id=1, source_target_pairs={{0,4},{4,8},{8,12},{12,0},{1,5},{5,9},{9,13},{13,1},{2,6},{6,10},{... | collective-permute-start | bytes 3145736 | tf_op jit(solution)/shard_map/ppermute | solution.py:395
  13.7 51.8 %collective-permute-start.3 = (f32[2,8,128,128]{3,2,1,0:T(8,128)}, f32[2,8,128,128]{3,2,1,0:T(8,128)}, u32[]{:S(2)}, u32[]{:S(2)}) collective-permute-start(f32[2,8,128,128]{3,2,1,0:T(8,128)} %get-tuple-element.50), channel_id=1, source_target_pairs={{0,8},{4,12},{8,0},{12,4},{1,9},{5,13},{9,1},{13,5},{2,10},{6,14},... | collective-permute-start | bytes 3145736 | tf_op jit(solution)/shard_map/ppermute | solution.py:395
  16.4 49.2 %collective-permute-start.4 = (f32[2,8,128,128]{3,2,1,0:T(8,128)}, f32[2,8,128,128]{3,2,1,0:T(8,128)}, u32[]{:S(2)}, u32[]{:S(2)}) collective-permute-start(f32[2,8,128,128]{3,2,1,0:T(8,128)} %get-tuple-element.51), channel_id=1, source_target_pairs={{0,12},{4,0},{8,4},{12,8},{1,13},{5,1},{9,5},{13,9},{2,14},{6,2},{... | collective-permute-start | bytes 3145736 | tf_op jit(solution)/shard_map/ppermute | solution.py:395
  19.7 38.5 %copy-start.1 = (bf16[2,2,2,256,256]{4,3,2,1,0:T(8,128)(2,1)S(1)}, bf16[2,2,2,256,256]{4,3,2,1,0:T(8,128)(2,1)}, u32[]{:S(2)}) copy-start(bf16[2,2,2,256,256]{4,3,2,1,0:T(8,128)(2,1)} %constant.25.clone.refs_1_.table_ref.table_z_ref) | copy-start | bytes 3145732
  20.6 45.9 %copy-start = (bf16[2,2,2,256,256]{4,3,2,1,0:T(8,128)(2,1)S(1)}, bf16[2,2,2,256,256]{4,3,2,1,0:T(8,128)(2,1)}, u32[]{:S(2)}) copy-start(bf16[2,2,2,256,256]{4,3,2,1,0:T(8,128)(2,1)} %constant.24.clone.table_ref.refs_4_.table_y_ref) | copy-start | bytes 3145732
  62.7 13.3 %collective-permute-start.1 = (f32[2,2,128,256]{3,2,1,0:T(8,128)}, f32[2,2,128,256]{3,2,1,0:T(8,128)S(1)}, u32[]{:S(2)}, u32[]{:S(2)}) collective-permute-start(f32[2,2,128,256]{3,2,1,0:T(8,128)} %get-tuple-element.46), channel_id=1, source_target_pairs={{0,12},{4,0},{8,4},{12,8},{1,13},{5,1},{9,5},{13,9},{2,14},{6,2},{... | collective-permute-start | bytes 1572872 | tf_op jit(solution)/shard_map/ppermute | solution.py:395
  65.5 13.8 %collective-permute-start = (f32[2,2,128,256]{3,2,1,0:T(8,128)}, f32[2,2,128,256]{3,2,1,0:T(8,128)S(1)}, u32[]{:S(2)}, u32[]{:S(2)}) collective-permute-start(f32[2,2,128,256]{3,2,1,0:T(8,128)} %get-tuple-element.45), channel_id=1, source_target_pairs={{0,4},{4,8},{8,12},{12,0},{1,5},{5,9},{9,13},{13,1},{2,6},{6,10},{... | collective-permute-start | bytes 1572872 | tf_op jit(solution)/shard_map/ppermute | solution.py:395
  65.5 1.0 copy-start.6
  69.9 3.5 %copy-start.8 = (f32[2,2,128,256]{3,2,1,0:T(8,128)S(1)}, f32[2,2,128,256]{3,2,1,0:T(8,128)}, u32[]{:S(2)}) copy-start(f32[2,2,128,256]{3,2,1,0:T(8,128)} %get-tuple-element.62) | copy-start | bytes 1572868
  69.9 5.2 %copy-start.9 = (f32[2,2,256,128]{3,2,1,0:T(8,128)S(1)}, f32[2,2,256,128]{3,2,1,0:T(8,128)}, u32[]{:S(2)}) copy-start(f32[2,2,256,128]{3,2,1,0:T(8,128)} %get-tuple-element.63) | copy-start | bytes 1572868
  69.9 13.4 %collective-permute-start.5 = (f32[2,2,256,128]{3,2,1,0:T(8,128)}, f32[2,2,256,128]{3,2,1,0:T(8,128)S(1)}, u32[]{:S(2)}, u32[]{:S(2)}) collective-permute-start(f32[2,2,256,128]{3,2,1,0:T(8,128)} %get-tuple-element.57), channel_id=1, source_target_pairs={{0,2},{1,3},{2,0},{3,1},{4,6},{5,7},{6,4},{7,5},{8,10},{9,11},{10,... | collective-permute-start | bytes 1572872 | tf_op jit(solution)/shard_map/ppermute | solution.py:395
  73.4 9.9 %copy-start.4 = (f32[2,2,256,128]{3,2,1,0:T(8,128)S(1)}, f32[2,2,256,128]{3,2,1,0:T(8,128)}, u32[]{:S(2)}) copy-start(f32[2,2,256,128]{3,2,1,0:T(8,128)} %get-tuple-element.60.p0) | copy-start | bytes 1572868
  73.4 15.6 %collective-permute-start.6 = (f32[2,2,128,256]{3,2,1,0:T(8,128)S(1)}, f32[2,2,128,256]{3,2,1,0:T(8,128)S(1)}, u32[]{:S(2)}, u32[]{:S(2)}) collective-permute-start(f32[2,2,128,256]{3,2,1,0:T(8,128)S(1)} %copy-done.8), channel_id=1, source_target_pairs={{0,8},{4,12},{8,0},{12,4},{1,9},{5,13},{9,1},{13,5},{2,10},{6,14},... | collective-permute-start | bytes 1572872 | tf_op jit(solution)/shard_map/ppermute | solution.py:395
  75.1 21.7 %collective-permute-start.7 = (f32[2,2,256,128]{3,2,1,0:T(8,128)S(1)}, f32[2,2,256,128]{3,2,1,0:T(8,128)S(1)}, u32[]{:S(2)}, u32[]{:S(2)}) collective-permute-start(f32[2,2,256,128]{3,2,1,0:T(8,128)S(1)} %copy-done.9), channel_id=1, source_target_pairs={{0,1},{1,2},{2,3},{3,0},{4,5},{5,6},{6,7},{7,4},{8,9},{9,10},{10,1... | collective-permute-start | bytes 1572872 | tf_op jit(solution)/shard_map/ppermute | solution.py:395
  76.0 20.7 %collective-permute-start.8 = (f32[2,2,256,128]{3,2,1,0:T(8,128)}, f32[2,2,256,128]{3,2,1,0:T(8,128)S(1)}, u32[]{:S(2)}, u32[]{:S(2)}) collective-permute-start(f32[2,2,256,128]{3,2,1,0:T(8,128)} %get-tuple-element.64), channel_id=1, source_target_pairs={{0,3},{1,0},{2,1},{3,2},{4,7},{5,4},{6,5},{7,6},{8,11},{9,8},{10,9... | collective-permute-start | bytes 1572872 | tf_op jit(solution)/shard_map/ppermute | solution.py:395
  80.2 16.5 %copy-start.3 = (f32[2,2,128,256]{3,2,1,0:T(8,128)S(1)}, f32[2,2,128,256]{3,2,1,0:T(8,128)}, u32[]{:S(2)}) copy-start(f32[2,2,128,256]{3,2,1,0:T(8,128)} %get-tuple-element.59.a0) | copy-start | bytes 1572868
  99.0 38.7 %copy-start.2 = (bf16[2,2,256,512]{3,2,1,0:T(8,128)(2,1)S(1)}, bf16[2,2,256,512]{3,2,1,0:T(8,128)(2,1)}, u32[]{:S(2)}) copy-start(bf16[2,2,256,512]{3,2,1,0:T(8,128)(2,1)} %constant.23.clone.table_ref) | copy-start | bytes 3145732
  99.0 38.7 %copy-start.5 = (bf16[256,256]{1,0:T(8,128)(2,1)S(1)}, bf16[256,256]{1,0:T(8,128)(2,1)}, u32[]{:S(2)}) copy-start(bf16[256,256]{1,0:T(8,128)(2,1)} %constant.26.clone.ordering_ref) | copy-start | bytes 393220

commit v16 on v15

--- a/solution.py
+++ b/solution.py
@@ -44,8 +44,8 @@
     table_y = np.concatenate([top, bottom], 2)
     gx, gy, gz = np.meshgrid(np.arange(8), np.arange(4), np.arange(4), indexing="ij")
     first = 64 * gx + 8 * gz + 2 * gy
-    second = 64 * gx + 32 + 8 * gy + 2 * gz
-    cells = np.stack([first, first + 1, second, second + 1], -1).reshape(128, 4)
+    second = 64 * gx + 32 + 8 * gy + gz
+    cells = np.stack([first, first + 1, second, second + 4], -1).reshape(128, 4)
     cosine, sine = cos_sin(cells[:64].reshape(-1), order)
     cosine, sine = (
         t.T.reshape(2, KEPT // 2, 64, 1, 4) for t in (cosine, sine)
@@ -96,18 +96,22 @@
     return [pltpu.with_memory_space_constraint(x, pltpu.HBM) for x in arrays]
 
 
-def scale_kernel(half, shifts, rotated, place_ref, normals_ref, spectrum_ref, *refs):
+def scale_kernel(part, shifts, place_ref, normals_ref, spectrum_ref, *refs):
     *out_refs, held_out, held_n, held_s, semaphores = refs
 
     def gets(i):
-        chunk = 4 * half + (lax.rem(place_ref[0] + shifts[i], 4) if rotated else shifts[i])
+        if part is None:
+            source_n, source_s = normals_ref.at[:, i], spectrum_ref.at[i]
+        else:
+            chunk = 4 + lax.rem(place_ref[0] + shifts[i], 4)
+            source_n, source_s = normals_ref.at[:, chunk, part], spectrum_ref.at[chunk, part]
         return (
-            pltpu.make_async_copy(normals_ref.at[:, chunk], held_n.at[i], semaphores.at[i, 0]),
-            pltpu.make_async_copy(spectrum_ref.at[chunk], held_s.at[i], semaphores.at[i, 1]),
+            pltpu.make_async_copy(source_n, held_n.at[i], semaphores.at[i, 0]),
+            pltpu.make_async_copy(source_s, held_s.at[i], semaphores.at[i, 1]),
         )
 
     def put(i):
-        target = out_refs[i] if rotated else out_refs[0].at[shifts[i]]
+        target = out_refs[0].at[i] if part is None else out_refs[i]
         return pltpu.make_async_copy(held_out.at[i], target, semaphores.at[i, 2])
 
     steps = range(len(shifts))
@@ -124,13 +128,14 @@
         put(i).wait()
 
 
-def scale(half, shifts, rotated, place, normals, spectrum):
-    chunk = (2, 8, 128, 128)
+def scale(part, shifts, place, normals, spectrum):
     count = len(shifts)
-    shapes = [chunk] * count if rotated else [(count,) + chunk]
+    chunk = (2, 8 if part is None else 4, 128, 128)
+    shapes = [(count,) + chunk] if part is None else [chunk] * count
+    view = (8, 8, 128, 128) if part is None else (8, 2, 4, 128, 128)
     hbm = pl.BlockSpec(memory_space=pltpu.HBM)
     return pl.pallas_call(
-        functools.partial(scale_kernel, half, shifts, rotated),
+        functools.partial(scale_kernel, part, shifts),
         in_specs=[pl.BlockSpec(memory_space=pltpu.SMEM)] + [hbm] * 2,
         out_specs=[hbm] * len(shapes),
         out_shape=[pltpu.HBM(shape, jnp.float32) for shape in shapes],
@@ -142,8 +147,8 @@
         ],
         compiler_params=params(VMEM),
         cost_estimate=cost(count << 18, 2 * count * MIB),
-        name="scale_b" if rotated else "scale_a",
-    )(place, *in_hbm(normals.reshape(2, 8, 8, 128, 128), spectrum.reshape(8, 8, 128, 128)))
+        name="scale_a" if part is None else "scale_b",
+    )(place, *in_hbm(normals.reshape((2,) + view), spectrum.reshape(view)))
 
 
 def transform(along_z, pairs, table_ref):
@@ -166,72 +171,115 @@
     return parts
 
 
-def first_kernel(along_z, shifts, dynamic, place_ref, to_ref, *refs):
-    in_refs, refs = (refs[:4], refs[4:]) if dynamic else (refs[:1], refs[1:])
-    table_ref, *out_refs, pieces, held_out, semaphores = refs
-
-    def gets(i):
+def first_z_kernel(shifts, to_ref, in_ref, table_ref, *refs):
+    *out_refs, pieces, held_out, semaphores = refs
+
+    def get(i):
         cells = pl.ds(2 * lax.rem(to_ref[0] + shifts[i], 4), 2)
-        if not dynamic:
-            source = in_refs[0].at[:, :, cells]
-            return [pltpu.make_async_copy(source, pieces.at[i], semaphores.at[i, 0])]
-        return [
-            pltpu.make_async_copy(ref.at[:, cells], pieces.at[i, s], semaphores.at[i, s])
-            for s, ref in enumerate(in_refs)
-        ]
+        return pltpu.make_async_copy(in_ref.at[:, :, cells], pieces.at[i], semaphores.at[i, 0])
 
     def put(i):
-        return pltpu.make_async_copy(held_out.at[i], out_refs[i], semaphores.at[i, 4])
+        return pltpu.make_async_copy(held_out.at[i], out_refs[i], semaphores.at[i, 1])
 
     steps = range(len(shifts))
     for i in steps:
-        for copy in gets(i):
-            copy.start()
-    for i in steps:
-        for copy in gets(i):
-            copy.wait()
-        if dynamic:
-            g, h = place_ref[0], lax.rem(place_ref[0] + 3, 4)
-        else:
-            g, h = 0, 1
-        pairs = [(pieces[i, 0], pieces[i, 2], g), (pieces[i, 1], pieces[i, 3], h)]
-        for odd, values in enumerate(transform(along_z, pairs, table_ref)):
+        get(i).start()
+    for i in steps:
+        get(i).wait()
+        pairs = [(pieces[i, 0], pieces[i, 2], 0), (pieces[i, 1], pieces[i, 3], 1)]
+        for odd, values in enumerate(transform(True, pairs, table_ref)):
             half = slice(odd * 128, (odd + 1) * 128)
             for plane in range(2):
                 part = slice(plane * 128, (plane + 1) * 128)
                 for x in range(2):
-                    cell = slice(x * 128, (x + 1) * 128)
-                    if along_z:
-                        held_out[i, plane, x, :, half] = values[cell, part]
-                    else:
-                        held_out[i, plane, x, half] = values[part, cell]
+                    held_out[i, plane, x, :, half] = values[x * 128 : (x + 1) * 128, part]
         put(i).start()
     for i in steps:
         put(i).wait()
 
 
-def first(along_z, shifts, place, to, arrived, table):
-    dynamic = isinstance(arrived, list)
-    operands = arrived if dynamic else [arrived]
-    shape = (2, 2, 128, KEPT) if along_z else (2, 2, KEPT, 128)
+def first_z(shifts, to, arrived, table):
+    shape = (2, 2, 128, KEPT)
     hbm = pl.BlockSpec(memory_space=pltpu.HBM)
     count = len(shifts)
     return pl.pallas_call(
-        functools.partial(first_kernel, along_z, shifts, dynamic),
-        in_specs=[pl.BlockSpec(memory_space=pltpu.SMEM)] * 2
-        + [hbm] * len(operands)
-        + [pl.BlockSpec(memory_space=pltpu.VMEM)],
+        functools.partial(first_z_kernel, shifts),
+        in_specs=[
+            pl.BlockSpec(memory_space=pltpu.SMEM),
+            hbm,
+            pl.BlockSpec(memory_space=pltpu.VMEM),
+        ],
         out_specs=[hbm] * count,
         out_shape=[pltpu.HBM(shape, jnp.float32)] * count,
         scratch_shapes=[
             pltpu.VMEM((count, 4, 2, 2, 128, 128), jnp.float32),
             pltpu.VMEM((count,) + shape, jnp.float32),
-            pltpu.SemaphoreType.DMA((count, 5)),
+            pltpu.SemaphoreType.DMA((count, 2)),
         ],
         compiler_params=params(VMEM),
         cost_estimate=cost(count * 256 * 512 * 512, 2 * count * MIB),
-        name="first_z" if along_z else "first_y",
-    )(place, to, *in_hbm(*operands), table)
+        name="first_z",
+    )(to, *in_hbm(arrived), table)
+
+
+def first_y_kernel(merge, place_ref, to_ref, *refs):
+    in_refs, refs = refs[:4], refs[4:]
+    before, refs = (refs[:2], refs[2:]) if merge else ((), refs)
+    table_ref, *out_refs, pieces, held_out, semaphores = refs
+    gets = [
+        pltpu.make_async_copy(ref, pieces.at[s], semaphores.at[0, s])
+        for s, ref in enumerate(in_refs)
+    ]
+    puts = []
+    for i, shift in enumerate((1, 3, 2, 0)):
+        whole = merge and i >= 2
+        source = held_out.at[lax.rem(to_ref[0] + shift, 4)]
+        target = out_refs[i].at[:, 1 if whole else 0]
+        puts.append(pltpu.make_async_copy(source, target, semaphores.at[1, i]))
+    moves = [
+        pltpu.make_async_copy(ref.at[:, 0], out_refs[2 + i].at[:, 0], semaphores.at[2, i])
+        for i, ref in enumerate(before)
+    ]
+    for copy in gets + moves:
+        copy.start()
+    for copy in gets:
+        copy.wait()
+    g, h = place_ref[0], lax.rem(place_ref[0] + 3, 4)
+    pairs = [(pieces[0], pieces[2], g), (pieces[1], pieces[3], h)]
+    for odd, values in enumerate(transform(False, pairs, table_ref)):
+        for plane in range(2):
+            for x in range(4):
+                held_out[x, plane, odd * 128 : (odd + 1) * 128] = values[
+                    plane * 128 : (plane + 1) * 128, x * 128 : (x + 1) * 128
+                ]
+    for copy in puts:
+        copy.start()
+    for copy in puts + moves:
+        copy.wait()
+
+
+def first_y(place, to, pieces, table, before=()):
+    merge = bool(before)
+    shape = (2, 1, KEPT, 128)
+    whole = (2, 2, KEPT, 128) if merge else shape
+    hbm = pl.BlockSpec(memory_space=pltpu.HBM)
+    operands = in_hbm(*pieces, *before)
+    return pl.pallas_call(
+        functools.partial(first_y_kernel, merge),
+        in_specs=[pl.BlockSpec(memory_space=pltpu.SMEM)] * 2
+        + [hbm] * len(operands)
+        + [pl.BlockSpec(memory_space=pltpu.VMEM)],
+        out_specs=[hbm] * 4,
+        out_shape=[pltpu.HBM(shape, jnp.float32)] * 2 + [pltpu.HBM(whole, jnp.float32)] * 2,
+        scratch_shapes=[
+            pltpu.VMEM((4, 2, 4, 128, 128), jnp.float32),
+            pltpu.VMEM((4, 2, KEPT, 128), jnp.float32),
+            pltpu.SemaphoreType.DMA((3, 4)),
+        ],
+        compiler_params=params(VMEM),
+        cost_estimate=cost(512 * 512 * 512, 4 * MIB),
+        name="first_y",
+    )(place, to, *operands, table)
 
 
 def part_y_kernel(place_ref, p1, p3, table_ref, out_ref):
@@ -257,31 +305,30 @@
     )(place, *pieces, table)
 
 
-def part_z_kernel(place_ref, p0, p2, table_ref, out_ref):
-    pairs = [(p0[...], p2[...], place_ref[0])]
-    for odd, values in enumerate(transform(True, pairs, table_ref)):
-        out_ref[0, :, odd * 256 : (odd + 1) * 256] = values
-
-
-def part_z(place, pieces, table):
-    return pl.pallas_call(
-        part_z_kernel,
-        grid_spec=pltpu.PrefetchScalarGridSpec(
-            num_scalar_prefetch=1,
-            grid=(2,),
-            in_specs=[pl.BlockSpec((2, 1, KEPT, 128), lambda i, place: (0, i, 0, 0))] * 2
-            + [pl.BlockSpec(table.shape, lambda i, place: (0, 0, 0, 0, 0))],
-            out_specs=pl.BlockSpec((1, KEPT, 512), lambda i, place: (i, 0, 0)),
-        ),
+def second_z_kernel(place_ref, b0, b2, c1, c3, d1, d3, table_ref, out_ref):
+    g, h = place_ref[0], lax.rem(place_ref[0] + 3, 4)
+    for x, (p1, p3) in enumerate(((c1, c3), (d1, d3))):
+        cell = slice(x, x + 1)
+        pairs = [(b0[:, cell], b2[:, cell], g), (p1[...], p3[...], h)]
+        for odd, values in enumerate(transform(True, pairs, table_ref)):
+            out_ref[x, :, odd * 256 : (odd + 1) * 256] = values
+
+
+def second_z(place, pieces, table):
+    vmem = pl.BlockSpec(memory_space=pltpu.VMEM)
+    return pl.pallas_call(
+        second_z_kernel,
+        in_specs=[pl.BlockSpec(memory_space=pltpu.SMEM)] + [vmem] * 7,
+        out_specs=vmem,
         out_shape=jax.ShapeDtypeStruct((2, KEPT, 512), jnp.float32),
         compiler_params=params(VMEM),
-        cost_estimate=cost(512 * 512 * 256, 4 * MIB),
-        name="part_z",
+        cost_estimate=cost(512 * 512 * 512, 4 * MIB),
+        name="second_z",
     )(place, *pieces, table)
 
 
 def second_kernel(
-    y_ref, z_ref, part_a, a0, a2, table_y_ref, part_b, b1, b3, table_z_ref, out_ref, held
+    y_ref, part_a, a0, a2, table_y_ref, done_b, out_ref, held
 ):
     odd = pl.program_id(0)
 
@@ -302,9 +349,8 @@
                     half,
                     plane * 4 + x,
                 )
-    parts = transform(True, [(b1[...], b3[...], lax.rem(z_ref[0] + 3, 4))], table_z_ref)
-    for half, values in enumerate(parts):
-        values = values + part_b[:, :, half * 256 : (half + 1) * 256].reshape(256, 256)
+    for half in range(2):
+        values = done_b[:, :, half * 256 : (half + 1) * 256].reshape(256, 256)
         for x in range(2):
             for plane in range(2):
                 put(
@@ -315,28 +361,26 @@
     out_ref[...] = held[...].reshape(128, 1, 2, 8, 128)
 
 
-def second(gy, gz, part_a, pieces_a, table_y, part_b, pieces_b, table_z):
+def second(gy, part_a, pieces_a, table_y, done_b):
     return pl.pallas_call(
         second_kernel,
         grid_spec=pltpu.PrefetchScalarGridSpec(
-            num_scalar_prefetch=2,
+            num_scalar_prefetch=1,
             grid=(2,),
-            in_specs=[pl.BlockSpec((1, KEPT, 512), lambda i, gy, gz: (i, 0, 0))]
-            + [pl.BlockSpec((2, 2, 128, KEPT), lambda i, gy, gz: (0, 0, 0, 0))] * 2
+            in_specs=[pl.BlockSpec((1, KEPT, 512), lambda i, gy: (i, 0, 0))]
+            + [pl.BlockSpec((2, 2, 128, KEPT), lambda i, gy: (0, 0, 0, 0))] * 2
             + [
-                pl.BlockSpec((2, 2, 1, KEPT, KEPT), lambda i, gy, gz: (0, 0, i, 0, 0)),
-                pl.BlockSpec((2, 128, 512), lambda i, gy, gz: (0, i, 0)),
-            ]
-            + [pl.BlockSpec((2, 2, 128, 128), lambda i, gy, gz: (0, 0, i, 0))] * 2
-            + [pl.BlockSpec(table_z.shape, lambda i, gy, gz: (0, 0, 0, 0, 0))],
-            out_specs=pl.BlockSpec((128, 1, 2, 8, 128), lambda i, gy, gz: (0, i, 0, 0, 0)),
+                pl.BlockSpec((2, 2, 1, KEPT, KEPT), lambda i, gy: (0, 0, i, 0, 0)),
+                pl.BlockSpec((2, 128, 512), lambda i, gy: (0, i, 0)),
+            ],
+            out_specs=pl.BlockSpec((128, 1, 2, 8, 128), lambda i, gy: (0, i, 0, 0, 0)),
             scratch_shapes=[pltpu.VMEM((2048, 128), jnp.float32)],
         ),
         out_shape=jax.ShapeDtypeStruct((128, 2, 2, 8, 128), jnp.float32),
         compiler_params=params(VMEM),
-        cost_estimate=cost(512 * 512 * 512, 8 * MIB),
+        cost_estimate=cost(512 * 512 * 256, 8 * MIB),
         name="second",
-    )(gy, gz, part_a, *pieces_a, table_y, part_b, *pieces_b, table_z)
+    )(gy, part_a, *pieces_a, table_y, done_b)
 
 
 def third_kernel(slot_ref, in_ref, table_ref, ordering_ref, out_ref, held):
@@ -407,30 +451,31 @@
     gy = lax.axis_index("gy").astype(jnp.int32).reshape(1)
     gz = lax.axis_index("gz").astype(jnp.int32).reshape(1)
 
-    (a,) = scale(0, (0, 1, 2, 3), False, gz, normals, spectrum)
+    (a,) = scale(None, (0, 1, 2, 3), gz, normals, spectrum)
     a, place = lax.optimization_barrier((a, gy))
     a = lax.all_to_all(a, "gz", split_axis=0, concat_axis=0, tiled=True)
-    b1, b3, b2 = scale(1, (1, 3, 2), True, place, normals, spectrum)
-    place, b1, b3, b2 = lax.optimization_barrier((place, b1, b3, b2))
-    b1, b3, b2 = shifted(b1, "gy", 1), shifted(b3, "gy", 3), shifted(b2, "gy", 2)
-    (b0,) = scale(1, (0,), True, place, normals, spectrum)
-
-    a, slots, b0 = lax.optimization_barrier((a, slots_of(block_owner), b0))
-    a1, a3, a2, a0 = first(True, (1, 3, 2, 0), gz, gy, a, table_z)
-    b1, b2, b3, _ = lax.optimization_barrier((b1, b2, b3, a1))
-    pieces = [b0, b1, b2, b3]
-    a1, a3 = shifted(a1, "gy", 1), shifted(a3, "gy", 3)
-    b2, b1 = first(False, (2, 1), gy, gz, pieces, table_y)
-    a2, b2, b1 = lax.optimization_barrier((a2, b2, b1))
-    b2, b1, a2 = shifted(b2, "gz", 2), shifted(b1, "gz", 1), shifted(a2, "gy", 2)
-    b3, b0 = first(False, (3, 0), gy, gz, pieces, table_y)
-    b3 = shifted(b3, "gz", 3)
+    c1, c3, c2 = scale(0, (1, 3, 2), place, normals, spectrum)
+    place, c1, c3, c2 = lax.optimization_barrier((place, c1, c3, c2))
+    c1, c3, c2 = shifted(c1, "gy", 1), shifted(c3, "gy", 3), shifted(c2, "gy", 2)
+    d1, d3, d2 = scale(1, (1, 3, 2), place, normals, spectrum)
+    place, d1, d3, d2 = lax.optimization_barrier((place, d1, d3, d2))
+    d1, d3, d2 = shifted(d1, "gy", 1), shifted(d3, "gy", 3), shifted(d2, "gy", 2)
+    (c0,) = scale(0, (0,), place, normals, spectrum)
+    (d0,) = scale(1, (0,), place, normals, spectrum)
+
+    c1, c3, c2, c0 = first_y(gy, gz, (c0, c1, c2, c3), table_y)
+    a, slots, _, d0 = lax.optimization_barrier((a, slots_of(block_owner), c1, d0))
+    c1, c3 = shifted(c1, "gz", 1), shifted(c3, "gz", 3)
+    a1, a3, a2, a0 = first_z((1, 3, 2, 0), gy, a, table_z)
+    d1, d2, d3, _ = lax.optimization_barrier((d1, d2, d3, a1))
+    a1, a3, a2 = shifted(a1, "gy", 1), shifted(a3, "gy", 3), shifted(a2, "gy", 2)
+    d1, d3, b2, b0 = first_y(gy, gz, (d0, d1, d2, d3), table_y, (c2, c0))
+    d1, d3, b2 = shifted(d1, "gz", 1), shifted(d3, "gz", 3), shifted(b2, "gz", 2)
 
     part_a = part_y(gy, (a1, a3), table_y)
-    part_a, b2 = lax.optimization_barrier((part_a, b2))
-    part_b = part_z(gz, (b0, b2), table_z)
-    part_b, a2, b1, b3 = lax.optimization_barrier((part_b, a2, b1, b3))
-    planes = second(gy, gz, part_a, (a0, a2), table_y, part_b, (b1, b3), table_z)
+    done_b = second_z(gz, (b0, b2, c1, c3, d1, d3), table_z)
+    part_a, done_b, a2 = lax.optimization_barrier((part_a, done_b, a2))
+    planes = second(gy, part_a, (a0, a2), table_y, done_b)
     lines = lax.all_to_all(planes, ALL, split_axis=0, concat_axis=0, tiled=True)
     outgoing = third(slots, lines, table_x, ordering)
     return lax.all_to_all(

time: 177 us -> 190 us (1.073)
  Pallas kernels: 27.7 us -> 44.5 us
  waiting for transfers between devices: 54 us -> 46.8 us
  starting transfers between devices: 18.8 us -> 23.6 us
    all_to_all x1, waiting for transfers between devices: 37.5 us -> 15.5 us  [per_device(): a = lax.all_to_all(a, 'gz', split_axis=0, concat_axis=0, tiled=True)]
    pallas_call x7 -> x9, Pallas kernels: 20.9 us -> 38.3 us  [the longest x2 20.8 us: first_y(): pl.pallas_call(functools.partial(first_y_kernel, merge), in_specs=[pl.Blo...]
    ppermute x9 -> x14, waiting for transfers between devices: 16.5 us -> 31.2 us  [shifted(): lax.ppermute(piece, axis, [(i, (i + shift) % size) for i in range(size)])]
    ppermute x9 -> x14, starting transfers between devices: 13 us -> 17.7 us  [shifted(): lax.ppermute(piece, axis, [(i, (i + shift) % size) for i in range(size)])]
  transfers between devices with their start and end apart: 10 -> 15, of which waited for: 5 -> 6; matrix products, arithmetic and copies ran while one was open for 0% -> 0% of each run, Pallas kernels for 10% -> 19%
where the time goes in v16:
time: 190 us
  blocking collectives  71.5 us (38%)
  waiting for transfers between devices  46.8 us (25%)
  Pallas kernels  44.5 us (23%)
  starting transfers between devices  23.6 us (12%)
  local copies, waits for them, and re-layouts  2.44 us (1%)
    all_to_all x1, blocking collectives, per_device(): lines = lax.all_to_all(planes, ALL, split_axis=0, concat_axis=0, tiled=True)  37.3 us
    all_to_all x1, blocking collectives, per_device(): lax.all_to_all(outgoing.reshape(128, 1, CAP, 2, BW), ALL, split_axis=0, c...  34.2 us
    ppermute x14, waiting for transfers between devices, shifted(): lax.ppermute(piece, axis, [(i, (i + shift) % size) for i in range(size)])  31.2 us
    pallas_call x2, Pallas kernels, first_y(): pl.pallas_call(functools.partial(first_y_kernel, merge), in_specs=[pl.Blo...  20.8 us
    ppermute x14, starting transfers between devices, shifted(): lax.ppermute(piece, axis, [(i, (i + shift) % size) for i in range(size)])  17.7 us
    all_to_all x1, waiting for transfers between devices, per_device(): a = lax.all_to_all(a, 'gz', split_axis=0, concat_axis=0, tiled=True)  15.5 us
    pallas_call x5, Pallas kernels, scale(): pl.pallas_call(functools.partial(scale_kernel, part, shifts), in_specs=[p...  11.9 us
    all_to_all x1, starting transfers between devices, per_device(): a = lax.all_to_all(a, 'gz', split_axis=0, concat_axis=0, tiled=True)  5.87 us
  transfers between devices with their start and end apart: 15, of which 6 were waited for; matrix products, arithmetic and copies ran while one was open for 0% of the time, Pallas kernels for 19%

profile of v16, /device:TPU:1, one launch (start us, length us, event | category | flops | bytes accessed | tf_op | source)
XLA Modules:
  0.0 189.8 jit_solution(8594342778356161756)
XLA Ops:
  0.0 3.4 %scale_a.1 = f32[4,2,8,128,128]{4,3,2,1,0:T(8,128)} custom-call(s32[1]{0:T(128)} %bitcast.place_ref.to_ref, bf16[2,8,8,128,128]{4,3,2,1,0:T(8,128)(2,1)} %bitcast.23, f32[8,8,128,128]{3,2,1,0:T(8,128)} %bitcast.28), custom_call_target="tpu_custom_call" | custom-call | flops 16 | bytes 128 | tf_op jit(solution)/shard_map/scale_a/pallas_call | solution.py:137
  3.4 5.9 %all-to-all-start = ((f32[4,2,8,128,128]{4,3,2,1,0:T(8,128)}), f32[4,2,8,128,128]{4,3,2,1,0:T(8,128)}, u32[]{:S(2)}, u32[]{:S(2)}) async-start(f32[4,2,8,128,128]{4,3,2,1,0:T(8,128)} %scale_a.1), calls=%async_computation | async-start | bytes 8388608 | tf_op jit(solution)/shard_map/all_to_all | solution.py:456
  9.3 2.3 %scale_b.4 = (f32[2,4,128,128]{3,2,1,0:T(8,128)}, f32[2,4,128,128]{3,2,1,0:T(8,128)}, f32[2,4,128,128]{3,2,1,0:T(8,128)}) custom-call(s32[1]{0:T(128)} %bitcast.3.place_ref.to_ref.y_ref, bf16[2,8,2,4,128,128]{5,4,3,2,1,0:T(8,128)(2,1)} %bitcast.24, f32[8,2,4,128,128]{4,3,2,1,0:T(8,128)} %bitcast.29), custom_call_target="tpu_custom_call" | custom-call | flops 12 | bytes 96 | tf_op jit(solution)/shard_map/scale_b/pallas_call | solution.py:137
  11.6 0.0 copy-start.9
  11.6 1.4 collective-permute-start
  12.9 2.6 %collective-permute-start.1 = (f32[2,4,128,128]{3,2,1,0:T(8,128)}, f32[2,4,128,128]{3,2,1,0:T(8,128)}, u32[]{:S(2)}, u32[]{:S(2)}) collective-permute-start(f32[2,4,128,128]{3,2,1,0:T(8,128)} %get-tuple-element.53), channel_id=1, source_target_pairs={{0,8},{4,12},{8,0},{12,4},{1,9},{5,13},{9,1},{13,5},{2,10},{6,14},... | collective-permute-start | bytes 1572872 | tf_op jit(solution)/shard_map/ppermute | solution.py:439
  15.6 1.1 collective-permute-start.2
  16.6 2.3 %scale_b.5 = (f32[2,4,128,128]{3,2,1,0:T(8,128)}, f32[2,4,128,128]{3,2,1,0:T(8,128)}, f32[2,4,128,128]{3,2,1,0:T(8,128)}) custom-call(s32[1]{0:T(128)} %bitcast.3.place_ref.to_ref.y_ref, bf16[2,8,2,4,128,128]{5,4,3,2,1,0:T(8,128)(2,1)} %bitcast.25, f32[8,2,4,128,128]{4,3,2,1,0:T(8,128)} %bitcast.30), custom_call_target="tpu_custom_call" | custom-call | flops 12 | bytes 96 | tf_op jit(solution)/shard_map/scale_b/pallas_call | solution.py:137
  18.9 0.5 collective-permute-start.5
  19.4 0.8 collective-permute-start.6
  20.2 0.1 copy.11
  20.3 0.2 fusion.2
  20.6 0.1 copy.12
  20.7 5.1 %collective-permute-done.refs_1_ = f32[2,4,128,128]{3,2,1,0:T(8,128)S(1)} collective-permute-done((f32[2,4,128,128]{3,2,1,0:T(8,128)}, f32[2,4,128,128]{3,2,1,0:T(8,128)S(1)}, u32[]{:S(2)}, u32[]{:S(2)}) %collective-permute-start) | collective-permute-done | bytes 524320 | tf_op jit(solution)/shard_map/ppermute | solution.py:439
  25.8 1.4 collective-permute-start.7
  27.2 0.4 fusion.1
  27.6 2.0 %scale_b.7.refs_0_ = f32[2,4,128,128]{3,2,1,0:T(8,128)} custom-call(s32[1]{0:T(128)} %bitcast.3.place_ref.to_ref.y_ref, bf16[2,8,2,4,128,128]{5,4,3,2,1,0:T(8,128)(2,1)} %bitcast.26, f32[8,2,4,128,128]{4,3,2,1,0:T(8,128)} %bitcast.31), custom_call_target="tpu_custom_call" | custom-call | flops 4 | bytes 32 | tf_op jit(solution)/shard_map/scale_b/pallas_call | solution.py:137
  29.5 0.0 copy-start
  29.5 2.0 %scale_b.6.refs_0_ = f32[2,4,128,128]{3,2,1,0:T(8,128)} custom-call(s32[1]{0:T(128)} %bitcast.3.place_ref.to_ref.y_ref, bf16[2,8,2,4,128,128]{5,4,3,2,1,0:T(8,128)(2,1)} %bitcast.27, f32[8,2,4,128,128]{4,3,2,1,0:T(8,128)} %bitcast.32), custom_call_target="tpu_custom_call" | custom-call | flops 4 | bytes 32 | tf_op jit(solution)/shard_map/scale_b/pallas_call | solution.py:137
  31.5 0.0 copy-start.1
  31.5 6.6 %collective-permute-done.1.refs_2_ = f32[2,4,128,128]{3,2,1,0:T(8,128)} collective-permute-done((f32[2,4,128,128]{3,2,1,0:T(8,128)}, f32[2,4,128,128]{3,2,1,0:T(8,128)}, u32[]{:S(2)}, u32[]{:S(2)}) %collective-permute-start.1) | collective-permute-done | bytes 524320 | tf_op jit(solution)/shard_map/ppermute | solution.py:439
  38.2 0.8 collective-permute-done.2.refs_3_
  38.9 3.7 %first_y.2 = (f32[2,1,256,128]{3,2,1,0:T(8,128)}, f32[2,1,256,128]{3,2,1,0:T(8,128)}, f32[2,1,256,128]{3,2,1,0:T(8,128)}, f32[2,1,256,128]{3,2,1,0:T(8,128)}) custom-call(s32[1]{0:T(128)} %bitcast.3.place_ref.to_ref.y_ref, s32[1]{0:T(128)} %bitcast.place_ref.to_ref, f32[2,4,128,128]{3,2,1,0:T(8,128)} %scale_b.6.refs_0_, f32[2,4,128,128]{3,2,1,0:T(8,128)} %copy-done.8, ...), custom_call_target="tpu_custom_call" | custom-call | flops 2048 | bytes 64 | tf_op jit(solution)/shard_map/first_y/pallas_call | solution.py:267
  42.7 15.5 %all-to-all-done.in_ref = f32[4,2,8,128,128]{4,3,2,1,0:T(8,128)} async-done(((f32[4,2,8,128,128]{4,3,2,1,0:T(8,128)}), f32[4,2,8,128,128]{4,3,2,1,0:T(8,128)}, u32[]{:S(2)}, u32[]{:S(2)}) %all-to-all-start) | async-done | bytes 4194336 | tf_op jit(solution)/shard_map/all_to_all | solution.py:456
  58.2 4.5 %first_z.1 = (f32[2,2,128,256]{3,2,1,0:T(8,128)}, f32[2,2,128,256]{3,2,1,0:T(8,128)}, f32[2,2,128,256]{3,2,1,0:T(8,128)}, f32[2,2,128,256]{3,2,1,0:T(8,128)}) custom-call(s32[1]{0:T(128)} %bitcast.3.place_ref.to_ref.y_ref, f32[4,2,8,128,128]{4,3,2,1,0:T(8,128)} %all-to-all-done.in_ref, bf16[2,2,2,256,256]{4,3,2,1,0:T(8,128)(2,1)S(1)} %copy-done.1), custom_call_target="tpu_custom_call" | custom-call | flops 4096 | bytes 128 | tf_op jit(solution)/shard_map/first_z/pallas_call | solution.py:205
  62.8 2.8 %collective-permute-start.4 = (f32[2,2,128,256]{3,2,1,0:T(8,128)}, f32[2,2,128,256]{3,2,1,0:T(8,128)S(1)}, u32[]{:S(2)}, u32[]{:S(2)}) collective-permute-start(f32[2,2,128,256]{3,2,1,0:T(8,128)} %get-tuple-element.59), channel_id=1, source_target_pairs={{0,12},{4,0},{8,4},{12,8},{1,13},{5,1},{9,5},{13,9},{2,14},{6,2},{... | collective-permute-start | bytes 1572872 | tf_op jit(solution)/shard_map/ppermute | solution.py:439
  65.6 0.1 collective-permute-start.10
  65.7 0.0 collective-permute-done.6.refs_2_
  65.7 0.0 collective-permute-done.7.refs_3_
  65.7 0.7 copy-done.6
  66.4 0.2 copy-done.7
  66.6 17.1 %first_y.3 = (f32[2,1,256,128]{3,2,1,0:T(8,128)}, f32[2,1,256,128]{3,2,1,0:T(8,128)}, f32[2,2,256,128]{3,2,1,0:T(8,128)}, f32[2,2,256,128]{3,2,1,0:T(8,128)}) custom-call(s32[1]{0:T(128)} %bitcast.3.place_ref.to_ref.y_ref, s32[1]{0:T(128)} %bitcast.place_ref.to_ref, f32[2,4,128,128]{3,2,1,0:T(8,128)} %scale_b.7.refs_0_, f32[2,4,128,128]{3,2,1,0:T(8,128)} %copy-done.6, ...), custom_call_target="tpu_custom_call" | custom-call | flops 2048 | bytes 64 | tf_op jit(solution)/shard_map/first_y/pallas_call | solution.py:267
  83.7 2.6 %collective-permute-start.8 = (f32[2,2,256,128]{3,2,1,0:T(8,128)}, f32[2,2,256,128]{3,2,1,0:T(8,128)S(1)}, u32[]{:S(2)}, u32[]{:S(2)}) collective-permute-start(f32[2,2,256,128]{3,2,1,0:T(8,128)} %get-tuple-element.70), channel_id=1, source_target_pairs={{0,2},{1,3},{2,0},{3,1},{4,6},{5,7},{6,4},{7,5},{8,10},{9,11},{10,... | collective-permute-start | bytes 1572872 | tf_op jit(solution)/shard_map/ppermute | solution.py:439
  86.3 1.6 collective-permute-start.13
  87.9 0.0 collective-permute-done.10.c3
  88.0 0.1 collective-permute-start.11
  88.1 2.8 %collective-permute-start.12 = (f32[2,1,256,128]{3,2,1,0:T(8,128)}, f32[2,1,256,128]{3,2,1,0:T(8,128)S(1)}, u32[]{:S(2)}, u32[]{:S(2)}) collective-permute-start(f32[2,1,256,128]{3,2,1,0:T(8,128)} %get-tuple-element.73), channel_id=1, source_target_pairs={{0,3},{1,0},{2,1},{3,2},{4,7},{5,4},{6,5},{7,6},{8,11},{9,8},{10,9... | collective-permute-start | bytes 786440 | tf_op jit(solution)/shard_map/ppermute | solution.py:439
  90.9 0.9 part_y.1.part_a
  91.8 13.1 %collective-permute-done.9.c1 = f32[2,1,256,128]{3,2,1,0:T(8,128)S(1)} collective-permute-done((f32[2,1,256,128]{3,2,1,0:T(8,128)S(1)}, f32[2,1,256,128]{3,2,1,0:T(8,128)S(1)}, u32[]{:S(2)}, u32[]{:S(2)}) %collective-permute-start.9) | collective-permute-done | bytes 262176 | tf_op jit(solution)/shard_map/ppermute | solution.py:439
  105.0 5.6 %collective-permute-done.11.d1 = f32[2,1,256,128]{3,2,1,0:T(8,128)S(1)} collective-permute-done((f32[2,1,256,128]{3,2,1,0:T(8,128)}, f32[2,1,256,128]{3,2,1,0:T(8,128)S(1)}, u32[]{:S(2)}, u32[]{:S(2)}) %collective-permute-start.11) | collective-permute-done | bytes 262176 | tf_op jit(solution)/shard_map/ppermute | solution.py:439
  110.6 1.0 second_z.1.done_b
  111.7 1.5 second.1
  113.2 0.0 copy-start.2
  113.2 0.0 copy-start.5
  113.2 37.3 %all_to_all.22.in_ref = f32[128,2,2,8,128]{4,3,2,1,0:T(8,128)S(1)} all-to-all(f32[128,2,2,8,128]{4,3,2,1,0:T(8,128)S(1)} %second.1), channel_id=1, replica_groups=mesh['gx'=8,'gy'=4,'gz'=4] {'gx','gy','gz'}, dimensions={0} | all-to-all | bytes 4194304 | tf_op jit(solution)/shard_map/all_to_all | solution.py:479
  150.5 3.7 %third.1 = f32[4096,128]{1,0:T(8,128)S(1)} custom-call(s32[1024]{0:T(1024)S(1)} %multiply_add_fusion.slot_ref, f32[128,2,2,8,128]{4,3,2,1,0:T(8,128)S(1)} %all_to_all.22.in_ref, bf16[2,2,256,512]{3,2,1,0:T(8,128)(2,1)S(1)} %copy-done.2, bf16[256,256]{1,0:T(8,128)(2,1)S(1)} %copy-done.5), custom_call_target="tpu_custom_call" | custom-call | flops 3072 | bytes 96 | tf_op jit(solution)/shard_map/third/pallas_call | solution.py:425
  154.2 34.2 %all_to_all.23 = f32[128,1,16,2,128]{4,3,2,1,0:T(2,128)S(1)} all-to-all(f32[128,1,16,2,128]{4,3,2,1,0:T(2,128)S(1)} %bitcast.22), channel_id=1, replica_groups=mesh['gx'=8,'gy'=4,'gz'=4] {'gx','gy','gz'}, dimensions={0} | all-to-all | bytes 4194304 | tf_op jit(solution)/shard_map/all_to_all | solution.py:481
  188.4 1.3 copy.15
  (32 shorter events, 0.1 us)
Async XLA Ops:
  3.4 54.8 %all-to-all-start = ((f32[4,2,8,128,128]{4,3,2,1,0:T(8,128)}), f32[4,2,8,128,128]{4,3,2,1,0:T(8,128)}, u32[]{:S(2)}, u32[]{:S(2)}) async-start(f32[4,2,8,128,128]{4,3,2,1,0:T(8,128)} %scale_a.1), calls=%async_computation | async-start | bytes 8388608 | tf_op jit(solution)/shard_map/all_to_all | solution.py:456
  11.6 8.6 %copy-start.9 = (s32[1024,1]{0,1:T(1,128)S(1)}, s32[1024,1]{0,1:T(1,128)}, u32[]{:S(2)}) copy-start(s32[1024,1]{0,1:T(1,128)} %param.9) | copy-start | bytes 12292
  11.6 14.2 %collective-permute-start = (f32[2,4,128,128]{3,2,1,0:T(8,128)}, f32[2,4,128,128]{3,2,1,0:T(8,128)S(1)}, u32[]{:S(2)}, u32[]{:S(2)}) collective-permute-start(f32[2,4,128,128]{3,2,1,0:T(8,128)} %get-tuple-element.52), channel_id=1, source_target_pairs={{0,4},{4,8},{8,12},{12,0},{1,5},{5,9},{9,13},{13,1},{2,6},{6,10},{... | collective-permute-start | bytes 1572872 | tf_op jit(solution)/shard_map/ppermute | solution.py:439
  12.9 25.2 %collective-permute-start.1 = (f32[2,4,128,128]{3,2,1,0:T(8,128)}, f32[2,4,128,128]{3,2,1,0:T(8,128)}, u32[]{:S(2)}, u32[]{:S(2)}) collective-permute-start(f32[2,4,128,128]{3,2,1,0:T(8,128)} %get-tuple-element.53), channel_id=1, source_target_pairs={{0,8},{4,12},{8,0},{12,4},{1,9},{5,13},{9,1},{13,5},{2,10},{6,14},... | collective-permute-start | bytes 1572872 | tf_op jit(solution)/shard_map/ppermute | solution.py:439
  15.6 23.4 %collective-permute-start.2 = (f32[2,4,128,128]{3,2,1,0:T(8,128)}, f32[2,4,128,128]{3,2,1,0:T(8,128)}, u32[]{:S(2)}, u32[]{:S(2)}) collective-permute-start(f32[2,4,128,128]{3,2,1,0:T(8,128)} %get-tuple-element.54), channel_id=1, source_target_pairs={{0,12},{4,0},{8,4},{12,8},{1,13},{5,1},{9,5},{13,9},{2,14},{6,2},{... | collective-permute-start | bytes 1572872 | tf_op jit(solution)/shard_map/ppermute | solution.py:439
  18.9 46.7 %collective-permute-start.5 = (f32[2,4,128,128]{3,2,1,0:T(8,128)}, f32[2,4,128,128]{3,2,1,0:T(8,128)S(1)}, u32[]{:S(2)}, u32[]{:S(2)}) collective-permute-start(f32[2,4,128,128]{3,2,1,0:T(8,128)} %get-tuple-element.61), channel_id=1, source_target_pairs={{0,4},{4,8},{8,12},{12,0},{1,5},{5,9},{9,13},{13,1},{2,6},{6,10},{... | collective-permute-start | bytes 1572872 | tf_op jit(solution)/shard_map/ppermute | solution.py:439
  19.4 46.3 %collective-permute-start.6 = (f32[2,4,128,128]{3,2,1,0:T(8,128)}, f32[2,4,128,128]{3,2,1,0:T(8,128)S(1)}, u32[]{:S(2)}, u32[]{:S(2)}) collective-permute-start(f32[2,4,128,128]{3,2,1,0:T(8,128)} %get-tuple-element.62), channel_id=1, source_target_pairs={{0,8},{4,12},{8,0},{12,4},{1,9},{5,13},{9,1},{13,5},{2,10},{6,14},... | collective-permute-start | bytes 1572872 | tf_op jit(solution)/shard_map/ppermute | solution.py:439
  25.8 1.8 copy-start.8
  25.8 40.0 %collective-permute-start.7 = (f32[2,4,128,128]{3,2,1,0:T(8,128)}, f32[2,4,128,128]{3,2,1,0:T(8,128)}, u32[]{:S(2)}, u32[]{:S(2)}) collective-permute-start(f32[2,4,128,128]{3,2,1,0:T(8,128)} %get-tuple-element.63), channel_id=1, source_target_pairs={{0,12},{4,0},{8,4},{12,8},{1,13},{5,1},{9,5},{13,9},{2,14},{6,2},{... | collective-permute-start | bytes 1572872 | tf_op jit(solution)/shard_map/ppermute | solution.py:439
  29.5 9.4 %copy-start = (bf16[2,2,2,256,256]{4,3,2,1,0:T(8,128)(2,1)S(1)}, bf16[2,2,2,256,256]{4,3,2,1,0:T(8,128)(2,1)}, u32[]{:S(2)}) copy-start(bf16[2,2,2,256,256]{4,3,2,1,0:T(8,128)(2,1)} %constant.24.clone.refs_4_.table_ref.refs_6_.table_y_ref) | copy-start | bytes 3145732
  31.5 26.7 %copy-start.1 = (bf16[2,2,2,256,256]{4,3,2,1,0:T(8,128)(2,1)S(1)}, bf16[2,2,2,256,256]{4,3,2,1,0:T(8,128)(2,1)}, u32[]{:S(2)}) copy-start(bf16[2,2,2,256,256]{4,3,2,1,0:T(8,128)(2,1)} %constant.25.clone.table_ref) | copy-start | bytes 3145732
  58.2 7.4 %copy-start.12 = (f32[2,1,256,128]{3,2,1,0:T(8,128)S(1)}, f32[2,1,256,128]{3,2,1,0:T(8,128)}, u32[]{:S(2)}) copy-start(f32[2,1,256,128]{3,2,1,0:T(8,128)} %get-tuple-element.71) | copy-start | bytes 786436
  62.8 23.5 %copy-start.10 = (f32[2,2,128,256]{3,2,1,0:T(8,128)S(1)}, f32[2,2,128,256]{3,2,1,0:T(8,128)}, u32[]{:S(2)}) copy-start(f32[2,2,128,256]{3,2,1,0:T(8,128)} %get-tuple-element.74) | copy-start | bytes 1572868
  62.8 25.1 %copy-start.11 = (f32[2,1,256,128]{3,2,1,0:T(8,128)S(1)}, f32[2,1,256,128]{3,2,1,0:T(8,128)}, u32[]{:S(2)}) copy-start(f32[2,1,256,128]{3,2,1,0:T(8,128)} %get-tuple-element.55) | copy-start | bytes 786436
  62.8 25.1 %collective-permute-start.4 = (f32[2,2,128,256]{3,2,1,0:T(8,128)}, f32[2,2,128,256]{3,2,1,0:T(8,128)S(1)}, u32[]{:S(2)}, u32[]{:S(2)}) collective-permute-start(f32[2,2,128,256]{3,2,1,0:T(8,128)} %get-tuple-element.59), channel_id=1, source_target_pairs={{0,12},{4,0},{8,4},{12,8},{1,13},{5,1},{9,5},{13,9},{2,14},{6,2},{... | collective-permute-start | bytes 1572872 | tf_op jit(solution)/shard_map/ppermute | solution.py:439
  65.6 22.5 %collective-permute-start.3 = (f32[2,2,128,256]{3,2,1,0:T(8,128)}, f32[2,2,128,256]{3,2,1,0:T(8,128)S(1)}, u32[]{:S(2)}, u32[]{:S(2)}) collective-permute-start(f32[2,2,128,256]{3,2,1,0:T(8,128)} %get-tuple-element.58), channel_id=1, source_target_pairs={{0,4},{4,8},{8,12},{12,0},{1,5},{5,9},{9,13},{13,1},{2,6},{6,10},{... | collective-permute-start | bytes 1572872 | tf_op jit(solution)/shard_map/ppermute | solution.py:439
  65.6 0.8 copy-start.6
  65.6 22.3 %collective-permute-start.10 = (f32[2,1,256,128]{3,2,1,0:T(8,128)S(1)}, f32[2,1,256,128]{3,2,1,0:T(8,128)S(1)}, u32[]{:S(2)}, u32[]{:S(2)}) collective-permute-start(f32[2,1,256,128]{3,2,1,0:T(8,128)S(1)} %copy-done.12), channel_id=1, source_target_pairs={{0,3},{1,0},{2,1},{3,2},{4,7},{5,4},{6,5},{7,6},{8,11},{9,8},{10,9... | collective-permute-start | bytes 786440 | tf_op jit(solution)/shard_map/ppermute | solution.py:439
  65.7 0.9 copy-start.7
  83.7 26.9 %copy-start.4 = (f32[2,2,256,128]{3,2,1,0:T(8,128)S(1)}, f32[2,2,256,128]{3,2,1,0:T(8,128)}, u32[]{:S(2)}) copy-start(f32[2,2,256,128]{3,2,1,0:T(8,128)} %get-tuple-element.69.b0) | copy-start | bytes 1572868
  83.7 26.9 %collective-permute-start.8 = (f32[2,2,256,128]{3,2,1,0:T(8,128)}, f32[2,2,256,128]{3,2,1,0:T(8,128)S(1)}, u32[]{:S(2)}, u32[]{:S(2)}) collective-permute-start(f32[2,2,256,128]{3,2,1,0:T(8,128)} %get-tuple-element.70), channel_id=1, source_target_pairs={{0,2},{1,3},{2,0},{3,1},{4,6},{5,7},{6,4},{7,5},{8,10},{9,11},{10,... | collective-permute-start | bytes 1572872 | tf_op jit(solution)/shard_map/ppermute | solution.py:439
  86.3 25.3 %collective-permute-start.13 = (f32[2,2,128,256]{3,2,1,0:T(8,128)S(1)}, f32[2,2,128,256]{3,2,1,0:T(8,128)S(1)}, u32[]{:S(2)}, u32[]{:S(2)}) collective-permute-start(f32[2,2,128,256]{3,2,1,0:T(8,128)S(1)} %copy-done.10), channel_id=1, source_target_pairs={{0,8},{4,12},{8,0},{12,4},{1,9},{5,13},{9,1},{13,5},{2,10},{6,14},... | collective-permute-start | bytes 1572872 | tf_op jit(solution)/shard_map/ppermute | solution.py:439
  87.9 17.0 %collective-permute-start.9 = (f32[2,1,256,128]{3,2,1,0:T(8,128)S(1)}, f32[2,1,256,128]{3,2,1,0:T(8,128)S(1)}, u32[]{:S(2)}, u32[]{:S(2)}) collective-permute-start(f32[2,1,256,128]{3,2,1,0:T(8,128)S(1)} %copy-done.11), channel_id=1, source_target_pairs={{0,1},{1,2},{2,3},{3,0},{4,5},{5,6},{6,7},{7,4},{8,9},{9,10},{10,1... | collective-permute-start | bytes 786440 | tf_op jit(solution)/shard_map/ppermute | solution.py:439
  88.0 22.6 %collective-permute-start.11 = (f32[2,1,256,128]{3,2,1,0:T(8,128)}, f32[2,1,256,128]{3,2,1,0:T(8,128)S(1)}, u32[]{:S(2)}, u32[]{:S(2)}) collective-permute-start(f32[2,1,256,128]{3,2,1,0:T(8,128)} %get-tuple-element.72), channel_id=1, source_target_pairs={{0,1},{1,2},{2,3},{3,0},{4,5},{5,6},{6,7},{7,4},{8,9},{9,10},{10,1... | collective-permute-start | bytes 786440 | tf_op jit(solution)/shard_map/ppermute | solution.py:439
  88.1 22.5 %collective-permute-start.12 = (f32[2,1,256,128]{3,2,1,0:T(8,128)}, f32[2,1,256,128]{3,2,1,0:T(8,128)S(1)}, u32[]{:S(2)}, u32[]{:S(2)}) collective-permute-start(f32[2,1,256,128]{3,2,1,0:T(8,128)} %get-tuple-element.73), channel_id=1, source_target_pairs={{0,3},{1,0},{2,1},{3,2},{4,7},{5,4},{6,5},{7,6},{8,11},{9,8},{10,9... | collective-permute-start | bytes 786440 | tf_op jit(solution)/shard_map/ppermute | solution.py:439
  110.6 1.1 copy-start.3
  113.2 37.3 %copy-start.2 = (bf16[2,2,256,512]{3,2,1,0:T(8,128)(2,1)S(1)}, bf16[2,2,256,512]{3,2,1,0:T(8,128)(2,1)}, u32[]{:S(2)}) copy-start(bf16[2,2,256,512]{3,2,1,0:T(8,128)(2,1)} %constant.23.clone.table_ref) | copy-start | bytes 3145732
  113.2 37.3 %copy-start.5 = (bf16[256,256]{1,0:T(8,128)(2,1)S(1)}, bf16[256,256]{1,0:T(8,128)(2,1)}, u32[]{:S(2)}) copy-start(bf16[256,256]{1,0:T(8,128)(2,1)} %constant.26.clone.ordering_ref) | copy-start | bytes 393220

commit v17 on v16

--- a/solution.py
+++ b/solution.py
@@ -225,7 +225,7 @@
 def first_y_kernel(merge, place_ref, to_ref, *refs):
     in_refs, refs = refs[:4], refs[4:]
     before, refs = (refs[:2], refs[2:]) if merge else ((), refs)
-    table_ref, *out_refs, pieces, held_out, semaphores = refs
+    table_ref, *out_refs, pieces, held_out, held_before, semaphores = refs
     gets = [
         pltpu.make_async_copy(ref, pieces.at[s], semaphores.at[0, s])
         for s, ref in enumerate(in_refs)
@@ -236,11 +236,21 @@
         source = held_out.at[lax.rem(to_ref[0] + shift, 4)]
         target = out_refs[i].at[:, 1 if whole else 0]
         puts.append(pltpu.make_async_copy(source, target, semaphores.at[1, i]))
-    moves = [
-        pltpu.make_async_copy(ref.at[:, 0], out_refs[2 + i].at[:, 0], semaphores.at[2, i])
+    gets_before = [
+        pltpu.make_async_copy(ref, held_before.at[i], semaphores.at[2, i])
         for i, ref in enumerate(before)
     ]
-    for copy in gets + moves:
+    puts_before = [
+        pltpu.make_async_copy(
+            held_before.at[i], out_refs[2 + i].at[:, 0:1], semaphores.at[2, 2 + i]
+        )
+        for i in range(len(before))
+    ]
+    for copy in gets + gets_before:
+        copy.start()
+    for copy in gets_before:
+        copy.wait()
+    for copy in puts_before:
         copy.start()
     for copy in gets:
         copy.wait()
@@ -254,7 +264,7 @@
                 ]
     for copy in puts:
         copy.start()
-    for copy in puts + moves:
+    for copy in puts + puts_before:
         copy.wait()
 
 
@@ -274,6 +284,7 @@
         scratch_shapes=[
             pltpu.VMEM((4, 2, 4, 128, 128), jnp.float32),
             pltpu.VMEM((4, 2, KEPT, 128), jnp.float32),
+            pltpu.VMEM((2,) + shape, jnp.float32),
             pltpu.SemaphoreType.DMA((3, 4)),
         ],
         compiler_params=params(VMEM),
@@ -467,7 +478,7 @@
     a, slots, _, d0 = lax.optimization_barrier((a, slots_of(block_owner), c1, d0))
     c1, c3 = shifted(c1, "gz", 1), shifted(c3, "gz", 3)
     a1, a3, a2, a0 = first_z((1, 3, 2, 0), gy, a, table_z)
-    d1, d2, d3, _ = lax.optimization_barrier((d1, d2, d3, a1))
+    d1, d2, d3, c1, c3, _ = lax.optimization_barrier((d1, d2, d3, c1, c3, a1))
     a1, a3, a2 = shifted(a1, "gy", 1), shifted(a3, "gy", 3), shifted(a2, "gy", 2)
     d1, d3, b2, b0 = first_y(gy, gz, (d0, d1, d2, d3), table_y, (c2, c0))
     d1, d3, b2 = shifted(d1, "gz", 1), shifted(d3, "gz", 3), shifted(b2, "gz", 2)

time: 190 us -> 175 us (0.921)
  Pallas kernels: 44.5 us -> 31.1 us
  blocking collectives: 71.5 us -> 76.5 us
  waiting for transfers between devices: 46.8 us -> 42 us
    pallas_call x2, Pallas kernels: 20.8 us -> 7.55 us  [first_y(): pl.pallas_call(functools.partial(first_y_kernel, merge), in_specs=[pl.Blo...]
    all_to_all x1, blocking collectives: 37.3 us -> 42.3 us  [per_device(): lines = lax.all_to_all(planes, ALL, split_axis=0, concat_axis=0, tiled=True)]
    all_to_all x1, waiting for transfers between devices: 15.5 us -> 12.2 us  [per_device(): a = lax.all_to_all(a, 'gz', split_axis=0, concat_axis=0, tiled=True)]
  transfers between devices with their start and end apart: 15 -> 15, of which waited for: 6 -> 7; matrix products, arithmetic and copies ran while one was open for 0% -> 0% of each run, Pallas kernels for 19% -> 13%
where the time goes in v17:
time: 175 us
  blocking collectives  76.5 us (44%)
  waiting for transfers between devices  42 us (24%)
  Pallas kernels  31.1 us (18%)
  starting transfers between devices  22.7 us (13%)
    all_to_all x1, blocking collectives, per_device(): lines = lax.all_to_all(planes, ALL, split_axis=0, concat_axis=0, tiled=True)  42.3 us
    all_to_all x1, blocking collectives, per_device(): lax.all_to_all(outgoing.reshape(128, 1, CAP, 2, BW), ALL, split_axis=0, c...  34.2 us
    ppermute x14, waiting for transfers between devices, shifted(): lax.ppermute(piece, axis, [(i, (i + shift) % size) for i in range(size)])  29.8 us
    ppermute x14, starting transfers between devices, shifted(): lax.ppermute(piece, axis, [(i, (i + shift) % size) for i in range(size)])  16.8 us
    all_to_all x1, waiting for transfers between devices, per_device(): a = lax.all_to_all(a, 'gz', split_axis=0, concat_axis=0, tiled=True)  12.2 us
    pallas_call x5, Pallas kernels, scale(): pl.pallas_call(functools.partial(scale_kernel, part, shifts), in_specs=[p...  11.9 us
    pallas_call x2, Pallas kernels, first_y(): pl.pallas_call(functools.partial(first_y_kernel, merge), in_specs=[pl.Blo...  7.55 us
    all_to_all x1, starting transfers between devices, per_device(): a = lax.all_to_all(a, 'gz', split_axis=0, concat_axis=0, tiled=True)  5.87 us
  transfers between devices with their start and end apart: 15, of which 7 were waited for; matrix products, arithmetic and copies ran while one was open for 0% of the time, Pallas kernels for 13%

profile of v17, /device:TPU:1, one launch (start us, length us, event | category | flops | bytes accessed | tf_op | source)
XLA Modules:
  0.0 174.8 jit_solution(2853027074426312800)
XLA Ops:
  0.0 3.4 %scale_a.1 = f32[4,2,8,128,128]{4,3,2,1,0:T(8,128)} custom-call(s32[1]{0:T(128)} %bitcast.place_ref.to_ref, bf16[2,8,8,128,128]{4,3,2,1,0:T(8,128)(2,1)} %bitcast.23, f32[8,8,128,128]{3,2,1,0:T(8,128)} %bitcast.28), custom_call_target="tpu_custom_call" | custom-call | flops 16 | bytes 128 | tf_op jit(solution)/shard_map/scale_a/pallas_call | solution.py:137
  3.4 5.9 %all-to-all-start = ((f32[4,2,8,128,128]{4,3,2,1,0:T(8,128)}), f32[4,2,8,128,128]{4,3,2,1,0:T(8,128)}, u32[]{:S(2)}, u32[]{:S(2)}) async-start(f32[4,2,8,128,128]{4,3,2,1,0:T(8,128)} %scale_a.1), calls=%async_computation | async-start | bytes 8388608 | tf_op jit(solution)/shard_map/all_to_all | solution.py:467
  9.3 2.3 %scale_b.4 = (f32[2,4,128,128]{3,2,1,0:T(8,128)}, f32[2,4,128,128]{3,2,1,0:T(8,128)}, f32[2,4,128,128]{3,2,1,0:T(8,128)}) custom-call(s32[1]{0:T(128)} %bitcast.3.place_ref.to_ref.y_ref, bf16[2,8,2,4,128,128]{5,4,3,2,1,0:T(8,128)(2,1)} %bitcast.24, f32[8,2,4,128,128]{4,3,2,1,0:T(8,128)} %bitcast.29), custom_call_target="tpu_custom_call" | custom-call | flops 12 | bytes 96 | tf_op jit(solution)/shard_map/scale_b/pallas_call | solution.py:137
  11.6 0.0 copy-start.8
  11.6 1.4 collective-permute-start
  12.9 2.6 %collective-permute-start.1 = (f32[2,4,128,128]{3,2,1,0:T(8,128)}, f32[2,4,128,128]{3,2,1,0:T(8,128)}, u32[]{:S(2)}, u32[]{:S(2)}) collective-permute-start(f32[2,4,128,128]{3,2,1,0:T(8,128)} %get-tuple-element.55), channel_id=1, source_target_pairs={{0,8},{4,12},{8,0},{12,4},{1,9},{5,13},{9,1},{13,5},{2,10},{6,14},... | collective-permute-start | bytes 1572872 | tf_op jit(solution)/shard_map/ppermute | solution.py:450
  15.6 1.1 collective-permute-start.2
  16.6 2.3 %scale_b.5 = (f32[2,4,128,128]{3,2,1,0:T(8,128)}, f32[2,4,128,128]{3,2,1,0:T(8,128)}, f32[2,4,128,128]{3,2,1,0:T(8,128)}) custom-call(s32[1]{0:T(128)} %bitcast.3.place_ref.to_ref.y_ref, bf16[2,8,2,4,128,128]{5,4,3,2,1,0:T(8,128)(2,1)} %bitcast.25, f32[8,2,4,128,128]{4,3,2,1,0:T(8,128)} %bitcast.30), custom_call_target="tpu_custom_call" | custom-call | flops 12 | bytes 96 | tf_op jit(solution)/shard_map/scale_b/pallas_call | solution.py:137
  18.9 0.5 collective-permute-start.5
  19.4 0.8 collective-permute-start.6
  20.2 0.1 copy.11
  20.3 0.2 fusion.2
  20.6 0.1 copy.12
  20.7 5.1 %collective-permute-done.refs_1_ = f32[2,4,128,128]{3,2,1,0:T(8,128)S(1)} collective-permute-done((f32[2,4,128,128]{3,2,1,0:T(8,128)}, f32[2,4,128,128]{3,2,1,0:T(8,128)S(1)}, u32[]{:S(2)}, u32[]{:S(2)}) %collective-permute-start) | collective-permute-done | bytes 524320 | tf_op jit(solution)/shard_map/ppermute | solution.py:450
  25.8 1.4 collective-permute-start.7
  27.2 0.4 fusion.1
  27.5 1.9 %scale_b.7.refs_0_ = f32[2,4,128,128]{3,2,1,0:T(8,128)} custom-call(s32[1]{0:T(128)} %bitcast.3.place_ref.to_ref.y_ref, bf16[2,8,2,4,128,128]{5,4,3,2,1,0:T(8,128)(2,1)} %bitcast.26, f32[8,2,4,128,128]{4,3,2,1,0:T(8,128)} %bitcast.31), custom_call_target="tpu_custom_call" | custom-call | flops 4 | bytes 32 | tf_op jit(solution)/shard_map/scale_b/pallas_call | solution.py:137
  29.5 0.0 copy-start
  29.5 2.0 %scale_b.6.refs_0_ = f32[2,4,128,128]{3,2,1,0:T(8,128)} custom-call(s32[1]{0:T(128)} %bitcast.3.place_ref.to_ref.y_ref, bf16[2,8,2,4,128,128]{5,4,3,2,1,0:T(8,128)(2,1)} %bitcast.27, f32[8,2,4,128,128]{4,3,2,1,0:T(8,128)} %bitcast.32), custom_call_target="tpu_custom_call" | custom-call | flops 4 | bytes 32 | tf_op jit(solution)/shard_map/scale_b/pallas_call | solution.py:137
  31.5 0.0 copy-start.1
  31.5 6.7 %collective-permute-done.1.refs_2_ = f32[2,4,128,128]{3,2,1,0:T(8,128)} collective-permute-done((f32[2,4,128,128]{3,2,1,0:T(8,128)}, f32[2,4,128,128]{3,2,1,0:T(8,128)}, u32[]{:S(2)}, u32[]{:S(2)}) %collective-permute-start.1) | collective-permute-done | bytes 524320 | tf_op jit(solution)/shard_map/ppermute | solution.py:450
  38.2 0.8 collective-permute-done.2.refs_3_
  38.9 3.7 %first_y.2 = (f32[2,1,256,128]{3,2,1,0:T(8,128)}, f32[2,1,256,128]{3,2,1,0:T(8,128)}, f32[2,1,256,128]{3,2,1,0:T(8,128)}, f32[2,1,256,128]{3,2,1,0:T(8,128)}) custom-call(s32[1]{0:T(128)} %bitcast.3.place_ref.to_ref.y_ref, s32[1]{0:T(128)} %bitcast.place_ref.to_ref, f32[2,4,128,128]{3,2,1,0:T(8,128)} %scale_b.6.refs_0_, f32[2,4,128,128]{3,2,1,0:T(8,128)} %copy-done.7, ...), custom_call_target="tpu_custom_call" | custom-call | flops 2048 | bytes 64 | tf_op jit(solution)/shard_map/first_y/pallas_call | solution.py:277
  42.7 3.3 %collective-permute-start.9 = (f32[2,1,256,128]{3,2,1,0:T(8,128)}, f32[2,1,256,128]{3,2,1,0:T(8,128)S(1)}, u32[]{:S(2)}, u32[]{:S(2)}) collective-permute-start(f32[2,1,256,128]{3,2,1,0:T(8,128)} %get-tuple-element.66), channel_id=1, source_target_pairs={{0,3},{1,0},{2,1},{3,2},{4,7},{5,4},{6,5},{7,6},{8,11},{9,8},{10,9... | collective-permute-start | bytes 786440 | tf_op jit(solution)/shard_map/ppermute | solution.py:450
  46.0 12.2 %all-to-all-done.in_ref = f32[4,2,8,128,128]{4,3,2,1,0:T(8,128)} async-done(((f32[4,2,8,128,128]{4,3,2,1,0:T(8,128)}), f32[4,2,8,128,128]{4,3,2,1,0:T(8,128)}, u32[]{:S(2)}, u32[]{:S(2)}) %all-to-all-start) | async-done | bytes 4194336 | tf_op jit(solution)/shard_map/all_to_all | solution.py:467
  58.2 4.5 %first_z.1 = (f32[2,2,128,256]{3,2,1,0:T(8,128)}, f32[2,2,128,256]{3,2,1,0:T(8,128)}, f32[2,2,128,256]{3,2,1,0:T(8,128)}, f32[2,2,128,256]{3,2,1,0:T(8,128)}) custom-call(s32[1]{0:T(128)} %bitcast.3.place_ref.to_ref.y_ref, f32[4,2,8,128,128]{4,3,2,1,0:T(8,128)} %all-to-all-done.in_ref, bf16[2,2,2,256,256]{4,3,2,1,0:T(8,128)(2,1)S(1)} %copy-done.1), custom_call_target="tpu_custom_call" | custom-call | flops 4096 | bytes 128 | tf_op jit(solution)/shard_map/first_z/pallas_call | solution.py:205
  62.7 0.0 collective-permute-done.5.refs_1_
  62.7 2.8 %collective-permute-start.4 = (f32[2,2,128,256]{3,2,1,0:T(8,128)}, f32[2,2,128,256]{3,2,1,0:T(8,128)S(1)}, u32[]{:S(2)}, u32[]{:S(2)}) collective-permute-start(f32[2,2,128,256]{3,2,1,0:T(8,128)} %get-tuple-element.61), channel_id=1, source_target_pairs={{0,12},{4,0},{8,4},{12,8},{1,13},{5,1},{9,5},{13,9},{2,14},{6,2},{... | collective-permute-start | bytes 1572872 | tf_op jit(solution)/shard_map/ppermute | solution.py:450
  65.6 0.0 collective-permute-done.6.refs_2_
  65.6 0.0 collective-permute-start.3
  65.6 0.0 collective-permute-done.7.refs_3_
  65.6 3.8 %first_y.3 = (f32[2,1,256,128]{3,2,1,0:T(8,128)}, f32[2,1,256,128]{3,2,1,0:T(8,128)}, f32[2,2,256,128]{3,2,1,0:T(8,128)}, f32[2,2,256,128]{3,2,1,0:T(8,128)}) custom-call(s32[1]{0:T(128)} %bitcast.3.place_ref.to_ref.y_ref, s32[1]{0:T(128)} %bitcast.place_ref.to_ref, f32[2,4,128,128]{3,2,1,0:T(8,128)} %scale_b.7.refs_0_, f32[2,4,128,128]{3,2,1,0:T(8,128)} %copy-done.6, ...), custom_call_target="tpu_custom_call" | custom-call | flops 2048 | bytes 64 | tf_op jit(solution)/shard_map/first_y/pallas_call | solution.py:277
  69.4 0.1 collective-permute-start.10
  69.5 2.5 %collective-permute-start.13 = (f32[2,2,128,256]{3,2,1,0:T(8,128)S(1)}, f32[2,2,128,256]{3,2,1,0:T(8,128)S(1)}, u32[]{:S(2)}, u32[]{:S(2)}) collective-permute-start(f32[2,2,128,256]{3,2,1,0:T(8,128)S(1)} %copy-done.9), channel_id=1, source_target_pairs={{0,8},{4,12},{8,0},{12,4},{1,9},{5,13},{9,1},{13,5},{2,10},{6,14},... | collective-permute-start | bytes 1572872 | tf_op jit(solution)/shard_map/ppermute | solution.py:450
  72.1 0.4 collective-permute-start.11
  72.5 3.2 %collective-permute-done.4.p3 = f32[2,2,128,256]{3,2,1,0:T(8,128)S(1)} collective-permute-done((f32[2,2,128,256]{3,2,1,0:T(8,128)}, f32[2,2,128,256]{3,2,1,0:T(8,128)S(1)}, u32[]{:S(2)}, u32[]{:S(2)}) %collective-permute-start.4) | collective-permute-done | bytes 524320 | tf_op jit(solution)/shard_map/ppermute | solution.py:450
  75.6 0.0 collective-permute-start.12
  75.7 3.1 %collective-permute-done.3.p1 = f32[2,2,128,256]{3,2,1,0:T(8,128)S(1)} collective-permute-done((f32[2,2,128,256]{3,2,1,0:T(8,128)}, f32[2,2,128,256]{3,2,1,0:T(8,128)S(1)}, u32[]{:S(2)}, u32[]{:S(2)}) %collective-permute-start.3) | collective-permute-done | bytes 524320 | tf_op jit(solution)/shard_map/ppermute | solution.py:450
  78.7 0.9 part_y.1.part_a
  79.7 11.0 %collective-permute-done.11.d1 = f32[2,1,256,128]{3,2,1,0:T(8,128)S(1)} collective-permute-done((f32[2,1,256,128]{3,2,1,0:T(8,128)}, f32[2,1,256,128]{3,2,1,0:T(8,128)S(1)}, u32[]{:S(2)}, u32[]{:S(2)}) %collective-permute-start.11) | collective-permute-done | bytes 262176 | tf_op jit(solution)/shard_map/ppermute | solution.py:450
  90.7 1.0 second_z.1.done_b
  91.8 1.5 second.1
  93.3 0.0 copy-start.2
  93.3 0.0 copy-start.5
  93.3 42.3 %all_to_all.22.in_ref = f32[128,2,2,8,128]{4,3,2,1,0:T(8,128)S(1)} all-to-all(f32[128,2,2,8,128]{4,3,2,1,0:T(8,128)S(1)} %second.1), channel_id=1, replica_groups=mesh['gx'=8,'gy'=4,'gz'=4] {'gx','gy','gz'}, dimensions={0} | all-to-all | bytes 4194304 | tf_op jit(solution)/shard_map/all_to_all | solution.py:490
  135.6 3.7 %third.1 = f32[4096,128]{1,0:T(8,128)S(1)} custom-call(s32[1024]{0:T(1024)S(1)} %multiply_add_fusion.slot_ref, f32[128,2,2,8,128]{4,3,2,1,0:T(8,128)S(1)} %all_to_all.22.in_ref, bf16[2,2,256,512]{3,2,1,0:T(8,128)(2,1)S(1)} %copy-done.2, bf16[256,256]{1,0:T(8,128)(2,1)S(1)} %copy-done.5), custom_call_target="tpu_custom_call" | custom-call | flops 3072 | bytes 96 | tf_op jit(solution)/shard_map/third/pallas_call | solution.py:436
  139.3 34.2 %all_to_all.23 = f32[128,1,16,2,128]{4,3,2,1,0:T(2,128)S(1)} all-to-all(f32[128,1,16,2,128]{4,3,2,1,0:T(2,128)S(1)} %bitcast.22), channel_id=1, replica_groups=mesh['gx'=8,'gy'=4,'gz'=4] {'gx','gy','gz'}, dimensions={0} | all-to-all | bytes 4194304 | tf_op jit(solution)/shard_map/all_to_all | solution.py:492
  173.5 1.3 copy.15
  (26 shorter events, 0.1 us)
Async XLA Ops:
  3.4 54.8 %all-to-all-start = ((f32[4,2,8,128,128]{4,3,2,1,0:T(8,128)}), f32[4,2,8,128,128]{4,3,2,1,0:T(8,128)}, u32[]{:S(2)}, u32[]{:S(2)}) async-start(f32[4,2,8,128,128]{4,3,2,1,0:T(8,128)} %scale_a.1), calls=%async_computation | async-start | bytes 8388608 | tf_op jit(solution)/shard_map/all_to_all | solution.py:467
  11.6 8.6 %copy-start.8 = (s32[1024,1]{0,1:T(1,128)S(1)}, s32[1024,1]{0,1:T(1,128)}, u32[]{:S(2)}) copy-start(s32[1024,1]{0,1:T(1,128)} %param.9) | copy-start | bytes 12292
  11.6 14.2 %collective-permute-start = (f32[2,4,128,128]{3,2,1,0:T(8,128)}, f32[2,4,128,128]{3,2,1,0:T(8,128)S(1)}, u32[]{:S(2)}, u32[]{:S(2)}) collective-permute-start(f32[2,4,128,128]{3,2,1,0:T(8,128)} %get-tuple-element.54), channel_id=1, source_target_pairs={{0,4},{4,8},{8,12},{12,0},{1,5},{5,9},{9,13},{13,1},{2,6},{6,10},{... | collective-permute-start | bytes 1572872 | tf_op jit(solution)/shard_map/ppermute | solution.py:450
  12.9 25.2 %collective-permute-start.1 = (f32[2,4,128,128]{3,2,1,0:T(8,128)}, f32[2,4,128,128]{3,2,1,0:T(8,128)}, u32[]{:S(2)}, u32[]{:S(2)}) collective-permute-start(f32[2,4,128,128]{3,2,1,0:T(8,128)} %get-tuple-element.55), channel_id=1, source_target_pairs={{0,8},{4,12},{8,0},{12,4},{1,9},{5,13},{9,1},{13,5},{2,10},{6,14},... | collective-permute-start | bytes 1572872 | tf_op jit(solution)/shard_map/ppermute | solution.py:450
  15.6 23.4 %collective-permute-start.2 = (f32[2,4,128,128]{3,2,1,0:T(8,128)}, f32[2,4,128,128]{3,2,1,0:T(8,128)}, u32[]{:S(2)}, u32[]{:S(2)}) collective-permute-start(f32[2,4,128,128]{3,2,1,0:T(8,128)} %get-tuple-element.56), channel_id=1, source_target_pairs={{0,12},{4,0},{8,4},{12,8},{1,13},{5,1},{9,5},{13,9},{2,14},{6,2},{... | collective-permute-start | bytes 1572872 | tf_op jit(solution)/shard_map/ppermute | solution.py:450
  18.9 43.8 %collective-permute-start.5 = (f32[2,4,128,128]{3,2,1,0:T(8,128)}, f32[2,4,128,128]{3,2,1,0:T(8,128)S(1)}, u32[]{:S(2)}, u32[]{:S(2)}) collective-permute-start(f32[2,4,128,128]{3,2,1,0:T(8,128)} %get-tuple-element.63), channel_id=1, source_target_pairs={{0,4},{4,8},{8,12},{12,0},{1,5},{5,9},{9,13},{13,1},{2,6},{6,10},{... | collective-permute-start | bytes 1572872 | tf_op jit(solution)/shard_map/ppermute | solution.py:450
  19.4 46.1 %collective-permute-start.6 = (f32[2,4,128,128]{3,2,1,0:T(8,128)}, f32[2,4,128,128]{3,2,1,0:T(8,128)}, u32[]{:S(2)}, u32[]{:S(2)}) collective-permute-start(f32[2,4,128,128]{3,2,1,0:T(8,128)} %get-tuple-element.64), channel_id=1, source_target_pairs={{0,8},{4,12},{8,0},{12,4},{1,9},{5,13},{9,1},{13,5},{2,10},{6,14},... | collective-permute-start | bytes 1572872 | tf_op jit(solution)/shard_map/ppermute | solution.py:450
  25.8 3.7 %copy-start.7 = (f32[2,4,128,128]{3,2,1,0:T(8,128)}, f32[2,4,128,128]{3,2,1,0:T(8,128)S(1)}, u32[]{:S(2)}) copy-start(f32[2,4,128,128]{3,2,1,0:T(8,128)S(1)} %collective-permute-done.refs_1_) | copy-start | bytes 1572868
  25.8 39.8 %collective-permute-start.7 = (f32[2,4,128,128]{3,2,1,0:T(8,128)}, f32[2,4,128,128]{3,2,1,0:T(8,128)}, u32[]{:S(2)}, u32[]{:S(2)}) collective-permute-start(f32[2,4,128,128]{3,2,1,0:T(8,128)} %get-tuple-element.65), channel_id=1, source_target_pairs={{0,12},{4,0},{8,4},{12,8},{1,13},{5,1},{9,5},{13,9},{2,14},{6,2},{... | collective-permute-start | bytes 1572872 | tf_op jit(solution)/shard_map/ppermute | solution.py:450
  29.5 9.5 %copy-start = (bf16[2,2,2,256,256]{4,3,2,1,0:T(8,128)(2,1)S(1)}, bf16[2,2,2,256,256]{4,3,2,1,0:T(8,128)(2,1)}, u32[]{:S(2)}) copy-start(bf16[2,2,2,256,256]{4,3,2,1,0:T(8,128)(2,1)} %constant.24.clone.refs_4_.table_ref.refs_6_.table_y_ref) | copy-start | bytes 3145732
  31.5 26.7 %copy-start.1 = (bf16[2,2,2,256,256]{4,3,2,1,0:T(8,128)(2,1)S(1)}, bf16[2,2,2,256,256]{4,3,2,1,0:T(8,128)(2,1)}, u32[]{:S(2)}) copy-start(bf16[2,2,2,256,256]{4,3,2,1,0:T(8,128)(2,1)} %constant.25.clone.table_ref) | copy-start | bytes 3145732
  42.7 22.9 %collective-permute-start.9 = (f32[2,1,256,128]{3,2,1,0:T(8,128)}, f32[2,1,256,128]{3,2,1,0:T(8,128)S(1)}, u32[]{:S(2)}, u32[]{:S(2)}) collective-permute-start(f32[2,1,256,128]{3,2,1,0:T(8,128)} %get-tuple-element.66), channel_id=1, source_target_pairs={{0,3},{1,0},{2,1},{3,2},{4,7},{5,4},{6,5},{7,6},{8,11},{9,8},{10,9... | collective-permute-start | bytes 786440 | tf_op jit(solution)/shard_map/ppermute | solution.py:450
  46.0 19.6 %collective-permute-start.8 = (f32[2,1,256,128]{3,2,1,0:T(8,128)}, f32[2,1,256,128]{3,2,1,0:T(8,128)S(1)}, u32[]{:S(2)}, u32[]{:S(2)}) collective-permute-start(f32[2,1,256,128]{3,2,1,0:T(8,128)} %get-tuple-element.57), channel_id=1, source_target_pairs={{0,1},{1,2},{2,3},{3,0},{4,5},{5,6},{6,7},{7,4},{8,9},{9,10},{10,1... | collective-permute-start | bytes 786440 | tf_op jit(solution)/shard_map/ppermute | solution.py:450
  62.7 6.8 %copy-start.9 = (f32[2,2,128,256]{3,2,1,0:T(8,128)S(1)}, f32[2,2,128,256]{3,2,1,0:T(8,128)}, u32[]{:S(2)}) copy-start(f32[2,2,128,256]{3,2,1,0:T(8,128)} %get-tuple-element.78) | copy-start | bytes 1572868
  62.7 2.8 %copy-start.6 = (f32[2,4,128,128]{3,2,1,0:T(8,128)}, f32[2,4,128,128]{3,2,1,0:T(8,128)S(1)}, u32[]{:S(2)}) copy-start(f32[2,4,128,128]{3,2,1,0:T(8,128)S(1)} %collective-permute-done.5.refs_1_) | copy-start | bytes 1572868
  62.7 12.9 %collective-permute-start.4 = (f32[2,2,128,256]{3,2,1,0:T(8,128)}, f32[2,2,128,256]{3,2,1,0:T(8,128)S(1)}, u32[]{:S(2)}, u32[]{:S(2)}) collective-permute-start(f32[2,2,128,256]{3,2,1,0:T(8,128)} %get-tuple-element.61), channel_id=1, source_target_pairs={{0,12},{4,0},{8,4},{12,8},{1,13},{5,1},{9,5},{13,9},{2,14},{6,2},{... | collective-permute-start | bytes 1572872 | tf_op jit(solution)/shard_map/ppermute | solution.py:450
  65.6 13.2 %collective-permute-start.3 = (f32[2,2,128,256]{3,2,1,0:T(8,128)}, f32[2,2,128,256]{3,2,1,0:T(8,128)S(1)}, u32[]{:S(2)}, u32[]{:S(2)}) collective-permute-start(f32[2,2,128,256]{3,2,1,0:T(8,128)} %get-tuple-element.60), channel_id=1, source_target_pairs={{0,4},{4,8},{8,12},{12,0},{1,5},{5,9},{9,13},{13,1},{2,6},{6,10},{... | collective-permute-start | bytes 1572872 | tf_op jit(solution)/shard_map/ppermute | solution.py:450
  69.4 21.3 %copy-start.4 = (f32[2,2,256,128]{3,2,1,0:T(8,128)S(1)}, f32[2,2,256,128]{3,2,1,0:T(8,128)}, u32[]{:S(2)}) copy-start(f32[2,2,256,128]{3,2,1,0:T(8,128)} %get-tuple-element.72.b0) | copy-start | bytes 1572868
  69.4 21.3 %collective-permute-start.10 = (f32[2,2,256,128]{3,2,1,0:T(8,128)}, f32[2,2,256,128]{3,2,1,0:T(8,128)S(1)}, u32[]{:S(2)}, u32[]{:S(2)}) collective-permute-start(f32[2,2,256,128]{3,2,1,0:T(8,128)} %get-tuple-element.73), channel_id=1, source_target_pairs={{0,2},{1,3},{2,0},{3,1},{4,6},{5,7},{6,4},{7,5},{8,10},{9,11},{10,... | collective-permute-start | bytes 1572872 | tf_op jit(solution)/shard_map/ppermute | solution.py:450
  69.5 22.2 %collective-permute-start.13 = (f32[2,2,128,256]{3,2,1,0:T(8,128)S(1)}, f32[2,2,128,256]{3,2,1,0:T(8,128)S(1)}, u32[]{:S(2)}, u32[]{:S(2)}) collective-permute-start(f32[2,2,128,256]{3,2,1,0:T(8,128)S(1)} %copy-done.9), channel_id=1, source_target_pairs={{0,8},{4,12},{8,0},{12,4},{1,9},{5,13},{9,1},{13,5},{2,10},{6,14},... | collective-permute-start | bytes 1572872 | tf_op jit(solution)/shard_map/ppermute | solution.py:450
  72.1 18.6 %collective-permute-start.11 = (f32[2,1,256,128]{3,2,1,0:T(8,128)}, f32[2,1,256,128]{3,2,1,0:T(8,128)S(1)}, u32[]{:S(2)}, u32[]{:S(2)}) collective-permute-start(f32[2,1,256,128]{3,2,1,0:T(8,128)} %get-tuple-element.76), channel_id=1, source_target_pairs={{0,1},{1,2},{2,3},{3,0},{4,5},{5,6},{6,7},{7,4},{8,9},{9,10},{10,1... | collective-permute-start | bytes 786440 | tf_op jit(solution)/shard_map/ppermute | solution.py:450
  75.6 15.1 %collective-permute-start.12 = (f32[2,1,256,128]{3,2,1,0:T(8,128)}, f32[2,1,256,128]{3,2,1,0:T(8,128)S(1)}, u32[]{:S(2)}, u32[]{:S(2)}) collective-permute-start(f32[2,1,256,128]{3,2,1,0:T(8,128)} %get-tuple-element.77), channel_id=1, source_target_pairs={{0,3},{1,0},{2,1},{3,2},{4,7},{5,4},{6,5},{7,6},{8,11},{9,8},{10,9... | collective-permute-start | bytes 786440 | tf_op jit(solution)/shard_map/ppermute | solution.py:450
  90.7 1.0 copy-start.3
  93.3 42.3 %copy-start.2 = (bf16[2,2,256,512]{3,2,1,0:T(8,128)(2,1)S(1)}, bf16[2,2,256,512]{3,2,1,0:T(8,128)(2,1)}, u32[]{:S(2)}) copy-start(bf16[2,2,256,512]{3,2,1,0:T(8,128)(2,1)} %constant.23.clone.table_ref) | copy-start | bytes 3145732
  93.3 42.3 %copy-start.5 = (bf16[256,256]{1,0:T(8,128)(2,1)S(1)}, bf16[256,256]{1,0:T(8,128)(2,1)}, u32[]{:S(2)}) copy-start(bf16[256,256]{1,0:T(8,128)(2,1)} %constant.26.clone.ordering_ref) | copy-start | bytes 393220

commit v18 on v17

--- a/solution.py
+++ b/solution.py
@@ -171,20 +171,17 @@
     return parts
 
 
-def first_z_kernel(shifts, to_ref, in_ref, table_ref, *refs):
-    *out_refs, pieces, held_out, semaphores = refs
-
+def first_z_kernel(in_ref, table_ref, out_ref, pieces, held_out, semaphores):
     def get(i):
-        cells = pl.ds(2 * lax.rem(to_ref[0] + shifts[i], 4), 2)
+        cells = pl.ds(2 * i, 2)
         return pltpu.make_async_copy(in_ref.at[:, :, cells], pieces.at[i], semaphores.at[i, 0])
 
     def put(i):
-        return pltpu.make_async_copy(held_out.at[i], out_refs[i], semaphores.at[i, 1])
-
-    steps = range(len(shifts))
-    for i in steps:
+        return pltpu.make_async_copy(held_out.at[i], out_ref.at[i], semaphores.at[i, 1])
+
+    for i in range(4):
         get(i).start()
-    for i in steps:
+    for i in range(4):
         get(i).wait()
         pairs = [(pieces[i, 0], pieces[i, 2], 0), (pieces[i, 1], pieces[i, 3], 1)]
         for odd, values in enumerate(transform(True, pairs, table_ref)):
@@ -194,32 +191,27 @@
                 for x in range(2):
                     held_out[i, plane, x, :, half] = values[x * 128 : (x + 1) * 128, part]
         put(i).start()
-    for i in steps:
+    for i in range(4):
         put(i).wait()
 
 
-def first_z(shifts, to, arrived, table):
-    shape = (2, 2, 128, KEPT)
+def first_z(arrived, table):
+    shape = (4, 2, 2, 128, KEPT)
     hbm = pl.BlockSpec(memory_space=pltpu.HBM)
-    count = len(shifts)
-    return pl.pallas_call(
-        functools.partial(first_z_kernel, shifts),
-        in_specs=[
-            pl.BlockSpec(memory_space=pltpu.SMEM),
-            hbm,
-            pl.BlockSpec(memory_space=pltpu.VMEM),
+    return pl.pallas_call(
+        first_z_kernel,
+        in_specs=[hbm, pl.BlockSpec(memory_space=pltpu.VMEM)],
+        out_specs=hbm,
+        out_shape=pltpu.HBM(shape, jnp.float32),
+        scratch_shapes=[
+            pltpu.VMEM((4, 4, 2, 2, 128, 128), jnp.float32),
+            pltpu.VMEM(shape, jnp.float32),
+            pltpu.SemaphoreType.DMA((4, 2)),
         ],
-        out_specs=[hbm] * count,
-        out_shape=[pltpu.HBM(shape, jnp.float32)] * count,
-        scratch_shapes=[
-            pltpu.VMEM((count, 4, 2, 2, 128, 128), jnp.float32),
-            pltpu.VMEM((count,) + shape, jnp.float32),
-            pltpu.SemaphoreType.DMA((count, 2)),
-        ],
-        compiler_params=params(VMEM),
-        cost_estimate=cost(count * 256 * 512 * 512, 2 * count * MIB),
+        compiler_params=params(VMEM),
+        cost_estimate=cost(4 * 256 * 512 * 512, 8 * MIB),
         name="first_z",
-    )(to, *in_hbm(arrived), table)
+    )(*in_hbm(arrived), table)
 
 
 def first_y_kernel(merge, place_ref, to_ref, *refs):
@@ -293,27 +285,27 @@
     )(place, to, *operands, table)
 
 
-def part_y_kernel(place_ref, p1, p3, table_ref, out_ref):
-    pairs = [(p1[...], p3[...], lax.rem(place_ref[0] + 3, 4))]
+def second_y_kernel(p0, p1, p2, p3, table_ref, out_ref):
+    pairs = [(p0[0], p2[0], 0), (p1[0], p3[0], 1)]
     for odd, values in enumerate(transform(False, pairs, table_ref)):
         out_ref[odd] = values
 
 
-def part_y(place, pieces, table):
-    return pl.pallas_call(
-        part_y_kernel,
-        grid_spec=pltpu.PrefetchScalarGridSpec(
-            num_scalar_prefetch=1,
-            grid=(2,),
-            in_specs=[pl.BlockSpec((2, 1, 128, KEPT), lambda i, place: (0, i, 0, 0))] * 2
-            + [pl.BlockSpec(table.shape, lambda i, place: (0, 0, 0, 0, 0))],
-            out_specs=pl.BlockSpec((2, KEPT, KEPT), lambda i, place: (0, 0, i)),
-        ),
+def second_y(arrived, table):
+    def from_device(g):
+        return pl.BlockSpec((1, 2, 1, 128, KEPT), lambda i: (g, 0, i, 0, 0))
+
+    return pl.pallas_call(
+        second_y_kernel,
+        grid=(2,),
+        in_specs=[from_device(g) for g in range(4)]
+        + [pl.BlockSpec(table.shape, lambda i: (0, 0, 0, 0, 0))],
+        out_specs=pl.BlockSpec((2, KEPT, KEPT), lambda i: (0, 0, i)),
         out_shape=jax.ShapeDtypeStruct((2, KEPT, 512), jnp.float32),
         compiler_params=params(VMEM),
-        cost_estimate=cost(512 * 512 * 256, 4 * MIB),
-        name="part_y",
-    )(place, *pieces, table)
+        cost_estimate=cost(512 * 512 * 512, 5 * MIB),
+        name="second_y",
+    )(arrived, arrived, arrived, arrived, table)
 
 
 def second_z_kernel(place_ref, b0, b2, c1, c3, d1, d3, table_ref, out_ref):
@@ -338,60 +330,36 @@
     )(place, *pieces, table)
 
 
-def second_kernel(
-    y_ref, part_a, a0, a2, table_y_ref, done_b, out_ref, held
-):
-    odd = pl.program_id(0)
-
+def second_kernel(done_a, done_b, out_ref, held):
     def put(values, half, row):
         held[pl.ds(half * 8 + row, 128, stride=16), :] = values
 
-    base = lax.rem(y_ref[0], 2)
-    flip = jnp.where(odd == 0, 1.0, -1.0).astype(jnp.float32)
-    sign = jnp.where((odd == 0) | (y_ref[0] < 2), 1.0, -1.0).astype(jnp.float32)
-    table = (table_y_ref[0, base, 0], table_y_ref[1, base, 0])
-    values = part_a[0] + product(table, columns_y((a0[...] + flip * a2[...]) * sign))
     for plane in range(2):
+        pairs = slice(plane * 128, (plane + 1) * 128)
         for x in range(2):
             for half in range(2):
                 start = x * KEPT + half * 128
-                put(
-                    values[plane * 128 : (plane + 1) * 128, start : start + 128],
-                    half,
-                    plane * 4 + x,
-                )
-    for half in range(2):
-        values = done_b[:, :, half * 256 : (half + 1) * 256].reshape(256, 256)
-        for x in range(2):
-            for plane in range(2):
-                put(
-                    values[x * 128 : (x + 1) * 128, plane * 128 : (plane + 1) * 128],
-                    half,
-                    plane * 4 + 2 + x,
-                )
+                put(done_a[0, pairs, start : start + 128], half, plane * 4 + x)
+                start = half * KEPT + plane * 128
+                put(done_b[x, :, start : start + 128], half, plane * 4 + 2 + x)
     out_ref[...] = held[...].reshape(128, 1, 2, 8, 128)
 
 
-def second(gy, part_a, pieces_a, table_y, done_b):
+def second(done_a, done_b):
     return pl.pallas_call(
         second_kernel,
-        grid_spec=pltpu.PrefetchScalarGridSpec(
-            num_scalar_prefetch=1,
-            grid=(2,),
-            in_specs=[pl.BlockSpec((1, KEPT, 512), lambda i, gy: (i, 0, 0))]
-            + [pl.BlockSpec((2, 2, 128, KEPT), lambda i, gy: (0, 0, 0, 0))] * 2
-            + [
-                pl.BlockSpec((2, 2, 1, KEPT, KEPT), lambda i, gy: (0, 0, i, 0, 0)),
-                pl.BlockSpec((2, 128, 512), lambda i, gy: (0, i, 0)),
-            ],
-            out_specs=pl.BlockSpec((128, 1, 2, 8, 128), lambda i, gy: (0, i, 0, 0, 0)),
-            scratch_shapes=[pltpu.VMEM((2048, 128), jnp.float32)],
-        ),
+        grid=(2,),
+        in_specs=[
+            pl.BlockSpec((1, KEPT, 512), lambda i: (i, 0, 0)),
+            pl.BlockSpec((2, 128, 512), lambda i: (0, i, 0)),
+        ],
+        out_specs=pl.BlockSpec((128, 1, 2, 8, 128), lambda i: (0, i, 0, 0, 0)),
         out_shape=jax.ShapeDtypeStruct((128, 2, 2, 8, 128), jnp.float32),
-        compiler_params=params(VMEM),
-        cost_estimate=cost(512 * 512 * 256, 8 * MIB),
+        scratch_shapes=[pltpu.VMEM((2048, 128), jnp.float32)],
+        compiler_params=params(VMEM),
+        cost_estimate=cost(1 << 20, 4 * MIB),
         name="second",
-    )(gy, part_a, *pieces_a, table_y, done_b)
+    )(done_a, done_b)
 
 
 def third_kernel(slot_ref, in_ref, table_ref, ordering_ref, out_ref, held):
@@ -477,16 +445,15 @@
     c1, c3, c2, c0 = first_y(gy, gz, (c0, c1, c2, c3), table_y)
     a, slots, _, d0 = lax.optimization_barrier((a, slots_of(block_owner), c1, d0))
     c1, c3 = shifted(c1, "gz", 1), shifted(c3, "gz", 3)
-    a1, a3, a2, a0 = first_z((1, 3, 2, 0), gy, a, table_z)
-    d1, d2, d3, c1, c3, _ = lax.optimization_barrier((d1, d2, d3, c1, c3, a1))
-    a1, a3, a2 = shifted(a1, "gy", 1), shifted(a3, "gy", 3), shifted(a2, "gy", 2)
+    a = first_z(a, table_z)
+    d1, d2, d3, c1, c3, _ = lax.optimization_barrier((d1, d2, d3, c1, c3, a))
+    a = lax.all_to_all(a, "gy", split_axis=0, concat_axis=0, tiled=True)
     d1, d3, b2, b0 = first_y(gy, gz, (d0, d1, d2, d3), table_y, (c2, c0))
     d1, d3, b2 = shifted(d1, "gz", 1), shifted(d3, "gz", 3), shifted(b2, "gz", 2)
 
-    part_a = part_y(gy, (a1, a3), table_y)
-    done_b = second_z(gz, (b0, b2, c1, c3, d1, d3), table_z)
-    part_a, done_b, a2 = lax.optimization_barrier((part_a, done_b, a2))
-    planes = second(gy, part_a, (a0, a2), table_y, done_b)
+    a = second_y(a, table_y)
+    a, d1, d3, b2 = lax.optimization_barrier((a, d1, d3, b2))
+    planes = second(a, second_z(gz, (b0, b2, c1, c3, d1, d3), table_z))
     lines = lax.all_to_all(planes, ALL, split_axis=0, concat_axis=0, tiled=True)
     outgoing = third(slots, lines, table_x, ordering)
     return lax.all_to_all(

time: 175 us -> 219 us (1.25)
  waiting for transfers between devices: 42 us -> 86.9 us
  blocking collectives: 76.5 us -> 69.8 us
  starting transfers between devices: 22.7 us -> 25.2 us
    ppermute x14 -> x11, waiting for transfers between devices: 29.8 us -> 71.3 us  [shifted(): lax.ppermute(piece, axis, [(i, (i + shift) % size) for i in range(size)])]
    all_to_all x1, blocking collectives: 42.3 us -> 35.5 us  [per_device(): lines = lax.all_to_all(planes, ALL, split_axis=0, concat_axis=0, tiled=True)]
    all_to_all x0 -> x1, starting transfers between devices: none -> 4.2 us  [per_device(): a = lax.all_to_all(a, 'gy', split_axis=0, concat_axis=0, tiled=True)]
    all_to_all x1, waiting for transfers between devices: 12.2 us -> 15.6 us  [per_device(): a = lax.all_to_all(a, 'gz', split_axis=0, concat_axis=0, tiled=True)]
    ppermute x14 -> x11, starting transfers between devices: 16.8 us -> 15.1 us  [shifted(): lax.ppermute(piece, axis, [(i, (i + shift) % size) for i in range(size)])]
  transfers between devices with their start and end apart: 15 -> 13, of which waited for: 7 -> 6; matrix products, arithmetic and copies ran while one was open for 0% -> 0% of each run, Pallas kernels for 13% -> 8%
where the time goes in v18:
time: 219 us
  waiting for transfers between devices  86.9 us (40%)
  blocking collectives  69.8 us (32%)
  Pallas kernels  32.7 us (15%)
  starting transfers between devices  25.2 us (12%)
  local copies, waits for them, and re-layouts  3.42 us (2%)
    ppermute x11, waiting for transfers between devices, shifted(): lax.ppermute(piece, axis, [(i, (i + shift) % size) for i in range(size)])  71.3 us
    all_to_all x1, blocking collectives, per_device(): lines = lax.all_to_all(planes, ALL, split_axis=0, concat_axis=0, tiled=True)  35.5 us
    all_to_all x1, blocking collectives, per_device(): lax.all_to_all(outgoing.reshape(128, 1, CAP, 2, BW), ALL, split_axis=0, c...  34.2 us
    all_to_all x1, waiting for transfers between devices, per_device(): a = lax.all_to_all(a, 'gz', split_axis=0, concat_axis=0, tiled=True)  15.6 us
    ppermute x11, starting transfers between devices, shifted(): lax.ppermute(piece, axis, [(i, (i + shift) % size) for i in range(size)])  15.1 us
    pallas_call x5, Pallas kernels, scale(): pl.pallas_call(functools.partial(scale_kernel, part, shifts), in_specs=[p...  11.9 us
    pallas_call x2, Pallas kernels, first_y(): pl.pallas_call(functools.partial(first_y_kernel, merge), in_specs=[pl.Blo...  7.48 us
    all_to_all x1, starting transfers between devices, per_device(): a = lax.all_to_all(a, 'gz', split_axis=0, concat_axis=0, tiled=True)  5.87 us
  transfers between devices with their start and end apart: 13, of which 6 were waited for; matrix products, arithmetic and copies ran while one was open for 0% of the time, Pallas kernels for 8%

profile of v18, /device:TPU:1, one launch (start us, length us, event | category | flops | bytes accessed | tf_op | source)
XLA Modules:
  0.0 218.9 jit_solution(15418531807800449363)
XLA Ops:
  0.0 3.4 %scale_a.1 = f32[4,2,8,128,128]{4,3,2,1,0:T(8,128)} custom-call(s32[1]{0:T(128)} %bitcast.place_ref.to_ref, bf16[2,8,8,128,128]{4,3,2,1,0:T(8,128)(2,1)} %bitcast.23, f32[8,8,128,128]{3,2,1,0:T(8,128)} %bitcast.28), custom_call_target="tpu_custom_call" | custom-call | flops 16 | bytes 128 | tf_op jit(solution)/shard_map/scale_a/pallas_call | solution.py:137
  3.4 5.9 %all-to-all-start = ((f32[4,2,8,128,128]{4,3,2,1,0:T(8,128)}), f32[4,2,8,128,128]{4,3,2,1,0:T(8,128)}, u32[]{:S(2)}, u32[]{:S(2)}) async-start(f32[4,2,8,128,128]{4,3,2,1,0:T(8,128)} %scale_a.1), calls=%async_computation | async-start | bytes 8388608 | tf_op jit(solution)/shard_map/all_to_all | solution.py:435
  9.3 2.3 %scale_b.4 = (f32[2,4,128,128]{3,2,1,0:T(8,128)}, f32[2,4,128,128]{3,2,1,0:T(8,128)}, f32[2,4,128,128]{3,2,1,0:T(8,128)}) custom-call(s32[1]{0:T(128)} %bitcast.3.place_ref, bf16[2,8,2,4,128,128]{5,4,3,2,1,0:T(8,128)(2,1)} %bitcast.24, f32[8,2,4,128,128]{4,3,2,1,0:T(8,128)} %bitcast.29), custom_call_target="tpu_custom_call" | custom-call | flops 12 | bytes 96 | tf_op jit(solution)/shard_map/scale_b/pallas_call | solution.py:137
  11.6 1.4 collective-permute-start
  13.0 2.6 %collective-permute-start.1 = (f32[2,4,128,128]{3,2,1,0:T(8,128)}, f32[2,4,128,128]{3,2,1,0:T(8,128)S(1)}, u32[]{:S(2)}, u32[]{:S(2)}) collective-permute-start(f32[2,4,128,128]{3,2,1,0:T(8,128)} %get-tuple-element.52), channel_id=1, source_target_pairs={{0,8},{4,12},{8,0},{12,4},{1,9},{5,13},{9,1},{13,5},{2,10},{6,14},... | collective-permute-start | bytes 1572872 | tf_op jit(solution)/shard_map/ppermute | solution.py:418
  15.6 1.1 collective-permute-start.2
  16.7 2.3 %scale_b.5 = (f32[2,4,128,128]{3,2,1,0:T(8,128)}, f32[2,4,128,128]{3,2,1,0:T(8,128)}, f32[2,4,128,128]{3,2,1,0:T(8,128)}) custom-call(s32[1]{0:T(128)} %bitcast.3.place_ref, bf16[2,8,2,4,128,128]{5,4,3,2,1,0:T(8,128)(2,1)} %bitcast.25, f32[8,2,4,128,128]{4,3,2,1,0:T(8,128)} %bitcast.30), custom_call_target="tpu_custom_call" | custom-call | flops 12 | bytes 96 | tf_op jit(solution)/shard_map/scale_b/pallas_call | solution.py:137
  19.0 2.0 scale_b.7.refs_0_
  20.9 0.0 copy-start.13
  20.9 1.9 scale_b.6.refs_0_
  22.8 0.0 copy-start
  22.9 0.1 copy.11
  23.0 0.2 fusion.2
  23.3 0.1 copy.12
  23.4 0.0 copy-start.1
  23.4 0.4 fusion.1
  23.8 2.0 collective-permute-done.refs_1_
  25.8 12.3 %collective-permute-done.1.refs_2_ = f32[2,4,128,128]{3,2,1,0:T(8,128)S(1)} collective-permute-done((f32[2,4,128,128]{3,2,1,0:T(8,128)}, f32[2,4,128,128]{3,2,1,0:T(8,128)S(1)}, u32[]{:S(2)}, u32[]{:S(2)}) %collective-permute-start.1) | collective-permute-done | bytes 524320 | tf_op jit(solution)/shard_map/ppermute | solution.py:418
  38.2 0.0 collective-permute-done.2.refs_3_
  38.2 0.8 copy-done.9
  38.9 3.7 %first_y.2 = (f32[2,1,256,128]{3,2,1,0:T(8,128)}, f32[2,1,256,128]{3,2,1,0:T(8,128)}, f32[2,1,256,128]{3,2,1,0:T(8,128)}, f32[2,1,256,128]{3,2,1,0:T(8,128)}) custom-call(s32[1]{0:T(128)} %bitcast.3.place_ref, s32[1]{0:T(128)} %bitcast.place_ref.to_ref, f32[2,4,128,128]{3,2,1,0:T(8,128)} %scale_b.6.refs_0_, f32[2,4,128,128]{3,2,1,0:T(8,128)} %copy-done.8, ...), custom_call_target="tpu_custom_call" | custom-call | flops 2048 | bytes 64 | tf_op jit(solution)/shard_map/first_y/pallas_call | solution.py:269
  42.6 15.6 %all-to-all-done.in_ref = f32[4,2,8,128,128]{4,3,2,1,0:T(8,128)} async-done(((f32[4,2,8,128,128]{4,3,2,1,0:T(8,128)}), f32[4,2,8,128,128]{4,3,2,1,0:T(8,128)}, u32[]{:S(2)}, u32[]{:S(2)}) %all-to-all-start) | async-done | bytes 4194336 | tf_op jit(solution)/shard_map/all_to_all | solution.py:435
  58.2 4.5 %first_z.1 = f32[4,2,2,128,256]{4,3,2,1,0:T(8,128)} custom-call(f32[4,2,8,128,128]{4,3,2,1,0:T(8,128)} %all-to-all-done.in_ref, bf16[2,2,2,256,256]{4,3,2,1,0:T(8,128)(2,1)S(1)} %copy-done.1), custom_call_target="tpu_custom_call" | custom-call | flops 4096 | bytes 128 | tf_op jit(solution)/shard_map/first_z/pallas_call | solution.py:201
  62.7 4.2 %all-to-all-start.1 = ((f32[4,2,2,128,256]{4,3,2,1,0:T(8,128)}), f32[4,2,2,128,256]{4,3,2,1,0:T(8,128)S(1)}, u32[]{:S(2)}, u32[]{:S(2)}) async-start(f32[4,2,2,128,256]{4,3,2,1,0:T(8,128)} %first_z.1), calls=%async_computation.1 | async-start | bytes 4194304 | tf_op jit(solution)/shard_map/all_to_all | solution.py:450
  66.9 1.5 collective-permute-start.3
  68.4 2.4 %collective-permute-start.4 = (f32[2,4,128,128]{3,2,1,0:T(8,128)}, f32[2,4,128,128]{3,2,1,0:T(8,128)S(1)}, u32[]{:S(2)}, u32[]{:S(2)}) collective-permute-start(f32[2,4,128,128]{3,2,1,0:T(8,128)} %get-tuple-element.59), channel_id=1, source_target_pairs={{0,8},{4,12},{8,0},{12,4},{1,9},{5,13},{9,1},{13,5},{2,10},{6,14},... | collective-permute-start | bytes 1572872 | tf_op jit(solution)/shard_map/ppermute | solution.py:418
  70.8 1.2 collective-permute-start.5
  72.0 1.5 collective-permute-start.6
  73.5 29.0 %collective-permute-done.3.refs_1_ = f32[2,4,128,128]{3,2,1,0:T(8,128)S(1)} collective-permute-done((f32[2,4,128,128]{3,2,1,0:T(8,128)}, f32[2,4,128,128]{3,2,1,0:T(8,128)S(1)}, u32[]{:S(2)}, u32[]{:S(2)}) %collective-permute-start.3) | collective-permute-done | bytes 524320 | tf_op jit(solution)/shard_map/ppermute | solution.py:418
  102.5 11.6 %collective-permute-done.4.refs_2_ = f32[2,4,128,128]{3,2,1,0:T(8,128)S(1)} collective-permute-done((f32[2,4,128,128]{3,2,1,0:T(8,128)}, f32[2,4,128,128]{3,2,1,0:T(8,128)S(1)}, u32[]{:S(2)}, u32[]{:S(2)}) %collective-permute-start.4) | collective-permute-done | bytes 524320 | tf_op jit(solution)/shard_map/ppermute | solution.py:418
  114.1 0.0 collective-permute-done.5.refs_3_
  114.1 0.8 copy-done.5
  114.9 0.1 copy-done.11
  115.0 0.2 copy-done.12
  115.2 3.8 %first_y.3 = (f32[2,1,256,128]{3,2,1,0:T(8,128)}, f32[2,1,256,128]{3,2,1,0:T(8,128)}, f32[2,2,256,128]{3,2,1,0:T(8,128)}, f32[2,2,256,128]{3,2,1,0:T(8,128)}) custom-call(s32[1]{0:T(128)} %bitcast.3.place_ref, s32[1]{0:T(128)} %bitcast.place_ref.to_ref, f32[2,4,128,128]{3,2,1,0:T(8,128)} %scale_b.7.refs_0_, f32[2,4,128,128]{3,2,1,0:T(8,128)} %copy-done.10, ...), custom_call_target="tpu_custom_call" | custom-call | flops 2048 | bytes 64 | tf_op jit(solution)/shard_map/first_y/pallas_call | solution.py:269
  119.0 0.1 collective-permute-start.10
  119.1 1.1 collective-permute-start.8
  120.2 2.3 %collective-permute-start.9 = (f32[2,1,256,128]{3,2,1,0:T(8,128)}, f32[2,1,256,128]{3,2,1,0:T(8,128)}, u32[]{:S(2)}, u32[]{:S(2)}) collective-permute-start(f32[2,1,256,128]{3,2,1,0:T(8,128)} %get-tuple-element.68), channel_id=1, source_target_pairs={{0,3},{1,0},{2,1},{3,2},{4,7},{5,4},{6,5},{7,6},{8,11},{9,8},{10,9... | collective-permute-start | bytes 786440 | tf_op jit(solution)/shard_map/ppermute | solution.py:418
  122.5 1.5 second_y.1.done_a
  124.0 16.3 %collective-permute-done.8.d1 = f32[2,1,256,128]{3,2,1,0:T(8,128)} collective-permute-done((f32[2,1,256,128]{3,2,1,0:T(8,128)}, f32[2,1,256,128]{3,2,1,0:T(8,128)}, u32[]{:S(2)}, u32[]{:S(2)}) %collective-permute-start.8) | collective-permute-done | bytes 262176 | tf_op jit(solution)/shard_map/ppermute | solution.py:418
  140.4 2.2 second_z.1.done_b
  142.5 1.5 second.1
  144.0 0.0 copy-start.3
  144.1 0.0 copy-start.7
  144.1 35.5 %all_to_all.27.in_ref = f32[128,2,2,8,128]{4,3,2,1,0:T(8,128)S(1)} all-to-all(f32[128,2,2,8,128]{4,3,2,1,0:T(8,128)S(1)} %second.1), channel_id=1, replica_groups=mesh['gx'=8,'gy'=4,'gz'=4] {'gx','gy','gz'}, dimensions={0} | all-to-all | bytes 4194304 | tf_op jit(solution)/shard_map/all_to_all | solution.py:457
  179.6 3.7 %third.1 = f32[4096,128]{1,0:T(8,128)S(1)} custom-call(s32[1024]{0:T(1024)S(1)} %multiply_add_fusion.slot_ref, f32[128,2,2,8,128]{4,3,2,1,0:T(8,128)S(1)} %all_to_all.27.in_ref, bf16[2,2,256,512]{3,2,1,0:T(8,128)(2,1)S(1)} %copy-done.3, bf16[256,256]{1,0:T(8,128)(2,1)S(1)} %copy-done.7), custom_call_target="tpu_custom_call" | custom-call | flops 3072 | bytes 96 | tf_op jit(solution)/shard_map/third/pallas_call | solution.py:404
  183.3 34.2 %all_to_all.28 = f32[128,1,16,2,128]{4,3,2,1,0:T(2,128)S(1)} all-to-all(f32[128,1,16,2,128]{4,3,2,1,0:T(2,128)S(1)} %bitcast.22), channel_id=1, replica_groups=mesh['gx'=8,'gy'=4,'gz'=4] {'gx','gy','gz'}, dimensions={0} | all-to-all | bytes 4194304 | tf_op jit(solution)/shard_map/all_to_all | solution.py:459
  217.6 1.3 copy.15
  (30 shorter events, 0.1 us)
Async XLA Ops:
  3.4 54.8 %all-to-all-start = ((f32[4,2,8,128,128]{4,3,2,1,0:T(8,128)}), f32[4,2,8,128,128]{4,3,2,1,0:T(8,128)}, u32[]{:S(2)}, u32[]{:S(2)}) async-start(f32[4,2,8,128,128]{4,3,2,1,0:T(8,128)} %scale_a.1), calls=%async_computation | async-start | bytes 8388608 | tf_op jit(solution)/shard_map/all_to_all | solution.py:435
  11.6 14.2 %collective-permute-start = (f32[2,4,128,128]{3,2,1,0:T(8,128)}, f32[2,4,128,128]{3,2,1,0:T(8,128)S(1)}, u32[]{:S(2)}, u32[]{:S(2)}) collective-permute-start(f32[2,4,128,128]{3,2,1,0:T(8,128)} %get-tuple-element.51), channel_id=1, source_target_pairs={{0,4},{4,8},{8,12},{12,0},{1,5},{5,9},{9,13},{13,1},{2,6},{6,10},{... | collective-permute-start | bytes 1572872 | tf_op jit(solution)/shard_map/ppermute | solution.py:418
  13.0 25.2 %collective-permute-start.1 = (f32[2,4,128,128]{3,2,1,0:T(8,128)}, f32[2,4,128,128]{3,2,1,0:T(8,128)S(1)}, u32[]{:S(2)}, u32[]{:S(2)}) collective-permute-start(f32[2,4,128,128]{3,2,1,0:T(8,128)} %get-tuple-element.52), channel_id=1, source_target_pairs={{0,8},{4,12},{8,0},{12,4},{1,9},{5,13},{9,1},{13,5},{2,10},{6,14},... | collective-permute-start | bytes 1572872 | tf_op jit(solution)/shard_map/ppermute | solution.py:418
  15.6 22.6 %collective-permute-start.2 = (f32[2,4,128,128]{3,2,1,0:T(8,128)}, f32[2,4,128,128]{3,2,1,0:T(8,128)}, u32[]{:S(2)}, u32[]{:S(2)}) collective-permute-start(f32[2,4,128,128]{3,2,1,0:T(8,128)} %get-tuple-element.53), channel_id=1, source_target_pairs={{0,12},{4,0},{8,4},{12,8},{1,13},{5,1},{9,5},{13,9},{2,14},{6,2},{... | collective-permute-start | bytes 1572872 | tf_op jit(solution)/shard_map/ppermute | solution.py:418
  20.9 1.9 copy-start.13
  22.8 16.1 %copy-start = (bf16[2,2,2,256,256]{4,3,2,1,0:T(8,128)(2,1)S(1)}, bf16[2,2,2,256,256]{4,3,2,1,0:T(8,128)(2,1)}, u32[]{:S(2)}) copy-start(bf16[2,2,2,256,256]{4,3,2,1,0:T(8,128)(2,1)} %constant.24.clone.refs_4_.table_ref.refs_6_) | copy-start | bytes 3145732
  23.4 34.9 %copy-start.1 = (bf16[2,2,2,256,256]{4,3,2,1,0:T(8,128)(2,1)S(1)}, bf16[2,2,2,256,256]{4,3,2,1,0:T(8,128)(2,1)}, u32[]{:S(2)}) copy-start(bf16[2,2,2,256,256]{4,3,2,1,0:T(8,128)(2,1)} %constant.25.clone.table_ref) | copy-start | bytes 3145732
  25.8 12.4 %copy-start.8 = (f32[2,4,128,128]{3,2,1,0:T(8,128)}, f32[2,4,128,128]{3,2,1,0:T(8,128)S(1)}, u32[]{:S(2)}) copy-start(f32[2,4,128,128]{3,2,1,0:T(8,128)S(1)} %collective-permute-done.refs_1_) | copy-start | bytes 1572868
  38.2 0.8 copy-start.9
  62.7 59.8 %all-to-all-start.1 = ((f32[4,2,2,128,256]{4,3,2,1,0:T(8,128)}), f32[4,2,2,128,256]{4,3,2,1,0:T(8,128)S(1)}, u32[]{:S(2)}, u32[]{:S(2)}) async-start(f32[4,2,2,128,256]{4,3,2,1,0:T(8,128)} %first_z.1), calls=%async_computation.1 | async-start | bytes 4194304 | tf_op jit(solution)/shard_map/all_to_all | solution.py:450
  66.9 35.6 %collective-permute-start.3 = (f32[2,4,128,128]{3,2,1,0:T(8,128)}, f32[2,4,128,128]{3,2,1,0:T(8,128)S(1)}, u32[]{:S(2)}, u32[]{:S(2)}) collective-permute-start(f32[2,4,128,128]{3,2,1,0:T(8,128)} %get-tuple-element.58), channel_id=1, source_target_pairs={{0,4},{4,8},{8,12},{12,0},{1,5},{5,9},{9,13},{13,1},{2,6},{6,10},{... | collective-permute-start | bytes 1572872 | tf_op jit(solution)/shard_map/ppermute | solution.py:418
  68.4 45.7 %collective-permute-start.4 = (f32[2,4,128,128]{3,2,1,0:T(8,128)}, f32[2,4,128,128]{3,2,1,0:T(8,128)S(1)}, u32[]{:S(2)}, u32[]{:S(2)}) collective-permute-start(f32[2,4,128,128]{3,2,1,0:T(8,128)} %get-tuple-element.59), channel_id=1, source_target_pairs={{0,8},{4,12},{8,0},{12,4},{1,9},{5,13},{9,1},{13,5},{2,10},{6,14},... | collective-permute-start | bytes 1572872 | tf_op jit(solution)/shard_map/ppermute | solution.py:418
  70.8 43.3 %collective-permute-start.5 = (f32[2,4,128,128]{3,2,1,0:T(8,128)}, f32[2,4,128,128]{3,2,1,0:T(8,128)S(1)}, u32[]{:S(2)}, u32[]{:S(2)}) collective-permute-start(f32[2,4,128,128]{3,2,1,0:T(8,128)} %get-tuple-element.60), channel_id=1, source_target_pairs={{0,12},{4,0},{8,4},{12,8},{1,13},{5,1},{9,5},{13,9},{2,14},{6,2},{... | collective-permute-start | bytes 1572872 | tf_op jit(solution)/shard_map/ppermute | solution.py:418
  72.0 42.1 %collective-permute-start.7 = (f32[2,1,256,128]{3,2,1,0:T(8,128)}, f32[2,1,256,128]{3,2,1,0:T(8,128)S(1)}, u32[]{:S(2)}, u32[]{:S(2)}) collective-permute-start(f32[2,1,256,128]{3,2,1,0:T(8,128)} %get-tuple-element.61), channel_id=1, source_target_pairs={{0,3},{1,0},{2,1},{3,2},{4,7},{5,4},{6,5},{7,6},{8,11},{9,8},{10,9... | collective-permute-start | bytes 786440 | tf_op jit(solution)/shard_map/ppermute | solution.py:418
  72.0 42.1 %collective-permute-start.6 = (f32[2,1,256,128]{3,2,1,0:T(8,128)}, f32[2,1,256,128]{3,2,1,0:T(8,128)S(1)}, u32[]{:S(2)}, u32[]{:S(2)}) collective-permute-start(f32[2,1,256,128]{3,2,1,0:T(8,128)} %get-tuple-element.54), channel_id=1, source_target_pairs={{0,1},{1,2},{2,3},{3,0},{4,5},{5,6},{6,7},{7,4},{8,9},{9,10},{10,1... | collective-permute-start | bytes 786440 | tf_op jit(solution)/shard_map/ppermute | solution.py:418
  102.5 12.4 %copy-start.10 = (f32[2,4,128,128]{3,2,1,0:T(8,128)}, f32[2,4,128,128]{3,2,1,0:T(8,128)S(1)}, u32[]{:S(2)}) copy-start(f32[2,4,128,128]{3,2,1,0:T(8,128)S(1)} %collective-permute-done.3.refs_1_) | copy-start | bytes 1572868
  114.1 0.9 copy-start.11
  114.1 1.1 copy-start.12
  114.1 0.8 copy-start.5
  119.0 21.4 %collective-permute-start.10 = (f32[2,2,256,128]{3,2,1,0:T(8,128)}, f32[2,2,256,128]{3,2,1,0:T(8,128)}, u32[]{:S(2)}, u32[]{:S(2)}) collective-permute-start(f32[2,2,256,128]{3,2,1,0:T(8,128)} %get-tuple-element.69), channel_id=1, source_target_pairs={{0,2},{1,3},{2,0},{3,1},{4,6},{5,7},{6,4},{7,5},{8,10},{9,11},{10,... | collective-permute-start | bytes 1572872 | tf_op jit(solution)/shard_map/ppermute | solution.py:418
  119.1 21.3 %collective-permute-start.8 = (f32[2,1,256,128]{3,2,1,0:T(8,128)}, f32[2,1,256,128]{3,2,1,0:T(8,128)}, u32[]{:S(2)}, u32[]{:S(2)}) collective-permute-start(f32[2,1,256,128]{3,2,1,0:T(8,128)} %get-tuple-element.67), channel_id=1, source_target_pairs={{0,1},{1,2},{2,3},{3,0},{4,5},{5,6},{6,7},{7,4},{8,9},{9,10},{10,1... | collective-permute-start | bytes 786440 | tf_op jit(solution)/shard_map/ppermute | solution.py:418
  120.2 20.1 %collective-permute-start.9 = (f32[2,1,256,128]{3,2,1,0:T(8,128)}, f32[2,1,256,128]{3,2,1,0:T(8,128)}, u32[]{:S(2)}, u32[]{:S(2)}) collective-permute-start(f32[2,1,256,128]{3,2,1,0:T(8,128)} %get-tuple-element.68), channel_id=1, source_target_pairs={{0,3},{1,0},{2,1},{3,2},{4,7},{5,4},{6,5},{7,6},{8,11},{9,8},{10,9... | collective-permute-start | bytes 786440 | tf_op jit(solution)/shard_map/ppermute | solution.py:418
  122.5 17.8 %copy-start.2 = (bf16[2,2,2,256,256]{4,3,2,1,0:T(8,128)(2,1)S(1)}, bf16[2,2,2,256,256]{4,3,2,1,0:T(8,128)(2,1)}, u32[]{:S(2)}) copy-start(bf16[2,2,2,256,256]{4,3,2,1,0:T(8,128)(2,1)} %constant.25.clone.table_ref) | copy-start | bytes 3145732
  122.5 17.8 %copy-start.4 = (f32[2,2,256,128]{3,2,1,0:T(8,128)S(1)}, f32[2,2,256,128]{3,2,1,0:T(8,128)}, u32[]{:S(2)}) copy-start(f32[2,2,256,128]{3,2,1,0:T(8,128)} %get-tuple-element.71.b0) | copy-start | bytes 1572868
  122.5 17.8 %copy-start.6 = (f32[2,1,256,128]{3,2,1,0:T(8,128)S(1)}, f32[2,1,256,128]{3,2,1,0:T(8,128)}, u32[]{:S(2)}) copy-start(f32[2,1,256,128]{3,2,1,0:T(8,128)} %copy-done.5) | copy-start | bytes 786436
  144.0 35.6 %copy-start.3 = (bf16[2,2,256,512]{3,2,1,0:T(8,128)(2,1)S(1)}, bf16[2,2,256,512]{3,2,1,0:T(8,128)(2,1)}, u32[]{:S(2)}) copy-start(bf16[2,2,256,512]{3,2,1,0:T(8,128)(2,1)} %constant.23.clone.table_ref) | copy-start | bytes 3145732
  144.1 35.6 %copy-start.7 = (bf16[256,256]{1,0:T(8,128)(2,1)S(1)}, bf16[256,256]{1,0:T(8,128)(2,1)}, u32[]{:S(2)}) copy-start(bf16[256,256]{1,0:T(8,128)(2,1)} %constant.26.clone.ordering_ref) | copy-start | bytes 393220

commit v19 on v17

--- a/solution.py
+++ b/solution.py
@@ -481,7 +481,9 @@
     d1, d2, d3, c1, c3, _ = lax.optimization_barrier((d1, d2, d3, c1, c3, a1))
     a1, a3, a2 = shifted(a1, "gy", 1), shifted(a3, "gy", 3), shifted(a2, "gy", 2)
     d1, d3, b2, b0 = first_y(gy, gz, (d0, d1, d2, d3), table_y, (c2, c0))
-    d1, d3, b2 = shifted(d1, "gz", 1), shifted(d3, "gz", 3), shifted(b2, "gz", 2)
+    d1, b2 = shifted(d1, "gz", 1), shifted(b2, "gz", 2)
+    d3, d1 = lax.optimization_barrier((d3, d1))
+    d3 = shifted(d3, "gz", 3)
 
     part_a = part_y(gy, (a1, a3), table_y)
     done_b = second_z(gz, (b0, b2, c1, c3, d1, d3), table_z)

time: 175 us -> 177 us (1.011)
  waiting for transfers between devices: 42 us -> 44.7 us
    ppermute x14, waiting for transfers between devices: 29.8 us -> 35.5 us  [shifted(): lax.ppermute(piece, axis, [(i, (i + shift) % size) for i in range(size)])]
    all_to_all x1, waiting for transfers between devices: 12.2 us -> 9.24 us  [per_device(): a = lax.all_to_all(a, 'gz', split_axis=0, concat_axis=0, tiled=True)]
  transfers between devices with their start and end apart: 15 -> 15, of which waited for: 7 -> 10; matrix products, arithmetic and copies ran while one was open for 0% -> 0% of each run, Pallas kernels for 13% -> 11%
where the time goes in v19:
time: 177 us
  blocking collectives  75 us (42%)
  waiting for transfers between devices  44.7 us (25%)
  Pallas kernels  31 us (18%)
  starting transfers between devices  23.4 us (13%)
    all_to_all x1, blocking collectives, per_device(): lines = lax.all_to_all(planes, ALL, split_axis=0, concat_axis=0, tiled=True)  40.8 us
    ppermute x14, waiting for transfers between devices, shifted(): lax.ppermute(piece, axis, [(i, (i + shift) % size) for i in range(size)])  35.5 us
    all_to_all x1, blocking collectives, per_device(): lax.all_to_all(outgoing.reshape(128, 1, CAP, 2, BW), ALL, split_axis=0, c...  34.2 us
    ppermute x14, starting transfers between devices, shifted(): lax.ppermute(piece, axis, [(i, (i + shift) % size) for i in range(size)])  17.6 us
    pallas_call x5, Pallas kernels, scale(): pl.pallas_call(functools.partial(scale_kernel, part, shifts), in_specs=[p...  11.9 us
    all_to_all x1, waiting for transfers between devices, per_device(): a = lax.all_to_all(a, 'gz', split_axis=0, concat_axis=0, tiled=True)  9.24 us
    pallas_call x2, Pallas kernels, first_y(): pl.pallas_call(functools.partial(first_y_kernel, merge), in_specs=[pl.Blo...  7.43 us
    all_to_all x1, starting transfers between devices, per_device(): a = lax.all_to_all(a, 'gz', split_axis=0, concat_axis=0, tiled=True)  5.87 us
  transfers between devices with their start and end apart: 15, of which 10 were waited for; matrix products, arithmetic and copies ran while one was open for 0% of the time, Pallas kernels for 11%

profile of v19, /device:TPU:1, one launch (start us, length us, event | category | flops | bytes accessed | tf_op | source)
XLA Modules:
  0.0 176.7 jit_solution(18341175399456615061)
XLA Ops:
  0.0 3.4 %scale_a.1 = f32[4,2,8,128,128]{4,3,2,1,0:T(8,128)} custom-call(s32[1]{0:T(128)} %bitcast.place_ref.to_ref, bf16[2,8,8,128,128]{4,3,2,1,0:T(8,128)(2,1)} %bitcast.23, f32[8,8,128,128]{3,2,1,0:T(8,128)} %bitcast.28), custom_call_target="tpu_custom_call" | custom-call | flops 16 | bytes 128 | tf_op jit(solution)/shard_map/scale_a/pallas_call | solution.py:137
  3.4 5.9 %all-to-all-start = ((f32[4,2,8,128,128]{4,3,2,1,0:T(8,128)}), f32[4,2,8,128,128]{4,3,2,1,0:T(8,128)}, u32[]{:S(2)}, u32[]{:S(2)}) async-start(f32[4,2,8,128,128]{4,3,2,1,0:T(8,128)} %scale_a.1), calls=%async_computation | async-start | bytes 8388608 | tf_op jit(solution)/shard_map/all_to_all | solution.py:467
  9.3 2.3 %scale_b.4 = (f32[2,4,128,128]{3,2,1,0:T(8,128)}, f32[2,4,128,128]{3,2,1,0:T(8,128)}, f32[2,4,128,128]{3,2,1,0:T(8,128)}) custom-call(s32[1]{0:T(128)} %bitcast.3.place_ref.to_ref.y_ref, bf16[2,8,2,4,128,128]{5,4,3,2,1,0:T(8,128)(2,1)} %bitcast.24, f32[8,2,4,128,128]{4,3,2,1,0:T(8,128)} %bitcast.29), custom_call_target="tpu_custom_call" | custom-call | flops 12 | bytes 96 | tf_op jit(solution)/shard_map/scale_b/pallas_call | solution.py:137
  11.6 0.0 copy-start.9
  11.6 1.4 collective-permute-start
  13.0 2.6 %collective-permute-start.1 = (f32[2,4,128,128]{3,2,1,0:T(8,128)}, f32[2,4,128,128]{3,2,1,0:T(8,128)S(1)}, u32[]{:S(2)}, u32[]{:S(2)}) collective-permute-start(f32[2,4,128,128]{3,2,1,0:T(8,128)} %get-tuple-element.57), channel_id=1, source_target_pairs={{0,8},{4,12},{8,0},{12,4},{1,9},{5,13},{9,1},{13,5},{2,10},{6,14},... | collective-permute-start | bytes 1572872 | tf_op jit(solution)/shard_map/ppermute | solution.py:450
  15.6 1.1 collective-permute-start.2
  16.7 2.3 %scale_b.5 = (f32[2,4,128,128]{3,2,1,0:T(8,128)}, f32[2,4,128,128]{3,2,1,0:T(8,128)}, f32[2,4,128,128]{3,2,1,0:T(8,128)}) custom-call(s32[1]{0:T(128)} %bitcast.3.place_ref.to_ref.y_ref, bf16[2,8,2,4,128,128]{5,4,3,2,1,0:T(8,128)(2,1)} %bitcast.25, f32[8,2,4,128,128]{4,3,2,1,0:T(8,128)} %bitcast.30), custom_call_target="tpu_custom_call" | custom-call | flops 12 | bytes 96 | tf_op jit(solution)/shard_map/scale_b/pallas_call | solution.py:137
  19.0 0.5 collective-permute-start.5
  19.4 0.8 collective-permute-start.6
  20.2 0.1 copy.11
  20.3 0.2 fusion.2
  20.5 1.9 %scale_b.6.refs_0_ = f32[2,4,128,128]{3,2,1,0:T(8,128)} custom-call(s32[1]{0:T(128)} %bitcast.3.place_ref.to_ref.y_ref, bf16[2,8,2,4,128,128]{5,4,3,2,1,0:T(8,128)(2,1)} %bitcast.26, f32[8,2,4,128,128]{4,3,2,1,0:T(8,128)} %bitcast.31), custom_call_target="tpu_custom_call" | custom-call | flops 4 | bytes 32 | tf_op jit(solution)/shard_map/scale_b/pallas_call | solution.py:137
  22.4 0.0 copy-start
  22.5 3.3 %collective-permute-done.refs_1_ = f32[2,4,128,128]{3,2,1,0:T(8,128)S(1)} collective-permute-done((f32[2,4,128,128]{3,2,1,0:T(8,128)}, f32[2,4,128,128]{3,2,1,0:T(8,128)S(1)}, u32[]{:S(2)}, u32[]{:S(2)}) %collective-permute-start) | collective-permute-done | bytes 524320 | tf_op jit(solution)/shard_map/ppermute | solution.py:450
  25.8 1.4 collective-permute-start.7
  27.2 0.1 copy.12
  27.3 10.8 %collective-permute-done.1.refs_2_ = f32[2,4,128,128]{3,2,1,0:T(8,128)S(1)} collective-permute-done((f32[2,4,128,128]{3,2,1,0:T(8,128)}, f32[2,4,128,128]{3,2,1,0:T(8,128)S(1)}, u32[]{:S(2)}, u32[]{:S(2)}) %collective-permute-start.1) | collective-permute-done | bytes 524320 | tf_op jit(solution)/shard_map/ppermute | solution.py:450
  38.2 0.8 collective-permute-done.2.refs_3_
  39.0 0.0 copy-done.8
  39.0 3.6 %first_y.2 = (f32[2,1,256,128]{3,2,1,0:T(8,128)}, f32[2,1,256,128]{3,2,1,0:T(8,128)}, f32[2,1,256,128]{3,2,1,0:T(8,128)}, f32[2,1,256,128]{3,2,1,0:T(8,128)}) custom-call(s32[1]{0:T(128)} %bitcast.3.place_ref.to_ref.y_ref, s32[1]{0:T(128)} %bitcast.place_ref.to_ref, f32[2,4,128,128]{3,2,1,0:T(8,128)} %scale_b.6.refs_0_, f32[2,4,128,128]{3,2,1,0:T(8,128)} %copy-done.7, ...), custom_call_target="tpu_custom_call" | custom-call | flops 2048 | bytes 64 | tf_op jit(solution)/shard_map/first_y/pallas_call | solution.py:277
  42.7 4.0 %collective-permute-start.9 = (f32[2,1,256,128]{3,2,1,0:T(8,128)}, f32[2,1,256,128]{3,2,1,0:T(8,128)S(1)}, u32[]{:S(2)}, u32[]{:S(2)}) collective-permute-start(f32[2,1,256,128]{3,2,1,0:T(8,128)} %get-tuple-element.68), channel_id=1, source_target_pairs={{0,3},{1,0},{2,1},{3,2},{4,7},{5,4},{6,5},{7,6},{8,11},{9,8},{10,9... | collective-permute-start | bytes 786440 | tf_op jit(solution)/shard_map/ppermute | solution.py:450
  46.6 0.4 fusion.1
  47.0 0.0 copy-start.1
  47.0 2.0 %scale_b.7.refs_0_ = f32[2,4,128,128]{3,2,1,0:T(8,128)} custom-call(s32[1]{0:T(128)} %bitcast.3.place_ref.to_ref.y_ref, bf16[2,8,2,4,128,128]{5,4,3,2,1,0:T(8,128)(2,1)} %bitcast.27, f32[8,2,4,128,128]{4,3,2,1,0:T(8,128)} %bitcast.32), custom_call_target="tpu_custom_call" | custom-call | flops 4 | bytes 32 | tf_op jit(solution)/shard_map/scale_b/pallas_call | solution.py:137
  49.0 9.2 %all-to-all-done.in_ref = f32[4,2,8,128,128]{4,3,2,1,0:T(8,128)} async-done(((f32[4,2,8,128,128]{4,3,2,1,0:T(8,128)}), f32[4,2,8,128,128]{4,3,2,1,0:T(8,128)}, u32[]{:S(2)}, u32[]{:S(2)}) %all-to-all-start) | async-done | bytes 4194336 | tf_op jit(solution)/shard_map/all_to_all | solution.py:467
  58.2 4.5 %first_z.1 = (f32[2,2,128,256]{3,2,1,0:T(8,128)}, f32[2,2,128,256]{3,2,1,0:T(8,128)}, f32[2,2,128,256]{3,2,1,0:T(8,128)}, f32[2,2,128,256]{3,2,1,0:T(8,128)}) custom-call(s32[1]{0:T(128)} %bitcast.3.place_ref.to_ref.y_ref, f32[4,2,8,128,128]{4,3,2,1,0:T(8,128)} %all-to-all-done.in_ref, bf16[2,2,2,256,256]{4,3,2,1,0:T(8,128)(2,1)S(1)} %copy-done.1), custom_call_target="tpu_custom_call" | custom-call | flops 4096 | bytes 128 | tf_op jit(solution)/shard_map/first_z/pallas_call | solution.py:205
  62.7 0.0 copy-start.11
  62.8 2.0 %collective-permute-done.8.c1 = f32[2,1,256,128]{3,2,1,0:T(8,128)S(1)} collective-permute-done((f32[2,1,256,128]{3,2,1,0:T(8,128)}, f32[2,1,256,128]{3,2,1,0:T(8,128)S(1)}, u32[]{:S(2)}, u32[]{:S(2)}) %collective-permute-start.8) | collective-permute-done | bytes 262176 | tf_op jit(solution)/shard_map/ppermute | solution.py:450
  64.8 3.8 %first_y.3 = (f32[2,1,256,128]{3,2,1,0:T(8,128)}, f32[2,1,256,128]{3,2,1,0:T(8,128)}, f32[2,2,256,128]{3,2,1,0:T(8,128)}, f32[2,2,256,128]{3,2,1,0:T(8,128)}) custom-call(s32[1]{0:T(128)} %bitcast.3.place_ref.to_ref.y_ref, s32[1]{0:T(128)} %bitcast.place_ref.to_ref, f32[2,4,128,128]{3,2,1,0:T(8,128)} %scale_b.7.refs_0_, f32[2,4,128,128]{3,2,1,0:T(8,128)} %copy-done.6, ...), custom_call_target="tpu_custom_call" | custom-call | flops 2048 | bytes 64 | tf_op jit(solution)/shard_map/first_y/pallas_call | solution.py:277
  68.6 0.6 collective-permute-start.11
  69.2 2.7 %collective-permute-start.4 = (f32[2,2,128,256]{3,2,1,0:T(8,128)S(1)}, f32[2,2,128,256]{3,2,1,0:T(8,128)S(1)}, u32[]{:S(2)}, u32[]{:S(2)}) collective-permute-start(f32[2,2,128,256]{3,2,1,0:T(8,128)S(1)} %copy-done.12), channel_id=1, source_target_pairs={{0,12},{4,0},{8,4},{12,8},{1,13},{5,1},{9,5},{13,9},{2,14},{6,2},{... | collective-permute-start | bytes 1572872 | tf_op jit(solution)/shard_map/ppermute | solution.py:450
  71.9 0.9 collective-permute-start.10
  72.9 1.6 collective-permute-start.13
  74.5 2.5 %collective-permute-done.11.d1 = f32[2,1,256,128]{3,2,1,0:T(8,128)S(1)} collective-permute-done((f32[2,1,256,128]{3,2,1,0:T(8,128)}, f32[2,1,256,128]{3,2,1,0:T(8,128)S(1)}, u32[]{:S(2)}, u32[]{:S(2)}) %collective-permute-start.11) | collective-permute-done | bytes 262176 | tf_op jit(solution)/shard_map/ppermute | solution.py:450
  77.0 5.7 %collective-permute-done.4.p3 = f32[2,2,128,256]{3,2,1,0:T(8,128)S(1)} collective-permute-done((f32[2,2,128,256]{3,2,1,0:T(8,128)S(1)}, f32[2,2,128,256]{3,2,1,0:T(8,128)S(1)}, u32[]{:S(2)}, u32[]{:S(2)}) %collective-permute-start.4) | collective-permute-done | bytes 524320 | tf_op jit(solution)/shard_map/ppermute | solution.py:450
  82.7 3.1 %collective-permute-done.3.p1 = f32[2,2,128,256]{3,2,1,0:T(8,128)S(1)} collective-permute-done((f32[2,2,128,256]{3,2,1,0:T(8,128)S(1)}, f32[2,2,128,256]{3,2,1,0:T(8,128)S(1)}, u32[]{:S(2)}, u32[]{:S(2)}) %collective-permute-start.3) | collective-permute-done | bytes 524320 | tf_op jit(solution)/shard_map/ppermute | solution.py:450
  85.8 0.9 part_y.1.part_a
  86.8 3.4 %collective-permute-done.12.d3 = f32[2,1,256,128]{3,2,1,0:T(8,128)S(1)} collective-permute-done((f32[2,1,256,128]{3,2,1,0:T(8,128)}, f32[2,1,256,128]{3,2,1,0:T(8,128)S(1)}, u32[]{:S(2)}, u32[]{:S(2)}) %collective-permute-start.12) | collective-permute-done | bytes 262176 | tf_op jit(solution)/shard_map/ppermute | solution.py:450
  90.2 1.0 second_z.1.done_b
  91.3 3.8 %collective-permute-done.13.a2 = f32[2,2,128,256]{3,2,1,0:T(8,128)S(1)} collective-permute-done((f32[2,2,128,256]{3,2,1,0:T(8,128)S(1)}, f32[2,2,128,256]{3,2,1,0:T(8,128)S(1)}, u32[]{:S(2)}, u32[]{:S(2)}) %collective-permute-start.13) | collective-permute-done | bytes 524320 | tf_op jit(solution)/shard_map/ppermute | solution.py:450
  95.1 1.5 second.1
  96.6 0.0 copy-start.2
  96.6 0.0 copy-start.5
  96.6 40.8 %all_to_all.22.in_ref = f32[128,2,2,8,128]{4,3,2,1,0:T(8,128)S(1)} all-to-all(f32[128,2,2,8,128]{4,3,2,1,0:T(8,128)S(1)} %second.1), channel_id=1, replica_groups=mesh['gx'=8,'gy'=4,'gz'=4] {'gx','gy','gz'}, dimensions={0} | all-to-all | bytes 4194304 | tf_op jit(solution)/shard_map/all_to_all | solution.py:492
  137.4 3.7 %third.1 = f32[4096,128]{1,0:T(8,128)S(1)} custom-call(s32[1024]{0:T(1024)S(1)} %multiply_add_fusion.slot_ref, f32[128,2,2,8,128]{4,3,2,1,0:T(8,128)S(1)} %all_to_all.22.in_ref, bf16[2,2,256,512]{3,2,1,0:T(8,128)(2,1)S(1)} %copy-done.2, bf16[256,256]{1,0:T(8,128)(2,1)S(1)} %copy-done.5), custom_call_target="tpu_custom_call" | custom-call | flops 3072 | bytes 96 | tf_op jit(solution)/shard_map/third/pallas_call | solution.py:436
  141.1 34.2 %all_to_all.23 = f32[128,1,16,2,128]{4,3,2,1,0:T(2,128)S(1)} all-to-all(f32[128,1,16,2,128]{4,3,2,1,0:T(2,128)S(1)} %bitcast.22), channel_id=1, replica_groups=mesh['gx'=8,'gy'=4,'gz'=4] {'gx','gy','gz'}, dimensions={0} | all-to-all | bytes 4194304 | tf_op jit(solution)/shard_map/all_to_all | solution.py:494
  175.3 1.3 copy.15
  (32 shorter events, 0.1 us)
Async XLA Ops:
  3.4 54.8 %all-to-all-start = ((f32[4,2,8,128,128]{4,3,2,1,0:T(8,128)}), f32[4,2,8,128,128]{4,3,2,1,0:T(8,128)}, u32[]{:S(2)}, u32[]{:S(2)}) async-start(f32[4,2,8,128,128]{4,3,2,1,0:T(8,128)} %scale_a.1), calls=%async_computation | async-start | bytes 8388608 | tf_op jit(solution)/shard_map/all_to_all | solution.py:467
  11.6 8.6 %copy-start.9 = (s32[1024,1]{0,1:T(1,128)S(1)}, s32[1024,1]{0,1:T(1,128)}, u32[]{:S(2)}) copy-start(s32[1024,1]{0,1:T(1,128)} %param.9) | copy-start | bytes 12292
  11.6 14.2 %collective-permute-start = (f32[2,4,128,128]{3,2,1,0:T(8,128)}, f32[2,4,128,128]{3,2,1,0:T(8,128)S(1)}, u32[]{:S(2)}, u32[]{:S(2)}) collective-permute-start(f32[2,4,128,128]{3,2,1,0:T(8,128)} %get-tuple-element.56), channel_id=1, source_target_pairs={{0,4},{4,8},{8,12},{12,0},{1,5},{5,9},{9,13},{13,1},{2,6},{6,10},{... | collective-permute-start | bytes 1572872 | tf_op jit(solution)/shard_map/ppermute | solution.py:450
  13.0 25.2 %collective-permute-start.1 = (f32[2,4,128,128]{3,2,1,0:T(8,128)}, f32[2,4,128,128]{3,2,1,0:T(8,128)S(1)}, u32[]{:S(2)}, u32[]{:S(2)}) collective-permute-start(f32[2,4,128,128]{3,2,1,0:T(8,128)} %get-tuple-element.57), channel_id=1, source_target_pairs={{0,8},{4,12},{8,0},{12,4},{1,9},{5,13},{9,1},{13,5},{2,10},{6,14},... | collective-permute-start | bytes 1572872 | tf_op jit(solution)/shard_map/ppermute | solution.py:450
  15.6 23.4 %collective-permute-start.2 = (f32[2,4,128,128]{3,2,1,0:T(8,128)}, f32[2,4,128,128]{3,2,1,0:T(8,128)}, u32[]{:S(2)}, u32[]{:S(2)}) collective-permute-start(f32[2,4,128,128]{3,2,1,0:T(8,128)} %get-tuple-element.58), channel_id=1, source_target_pairs={{0,12},{4,0},{8,4},{12,8},{1,13},{5,1},{9,5},{13,9},{2,14},{6,2},{... | collective-permute-start | bytes 1572872 | tf_op jit(solution)/shard_map/ppermute | solution.py:450
  19.0 43.8 %collective-permute-start.5 = (f32[2,4,128,128]{3,2,1,0:T(8,128)}, f32[2,4,128,128]{3,2,1,0:T(8,128)S(1)}, u32[]{:S(2)}, u32[]{:S(2)}) collective-permute-start(f32[2,4,128,128]{3,2,1,0:T(8,128)} %get-tuple-element.65), channel_id=1, source_target_pairs={{0,4},{4,8},{8,12},{12,0},{1,5},{5,9},{9,13},{13,1},{2,6},{6,10},{... | collective-permute-start | bytes 1572872 | tf_op jit(solution)/shard_map/ppermute | solution.py:450
  19.4 43.4 %collective-permute-start.6 = (f32[2,4,128,128]{3,2,1,0:T(8,128)}, f32[2,4,128,128]{3,2,1,0:T(8,128)}, u32[]{:S(2)}, u32[]{:S(2)}) collective-permute-start(f32[2,4,128,128]{3,2,1,0:T(8,128)} %get-tuple-element.66), channel_id=1, source_target_pairs={{0,8},{4,12},{8,0},{12,4},{1,9},{5,13},{9,1},{13,5},{2,10},{6,14},... | collective-permute-start | bytes 1572872 | tf_op jit(solution)/shard_map/ppermute | solution.py:450
  22.4 16.6 %copy-start = (bf16[2,2,2,256,256]{4,3,2,1,0:T(8,128)(2,1)S(1)}, bf16[2,2,2,256,256]{4,3,2,1,0:T(8,128)(2,1)}, u32[]{:S(2)}) copy-start(bf16[2,2,2,256,256]{4,3,2,1,0:T(8,128)(2,1)} %constant.24.clone.refs_4_.table_ref.refs_6_.table_y_ref) | copy-start | bytes 3145732
  25.8 13.2 %copy-start.7 = (f32[2,4,128,128]{3,2,1,0:T(8,128)}, f32[2,4,128,128]{3,2,1,0:T(8,128)S(1)}, u32[]{:S(2)}) copy-start(f32[2,4,128,128]{3,2,1,0:T(8,128)S(1)} %collective-permute-done.refs_1_) | copy-start | bytes 1572868
  25.8 37.0 %collective-permute-start.7 = (f32[2,4,128,128]{3,2,1,0:T(8,128)}, f32[2,4,128,128]{3,2,1,0:T(8,128)}, u32[]{:S(2)}, u32[]{:S(2)}) collective-permute-start(f32[2,4,128,128]{3,2,1,0:T(8,128)} %get-tuple-element.67), channel_id=1, source_target_pairs={{0,12},{4,0},{8,4},{12,8},{1,13},{5,1},{9,5},{13,9},{2,14},{6,2},{... | collective-permute-start | bytes 1572872 | tf_op jit(solution)/shard_map/ppermute | solution.py:450
  38.2 0.8 copy-start.8
  42.7 20.2 %collective-permute-start.9 = (f32[2,1,256,128]{3,2,1,0:T(8,128)}, f32[2,1,256,128]{3,2,1,0:T(8,128)S(1)}, u32[]{:S(2)}, u32[]{:S(2)}) collective-permute-start(f32[2,1,256,128]{3,2,1,0:T(8,128)} %get-tuple-element.68), channel_id=1, source_target_pairs={{0,3},{1,0},{2,1},{3,2},{4,7},{5,4},{6,5},{7,6},{8,11},{9,8},{10,9... | collective-permute-start | bytes 786440 | tf_op jit(solution)/shard_map/ppermute | solution.py:450
  46.6 18.2 %collective-permute-start.8 = (f32[2,1,256,128]{3,2,1,0:T(8,128)}, f32[2,1,256,128]{3,2,1,0:T(8,128)S(1)}, u32[]{:S(2)}, u32[]{:S(2)}) collective-permute-start(f32[2,1,256,128]{3,2,1,0:T(8,128)} %get-tuple-element.59), channel_id=1, source_target_pairs={{0,1},{1,2},{2,3},{3,0},{4,5},{5,6},{6,7},{7,4},{8,9},{9,10},{10,1... | collective-permute-start | bytes 786440 | tf_op jit(solution)/shard_map/ppermute | solution.py:450
  47.0 11.3 %copy-start.1 = (bf16[2,2,2,256,256]{4,3,2,1,0:T(8,128)(2,1)S(1)}, bf16[2,2,2,256,256]{4,3,2,1,0:T(8,128)(2,1)}, u32[]{:S(2)}) copy-start(bf16[2,2,2,256,256]{4,3,2,1,0:T(8,128)(2,1)} %constant.25.clone.table_ref) | copy-start | bytes 3145732
  62.7 6.5 %copy-start.12 = (f32[2,2,128,256]{3,2,1,0:T(8,128)S(1)}, f32[2,2,128,256]{3,2,1,0:T(8,128)}, u32[]{:S(2)}) copy-start(f32[2,2,128,256]{3,2,1,0:T(8,128)} %get-tuple-element.63) | copy-start | bytes 1572868
  62.7 9.2 %copy-start.11 = (f32[2,2,128,256]{3,2,1,0:T(8,128)S(1)}, f32[2,2,128,256]{3,2,1,0:T(8,128)}, u32[]{:S(2)}) copy-start(f32[2,2,128,256]{3,2,1,0:T(8,128)} %get-tuple-element.62) | copy-start | bytes 1572868
  62.8 10.1 %copy-start.10 = (f32[2,2,128,256]{3,2,1,0:T(8,128)S(1)}, f32[2,2,128,256]{3,2,1,0:T(8,128)}, u32[]{:S(2)}) copy-start(f32[2,2,128,256]{3,2,1,0:T(8,128)} %get-tuple-element.82) | copy-start | bytes 1572868
  62.8 2.0 %copy-start.6 = (f32[2,4,128,128]{3,2,1,0:T(8,128)}, f32[2,4,128,128]{3,2,1,0:T(8,128)S(1)}, u32[]{:S(2)}) copy-start(f32[2,4,128,128]{3,2,1,0:T(8,128)S(1)} %collective-permute-done.5.refs_1_) | copy-start | bytes 1572868
  68.6 21.6 %copy-start.4 = (f32[2,2,256,128]{3,2,1,0:T(8,128)S(1)}, f32[2,2,256,128]{3,2,1,0:T(8,128)}, u32[]{:S(2)}) copy-start(f32[2,2,256,128]{3,2,1,0:T(8,128)} %get-tuple-element.74.b0) | copy-start | bytes 1572868
  68.6 8.4 %collective-permute-start.11 = (f32[2,1,256,128]{3,2,1,0:T(8,128)}, f32[2,1,256,128]{3,2,1,0:T(8,128)S(1)}, u32[]{:S(2)}, u32[]{:S(2)}) collective-permute-start(f32[2,1,256,128]{3,2,1,0:T(8,128)} %get-tuple-element.79), channel_id=1, source_target_pairs={{0,1},{1,2},{2,3},{3,0},{4,5},{5,6},{6,7},{7,4},{8,9},{9,10},{10,1... | collective-permute-start | bytes 786440 | tf_op jit(solution)/shard_map/ppermute | solution.py:450
  69.2 13.5 %collective-permute-start.4 = (f32[2,2,128,256]{3,2,1,0:T(8,128)S(1)}, f32[2,2,128,256]{3,2,1,0:T(8,128)S(1)}, u32[]{:S(2)}, u32[]{:S(2)}) collective-permute-start(f32[2,2,128,256]{3,2,1,0:T(8,128)S(1)} %copy-done.12), channel_id=1, source_target_pairs={{0,12},{4,0},{8,4},{12,8},{1,13},{5,1},{9,5},{13,9},{2,14},{6,2},{... | collective-permute-start | bytes 1572872 | tf_op jit(solution)/shard_map/ppermute | solution.py:450
  71.9 13.9 %collective-permute-start.3 = (f32[2,2,128,256]{3,2,1,0:T(8,128)S(1)}, f32[2,2,128,256]{3,2,1,0:T(8,128)S(1)}, u32[]{:S(2)}, u32[]{:S(2)}) collective-permute-start(f32[2,2,128,256]{3,2,1,0:T(8,128)S(1)} %copy-done.11), channel_id=1, source_target_pairs={{0,4},{4,8},{8,12},{12,0},{1,5},{5,9},{9,13},{13,1},{2,6},{6,10},{... | collective-permute-start | bytes 1572872 | tf_op jit(solution)/shard_map/ppermute | solution.py:450
  71.9 18.3 %collective-permute-start.10 = (f32[2,2,256,128]{3,2,1,0:T(8,128)}, f32[2,2,256,128]{3,2,1,0:T(8,128)S(1)}, u32[]{:S(2)}, u32[]{:S(2)}) collective-permute-start(f32[2,2,256,128]{3,2,1,0:T(8,128)} %get-tuple-element.75), channel_id=1, source_target_pairs={{0,2},{1,3},{2,0},{3,1},{4,6},{5,7},{6,4},{7,5},{8,10},{9,11},{10,... | collective-permute-start | bytes 1572872 | tf_op jit(solution)/shard_map/ppermute | solution.py:450
  72.9 22.2 %collective-permute-start.13 = (f32[2,2,128,256]{3,2,1,0:T(8,128)S(1)}, f32[2,2,128,256]{3,2,1,0:T(8,128)S(1)}, u32[]{:S(2)}, u32[]{:S(2)}) collective-permute-start(f32[2,2,128,256]{3,2,1,0:T(8,128)S(1)} %copy-done.10), channel_id=1, source_target_pairs={{0,8},{4,12},{8,0},{12,4},{1,9},{5,13},{9,1},{13,5},{2,10},{6,14},... | collective-permute-start | bytes 1572872 | tf_op jit(solution)/shard_map/ppermute | solution.py:450
  77.0 13.2 %collective-permute-start.12 = (f32[2,1,256,128]{3,2,1,0:T(8,128)}, f32[2,1,256,128]{3,2,1,0:T(8,128)S(1)}, u32[]{:S(2)}, u32[]{:S(2)}) collective-permute-start(f32[2,1,256,128]{3,2,1,0:T(8,128)} %get-tuple-element.81), channel_id=1, source_target_pairs={{0,3},{1,0},{2,1},{3,2},{4,7},{5,4},{6,5},{7,6},{8,11},{9,8},{10,9... | collective-permute-start | bytes 786440 | tf_op jit(solution)/shard_map/ppermute | solution.py:450
  90.2 4.8 %copy-start.3 = (f32[2,2,128,256]{3,2,1,0:T(8,128)S(1)}, f32[2,2,128,256]{3,2,1,0:T(8,128)}, u32[]{:S(2)}) copy-start(f32[2,2,128,256]{3,2,1,0:T(8,128)} %get-tuple-element.84.a0) | copy-start | bytes 1572868
  96.6 40.8 %copy-start.2 = (bf16[2,2,256,512]{3,2,1,0:T(8,128)(2,1)S(1)}, bf16[2,2,256,512]{3,2,1,0:T(8,128)(2,1)}, u32[]{:S(2)}) copy-start(bf16[2,2,256,512]{3,2,1,0:T(8,128)(2,1)} %constant.23.clone.table_ref) | copy-start | bytes 3145732
  96.6 40.8 %copy-start.5 = (bf16[256,256]{1,0:T(8,128)(2,1)S(1)}, bf16[256,256]{1,0:T(8,128)(2,1)}, u32[]{:S(2)}) copy-start(bf16[256,256]{1,0:T(8,128)(2,1)} %constant.26.clone.ordering_ref) | copy-start | bytes 393220

commit v20 on v17

--- a/solution.py
+++ b/solution.py
@@ -293,8 +293,8 @@
     )(place, to, *operands, table)
 
 
-def part_y_kernel(place_ref, p1, p3, table_ref, out_ref):
-    pairs = [(p1[...], p3[...], lax.rem(place_ref[0] + 3, 4))]
+def part_y_kernel(place_ref, p0, p2, table_ref, out_ref):
+    pairs = [(p0[...], p2[...], place_ref[0])]
     for odd, values in enumerate(transform(False, pairs, table_ref)):
         out_ref[odd] = values
 
@@ -339,18 +339,19 @@
 
 
 def second_kernel(
-    y_ref, part_a, a0, a2, table_y_ref, done_b, out_ref, held
+    y_ref, part_a, a1, a3, table_y_ref, done_b, out_ref, held
 ):
     odd = pl.program_id(0)
 
     def put(values, half, row):
         held[pl.ds(half * 8 + row, 128, stride=16), :] = values
 
-    base = lax.rem(y_ref[0], 2)
+    g = lax.rem(y_ref[0] + 3, 4)
+    base = lax.rem(g, 2)
     flip = jnp.where(odd == 0, 1.0, -1.0).astype(jnp.float32)
-    sign = jnp.where((odd == 0) | (y_ref[0] < 2), 1.0, -1.0).astype(jnp.float32)
+    sign = jnp.where((odd == 0) | (g < 2), 1.0, -1.0).astype(jnp.float32)
     table = (table_y_ref[0, base, 0], table_y_ref[1, base, 0])
-    values = part_a[0] + product(table, columns_y((a0[...] + flip * a2[...]) * sign))
+    values = part_a[0] + product(table, columns_y((a1[...] + flip * a3[...]) * sign))
     for plane in range(2):
         for x in range(2):
             for half in range(2):
@@ -477,16 +478,17 @@
     c1, c3, c2, c0 = first_y(gy, gz, (c0, c1, c2, c3), table_y)
     a, slots, _, d0 = lax.optimization_barrier((a, slots_of(block_owner), c1, d0))
     c1, c3 = shifted(c1, "gz", 1), shifted(c3, "gz", 3)
-    a1, a3, a2, a0 = first_z((1, 3, 2, 0), gy, a, table_z)
-    d1, d2, d3, c1, c3, _ = lax.optimization_barrier((d1, d2, d3, c1, c3, a1))
+    a2, a1, a3, a0 = first_z((2, 1, 3, 0), gy, a, table_z)
+    d1, d2, d3, c1, c3, _ = lax.optimization_barrier((d1, d2, d3, c1, c3, a2))
     a1, a3, a2 = shifted(a1, "gy", 1), shifted(a3, "gy", 3), shifted(a2, "gy", 2)
     d1, d3, b2, b0 = first_y(gy, gz, (d0, d1, d2, d3), table_y, (c2, c0))
     d1, d3, b2 = shifted(d1, "gz", 1), shifted(d3, "gz", 3), shifted(b2, "gz", 2)
 
-    part_a = part_y(gy, (a1, a3), table_y)
+    part_a = part_y(gy, (a0, a2), table_y)
+    part_a, b2 = lax.optimization_barrier((part_a, b2))
     done_b = second_z(gz, (b0, b2, c1, c3, d1, d3), table_z)
-    part_a, done_b, a2 = lax.optimization_barrier((part_a, done_b, a2))
-    planes = second(gy, part_a, (a0, a2), table_y, done_b)
+    part_a, done_b, a1, a3 = lax.optimization_barrier((part_a, done_b, a1, a3))
+    planes = second(gy, part_a, (a1, a3), table_y, done_b)
     lines = lax.all_to_all(planes, ALL, split_axis=0, concat_axis=0, tiled=True)
     outgoing = third(slots, lines, table_x, ordering)
     return lax.all_to_all(

time: 175 us -> 169 us (0.966)
  blocking collectives: 76.5 us -> 70.4 us
  waiting for transfers between devices: 42 us -> 39.8 us
    all_to_all x1, blocking collectives: 42.3 us -> 36.2 us  [per_device(): lines = lax.all_to_all(planes, ALL, split_axis=0, concat_axis=0, tiled=True)]
    all_to_all x1, waiting for transfers between devices: 12.2 us -> 8.78 us  [per_device(): a = lax.all_to_all(a, 'gz', split_axis=0, concat_axis=0, tiled=True)]
where the time goes in v20:
time: 169 us
  blocking collectives  70.4 us (42%)
  waiting for transfers between devices  39.8 us (24%)
  Pallas kernels  31.2 us (18%)
  starting transfers between devices  24.2 us (14%)
  local copies, waits for them, and re-layouts  2.41 us (1%)
    all_to_all x1, blocking collectives, per_device(): lines = lax.all_to_all(planes, ALL, split_axis=0, concat_axis=0, tiled=True)  36.2 us
    all_to_all x1, blocking collectives, per_device(): lax.all_to_all(outgoing.reshape(128, 1, CAP, 2, BW), ALL, split_axis=0, c...  34.2 us
    ppermute x14, waiting for transfers between devices, shifted(): lax.ppermute(piece, axis, [(i, (i + shift) % size) for i in range(size)])  31.1 us
    ppermute x14, starting transfers between devices, shifted(): lax.ppermute(piece, axis, [(i, (i + shift) % size) for i in range(size)])  18.4 us
    pallas_call x5, Pallas kernels, scale(): pl.pallas_call(functools.partial(scale_kernel, part, shifts), in_specs=[p...  12 us
    all_to_all x1, waiting for transfers between devices, per_device(): a = lax.all_to_all(a, 'gz', split_axis=0, concat_axis=0, tiled=True)  8.78 us
    pallas_call x2, Pallas kernels, first_y(): pl.pallas_call(functools.partial(first_y_kernel, merge), in_specs=[pl.Blo...  7.49 us
    all_to_all x1, starting transfers between devices, per_device(): a = lax.all_to_all(a, 'gz', split_axis=0, concat_axis=0, tiled=True)  5.87 us
  transfers between devices with their start and end apart: 15, of which 7 were waited for; matrix products, arithmetic and copies ran while one was open for 0% of the time, Pallas kernels for 13%

profile of v20, /device:TPU:1, one launch (start us, length us, event | category | flops | bytes accessed | tf_op | source)
XLA Modules:
  0.0 168.9 jit_solution(18142789757407180941)
XLA Ops:
  0.0 3.4 %scale_a.1 = f32[4,2,8,128,128]{4,3,2,1,0:T(8,128)} custom-call(s32[1]{0:T(128)} %bitcast.place_ref.to_ref, bf16[2,8,8,128,128]{4,3,2,1,0:T(8,128)(2,1)} %bitcast.23, f32[8,8,128,128]{3,2,1,0:T(8,128)} %bitcast.28), custom_call_target="tpu_custom_call" | custom-call | flops 16 | bytes 128 | tf_op jit(solution)/shard_map/scale_a/pallas_call | solution.py:137
  3.4 5.9 %all-to-all-start = ((f32[4,2,8,128,128]{4,3,2,1,0:T(8,128)}), f32[4,2,8,128,128]{4,3,2,1,0:T(8,128)}, u32[]{:S(2)}, u32[]{:S(2)}) async-start(f32[4,2,8,128,128]{4,3,2,1,0:T(8,128)} %scale_a.1), calls=%async_computation | async-start | bytes 8388608 | tf_op jit(solution)/shard_map/all_to_all | solution.py:468
  9.3 2.3 %scale_b.4 = (f32[2,4,128,128]{3,2,1,0:T(8,128)}, f32[2,4,128,128]{3,2,1,0:T(8,128)}, f32[2,4,128,128]{3,2,1,0:T(8,128)}) custom-call(s32[1]{0:T(128)} %bitcast.3.place_ref.to_ref.y_ref, bf16[2,8,2,4,128,128]{5,4,3,2,1,0:T(8,128)(2,1)} %bitcast.24, f32[8,2,4,128,128]{4,3,2,1,0:T(8,128)} %bitcast.29), custom_call_target="tpu_custom_call" | custom-call | flops 12 | bytes 96 | tf_op jit(solution)/shard_map/scale_b/pallas_call | solution.py:137
  11.6 0.0 copy-start.10
  11.6 1.4 collective-permute-start
  13.0 2.6 %collective-permute-start.1 = (f32[2,4,128,128]{3,2,1,0:T(8,128)}, f32[2,4,128,128]{3,2,1,0:T(8,128)S(1)}, u32[]{:S(2)}, u32[]{:S(2)}) collective-permute-start(f32[2,4,128,128]{3,2,1,0:T(8,128)} %get-tuple-element.58), channel_id=1, source_target_pairs={{0,8},{4,12},{8,0},{12,4},{1,9},{5,13},{9,1},{13,5},{2,10},{6,14},... | collective-permute-start | bytes 1572872 | tf_op jit(solution)/shard_map/ppermute | solution.py:451
  15.6 1.1 collective-permute-start.2
  16.7 2.3 %scale_b.5 = (f32[2,4,128,128]{3,2,1,0:T(8,128)}, f32[2,4,128,128]{3,2,1,0:T(8,128)}, f32[2,4,128,128]{3,2,1,0:T(8,128)}) custom-call(s32[1]{0:T(128)} %bitcast.3.place_ref.to_ref.y_ref, bf16[2,8,2,4,128,128]{5,4,3,2,1,0:T(8,128)(2,1)} %bitcast.25, f32[8,2,4,128,128]{4,3,2,1,0:T(8,128)} %bitcast.30), custom_call_target="tpu_custom_call" | custom-call | flops 12 | bytes 96 | tf_op jit(solution)/shard_map/scale_b/pallas_call | solution.py:137
  19.0 0.5 collective-permute-start.4
  19.4 0.8 collective-permute-start.5
  20.2 0.1 copy.11
  20.3 0.2 fusion.2
  20.6 0.1 copy.12
  20.7 5.1 %collective-permute-done.refs_1_ = f32[2,4,128,128]{3,2,1,0:T(8,128)S(1)} collective-permute-done((f32[2,4,128,128]{3,2,1,0:T(8,128)}, f32[2,4,128,128]{3,2,1,0:T(8,128)S(1)}, u32[]{:S(2)}, u32[]{:S(2)}) %collective-permute-start) | collective-permute-done | bytes 524320 | tf_op jit(solution)/shard_map/ppermute | solution.py:451
  25.8 1.4 collective-permute-start.6
  27.2 0.4 fusion.1
  27.6 0.0 copy-start
  27.6 2.0 %scale_b.6.refs_0_ = f32[2,4,128,128]{3,2,1,0:T(8,128)} custom-call(s32[1]{0:T(128)} %bitcast.3.place_ref.to_ref.y_ref, bf16[2,8,2,4,128,128]{5,4,3,2,1,0:T(8,128)(2,1)} %bitcast.26, f32[8,2,4,128,128]{4,3,2,1,0:T(8,128)} %bitcast.31), custom_call_target="tpu_custom_call" | custom-call | flops 4 | bytes 32 | tf_op jit(solution)/shard_map/scale_b/pallas_call | solution.py:137
  29.6 8.6 %collective-permute-done.1.refs_2_ = f32[2,4,128,128]{3,2,1,0:T(8,128)S(1)} collective-permute-done((f32[2,4,128,128]{3,2,1,0:T(8,128)}, f32[2,4,128,128]{3,2,1,0:T(8,128)S(1)}, u32[]{:S(2)}, u32[]{:S(2)}) %collective-permute-start.1) | collective-permute-done | bytes 524320 | tf_op jit(solution)/shard_map/ppermute | solution.py:451
  38.2 0.8 collective-permute-done.2.refs_3_
  39.0 0.0 copy-done.8
  39.0 0.8 copy-done.9
  39.8 3.7 %first_y.2 = (f32[2,1,256,128]{3,2,1,0:T(8,128)}, f32[2,1,256,128]{3,2,1,0:T(8,128)}, f32[2,1,256,128]{3,2,1,0:T(8,128)}, f32[2,1,256,128]{3,2,1,0:T(8,128)}) custom-call(s32[1]{0:T(128)} %bitcast.3.place_ref.to_ref.y_ref, s32[1]{0:T(128)} %bitcast.place_ref.to_ref, f32[2,4,128,128]{3,2,1,0:T(8,128)} %scale_b.6.refs_0_, f32[2,4,128,128]{3,2,1,0:T(8,128)} %copy-done.7, ...), custom_call_target="tpu_custom_call" | custom-call | flops 2048 | bytes 64 | tf_op jit(solution)/shard_map/first_y/pallas_call | solution.py:277
  43.5 4.0 %collective-permute-start.8 = (f32[2,1,256,128]{3,2,1,0:T(8,128)}, f32[2,1,256,128]{3,2,1,0:T(8,128)S(1)}, u32[]{:S(2)}, u32[]{:S(2)}) collective-permute-start(f32[2,1,256,128]{3,2,1,0:T(8,128)} %get-tuple-element.69), channel_id=1, source_target_pairs={{0,3},{1,0},{2,1},{3,2},{4,7},{5,4},{6,5},{7,6},{8,11},{9,8},{10,9... | collective-permute-start | bytes 786440 | tf_op jit(solution)/shard_map/ppermute | solution.py:451
  47.4 0.0 collective-permute-start.7
  47.5 2.0 %scale_b.7.refs_0_ = f32[2,4,128,128]{3,2,1,0:T(8,128)} custom-call(s32[1]{0:T(128)} %bitcast.3.place_ref.to_ref.y_ref, bf16[2,8,2,4,128,128]{5,4,3,2,1,0:T(8,128)(2,1)} %bitcast.27, f32[8,2,4,128,128]{4,3,2,1,0:T(8,128)} %bitcast.32), custom_call_target="tpu_custom_call" | custom-call | flops 4 | bytes 32 | tf_op jit(solution)/shard_map/scale_b/pallas_call | solution.py:137
  49.4 8.8 %all-to-all-done.in_ref = f32[4,2,8,128,128]{4,3,2,1,0:T(8,128)} async-done(((f32[4,2,8,128,128]{4,3,2,1,0:T(8,128)}), f32[4,2,8,128,128]{4,3,2,1,0:T(8,128)}, u32[]{:S(2)}, u32[]{:S(2)}) %all-to-all-start) | async-done | bytes 4194336 | tf_op jit(solution)/shard_map/all_to_all | solution.py:468
  58.2 4.5 %first_z.1 = (f32[2,2,128,256]{3,2,1,0:T(8,128)}, f32[2,2,128,256]{3,2,1,0:T(8,128)}, f32[2,2,128,256]{3,2,1,0:T(8,128)}, f32[2,2,128,256]{3,2,1,0:T(8,128)}) custom-call(s32[1]{0:T(128)} %bitcast.3.place_ref.to_ref.y_ref, f32[4,2,8,128,128]{4,3,2,1,0:T(8,128)} %all-to-all-done.in_ref, bf16[2,2,2,256,256]{4,3,2,1,0:T(8,128)(2,1)S(1)} %copy-done.1), custom_call_target="tpu_custom_call" | custom-call | flops 4096 | bytes 128 | tf_op jit(solution)/shard_map/first_z/pallas_call | solution.py:205
  62.8 3.0 %collective-permute-start.3 = (f32[2,2,128,256]{3,2,1,0:T(8,128)}, f32[2,2,128,256]{3,2,1,0:T(8,128)S(1)}, u32[]{:S(2)}, u32[]{:S(2)}) collective-permute-start(f32[2,2,128,256]{3,2,1,0:T(8,128)} %get-tuple-element.64), channel_id=1, source_target_pairs={{0,8},{4,12},{8,0},{12,4},{1,9},{5,13},{9,1},{13,5},{2,10},{6,14},... | collective-permute-start | bytes 1572872 | tf_op jit(solution)/shard_map/ppermute | solution.py:451
  65.8 0.0 collective-permute-done.8.c3
  65.8 3.8 %first_y.3 = (f32[2,1,256,128]{3,2,1,0:T(8,128)}, f32[2,1,256,128]{3,2,1,0:T(8,128)}, f32[2,2,256,128]{3,2,1,0:T(8,128)}, f32[2,2,256,128]{3,2,1,0:T(8,128)}) custom-call(s32[1]{0:T(128)} %bitcast.3.place_ref.to_ref.y_ref, s32[1]{0:T(128)} %bitcast.place_ref.to_ref, f32[2,4,128,128]{3,2,1,0:T(8,128)} %scale_b.7.refs_0_, f32[2,4,128,128]{3,2,1,0:T(8,128)} %copy-done.6, ...), custom_call_target="tpu_custom_call" | custom-call | flops 2048 | bytes 64 | tf_op jit(solution)/shard_map/first_y/pallas_call | solution.py:277
  69.6 0.1 collective-permute-start.9
  69.7 0.5 collective-permute-start.12
  70.2 2.3 %collective-permute-start.13 = (f32[2,2,128,256]{3,2,1,0:T(8,128)S(1)}, f32[2,2,128,256]{3,2,1,0:T(8,128)S(1)}, u32[]{:S(2)}, u32[]{:S(2)}) collective-permute-start(f32[2,2,128,256]{3,2,1,0:T(8,128)S(1)} %copy-done.11), channel_id=1, source_target_pairs={{0,12},{4,0},{8,4},{12,8},{1,13},{5,1},{9,5},{13,9},{2,14},{6,2},{... | collective-permute-start | bytes 1572872 | tf_op jit(solution)/shard_map/ppermute | solution.py:451
  72.5 0.9 collective-permute-start.10
  73.3 2.3 %collective-permute-done.3.p2 = f32[2,2,128,256]{3,2,1,0:T(8,128)S(1)} collective-permute-done((f32[2,2,128,256]{3,2,1,0:T(8,128)}, f32[2,2,128,256]{3,2,1,0:T(8,128)S(1)}, u32[]{:S(2)}, u32[]{:S(2)}) %collective-permute-start.3) | collective-permute-done | bytes 524320 | tf_op jit(solution)/shard_map/ppermute | solution.py:451
  75.7 0.0 collective-permute-start.11
  75.7 0.9 part_y.1.part_a
  76.6 5.6 %collective-permute-done.9.b2 = f32[2,2,256,128]{3,2,1,0:T(8,128)S(1)} collective-permute-done((f32[2,2,256,128]{3,2,1,0:T(8,128)}, f32[2,2,256,128]{3,2,1,0:T(8,128)S(1)}, u32[]{:S(2)}, u32[]{:S(2)}) %collective-permute-start.9) | collective-permute-done | bytes 524320 | tf_op jit(solution)/shard_map/ppermute | solution.py:451
  82.2 8.7 %collective-permute-done.10.d1 = f32[2,1,256,128]{3,2,1,0:T(8,128)S(1)} collective-permute-done((f32[2,1,256,128]{3,2,1,0:T(8,128)}, f32[2,1,256,128]{3,2,1,0:T(8,128)S(1)}, u32[]{:S(2)}, u32[]{:S(2)}) %collective-permute-start.10) | collective-permute-done | bytes 262176 | tf_op jit(solution)/shard_map/ppermute | solution.py:451
  90.9 1.0 second_z.1.done_b
  91.9 1.5 second.1
  93.5 0.0 copy-start.2
  93.5 0.0 copy-start.5
  93.5 36.2 %all_to_all.22.in_ref = f32[128,2,2,8,128]{4,3,2,1,0:T(8,128)S(1)} all-to-all(f32[128,2,2,8,128]{4,3,2,1,0:T(8,128)S(1)} %second.1), channel_id=1, replica_groups=mesh['gx'=8,'gy'=4,'gz'=4] {'gx','gy','gz'}, dimensions={0} | all-to-all | bytes 4194304 | tf_op jit(solution)/shard_map/all_to_all | solution.py:492
  129.7 3.7 %third.1 = f32[4096,128]{1,0:T(8,128)S(1)} custom-call(s32[1024]{0:T(1024)S(1)} %multiply_add_fusion.slot_ref, f32[128,2,2,8,128]{4,3,2,1,0:T(8,128)S(1)} %all_to_all.22.in_ref, bf16[2,2,256,512]{3,2,1,0:T(8,128)(2,1)S(1)} %copy-done.2, bf16[256,256]{1,0:T(8,128)(2,1)S(1)} %copy-done.5), custom_call_target="tpu_custom_call" | custom-call | flops 3072 | bytes 96 | tf_op jit(solution)/shard_map/third/pallas_call | solution.py:437
  133.4 34.2 %all_to_all.23 = f32[128,1,16,2,128]{4,3,2,1,0:T(2,128)S(1)} all-to-all(f32[128,1,16,2,128]{4,3,2,1,0:T(2,128)S(1)} %bitcast.22), channel_id=1, replica_groups=mesh['gx'=8,'gy'=4,'gz'=4] {'gx','gy','gz'}, dimensions={0} | all-to-all | bytes 4194304 | tf_op jit(solution)/shard_map/all_to_all | solution.py:494
  167.6 1.3 copy.15
  (32 shorter events, 0.1 us)
Async XLA Ops:
  3.4 54.8 %all-to-all-start = ((f32[4,2,8,128,128]{4,3,2,1,0:T(8,128)}), f32[4,2,8,128,128]{4,3,2,1,0:T(8,128)}, u32[]{:S(2)}, u32[]{:S(2)}) async-start(f32[4,2,8,128,128]{4,3,2,1,0:T(8,128)} %scale_a.1), calls=%async_computation | async-start | bytes 8388608 | tf_op jit(solution)/shard_map/all_to_all | solution.py:468
  11.6 8.6 %copy-start.10 = (s32[1024,1]{0,1:T(1,128)S(1)}, s32[1024,1]{0,1:T(1,128)}, u32[]{:S(2)}) copy-start(s32[1024,1]{0,1:T(1,128)} %param.9) | copy-start | bytes 12292
  11.6 14.2 %collective-permute-start = (f32[2,4,128,128]{3,2,1,0:T(8,128)}, f32[2,4,128,128]{3,2,1,0:T(8,128)S(1)}, u32[]{:S(2)}, u32[]{:S(2)}) collective-permute-start(f32[2,4,128,128]{3,2,1,0:T(8,128)} %get-tuple-element.57), channel_id=1, source_target_pairs={{0,4},{4,8},{8,12},{12,0},{1,5},{5,9},{9,13},{13,1},{2,6},{6,10},{... | collective-permute-start | bytes 1572872 | tf_op jit(solution)/shard_map/ppermute | solution.py:451
  13.0 25.2 %collective-permute-start.1 = (f32[2,4,128,128]{3,2,1,0:T(8,128)}, f32[2,4,128,128]{3,2,1,0:T(8,128)S(1)}, u32[]{:S(2)}, u32[]{:S(2)}) collective-permute-start(f32[2,4,128,128]{3,2,1,0:T(8,128)} %get-tuple-element.58), channel_id=1, source_target_pairs={{0,8},{4,12},{8,0},{12,4},{1,9},{5,13},{9,1},{13,5},{2,10},{6,14},... | collective-permute-start | bytes 1572872 | tf_op jit(solution)/shard_map/ppermute | solution.py:451
  15.6 23.4 %collective-permute-start.2 = (f32[2,4,128,128]{3,2,1,0:T(8,128)}, f32[2,4,128,128]{3,2,1,0:T(8,128)S(1)}, u32[]{:S(2)}, u32[]{:S(2)}) collective-permute-start(f32[2,4,128,128]{3,2,1,0:T(8,128)} %get-tuple-element.59), channel_id=1, source_target_pairs={{0,12},{4,0},{8,4},{12,8},{1,13},{5,1},{9,5},{13,9},{2,14},{6,2},{... | collective-permute-start | bytes 1572872 | tf_op jit(solution)/shard_map/ppermute | solution.py:451
  19.0 43.8 %collective-permute-start.4 = (f32[2,4,128,128]{3,2,1,0:T(8,128)}, f32[2,4,128,128]{3,2,1,0:T(8,128)S(1)}, u32[]{:S(2)}, u32[]{:S(2)}) collective-permute-start(f32[2,4,128,128]{3,2,1,0:T(8,128)} %get-tuple-element.66), channel_id=1, source_target_pairs={{0,4},{4,8},{8,12},{12,0},{1,5},{5,9},{9,13},{13,1},{2,6},{6,10},{... | collective-permute-start | bytes 1572872 | tf_op jit(solution)/shard_map/ppermute | solution.py:451
  19.4 46.4 %collective-permute-start.5 = (f32[2,4,128,128]{3,2,1,0:T(8,128)}, f32[2,4,128,128]{3,2,1,0:T(8,128)}, u32[]{:S(2)}, u32[]{:S(2)}) collective-permute-start(f32[2,4,128,128]{3,2,1,0:T(8,128)} %get-tuple-element.67), channel_id=1, source_target_pairs={{0,8},{4,12},{8,0},{12,4},{1,9},{5,13},{9,1},{13,5},{2,10},{6,14},... | collective-permute-start | bytes 1572872 | tf_op jit(solution)/shard_map/ppermute | solution.py:451
  25.8 3.8 %copy-start.7 = (f32[2,4,128,128]{3,2,1,0:T(8,128)}, f32[2,4,128,128]{3,2,1,0:T(8,128)S(1)}, u32[]{:S(2)}) copy-start(f32[2,4,128,128]{3,2,1,0:T(8,128)S(1)} %collective-permute-done.refs_1_) | copy-start | bytes 1572868
  25.8 40.0 %collective-permute-start.6 = (f32[2,4,128,128]{3,2,1,0:T(8,128)}, f32[2,4,128,128]{3,2,1,0:T(8,128)}, u32[]{:S(2)}, u32[]{:S(2)}) collective-permute-start(f32[2,4,128,128]{3,2,1,0:T(8,128)} %get-tuple-element.68), channel_id=1, source_target_pairs={{0,12},{4,0},{8,4},{12,8},{1,13},{5,1},{9,5},{13,9},{2,14},{6,2},{... | collective-permute-start | bytes 1572872 | tf_op jit(solution)/shard_map/ppermute | solution.py:451
  27.6 12.2 %copy-start = (bf16[2,2,2,256,256]{4,3,2,1,0:T(8,128)(2,1)S(1)}, bf16[2,2,2,256,256]{4,3,2,1,0:T(8,128)(2,1)}, u32[]{:S(2)}) copy-start(bf16[2,2,2,256,256]{4,3,2,1,0:T(8,128)(2,1)} %constant.24.clone.refs_4_.table_ref.refs_6_.table_y_ref) | copy-start | bytes 3145732
  38.2 0.8 copy-start.8
  39.0 0.8 copy-start.9
  43.5 22.3 %collective-permute-start.8 = (f32[2,1,256,128]{3,2,1,0:T(8,128)}, f32[2,1,256,128]{3,2,1,0:T(8,128)S(1)}, u32[]{:S(2)}, u32[]{:S(2)}) collective-permute-start(f32[2,1,256,128]{3,2,1,0:T(8,128)} %get-tuple-element.69), channel_id=1, source_target_pairs={{0,3},{1,0},{2,1},{3,2},{4,7},{5,4},{6,5},{7,6},{8,11},{9,8},{10,9... | collective-permute-start | bytes 786440 | tf_op jit(solution)/shard_map/ppermute | solution.py:451
  47.4 18.3 %collective-permute-start.7 = (f32[2,1,256,128]{3,2,1,0:T(8,128)}, f32[2,1,256,128]{3,2,1,0:T(8,128)S(1)}, u32[]{:S(2)}, u32[]{:S(2)}) collective-permute-start(f32[2,1,256,128]{3,2,1,0:T(8,128)} %get-tuple-element.60), channel_id=1, source_target_pairs={{0,1},{1,2},{2,3},{3,0},{4,5},{5,6},{6,7},{7,4},{8,9},{9,10},{10,1... | collective-permute-start | bytes 786440 | tf_op jit(solution)/shard_map/ppermute | solution.py:451
  47.5 10.8 %copy-start.1 = (bf16[2,2,2,256,256]{4,3,2,1,0:T(8,128)(2,1)S(1)}, bf16[2,2,2,256,256]{4,3,2,1,0:T(8,128)(2,1)}, u32[]{:S(2)}) copy-start(bf16[2,2,2,256,256]{4,3,2,1,0:T(8,128)(2,1)} %constant.25.clone.table_ref) | copy-start | bytes 3145732
  62.7 7.0 %copy-start.12 = (f32[2,2,128,256]{3,2,1,0:T(8,128)S(1)}, f32[2,2,128,256]{3,2,1,0:T(8,128)}, u32[]{:S(2)}) copy-start(f32[2,2,128,256]{3,2,1,0:T(8,128)} %get-tuple-element.83) | copy-start | bytes 1572868
  62.7 7.5 %copy-start.11 = (f32[2,2,128,256]{3,2,1,0:T(8,128)S(1)}, f32[2,2,128,256]{3,2,1,0:T(8,128)}, u32[]{:S(2)}) copy-start(f32[2,2,128,256]{3,2,1,0:T(8,128)} %get-tuple-element.84) | copy-start | bytes 1572868
  62.8 12.9 %copy-start.4 = (f32[2,2,128,256]{3,2,1,0:T(8,128)S(1)}, f32[2,2,128,256]{3,2,1,0:T(8,128)}, u32[]{:S(2)}) copy-start(f32[2,2,128,256]{3,2,1,0:T(8,128)} %get-tuple-element.63.p0) | copy-start | bytes 1572868
  62.8 3.0 %copy-start.6 = (f32[2,4,128,128]{3,2,1,0:T(8,128)}, f32[2,4,128,128]{3,2,1,0:T(8,128)S(1)}, u32[]{:S(2)}) copy-start(f32[2,4,128,128]{3,2,1,0:T(8,128)S(1)} %collective-permute-done.4.refs_1_) | copy-start | bytes 1572868
  62.8 12.9 %collective-permute-start.3 = (f32[2,2,128,256]{3,2,1,0:T(8,128)}, f32[2,2,128,256]{3,2,1,0:T(8,128)S(1)}, u32[]{:S(2)}, u32[]{:S(2)}) collective-permute-start(f32[2,2,128,256]{3,2,1,0:T(8,128)} %get-tuple-element.64), channel_id=1, source_target_pairs={{0,8},{4,12},{8,0},{12,4},{1,9},{5,13},{9,1},{13,5},{2,10},{6,14},... | collective-permute-start | bytes 1572872 | tf_op jit(solution)/shard_map/ppermute | solution.py:451
  69.6 21.3 %copy-start.3 = (f32[2,2,256,128]{3,2,1,0:T(8,128)S(1)}, f32[2,2,256,128]{3,2,1,0:T(8,128)}, u32[]{:S(2)}) copy-start(f32[2,2,256,128]{3,2,1,0:T(8,128)} %get-tuple-element.77.b0) | copy-start | bytes 1572868
  69.6 12.6 %collective-permute-start.9 = (f32[2,2,256,128]{3,2,1,0:T(8,128)}, f32[2,2,256,128]{3,2,1,0:T(8,128)S(1)}, u32[]{:S(2)}, u32[]{:S(2)}) collective-permute-start(f32[2,2,256,128]{3,2,1,0:T(8,128)} %get-tuple-element.75), channel_id=1, source_target_pairs={{0,2},{1,3},{2,0},{3,1},{4,6},{5,7},{6,4},{7,5},{8,10},{9,11},{10,... | collective-permute-start | bytes 1572872 | tf_op jit(solution)/shard_map/ppermute | solution.py:451
  69.7 22.2 %collective-permute-start.12 = (f32[2,2,128,256]{3,2,1,0:T(8,128)S(1)}, f32[2,2,128,256]{3,2,1,0:T(8,128)S(1)}, u32[]{:S(2)}, u32[]{:S(2)}) collective-permute-start(f32[2,2,128,256]{3,2,1,0:T(8,128)S(1)} %copy-done.12), channel_id=1, source_target_pairs={{0,4},{4,8},{8,12},{12,0},{1,5},{5,9},{9,13},{13,1},{2,6},{6,10},{... | collective-permute-start | bytes 1572872 | tf_op jit(solution)/shard_map/ppermute | solution.py:451
  70.2 21.7 %collective-permute-start.13 = (f32[2,2,128,256]{3,2,1,0:T(8,128)S(1)}, f32[2,2,128,256]{3,2,1,0:T(8,128)S(1)}, u32[]{:S(2)}, u32[]{:S(2)}) collective-permute-start(f32[2,2,128,256]{3,2,1,0:T(8,128)S(1)} %copy-done.11), channel_id=1, source_target_pairs={{0,12},{4,0},{8,4},{12,8},{1,13},{5,1},{9,5},{13,9},{2,14},{6,2},{... | collective-permute-start | bytes 1572872 | tf_op jit(solution)/shard_map/ppermute | solution.py:451
  72.5 18.4 %collective-permute-start.10 = (f32[2,1,256,128]{3,2,1,0:T(8,128)}, f32[2,1,256,128]{3,2,1,0:T(8,128)S(1)}, u32[]{:S(2)}, u32[]{:S(2)}) collective-permute-start(f32[2,1,256,128]{3,2,1,0:T(8,128)} %get-tuple-element.81), channel_id=1, source_target_pairs={{0,1},{1,2},{2,3},{3,0},{4,5},{5,6},{6,7},{7,4},{8,9},{9,10},{10,1... | collective-permute-start | bytes 786440 | tf_op jit(solution)/shard_map/ppermute | solution.py:451
  75.7 15.2 %collective-permute-start.11 = (f32[2,1,256,128]{3,2,1,0:T(8,128)}, f32[2,1,256,128]{3,2,1,0:T(8,128)S(1)}, u32[]{:S(2)}, u32[]{:S(2)}) collective-permute-start(f32[2,1,256,128]{3,2,1,0:T(8,128)} %get-tuple-element.82), channel_id=1, source_target_pairs={{0,3},{1,0},{2,1},{3,2},{4,7},{5,4},{6,5},{7,6},{8,11},{9,8},{10,9... | collective-permute-start | bytes 786440 | tf_op jit(solution)/shard_map/ppermute | solution.py:451
  93.5 36.2 %copy-start.2 = (bf16[2,2,256,512]{3,2,1,0:T(8,128)(2,1)S(1)}, bf16[2,2,256,512]{3,2,1,0:T(8,128)(2,1)}, u32[]{:S(2)}) copy-start(bf16[2,2,256,512]{3,2,1,0:T(8,128)(2,1)} %constant.23.clone.table_ref) | copy-start | bytes 3145732
  93.5 36.2 %copy-start.5 = (bf16[256,256]{1,0:T(8,128)(2,1)S(1)}, bf16[256,256]{1,0:T(8,128)(2,1)}, u32[]{:S(2)}) copy-start(bf16[256,256]{1,0:T(8,128)(2,1)} %constant.26.clone.ordering_ref) | copy-start | bytes 393220

commit v21 on v20

--- a/solution.py
+++ b/solution.py
@@ -182,10 +182,12 @@
         return pltpu.make_async_copy(held_out.at[i], out_refs[i], semaphores.at[i, 1])
 
     steps = range(len(shifts))
-    for i in steps:
+    for i in steps[:2]:
         get(i).start()
     for i in steps:
         get(i).wait()
+        if i + 2 < len(shifts):
+            get(i + 2).start()
         pairs = [(pieces[i, 0], pieces[i, 2], 0), (pieces[i, 1], pieces[i, 3], 1)]
         for odd, values in enumerate(transform(True, pairs, table_ref)):
             half = slice(odd * 128, (odd + 1) * 128)
@@ -476,7 +478,7 @@
     (d0,) = scale(1, (0,), place, normals, spectrum)
 
     c1, c3, c2, c0 = first_y(gy, gz, (c0, c1, c2, c3), table_y)
-    a, slots, _, d0 = lax.optimization_barrier((a, slots_of(block_owner), c1, d0))
+    a, slots, c1, c3, d0 = lax.optimization_barrier((a, slots_of(block_owner), c1, c3, d0))
     c1, c3 = shifted(c1, "gz", 1), shifted(c3, "gz", 3)
     a2, a1, a3, a0 = first_z((2, 1, 3, 0), gy, a, table_z)
     d1, d2, d3, c1, c3, _ = lax.optimization_barrier((d1, d2, d3, c1, c3, a2))

time: 169 us -> 172 us (1.018)
  waiting for transfers between devices: 39.8 us -> 44.7 us
    all_to_all x1, waiting for transfers between devices: 8.78 us -> 15.6 us  [per_device(): a = lax.all_to_all(a, 'gz', split_axis=0, concat_axis=0, tiled=True)]
    ppermute x14, waiting for transfers between devices: 31.1 us -> 29.1 us  [shifted(): lax.ppermute(piece, axis, [(i, (i + shift) % size) for i in range(size)])]
where the time goes in v21:
time: 172 us; the launch traced here: 171 us
  blocking collectives  69.1 us (40%)
  waiting for transfers between devices  44.7 us (26%)
  Pallas kernels  31.5 us (18%)
  starting transfers between devices  22.9 us (13%)
  local copies, waits for them, and re-layouts  2.36 us (1%)
    all_to_all x1, blocking collectives, per_device(): lines = lax.all_to_all(planes, ALL, split_axis=0, concat_axis=0, tiled=True)  34.9 us
    all_to_all x1, blocking collectives, per_device(): lax.all_to_all(outgoing.reshape(128, 1, CAP, 2, BW), ALL, split_axis=0, c...  34.2 us
    ppermute x14, waiting for transfers between devices, shifted(): lax.ppermute(piece, axis, [(i, (i + shift) % size) for i in range(size)])  29.1 us
    ppermute x14, starting transfers between devices, shifted(): lax.ppermute(piece, axis, [(i, (i + shift) % size) for i in range(size)])  17 us
    all_to_all x1, waiting for transfers between devices, per_device(): a = lax.all_to_all(a, 'gz', split_axis=0, concat_axis=0, tiled=True)  15.6 us
    pallas_call x5, Pallas kernels, scale(): pl.pallas_call(functools.partial(scale_kernel, part, shifts), in_specs=[p...  11.9 us
    pallas_call x2, Pallas kernels, first_y(): pl.pallas_call(functools.partial(first_y_kernel, merge), in_specs=[pl.Blo...  7.59 us
    all_to_all x1, starting transfers between devices, per_device(): a = lax.all_to_all(a, 'gz', split_axis=0, concat_axis=0, tiled=True)  5.87 us
  transfers between devices with their start and end apart: 15, of which 7 were waited for; matrix products, arithmetic and copies ran while one was open for 0% of the time, Pallas kernels for 13%

profile of v21, /device:TPU:1, one launch (start us, length us, event | category | flops | bytes accessed | tf_op | source)
XLA Modules:
  0.0 171.4 jit_solution(14721540075664365192)
XLA Ops:
  0.0 3.4 %scale_a.1 = f32[4,2,8,128,128]{4,3,2,1,0:T(8,128)} custom-call(s32[1]{0:T(128)} %bitcast.place_ref.to_ref, bf16[2,8,8,128,128]{4,3,2,1,0:T(8,128)(2,1)} %bitcast.23, f32[8,8,128,128]{3,2,1,0:T(8,128)} %bitcast.28), custom_call_target="tpu_custom_call" | custom-call | flops 16 | bytes 128 | tf_op jit(solution)/shard_map/scale_a/pallas_call | solution.py:137
  3.4 5.9 %all-to-all-start = ((f32[4,2,8,128,128]{4,3,2,1,0:T(8,128)}), f32[4,2,8,128,128]{4,3,2,1,0:T(8,128)}, u32[]{:S(2)}, u32[]{:S(2)}) async-start(f32[4,2,8,128,128]{4,3,2,1,0:T(8,128)} %scale_a.1), calls=%async_computation | async-start | bytes 8388608 | tf_op jit(solution)/shard_map/all_to_all | solution.py:470
  9.3 2.3 %scale_b.4 = (f32[2,4,128,128]{3,2,1,0:T(8,128)}, f32[2,4,128,128]{3,2,1,0:T(8,128)}, f32[2,4,128,128]{3,2,1,0:T(8,128)}) custom-call(s32[1]{0:T(128)} %bitcast.3.place_ref.to_ref.y_ref, bf16[2,8,2,4,128,128]{5,4,3,2,1,0:T(8,128)(2,1)} %bitcast.24, f32[8,2,4,128,128]{4,3,2,1,0:T(8,128)} %bitcast.29), custom_call_target="tpu_custom_call" | custom-call | flops 12 | bytes 96 | tf_op jit(solution)/shard_map/scale_b/pallas_call | solution.py:137
  11.5 0.0 copy-start.9
  11.6 1.4 collective-permute-start
  12.9 2.6 %collective-permute-start.1 = (f32[2,4,128,128]{3,2,1,0:T(8,128)}, f32[2,4,128,128]{3,2,1,0:T(8,128)}, u32[]{:S(2)}, u32[]{:S(2)}) collective-permute-start(f32[2,4,128,128]{3,2,1,0:T(8,128)} %get-tuple-element.60), channel_id=1, source_target_pairs={{0,8},{4,12},{8,0},{12,4},{1,9},{5,13},{9,1},{13,5},{2,10},{6,14},... | collective-permute-start | bytes 1572872 | tf_op jit(solution)/shard_map/ppermute | solution.py:453
  15.5 1.1 collective-permute-start.2
  16.6 2.3 %scale_b.5 = (f32[2,4,128,128]{3,2,1,0:T(8,128)}, f32[2,4,128,128]{3,2,1,0:T(8,128)}, f32[2,4,128,128]{3,2,1,0:T(8,128)}) custom-call(s32[1]{0:T(128)} %bitcast.3.place_ref.to_ref.y_ref, bf16[2,8,2,4,128,128]{5,4,3,2,1,0:T(8,128)(2,1)} %bitcast.25, f32[8,2,4,128,128]{4,3,2,1,0:T(8,128)} %bitcast.30), custom_call_target="tpu_custom_call" | custom-call | flops 12 | bytes 96 | tf_op jit(solution)/shard_map/scale_b/pallas_call | solution.py:137
  18.9 0.5 collective-permute-start.4
  19.4 0.8 collective-permute-start.5
  20.2 0.1 copy.11
  20.3 0.2 fusion.2
  20.6 0.1 copy.12
  20.7 5.1 %collective-permute-done.refs_1_ = f32[2,4,128,128]{3,2,1,0:T(8,128)S(1)} collective-permute-done((f32[2,4,128,128]{3,2,1,0:T(8,128)}, f32[2,4,128,128]{3,2,1,0:T(8,128)S(1)}, u32[]{:S(2)}, u32[]{:S(2)}) %collective-permute-start) | collective-permute-done | bytes 524320 | tf_op jit(solution)/shard_map/ppermute | solution.py:453
  25.8 1.4 collective-permute-start.6
  27.2 0.4 fusion.1
  27.5 2.0 %scale_b.7.refs_0_ = f32[2,4,128,128]{3,2,1,0:T(8,128)} custom-call(s32[1]{0:T(128)} %bitcast.3.place_ref.to_ref.y_ref, bf16[2,8,2,4,128,128]{5,4,3,2,1,0:T(8,128)(2,1)} %bitcast.26, f32[8,2,4,128,128]{4,3,2,1,0:T(8,128)} %bitcast.31), custom_call_target="tpu_custom_call" | custom-call | flops 4 | bytes 32 | tf_op jit(solution)/shard_map/scale_b/pallas_call | solution.py:137
  29.5 0.0 copy-start
  29.5 2.0 %scale_b.6.refs_0_ = f32[2,4,128,128]{3,2,1,0:T(8,128)} custom-call(s32[1]{0:T(128)} %bitcast.3.place_ref.to_ref.y_ref, bf16[2,8,2,4,128,128]{5,4,3,2,1,0:T(8,128)(2,1)} %bitcast.27, f32[8,2,4,128,128]{4,3,2,1,0:T(8,128)} %bitcast.32), custom_call_target="tpu_custom_call" | custom-call | flops 4 | bytes 32 | tf_op jit(solution)/shard_map/scale_b/pallas_call | solution.py:137
  31.5 0.0 copy-start.1
  31.5 6.6 %collective-permute-done.1.refs_2_ = f32[2,4,128,128]{3,2,1,0:T(8,128)} collective-permute-done((f32[2,4,128,128]{3,2,1,0:T(8,128)}, f32[2,4,128,128]{3,2,1,0:T(8,128)}, u32[]{:S(2)}, u32[]{:S(2)}) %collective-permute-start.1) | collective-permute-done | bytes 524320 | tf_op jit(solution)/shard_map/ppermute | solution.py:453
  38.1 0.8 collective-permute-done.2.refs_3_
  38.9 3.7 %first_y.2 = (f32[2,1,256,128]{3,2,1,0:T(8,128)}, f32[2,1,256,128]{3,2,1,0:T(8,128)}, f32[2,1,256,128]{3,2,1,0:T(8,128)}, f32[2,1,256,128]{3,2,1,0:T(8,128)}) custom-call(s32[1]{0:T(128)} %bitcast.3.place_ref.to_ref.y_ref, s32[1]{0:T(128)} %bitcast.place_ref.to_ref, f32[2,4,128,128]{3,2,1,0:T(8,128)} %scale_b.6.refs_0_, f32[2,4,128,128]{3,2,1,0:T(8,128)} %copy-done.8, ...), custom_call_target="tpu_custom_call" | custom-call | flops 2048 | bytes 64 | tf_op jit(solution)/shard_map/first_y/pallas_call | solution.py:279
  42.7 15.6 %all-to-all-done.in_ref = f32[4,2,8,128,128]{4,3,2,1,0:T(8,128)} async-done(((f32[4,2,8,128,128]{4,3,2,1,0:T(8,128)}), f32[4,2,8,128,128]{4,3,2,1,0:T(8,128)}, u32[]{:S(2)}, u32[]{:S(2)}) %all-to-all-start) | async-done | bytes 4194336 | tf_op jit(solution)/shard_map/all_to_all | solution.py:470
  58.2 0.8 collective-permute-start.7
  59.1 1.8 %collective-permute-start.8 = (f32[2,1,256,128]{3,2,1,0:T(8,128)}, f32[2,1,256,128]{3,2,1,0:T(8,128)S(1)}, u32[]{:S(2)}, u32[]{:S(2)}) collective-permute-start(f32[2,1,256,128]{3,2,1,0:T(8,128)} %get-tuple-element.73), channel_id=1, source_target_pairs={{0,3},{1,0},{2,1},{3,2},{4,7},{5,4},{6,5},{7,6},{8,11},{9,8},{10,9... | collective-permute-start | bytes 786440 | tf_op jit(solution)/shard_map/ppermute | solution.py:453
  60.9 4.8 %first_z.1 = (f32[2,2,128,256]{3,2,1,0:T(8,128)}, f32[2,2,128,256]{3,2,1,0:T(8,128)}, f32[2,2,128,256]{3,2,1,0:T(8,128)}, f32[2,2,128,256]{3,2,1,0:T(8,128)}) custom-call(s32[1]{0:T(128)} %bitcast.3.place_ref.to_ref.y_ref, f32[4,2,8,128,128]{4,3,2,1,0:T(8,128)} %all-to-all-done.in_ref, bf16[2,2,2,256,256]{4,3,2,1,0:T(8,128)(2,1)S(1)} %copy-done.1), custom_call_target="tpu_custom_call" | custom-call | flops 4096 | bytes 128 | tf_op jit(solution)/shard_map/first_z/pallas_call | solution.py:207
  65.7 3.0 %collective-permute-start.3 = (f32[2,2,128,256]{3,2,1,0:T(8,128)}, f32[2,2,128,256]{3,2,1,0:T(8,128)S(1)}, u32[]{:S(2)}, u32[]{:S(2)}) collective-permute-start(f32[2,2,128,256]{3,2,1,0:T(8,128)} %get-tuple-element.67), channel_id=1, source_target_pairs={{0,8},{4,12},{8,0},{12,4},{1,9},{5,13},{9,1},{13,5},{2,10},{6,14},... | collective-permute-start | bytes 1572872 | tf_op jit(solution)/shard_map/ppermute | solution.py:453
  68.8 0.0 collective-permute-done.7.c1
  68.8 0.8 copy-done.7
  69.6 3.9 %first_y.3 = (f32[2,1,256,128]{3,2,1,0:T(8,128)}, f32[2,1,256,128]{3,2,1,0:T(8,128)}, f32[2,2,256,128]{3,2,1,0:T(8,128)}, f32[2,2,256,128]{3,2,1,0:T(8,128)}) custom-call(s32[1]{0:T(128)} %bitcast.3.place_ref.to_ref.y_ref, s32[1]{0:T(128)} %bitcast.place_ref.to_ref, f32[2,4,128,128]{3,2,1,0:T(8,128)} %scale_b.7.refs_0_, f32[2,4,128,128]{3,2,1,0:T(8,128)} %copy-done.6, ...), custom_call_target="tpu_custom_call" | custom-call | flops 2048 | bytes 64 | tf_op jit(solution)/shard_map/first_y/pallas_call | solution.py:279
  73.4 0.1 collective-permute-start.9
  73.5 0.5 collective-permute-start.12
  74.0 2.3 %collective-permute-start.13 = (f32[2,2,128,256]{3,2,1,0:T(8,128)S(1)}, f32[2,2,128,256]{3,2,1,0:T(8,128)S(1)}, u32[]{:S(2)}, u32[]{:S(2)}) collective-permute-start(f32[2,2,128,256]{3,2,1,0:T(8,128)S(1)} %copy-done.10), channel_id=1, source_target_pairs={{0,12},{4,0},{8,4},{12,8},{1,13},{5,1},{9,5},{13,9},{2,14},{6,2},{... | collective-permute-start | bytes 1572872 | tf_op jit(solution)/shard_map/ppermute | solution.py:453
  76.3 0.5 collective-permute-start.10
  76.8 2.1 %collective-permute-done.3.p2 = f32[2,2,128,256]{3,2,1,0:T(8,128)S(1)} collective-permute-done((f32[2,2,128,256]{3,2,1,0:T(8,128)}, f32[2,2,128,256]{3,2,1,0:T(8,128)S(1)}, u32[]{:S(2)}, u32[]{:S(2)}) %collective-permute-start.3) | collective-permute-done | bytes 524320 | tf_op jit(solution)/shard_map/ppermute | solution.py:453
  78.9 0.3 collective-permute-start.11
  79.2 1.0 part_y.1.part_a
  80.2 6.2 %collective-permute-done.9.b2 = f32[2,2,256,128]{3,2,1,0:T(8,128)S(1)} collective-permute-done((f32[2,2,256,128]{3,2,1,0:T(8,128)}, f32[2,2,256,128]{3,2,1,0:T(8,128)S(1)}, u32[]{:S(2)}, u32[]{:S(2)}) %collective-permute-start.9) | collective-permute-done | bytes 524320 | tf_op jit(solution)/shard_map/ppermute | solution.py:453
  86.4 8.3 %collective-permute-done.10.d1 = f32[2,1,256,128]{3,2,1,0:T(8,128)S(1)} collective-permute-done((f32[2,1,256,128]{3,2,1,0:T(8,128)}, f32[2,1,256,128]{3,2,1,0:T(8,128)S(1)}, u32[]{:S(2)}, u32[]{:S(2)}) %collective-permute-start.10) | collective-permute-done | bytes 262176 | tf_op jit(solution)/shard_map/ppermute | solution.py:453
  94.7 1.0 second_z.1.done_b
  95.7 1.5 second.1
  97.3 0.0 copy-start.2
  97.3 0.0 copy-start.5
  97.3 34.9 %all_to_all.22.in_ref = f32[128,2,2,8,128]{4,3,2,1,0:T(8,128)S(1)} all-to-all(f32[128,2,2,8,128]{4,3,2,1,0:T(8,128)S(1)} %second.1), channel_id=1, replica_groups=mesh['gx'=8,'gy'=4,'gz'=4] {'gx','gy','gz'}, dimensions={0} | all-to-all | bytes 4194304 | tf_op jit(solution)/shard_map/all_to_all | solution.py:494
  132.2 3.7 %third.1 = f32[4096,128]{1,0:T(8,128)S(1)} custom-call(s32[1024]{0:T(1024)S(1)} %multiply_add_fusion.slot_ref, f32[128,2,2,8,128]{4,3,2,1,0:T(8,128)S(1)} %all_to_all.22.in_ref, bf16[2,2,256,512]{3,2,1,0:T(8,128)(2,1)S(1)} %copy-done.2, bf16[256,256]{1,0:T(8,128)(2,1)S(1)} %copy-done.5), custom_call_target="tpu_custom_call" | custom-call | flops 3072 | bytes 96 | tf_op jit(solution)/shard_map/third/pallas_call | solution.py:439
  135.9 34.2 %all_to_all.23 = f32[128,1,16,2,128]{4,3,2,1,0:T(2,128)S(1)} all-to-all(f32[128,1,16,2,128]{4,3,2,1,0:T(2,128)S(1)} %bitcast.22), channel_id=1, replica_groups=mesh['gx'=8,'gy'=4,'gz'=4] {'gx','gy','gz'}, dimensions={0} | all-to-all | bytes 4194304 | tf_op jit(solution)/shard_map/all_to_all | solution.py:496
  170.1 1.3 copy.15
  (30 shorter events, 0.1 us)
Async XLA Ops:
  3.4 54.8 %all-to-all-start = ((f32[4,2,8,128,128]{4,3,2,1,0:T(8,128)}), f32[4,2,8,128,128]{4,3,2,1,0:T(8,128)}, u32[]{:S(2)}, u32[]{:S(2)}) async-start(f32[4,2,8,128,128]{4,3,2,1,0:T(8,128)} %scale_a.1), calls=%async_computation | async-start | bytes 8388608 | tf_op jit(solution)/shard_map/all_to_all | solution.py:470
  11.5 8.6 %copy-start.9 = (s32[1024,1]{0,1:T(1,128)S(1)}, s32[1024,1]{0,1:T(1,128)}, u32[]{:S(2)}) copy-start(s32[1024,1]{0,1:T(1,128)} %param.9) | copy-start | bytes 12292
  11.6 14.2 %collective-permute-start = (f32[2,4,128,128]{3,2,1,0:T(8,128)}, f32[2,4,128,128]{3,2,1,0:T(8,128)S(1)}, u32[]{:S(2)}, u32[]{:S(2)}) collective-permute-start(f32[2,4,128,128]{3,2,1,0:T(8,128)} %get-tuple-element.59), channel_id=1, source_target_pairs={{0,4},{4,8},{8,12},{12,0},{1,5},{5,9},{9,13},{13,1},{2,6},{6,10},{... | collective-permute-start | bytes 1572872 | tf_op jit(solution)/shard_map/ppermute | solution.py:453
  12.9 25.2 %collective-permute-start.1 = (f32[2,4,128,128]{3,2,1,0:T(8,128)}, f32[2,4,128,128]{3,2,1,0:T(8,128)}, u32[]{:S(2)}, u32[]{:S(2)}) collective-permute-start(f32[2,4,128,128]{3,2,1,0:T(8,128)} %get-tuple-element.60), channel_id=1, source_target_pairs={{0,8},{4,12},{8,0},{12,4},{1,9},{5,13},{9,1},{13,5},{2,10},{6,14},... | collective-permute-start | bytes 1572872 | tf_op jit(solution)/shard_map/ppermute | solution.py:453
  15.5 23.4 %collective-permute-start.2 = (f32[2,4,128,128]{3,2,1,0:T(8,128)}, f32[2,4,128,128]{3,2,1,0:T(8,128)}, u32[]{:S(2)}, u32[]{:S(2)}) collective-permute-start(f32[2,4,128,128]{3,2,1,0:T(8,128)} %get-tuple-element.61), channel_id=1, source_target_pairs={{0,12},{4,0},{8,4},{12,8},{1,13},{5,1},{9,5},{13,9},{2,14},{6,2},{... | collective-permute-start | bytes 1572872 | tf_op jit(solution)/shard_map/ppermute | solution.py:453
  18.9 46.8 %collective-permute-start.4 = (f32[2,4,128,128]{3,2,1,0:T(8,128)}, f32[2,4,128,128]{3,2,1,0:T(8,128)S(1)}, u32[]{:S(2)}, u32[]{:S(2)}) collective-permute-start(f32[2,4,128,128]{3,2,1,0:T(8,128)} %get-tuple-element.69), channel_id=1, source_target_pairs={{0,4},{4,8},{8,12},{12,0},{1,5},{5,9},{9,13},{13,1},{2,6},{6,10},{... | collective-permute-start | bytes 1572872 | tf_op jit(solution)/shard_map/ppermute | solution.py:453
  19.4 49.4 %collective-permute-start.5 = (f32[2,4,128,128]{3,2,1,0:T(8,128)}, f32[2,4,128,128]{3,2,1,0:T(8,128)S(1)}, u32[]{:S(2)}, u32[]{:S(2)}) collective-permute-start(f32[2,4,128,128]{3,2,1,0:T(8,128)} %get-tuple-element.70), channel_id=1, source_target_pairs={{0,8},{4,12},{8,0},{12,4},{1,9},{5,13},{9,1},{13,5},{2,10},{6,14},... | collective-permute-start | bytes 1572872 | tf_op jit(solution)/shard_map/ppermute | solution.py:453
  25.8 1.8 %copy-start.8 = (f32[2,4,128,128]{3,2,1,0:T(8,128)}, f32[2,4,128,128]{3,2,1,0:T(8,128)S(1)}, u32[]{:S(2)}) copy-start(f32[2,4,128,128]{3,2,1,0:T(8,128)S(1)} %collective-permute-done.refs_1_) | copy-start | bytes 1572868
  25.8 43.0 %collective-permute-start.6 = (f32[2,4,128,128]{3,2,1,0:T(8,128)}, f32[2,4,128,128]{3,2,1,0:T(8,128)}, u32[]{:S(2)}, u32[]{:S(2)}) collective-permute-start(f32[2,4,128,128]{3,2,1,0:T(8,128)} %get-tuple-element.71), channel_id=1, source_target_pairs={{0,12},{4,0},{8,4},{12,8},{1,13},{5,1},{9,5},{13,9},{2,14},{6,2},{... | collective-permute-start | bytes 1572872 | tf_op jit(solution)/shard_map/ppermute | solution.py:453
  29.5 9.4 %copy-start = (bf16[2,2,2,256,256]{4,3,2,1,0:T(8,128)(2,1)S(1)}, bf16[2,2,2,256,256]{4,3,2,1,0:T(8,128)(2,1)}, u32[]{:S(2)}) copy-start(bf16[2,2,2,256,256]{4,3,2,1,0:T(8,128)(2,1)} %constant.24.clone.refs_4_.table_ref.refs_6_.table_y_ref) | copy-start | bytes 3145732
  31.5 29.4 %copy-start.1 = (bf16[2,2,2,256,256]{4,3,2,1,0:T(8,128)(2,1)S(1)}, bf16[2,2,2,256,256]{4,3,2,1,0:T(8,128)(2,1)}, u32[]{:S(2)}) copy-start(bf16[2,2,2,256,256]{4,3,2,1,0:T(8,128)(2,1)} %constant.25.clone.table_ref) | copy-start | bytes 3145732
  58.2 10.5 %collective-permute-start.7 = (f32[2,1,256,128]{3,2,1,0:T(8,128)}, f32[2,1,256,128]{3,2,1,0:T(8,128)S(1)}, u32[]{:S(2)}, u32[]{:S(2)}) collective-permute-start(f32[2,1,256,128]{3,2,1,0:T(8,128)} %get-tuple-element.72), channel_id=1, source_target_pairs={{0,1},{1,2},{2,3},{3,0},{4,5},{5,6},{6,7},{7,4},{8,9},{9,10},{10,1... | collective-permute-start | bytes 786440 | tf_op jit(solution)/shard_map/ppermute | solution.py:453
  59.1 9.7 %collective-permute-start.8 = (f32[2,1,256,128]{3,2,1,0:T(8,128)}, f32[2,1,256,128]{3,2,1,0:T(8,128)S(1)}, u32[]{:S(2)}, u32[]{:S(2)}) collective-permute-start(f32[2,1,256,128]{3,2,1,0:T(8,128)} %get-tuple-element.73), channel_id=1, source_target_pairs={{0,3},{1,0},{2,1},{3,2},{4,7},{5,4},{6,5},{7,6},{8,11},{9,8},{10,9... | collective-permute-start | bytes 786440 | tf_op jit(solution)/shard_map/ppermute | solution.py:453
  65.7 7.8 %copy-start.11 = (f32[2,2,128,256]{3,2,1,0:T(8,128)S(1)}, f32[2,2,128,256]{3,2,1,0:T(8,128)}, u32[]{:S(2)}) copy-start(f32[2,2,128,256]{3,2,1,0:T(8,128)} %get-tuple-element.87) | copy-start | bytes 1572868
  65.7 8.3 %copy-start.10 = (f32[2,2,128,256]{3,2,1,0:T(8,128)S(1)}, f32[2,2,128,256]{3,2,1,0:T(8,128)}, u32[]{:S(2)}) copy-start(f32[2,2,128,256]{3,2,1,0:T(8,128)} %get-tuple-element.88) | copy-start | bytes 1572868
  65.7 13.5 %copy-start.4 = (f32[2,2,128,256]{3,2,1,0:T(8,128)S(1)}, f32[2,2,128,256]{3,2,1,0:T(8,128)}, u32[]{:S(2)}) copy-start(f32[2,2,128,256]{3,2,1,0:T(8,128)} %get-tuple-element.66.p0) | copy-start | bytes 1572868
  65.7 3.0 %copy-start.6 = (f32[2,4,128,128]{3,2,1,0:T(8,128)}, f32[2,4,128,128]{3,2,1,0:T(8,128)S(1)}, u32[]{:S(2)}) copy-start(f32[2,4,128,128]{3,2,1,0:T(8,128)S(1)} %collective-permute-done.4.refs_1_) | copy-start | bytes 1572868
  65.7 13.2 %collective-permute-start.3 = (f32[2,2,128,256]{3,2,1,0:T(8,128)}, f32[2,2,128,256]{3,2,1,0:T(8,128)S(1)}, u32[]{:S(2)}, u32[]{:S(2)}) collective-permute-start(f32[2,2,128,256]{3,2,1,0:T(8,128)} %get-tuple-element.67), channel_id=1, source_target_pairs={{0,8},{4,12},{8,0},{12,4},{1,9},{5,13},{9,1},{13,5},{2,10},{6,14},... | collective-permute-start | bytes 1572872 | tf_op jit(solution)/shard_map/ppermute | solution.py:453
  68.8 0.8 copy-start.7
  73.4 21.3 %copy-start.3 = (f32[2,2,256,128]{3,2,1,0:T(8,128)S(1)}, f32[2,2,256,128]{3,2,1,0:T(8,128)}, u32[]{:S(2)}) copy-start(f32[2,2,256,128]{3,2,1,0:T(8,128)} %get-tuple-element.81.b0) | copy-start | bytes 1572868
  73.4 12.9 %collective-permute-start.9 = (f32[2,2,256,128]{3,2,1,0:T(8,128)}, f32[2,2,256,128]{3,2,1,0:T(8,128)S(1)}, u32[]{:S(2)}, u32[]{:S(2)}) collective-permute-start(f32[2,2,256,128]{3,2,1,0:T(8,128)} %get-tuple-element.79), channel_id=1, source_target_pairs={{0,2},{1,3},{2,0},{3,1},{4,6},{5,7},{6,4},{7,5},{8,10},{9,11},{10,... | collective-permute-start | bytes 1572872 | tf_op jit(solution)/shard_map/ppermute | solution.py:453
  73.5 22.2 %collective-permute-start.12 = (f32[2,2,128,256]{3,2,1,0:T(8,128)S(1)}, f32[2,2,128,256]{3,2,1,0:T(8,128)S(1)}, u32[]{:S(2)}, u32[]{:S(2)}) collective-permute-start(f32[2,2,128,256]{3,2,1,0:T(8,128)S(1)} %copy-done.11), channel_id=1, source_target_pairs={{0,4},{4,8},{8,12},{12,0},{1,5},{5,9},{9,13},{13,1},{2,6},{6,10},{... | collective-permute-start | bytes 1572872 | tf_op jit(solution)/shard_map/ppermute | solution.py:453
  74.0 21.7 %collective-permute-start.13 = (f32[2,2,128,256]{3,2,1,0:T(8,128)S(1)}, f32[2,2,128,256]{3,2,1,0:T(8,128)S(1)}, u32[]{:S(2)}, u32[]{:S(2)}) collective-permute-start(f32[2,2,128,256]{3,2,1,0:T(8,128)S(1)} %copy-done.10), channel_id=1, source_target_pairs={{0,12},{4,0},{8,4},{12,8},{1,13},{5,1},{9,5},{13,9},{2,14},{6,2},{... | collective-permute-start | bytes 1572872 | tf_op jit(solution)/shard_map/ppermute | solution.py:453
  76.3 18.4 %collective-permute-start.10 = (f32[2,1,256,128]{3,2,1,0:T(8,128)}, f32[2,1,256,128]{3,2,1,0:T(8,128)S(1)}, u32[]{:S(2)}, u32[]{:S(2)}) collective-permute-start(f32[2,1,256,128]{3,2,1,0:T(8,128)} %get-tuple-element.85), channel_id=1, source_target_pairs={{0,1},{1,2},{2,3},{3,0},{4,5},{5,6},{6,7},{7,4},{8,9},{9,10},{10,1... | collective-permute-start | bytes 786440 | tf_op jit(solution)/shard_map/ppermute | solution.py:453
  78.9 15.8 %collective-permute-start.11 = (f32[2,1,256,128]{3,2,1,0:T(8,128)}, f32[2,1,256,128]{3,2,1,0:T(8,128)S(1)}, u32[]{:S(2)}, u32[]{:S(2)}) collective-permute-start(f32[2,1,256,128]{3,2,1,0:T(8,128)} %get-tuple-element.86), channel_id=1, source_target_pairs={{0,3},{1,0},{2,1},{3,2},{4,7},{5,4},{6,5},{7,6},{8,11},{9,8},{10,9... | collective-permute-start | bytes 786440 | tf_op jit(solution)/shard_map/ppermute | solution.py:453
  97.3 34.9 %copy-start.2 = (bf16[2,2,256,512]{3,2,1,0:T(8,128)(2,1)S(1)}, bf16[2,2,256,512]{3,2,1,0:T(8,128)(2,1)}, u32[]{:S(2)}) copy-start(bf16[2,2,256,512]{3,2,1,0:T(8,128)(2,1)} %constant.23.clone.table_ref) | copy-start | bytes 3145732
  97.3 34.9 %copy-start.5 = (bf16[256,256]{1,0:T(8,128)(2,1)S(1)}, bf16[256,256]{1,0:T(8,128)(2,1)}, u32[]{:S(2)}) copy-start(bf16[256,256]{1,0:T(8,128)(2,1)} %constant.26.clone.ordering_ref) | copy-start | bytes 393220

commit v22 on v20

--- a/solution.py
+++ b/solution.py
@@ -223,55 +223,46 @@
 
 
 def first_y_kernel(merge, place_ref, to_ref, *refs):
-    in_refs, refs = refs[:4], refs[4:]
-    before, refs = (refs[:2], refs[2:]) if merge else ((), refs)
-    table_ref, *out_refs, pieces, held_out, held_before, semaphores = refs
-    gets = [
-        pltpu.make_async_copy(ref, pieces.at[s], semaphores.at[0, s])
-        for s, ref in enumerate(in_refs)
-    ]
-    puts = []
-    for i, shift in enumerate((1, 3, 2, 0)):
-        whole = merge and i >= 2
-        source = held_out.at[lax.rem(to_ref[0] + shift, 4)]
-        target = out_refs[i].at[:, 1 if whole else 0]
-        puts.append(pltpu.make_async_copy(source, target, semaphores.at[1, i]))
-    gets_before = [
-        pltpu.make_async_copy(ref, held_before.at[i], semaphores.at[2, i])
-        for i, ref in enumerate(before)
-    ]
-    puts_before = [
-        pltpu.make_async_copy(
-            held_before.at[i], out_refs[2 + i].at[:, 0:1], semaphores.at[2, 2 + i]
+    in_refs, refs = refs[:4], refs[6 if merge else 4 :]
+    table_ref, *out_refs, pieces, held_out, semaphores = refs
+
+    def gets(i):
+        x = pl.ds(lax.rem(to_ref[0] + (1, 3, 2, 0)[i], 4), 1)
+        return [
+            pltpu.make_async_copy(ref.at[:, x], pieces.at[i, s], semaphores.at[i, s])
+            for s, ref in enumerate(in_refs)
+        ]
+
+    def put(i):
+        target = out_refs[i].at[:, 1:2] if merge and i >= 2 else out_refs[i].at[:, 0:1]
+        return pltpu.make_async_copy(held_out.at[i], target, semaphores.at[i, 4])
+
+    for i in range(4):
+        for copy in gets(i):
+            copy.start()
+    g, h = place_ref[0], lax.rem(place_ref[0] + 3, 4)
+    for group in ((0, 1), (2, 3)):
+        for i in group:
+            for copy in gets(i):
+                copy.wait()
+        p0, p1, p2, p3 = (
+            jnp.concatenate([pieces[i, s] for i in group], axis=1) for s in range(4)
         )
-        for i in range(len(before))
-    ]
-    for copy in gets + gets_before:
-        copy.start()
-    for copy in gets_before:
-        copy.wait()
-    for copy in puts_before:
-        copy.start()
-    for copy in gets:
-        copy.wait()
-    g, h = place_ref[0], lax.rem(place_ref[0] + 3, 4)
-    pairs = [(pieces[0], pieces[2], g), (pieces[1], pieces[3], h)]
-    for odd, values in enumerate(transform(False, pairs, table_ref)):
-        for plane in range(2):
-            for x in range(4):
-                held_out[x, plane, odd * 128 : (odd + 1) * 128] = values[
-                    plane * 128 : (plane + 1) * 128, x * 128 : (x + 1) * 128
-                ]
-    for copy in puts:
-        copy.start()
-    for copy in puts + puts_before:
-        copy.wait()
+        for odd, values in enumerate(transform(False, [(p0, p2, g), (p1, p3, h)], table_ref)):
+            for plane in range(2):
+                for x, i in enumerate(group):
+                    held_out[i, plane, 0, odd * 128 : (odd + 1) * 128] = values[
+                        plane * 128 : (plane + 1) * 128, x * 128 : (x + 1) * 128
+                    ]
+        for i in group:
+            put(i).start()
+    for i in range(4):
+        put(i).wait()
 
 
 def first_y(place, to, pieces, table, before=()):
     merge = bool(before)
-    shape = (2, 1, KEPT, 128)
-    whole = (2, 2, KEPT, 128) if merge else shape
+    shape, whole = (2, 1, KEPT, 128), (2, 2, KEPT, 128)
     hbm = pl.BlockSpec(memory_space=pltpu.HBM)
     operands = in_hbm(*pieces, *before)
     return pl.pallas_call(
@@ -282,11 +273,11 @@
         out_specs=[hbm] * 4,
         out_shape=[pltpu.HBM(shape, jnp.float32)] * 2 + [pltpu.HBM(whole, jnp.float32)] * 2,
         scratch_shapes=[
-            pltpu.VMEM((4, 2, 4, 128, 128), jnp.float32),
-            pltpu.VMEM((4, 2, KEPT, 128), jnp.float32),
-            pltpu.VMEM((2,) + shape, jnp.float32),
-            pltpu.SemaphoreType.DMA((3, 4)),
+            pltpu.VMEM((4, 4, 2, 1, 128, 128), jnp.float32),
+            pltpu.VMEM((4,) + shape, jnp.float32),
+            pltpu.SemaphoreType.DMA((4, 5)),
         ],
+        input_output_aliases={6: 2, 7: 3} if merge else {},
         compiler_params=params(VMEM),
         cost_estimate=cost(512 * 512 * 512, 4 * MIB),
         name="first_y",
@@ -417,9 +408,9 @@
                     ]
 
     def place_rows(group, carry):
-        for offset in range(4):
-            x = group * 4 + offset
-            row = group * 2 + offset // 2 + 128 * (offset % 2)
+        for offset in range(8):
+            x = group * 8 + offset
+            row = group * 4 + offset // 2 + 128 * (offset % 2)
             for parity in range(2):
                 for half in range(2):
                     slot = slot_ref[x * 4 + parity * 2 + half]
@@ -429,7 +420,7 @@
                         ]
         return carry
 
-    lax.fori_loop(0, KEPT // 4, place_rows, 0)
+    lax.fori_loop(0, KEPT // 8, place_rows, 0)
 
 
 def third(slots, arrived, table_x, ordering):

time: 169 us -> 169 us (level)
  no operation moved by 1% of the time
where the time goes in v22:
time: 169 us
  blocking collectives  70.4 us (42%)
  waiting for transfers between devices  40.1 us (24%)
  Pallas kernels  30.6 us (18%)
  starting transfers between devices  24.2 us (14%)
  local copies, waits for them, and re-layouts  2.47 us (1%)
    all_to_all x1, blocking collectives, per_device(): lines = lax.all_to_all(planes, ALL, split_axis=0, concat_axis=0, tiled=True)  36.2 us
    all_to_all x1, blocking collectives, per_device(): lax.all_to_all(outgoing.reshape(128, 1, CAP, 2, BW), ALL, split_axis=0, c...  34.2 us
    ppermute x14, waiting for transfers between devices, shifted(): lax.ppermute(piece, axis, [(i, (i + shift) % size) for i in range(size)])  31.1 us
    ppermute x14, starting transfers between devices, shifted(): lax.ppermute(piece, axis, [(i, (i + shift) % size) for i in range(size)])  18.4 us
    pallas_call x5, Pallas kernels, scale(): pl.pallas_call(functools.partial(scale_kernel, part, shifts), in_specs=[p...  11.9 us
    all_to_all x1, waiting for transfers between devices, per_device(): a = lax.all_to_all(a, 'gz', split_axis=0, concat_axis=0, tiled=True)  9 us
    pallas_call x2, Pallas kernels, first_y(): pl.pallas_call(functools.partial(first_y_kernel, merge), in_specs=[pl.Blo...  7 us
    all_to_all x1, starting transfers between devices, per_device(): a = lax.all_to_all(a, 'gz', split_axis=0, concat_axis=0, tiled=True)  5.87 us
  transfers between devices with their start and end apart: 15, of which 7 were waited for; matrix products, arithmetic and copies ran while one was open for 0% of the time, Pallas kernels for 13%

profile of v22, /device:TPU:1, one launch (start us, length us, event | category | flops | bytes accessed | tf_op | source)
XLA Modules:
  0.0 168.7 jit_solution(8102141242560667744)
XLA Ops:
  0.0 3.4 %scale_a.1 = f32[4,2,8,128,128]{4,3,2,1,0:T(8,128)} custom-call(s32[1]{0:T(128)} %bitcast.place_ref.to_ref, bf16[2,8,8,128,128]{4,3,2,1,0:T(8,128)(2,1)} %bitcast.23, f32[8,8,128,128]{3,2,1,0:T(8,128)} %bitcast.28), custom_call_target="tpu_custom_call" | custom-call | flops 16 | bytes 128 | tf_op jit(solution)/shard_map/scale_a/pallas_call | solution.py:137
  3.4 5.9 %all-to-all-start = ((f32[4,2,8,128,128]{4,3,2,1,0:T(8,128)}), f32[4,2,8,128,128]{4,3,2,1,0:T(8,128)}, u32[]{:S(2)}, u32[]{:S(2)}) async-start(f32[4,2,8,128,128]{4,3,2,1,0:T(8,128)} %scale_a.1), calls=%async_computation | async-start | bytes 8388608 | tf_op jit(solution)/shard_map/all_to_all | solution.py:459
  9.3 2.3 %scale_b.4 = (f32[2,4,128,128]{3,2,1,0:T(8,128)}, f32[2,4,128,128]{3,2,1,0:T(8,128)}, f32[2,4,128,128]{3,2,1,0:T(8,128)}) custom-call(s32[1]{0:T(128)} %bitcast.3.place_ref.to_ref.y_ref, bf16[2,8,2,4,128,128]{5,4,3,2,1,0:T(8,128)(2,1)} %bitcast.24, f32[8,2,4,128,128]{4,3,2,1,0:T(8,128)} %bitcast.29), custom_call_target="tpu_custom_call" | custom-call | flops 12 | bytes 96 | tf_op jit(solution)/shard_map/scale_b/pallas_call | solution.py:137
  11.6 0.0 copy-start.10
  11.6 1.4 collective-permute-start
  12.9 2.6 %collective-permute-start.1 = (f32[2,4,128,128]{3,2,1,0:T(8,128)}, f32[2,4,128,128]{3,2,1,0:T(8,128)S(1)}, u32[]{:S(2)}, u32[]{:S(2)}) collective-permute-start(f32[2,4,128,128]{3,2,1,0:T(8,128)} %get-tuple-element.58), channel_id=1, source_target_pairs={{0,8},{4,12},{8,0},{12,4},{1,9},{5,13},{9,1},{13,5},{2,10},{6,14},... | collective-permute-start | bytes 1572872 | tf_op jit(solution)/shard_map/ppermute | solution.py:442
  15.6 1.1 collective-permute-start.2
  16.6 2.3 %scale_b.5 = (f32[2,4,128,128]{3,2,1,0:T(8,128)}, f32[2,4,128,128]{3,2,1,0:T(8,128)}, f32[2,4,128,128]{3,2,1,0:T(8,128)}) custom-call(s32[1]{0:T(128)} %bitcast.3.place_ref.to_ref.y_ref, bf16[2,8,2,4,128,128]{5,4,3,2,1,0:T(8,128)(2,1)} %bitcast.25, f32[8,2,4,128,128]{4,3,2,1,0:T(8,128)} %bitcast.30), custom_call_target="tpu_custom_call" | custom-call | flops 12 | bytes 96 | tf_op jit(solution)/shard_map/scale_b/pallas_call | solution.py:137
  18.9 0.5 collective-permute-start.4
  19.4 0.8 collective-permute-start.5
  20.2 0.1 copy.13
  20.3 0.2 fusion.2
  20.6 0.1 copy.14
  20.7 5.1 %collective-permute-done.refs_1_ = f32[2,4,128,128]{3,2,1,0:T(8,128)S(1)} collective-permute-done((f32[2,4,128,128]{3,2,1,0:T(8,128)}, f32[2,4,128,128]{3,2,1,0:T(8,128)S(1)}, u32[]{:S(2)}, u32[]{:S(2)}) %collective-permute-start) | collective-permute-done | bytes 524320 | tf_op jit(solution)/shard_map/ppermute | solution.py:442
  25.8 1.4 collective-permute-start.6
  27.2 0.4 fusion.1
  27.5 0.0 copy-start
  27.5 2.0 %scale_b.6.refs_0_ = f32[2,4,128,128]{3,2,1,0:T(8,128)} custom-call(s32[1]{0:T(128)} %bitcast.3.place_ref.to_ref.y_ref, bf16[2,8,2,4,128,128]{5,4,3,2,1,0:T(8,128)(2,1)} %bitcast.26, f32[8,2,4,128,128]{4,3,2,1,0:T(8,128)} %bitcast.31), custom_call_target="tpu_custom_call" | custom-call | flops 4 | bytes 32 | tf_op jit(solution)/shard_map/scale_b/pallas_call | solution.py:137
  29.5 8.6 %collective-permute-done.1.refs_2_ = f32[2,4,128,128]{3,2,1,0:T(8,128)S(1)} collective-permute-done((f32[2,4,128,128]{3,2,1,0:T(8,128)}, f32[2,4,128,128]{3,2,1,0:T(8,128)S(1)}, u32[]{:S(2)}, u32[]{:S(2)}) %collective-permute-start.1) | collective-permute-done | bytes 524320 | tf_op jit(solution)/shard_map/ppermute | solution.py:442
  38.2 0.8 collective-permute-done.2.refs_3_
  38.9 0.1 copy-done.8
  39.0 0.8 copy-done.9
  39.8 3.4 %first_y.2 = (f32[2,1,256,128]{3,2,1,0:T(8,128)}, f32[2,1,256,128]{3,2,1,0:T(8,128)}, f32[2,2,256,128]{3,2,1,0:T(8,128)}, f32[2,2,256,128]{3,2,1,0:T(8,128)}) custom-call(s32[1]{0:T(128)} %bitcast.3.place_ref.to_ref.y_ref, s32[1]{0:T(128)} %bitcast.place_ref.to_ref, f32[2,4,128,128]{3,2,1,0:T(8,128)} %scale_b.6.refs_0_, f32[2,4,128,128]{3,2,1,0:T(8,128)} %copy-done.7, ...), custom_call_target="tpu_custom_call" | custom-call | flops 2048 | bytes 64 | tf_op jit(solution)/shard_map/first_y/pallas_call | solution.py:268
  43.3 4.0 %collective-permute-start.8 = (f32[2,1,256,128]{3,2,1,0:T(8,128)}, f32[2,1,256,128]{3,2,1,0:T(8,128)S(1)}, u32[]{:S(2)}, u32[]{:S(2)}) collective-permute-start(f32[2,1,256,128]{3,2,1,0:T(8,128)} %get-tuple-element.69), channel_id=1, source_target_pairs={{0,3},{1,0},{2,1},{3,2},{4,7},{5,4},{6,5},{7,6},{8,11},{9,8},{10,9... | collective-permute-start | bytes 786440 | tf_op jit(solution)/shard_map/ppermute | solution.py:442
  47.2 0.0 collective-permute-start.7
  47.2 2.0 %scale_b.7.refs_0_ = f32[2,4,128,128]{3,2,1,0:T(8,128)} custom-call(s32[1]{0:T(128)} %bitcast.3.place_ref.to_ref.y_ref, bf16[2,8,2,4,128,128]{5,4,3,2,1,0:T(8,128)(2,1)} %bitcast.27, f32[8,2,4,128,128]{4,3,2,1,0:T(8,128)} %bitcast.32), custom_call_target="tpu_custom_call" | custom-call | flops 4 | bytes 32 | tf_op jit(solution)/shard_map/scale_b/pallas_call | solution.py:137
  49.2 9.0 %all-to-all-done.in_ref = f32[4,2,8,128,128]{4,3,2,1,0:T(8,128)} async-done(((f32[4,2,8,128,128]{4,3,2,1,0:T(8,128)}), f32[4,2,8,128,128]{4,3,2,1,0:T(8,128)}, u32[]{:S(2)}, u32[]{:S(2)}) %all-to-all-start) | async-done | bytes 4194336 | tf_op jit(solution)/shard_map/all_to_all | solution.py:459
  58.2 4.5 %first_z.1 = (f32[2,2,128,256]{3,2,1,0:T(8,128)}, f32[2,2,128,256]{3,2,1,0:T(8,128)}, f32[2,2,128,256]{3,2,1,0:T(8,128)}, f32[2,2,128,256]{3,2,1,0:T(8,128)}) custom-call(s32[1]{0:T(128)} %bitcast.3.place_ref.to_ref.y_ref, f32[4,2,8,128,128]{4,3,2,1,0:T(8,128)} %all-to-all-done.in_ref, bf16[2,2,2,256,256]{4,3,2,1,0:T(8,128)(2,1)S(1)} %copy-done.1), custom_call_target="tpu_custom_call" | custom-call | flops 4096 | bytes 128 | tf_op jit(solution)/shard_map/first_z/pallas_call | solution.py:205
  62.8 3.0 %collective-permute-start.3 = (f32[2,2,128,256]{3,2,1,0:T(8,128)}, f32[2,2,128,256]{3,2,1,0:T(8,128)S(1)}, u32[]{:S(2)}, u32[]{:S(2)}) collective-permute-start(f32[2,2,128,256]{3,2,1,0:T(8,128)} %get-tuple-element.64), channel_id=1, source_target_pairs={{0,8},{4,12},{8,0},{12,4},{1,9},{5,13},{9,1},{13,5},{2,10},{6,14},... | collective-permute-start | bytes 1572872 | tf_op jit(solution)/shard_map/ppermute | solution.py:442
  65.8 0.0 collective-permute-done.8.c3
  65.8 3.6 %first_y.3 = (f32[2,1,256,128]{3,2,1,0:T(8,128)}, f32[2,1,256,128]{3,2,1,0:T(8,128)}, f32[2,2,256,128]{3,2,1,0:T(8,128)}, f32[2,2,256,128]{3,2,1,0:T(8,128)}) custom-call(s32[1]{0:T(128)} %bitcast.3.place_ref.to_ref.y_ref, s32[1]{0:T(128)} %bitcast.place_ref.to_ref, ...), custom_call_target="tpu_custom_call", output_to_operand_aliasing={{2}: (6, {}), {3}: (7, {})} | custom-call | flops 2048 | bytes 64 | tf_op jit(solution)/shard_map/first_y/pallas_call | solution.py:268
  69.4 0.1 collective-permute-start.9
  69.5 0.6 collective-permute-start.12
  70.1 2.1 %collective-permute-start.13 = (f32[2,2,128,256]{3,2,1,0:T(8,128)S(1)}, f32[2,2,128,256]{3,2,1,0:T(8,128)S(1)}, u32[]{:S(2)}, u32[]{:S(2)}) collective-permute-start(f32[2,2,128,256]{3,2,1,0:T(8,128)S(1)} %copy-done.11), channel_id=1, source_target_pairs={{0,12},{4,0},{8,4},{12,8},{1,13},{5,1},{9,5},{13,9},{2,14},{6,2},{... | collective-permute-start | bytes 1572872 | tf_op jit(solution)/shard_map/ppermute | solution.py:442
  72.2 0.9 collective-permute-start.10
  73.1 2.5 %collective-permute-done.3.p2 = f32[2,2,128,256]{3,2,1,0:T(8,128)S(1)} collective-permute-done((f32[2,2,128,256]{3,2,1,0:T(8,128)}, f32[2,2,128,256]{3,2,1,0:T(8,128)S(1)}, u32[]{:S(2)}, u32[]{:S(2)}) %collective-permute-start.3) | collective-permute-done | bytes 524320 | tf_op jit(solution)/shard_map/ppermute | solution.py:442
  75.6 0.0 collective-permute-start.11
  75.7 0.9 part_y.1.part_a
  76.6 5.4 %collective-permute-done.9.b2 = f32[2,2,256,128]{3,2,1,0:T(8,128)S(1)} collective-permute-done((f32[2,2,256,128]{3,2,1,0:T(8,128)}, f32[2,2,256,128]{3,2,1,0:T(8,128)S(1)}, u32[]{:S(2)}, u32[]{:S(2)}) %collective-permute-start.9) | collective-permute-done | bytes 524320 | tf_op jit(solution)/shard_map/ppermute | solution.py:442
  82.0 8.6 %collective-permute-done.10.d1 = f32[2,1,256,128]{3,2,1,0:T(8,128)S(1)} collective-permute-done((f32[2,1,256,128]{3,2,1,0:T(8,128)}, f32[2,1,256,128]{3,2,1,0:T(8,128)S(1)}, u32[]{:S(2)}, u32[]{:S(2)}) %collective-permute-start.10) | collective-permute-done | bytes 262176 | tf_op jit(solution)/shard_map/ppermute | solution.py:442
  90.7 1.0 second_z.1.done_b
  91.7 1.5 second.1
  93.2 0.0 copy-start.3
  93.3 0.0 copy-start.5
  93.3 36.2 %all_to_all.22.in_ref = f32[128,2,2,8,128]{4,3,2,1,0:T(8,128)S(1)} all-to-all(f32[128,2,2,8,128]{4,3,2,1,0:T(8,128)S(1)} %second.1), channel_id=1, replica_groups=mesh['gx'=8,'gy'=4,'gz'=4] {'gx','gy','gz'}, dimensions={0} | all-to-all | bytes 4194304 | tf_op jit(solution)/shard_map/all_to_all | solution.py:483
  129.5 3.7 %third.1 = f32[4096,128]{1,0:T(8,128)S(1)} custom-call(s32[1024]{0:T(1024)S(1)} %multiply_add_fusion.slot_ref, f32[128,2,2,8,128]{4,3,2,1,0:T(8,128)S(1)} %all_to_all.22.in_ref, bf16[2,2,256,512]{3,2,1,0:T(8,128)(2,1)S(1)} %copy-done.3, bf16[256,256]{1,0:T(8,128)(2,1)S(1)} %copy-done.5), custom_call_target="tpu_custom_call" | custom-call | flops 3072 | bytes 96 | tf_op jit(solution)/shard_map/third/pallas_call | solution.py:428
  133.2 34.2 %all_to_all.23 = f32[128,1,16,2,128]{4,3,2,1,0:T(2,128)S(1)} all-to-all(f32[128,1,16,2,128]{4,3,2,1,0:T(2,128)S(1)} %bitcast.22), channel_id=1, replica_groups=mesh['gx'=8,'gy'=4,'gz'=4] {'gx','gy','gz'}, dimensions={0} | all-to-all | bytes 4194304 | tf_op jit(solution)/shard_map/all_to_all | solution.py:485
  167.4 1.3 copy.19
  (32 shorter events, 0.1 us)
Async XLA Ops:
  3.4 54.8 %all-to-all-start = ((f32[4,2,8,128,128]{4,3,2,1,0:T(8,128)}), f32[4,2,8,128,128]{4,3,2,1,0:T(8,128)}, u32[]{:S(2)}, u32[]{:S(2)}) async-start(f32[4,2,8,128,128]{4,3,2,1,0:T(8,128)} %scale_a.1), calls=%async_computation | async-start | bytes 8388608 | tf_op jit(solution)/shard_map/all_to_all | solution.py:459
  11.6 8.6 %copy-start.10 = (s32[1024,1]{0,1:T(1,128)S(1)}, s32[1024,1]{0,1:T(1,128)}, u32[]{:S(2)}) copy-start(s32[1024,1]{0,1:T(1,128)} %param.9) | copy-start | bytes 12292
  11.6 14.2 %collective-permute-start = (f32[2,4,128,128]{3,2,1,0:T(8,128)}, f32[2,4,128,128]{3,2,1,0:T(8,128)S(1)}, u32[]{:S(2)}, u32[]{:S(2)}) collective-permute-start(f32[2,4,128,128]{3,2,1,0:T(8,128)} %get-tuple-element.57), channel_id=1, source_target_pairs={{0,4},{4,8},{8,12},{12,0},{1,5},{5,9},{9,13},{13,1},{2,6},{6,10},{... | collective-permute-start | bytes 1572872 | tf_op jit(solution)/shard_map/ppermute | solution.py:442
  12.9 25.2 %collective-permute-start.1 = (f32[2,4,128,128]{3,2,1,0:T(8,128)}, f32[2,4,128,128]{3,2,1,0:T(8,128)S(1)}, u32[]{:S(2)}, u32[]{:S(2)}) collective-permute-start(f32[2,4,128,128]{3,2,1,0:T(8,128)} %get-tuple-element.58), channel_id=1, source_target_pairs={{0,8},{4,12},{8,0},{12,4},{1,9},{5,13},{9,1},{13,5},{2,10},{6,14},... | collective-permute-start | bytes 1572872 | tf_op jit(solution)/shard_map/ppermute | solution.py:442
  15.6 23.4 %collective-permute-start.2 = (f32[2,4,128,128]{3,2,1,0:T(8,128)}, f32[2,4,128,128]{3,2,1,0:T(8,128)S(1)}, u32[]{:S(2)}, u32[]{:S(2)}) collective-permute-start(f32[2,4,128,128]{3,2,1,0:T(8,128)} %get-tuple-element.59), channel_id=1, source_target_pairs={{0,12},{4,0},{8,4},{12,8},{1,13},{5,1},{9,5},{13,9},{2,14},{6,2},{... | collective-permute-start | bytes 1572872 | tf_op jit(solution)/shard_map/ppermute | solution.py:442
  18.9 43.8 %collective-permute-start.4 = (f32[2,4,128,128]{3,2,1,0:T(8,128)}, f32[2,4,128,128]{3,2,1,0:T(8,128)S(1)}, u32[]{:S(2)}, u32[]{:S(2)}) collective-permute-start(f32[2,4,128,128]{3,2,1,0:T(8,128)} %get-tuple-element.66), channel_id=1, source_target_pairs={{0,4},{4,8},{8,12},{12,0},{1,5},{5,9},{9,13},{13,1},{2,6},{6,10},{... | collective-permute-start | bytes 1572872 | tf_op jit(solution)/shard_map/ppermute | solution.py:442
  19.4 46.4 %collective-permute-start.5 = (f32[2,4,128,128]{3,2,1,0:T(8,128)}, f32[2,4,128,128]{3,2,1,0:T(8,128)}, u32[]{:S(2)}, u32[]{:S(2)}) collective-permute-start(f32[2,4,128,128]{3,2,1,0:T(8,128)} %get-tuple-element.67), channel_id=1, source_target_pairs={{0,8},{4,12},{8,0},{12,4},{1,9},{5,13},{9,1},{13,5},{2,10},{6,14},... | collective-permute-start | bytes 1572872 | tf_op jit(solution)/shard_map/ppermute | solution.py:442
  25.8 3.8 %copy-start.7 = (f32[2,4,128,128]{3,2,1,0:T(8,128)}, f32[2,4,128,128]{3,2,1,0:T(8,128)S(1)}, u32[]{:S(2)}) copy-start(f32[2,4,128,128]{3,2,1,0:T(8,128)S(1)} %collective-permute-done.refs_1_) | copy-start | bytes 1572868
  25.8 40.0 %collective-permute-start.6 = (f32[2,4,128,128]{3,2,1,0:T(8,128)}, f32[2,4,128,128]{3,2,1,0:T(8,128)}, u32[]{:S(2)}, u32[]{:S(2)}) collective-permute-start(f32[2,4,128,128]{3,2,1,0:T(8,128)} %get-tuple-element.68), channel_id=1, source_target_pairs={{0,12},{4,0},{8,4},{12,8},{1,13},{5,1},{9,5},{13,9},{2,14},{6,2},{... | collective-permute-start | bytes 1572872 | tf_op jit(solution)/shard_map/ppermute | solution.py:442
  27.5 12.3 %copy-start = (bf16[2,2,2,256,256]{4,3,2,1,0:T(8,128)(2,1)S(1)}, bf16[2,2,2,256,256]{4,3,2,1,0:T(8,128)(2,1)}, u32[]{:S(2)}) copy-start(bf16[2,2,2,256,256]{4,3,2,1,0:T(8,128)(2,1)} %constant.24.clone.refs_4_.table_ref.refs_6_.table_y_ref) | copy-start | bytes 3145732
  38.2 0.9 copy-start.8
  39.0 0.8 copy-start.9
  43.3 22.5 %collective-permute-start.8 = (f32[2,1,256,128]{3,2,1,0:T(8,128)}, f32[2,1,256,128]{3,2,1,0:T(8,128)S(1)}, u32[]{:S(2)}, u32[]{:S(2)}) collective-permute-start(f32[2,1,256,128]{3,2,1,0:T(8,128)} %get-tuple-element.69), channel_id=1, source_target_pairs={{0,3},{1,0},{2,1},{3,2},{4,7},{5,4},{6,5},{7,6},{8,11},{9,8},{10,9... | collective-permute-start | bytes 786440 | tf_op jit(solution)/shard_map/ppermute | solution.py:442
  47.2 18.5 %collective-permute-start.7 = (f32[2,1,256,128]{3,2,1,0:T(8,128)}, f32[2,1,256,128]{3,2,1,0:T(8,128)S(1)}, u32[]{:S(2)}, u32[]{:S(2)}) collective-permute-start(f32[2,1,256,128]{3,2,1,0:T(8,128)} %get-tuple-element.60), channel_id=1, source_target_pairs={{0,1},{1,2},{2,3},{3,0},{4,5},{5,6},{6,7},{7,4},{8,9},{9,10},{10,1... | collective-permute-start | bytes 786440 | tf_op jit(solution)/shard_map/ppermute | solution.py:442
  47.2 11.0 %copy-start.1 = (bf16[2,2,2,256,256]{4,3,2,1,0:T(8,128)(2,1)S(1)}, bf16[2,2,2,256,256]{4,3,2,1,0:T(8,128)(2,1)}, u32[]{:S(2)}) copy-start(bf16[2,2,2,256,256]{4,3,2,1,0:T(8,128)(2,1)} %constant.25.clone.table_ref) | copy-start | bytes 3145732
  62.7 3.0 %copy-start.6 = (f32[2,4,128,128]{3,2,1,0:T(8,128)}, f32[2,4,128,128]{3,2,1,0:T(8,128)S(1)}, u32[]{:S(2)}) copy-start(f32[2,4,128,128]{3,2,1,0:T(8,128)S(1)} %collective-permute-done.4.refs_1_) | copy-start | bytes 1572868
  62.8 12.9 %collective-permute-start.3 = (f32[2,2,128,256]{3,2,1,0:T(8,128)}, f32[2,2,128,256]{3,2,1,0:T(8,128)S(1)}, u32[]{:S(2)}, u32[]{:S(2)}) collective-permute-start(f32[2,2,128,256]{3,2,1,0:T(8,128)} %get-tuple-element.64), channel_id=1, source_target_pairs={{0,8},{4,12},{8,0},{12,4},{1,9},{5,13},{9,1},{13,5},{2,10},{6,14},... | collective-permute-start | bytes 1572872 | tf_op jit(solution)/shard_map/ppermute | solution.py:442
  65.8 3.7 %copy-start.12 = (f32[2,2,128,256]{3,2,1,0:T(8,128)S(1)}, f32[2,2,128,256]{3,2,1,0:T(8,128)}, u32[]{:S(2)}) copy-start(f32[2,2,128,256]{3,2,1,0:T(8,128)} %get-tuple-element.83) | copy-start | bytes 1572868
  65.8 4.4 %copy-start.11 = (f32[2,2,128,256]{3,2,1,0:T(8,128)S(1)}, f32[2,2,128,256]{3,2,1,0:T(8,128)}, u32[]{:S(2)}) copy-start(f32[2,2,128,256]{3,2,1,0:T(8,128)} %get-tuple-element.84) | copy-start | bytes 1572868
  65.8 9.8 %copy-start.4 = (f32[2,2,128,256]{3,2,1,0:T(8,128)S(1)}, f32[2,2,128,256]{3,2,1,0:T(8,128)}, u32[]{:S(2)}) copy-start(f32[2,2,128,256]{3,2,1,0:T(8,128)} %get-tuple-element.63.p0) | copy-start | bytes 1572868
  69.4 21.3 %copy-start.2 = (f32[2,2,256,128]{3,2,1,0:T(8,128)S(1)}, f32[2,2,256,128]{3,2,1,0:T(8,128)}, u32[]{:S(2)}) copy-start(f32[2,2,256,128]{3,2,1,0:T(8,128)} %get-tuple-element.77.b0) | copy-start | bytes 1572868
  69.4 12.6 %collective-permute-start.9 = (f32[2,2,256,128]{3,2,1,0:T(8,128)}, f32[2,2,256,128]{3,2,1,0:T(8,128)S(1)}, u32[]{:S(2)}, u32[]{:S(2)}) collective-permute-start(f32[2,2,256,128]{3,2,1,0:T(8,128)} %get-tuple-element.75), channel_id=1, source_target_pairs={{0,2},{1,3},{2,0},{3,1},{4,6},{5,7},{6,4},{7,5},{8,10},{9,11},{10,... | collective-permute-start | bytes 1572872 | tf_op jit(solution)/shard_map/ppermute | solution.py:442
  69.5 22.2 %collective-permute-start.12 = (f32[2,2,128,256]{3,2,1,0:T(8,128)S(1)}, f32[2,2,128,256]{3,2,1,0:T(8,128)S(1)}, u32[]{:S(2)}, u32[]{:S(2)}) collective-permute-start(f32[2,2,128,256]{3,2,1,0:T(8,128)S(1)} %copy-done.12), channel_id=1, source_target_pairs={{0,4},{4,8},{8,12},{12,0},{1,5},{5,9},{9,13},{13,1},{2,6},{6,10},{... | collective-permute-start | bytes 1572872 | tf_op jit(solution)/shard_map/ppermute | solution.py:442
  70.1 21.6 %collective-permute-start.13 = (f32[2,2,128,256]{3,2,1,0:T(8,128)S(1)}, f32[2,2,128,256]{3,2,1,0:T(8,128)S(1)}, u32[]{:S(2)}, u32[]{:S(2)}) collective-permute-start(f32[2,2,128,256]{3,2,1,0:T(8,128)S(1)} %copy-done.11), channel_id=1, source_target_pairs={{0,12},{4,0},{8,4},{12,8},{1,13},{5,1},{9,5},{13,9},{2,14},{6,2},{... | collective-permute-start | bytes 1572872 | tf_op jit(solution)/shard_map/ppermute | solution.py:442
  72.2 18.4 %collective-permute-start.10 = (f32[2,1,256,128]{3,2,1,0:T(8,128)}, f32[2,1,256,128]{3,2,1,0:T(8,128)S(1)}, u32[]{:S(2)}, u32[]{:S(2)}) collective-permute-start(f32[2,1,256,128]{3,2,1,0:T(8,128)} %get-tuple-element.81), channel_id=1, source_target_pairs={{0,1},{1,2},{2,3},{3,0},{4,5},{5,6},{6,7},{7,4},{8,9},{9,10},{10,1... | collective-permute-start | bytes 786440 | tf_op jit(solution)/shard_map/ppermute | solution.py:442
  75.6 15.0 %collective-permute-start.11 = (f32[2,1,256,128]{3,2,1,0:T(8,128)}, f32[2,1,256,128]{3,2,1,0:T(8,128)S(1)}, u32[]{:S(2)}, u32[]{:S(2)}) collective-permute-start(f32[2,1,256,128]{3,2,1,0:T(8,128)} %get-tuple-element.82), channel_id=1, source_target_pairs={{0,3},{1,0},{2,1},{3,2},{4,7},{5,4},{6,5},{7,6},{8,11},{9,8},{10,9... | collective-permute-start | bytes 786440 | tf_op jit(solution)/shard_map/ppermute | solution.py:442
  93.2 36.2 %copy-start.3 = (bf16[2,2,256,512]{3,2,1,0:T(8,128)(2,1)S(1)}, bf16[2,2,256,512]{3,2,1,0:T(8,128)(2,1)}, u32[]{:S(2)}) copy-start(bf16[2,2,256,512]{3,2,1,0:T(8,128)(2,1)} %constant.23.clone.table_ref) | copy-start | bytes 3145732
  93.3 36.2 %copy-start.5 = (bf16[256,256]{1,0:T(8,128)(2,1)S(1)}, bf16[256,256]{1,0:T(8,128)(2,1)}, u32[]{:S(2)}) copy-start(bf16[256,256]{1,0:T(8,128)(2,1)} %constant.26.clone.ordering_ref) | copy-start | bytes 393220

commit v23 on v22

--- a/solution.py
+++ b/solution.py
@@ -307,30 +307,22 @@
     )(place, *pieces, table)
 
 
-def second_z_kernel(place_ref, b0, b2, c1, c3, d1, d3, table_ref, out_ref):
-    g, h = place_ref[0], lax.rem(place_ref[0] + 3, 4)
-    for x, (p1, p3) in enumerate(((c1, c3), (d1, d3))):
-        cell = slice(x, x + 1)
-        pairs = [(b0[:, cell], b2[:, cell], g), (p1[...], p3[...], h)]
-        for odd, values in enumerate(transform(True, pairs, table_ref)):
-            out_ref[x, :, odd * 256 : (odd + 1) * 256] = values
-
-
-def second_z(place, pieces, table):
-    vmem = pl.BlockSpec(memory_space=pltpu.VMEM)
-    return pl.pallas_call(
-        second_z_kernel,
-        in_specs=[pl.BlockSpec(memory_space=pltpu.SMEM)] + [vmem] * 7,
-        out_specs=vmem,
-        out_shape=jax.ShapeDtypeStruct((2, KEPT, 512), jnp.float32),
-        compiler_params=params(VMEM),
-        cost_estimate=cost(512 * 512 * 512, 4 * MIB),
-        name="second_z",
-    )(place, *pieces, table)
-
-
 def second_kernel(
-    y_ref, part_a, a1, a3, table_y_ref, done_b, out_ref, held
+    y_ref,
+    z_ref,
+    part_a,
+    a1,
+    a3,
+    table_y_ref,
+    b0,
+    b2,
+    c1,
+    c3,
+    d1,
+    d3,
+    table_z_ref,
+    out_ref,
+    held,
 ):
     odd = pl.program_id(0)
 
@@ -352,8 +344,11 @@
                     half,
                     plane * 4 + x,
                 )
-    for half in range(2):
-        values = done_b[:, :, half * 256 : (half + 1) * 256].reshape(256, 256)
+    near, far = (
+        jnp.concatenate([c[...], d[...]], axis=1) for c, d in ((c1, d1), (c3, d3))
+    )
+    pairs = [(b0[...], b2[...], z_ref[0]), (near, far, lax.rem(z_ref[0] + 3, 4))]
+    for half, values in enumerate(transform(True, pairs, table_z_ref)):
         for x in range(2):
             for plane in range(2):
                 put(
@@ -364,26 +359,29 @@
     out_ref[...] = held[...].reshape(128, 1, 2, 8, 128)
 
 
-def second(gy, part_a, pieces_a, table_y, done_b):
+def second(gy, gz, part_a, pieces_a, table_y, pieces_b, table_z):
+    def rows(cells):
+        return pl.BlockSpec((2, cells, 128, 128), lambda i, gy, gz: (0, 0, i, 0))
+
     return pl.pallas_call(
         second_kernel,
         grid_spec=pltpu.PrefetchScalarGridSpec(
-            num_scalar_prefetch=1,
+            num_scalar_prefetch=2,
             grid=(2,),
-            in_specs=[pl.BlockSpec((1, KEPT, 512), lambda i, gy: (i, 0, 0))]
-            + [pl.BlockSpec((2, 2, 128, KEPT), lambda i, gy: (0, 0, 0, 0))] * 2
-            + [
-                pl.BlockSpec((2, 2, 1, KEPT, KEPT), lambda i, gy: (0, 0, i, 0, 0)),
-                pl.BlockSpec((2, 128, 512), lambda i, gy: (0, i, 0)),
-            ],
-            out_specs=pl.BlockSpec((128, 1, 2, 8, 128), lambda i, gy: (0, i, 0, 0, 0)),
+            in_specs=[pl.BlockSpec((1, KEPT, 512), lambda i, gy, gz: (i, 0, 0))]
+            + [pl.BlockSpec((2, 2, 128, KEPT), lambda i, gy, gz: (0, 0, 0, 0))] * 2
+            + [pl.BlockSpec((2, 2, 1, KEPT, KEPT), lambda i, gy, gz: (0, 0, i, 0, 0))]
+            + [rows(2)] * 2
+            + [rows(1)] * 4
+            + [pl.BlockSpec(table_z.shape, lambda i, gy, gz: (0, 0, 0, 0, 0))],
+            out_specs=pl.BlockSpec((128, 1, 2, 8, 128), lambda i, gy, gz: (0, i, 0, 0, 0)),
             scratch_shapes=[pltpu.VMEM((2048, 128), jnp.float32)],
         ),
         out_shape=jax.ShapeDtypeStruct((128, 2, 2, 8, 128), jnp.float32),
         compiler_params=params(VMEM),
-        cost_estimate=cost(512 * 512 * 256, 8 * MIB),
+        cost_estimate=cost(512 * 512 * 768, 8 * MIB),
         name="second",
-    )(gy, part_a, *pieces_a, table_y, done_b)
+    )(gy, gz, part_a, *pieces_a, table_y, *pieces_b, table_z)
 
 
 def third_kernel(slot_ref, in_ref, table_ref, ordering_ref, out_ref, held):
@@ -477,9 +475,11 @@
 
     part_a = part_y(gy, (a0, a2), table_y)
     part_a, b2 = lax.optimization_barrier((part_a, b2))
-    done_b = second_z(gz, (b0, b2, c1, c3, d1, d3), table_z)
-    part_a, done_b, a1, a3 = lax.optimization_barrier((part_a, done_b, a1, a3))
-    planes = second(gy, part_a, (a1, a3), table_y, done_b)
+    b2, d1, d3 = lax.optimization_barrier((b2, d1, d3))
+    part_a, a1, a3, d1, d3 = lax.optimization_barrier((part_a, a1, a3, d1, d3))
+    planes = second(
+        gy, gz, part_a, (a1, a3), table_y, (b0, b2, c1, c3, d1, d3), table_z
+    )
     lines = lax.all_to_all(planes, ALL, split_axis=0, concat_axis=0, tiled=True)
     outgoing = third(slots, lines, table_x, ordering)
     return lax.all_to_all(

time: 169 us -> 169 us (level)
  transfers between devices with their start and end apart: 15 -> 15, of which waited for: 7 -> 7; matrix products, arithmetic and copies ran while one was open for 0% -> 0% of each run, Pallas kernels for 13% -> 12%
where the time goes in v23:
time: 169 us
  blocking collectives  70.4 us (42%)
  waiting for transfers between devices  40.9 us (24%)
  Pallas kernels  30.8 us (18%)
  starting transfers between devices  24.2 us (14%)
    all_to_all x1, blocking collectives, per_device(): lines = lax.all_to_all(planes, ALL, split_axis=0, concat_axis=0, tiled=True)  36.2 us
    all_to_all x1, blocking collectives, per_device(): lax.all_to_all(outgoing.reshape(128, 1, CAP, 2, BW), ALL, split_axis=0, c...  34.2 us
    ppermute x14, waiting for transfers between devices, shifted(): lax.ppermute(piece, axis, [(i, (i + shift) % size) for i in range(size)])  31.1 us
    ppermute x14, starting transfers between devices, shifted(): lax.ppermute(piece, axis, [(i, (i + shift) % size) for i in range(size)])  18.4 us
    pallas_call x5, Pallas kernels, scale(): pl.pallas_call(functools.partial(scale_kernel, part, shifts), in_specs=[p...  11.9 us
    all_to_all x1, waiting for transfers between devices, per_device(): a = lax.all_to_all(a, 'gz', split_axis=0, concat_axis=0, tiled=True)  9.81 us
    pallas_call x2, Pallas kernels, first_y(): pl.pallas_call(functools.partial(first_y_kernel, merge), in_specs=[pl.Blo...  7.05 us
    all_to_all x1, starting transfers between devices, per_device(): a = lax.all_to_all(a, 'gz', split_axis=0, concat_axis=0, tiled=True)  5.87 us
  transfers between devices with their start and end apart: 15, of which 7 were waited for; matrix products, arithmetic and copies ran while one was open for 0% of the time, Pallas kernels for 12%

profile of v23, /device:TPU:1, one launch (start us, length us, event | category | flops | bytes accessed | tf_op | source)
XLA Modules:
  0.0 168.8 jit_solution(10697424121021257835)
XLA Ops:
  0.0 3.4 %scale_a.1 = f32[4,2,8,128,128]{4,3,2,1,0:T(8,128)} custom-call(s32[1]{0:T(128)} %bitcast.place_ref.to_ref.z_ref, bf16[2,8,8,128,128]{4,3,2,1,0:T(8,128)(2,1)} %bitcast.23, f32[8,8,128,128]{3,2,1,0:T(8,128)} %bitcast.28), custom_call_target="tpu_custom_call" | custom-call | flops 16 | bytes 128 | tf_op jit(solution)/shard_map/scale_a/pallas_call | solution.py:137
  3.4 5.9 %all-to-all-start = ((f32[4,2,8,128,128]{4,3,2,1,0:T(8,128)}), f32[4,2,8,128,128]{4,3,2,1,0:T(8,128)}, u32[]{:S(2)}, u32[]{:S(2)}) async-start(f32[4,2,8,128,128]{4,3,2,1,0:T(8,128)} %scale_a.1), calls=%async_computation | async-start | bytes 8388608 | tf_op jit(solution)/shard_map/all_to_all | solution.py:457
  9.3 2.3 %scale_b.4 = (f32[2,4,128,128]{3,2,1,0:T(8,128)}, f32[2,4,128,128]{3,2,1,0:T(8,128)}, f32[2,4,128,128]{3,2,1,0:T(8,128)}) custom-call(s32[1]{0:T(128)} %bitcast.3.place_ref.to_ref.y_ref, bf16[2,8,2,4,128,128]{5,4,3,2,1,0:T(8,128)(2,1)} %bitcast.24, f32[8,2,4,128,128]{4,3,2,1,0:T(8,128)} %bitcast.29), custom_call_target="tpu_custom_call" | custom-call | flops 12 | bytes 96 | tf_op jit(solution)/shard_map/scale_b/pallas_call | solution.py:137
  11.6 0.0 copy-start.9
  11.6 1.4 collective-permute-start
  12.9 2.6 %collective-permute-start.1 = (f32[2,4,128,128]{3,2,1,0:T(8,128)}, f32[2,4,128,128]{3,2,1,0:T(8,128)S(1)}, u32[]{:S(2)}, u32[]{:S(2)}) collective-permute-start(f32[2,4,128,128]{3,2,1,0:T(8,128)} %get-tuple-element.62), channel_id=1, source_target_pairs={{0,8},{4,12},{8,0},{12,4},{1,9},{5,13},{9,1},{13,5},{2,10},{6,14},... | collective-permute-start | bytes 1572872 | tf_op jit(solution)/shard_map/ppermute | solution.py:440
  15.6 1.1 collective-permute-start.2
  16.6 2.3 %scale_b.5 = (f32[2,4,128,128]{3,2,1,0:T(8,128)}, f32[2,4,128,128]{3,2,1,0:T(8,128)}, f32[2,4,128,128]{3,2,1,0:T(8,128)}) custom-call(s32[1]{0:T(128)} %bitcast.3.place_ref.to_ref.y_ref, bf16[2,8,2,4,128,128]{5,4,3,2,1,0:T(8,128)(2,1)} %bitcast.25, f32[8,2,4,128,128]{4,3,2,1,0:T(8,128)} %bitcast.30), custom_call_target="tpu_custom_call" | custom-call | flops 12 | bytes 96 | tf_op jit(solution)/shard_map/scale_b/pallas_call | solution.py:137
  18.9 0.5 collective-permute-start.4
  19.4 0.8 collective-permute-start.5
  20.2 0.1 copy.13
  20.3 0.2 fusion.2
  20.6 0.1 copy.14
  20.7 5.1 %collective-permute-done.refs_1_ = f32[2,4,128,128]{3,2,1,0:T(8,128)S(1)} collective-permute-done((f32[2,4,128,128]{3,2,1,0:T(8,128)}, f32[2,4,128,128]{3,2,1,0:T(8,128)S(1)}, u32[]{:S(2)}, u32[]{:S(2)}) %collective-permute-start) | collective-permute-done | bytes 524320 | tf_op jit(solution)/shard_map/ppermute | solution.py:440
  25.8 1.4 collective-permute-start.6
  27.2 0.4 fusion.1
  27.5 0.0 copy-start
  27.5 2.0 %scale_b.6.refs_0_ = f32[2,4,128,128]{3,2,1,0:T(8,128)} custom-call(s32[1]{0:T(128)} %bitcast.3.place_ref.to_ref.y_ref, bf16[2,8,2,4,128,128]{5,4,3,2,1,0:T(8,128)(2,1)} %bitcast.26, f32[8,2,4,128,128]{4,3,2,1,0:T(8,128)} %bitcast.31), custom_call_target="tpu_custom_call" | custom-call | flops 4 | bytes 32 | tf_op jit(solution)/shard_map/scale_b/pallas_call | solution.py:137
  29.5 8.6 %collective-permute-done.1.refs_2_ = f32[2,4,128,128]{3,2,1,0:T(8,128)S(1)} collective-permute-done((f32[2,4,128,128]{3,2,1,0:T(8,128)}, f32[2,4,128,128]{3,2,1,0:T(8,128)S(1)}, u32[]{:S(2)}, u32[]{:S(2)}) %collective-permute-start.1) | collective-permute-done | bytes 524320 | tf_op jit(solution)/shard_map/ppermute | solution.py:440
  38.2 0.8 collective-permute-done.2.refs_3_
  38.9 0.0 copy-done.8
  38.9 3.5 %first_y.2 = (f32[2,1,256,128]{3,2,1,0:T(8,128)}, f32[2,1,256,128]{3,2,1,0:T(8,128)}, f32[2,2,256,128]{3,2,1,0:T(8,128)}, f32[2,2,256,128]{3,2,1,0:T(8,128)}) custom-call(s32[1]{0:T(128)} %bitcast.3.place_ref.to_ref.y_ref, s32[1]{0:T(128)} %bitcast.place_ref.to_ref.z_ref, f32[2,4,128,128]{3,2,1,0:T(8,128)} %scale_b.6.refs_0_, f32[2,4,128,128]{3,2,1,0:T(8,128)} %copy-done.7, ...), custom_call_target="tpu_custom_call" | custom-call | flops 2048 | bytes 64 | tf_op jit(solution)/shard_map/first_y/pallas_call | solution.py:268
  42.4 4.0 %collective-permute-start.8 = (f32[2,1,256,128]{3,2,1,0:T(8,128)}, f32[2,1,256,128]{3,2,1,0:T(8,128)S(1)}, u32[]{:S(2)}, u32[]{:S(2)}) collective-permute-start(f32[2,1,256,128]{3,2,1,0:T(8,128)} %get-tuple-element.73), channel_id=1, source_target_pairs={{0,3},{1,0},{2,1},{3,2},{4,7},{5,4},{6,5},{7,6},{8,11},{9,8},{10,9... | collective-permute-start | bytes 786440 | tf_op jit(solution)/shard_map/ppermute | solution.py:440
  46.4 0.0 collective-permute-start.7
  46.4 2.0 %scale_b.7.refs_0_ = f32[2,4,128,128]{3,2,1,0:T(8,128)} custom-call(s32[1]{0:T(128)} %bitcast.3.place_ref.to_ref.y_ref, bf16[2,8,2,4,128,128]{5,4,3,2,1,0:T(8,128)(2,1)} %bitcast.27, f32[8,2,4,128,128]{4,3,2,1,0:T(8,128)} %bitcast.32), custom_call_target="tpu_custom_call" | custom-call | flops 4 | bytes 32 | tf_op jit(solution)/shard_map/scale_b/pallas_call | solution.py:137
  48.4 9.8 %all-to-all-done.in_ref = f32[4,2,8,128,128]{4,3,2,1,0:T(8,128)} async-done(((f32[4,2,8,128,128]{4,3,2,1,0:T(8,128)}), f32[4,2,8,128,128]{4,3,2,1,0:T(8,128)}, u32[]{:S(2)}, u32[]{:S(2)}) %all-to-all-start) | async-done | bytes 4194336 | tf_op jit(solution)/shard_map/all_to_all | solution.py:457
  58.2 4.6 %first_z.1 = (f32[2,2,128,256]{3,2,1,0:T(8,128)}, f32[2,2,128,256]{3,2,1,0:T(8,128)}, f32[2,2,128,256]{3,2,1,0:T(8,128)}, f32[2,2,128,256]{3,2,1,0:T(8,128)}) custom-call(s32[1]{0:T(128)} %bitcast.3.place_ref.to_ref.y_ref, f32[4,2,8,128,128]{4,3,2,1,0:T(8,128)} %all-to-all-done.in_ref, bf16[2,2,2,256,256]{4,3,2,1,0:T(8,128)(2,1)S(1)} %copy-done.1), custom_call_target="tpu_custom_call" | custom-call | flops 4096 | bytes 128 | tf_op jit(solution)/shard_map/first_z/pallas_call | solution.py:205
  62.8 3.0 %collective-permute-start.3 = (f32[2,2,128,256]{3,2,1,0:T(8,128)}, f32[2,2,128,256]{3,2,1,0:T(8,128)S(1)}, u32[]{:S(2)}, u32[]{:S(2)}) collective-permute-start(f32[2,2,128,256]{3,2,1,0:T(8,128)} %get-tuple-element.68), channel_id=1, source_target_pairs={{0,8},{4,12},{8,0},{12,4},{1,9},{5,13},{9,1},{13,5},{2,10},{6,14},... | collective-permute-start | bytes 1572872 | tf_op jit(solution)/shard_map/ppermute | solution.py:440
  65.8 0.0 collective-permute-done.7.c1
  65.9 3.6 %first_y.3 = (f32[2,1,256,128]{3,2,1,0:T(8,128)}, f32[2,1,256,128]{3,2,1,0:T(8,128)}, f32[2,2,256,128]{3,2,1,0:T(8,128)}, f32[2,2,256,128]{3,2,1,0:T(8,128)}) custom-call(s32[1]{0:T(128)} %bitcast.3.place_ref.to_ref.y_ref, s32[1]{0:T(128)} %bitcast.place_ref.to_ref.z_ref, ...), custom_call_target="tpu_custom_call", output_to_operand_aliasing={{2}: (6, {}), {3}: (7, {})} | custom-call | flops 2048 | bytes 64 | tf_op jit(solution)/shard_map/first_y/pallas_call | solution.py:268
  69.4 0.1 collective-permute-start.9
  69.6 0.7 collective-permute-start.10
  70.2 2.1 %collective-permute-start.11 = (f32[2,2,128,256]{3,2,1,0:T(8,128)S(1)}, f32[2,2,128,256]{3,2,1,0:T(8,128)S(1)}, u32[]{:S(2)}, u32[]{:S(2)}) collective-permute-start(f32[2,2,128,256]{3,2,1,0:T(8,128)S(1)} %copy-done.10), channel_id=1, source_target_pairs={{0,12},{4,0},{8,4},{12,8},{1,13},{5,1},{9,5},{13,9},{2,14},{6,2},{... | collective-permute-start | bytes 1572872 | tf_op jit(solution)/shard_map/ppermute | solution.py:440
  72.3 0.9 collective-permute-start.12
  73.2 2.5 %collective-permute-done.3.p2 = f32[2,2,128,256]{3,2,1,0:T(8,128)S(1)} collective-permute-done((f32[2,2,128,256]{3,2,1,0:T(8,128)}, f32[2,2,128,256]{3,2,1,0:T(8,128)S(1)}, u32[]{:S(2)}, u32[]{:S(2)}) %collective-permute-start.3) | collective-permute-done | bytes 524320 | tf_op jit(solution)/shard_map/ppermute | solution.py:440
  75.7 0.9 part_y.1.part_a
  76.7 5.4 %collective-permute-done.9.b2 = f32[2,2,256,128]{3,2,1,0:T(8,128)S(1)} collective-permute-done((f32[2,2,256,128]{3,2,1,0:T(8,128)}, f32[2,2,256,128]{3,2,1,0:T(8,128)S(1)}, u32[]{:S(2)}, u32[]{:S(2)}) %collective-permute-start.9) | collective-permute-done | bytes 524320 | tf_op jit(solution)/shard_map/ppermute | solution.py:440
  82.1 8.6 %collective-permute-done.12.d1 = f32[2,1,256,128]{3,2,1,0:T(8,128)S(1)} collective-permute-done((f32[2,1,256,128]{3,2,1,0:T(8,128)}, f32[2,1,256,128]{3,2,1,0:T(8,128)S(1)}, u32[]{:S(2)}, u32[]{:S(2)}) %collective-permute-start.12) | collective-permute-done | bytes 262176 | tf_op jit(solution)/shard_map/ppermute | solution.py:440
  90.7 0.0 collective-permute-done.13.d3
  90.7 0.0 collective-permute-done.10.a1
  90.7 0.0 collective-permute-done.11.a3
  90.7 2.7 %second.1 = f32[128,2,2,8,128]{4,3,2,1,0:T(8,128)S(1)} custom-call(s32[1]{0:T(128)} %bitcast.3.place_ref.to_ref.y_ref, s32[1]{0:T(128)} %bitcast.place_ref.to_ref.z_ref, f32[2,256,512]{2,1,0:T(8,128)S(1)} %part_y.1.part_a, f32[2,2,128,256]{3,2,1,0:T(8,128)S(1)} %collective-permute-done.10.a1, f32[2,2,128,256]{3,2,1,0:T(8,128)S(1)} %collective-permute-done.11.a3, ...), custom_call_target="tpu_custom_call" | custom-call | flops 3072 | bytes 128 | tf_op jit(solution)/shard_map/second/pallas_call | solution.py:366
  93.4 0.0 copy-start.3
  93.4 0.0 copy-start.5
  93.4 36.2 %all_to_all.22.in_ref = f32[128,2,2,8,128]{4,3,2,1,0:T(8,128)S(1)} all-to-all(f32[128,2,2,8,128]{4,3,2,1,0:T(8,128)S(1)} %second.1), channel_id=1, replica_groups=mesh['gx'=8,'gy'=4,'gz'=4] {'gx','gy','gz'}, dimensions={0} | all-to-all | bytes 4194304 | tf_op jit(solution)/shard_map/all_to_all | solution.py:483
  129.6 3.7 %third.1 = f32[4096,128]{1,0:T(8,128)S(1)} custom-call(s32[1024]{0:T(1024)S(1)} %multiply_add_fusion.slot_ref, f32[128,2,2,8,128]{4,3,2,1,0:T(8,128)S(1)} %all_to_all.22.in_ref, bf16[2,2,256,512]{3,2,1,0:T(8,128)(2,1)S(1)} %copy-done.3, bf16[256,256]{1,0:T(8,128)(2,1)S(1)} %copy-done.5), custom_call_target="tpu_custom_call" | custom-call | flops 3072 | bytes 96 | tf_op jit(solution)/shard_map/third/pallas_call | solution.py:426
  133.3 34.2 %all_to_all.23 = f32[128,1,16,2,128]{4,3,2,1,0:T(2,128)S(1)} all-to-all(f32[128,1,16,2,128]{4,3,2,1,0:T(2,128)S(1)} %bitcast.22), channel_id=1, replica_groups=mesh['gx'=8,'gy'=4,'gz'=4] {'gx','gy','gz'}, dimensions={0} | all-to-all | bytes 4194304 | tf_op jit(solution)/shard_map/all_to_all | solution.py:485
  167.5 1.3 copy.19
  (29 shorter events, 0.1 us)
Async XLA Ops:
  3.4 54.8 %all-to-all-start = ((f32[4,2,8,128,128]{4,3,2,1,0:T(8,128)}), f32[4,2,8,128,128]{4,3,2,1,0:T(8,128)}, u32[]{:S(2)}, u32[]{:S(2)}) async-start(f32[4,2,8,128,128]{4,3,2,1,0:T(8,128)} %scale_a.1), calls=%async_computation | async-start | bytes 8388608 | tf_op jit(solution)/shard_map/all_to_all | solution.py:457
  11.6 8.6 %copy-start.9 = (s32[1024,1]{0,1:T(1,128)S(1)}, s32[1024,1]{0,1:T(1,128)}, u32[]{:S(2)}) copy-start(s32[1024,1]{0,1:T(1,128)} %param.9) | copy-start | bytes 12292
  11.6 14.2 %collective-permute-start = (f32[2,4,128,128]{3,2,1,0:T(8,128)}, f32[2,4,128,128]{3,2,1,0:T(8,128)S(1)}, u32[]{:S(2)}, u32[]{:S(2)}) collective-permute-start(f32[2,4,128,128]{3,2,1,0:T(8,128)} %get-tuple-element.61), channel_id=1, source_target_pairs={{0,4},{4,8},{8,12},{12,0},{1,5},{5,9},{9,13},{13,1},{2,6},{6,10},{... | collective-permute-start | bytes 1572872 | tf_op jit(solution)/shard_map/ppermute | solution.py:440
  12.9 25.2 %collective-permute-start.1 = (f32[2,4,128,128]{3,2,1,0:T(8,128)}, f32[2,4,128,128]{3,2,1,0:T(8,128)S(1)}, u32[]{:S(2)}, u32[]{:S(2)}) collective-permute-start(f32[2,4,128,128]{3,2,1,0:T(8,128)} %get-tuple-element.62), channel_id=1, source_target_pairs={{0,8},{4,12},{8,0},{12,4},{1,9},{5,13},{9,1},{13,5},{2,10},{6,14},... | collective-permute-start | bytes 1572872 | tf_op jit(solution)/shard_map/ppermute | solution.py:440
  15.6 23.4 %collective-permute-start.2 = (f32[2,4,128,128]{3,2,1,0:T(8,128)}, f32[2,4,128,128]{3,2,1,0:T(8,128)}, u32[]{:S(2)}, u32[]{:S(2)}) collective-permute-start(f32[2,4,128,128]{3,2,1,0:T(8,128)} %get-tuple-element.63), channel_id=1, source_target_pairs={{0,12},{4,0},{8,4},{12,8},{1,13},{5,1},{9,5},{13,9},{2,14},{6,2},{... | collective-permute-start | bytes 1572872 | tf_op jit(solution)/shard_map/ppermute | solution.py:440
  18.9 43.9 %collective-permute-start.4 = (f32[2,4,128,128]{3,2,1,0:T(8,128)}, f32[2,4,128,128]{3,2,1,0:T(8,128)S(1)}, u32[]{:S(2)}, u32[]{:S(2)}) collective-permute-start(f32[2,4,128,128]{3,2,1,0:T(8,128)} %get-tuple-element.70), channel_id=1, source_target_pairs={{0,4},{4,8},{8,12},{12,0},{1,5},{5,9},{9,13},{13,1},{2,6},{6,10},{... | collective-permute-start | bytes 1572872 | tf_op jit(solution)/shard_map/ppermute | solution.py:440
  19.4 46.4 %collective-permute-start.5 = (f32[2,4,128,128]{3,2,1,0:T(8,128)}, f32[2,4,128,128]{3,2,1,0:T(8,128)}, u32[]{:S(2)}, u32[]{:S(2)}) collective-permute-start(f32[2,4,128,128]{3,2,1,0:T(8,128)} %get-tuple-element.71), channel_id=1, source_target_pairs={{0,8},{4,12},{8,0},{12,4},{1,9},{5,13},{9,1},{13,5},{2,10},{6,14},... | collective-permute-start | bytes 1572872 | tf_op jit(solution)/shard_map/ppermute | solution.py:440
  25.8 3.8 %copy-start.7 = (f32[2,4,128,128]{3,2,1,0:T(8,128)}, f32[2,4,128,128]{3,2,1,0:T(8,128)S(1)}, u32[]{:S(2)}) copy-start(f32[2,4,128,128]{3,2,1,0:T(8,128)S(1)} %collective-permute-done.refs_1_) | copy-start | bytes 1572868
  25.8 40.0 %collective-permute-start.6 = (f32[2,4,128,128]{3,2,1,0:T(8,128)}, f32[2,4,128,128]{3,2,1,0:T(8,128)}, u32[]{:S(2)}, u32[]{:S(2)}) collective-permute-start(f32[2,4,128,128]{3,2,1,0:T(8,128)} %get-tuple-element.72), channel_id=1, source_target_pairs={{0,12},{4,0},{8,4},{12,8},{1,13},{5,1},{9,5},{13,9},{2,14},{6,2},{... | collective-permute-start | bytes 1572872 | tf_op jit(solution)/shard_map/ppermute | solution.py:440
  27.5 11.4 %copy-start = (bf16[2,2,2,256,256]{4,3,2,1,0:T(8,128)(2,1)S(1)}, bf16[2,2,2,256,256]{4,3,2,1,0:T(8,128)(2,1)}, u32[]{:S(2)}) copy-start(bf16[2,2,2,256,256]{4,3,2,1,0:T(8,128)(2,1)} %constant.24.clone.refs_4_.table_ref.refs_6_.table_y_ref) | copy-start | bytes 3145732
  38.2 0.8 copy-start.8
  42.4 23.4 %collective-permute-start.8 = (f32[2,1,256,128]{3,2,1,0:T(8,128)}, f32[2,1,256,128]{3,2,1,0:T(8,128)S(1)}, u32[]{:S(2)}, u32[]{:S(2)}) collective-permute-start(f32[2,1,256,128]{3,2,1,0:T(8,128)} %get-tuple-element.73), channel_id=1, source_target_pairs={{0,3},{1,0},{2,1},{3,2},{4,7},{5,4},{6,5},{7,6},{8,11},{9,8},{10,9... | collective-permute-start | bytes 786440 | tf_op jit(solution)/shard_map/ppermute | solution.py:440
  46.4 19.4 %collective-permute-start.7 = (f32[2,1,256,128]{3,2,1,0:T(8,128)}, f32[2,1,256,128]{3,2,1,0:T(8,128)S(1)}, u32[]{:S(2)}, u32[]{:S(2)}) collective-permute-start(f32[2,1,256,128]{3,2,1,0:T(8,128)} %get-tuple-element.64), channel_id=1, source_target_pairs={{0,1},{1,2},{2,3},{3,0},{4,5},{5,6},{6,7},{7,4},{8,9},{9,10},{10,1... | collective-permute-start | bytes 786440 | tf_op jit(solution)/shard_map/ppermute | solution.py:440
  46.4 11.8 %copy-start.1 = (bf16[2,2,2,256,256]{4,3,2,1,0:T(8,128)(2,1)S(1)}, bf16[2,2,2,256,256]{4,3,2,1,0:T(8,128)(2,1)}, u32[]{:S(2)}) copy-start(bf16[2,2,2,256,256]{4,3,2,1,0:T(8,128)(2,1)} %constant.25.clone.table_ref.table_z_ref) | copy-start | bytes 3145732
  62.8 3.0 %copy-start.6 = (f32[2,4,128,128]{3,2,1,0:T(8,128)}, f32[2,4,128,128]{3,2,1,0:T(8,128)S(1)}, u32[]{:S(2)}) copy-start(f32[2,4,128,128]{3,2,1,0:T(8,128)S(1)} %collective-permute-done.4.refs_1_) | copy-start | bytes 1572868
  62.8 12.9 %collective-permute-start.3 = (f32[2,2,128,256]{3,2,1,0:T(8,128)}, f32[2,2,128,256]{3,2,1,0:T(8,128)S(1)}, u32[]{:S(2)}, u32[]{:S(2)}) collective-permute-start(f32[2,2,128,256]{3,2,1,0:T(8,128)} %get-tuple-element.68), channel_id=1, source_target_pairs={{0,8},{4,12},{8,0},{12,4},{1,9},{5,13},{9,1},{13,5},{2,10},{6,14},... | collective-permute-start | bytes 1572872 | tf_op jit(solution)/shard_map/ppermute | solution.py:440
  65.8 3.7 %copy-start.11 = (f32[2,2,128,256]{3,2,1,0:T(8,128)S(1)}, f32[2,2,128,256]{3,2,1,0:T(8,128)}, u32[]{:S(2)}) copy-start(f32[2,2,128,256]{3,2,1,0:T(8,128)} %get-tuple-element.81) | copy-start | bytes 1572868
  65.8 4.4 %copy-start.10 = (f32[2,2,128,256]{3,2,1,0:T(8,128)S(1)}, f32[2,2,128,256]{3,2,1,0:T(8,128)}, u32[]{:S(2)}) copy-start(f32[2,2,128,256]{3,2,1,0:T(8,128)} %get-tuple-element.82) | copy-start | bytes 1572868
  65.8 9.9 %copy-start.4 = (f32[2,2,128,256]{3,2,1,0:T(8,128)S(1)}, f32[2,2,128,256]{3,2,1,0:T(8,128)}, u32[]{:S(2)}) copy-start(f32[2,2,128,256]{3,2,1,0:T(8,128)} %get-tuple-element.67.p0) | copy-start | bytes 1572868
  69.4 21.3 %copy-start.2 = (f32[2,2,256,128]{3,2,1,0:T(8,128)S(1)}, f32[2,2,256,128]{3,2,1,0:T(8,128)}, u32[]{:S(2)}) copy-start(f32[2,2,256,128]{3,2,1,0:T(8,128)} %get-tuple-element.91.b0) | copy-start | bytes 1572868
  69.4 12.6 %collective-permute-start.9 = (f32[2,2,256,128]{3,2,1,0:T(8,128)}, f32[2,2,256,128]{3,2,1,0:T(8,128)S(1)}, u32[]{:S(2)}, u32[]{:S(2)}) collective-permute-start(f32[2,2,256,128]{3,2,1,0:T(8,128)} %get-tuple-element.79), channel_id=1, source_target_pairs={{0,2},{1,3},{2,0},{3,1},{4,6},{5,7},{6,4},{7,5},{8,10},{9,11},{10,... | collective-permute-start | bytes 1572872 | tf_op jit(solution)/shard_map/ppermute | solution.py:440
  69.6 21.2 %collective-permute-start.10 = (f32[2,2,128,256]{3,2,1,0:T(8,128)S(1)}, f32[2,2,128,256]{3,2,1,0:T(8,128)S(1)}, u32[]{:S(2)}, u32[]{:S(2)}) collective-permute-start(f32[2,2,128,256]{3,2,1,0:T(8,128)S(1)} %copy-done.11), channel_id=1, source_target_pairs={{0,4},{4,8},{8,12},{12,0},{1,5},{5,9},{9,13},{13,1},{2,6},{6,10},{... | collective-permute-start | bytes 1572872 | tf_op jit(solution)/shard_map/ppermute | solution.py:440
  70.2 20.5 %collective-permute-start.11 = (f32[2,2,128,256]{3,2,1,0:T(8,128)S(1)}, f32[2,2,128,256]{3,2,1,0:T(8,128)S(1)}, u32[]{:S(2)}, u32[]{:S(2)}) collective-permute-start(f32[2,2,128,256]{3,2,1,0:T(8,128)S(1)} %copy-done.10), channel_id=1, source_target_pairs={{0,12},{4,0},{8,4},{12,8},{1,13},{5,1},{9,5},{13,9},{2,14},{6,2},{... | collective-permute-start | bytes 1572872 | tf_op jit(solution)/shard_map/ppermute | solution.py:440
  72.3 18.4 %collective-permute-start.12 = (f32[2,1,256,128]{3,2,1,0:T(8,128)}, f32[2,1,256,128]{3,2,1,0:T(8,128)S(1)}, u32[]{:S(2)}, u32[]{:S(2)}) collective-permute-start(f32[2,1,256,128]{3,2,1,0:T(8,128)} %get-tuple-element.84), channel_id=1, source_target_pairs={{0,1},{1,2},{2,3},{3,0},{4,5},{5,6},{6,7},{7,4},{8,9},{9,10},{10,1... | collective-permute-start | bytes 786440 | tf_op jit(solution)/shard_map/ppermute | solution.py:440
  75.7 15.0 %collective-permute-start.13 = (f32[2,1,256,128]{3,2,1,0:T(8,128)}, f32[2,1,256,128]{3,2,1,0:T(8,128)S(1)}, u32[]{:S(2)}, u32[]{:S(2)}) collective-permute-start(f32[2,1,256,128]{3,2,1,0:T(8,128)} %get-tuple-element.85), channel_id=1, source_target_pairs={{0,3},{1,0},{2,1},{3,2},{4,7},{5,4},{6,5},{7,6},{8,11},{9,8},{10,9... | collective-permute-start | bytes 786440 | tf_op jit(solution)/shard_map/ppermute | solution.py:440
  93.4 36.2 %copy-start.3 = (bf16[2,2,256,512]{3,2,1,0:T(8,128)(2,1)S(1)}, bf16[2,2,256,512]{3,2,1,0:T(8,128)(2,1)}, u32[]{:S(2)}) copy-start(bf16[2,2,256,512]{3,2,1,0:T(8,128)(2,1)} %constant.23.clone.table_ref) | copy-start | bytes 3145732
  93.4 36.2 %copy-start.5 = (bf16[256,256]{1,0:T(8,128)(2,1)S(1)}, bf16[256,256]{1,0:T(8,128)(2,1)}, u32[]{:S(2)}) copy-start(bf16[256,256]{1,0:T(8,128)(2,1)} %constant.26.clone.ordering_ref) | copy-start | bytes 393220

commit v24 on v23

--- a/solution.py
+++ b/solution.py
@@ -98,34 +98,41 @@
 
 def scale_kernel(part, shifts, place_ref, normals_ref, spectrum_ref, *refs):
     *out_refs, held_out, held_n, held_s, semaphores = refs
-
-    def gets(i):
+    half = held_n.shape[2] // 2
+    steps = [(i, side, pl.ds(side * half, half)) for i in range(len(shifts)) for side in range(2)]
+
+    def gets(i, side, cells):
         if part is None:
-            source_n, source_s = normals_ref.at[:, i], spectrum_ref.at[i]
+            source_n, source_s = normals_ref.at[:, i, cells], spectrum_ref.at[i, cells]
         else:
             chunk = 4 + lax.rem(place_ref[0] + shifts[i], 4)
-            source_n, source_s = normals_ref.at[:, chunk, part], spectrum_ref.at[chunk, part]
+            source_n = normals_ref.at[:, chunk, part, cells]
+            source_s = spectrum_ref.at[chunk, part, cells]
         return (
-            pltpu.make_async_copy(source_n, held_n.at[i], semaphores.at[i, 0]),
-            pltpu.make_async_copy(source_s, held_s.at[i], semaphores.at[i, 1]),
+            pltpu.make_async_copy(source_n, held_n.at[i, :, cells], semaphores.at[i, side, 0]),
+            pltpu.make_async_copy(source_s, held_s.at[i, cells], semaphores.at[i, side, 1]),
         )
 
-    def put(i):
-        target = out_refs[0].at[i] if part is None else out_refs[i]
-        return pltpu.make_async_copy(held_out.at[i], target, semaphores.at[i, 2])
-
-    steps = range(len(shifts))
-    for i in steps:
-        for copy in gets(i):
+    def put(i, side, cells):
+        target = out_refs[0].at[i, :, cells] if part is None else out_refs[i].at[:, cells]
+        return pltpu.make_async_copy(
+            held_out.at[i, :, cells], target, semaphores.at[i, side, 2]
+        )
+
+    for step in steps:
+        for copy in gets(*step):
             copy.start()
-    for i in steps:
-        for copy in gets(i):
+    for step in steps:
+        for copy in gets(*step):
             copy.wait()
+        i, side, cells = step
         for plane in range(2):
-            held_out[i, plane] = held_n[i, plane].astype(jnp.float32) * held_s[i]
-        put(i).start()
-    for i in steps:
-        put(i).wait()
+            held_out[i, plane, cells] = (
+                held_n[i, plane, cells].astype(jnp.float32) * held_s[i, cells]
+            )
+        put(*step).start()
+    for step in steps:
+        put(*step).wait()
 
 
 def scale(part, shifts, place, normals, spectrum):
@@ -143,7 +150,7 @@
             pltpu.VMEM((count,) + chunk, jnp.float32),
             pltpu.VMEM((count,) + chunk, jnp.bfloat16),
             pltpu.VMEM((count,) + chunk[1:], jnp.float32),
-            pltpu.SemaphoreType.DMA((count, 3)),
+            pltpu.SemaphoreType.DMA((count, 2, 3)),
         ],
         compiler_params=params(VMEM),
         cost_estimate=cost(count << 18, 2 * count * MIB),

time: 169 us -> 169 us (level)
  transfers between devices with their start and end apart: 15 -> 15, of which waited for: 7 -> 7; matrix products, arithmetic and copies ran while one was open for 0% -> 0% of each run, Pallas kernels for 12% -> 13%
where the time goes in v24:
time: 169 us
  blocking collectives  70.4 us (42%)
  waiting for transfers between devices  40.7 us (24%)
  Pallas kernels  31.2 us (18%)
  starting transfers between devices  24.3 us (14%)
    all_to_all x1, blocking collectives, per_device(): lines = lax.all_to_all(planes, ALL, split_axis=0, concat_axis=0, tiled=True)  36.2 us
    all_to_all x1, blocking collectives, per_device(): lax.all_to_all(outgoing.reshape(128, 1, CAP, 2, BW), ALL, split_axis=0, c...  34.2 us
    ppermute x14, waiting for transfers between devices, shifted(): lax.ppermute(piece, axis, [(i, (i + shift) % size) for i in range(size)])  31 us
    ppermute x14, starting transfers between devices, shifted(): lax.ppermute(piece, axis, [(i, (i + shift) % size) for i in range(size)])  18.4 us
    pallas_call x5, Pallas kernels, scale(): pl.pallas_call(functools.partial(scale_kernel, part, shifts), in_specs=[p...  12.3 us
    all_to_all x1, waiting for transfers between devices, per_device(): a = lax.all_to_all(a, 'gz', split_axis=0, concat_axis=0, tiled=True)  9.77 us
    pallas_call x2, Pallas kernels, first_y(): pl.pallas_call(functools.partial(first_y_kernel, merge), in_specs=[pl.Blo...  7.06 us
    all_to_all x1, starting transfers between devices, per_device(): a = lax.all_to_all(a, 'gz', split_axis=0, concat_axis=0, tiled=True)  5.87 us
  transfers between devices with their start and end apart: 15, of which 7 were waited for; matrix products, arithmetic and copies ran while one was open for 0% of the time, Pallas kernels for 13%

profile of v24, /device:TPU:1, one launch (start us, length us, event | category | flops | bytes accessed | tf_op | source)
XLA Modules:
  0.0 169.1 jit_solution(14692774214115410016)
XLA Ops:
  0.0 3.7 %scale_a.1 = f32[4,2,8,128,128]{4,3,2,1,0:T(8,128)} custom-call(s32[1]{0:T(128)} %bitcast.place_ref.to_ref.z_ref, bf16[2,8,8,128,128]{4,3,2,1,0:T(8,128)(2,1)} %bitcast.23, f32[8,8,128,128]{3,2,1,0:T(8,128)} %bitcast.28), custom_call_target="tpu_custom_call" | custom-call | flops 16 | bytes 128 | tf_op jit(solution)/shard_map/scale_a/pallas_call | solution.py:144
  3.7 5.9 %all-to-all-start = ((f32[4,2,8,128,128]{4,3,2,1,0:T(8,128)}), f32[4,2,8,128,128]{4,3,2,1,0:T(8,128)}, u32[]{:S(2)}, u32[]{:S(2)}) async-start(f32[4,2,8,128,128]{4,3,2,1,0:T(8,128)} %scale_a.1), calls=%async_computation | async-start | bytes 8388608 | tf_op jit(solution)/shard_map/all_to_all | solution.py:464
  9.5 2.3 %scale_b.4 = (f32[2,4,128,128]{3,2,1,0:T(8,128)}, f32[2,4,128,128]{3,2,1,0:T(8,128)}, f32[2,4,128,128]{3,2,1,0:T(8,128)}) custom-call(s32[1]{0:T(128)} %bitcast.3.place_ref.to_ref.y_ref, bf16[2,8,2,4,128,128]{5,4,3,2,1,0:T(8,128)(2,1)} %bitcast.24, f32[8,2,4,128,128]{4,3,2,1,0:T(8,128)} %bitcast.29), custom_call_target="tpu_custom_call" | custom-call | flops 12 | bytes 96 | tf_op jit(solution)/shard_map/scale_b/pallas_call | solution.py:144
  11.9 0.0 copy-start.9
  11.9 1.4 collective-permute-start
  13.3 2.6 %collective-permute-start.1 = (f32[2,4,128,128]{3,2,1,0:T(8,128)}, f32[2,4,128,128]{3,2,1,0:T(8,128)S(1)}, u32[]{:S(2)}, u32[]{:S(2)}) collective-permute-start(f32[2,4,128,128]{3,2,1,0:T(8,128)} %get-tuple-element.62), channel_id=1, source_target_pairs={{0,8},{4,12},{8,0},{12,4},{1,9},{5,13},{9,1},{13,5},{2,10},{6,14},... | collective-permute-start | bytes 1572872 | tf_op jit(solution)/shard_map/ppermute | solution.py:447
  15.9 1.1 collective-permute-start.2
  17.0 2.4 %scale_b.5 = (f32[2,4,128,128]{3,2,1,0:T(8,128)}, f32[2,4,128,128]{3,2,1,0:T(8,128)}, f32[2,4,128,128]{3,2,1,0:T(8,128)}) custom-call(s32[1]{0:T(128)} %bitcast.3.place_ref.to_ref.y_ref, bf16[2,8,2,4,128,128]{5,4,3,2,1,0:T(8,128)(2,1)} %bitcast.25, f32[8,2,4,128,128]{4,3,2,1,0:T(8,128)} %bitcast.30), custom_call_target="tpu_custom_call" | custom-call | flops 12 | bytes 96 | tf_op jit(solution)/shard_map/scale_b/pallas_call | solution.py:144
  19.3 0.5 collective-permute-start.4
  19.8 0.8 collective-permute-start.5
  20.6 0.1 copy.13
  20.7 0.2 fusion.2
  21.0 0.1 copy.14
  21.1 5.0 %collective-permute-done.refs_1_ = f32[2,4,128,128]{3,2,1,0:T(8,128)S(1)} collective-permute-done((f32[2,4,128,128]{3,2,1,0:T(8,128)}, f32[2,4,128,128]{3,2,1,0:T(8,128)S(1)}, u32[]{:S(2)}, u32[]{:S(2)}) %collective-permute-start) | collective-permute-done | bytes 524320 | tf_op jit(solution)/shard_map/ppermute | solution.py:447
  26.1 1.4 collective-permute-start.6
  27.5 0.4 fusion.1
  27.9 0.0 copy-start
  27.9 2.0 %scale_b.6.refs_0_ = f32[2,4,128,128]{3,2,1,0:T(8,128)} custom-call(s32[1]{0:T(128)} %bitcast.3.place_ref.to_ref.y_ref, bf16[2,8,2,4,128,128]{5,4,3,2,1,0:T(8,128)(2,1)} %bitcast.26, f32[8,2,4,128,128]{4,3,2,1,0:T(8,128)} %bitcast.31), custom_call_target="tpu_custom_call" | custom-call | flops 4 | bytes 32 | tf_op jit(solution)/shard_map/scale_b/pallas_call | solution.py:144
  29.9 8.6 %collective-permute-done.1.refs_2_ = f32[2,4,128,128]{3,2,1,0:T(8,128)S(1)} collective-permute-done((f32[2,4,128,128]{3,2,1,0:T(8,128)}, f32[2,4,128,128]{3,2,1,0:T(8,128)S(1)}, u32[]{:S(2)}, u32[]{:S(2)}) %collective-permute-start.1) | collective-permute-done | bytes 524320 | tf_op jit(solution)/shard_map/ppermute | solution.py:447
  38.5 0.8 collective-permute-done.2.refs_3_
  39.3 0.0 copy-done.8
  39.3 3.5 %first_y.2 = (f32[2,1,256,128]{3,2,1,0:T(8,128)}, f32[2,1,256,128]{3,2,1,0:T(8,128)}, f32[2,2,256,128]{3,2,1,0:T(8,128)}, f32[2,2,256,128]{3,2,1,0:T(8,128)}) custom-call(s32[1]{0:T(128)} %bitcast.3.place_ref.to_ref.y_ref, s32[1]{0:T(128)} %bitcast.place_ref.to_ref.z_ref, f32[2,4,128,128]{3,2,1,0:T(8,128)} %scale_b.6.refs_0_, f32[2,4,128,128]{3,2,1,0:T(8,128)} %copy-done.7, ...), custom_call_target="tpu_custom_call" | custom-call | flops 2048 | bytes 64 | tf_op jit(solution)/shard_map/first_y/pallas_call | solution.py:275
  42.8 4.0 %collective-permute-start.8 = (f32[2,1,256,128]{3,2,1,0:T(8,128)}, f32[2,1,256,128]{3,2,1,0:T(8,128)S(1)}, u32[]{:S(2)}, u32[]{:S(2)}) collective-permute-start(f32[2,1,256,128]{3,2,1,0:T(8,128)} %get-tuple-element.73), channel_id=1, source_target_pairs={{0,3},{1,0},{2,1},{3,2},{4,7},{5,4},{6,5},{7,6},{8,11},{9,8},{10,9... | collective-permute-start | bytes 786440 | tf_op jit(solution)/shard_map/ppermute | solution.py:447
  46.7 2.0 %scale_b.7.refs_0_ = f32[2,4,128,128]{3,2,1,0:T(8,128)} custom-call(s32[1]{0:T(128)} %bitcast.3.place_ref.to_ref.y_ref, bf16[2,8,2,4,128,128]{5,4,3,2,1,0:T(8,128)(2,1)} %bitcast.27, f32[8,2,4,128,128]{4,3,2,1,0:T(8,128)} %bitcast.32), custom_call_target="tpu_custom_call" | custom-call | flops 4 | bytes 32 | tf_op jit(solution)/shard_map/scale_b/pallas_call | solution.py:144
  48.7 9.8 %all-to-all-done.in_ref = f32[4,2,8,128,128]{4,3,2,1,0:T(8,128)} async-done(((f32[4,2,8,128,128]{4,3,2,1,0:T(8,128)}), f32[4,2,8,128,128]{4,3,2,1,0:T(8,128)}, u32[]{:S(2)}, u32[]{:S(2)}) %all-to-all-start) | async-done | bytes 4194336 | tf_op jit(solution)/shard_map/all_to_all | solution.py:464
  58.5 4.5 %first_z.1 = (f32[2,2,128,256]{3,2,1,0:T(8,128)}, f32[2,2,128,256]{3,2,1,0:T(8,128)}, f32[2,2,128,256]{3,2,1,0:T(8,128)}, f32[2,2,128,256]{3,2,1,0:T(8,128)}) custom-call(s32[1]{0:T(128)} %bitcast.3.place_ref.to_ref.y_ref, f32[4,2,8,128,128]{4,3,2,1,0:T(8,128)} %all-to-all-done.in_ref, bf16[2,2,2,256,256]{4,3,2,1,0:T(8,128)(2,1)S(1)} %copy-done.1), custom_call_target="tpu_custom_call" | custom-call | flops 4096 | bytes 128 | tf_op jit(solution)/shard_map/first_z/pallas_call | solution.py:212
  63.0 0.0 collective-permute-done.4.refs_1_
  63.1 3.0 %collective-permute-start.3 = (f32[2,2,128,256]{3,2,1,0:T(8,128)}, f32[2,2,128,256]{3,2,1,0:T(8,128)S(1)}, u32[]{:S(2)}, u32[]{:S(2)}) collective-permute-start(f32[2,2,128,256]{3,2,1,0:T(8,128)} %get-tuple-element.68), channel_id=1, source_target_pairs={{0,8},{4,12},{8,0},{12,4},{1,9},{5,13},{9,1},{13,5},{2,10},{6,14},... | collective-permute-start | bytes 1572872 | tf_op jit(solution)/shard_map/ppermute | solution.py:447
  66.0 0.0 collective-permute-done.6.refs_3_
  66.0 0.0 collective-permute-done.8.c3
  66.1 3.6 %first_y.3 = (f32[2,1,256,128]{3,2,1,0:T(8,128)}, f32[2,1,256,128]{3,2,1,0:T(8,128)}, f32[2,2,256,128]{3,2,1,0:T(8,128)}, f32[2,2,256,128]{3,2,1,0:T(8,128)}) custom-call(s32[1]{0:T(128)} %bitcast.3.place_ref.to_ref.y_ref, s32[1]{0:T(128)} %bitcast.place_ref.to_ref.z_ref, ...), custom_call_target="tpu_custom_call", output_to_operand_aliasing={{2}: (6, {}), {3}: (7, {})} | custom-call | flops 2048 | bytes 64 | tf_op jit(solution)/shard_map/first_y/pallas_call | solution.py:275
  69.7 0.1 collective-permute-start.9
  69.8 0.7 collective-permute-start.10
  70.5 2.0 %collective-permute-start.11 = (f32[2,2,128,256]{3,2,1,0:T(8,128)S(1)}, f32[2,2,128,256]{3,2,1,0:T(8,128)S(1)}, u32[]{:S(2)}, u32[]{:S(2)}) collective-permute-start(f32[2,2,128,256]{3,2,1,0:T(8,128)S(1)} %copy-done.10), channel_id=1, source_target_pairs={{0,12},{4,0},{8,4},{12,8},{1,13},{5,1},{9,5},{13,9},{2,14},{6,2},{... | collective-permute-start | bytes 1572872 | tf_op jit(solution)/shard_map/ppermute | solution.py:447
  72.6 0.9 collective-permute-start.12
  73.5 2.5 %collective-permute-done.3.p2 = f32[2,2,128,256]{3,2,1,0:T(8,128)S(1)} collective-permute-done((f32[2,2,128,256]{3,2,1,0:T(8,128)}, f32[2,2,128,256]{3,2,1,0:T(8,128)S(1)}, u32[]{:S(2)}, u32[]{:S(2)}) %collective-permute-start.3) | collective-permute-done | bytes 524320 | tf_op jit(solution)/shard_map/ppermute | solution.py:447
  76.0 0.0 collective-permute-start.13
  76.0 0.9 part_y.1.part_a
  76.9 5.3 %collective-permute-done.9.b2 = f32[2,2,256,128]{3,2,1,0:T(8,128)S(1)} collective-permute-done((f32[2,2,256,128]{3,2,1,0:T(8,128)}, f32[2,2,256,128]{3,2,1,0:T(8,128)S(1)}, u32[]{:S(2)}, u32[]{:S(2)}) %collective-permute-start.9) | collective-permute-done | bytes 524320 | tf_op jit(solution)/shard_map/ppermute | solution.py:447
  82.3 8.7 %collective-permute-done.12.d1 = f32[2,1,256,128]{3,2,1,0:T(8,128)S(1)} collective-permute-done((f32[2,1,256,128]{3,2,1,0:T(8,128)}, f32[2,1,256,128]{3,2,1,0:T(8,128)S(1)}, u32[]{:S(2)}, u32[]{:S(2)}) %collective-permute-start.12) | collective-permute-done | bytes 262176 | tf_op jit(solution)/shard_map/ppermute | solution.py:447
  91.0 0.0 collective-permute-done.13.d3
  91.0 2.7 %second.1 = f32[128,2,2,8,128]{4,3,2,1,0:T(8,128)S(1)} custom-call(s32[1]{0:T(128)} %bitcast.3.place_ref.to_ref.y_ref, s32[1]{0:T(128)} %bitcast.place_ref.to_ref.z_ref, f32[2,256,512]{2,1,0:T(8,128)S(1)} %part_y.1.part_a, f32[2,2,128,256]{3,2,1,0:T(8,128)S(1)} %collective-permute-done.10.a1, f32[2,2,128,256]{3,2,1,0:T(8,128)S(1)} %collective-permute-done.11.a3, ...), custom_call_target="tpu_custom_call" | custom-call | flops 3072 | bytes 128 | tf_op jit(solution)/shard_map/second/pallas_call | solution.py:373
  93.6 0.0 copy-start.3
  93.7 0.0 copy-start.5
  93.7 36.2 %all_to_all.22.in_ref = f32[128,2,2,8,128]{4,3,2,1,0:T(8,128)S(1)} all-to-all(f32[128,2,2,8,128]{4,3,2,1,0:T(8,128)S(1)} %second.1), channel_id=1, replica_groups=mesh['gx'=8,'gy'=4,'gz'=4] {'gx','gy','gz'}, dimensions={0} | all-to-all | bytes 4194304 | tf_op jit(solution)/shard_map/all_to_all | solution.py:490
  129.9 3.7 %third.1 = f32[4096,128]{1,0:T(8,128)S(1)} custom-call(s32[1024]{0:T(1024)S(1)} %multiply_add_fusion.slot_ref, f32[128,2,2,8,128]{4,3,2,1,0:T(8,128)S(1)} %all_to_all.22.in_ref, bf16[2,2,256,512]{3,2,1,0:T(8,128)(2,1)S(1)} %copy-done.3, bf16[256,256]{1,0:T(8,128)(2,1)S(1)} %copy-done.5), custom_call_target="tpu_custom_call" | custom-call | flops 3072 | bytes 96 | tf_op jit(solution)/shard_map/third/pallas_call | solution.py:433
  133.5 34.2 %all_to_all.23 = f32[128,1,16,2,128]{4,3,2,1,0:T(2,128)S(1)} all-to-all(f32[128,1,16,2,128]{4,3,2,1,0:T(2,128)S(1)} %bitcast.22), channel_id=1, replica_groups=mesh['gx'=8,'gy'=4,'gz'=4] {'gx','gy','gz'}, dimensions={0} | all-to-all | bytes 4194304 | tf_op jit(solution)/shard_map/all_to_all | solution.py:492
  167.8 1.3 copy.19
  (29 shorter events, 0.1 us)
Async XLA Ops:
  3.7 54.8 %all-to-all-start = ((f32[4,2,8,128,128]{4,3,2,1,0:T(8,128)}), f32[4,2,8,128,128]{4,3,2,1,0:T(8,128)}, u32[]{:S(2)}, u32[]{:S(2)}) async-start(f32[4,2,8,128,128]{4,3,2,1,0:T(8,128)} %scale_a.1), calls=%async_computation | async-start | bytes 8388608 | tf_op jit(solution)/shard_map/all_to_all | solution.py:464
  11.9 8.7 %copy-start.9 = (s32[1024,1]{0,1:T(1,128)S(1)}, s32[1024,1]{0,1:T(1,128)}, u32[]{:S(2)}) copy-start(s32[1024,1]{0,1:T(1,128)} %param.9) | copy-start | bytes 12292
  11.9 14.2 %collective-permute-start = (f32[2,4,128,128]{3,2,1,0:T(8,128)}, f32[2,4,128,128]{3,2,1,0:T(8,128)S(1)}, u32[]{:S(2)}, u32[]{:S(2)}) collective-permute-start(f32[2,4,128,128]{3,2,1,0:T(8,128)} %get-tuple-element.61), channel_id=1, source_target_pairs={{0,4},{4,8},{8,12},{12,0},{1,5},{5,9},{9,13},{13,1},{2,6},{6,10},{... | collective-permute-start | bytes 1572872 | tf_op jit(solution)/shard_map/ppermute | solution.py:447
  13.3 25.2 %collective-permute-start.1 = (f32[2,4,128,128]{3,2,1,0:T(8,128)}, f32[2,4,128,128]{3,2,1,0:T(8,128)S(1)}, u32[]{:S(2)}, u32[]{:S(2)}) collective-permute-start(f32[2,4,128,128]{3,2,1,0:T(8,128)} %get-tuple-element.62), channel_id=1, source_target_pairs={{0,8},{4,12},{8,0},{12,4},{1,9},{5,13},{9,1},{13,5},{2,10},{6,14},... | collective-permute-start | bytes 1572872 | tf_op jit(solution)/shard_map/ppermute | solution.py:447
  15.9 23.4 %collective-permute-start.2 = (f32[2,4,128,128]{3,2,1,0:T(8,128)}, f32[2,4,128,128]{3,2,1,0:T(8,128)}, u32[]{:S(2)}, u32[]{:S(2)}) collective-permute-start(f32[2,4,128,128]{3,2,1,0:T(8,128)} %get-tuple-element.63), channel_id=1, source_target_pairs={{0,12},{4,0},{8,4},{12,8},{1,13},{5,1},{9,5},{13,9},{2,14},{6,2},{... | collective-permute-start | bytes 1572872 | tf_op jit(solution)/shard_map/ppermute | solution.py:447
  19.3 43.7 %collective-permute-start.4 = (f32[2,4,128,128]{3,2,1,0:T(8,128)}, f32[2,4,128,128]{3,2,1,0:T(8,128)S(1)}, u32[]{:S(2)}, u32[]{:S(2)}) collective-permute-start(f32[2,4,128,128]{3,2,1,0:T(8,128)} %get-tuple-element.70), channel_id=1, source_target_pairs={{0,4},{4,8},{8,12},{12,0},{1,5},{5,9},{9,13},{13,1},{2,6},{6,10},{... | collective-permute-start | bytes 1572872 | tf_op jit(solution)/shard_map/ppermute | solution.py:447
  19.8 46.2 %collective-permute-start.5 = (f32[2,4,128,128]{3,2,1,0:T(8,128)}, f32[2,4,128,128]{3,2,1,0:T(8,128)}, u32[]{:S(2)}, u32[]{:S(2)}) collective-permute-start(f32[2,4,128,128]{3,2,1,0:T(8,128)} %get-tuple-element.71), channel_id=1, source_target_pairs={{0,8},{4,12},{8,0},{12,4},{1,9},{5,13},{9,1},{13,5},{2,10},{6,14},... | collective-permute-start | bytes 1572872 | tf_op jit(solution)/shard_map/ppermute | solution.py:447
  26.1 3.7 %copy-start.7 = (f32[2,4,128,128]{3,2,1,0:T(8,128)}, f32[2,4,128,128]{3,2,1,0:T(8,128)S(1)}, u32[]{:S(2)}) copy-start(f32[2,4,128,128]{3,2,1,0:T(8,128)S(1)} %collective-permute-done.refs_1_) | copy-start | bytes 1572868
  26.1 39.9 %collective-permute-start.6 = (f32[2,4,128,128]{3,2,1,0:T(8,128)}, f32[2,4,128,128]{3,2,1,0:T(8,128)}, u32[]{:S(2)}, u32[]{:S(2)}) collective-permute-start(f32[2,4,128,128]{3,2,1,0:T(8,128)} %get-tuple-element.72), channel_id=1, source_target_pairs={{0,12},{4,0},{8,4},{12,8},{1,13},{5,1},{9,5},{13,9},{2,14},{6,2},{... | collective-permute-start | bytes 1572872 | tf_op jit(solution)/shard_map/ppermute | solution.py:447
  27.9 11.4 %copy-start = (bf16[2,2,2,256,256]{4,3,2,1,0:T(8,128)(2,1)S(1)}, bf16[2,2,2,256,256]{4,3,2,1,0:T(8,128)(2,1)}, u32[]{:S(2)}) copy-start(bf16[2,2,2,256,256]{4,3,2,1,0:T(8,128)(2,1)} %constant.24.clone.refs_4_.table_ref.refs_6_.table_y_ref) | copy-start | bytes 3145732
  38.5 0.8 copy-start.8
  42.8 23.3 %collective-permute-start.8 = (f32[2,1,256,128]{3,2,1,0:T(8,128)}, f32[2,1,256,128]{3,2,1,0:T(8,128)S(1)}, u32[]{:S(2)}, u32[]{:S(2)}) collective-permute-start(f32[2,1,256,128]{3,2,1,0:T(8,128)} %get-tuple-element.73), channel_id=1, source_target_pairs={{0,3},{1,0},{2,1},{3,2},{4,7},{5,4},{6,5},{7,6},{8,11},{9,8},{10,9... | collective-permute-start | bytes 786440 | tf_op jit(solution)/shard_map/ppermute | solution.py:447
  46.7 19.3 %collective-permute-start.7 = (f32[2,1,256,128]{3,2,1,0:T(8,128)}, f32[2,1,256,128]{3,2,1,0:T(8,128)S(1)}, u32[]{:S(2)}, u32[]{:S(2)}) collective-permute-start(f32[2,1,256,128]{3,2,1,0:T(8,128)} %get-tuple-element.64), channel_id=1, source_target_pairs={{0,1},{1,2},{2,3},{3,0},{4,5},{5,6},{6,7},{7,4},{8,9},{9,10},{10,1... | collective-permute-start | bytes 786440 | tf_op jit(solution)/shard_map/ppermute | solution.py:447
  46.7 11.8 %copy-start.1 = (bf16[2,2,2,256,256]{4,3,2,1,0:T(8,128)(2,1)S(1)}, bf16[2,2,2,256,256]{4,3,2,1,0:T(8,128)(2,1)}, u32[]{:S(2)}) copy-start(bf16[2,2,2,256,256]{4,3,2,1,0:T(8,128)(2,1)} %constant.25.clone.table_ref.table_z_ref) | copy-start | bytes 3145732
  63.1 3.0 %copy-start.6 = (f32[2,4,128,128]{3,2,1,0:T(8,128)}, f32[2,4,128,128]{3,2,1,0:T(8,128)S(1)}, u32[]{:S(2)}) copy-start(f32[2,4,128,128]{3,2,1,0:T(8,128)S(1)} %collective-permute-done.4.refs_1_) | copy-start | bytes 1572868
  63.1 12.9 %collective-permute-start.3 = (f32[2,2,128,256]{3,2,1,0:T(8,128)}, f32[2,2,128,256]{3,2,1,0:T(8,128)S(1)}, u32[]{:S(2)}, u32[]{:S(2)}) collective-permute-start(f32[2,2,128,256]{3,2,1,0:T(8,128)} %get-tuple-element.68), channel_id=1, source_target_pairs={{0,8},{4,12},{8,0},{12,4},{1,9},{5,13},{9,1},{13,5},{2,10},{6,14},... | collective-permute-start | bytes 1572872 | tf_op jit(solution)/shard_map/ppermute | solution.py:447
  66.1 3.7 %copy-start.11 = (f32[2,2,128,256]{3,2,1,0:T(8,128)S(1)}, f32[2,2,128,256]{3,2,1,0:T(8,128)}, u32[]{:S(2)}) copy-start(f32[2,2,128,256]{3,2,1,0:T(8,128)} %get-tuple-element.81) | copy-start | bytes 1572868
  66.1 4.4 %copy-start.10 = (f32[2,2,128,256]{3,2,1,0:T(8,128)S(1)}, f32[2,2,128,256]{3,2,1,0:T(8,128)}, u32[]{:S(2)}) copy-start(f32[2,2,128,256]{3,2,1,0:T(8,128)} %get-tuple-element.82) | copy-start | bytes 1572868
  66.1 9.9 %copy-start.4 = (f32[2,2,128,256]{3,2,1,0:T(8,128)S(1)}, f32[2,2,128,256]{3,2,1,0:T(8,128)}, u32[]{:S(2)}) copy-start(f32[2,2,128,256]{3,2,1,0:T(8,128)} %get-tuple-element.67.p0) | copy-start | bytes 1572868
  69.7 21.3 %copy-start.2 = (f32[2,2,256,128]{3,2,1,0:T(8,128)S(1)}, f32[2,2,256,128]{3,2,1,0:T(8,128)}, u32[]{:S(2)}) copy-start(f32[2,2,256,128]{3,2,1,0:T(8,128)} %get-tuple-element.91.b0) | copy-start | bytes 1572868
  69.7 12.6 %collective-permute-start.9 = (f32[2,2,256,128]{3,2,1,0:T(8,128)}, f32[2,2,256,128]{3,2,1,0:T(8,128)S(1)}, u32[]{:S(2)}, u32[]{:S(2)}) collective-permute-start(f32[2,2,256,128]{3,2,1,0:T(8,128)} %get-tuple-element.79), channel_id=1, source_target_pairs={{0,2},{1,3},{2,0},{3,1},{4,6},{5,7},{6,4},{7,5},{8,10},{9,11},{10,... | collective-permute-start | bytes 1572872 | tf_op jit(solution)/shard_map/ppermute | solution.py:447
  69.8 21.2 %collective-permute-start.10 = (f32[2,2,128,256]{3,2,1,0:T(8,128)S(1)}, f32[2,2,128,256]{3,2,1,0:T(8,128)S(1)}, u32[]{:S(2)}, u32[]{:S(2)}) collective-permute-start(f32[2,2,128,256]{3,2,1,0:T(8,128)S(1)} %copy-done.11), channel_id=1, source_target_pairs={{0,4},{4,8},{8,12},{12,0},{1,5},{5,9},{9,13},{13,1},{2,6},{6,10},{... | collective-permute-start | bytes 1572872 | tf_op jit(solution)/shard_map/ppermute | solution.py:447
  70.5 20.5 %collective-permute-start.11 = (f32[2,2,128,256]{3,2,1,0:T(8,128)S(1)}, f32[2,2,128,256]{3,2,1,0:T(8,128)S(1)}, u32[]{:S(2)}, u32[]{:S(2)}) collective-permute-start(f32[2,2,128,256]{3,2,1,0:T(8,128)S(1)} %copy-done.10), channel_id=1, source_target_pairs={{0,12},{4,0},{8,4},{12,8},{1,13},{5,1},{9,5},{13,9},{2,14},{6,2},{... | collective-permute-start | bytes 1572872 | tf_op jit(solution)/shard_map/ppermute | solution.py:447
  72.6 18.4 %collective-permute-start.12 = (f32[2,1,256,128]{3,2,1,0:T(8,128)}, f32[2,1,256,128]{3,2,1,0:T(8,128)S(1)}, u32[]{:S(2)}, u32[]{:S(2)}) collective-permute-start(f32[2,1,256,128]{3,2,1,0:T(8,128)} %get-tuple-element.84), channel_id=1, source_target_pairs={{0,1},{1,2},{2,3},{3,0},{4,5},{5,6},{6,7},{7,4},{8,9},{9,10},{10,1... | collective-permute-start | bytes 786440 | tf_op jit(solution)/shard_map/ppermute | solution.py:447
  76.0 15.0 %collective-permute-start.13 = (f32[2,1,256,128]{3,2,1,0:T(8,128)}, f32[2,1,256,128]{3,2,1,0:T(8,128)S(1)}, u32[]{:S(2)}, u32[]{:S(2)}) collective-permute-start(f32[2,1,256,128]{3,2,1,0:T(8,128)} %get-tuple-element.85), channel_id=1, source_target_pairs={{0,3},{1,0},{2,1},{3,2},{4,7},{5,4},{6,5},{7,6},{8,11},{9,8},{10,9... | collective-permute-start | bytes 786440 | tf_op jit(solution)/shard_map/ppermute | solution.py:447
  93.6 36.2 %copy-start.3 = (bf16[2,2,256,512]{3,2,1,0:T(8,128)(2,1)S(1)}, bf16[2,2,256,512]{3,2,1,0:T(8,128)(2,1)}, u32[]{:S(2)}) copy-start(bf16[2,2,256,512]{3,2,1,0:T(8,128)(2,1)} %constant.23.clone.table_ref) | copy-start | bytes 3145732
  93.7 36.2 %copy-start.5 = (bf16[256,256]{1,0:T(8,128)(2,1)S(1)}, bf16[256,256]{1,0:T(8,128)(2,1)}, u32[]{:S(2)}) copy-start(bf16[256,256]{1,0:T(8,128)(2,1)} %constant.26.clone.ordering_ref) | copy-start | bytes 393220

commit v25 on v23

--- a/solution.py
+++ b/solution.py
@@ -307,48 +307,54 @@
     )(place, *pieces, table)
 
 
-def second_kernel(
-    y_ref,
-    z_ref,
-    part_a,
-    a1,
-    a3,
-    table_y_ref,
-    b0,
-    b2,
-    c1,
-    c3,
-    d1,
-    d3,
-    table_z_ref,
-    out_ref,
-    held,
-):
+def sum_y_kernel(place_ref, part_ref, p1, p3, table_ref, out_ref):
     odd = pl.program_id(0)
-
-    def put(values, half, row):
-        held[pl.ds(half * 8 + row, 128, stride=16), :] = values
-
-    g = lax.rem(y_ref[0] + 3, 4)
+    g = lax.rem(place_ref[0] + 3, 4)
     base = lax.rem(g, 2)
     flip = jnp.where(odd == 0, 1.0, -1.0).astype(jnp.float32)
     sign = jnp.where((odd == 0) | (g < 2), 1.0, -1.0).astype(jnp.float32)
-    table = (table_y_ref[0, base, 0], table_y_ref[1, base, 0])
-    values = part_a[0] + product(table, columns_y((a1[...] + flip * a3[...]) * sign))
+    table = (table_ref[0, base, 0], table_ref[1, base, 0])
+    sides = (p1[...] + flip * p3[...]) * sign
+    out_ref[0] = part_ref[0] + product(table, columns_y(sides))
+
+
+def sum_y(place, part, pieces, table):
+    block = pl.BlockSpec((1, KEPT, 512), lambda i, place: (i, 0, 0))
+    return pl.pallas_call(
+        sum_y_kernel,
+        grid_spec=pltpu.PrefetchScalarGridSpec(
+            num_scalar_prefetch=1,
+            grid=(2,),
+            in_specs=[block]
+            + [pl.BlockSpec((2, 2, 128, KEPT), lambda i, place: (0, 0, 0, 0))] * 2
+            + [pl.BlockSpec((2, 2, 1, KEPT, KEPT), lambda i, place: (0, 0, i, 0, 0))],
+            out_specs=block,
+        ),
+        out_shape=jax.ShapeDtypeStruct((2, KEPT, 512), jnp.float32),
+        compiler_params=params(VMEM),
+        cost_estimate=cost(512 * 512 * 256, 4 * MIB),
+        name="sum_y",
+    )(place, part, *pieces, table)
+
+
+def second_kernel(place_ref, done_a, b0, b2, c1, c3, d1, d3, table_ref, out_ref, held):
+    def put(values, half, row):
+        held[pl.ds(half * 8 + row, 128, stride=16), :] = values
+
     for plane in range(2):
         for x in range(2):
             for half in range(2):
                 start = x * KEPT + half * 128
                 put(
-                    values[plane * 128 : (plane + 1) * 128, start : start + 128],
+                    done_a[0, plane * 128 : (plane + 1) * 128, start : start + 128],
                     half,
                     plane * 4 + x,
                 )
     near, far = (
         jnp.concatenate([c[...], d[...]], axis=1) for c, d in ((c1, d1), (c3, d3))
     )
-    pairs = [(b0[...], b2[...], z_ref[0]), (near, far, lax.rem(z_ref[0] + 3, 4))]
-    for half, values in enumerate(transform(True, pairs, table_z_ref)):
+    pairs = [(b0[...], b2[...], place_ref[0]), (near, far, lax.rem(place_ref[0] + 3, 4))]
+    for half, values in enumerate(transform(True, pairs, table_ref)):
         for x in range(2):
             for plane in range(2):
                 put(
@@ -359,29 +365,27 @@
     out_ref[...] = held[...].reshape(128, 1, 2, 8, 128)
 
 
-def second(gy, gz, part_a, pieces_a, table_y, pieces_b, table_z):
+def second(place, done_a, pieces_b, table_z):
     def rows(cells):
-        return pl.BlockSpec((2, cells, 128, 128), lambda i, gy, gz: (0, 0, i, 0))
+        return pl.BlockSpec((2, cells, 128, 128), lambda i, place: (0, 0, i, 0))
 
     return pl.pallas_call(
         second_kernel,
         grid_spec=pltpu.PrefetchScalarGridSpec(
-            num_scalar_prefetch=2,
+            num_scalar_prefetch=1,
             grid=(2,),
-            in_specs=[pl.BlockSpec((1, KEPT, 512), lambda i, gy, gz: (i, 0, 0))]
-            + [pl.BlockSpec((2, 2, 128, KEPT), lambda i, gy, gz: (0, 0, 0, 0))] * 2
-            + [pl.BlockSpec((2, 2, 1, KEPT, KEPT), lambda i, gy, gz: (0, 0, i, 0, 0))]
+            in_specs=[pl.BlockSpec((1, KEPT, 512), lambda i, place: (i, 0, 0))]
             + [rows(2)] * 2
             + [rows(1)] * 4
-            + [pl.BlockSpec(table_z.shape, lambda i, gy, gz: (0, 0, 0, 0, 0))],
-            out_specs=pl.BlockSpec((128, 1, 2, 8, 128), lambda i, gy, gz: (0, i, 0, 0, 0)),
+            + [pl.BlockSpec(table_z.shape, lambda i, place: (0, 0, 0, 0, 0))],
+            out_specs=pl.BlockSpec((128, 1, 2, 8, 128), lambda i, place: (0, i, 0, 0, 0)),
             scratch_shapes=[pltpu.VMEM((2048, 128), jnp.float32)],
         ),
         out_shape=jax.ShapeDtypeStruct((128, 2, 2, 8, 128), jnp.float32),
         compiler_params=params(VMEM),
-        cost_estimate=cost(512 * 512 * 768, 8 * MIB),
+        cost_estimate=cost(512 * 512 * 512, 8 * MIB),
         name="second",
-    )(gy, gz, part_a, *pieces_a, table_y, *pieces_b, table_z)
+    )(place, done_a, *pieces_b, table_z)
 
 
 def third_kernel(slot_ref, in_ref, table_ref, ordering_ref, out_ref, held):
@@ -475,11 +479,9 @@
 
     part_a = part_y(gy, (a0, a2), table_y)
     part_a, b2 = lax.optimization_barrier((part_a, b2))
-    b2, d1, d3 = lax.optimization_barrier((b2, d1, d3))
-    part_a, a1, a3, d1, d3 = lax.optimization_barrier((part_a, a1, a3, d1, d3))
-    planes = second(
-        gy, gz, part_a, (a1, a3), table_y, (b0, b2, c1, c3, d1, d3), table_z
-    )
+    done_a = sum_y(gy, part_a, (a1, a3), table_y)
+    done_a, b2, d1, d3 = lax.optimization_barrier((done_a, b2, d1, d3))
+    planes = second(gz, done_a, (b0, b2, c1, c3, d1, d3), table_z)
     lines = lax.all_to_all(planes, ALL, split_axis=0, concat_axis=0, tiled=True)
     outgoing = third(slots, lines, table_x, ordering)
     return lax.all_to_all(

time: 169 us -> 169 us (level)
  waiting for transfers between devices: 40.9 us -> 39.1 us
  transfers between devices with their start and end apart: 15 -> 15, of which waited for: 7 -> 8; matrix products, arithmetic and copies ran while one was open for 0% -> 0% of each run, Pallas kernels for 12% -> 13%
where the time goes in v25:
time: 169 us
  blocking collectives  71.1 us (42%)
  waiting for transfers between devices  39.1 us (23%)
  Pallas kernels  31 us (18%)
  starting transfers between devices  24.2 us (14%)
  local copies, waits for them, and re-layouts  2.47 us (1%)
    all_to_all x1, blocking collectives, per_device(): lines = lax.all_to_all(planes, ALL, split_axis=0, concat_axis=0, tiled=True)  36.9 us
    all_to_all x1, blocking collectives, per_device(): lax.all_to_all(outgoing.reshape(128, 1, CAP, 2, BW), ALL, split_axis=0, c...  34.2 us
    ppermute x14, waiting for transfers between devices, shifted(): lax.ppermute(piece, axis, [(i, (i + shift) % size) for i in range(size)])  30.1 us
    ppermute x14, starting transfers between devices, shifted(): lax.ppermute(piece, axis, [(i, (i + shift) % size) for i in range(size)])  18.4 us
    pallas_call x5, Pallas kernels, scale(): pl.pallas_call(functools.partial(scale_kernel, part, shifts), in_specs=[p...  11.9 us
    all_to_all x1, waiting for transfers between devices, per_device(): a = lax.all_to_all(a, 'gz', split_axis=0, concat_axis=0, tiled=True)  9 us
    pallas_call x2, Pallas kernels, first_y(): pl.pallas_call(functools.partial(first_y_kernel, merge), in_specs=[pl.Blo...  7 us
    all_to_all x1, starting transfers between devices, per_device(): a = lax.all_to_all(a, 'gz', split_axis=0, concat_axis=0, tiled=True)  5.87 us
  transfers between devices with their start and end apart: 15, of which 8 were waited for; matrix products, arithmetic and copies ran while one was open for 0% of the time, Pallas kernels for 13%

profile of v25, /device:TPU:1, one launch (start us, length us, event | category | flops | bytes accessed | tf_op | source)
XLA Modules:
  0.0 168.7 jit_solution(13416138875862699341)
XLA Ops:
  0.0 3.4 %scale_a.1 = f32[4,2,8,128,128]{4,3,2,1,0:T(8,128)} custom-call(s32[1]{0:T(128)} %bitcast.place_ref.to_ref, bf16[2,8,8,128,128]{4,3,2,1,0:T(8,128)(2,1)} %bitcast.23, f32[8,8,128,128]{3,2,1,0:T(8,128)} %bitcast.28), custom_call_target="tpu_custom_call" | custom-call | flops 16 | bytes 128 | tf_op jit(solution)/shard_map/scale_a/pallas_call | solution.py:137
  3.4 5.9 %all-to-all-start = ((f32[4,2,8,128,128]{4,3,2,1,0:T(8,128)}), f32[4,2,8,128,128]{4,3,2,1,0:T(8,128)}, u32[]{:S(2)}, u32[]{:S(2)}) async-start(f32[4,2,8,128,128]{4,3,2,1,0:T(8,128)} %scale_a.1), calls=%async_computation | async-start | bytes 8388608 | tf_op jit(solution)/shard_map/all_to_all | solution.py:461
  9.3 2.3 %scale_b.4 = (f32[2,4,128,128]{3,2,1,0:T(8,128)}, f32[2,4,128,128]{3,2,1,0:T(8,128)}, f32[2,4,128,128]{3,2,1,0:T(8,128)}) custom-call(s32[1]{0:T(128)} %bitcast.3.place_ref.to_ref, bf16[2,8,2,4,128,128]{5,4,3,2,1,0:T(8,128)(2,1)} %bitcast.24, f32[8,2,4,128,128]{4,3,2,1,0:T(8,128)} %bitcast.29), custom_call_target="tpu_custom_call" | custom-call | flops 12 | bytes 96 | tf_op jit(solution)/shard_map/scale_b/pallas_call | solution.py:137
  11.6 0.0 copy-start.10
  11.6 1.4 collective-permute-start
  12.9 2.6 %collective-permute-start.1 = (f32[2,4,128,128]{3,2,1,0:T(8,128)}, f32[2,4,128,128]{3,2,1,0:T(8,128)S(1)}, u32[]{:S(2)}, u32[]{:S(2)}) collective-permute-start(f32[2,4,128,128]{3,2,1,0:T(8,128)} %get-tuple-element.58), channel_id=1, source_target_pairs={{0,8},{4,12},{8,0},{12,4},{1,9},{5,13},{9,1},{13,5},{2,10},{6,14},... | collective-permute-start | bytes 1572872 | tf_op jit(solution)/shard_map/ppermute | solution.py:444
  15.6 1.1 collective-permute-start.2
  16.6 2.3 %scale_b.5 = (f32[2,4,128,128]{3,2,1,0:T(8,128)}, f32[2,4,128,128]{3,2,1,0:T(8,128)}, f32[2,4,128,128]{3,2,1,0:T(8,128)}) custom-call(s32[1]{0:T(128)} %bitcast.3.place_ref.to_ref, bf16[2,8,2,4,128,128]{5,4,3,2,1,0:T(8,128)(2,1)} %bitcast.25, f32[8,2,4,128,128]{4,3,2,1,0:T(8,128)} %bitcast.30), custom_call_target="tpu_custom_call" | custom-call | flops 12 | bytes 96 | tf_op jit(solution)/shard_map/scale_b/pallas_call | solution.py:137
  18.9 0.5 collective-permute-start.4
  19.4 0.8 collective-permute-start.5
  20.2 0.1 copy.13
  20.3 0.2 fusion.2
  20.6 0.1 copy.14
  20.7 5.1 %collective-permute-done.refs_1_ = f32[2,4,128,128]{3,2,1,0:T(8,128)S(1)} collective-permute-done((f32[2,4,128,128]{3,2,1,0:T(8,128)}, f32[2,4,128,128]{3,2,1,0:T(8,128)S(1)}, u32[]{:S(2)}, u32[]{:S(2)}) %collective-permute-start) | collective-permute-done | bytes 524320 | tf_op jit(solution)/shard_map/ppermute | solution.py:444
  25.8 1.4 collective-permute-start.6
  27.2 0.4 fusion.1
  27.5 0.0 copy-start
  27.5 2.0 %scale_b.6.refs_0_ = f32[2,4,128,128]{3,2,1,0:T(8,128)} custom-call(s32[1]{0:T(128)} %bitcast.3.place_ref.to_ref, bf16[2,8,2,4,128,128]{5,4,3,2,1,0:T(8,128)(2,1)} %bitcast.26, f32[8,2,4,128,128]{4,3,2,1,0:T(8,128)} %bitcast.31), custom_call_target="tpu_custom_call" | custom-call | flops 4 | bytes 32 | tf_op jit(solution)/shard_map/scale_b/pallas_call | solution.py:137
  29.5 8.6 %collective-permute-done.1.refs_2_ = f32[2,4,128,128]{3,2,1,0:T(8,128)S(1)} collective-permute-done((f32[2,4,128,128]{3,2,1,0:T(8,128)}, f32[2,4,128,128]{3,2,1,0:T(8,128)S(1)}, u32[]{:S(2)}, u32[]{:S(2)}) %collective-permute-start.1) | collective-permute-done | bytes 524320 | tf_op jit(solution)/shard_map/ppermute | solution.py:444
  38.2 0.8 collective-permute-done.2.refs_3_
  38.9 0.1 copy-done.8
  39.0 0.8 copy-done.9
  39.8 3.4 %first_y.2 = (f32[2,1,256,128]{3,2,1,0:T(8,128)}, f32[2,1,256,128]{3,2,1,0:T(8,128)}, f32[2,2,256,128]{3,2,1,0:T(8,128)}, f32[2,2,256,128]{3,2,1,0:T(8,128)}) custom-call(s32[1]{0:T(128)} %bitcast.3.place_ref.to_ref, s32[1]{0:T(128)} %bitcast.place_ref.to_ref, f32[2,4,128,128]{3,2,1,0:T(8,128)} %scale_b.6.refs_0_, f32[2,4,128,128]{3,2,1,0:T(8,128)} %copy-done.7, ...), custom_call_target="tpu_custom_call" | custom-call | flops 2048 | bytes 64 | tf_op jit(solution)/shard_map/first_y/pallas_call | solution.py:268
  43.3 4.0 %collective-permute-start.8 = (f32[2,1,256,128]{3,2,1,0:T(8,128)}, f32[2,1,256,128]{3,2,1,0:T(8,128)S(1)}, u32[]{:S(2)}, u32[]{:S(2)}) collective-permute-start(f32[2,1,256,128]{3,2,1,0:T(8,128)} %get-tuple-element.69), channel_id=1, source_target_pairs={{0,3},{1,0},{2,1},{3,2},{4,7},{5,4},{6,5},{7,6},{8,11},{9,8},{10,9... | collective-permute-start | bytes 786440 | tf_op jit(solution)/shard_map/ppermute | solution.py:444
  47.2 0.0 collective-permute-start.7
  47.2 2.0 %scale_b.7.refs_0_ = f32[2,4,128,128]{3,2,1,0:T(8,128)} custom-call(s32[1]{0:T(128)} %bitcast.3.place_ref.to_ref, bf16[2,8,2,4,128,128]{5,4,3,2,1,0:T(8,128)(2,1)} %bitcast.27, f32[8,2,4,128,128]{4,3,2,1,0:T(8,128)} %bitcast.32), custom_call_target="tpu_custom_call" | custom-call | flops 4 | bytes 32 | tf_op jit(solution)/shard_map/scale_b/pallas_call | solution.py:137
  49.2 9.0 %all-to-all-done.in_ref = f32[4,2,8,128,128]{4,3,2,1,0:T(8,128)} async-done(((f32[4,2,8,128,128]{4,3,2,1,0:T(8,128)}), f32[4,2,8,128,128]{4,3,2,1,0:T(8,128)}, u32[]{:S(2)}, u32[]{:S(2)}) %all-to-all-start) | async-done | bytes 4194336 | tf_op jit(solution)/shard_map/all_to_all | solution.py:461
  58.2 4.5 %first_z.1 = (f32[2,2,128,256]{3,2,1,0:T(8,128)}, f32[2,2,128,256]{3,2,1,0:T(8,128)}, f32[2,2,128,256]{3,2,1,0:T(8,128)}, f32[2,2,128,256]{3,2,1,0:T(8,128)}) custom-call(s32[1]{0:T(128)} %bitcast.3.place_ref.to_ref, f32[4,2,8,128,128]{4,3,2,1,0:T(8,128)} %all-to-all-done.in_ref, bf16[2,2,2,256,256]{4,3,2,1,0:T(8,128)(2,1)S(1)} %copy-done.1), custom_call_target="tpu_custom_call" | custom-call | flops 4096 | bytes 128 | tf_op jit(solution)/shard_map/first_z/pallas_call | solution.py:205
  62.8 3.0 %collective-permute-start.3 = (f32[2,2,128,256]{3,2,1,0:T(8,128)}, f32[2,2,128,256]{3,2,1,0:T(8,128)S(1)}, u32[]{:S(2)}, u32[]{:S(2)}) collective-permute-start(f32[2,2,128,256]{3,2,1,0:T(8,128)} %get-tuple-element.64), channel_id=1, source_target_pairs={{0,8},{4,12},{8,0},{12,4},{1,9},{5,13},{9,1},{13,5},{2,10},{6,14},... | collective-permute-start | bytes 1572872 | tf_op jit(solution)/shard_map/ppermute | solution.py:444
  65.8 0.0 collective-permute-done.8.c3
  65.8 3.6 %first_y.3 = (f32[2,1,256,128]{3,2,1,0:T(8,128)}, f32[2,1,256,128]{3,2,1,0:T(8,128)}, f32[2,2,256,128]{3,2,1,0:T(8,128)}, f32[2,2,256,128]{3,2,1,0:T(8,128)}) custom-call(s32[1]{0:T(128)} %bitcast.3.place_ref.to_ref, s32[1]{0:T(128)} %bitcast.place_ref.to_ref, f32[2,4,128,128]{3,2,1,0:T(8,128)} %scale_b.7.refs_0_, ...), custom_call_target="tpu_custom_call", output_to_operand_aliasing={{2}: (6, {}), {3}: (7, {})} | custom-call | flops 2048 | bytes 64 | tf_op jit(solution)/shard_map/first_y/pallas_call | solution.py:268
  69.4 0.1 collective-permute-start.9
  69.5 0.6 collective-permute-start.10
  70.1 2.1 %collective-permute-start.11 = (f32[2,2,128,256]{3,2,1,0:T(8,128)S(1)}, f32[2,2,128,256]{3,2,1,0:T(8,128)S(1)}, u32[]{:S(2)}, u32[]{:S(2)}) collective-permute-start(f32[2,2,128,256]{3,2,1,0:T(8,128)S(1)} %copy-done.11), channel_id=1, source_target_pairs={{0,12},{4,0},{8,4},{12,8},{1,13},{5,1},{9,5},{13,9},{2,14},{6,2},{... | collective-permute-start | bytes 1572872 | tf_op jit(solution)/shard_map/ppermute | solution.py:444
  72.2 0.9 collective-permute-start.12
  73.1 2.5 %collective-permute-done.3.p2 = f32[2,2,128,256]{3,2,1,0:T(8,128)S(1)} collective-permute-done((f32[2,2,128,256]{3,2,1,0:T(8,128)}, f32[2,2,128,256]{3,2,1,0:T(8,128)S(1)}, u32[]{:S(2)}, u32[]{:S(2)}) %collective-permute-start.3) | collective-permute-done | bytes 524320 | tf_op jit(solution)/shard_map/ppermute | solution.py:444
  75.6 0.9 part_y.1.part_ref
  76.6 5.4 %collective-permute-done.9.b2 = f32[2,2,256,128]{3,2,1,0:T(8,128)S(1)} collective-permute-done((f32[2,2,256,128]{3,2,1,0:T(8,128)}, f32[2,2,256,128]{3,2,1,0:T(8,128)S(1)}, u32[]{:S(2)}, u32[]{:S(2)}) %collective-permute-start.9) | collective-permute-done | bytes 524320 | tf_op jit(solution)/shard_map/ppermute | solution.py:444
  82.0 7.2 %collective-permute-done.10.p1 = f32[2,2,128,256]{3,2,1,0:T(8,128)S(1)} collective-permute-done((f32[2,2,128,256]{3,2,1,0:T(8,128)S(1)}, f32[2,2,128,256]{3,2,1,0:T(8,128)S(1)}, u32[]{:S(2)}, u32[]{:S(2)}) %collective-permute-start.10) | collective-permute-done | bytes 524320 | tf_op jit(solution)/shard_map/ppermute | solution.py:444
  89.2 0.9 sum_y.1.done_a
  90.1 0.5 collective-permute-done.12.d1
  90.6 2.0 %second.1 = f32[128,2,2,8,128]{4,3,2,1,0:T(8,128)S(1)} custom-call(s32[1]{0:T(128)} %bitcast.place_ref.to_ref, f32[2,256,512]{2,1,0:T(8,128)S(1)} %sum_y.1.done_a, f32[2,2,256,128]{3,2,1,0:T(8,128)S(1)} %copy-done.2, f32[2,2,256,128]{3,2,1,0:T(8,128)S(1)} %collective-permute-done.9.b2, f32[2,1,256,128]{3,2,1,0:T(8,128)S(1)} %collective-permute-done.7.c1, ...), custom_call_target="tpu_custom_call" | custom-call | flops 2048 | bytes 128 | tf_op jit(solution)/shard_map/second/pallas_call | solution.py:372
  92.6 0.0 copy-start.3
  92.6 0.0 copy-start.5
  92.6 36.9 %all_to_all.22.in_ref = f32[128,2,2,8,128]{4,3,2,1,0:T(8,128)S(1)} all-to-all(f32[128,2,2,8,128]{4,3,2,1,0:T(8,128)S(1)} %second.1), channel_id=1, replica_groups=mesh['gx'=8,'gy'=4,'gz'=4] {'gx','gy','gz'}, dimensions={0} | all-to-all | bytes 4194304 | tf_op jit(solution)/shard_map/all_to_all | solution.py:485
  129.5 3.7 %third.1 = f32[4096,128]{1,0:T(8,128)S(1)} custom-call(s32[1024]{0:T(1024)S(1)} %multiply_add_fusion.slot_ref, f32[128,2,2,8,128]{4,3,2,1,0:T(8,128)S(1)} %all_to_all.22.in_ref, bf16[2,2,256,512]{3,2,1,0:T(8,128)(2,1)S(1)} %copy-done.3, bf16[256,256]{1,0:T(8,128)(2,1)S(1)} %copy-done.5), custom_call_target="tpu_custom_call" | custom-call | flops 3072 | bytes 96 | tf_op jit(solution)/shard_map/third/pallas_call | solution.py:430
  133.2 34.2 %all_to_all.23 = f32[128,1,16,2,128]{4,3,2,1,0:T(2,128)S(1)} all-to-all(f32[128,1,16,2,128]{4,3,2,1,0:T(2,128)S(1)} %bitcast.22), channel_id=1, replica_groups=mesh['gx'=8,'gy'=4,'gz'=4] {'gx','gy','gz'}, dimensions={0} | all-to-all | bytes 4194304 | tf_op jit(solution)/shard_map/all_to_all | solution.py:487
  167.4 1.3 copy.19
  (32 shorter events, 0.1 us)
Async XLA Ops:
  3.4 54.8 %all-to-all-start = ((f32[4,2,8,128,128]{4,3,2,1,0:T(8,128)}), f32[4,2,8,128,128]{4,3,2,1,0:T(8,128)}, u32[]{:S(2)}, u32[]{:S(2)}) async-start(f32[4,2,8,128,128]{4,3,2,1,0:T(8,128)} %scale_a.1), calls=%async_computation | async-start | bytes 8388608 | tf_op jit(solution)/shard_map/all_to_all | solution.py:461
  11.6 8.6 %copy-start.10 = (s32[1024,1]{0,1:T(1,128)S(1)}, s32[1024,1]{0,1:T(1,128)}, u32[]{:S(2)}) copy-start(s32[1024,1]{0,1:T(1,128)} %param.9) | copy-start | bytes 12292
  11.6 14.2 %collective-permute-start = (f32[2,4,128,128]{3,2,1,0:T(8,128)}, f32[2,4,128,128]{3,2,1,0:T(8,128)S(1)}, u32[]{:S(2)}, u32[]{:S(2)}) collective-permute-start(f32[2,4,128,128]{3,2,1,0:T(8,128)} %get-tuple-element.57), channel_id=1, source_target_pairs={{0,4},{4,8},{8,12},{12,0},{1,5},{5,9},{9,13},{13,1},{2,6},{6,10},{... | collective-permute-start | bytes 1572872 | tf_op jit(solution)/shard_map/ppermute | solution.py:444
  12.9 25.2 %collective-permute-start.1 = (f32[2,4,128,128]{3,2,1,0:T(8,128)}, f32[2,4,128,128]{3,2,1,0:T(8,128)S(1)}, u32[]{:S(2)}, u32[]{:S(2)}) collective-permute-start(f32[2,4,128,128]{3,2,1,0:T(8,128)} %get-tuple-element.58), channel_id=1, source_target_pairs={{0,8},{4,12},{8,0},{12,4},{1,9},{5,13},{9,1},{13,5},{2,10},{6,14},... | collective-permute-start | bytes 1572872 | tf_op jit(solution)/shard_map/ppermute | solution.py:444
  15.6 23.4 %collective-permute-start.2 = (f32[2,4,128,128]{3,2,1,0:T(8,128)}, f32[2,4,128,128]{3,2,1,0:T(8,128)S(1)}, u32[]{:S(2)}, u32[]{:S(2)}) collective-permute-start(f32[2,4,128,128]{3,2,1,0:T(8,128)} %get-tuple-element.59), channel_id=1, source_target_pairs={{0,12},{4,0},{8,4},{12,8},{1,13},{5,1},{9,5},{13,9},{2,14},{6,2},{... | collective-permute-start | bytes 1572872 | tf_op jit(solution)/shard_map/ppermute | solution.py:444
  18.9 43.8 %collective-permute-start.4 = (f32[2,4,128,128]{3,2,1,0:T(8,128)}, f32[2,4,128,128]{3,2,1,0:T(8,128)S(1)}, u32[]{:S(2)}, u32[]{:S(2)}) collective-permute-start(f32[2,4,128,128]{3,2,1,0:T(8,128)} %get-tuple-element.66), channel_id=1, source_target_pairs={{0,4},{4,8},{8,12},{12,0},{1,5},{5,9},{9,13},{13,1},{2,6},{6,10},{... | collective-permute-start | bytes 1572872 | tf_op jit(solution)/shard_map/ppermute | solution.py:444
  19.4 46.4 %collective-permute-start.5 = (f32[2,4,128,128]{3,2,1,0:T(8,128)}, f32[2,4,128,128]{3,2,1,0:T(8,128)}, u32[]{:S(2)}, u32[]{:S(2)}) collective-permute-start(f32[2,4,128,128]{3,2,1,0:T(8,128)} %get-tuple-element.67), channel_id=1, source_target_pairs={{0,8},{4,12},{8,0},{12,4},{1,9},{5,13},{9,1},{13,5},{2,10},{6,14},... | collective-permute-start | bytes 1572872 | tf_op jit(solution)/shard_map/ppermute | solution.py:444
  25.8 3.8 %copy-start.7 = (f32[2,4,128,128]{3,2,1,0:T(8,128)}, f32[2,4,128,128]{3,2,1,0:T(8,128)S(1)}, u32[]{:S(2)}) copy-start(f32[2,4,128,128]{3,2,1,0:T(8,128)S(1)} %collective-permute-done.refs_1_) | copy-start | bytes 1572868
  25.8 40.0 %collective-permute-start.6 = (f32[2,4,128,128]{3,2,1,0:T(8,128)}, f32[2,4,128,128]{3,2,1,0:T(8,128)}, u32[]{:S(2)}, u32[]{:S(2)}) collective-permute-start(f32[2,4,128,128]{3,2,1,0:T(8,128)} %get-tuple-element.68), channel_id=1, source_target_pairs={{0,12},{4,0},{8,4},{12,8},{1,13},{5,1},{9,5},{13,9},{2,14},{6,2},{... | collective-permute-start | bytes 1572872 | tf_op jit(solution)/shard_map/ppermute | solution.py:444
  27.5 12.3 %copy-start = (bf16[2,2,2,256,256]{4,3,2,1,0:T(8,128)(2,1)S(1)}, bf16[2,2,2,256,256]{4,3,2,1,0:T(8,128)(2,1)}, u32[]{:S(2)}) copy-start(bf16[2,2,2,256,256]{4,3,2,1,0:T(8,128)(2,1)} %constant.24.clone.refs_4_.table_ref.refs_6_) | copy-start | bytes 3145732
  38.2 0.9 copy-start.8
  39.0 0.8 copy-start.9
  43.3 22.5 %collective-permute-start.8 = (f32[2,1,256,128]{3,2,1,0:T(8,128)}, f32[2,1,256,128]{3,2,1,0:T(8,128)S(1)}, u32[]{:S(2)}, u32[]{:S(2)}) collective-permute-start(f32[2,1,256,128]{3,2,1,0:T(8,128)} %get-tuple-element.69), channel_id=1, source_target_pairs={{0,3},{1,0},{2,1},{3,2},{4,7},{5,4},{6,5},{7,6},{8,11},{9,8},{10,9... | collective-permute-start | bytes 786440 | tf_op jit(solution)/shard_map/ppermute | solution.py:444
  47.2 18.5 %collective-permute-start.7 = (f32[2,1,256,128]{3,2,1,0:T(8,128)}, f32[2,1,256,128]{3,2,1,0:T(8,128)S(1)}, u32[]{:S(2)}, u32[]{:S(2)}) collective-permute-start(f32[2,1,256,128]{3,2,1,0:T(8,128)} %get-tuple-element.60), channel_id=1, source_target_pairs={{0,1},{1,2},{2,3},{3,0},{4,5},{5,6},{6,7},{7,4},{8,9},{9,10},{10,1... | collective-permute-start | bytes 786440 | tf_op jit(solution)/shard_map/ppermute | solution.py:444
  47.2 11.0 %copy-start.1 = (bf16[2,2,2,256,256]{4,3,2,1,0:T(8,128)(2,1)S(1)}, bf16[2,2,2,256,256]{4,3,2,1,0:T(8,128)(2,1)}, u32[]{:S(2)}) copy-start(bf16[2,2,2,256,256]{4,3,2,1,0:T(8,128)(2,1)} %constant.25.clone.table_ref) | copy-start | bytes 3145732
  62.7 3.0 %copy-start.6 = (f32[2,4,128,128]{3,2,1,0:T(8,128)}, f32[2,4,128,128]{3,2,1,0:T(8,128)S(1)}, u32[]{:S(2)}) copy-start(f32[2,4,128,128]{3,2,1,0:T(8,128)S(1)} %collective-permute-done.4.refs_1_) | copy-start | bytes 1572868
  62.8 12.9 %collective-permute-start.3 = (f32[2,2,128,256]{3,2,1,0:T(8,128)}, f32[2,2,128,256]{3,2,1,0:T(8,128)S(1)}, u32[]{:S(2)}, u32[]{:S(2)}) collective-permute-start(f32[2,2,128,256]{3,2,1,0:T(8,128)} %get-tuple-element.64), channel_id=1, source_target_pairs={{0,8},{4,12},{8,0},{12,4},{1,9},{5,13},{9,1},{13,5},{2,10},{6,14},... | collective-permute-start | bytes 1572872 | tf_op jit(solution)/shard_map/ppermute | solution.py:444
  65.8 3.7 %copy-start.12 = (f32[2,2,128,256]{3,2,1,0:T(8,128)S(1)}, f32[2,2,128,256]{3,2,1,0:T(8,128)}, u32[]{:S(2)}) copy-start(f32[2,2,128,256]{3,2,1,0:T(8,128)} %get-tuple-element.77) | copy-start | bytes 1572868
  65.8 4.3 %copy-start.11 = (f32[2,2,128,256]{3,2,1,0:T(8,128)S(1)}, f32[2,2,128,256]{3,2,1,0:T(8,128)}, u32[]{:S(2)}) copy-start(f32[2,2,128,256]{3,2,1,0:T(8,128)} %get-tuple-element.78) | copy-start | bytes 1572868
  65.8 9.8 %copy-start.4 = (f32[2,2,128,256]{3,2,1,0:T(8,128)S(1)}, f32[2,2,128,256]{3,2,1,0:T(8,128)}, u32[]{:S(2)}) copy-start(f32[2,2,128,256]{3,2,1,0:T(8,128)} %get-tuple-element.63.p0) | copy-start | bytes 1572868
  69.4 12.6 %collective-permute-start.9 = (f32[2,2,256,128]{3,2,1,0:T(8,128)}, f32[2,2,256,128]{3,2,1,0:T(8,128)S(1)}, u32[]{:S(2)}, u32[]{:S(2)}) collective-permute-start(f32[2,2,256,128]{3,2,1,0:T(8,128)} %get-tuple-element.75), channel_id=1, source_target_pairs={{0,2},{1,3},{2,0},{3,1},{4,6},{5,7},{6,4},{7,5},{8,10},{9,11},{10,... | collective-permute-start | bytes 1572872 | tf_op jit(solution)/shard_map/ppermute | solution.py:444
  69.5 19.7 %collective-permute-start.10 = (f32[2,2,128,256]{3,2,1,0:T(8,128)S(1)}, f32[2,2,128,256]{3,2,1,0:T(8,128)S(1)}, u32[]{:S(2)}, u32[]{:S(2)}) collective-permute-start(f32[2,2,128,256]{3,2,1,0:T(8,128)S(1)} %copy-done.12), channel_id=1, source_target_pairs={{0,4},{4,8},{8,12},{12,0},{1,5},{5,9},{9,13},{13,1},{2,6},{6,10},{... | collective-permute-start | bytes 1572872 | tf_op jit(solution)/shard_map/ppermute | solution.py:444
  70.1 19.0 %collective-permute-start.11 = (f32[2,2,128,256]{3,2,1,0:T(8,128)S(1)}, f32[2,2,128,256]{3,2,1,0:T(8,128)S(1)}, u32[]{:S(2)}, u32[]{:S(2)}) collective-permute-start(f32[2,2,128,256]{3,2,1,0:T(8,128)S(1)} %copy-done.11), channel_id=1, source_target_pairs={{0,12},{4,0},{8,4},{12,8},{1,13},{5,1},{9,5},{13,9},{2,14},{6,2},{... | collective-permute-start | bytes 1572872 | tf_op jit(solution)/shard_map/ppermute | solution.py:444
  72.2 18.4 %collective-permute-start.12 = (f32[2,1,256,128]{3,2,1,0:T(8,128)}, f32[2,1,256,128]{3,2,1,0:T(8,128)S(1)}, u32[]{:S(2)}, u32[]{:S(2)}) collective-permute-start(f32[2,1,256,128]{3,2,1,0:T(8,128)} %get-tuple-element.80), channel_id=1, source_target_pairs={{0,1},{1,2},{2,3},{3,0},{4,5},{5,6},{6,7},{7,4},{8,9},{9,10},{10,1... | collective-permute-start | bytes 786440 | tf_op jit(solution)/shard_map/ppermute | solution.py:444
  75.6 15.0 %collective-permute-start.13 = (f32[2,1,256,128]{3,2,1,0:T(8,128)}, f32[2,1,256,128]{3,2,1,0:T(8,128)S(1)}, u32[]{:S(2)}, u32[]{:S(2)}) collective-permute-start(f32[2,1,256,128]{3,2,1,0:T(8,128)} %get-tuple-element.81), channel_id=1, source_target_pairs={{0,3},{1,0},{2,1},{3,2},{4,7},{5,4},{6,5},{7,6},{8,11},{9,8},{10,9... | collective-permute-start | bytes 786440 | tf_op jit(solution)/shard_map/ppermute | solution.py:444
  76.6 14.0 %copy-start.2 = (f32[2,2,256,128]{3,2,1,0:T(8,128)S(1)}, f32[2,2,256,128]{3,2,1,0:T(8,128)}, u32[]{:S(2)}) copy-start(f32[2,2,256,128]{3,2,1,0:T(8,128)} %get-tuple-element.83.b0) | copy-start | bytes 1572868
  92.6 36.9 %copy-start.3 = (bf16[2,2,256,512]{3,2,1,0:T(8,128)(2,1)S(1)}, bf16[2,2,256,512]{3,2,1,0:T(8,128)(2,1)}, u32[]{:S(2)}) copy-start(bf16[2,2,256,512]{3,2,1,0:T(8,128)(2,1)} %constant.23.clone.table_ref) | copy-start | bytes 3145732
  92.6 36.9 %copy-start.5 = (bf16[256,256]{1,0:T(8,128)(2,1)S(1)}, bf16[256,256]{1,0:T(8,128)(2,1)}, u32[]{:S(2)}) copy-start(bf16[256,256]{1,0:T(8,128)(2,1)} %constant.26.clone.ordering_ref) | copy-start | bytes 393220

commit v26 on v25

--- a/solution.py
+++ b/solution.py
@@ -151,6 +151,57 @@
     )(place, *in_hbm(normals.reshape((2,) + view), spectrum.reshape(view)))
 
 
+def scale_first_kernel(normals_ref, spectrum_ref, out_ref, held_out, held_n, held_s, semaphores):
+    def gets(i):
+        chunks = pl.ds(2 * i, 2)
+        return (
+            pltpu.make_async_copy(normals_ref.at[:, chunks], held_n.at[i], semaphores.at[i, 0]),
+            pltpu.make_async_copy(spectrum_ref.at[chunks], held_s.at[i], semaphores.at[i, 1]),
+        )
+
+    def put(i):
+        chunks = pl.ds(2 * i, 2)
+        return pltpu.make_async_copy(
+            held_out.at[chunks], out_ref.at[chunks], semaphores.at[i, 2]
+        )
+
+    for i in range(2):
+        for copy in gets(i):
+            copy.start()
+    for i in range(2):
+        for copy in gets(i):
+            copy.wait()
+        for chunk in range(2):
+            for plane in range(2):
+                held_out[2 * i + chunk, plane] = (
+                    held_n[i, plane, chunk].astype(jnp.float32) * held_s[i, chunk]
+                )
+        put(i).start()
+    for i in range(2):
+        put(i).wait()
+
+
+def scale_first(normals, spectrum):
+    shape = (4, 2, 8, 128, 128)
+    view = (8, 8, 128, 128)
+    hbm = pl.BlockSpec(memory_space=pltpu.HBM)
+    return pl.pallas_call(
+        scale_first_kernel,
+        in_specs=[hbm] * 2,
+        out_specs=hbm,
+        out_shape=pltpu.HBM(shape, jnp.float32),
+        scratch_shapes=[
+            pltpu.VMEM(shape, jnp.float32),
+            pltpu.VMEM((2, 2, 2, 8, 128, 128), jnp.bfloat16),
+            pltpu.VMEM((2, 2, 8, 128, 128), jnp.float32),
+            pltpu.SemaphoreType.DMA((2, 3)),
+        ],
+        compiler_params=params(VMEM),
+        cost_estimate=cost(1 << 20, 8 * MIB),
+        name="scale_a",
+    )(*in_hbm(normals.reshape((2,) + view), spectrum.reshape(view)))
+
+
 def transform(along_z, pairs, table_ref):
     parts = []
     for odd in range(2):
@@ -456,7 +507,7 @@
     gy = lax.axis_index("gy").astype(jnp.int32).reshape(1)
     gz = lax.axis_index("gz").astype(jnp.int32).reshape(1)
 
-    (a,) = scale(None, (0, 1, 2, 3), gz, normals, spectrum)
+    a = scale_first(normals, spectrum)
     a, place = lax.optimization_barrier((a, gy))
     a = lax.all_to_all(a, "gz", split_axis=0, concat_axis=0, tiled=True)
     c1, c3, c2 = scale(0, (1, 3, 2), place, normals, spectrum)

time: 169 us -> 169 us (level)
    pallas_call x0 -> x1, Pallas kernels: none -> 3.77 us  [scale_first(): pl.pallas_call(scale_first_kernel, in_specs=[hbm] * 2, out_specs=hbm, out...]
    pallas_call x5 -> x4, Pallas kernels: 11.9 us -> 8.54 us  [scale(): pl.pallas_call(functools.partial(scale_kernel, part, shifts), in_specs=[p...]
where the time goes in v26:
time: 169 us
  blocking collectives  71.1 us (42%)
  waiting for transfers between devices  39.7 us (23%)
  Pallas kernels  31.3 us (19%)
  starting transfers between devices  23.7 us (14%)
  local copies, waits for them, and re-layouts  2.38 us (1%)
    all_to_all x1, blocking collectives, per_device(): lines = lax.all_to_all(planes, ALL, split_axis=0, concat_axis=0, tiled=True)  36.9 us
    all_to_all x1, blocking collectives, per_device(): lax.all_to_all(outgoing.reshape(128, 1, CAP, 2, BW), ALL, split_axis=0, c...  34.2 us
    ppermute x14, waiting for transfers between devices, shifted(): lax.ppermute(piece, axis, [(i, (i + shift) % size) for i in range(size)])  30.1 us
    ppermute x14, starting transfers between devices, shifted(): lax.ppermute(piece, axis, [(i, (i + shift) % size) for i in range(size)])  17.8 us
    all_to_all x1, waiting for transfers between devices, per_device(): a = lax.all_to_all(a, 'gz', split_axis=0, concat_axis=0, tiled=True)  9.61 us
    pallas_call x4, Pallas kernels, scale(): pl.pallas_call(functools.partial(scale_kernel, part, shifts), in_specs=[p...  8.54 us
    pallas_call x2, Pallas kernels, first_y(): pl.pallas_call(functools.partial(first_y_kernel, merge), in_specs=[pl.Blo...  7 us
    all_to_all x1, starting transfers between devices, per_device(): a = lax.all_to_all(a, 'gz', split_axis=0, concat_axis=0, tiled=True)  5.87 us
  transfers between devices with their start and end apart: 15, of which 8 were waited for; matrix products, arithmetic and copies ran while one was open for 0% of the time, Pallas kernels for 13%

profile of v26, /device:TPU:1, one launch (start us, length us, event | category | flops | bytes accessed | tf_op | source)
XLA Modules:
  0.0 169.1 jit_solution(3581289720591071221)
XLA Ops:
  0.0 3.8 %scale_a.1 = f32[4,2,8,128,128]{4,3,2,1,0:T(8,128)} custom-call(bf16[2,8,8,128,128]{4,3,2,1,0:T(8,128)(2,1)} %bitcast.23, f32[8,8,128,128]{3,2,1,0:T(8,128)} %bitcast.28), custom_call_target="tpu_custom_call" | custom-call | flops 16 | bytes 128 | tf_op jit(solution)/shard_map/scale_a/pallas_call | solution.py:188
  3.8 5.9 %all-to-all-start = ((f32[4,2,8,128,128]{4,3,2,1,0:T(8,128)}), f32[4,2,8,128,128]{4,3,2,1,0:T(8,128)}, u32[]{:S(2)}, u32[]{:S(2)}) async-start(f32[4,2,8,128,128]{4,3,2,1,0:T(8,128)} %scale_a.1), calls=%async_computation | async-start | bytes 8388608 | tf_op jit(solution)/shard_map/all_to_all | solution.py:512
  9.7 2.3 %scale_b.4 = (f32[2,4,128,128]{3,2,1,0:T(8,128)}, f32[2,4,128,128]{3,2,1,0:T(8,128)}, f32[2,4,128,128]{3,2,1,0:T(8,128)}) custom-call(s32[1]{0:T(128)} %bitcast.2.place_ref.to_ref, bf16[2,8,2,4,128,128]{5,4,3,2,1,0:T(8,128)(2,1)} %bitcast.24, f32[8,2,4,128,128]{4,3,2,1,0:T(8,128)} %bitcast.29), custom_call_target="tpu_custom_call" | custom-call | flops 12 | bytes 96 | tf_op jit(solution)/shard_map/scale_b/pallas_call | solution.py:137
  11.9 0.0 copy-start.10
  11.9 1.4 collective-permute-start
  13.3 2.6 %collective-permute-start.1 = (f32[2,4,128,128]{3,2,1,0:T(8,128)}, f32[2,4,128,128]{3,2,1,0:T(8,128)S(1)}, u32[]{:S(2)}, u32[]{:S(2)}) collective-permute-start(f32[2,4,128,128]{3,2,1,0:T(8,128)} %get-tuple-element.58), channel_id=1, source_target_pairs={{0,8},{4,12},{8,0},{12,4},{1,9},{5,13},{9,1},{13,5},{2,10},{6,14},... | collective-permute-start | bytes 1572872 | tf_op jit(solution)/shard_map/ppermute | solution.py:495
  15.9 1.1 collective-permute-start.2
  17.0 2.3 %scale_b.5 = (f32[2,4,128,128]{3,2,1,0:T(8,128)}, f32[2,4,128,128]{3,2,1,0:T(8,128)}, f32[2,4,128,128]{3,2,1,0:T(8,128)}) custom-call(s32[1]{0:T(128)} %bitcast.2.place_ref.to_ref, bf16[2,8,2,4,128,128]{5,4,3,2,1,0:T(8,128)(2,1)} %bitcast.25, f32[8,2,4,128,128]{4,3,2,1,0:T(8,128)} %bitcast.30), custom_call_target="tpu_custom_call" | custom-call | flops 12 | bytes 96 | tf_op jit(solution)/shard_map/scale_b/pallas_call | solution.py:137
  19.3 0.5 collective-permute-start.4
  19.8 0.8 collective-permute-start.5
  20.6 0.1 copy.13
  20.7 0.2 fusion.2
  21.0 0.1 copy.14
  21.1 5.1 %collective-permute-done.refs_1_ = f32[2,4,128,128]{3,2,1,0:T(8,128)S(1)} collective-permute-done((f32[2,4,128,128]{3,2,1,0:T(8,128)}, f32[2,4,128,128]{3,2,1,0:T(8,128)S(1)}, u32[]{:S(2)}, u32[]{:S(2)}) %collective-permute-start) | collective-permute-done | bytes 524320 | tf_op jit(solution)/shard_map/ppermute | solution.py:495
  26.1 1.4 collective-permute-start.6
  27.5 0.4 fusion.1
  27.9 0.0 copy-start
  27.9 2.0 %scale_b.6.refs_0_ = f32[2,4,128,128]{3,2,1,0:T(8,128)} custom-call(s32[1]{0:T(128)} %bitcast.2.place_ref.to_ref, bf16[2,8,2,4,128,128]{5,4,3,2,1,0:T(8,128)(2,1)} %bitcast.26, f32[8,2,4,128,128]{4,3,2,1,0:T(8,128)} %bitcast.31), custom_call_target="tpu_custom_call" | custom-call | flops 4 | bytes 32 | tf_op jit(solution)/shard_map/scale_b/pallas_call | solution.py:137
  29.9 8.6 %collective-permute-done.1.refs_2_ = f32[2,4,128,128]{3,2,1,0:T(8,128)S(1)} collective-permute-done((f32[2,4,128,128]{3,2,1,0:T(8,128)}, f32[2,4,128,128]{3,2,1,0:T(8,128)S(1)}, u32[]{:S(2)}, u32[]{:S(2)}) %collective-permute-start.1) | collective-permute-done | bytes 524320 | tf_op jit(solution)/shard_map/ppermute | solution.py:495
  38.5 0.8 collective-permute-done.2.refs_3_
  39.3 0.1 copy-done.8
  39.4 0.7 copy-done.9
  40.1 3.4 %first_y.2 = (f32[2,1,256,128]{3,2,1,0:T(8,128)}, f32[2,1,256,128]{3,2,1,0:T(8,128)}, f32[2,2,256,128]{3,2,1,0:T(8,128)}, f32[2,2,256,128]{3,2,1,0:T(8,128)}) custom-call(s32[1]{0:T(128)} %bitcast.2.place_ref.to_ref, s32[1]{0:T(128)} %bitcast.8.to_ref.place_ref, f32[2,4,128,128]{3,2,1,0:T(8,128)} %scale_b.6.refs_0_, f32[2,4,128,128]{3,2,1,0:T(8,128)} %copy-done.7, ...), custom_call_target="tpu_custom_call" | custom-call | flops 2048 | bytes 64 | tf_op jit(solution)/shard_map/first_y/pallas_call | solution.py:319
  43.5 3.4 %collective-permute-start.8 = (f32[2,1,256,128]{3,2,1,0:T(8,128)}, f32[2,1,256,128]{3,2,1,0:T(8,128)S(1)}, u32[]{:S(2)}, u32[]{:S(2)}) collective-permute-start(f32[2,1,256,128]{3,2,1,0:T(8,128)} %get-tuple-element.69), channel_id=1, source_target_pairs={{0,3},{1,0},{2,1},{3,2},{4,7},{5,4},{6,5},{7,6},{8,11},{9,8},{10,9... | collective-permute-start | bytes 786440 | tf_op jit(solution)/shard_map/ppermute | solution.py:495
  47.0 0.0 collective-permute-start.7
  47.0 2.0 %scale_b.7.refs_0_ = f32[2,4,128,128]{3,2,1,0:T(8,128)} custom-call(s32[1]{0:T(128)} %bitcast.2.place_ref.to_ref, bf16[2,8,2,4,128,128]{5,4,3,2,1,0:T(8,128)(2,1)} %bitcast.27, f32[8,2,4,128,128]{4,3,2,1,0:T(8,128)} %bitcast.32), custom_call_target="tpu_custom_call" | custom-call | flops 4 | bytes 32 | tf_op jit(solution)/shard_map/scale_b/pallas_call | solution.py:137
  49.0 9.6 %all-to-all-done.in_ref = f32[4,2,8,128,128]{4,3,2,1,0:T(8,128)} async-done(((f32[4,2,8,128,128]{4,3,2,1,0:T(8,128)}), f32[4,2,8,128,128]{4,3,2,1,0:T(8,128)}, u32[]{:S(2)}, u32[]{:S(2)}) %all-to-all-start) | async-done | bytes 4194336 | tf_op jit(solution)/shard_map/all_to_all | solution.py:512
  58.6 4.5 %first_z.1 = (f32[2,2,128,256]{3,2,1,0:T(8,128)}, f32[2,2,128,256]{3,2,1,0:T(8,128)}, f32[2,2,128,256]{3,2,1,0:T(8,128)}, f32[2,2,128,256]{3,2,1,0:T(8,128)}) custom-call(s32[1]{0:T(128)} %bitcast.2.place_ref.to_ref, f32[4,2,8,128,128]{4,3,2,1,0:T(8,128)} %all-to-all-done.in_ref, bf16[2,2,2,256,256]{4,3,2,1,0:T(8,128)(2,1)S(1)} %copy-done.1), custom_call_target="tpu_custom_call" | custom-call | flops 4096 | bytes 128 | tf_op jit(solution)/shard_map/first_z/pallas_call | solution.py:256
  63.1 3.0 %collective-permute-start.3 = (f32[2,2,128,256]{3,2,1,0:T(8,128)}, f32[2,2,128,256]{3,2,1,0:T(8,128)S(1)}, u32[]{:S(2)}, u32[]{:S(2)}) collective-permute-start(f32[2,2,128,256]{3,2,1,0:T(8,128)} %get-tuple-element.64), channel_id=1, source_target_pairs={{0,8},{4,12},{8,0},{12,4},{1,9},{5,13},{9,1},{13,5},{2,10},{6,14},... | collective-permute-start | bytes 1572872 | tf_op jit(solution)/shard_map/ppermute | solution.py:495
  66.1 0.0 collective-permute-done.5.refs_2_
  66.2 3.6 %first_y.3 = (f32[2,1,256,128]{3,2,1,0:T(8,128)}, f32[2,1,256,128]{3,2,1,0:T(8,128)}, f32[2,2,256,128]{3,2,1,0:T(8,128)}, f32[2,2,256,128]{3,2,1,0:T(8,128)}) custom-call(s32[1]{0:T(128)} %bitcast.2.place_ref.to_ref, s32[1]{0:T(128)} %bitcast.8.to_ref.place_ref, f32[2,4,128,128]{3,2,1,0:T(8,128)} %scale_b.7.refs_0_, ...), custom_call_target="tpu_custom_call", output_to_operand_aliasing={{2}: (6, {}), {3}: (7, {})} | custom-call | flops 2048 | bytes 64 | tf_op jit(solution)/shard_map/first_y/pallas_call | solution.py:319
  69.8 0.1 collective-permute-start.9
  69.9 0.7 collective-permute-start.10
  70.5 2.1 %collective-permute-start.11 = (f32[2,2,128,256]{3,2,1,0:T(8,128)S(1)}, f32[2,2,128,256]{3,2,1,0:T(8,128)S(1)}, u32[]{:S(2)}, u32[]{:S(2)}) collective-permute-start(f32[2,2,128,256]{3,2,1,0:T(8,128)S(1)} %copy-done.11), channel_id=1, source_target_pairs={{0,12},{4,0},{8,4},{12,8},{1,13},{5,1},{9,5},{13,9},{2,14},{6,2},{... | collective-permute-start | bytes 1572872 | tf_op jit(solution)/shard_map/ppermute | solution.py:495
  72.6 0.9 collective-permute-start.12
  73.5 2.5 %collective-permute-done.3.p2 = f32[2,2,128,256]{3,2,1,0:T(8,128)S(1)} collective-permute-done((f32[2,2,128,256]{3,2,1,0:T(8,128)}, f32[2,2,128,256]{3,2,1,0:T(8,128)S(1)}, u32[]{:S(2)}, u32[]{:S(2)}) %collective-permute-start.3) | collective-permute-done | bytes 524320 | tf_op jit(solution)/shard_map/ppermute | solution.py:495
  76.0 0.9 part_y.1.part_ref
  77.0 5.4 %collective-permute-done.9.b2 = f32[2,2,256,128]{3,2,1,0:T(8,128)S(1)} collective-permute-done((f32[2,2,256,128]{3,2,1,0:T(8,128)}, f32[2,2,256,128]{3,2,1,0:T(8,128)S(1)}, u32[]{:S(2)}, u32[]{:S(2)}) %collective-permute-start.9) | collective-permute-done | bytes 524320 | tf_op jit(solution)/shard_map/ppermute | solution.py:495
  82.4 7.2 %collective-permute-done.10.p1 = f32[2,2,128,256]{3,2,1,0:T(8,128)S(1)} collective-permute-done((f32[2,2,128,256]{3,2,1,0:T(8,128)S(1)}, f32[2,2,128,256]{3,2,1,0:T(8,128)S(1)}, u32[]{:S(2)}, u32[]{:S(2)}) %collective-permute-start.10) | collective-permute-done | bytes 524320 | tf_op jit(solution)/shard_map/ppermute | solution.py:495
  89.5 0.9 sum_y.1.done_a
  90.5 0.5 collective-permute-done.12.d1
  91.0 1.9 %second.1 = f32[128,2,2,8,128]{4,3,2,1,0:T(8,128)S(1)} custom-call(s32[1]{0:T(128)} %bitcast.8.to_ref.place_ref, f32[2,256,512]{2,1,0:T(8,128)S(1)} %sum_y.1.done_a, f32[2,2,256,128]{3,2,1,0:T(8,128)S(1)} %copy-done.2, f32[2,2,256,128]{3,2,1,0:T(8,128)S(1)} %collective-permute-done.9.b2, f32[2,1,256,128]{3,2,1,0:T(8,128)S(1)} %collective-permute-done.7.c1, ...), custom_call_target="tpu_custom_call" | custom-call | flops 2048 | bytes 128 | tf_op jit(solution)/shard_map/second/pallas_call | solution.py:423
  93.0 0.0 copy-start.3
  93.0 0.0 copy-start.5
  93.0 36.9 %all_to_all.22.in_ref = f32[128,2,2,8,128]{4,3,2,1,0:T(8,128)S(1)} all-to-all(f32[128,2,2,8,128]{4,3,2,1,0:T(8,128)S(1)} %second.1), channel_id=1, replica_groups=mesh['gx'=8,'gy'=4,'gz'=4] {'gx','gy','gz'}, dimensions={0} | all-to-all | bytes 4194304 | tf_op jit(solution)/shard_map/all_to_all | solution.py:536
  129.9 3.7 %third.1 = f32[4096,128]{1,0:T(8,128)S(1)} custom-call(s32[1024]{0:T(1024)S(1)} %multiply_add_fusion.slot_ref, f32[128,2,2,8,128]{4,3,2,1,0:T(8,128)S(1)} %all_to_all.22.in_ref, bf16[2,2,256,512]{3,2,1,0:T(8,128)(2,1)S(1)} %copy-done.3, bf16[256,256]{1,0:T(8,128)(2,1)S(1)} %copy-done.5), custom_call_target="tpu_custom_call" | custom-call | flops 3072 | bytes 96 | tf_op jit(solution)/shard_map/third/pallas_call | solution.py:481
  133.6 34.2 %all_to_all.23 = f32[128,1,16,2,128]{4,3,2,1,0:T(2,128)S(1)} all-to-all(f32[128,1,16,2,128]{4,3,2,1,0:T(2,128)S(1)} %bitcast.22), channel_id=1, replica_groups=mesh['gx'=8,'gy'=4,'gz'=4] {'gx','gy','gz'}, dimensions={0} | all-to-all | bytes 4194304 | tf_op jit(solution)/shard_map/all_to_all | solution.py:538
  167.8 1.3 copy.19
  (32 shorter events, 0.1 us)
Async XLA Ops:
  3.8 54.8 %all-to-all-start = ((f32[4,2,8,128,128]{4,3,2,1,0:T(8,128)}), f32[4,2,8,128,128]{4,3,2,1,0:T(8,128)}, u32[]{:S(2)}, u32[]{:S(2)}) async-start(f32[4,2,8,128,128]{4,3,2,1,0:T(8,128)} %scale_a.1), calls=%async_computation | async-start | bytes 8388608 | tf_op jit(solution)/shard_map/all_to_all | solution.py:512
  11.9 8.6 %copy-start.10 = (s32[1024,1]{0,1:T(1,128)S(1)}, s32[1024,1]{0,1:T(1,128)}, u32[]{:S(2)}) copy-start(s32[1024,1]{0,1:T(1,128)} %param.9) | copy-start | bytes 12292
  11.9 14.2 %collective-permute-start = (f32[2,4,128,128]{3,2,1,0:T(8,128)}, f32[2,4,128,128]{3,2,1,0:T(8,128)S(1)}, u32[]{:S(2)}, u32[]{:S(2)}) collective-permute-start(f32[2,4,128,128]{3,2,1,0:T(8,128)} %get-tuple-element.57), channel_id=1, source_target_pairs={{0,4},{4,8},{8,12},{12,0},{1,5},{5,9},{9,13},{13,1},{2,6},{6,10},{... | collective-permute-start | bytes 1572872 | tf_op jit(solution)/shard_map/ppermute | solution.py:495
  13.3 25.2 %collective-permute-start.1 = (f32[2,4,128,128]{3,2,1,0:T(8,128)}, f32[2,4,128,128]{3,2,1,0:T(8,128)S(1)}, u32[]{:S(2)}, u32[]{:S(2)}) collective-permute-start(f32[2,4,128,128]{3,2,1,0:T(8,128)} %get-tuple-element.58), channel_id=1, source_target_pairs={{0,8},{4,12},{8,0},{12,4},{1,9},{5,13},{9,1},{13,5},{2,10},{6,14},... | collective-permute-start | bytes 1572872 | tf_op jit(solution)/shard_map/ppermute | solution.py:495
  15.9 23.4 %collective-permute-start.2 = (f32[2,4,128,128]{3,2,1,0:T(8,128)}, f32[2,4,128,128]{3,2,1,0:T(8,128)S(1)}, u32[]{:S(2)}, u32[]{:S(2)}) collective-permute-start(f32[2,4,128,128]{3,2,1,0:T(8,128)} %get-tuple-element.59), channel_id=1, source_target_pairs={{0,12},{4,0},{8,4},{12,8},{1,13},{5,1},{9,5},{13,9},{2,14},{6,2},{... | collective-permute-start | bytes 1572872 | tf_op jit(solution)/shard_map/ppermute | solution.py:495
  19.3 43.8 %collective-permute-start.4 = (f32[2,4,128,128]{3,2,1,0:T(8,128)}, f32[2,4,128,128]{3,2,1,0:T(8,128)S(1)}, u32[]{:S(2)}, u32[]{:S(2)}) collective-permute-start(f32[2,4,128,128]{3,2,1,0:T(8,128)} %get-tuple-element.66), channel_id=1, source_target_pairs={{0,4},{4,8},{8,12},{12,0},{1,5},{5,9},{9,13},{13,1},{2,6},{6,10},{... | collective-permute-start | bytes 1572872 | tf_op jit(solution)/shard_map/ppermute | solution.py:495
  19.8 46.4 %collective-permute-start.5 = (f32[2,4,128,128]{3,2,1,0:T(8,128)}, f32[2,4,128,128]{3,2,1,0:T(8,128)}, u32[]{:S(2)}, u32[]{:S(2)}) collective-permute-start(f32[2,4,128,128]{3,2,1,0:T(8,128)} %get-tuple-element.67), channel_id=1, source_target_pairs={{0,8},{4,12},{8,0},{12,4},{1,9},{5,13},{9,1},{13,5},{2,10},{6,14},... | collective-permute-start | bytes 1572872 | tf_op jit(solution)/shard_map/ppermute | solution.py:495
  26.1 3.8 %copy-start.7 = (f32[2,4,128,128]{3,2,1,0:T(8,128)}, f32[2,4,128,128]{3,2,1,0:T(8,128)S(1)}, u32[]{:S(2)}) copy-start(f32[2,4,128,128]{3,2,1,0:T(8,128)S(1)} %collective-permute-done.refs_1_) | copy-start | bytes 1572868
  26.1 40.0 %collective-permute-start.6 = (f32[2,4,128,128]{3,2,1,0:T(8,128)}, f32[2,4,128,128]{3,2,1,0:T(8,128)}, u32[]{:S(2)}, u32[]{:S(2)}) collective-permute-start(f32[2,4,128,128]{3,2,1,0:T(8,128)} %get-tuple-element.68), channel_id=1, source_target_pairs={{0,12},{4,0},{8,4},{12,8},{1,13},{5,1},{9,5},{13,9},{2,14},{6,2},{... | collective-permute-start | bytes 1572872 | tf_op jit(solution)/shard_map/ppermute | solution.py:495
  27.9 12.2 %copy-start = (bf16[2,2,2,256,256]{4,3,2,1,0:T(8,128)(2,1)S(1)}, bf16[2,2,2,256,256]{4,3,2,1,0:T(8,128)(2,1)}, u32[]{:S(2)}) copy-start(bf16[2,2,2,256,256]{4,3,2,1,0:T(8,128)(2,1)} %constant.24.clone.refs_4_.table_ref.refs_6_) | copy-start | bytes 3145732
  38.5 0.9 copy-start.8
  39.3 0.8 copy-start.9
  43.5 22.6 %collective-permute-start.8 = (f32[2,1,256,128]{3,2,1,0:T(8,128)}, f32[2,1,256,128]{3,2,1,0:T(8,128)S(1)}, u32[]{:S(2)}, u32[]{:S(2)}) collective-permute-start(f32[2,1,256,128]{3,2,1,0:T(8,128)} %get-tuple-element.69), channel_id=1, source_target_pairs={{0,3},{1,0},{2,1},{3,2},{4,7},{5,4},{6,5},{7,6},{8,11},{9,8},{10,9... | collective-permute-start | bytes 786440 | tf_op jit(solution)/shard_map/ppermute | solution.py:495
  47.0 19.2 %collective-permute-start.7 = (f32[2,1,256,128]{3,2,1,0:T(8,128)}, f32[2,1,256,128]{3,2,1,0:T(8,128)S(1)}, u32[]{:S(2)}, u32[]{:S(2)}) collective-permute-start(f32[2,1,256,128]{3,2,1,0:T(8,128)} %get-tuple-element.60), channel_id=1, source_target_pairs={{0,1},{1,2},{2,3},{3,0},{4,5},{5,6},{6,7},{7,4},{8,9},{9,10},{10,1... | collective-permute-start | bytes 786440 | tf_op jit(solution)/shard_map/ppermute | solution.py:495
  47.0 11.6 %copy-start.1 = (bf16[2,2,2,256,256]{4,3,2,1,0:T(8,128)(2,1)S(1)}, bf16[2,2,2,256,256]{4,3,2,1,0:T(8,128)(2,1)}, u32[]{:S(2)}) copy-start(bf16[2,2,2,256,256]{4,3,2,1,0:T(8,128)(2,1)} %constant.25.clone.table_ref) | copy-start | bytes 3145732
  63.1 3.0 %copy-start.6 = (f32[2,4,128,128]{3,2,1,0:T(8,128)}, f32[2,4,128,128]{3,2,1,0:T(8,128)S(1)}, u32[]{:S(2)}) copy-start(f32[2,4,128,128]{3,2,1,0:T(8,128)S(1)} %collective-permute-done.4.refs_1_) | copy-start | bytes 1572868
  63.1 12.9 %collective-permute-start.3 = (f32[2,2,128,256]{3,2,1,0:T(8,128)}, f32[2,2,128,256]{3,2,1,0:T(8,128)S(1)}, u32[]{:S(2)}, u32[]{:S(2)}) collective-permute-start(f32[2,2,128,256]{3,2,1,0:T(8,128)} %get-tuple-element.64), channel_id=1, source_target_pairs={{0,8},{4,12},{8,0},{12,4},{1,9},{5,13},{9,1},{13,5},{2,10},{6,14},... | collective-permute-start | bytes 1572872 | tf_op jit(solution)/shard_map/ppermute | solution.py:495
  66.2 3.7 %copy-start.12 = (f32[2,2,128,256]{3,2,1,0:T(8,128)S(1)}, f32[2,2,128,256]{3,2,1,0:T(8,128)}, u32[]{:S(2)}) copy-start(f32[2,2,128,256]{3,2,1,0:T(8,128)} %get-tuple-element.77) | copy-start | bytes 1572868
  66.2 4.3 %copy-start.11 = (f32[2,2,128,256]{3,2,1,0:T(8,128)S(1)}, f32[2,2,128,256]{3,2,1,0:T(8,128)}, u32[]{:S(2)}) copy-start(f32[2,2,128,256]{3,2,1,0:T(8,128)} %get-tuple-element.78) | copy-start | bytes 1572868
  66.2 9.8 %copy-start.4 = (f32[2,2,128,256]{3,2,1,0:T(8,128)S(1)}, f32[2,2,128,256]{3,2,1,0:T(8,128)}, u32[]{:S(2)}) copy-start(f32[2,2,128,256]{3,2,1,0:T(8,128)} %get-tuple-element.63.p0) | copy-start | bytes 1572868
  69.8 12.6 %collective-permute-start.9 = (f32[2,2,256,128]{3,2,1,0:T(8,128)}, f32[2,2,256,128]{3,2,1,0:T(8,128)S(1)}, u32[]{:S(2)}, u32[]{:S(2)}) collective-permute-start(f32[2,2,256,128]{3,2,1,0:T(8,128)} %get-tuple-element.75), channel_id=1, source_target_pairs={{0,2},{1,3},{2,0},{3,1},{4,6},{5,7},{6,4},{7,5},{8,10},{9,11},{10,... | collective-permute-start | bytes 1572872 | tf_op jit(solution)/shard_map/ppermute | solution.py:495
  69.9 19.7 %collective-permute-start.10 = (f32[2,2,128,256]{3,2,1,0:T(8,128)S(1)}, f32[2,2,128,256]{3,2,1,0:T(8,128)S(1)}, u32[]{:S(2)}, u32[]{:S(2)}) collective-permute-start(f32[2,2,128,256]{3,2,1,0:T(8,128)S(1)} %copy-done.12), channel_id=1, source_target_pairs={{0,4},{4,8},{8,12},{12,0},{1,5},{5,9},{9,13},{13,1},{2,6},{6,10},{... | collective-permute-start | bytes 1572872 | tf_op jit(solution)/shard_map/ppermute | solution.py:495
  70.5 19.0 %collective-permute-start.11 = (f32[2,2,128,256]{3,2,1,0:T(8,128)S(1)}, f32[2,2,128,256]{3,2,1,0:T(8,128)S(1)}, u32[]{:S(2)}, u32[]{:S(2)}) collective-permute-start(f32[2,2,128,256]{3,2,1,0:T(8,128)S(1)} %copy-done.11), channel_id=1, source_target_pairs={{0,12},{4,0},{8,4},{12,8},{1,13},{5,1},{9,5},{13,9},{2,14},{6,2},{... | collective-permute-start | bytes 1572872 | tf_op jit(solution)/shard_map/ppermute | solution.py:495
  72.6 18.4 %collective-permute-start.12 = (f32[2,1,256,128]{3,2,1,0:T(8,128)}, f32[2,1,256,128]{3,2,1,0:T(8,128)S(1)}, u32[]{:S(2)}, u32[]{:S(2)}) collective-permute-start(f32[2,1,256,128]{3,2,1,0:T(8,128)} %get-tuple-element.80), channel_id=1, source_target_pairs={{0,1},{1,2},{2,3},{3,0},{4,5},{5,6},{6,7},{7,4},{8,9},{9,10},{10,1... | collective-permute-start | bytes 786440 | tf_op jit(solution)/shard_map/ppermute | solution.py:495
  76.0 15.0 %collective-permute-start.13 = (f32[2,1,256,128]{3,2,1,0:T(8,128)}, f32[2,1,256,128]{3,2,1,0:T(8,128)S(1)}, u32[]{:S(2)}, u32[]{:S(2)}) collective-permute-start(f32[2,1,256,128]{3,2,1,0:T(8,128)} %get-tuple-element.81), channel_id=1, source_target_pairs={{0,3},{1,0},{2,1},{3,2},{4,7},{5,4},{6,5},{7,6},{8,11},{9,8},{10,9... | collective-permute-start | bytes 786440 | tf_op jit(solution)/shard_map/ppermute | solution.py:495
  77.0 14.0 %copy-start.2 = (f32[2,2,256,128]{3,2,1,0:T(8,128)S(1)}, f32[2,2,256,128]{3,2,1,0:T(8,128)}, u32[]{:S(2)}) copy-start(f32[2,2,256,128]{3,2,1,0:T(8,128)} %get-tuple-element.83.b0) | copy-start | bytes 1572868
  93.0 36.9 %copy-start.3 = (bf16[2,2,256,512]{3,2,1,0:T(8,128)(2,1)S(1)}, bf16[2,2,256,512]{3,2,1,0:T(8,128)(2,1)}, u32[]{:S(2)}) copy-start(bf16[2,2,256,512]{3,2,1,0:T(8,128)(2,1)} %constant.23.clone.table_ref) | copy-start | bytes 3145732
  93.0 36.9 %copy-start.5 = (bf16[256,256]{1,0:T(8,128)(2,1)S(1)}, bf16[256,256]{1,0:T(8,128)(2,1)}, u32[]{:S(2)}) copy-start(bf16[256,256]{1,0:T(8,128)(2,1)} %constant.26.clone.ordering_ref) | copy-start | bytes 393220

commit v27 on v25

--- a/solution.py
+++ b/solution.py
@@ -15,7 +15,7 @@
 CAP = 16
 ALL = ("gx", "gy", "gz")
 MIB = 1 << 20
-VMEM = 24
+VMEM = 16
 
 
 def split_table(table):

time: 169 us -> 169 us (level)
  no operation moved by 1% of the time
where the time goes in v27:
time: 169 us
  blocking collectives  71.1 us (42%)
  waiting for transfers between devices  39.1 us (23%)
  Pallas kernels  31 us (18%)
  starting transfers between devices  24.2 us (14%)
  local copies, waits for them, and re-layouts  2.47 us (1%)
    all_to_all x1, blocking collectives, per_device(): lines = lax.all_to_all(planes, ALL, split_axis=0, concat_axis=0, tiled=True)  36.9 us
    all_to_all x1, blocking collectives, per_device(): lax.all_to_all(outgoing.reshape(128, 1, CAP, 2, BW), ALL, split_axis=0, c...  34.2 us
    ppermute x14, waiting for transfers between devices, shifted(): lax.ppermute(piece, axis, [(i, (i + shift) % size) for i in range(size)])  30.1 us
    ppermute x14, starting transfers between devices, shifted(): lax.ppermute(piece, axis, [(i, (i + shift) % size) for i in range(size)])  18.4 us
    pallas_call x5, Pallas kernels, scale(): pl.pallas_call(functools.partial(scale_kernel, part, shifts), in_specs=[p...  11.9 us
    all_to_all x1, waiting for transfers between devices, per_device(): a = lax.all_to_all(a, 'gz', split_axis=0, concat_axis=0, tiled=True)  9 us
    pallas_call x2, Pallas kernels, first_y(): pl.pallas_call(functools.partial(first_y_kernel, merge), in_specs=[pl.Blo...  7 us
    all_to_all x1, starting transfers between devices, per_device(): a = lax.all_to_all(a, 'gz', split_axis=0, concat_axis=0, tiled=True)  5.87 us
  transfers between devices with their start and end apart: 15, of which 8 were waited for; matrix products, arithmetic and copies ran while one was open for 0% of the time, Pallas kernels for 13%

profile of v27, /device:TPU:1, one launch (start us, length us, event | category | flops | bytes accessed | tf_op | source)
XLA Modules:
  0.0 168.7 jit_solution(7803879018882543348)
XLA Ops:
  0.0 3.4 %scale_a.1 = f32[4,2,8,128,128]{4,3,2,1,0:T(8,128)} custom-call(s32[1]{0:T(128)} %bitcast.place_ref.to_ref, bf16[2,8,8,128,128]{4,3,2,1,0:T(8,128)(2,1)} %bitcast.23, f32[8,8,128,128]{3,2,1,0:T(8,128)} %bitcast.28), custom_call_target="tpu_custom_call" | custom-call | flops 16 | bytes 128 | tf_op jit(solution)/shard_map/scale_a/pallas_call | solution.py:137
  3.4 5.9 %all-to-all-start = ((f32[4,2,8,128,128]{4,3,2,1,0:T(8,128)}), f32[4,2,8,128,128]{4,3,2,1,0:T(8,128)}, u32[]{:S(2)}, u32[]{:S(2)}) async-start(f32[4,2,8,128,128]{4,3,2,1,0:T(8,128)} %scale_a.1), calls=%async_computation | async-start | bytes 8388608 | tf_op jit(solution)/shard_map/all_to_all | solution.py:461
  9.3 2.3 %scale_b.4 = (f32[2,4,128,128]{3,2,1,0:T(8,128)}, f32[2,4,128,128]{3,2,1,0:T(8,128)}, f32[2,4,128,128]{3,2,1,0:T(8,128)}) custom-call(s32[1]{0:T(128)} %bitcast.3.place_ref.to_ref, bf16[2,8,2,4,128,128]{5,4,3,2,1,0:T(8,128)(2,1)} %bitcast.24, f32[8,2,4,128,128]{4,3,2,1,0:T(8,128)} %bitcast.29), custom_call_target="tpu_custom_call" | custom-call | flops 12 | bytes 96 | tf_op jit(solution)/shard_map/scale_b/pallas_call | solution.py:137
  11.6 0.0 copy-start.10
  11.6 1.4 collective-permute-start
  12.9 2.6 %collective-permute-start.1 = (f32[2,4,128,128]{3,2,1,0:T(8,128)}, f32[2,4,128,128]{3,2,1,0:T(8,128)S(1)}, u32[]{:S(2)}, u32[]{:S(2)}) collective-permute-start(f32[2,4,128,128]{3,2,1,0:T(8,128)} %get-tuple-element.58), channel_id=1, source_target_pairs={{0,8},{4,12},{8,0},{12,4},{1,9},{5,13},{9,1},{13,5},{2,10},{6,14},... | collective-permute-start | bytes 1572872 | tf_op jit(solution)/shard_map/ppermute | solution.py:444
  15.6 1.1 collective-permute-start.2
  16.6 2.3 %scale_b.5 = (f32[2,4,128,128]{3,2,1,0:T(8,128)}, f32[2,4,128,128]{3,2,1,0:T(8,128)}, f32[2,4,128,128]{3,2,1,0:T(8,128)}) custom-call(s32[1]{0:T(128)} %bitcast.3.place_ref.to_ref, bf16[2,8,2,4,128,128]{5,4,3,2,1,0:T(8,128)(2,1)} %bitcast.25, f32[8,2,4,128,128]{4,3,2,1,0:T(8,128)} %bitcast.30), custom_call_target="tpu_custom_call" | custom-call | flops 12 | bytes 96 | tf_op jit(solution)/shard_map/scale_b/pallas_call | solution.py:137
  18.9 0.5 collective-permute-start.4
  19.4 0.8 collective-permute-start.5
  20.2 0.1 copy.13
  20.3 0.2 fusion.2
  20.6 0.1 copy.14
  20.7 5.1 %collective-permute-done.refs_1_ = f32[2,4,128,128]{3,2,1,0:T(8,128)S(1)} collective-permute-done((f32[2,4,128,128]{3,2,1,0:T(8,128)}, f32[2,4,128,128]{3,2,1,0:T(8,128)S(1)}, u32[]{:S(2)}, u32[]{:S(2)}) %collective-permute-start) | collective-permute-done | bytes 524320 | tf_op jit(solution)/shard_map/ppermute | solution.py:444
  25.8 1.4 collective-permute-start.6
  27.2 0.4 fusion.1
  27.5 0.0 copy-start
  27.5 2.0 %scale_b.6.refs_0_ = f32[2,4,128,128]{3,2,1,0:T(8,128)} custom-call(s32[1]{0:T(128)} %bitcast.3.place_ref.to_ref, bf16[2,8,2,4,128,128]{5,4,3,2,1,0:T(8,128)(2,1)} %bitcast.26, f32[8,2,4,128,128]{4,3,2,1,0:T(8,128)} %bitcast.31), custom_call_target="tpu_custom_call" | custom-call | flops 4 | bytes 32 | tf_op jit(solution)/shard_map/scale_b/pallas_call | solution.py:137
  29.5 8.6 %collective-permute-done.1.refs_2_ = f32[2,4,128,128]{3,2,1,0:T(8,128)S(1)} collective-permute-done((f32[2,4,128,128]{3,2,1,0:T(8,128)}, f32[2,4,128,128]{3,2,1,0:T(8,128)S(1)}, u32[]{:S(2)}, u32[]{:S(2)}) %collective-permute-start.1) | collective-permute-done | bytes 524320 | tf_op jit(solution)/shard_map/ppermute | solution.py:444
  38.2 0.8 collective-permute-done.2.refs_3_
  38.9 0.1 copy-done.8
  39.0 0.8 copy-done.9
  39.8 3.4 %first_y.2 = (f32[2,1,256,128]{3,2,1,0:T(8,128)}, f32[2,1,256,128]{3,2,1,0:T(8,128)}, f32[2,2,256,128]{3,2,1,0:T(8,128)}, f32[2,2,256,128]{3,2,1,0:T(8,128)}) custom-call(s32[1]{0:T(128)} %bitcast.3.place_ref.to_ref, s32[1]{0:T(128)} %bitcast.place_ref.to_ref, f32[2,4,128,128]{3,2,1,0:T(8,128)} %scale_b.6.refs_0_, f32[2,4,128,128]{3,2,1,0:T(8,128)} %copy-done.7, ...), custom_call_target="tpu_custom_call" | custom-call | flops 2048 | bytes 64 | tf_op jit(solution)/shard_map/first_y/pallas_call | solution.py:268
  43.3 4.0 %collective-permute-start.8 = (f32[2,1,256,128]{3,2,1,0:T(8,128)}, f32[2,1,256,128]{3,2,1,0:T(8,128)S(1)}, u32[]{:S(2)}, u32[]{:S(2)}) collective-permute-start(f32[2,1,256,128]{3,2,1,0:T(8,128)} %get-tuple-element.69), channel_id=1, source_target_pairs={{0,3},{1,0},{2,1},{3,2},{4,7},{5,4},{6,5},{7,6},{8,11},{9,8},{10,9... | collective-permute-start | bytes 786440 | tf_op jit(solution)/shard_map/ppermute | solution.py:444
  47.2 0.0 collective-permute-start.7
  47.2 2.0 %scale_b.7.refs_0_ = f32[2,4,128,128]{3,2,1,0:T(8,128)} custom-call(s32[1]{0:T(128)} %bitcast.3.place_ref.to_ref, bf16[2,8,2,4,128,128]{5,4,3,2,1,0:T(8,128)(2,1)} %bitcast.27, f32[8,2,4,128,128]{4,3,2,1,0:T(8,128)} %bitcast.32), custom_call_target="tpu_custom_call" | custom-call | flops 4 | bytes 32 | tf_op jit(solution)/shard_map/scale_b/pallas_call | solution.py:137
  49.2 9.0 %all-to-all-done.in_ref = f32[4,2,8,128,128]{4,3,2,1,0:T(8,128)} async-done(((f32[4,2,8,128,128]{4,3,2,1,0:T(8,128)}), f32[4,2,8,128,128]{4,3,2,1,0:T(8,128)}, u32[]{:S(2)}, u32[]{:S(2)}) %all-to-all-start) | async-done | bytes 4194336 | tf_op jit(solution)/shard_map/all_to_all | solution.py:461
  58.2 4.5 %first_z.1 = (f32[2,2,128,256]{3,2,1,0:T(8,128)}, f32[2,2,128,256]{3,2,1,0:T(8,128)}, f32[2,2,128,256]{3,2,1,0:T(8,128)}, f32[2,2,128,256]{3,2,1,0:T(8,128)}) custom-call(s32[1]{0:T(128)} %bitcast.3.place_ref.to_ref, f32[4,2,8,128,128]{4,3,2,1,0:T(8,128)} %all-to-all-done.in_ref, bf16[2,2,2,256,256]{4,3,2,1,0:T(8,128)(2,1)S(1)} %copy-done.1), custom_call_target="tpu_custom_call" | custom-call | flops 4096 | bytes 128 | tf_op jit(solution)/shard_map/first_z/pallas_call | solution.py:205
  62.8 3.0 %collective-permute-start.3 = (f32[2,2,128,256]{3,2,1,0:T(8,128)}, f32[2,2,128,256]{3,2,1,0:T(8,128)S(1)}, u32[]{:S(2)}, u32[]{:S(2)}) collective-permute-start(f32[2,2,128,256]{3,2,1,0:T(8,128)} %get-tuple-element.64), channel_id=1, source_target_pairs={{0,8},{4,12},{8,0},{12,4},{1,9},{5,13},{9,1},{13,5},{2,10},{6,14},... | collective-permute-start | bytes 1572872 | tf_op jit(solution)/shard_map/ppermute | solution.py:444
  65.8 0.0 collective-permute-done.8.c3
  65.8 3.6 %first_y.3 = (f32[2,1,256,128]{3,2,1,0:T(8,128)}, f32[2,1,256,128]{3,2,1,0:T(8,128)}, f32[2,2,256,128]{3,2,1,0:T(8,128)}, f32[2,2,256,128]{3,2,1,0:T(8,128)}) custom-call(s32[1]{0:T(128)} %bitcast.3.place_ref.to_ref, s32[1]{0:T(128)} %bitcast.place_ref.to_ref, f32[2,4,128,128]{3,2,1,0:T(8,128)} %scale_b.7.refs_0_, ...), custom_call_target="tpu_custom_call", output_to_operand_aliasing={{2}: (6, {}), {3}: (7, {})} | custom-call | flops 2048 | bytes 64 | tf_op jit(solution)/shard_map/first_y/pallas_call | solution.py:268
  69.4 0.1 collective-permute-start.9
  69.5 0.6 collective-permute-start.10
  70.1 2.1 %collective-permute-start.11 = (f32[2,2,128,256]{3,2,1,0:T(8,128)S(1)}, f32[2,2,128,256]{3,2,1,0:T(8,128)S(1)}, u32[]{:S(2)}, u32[]{:S(2)}) collective-permute-start(f32[2,2,128,256]{3,2,1,0:T(8,128)S(1)} %copy-done.11), channel_id=1, source_target_pairs={{0,12},{4,0},{8,4},{12,8},{1,13},{5,1},{9,5},{13,9},{2,14},{6,2},{... | collective-permute-start | bytes 1572872 | tf_op jit(solution)/shard_map/ppermute | solution.py:444
  72.2 0.9 collective-permute-start.12
  73.1 2.5 %collective-permute-done.3.p2 = f32[2,2,128,256]{3,2,1,0:T(8,128)S(1)} collective-permute-done((f32[2,2,128,256]{3,2,1,0:T(8,128)}, f32[2,2,128,256]{3,2,1,0:T(8,128)S(1)}, u32[]{:S(2)}, u32[]{:S(2)}) %collective-permute-start.3) | collective-permute-done | bytes 524320 | tf_op jit(solution)/shard_map/ppermute | solution.py:444
  75.6 0.9 part_y.1.part_ref
  76.6 5.4 %collective-permute-done.9.b2 = f32[2,2,256,128]{3,2,1,0:T(8,128)S(1)} collective-permute-done((f32[2,2,256,128]{3,2,1,0:T(8,128)}, f32[2,2,256,128]{3,2,1,0:T(8,128)S(1)}, u32[]{:S(2)}, u32[]{:S(2)}) %collective-permute-start.9) | collective-permute-done | bytes 524320 | tf_op jit(solution)/shard_map/ppermute | solution.py:444
  82.0 7.2 %collective-permute-done.10.p1 = f32[2,2,128,256]{3,2,1,0:T(8,128)S(1)} collective-permute-done((f32[2,2,128,256]{3,2,1,0:T(8,128)S(1)}, f32[2,2,128,256]{3,2,1,0:T(8,128)S(1)}, u32[]{:S(2)}, u32[]{:S(2)}) %collective-permute-start.10) | collective-permute-done | bytes 524320 | tf_op jit(solution)/shard_map/ppermute | solution.py:444
  89.2 0.9 sum_y.1.done_a
  90.1 0.5 collective-permute-done.12.d1
  90.6 2.0 %second.1 = f32[128,2,2,8,128]{4,3,2,1,0:T(8,128)S(1)} custom-call(s32[1]{0:T(128)} %bitcast.place_ref.to_ref, f32[2,256,512]{2,1,0:T(8,128)S(1)} %sum_y.1.done_a, f32[2,2,256,128]{3,2,1,0:T(8,128)S(1)} %copy-done.2, f32[2,2,256,128]{3,2,1,0:T(8,128)S(1)} %collective-permute-done.9.b2, f32[2,1,256,128]{3,2,1,0:T(8,128)S(1)} %collective-permute-done.7.c1, ...), custom_call_target="tpu_custom_call" | custom-call | flops 2048 | bytes 128 | tf_op jit(solution)/shard_map/second/pallas_call | solution.py:372
  92.6 0.0 copy-start.3
  92.6 0.0 copy-start.5
  92.6 36.9 %all_to_all.22.in_ref = f32[128,2,2,8,128]{4,3,2,1,0:T(8,128)S(1)} all-to-all(f32[128,2,2,8,128]{4,3,2,1,0:T(8,128)S(1)} %second.1), channel_id=1, replica_groups=mesh['gx'=8,'gy'=4,'gz'=4] {'gx','gy','gz'}, dimensions={0} | all-to-all | bytes 4194304 | tf_op jit(solution)/shard_map/all_to_all | solution.py:485
  129.5 3.7 %third.1 = f32[4096,128]{1,0:T(8,128)S(1)} custom-call(s32[1024]{0:T(1024)S(1)} %multiply_add_fusion.slot_ref, f32[128,2,2,8,128]{4,3,2,1,0:T(8,128)S(1)} %all_to_all.22.in_ref, bf16[2,2,256,512]{3,2,1,0:T(8,128)(2,1)S(1)} %copy-done.3, bf16[256,256]{1,0:T(8,128)(2,1)S(1)} %copy-done.5), custom_call_target="tpu_custom_call" | custom-call | flops 3072 | bytes 96 | tf_op jit(solution)/shard_map/third/pallas_call | solution.py:430
  133.2 34.2 %all_to_all.23 = f32[128,1,16,2,128]{4,3,2,1,0:T(2,128)S(1)} all-to-all(f32[128,1,16,2,128]{4,3,2,1,0:T(2,128)S(1)} %bitcast.22), channel_id=1, replica_groups=mesh['gx'=8,'gy'=4,'gz'=4] {'gx','gy','gz'}, dimensions={0} | all-to-all | bytes 4194304 | tf_op jit(solution)/shard_map/all_to_all | solution.py:487
  167.4 1.3 copy.19
  (32 shorter events, 0.1 us)
Async XLA Ops:
  3.4 54.8 %all-to-all-start = ((f32[4,2,8,128,128]{4,3,2,1,0:T(8,128)}), f32[4,2,8,128,128]{4,3,2,1,0:T(8,128)}, u32[]{:S(2)}, u32[]{:S(2)}) async-start(f32[4,2,8,128,128]{4,3,2,1,0:T(8,128)} %scale_a.1), calls=%async_computation | async-start | bytes 8388608 | tf_op jit(solution)/shard_map/all_to_all | solution.py:461
  11.6 8.6 %copy-start.10 = (s32[1024,1]{0,1:T(1,128)S(1)}, s32[1024,1]{0,1:T(1,128)}, u32[]{:S(2)}) copy-start(s32[1024,1]{0,1:T(1,128)} %param.9) | copy-start | bytes 12292
  11.6 14.2 %collective-permute-start = (f32[2,4,128,128]{3,2,1,0:T(8,128)}, f32[2,4,128,128]{3,2,1,0:T(8,128)S(1)}, u32[]{:S(2)}, u32[]{:S(2)}) collective-permute-start(f32[2,4,128,128]{3,2,1,0:T(8,128)} %get-tuple-element.57), channel_id=1, source_target_pairs={{0,4},{4,8},{8,12},{12,0},{1,5},{5,9},{9,13},{13,1},{2,6},{6,10},{... | collective-permute-start | bytes 1572872 | tf_op jit(solution)/shard_map/ppermute | solution.py:444
  12.9 25.2 %collective-permute-start.1 = (f32[2,4,128,128]{3,2,1,0:T(8,128)}, f32[2,4,128,128]{3,2,1,0:T(8,128)S(1)}, u32[]{:S(2)}, u32[]{:S(2)}) collective-permute-start(f32[2,4,128,128]{3,2,1,0:T(8,128)} %get-tuple-element.58), channel_id=1, source_target_pairs={{0,8},{4,12},{8,0},{12,4},{1,9},{5,13},{9,1},{13,5},{2,10},{6,14},... | collective-permute-start | bytes 1572872 | tf_op jit(solution)/shard_map/ppermute | solution.py:444
  15.6 23.4 %collective-permute-start.2 = (f32[2,4,128,128]{3,2,1,0:T(8,128)}, f32[2,4,128,128]{3,2,1,0:T(8,128)S(1)}, u32[]{:S(2)}, u32[]{:S(2)}) collective-permute-start(f32[2,4,128,128]{3,2,1,0:T(8,128)} %get-tuple-element.59), channel_id=1, source_target_pairs={{0,12},{4,0},{8,4},{12,8},{1,13},{5,1},{9,5},{13,9},{2,14},{6,2},{... | collective-permute-start | bytes 1572872 | tf_op jit(solution)/shard_map/ppermute | solution.py:444
  18.9 43.8 %collective-permute-start.4 = (f32[2,4,128,128]{3,2,1,0:T(8,128)}, f32[2,4,128,128]{3,2,1,0:T(8,128)S(1)}, u32[]{:S(2)}, u32[]{:S(2)}) collective-permute-start(f32[2,4,128,128]{3,2,1,0:T(8,128)} %get-tuple-element.66), channel_id=1, source_target_pairs={{0,4},{4,8},{8,12},{12,0},{1,5},{5,9},{9,13},{13,1},{2,6},{6,10},{... | collective-permute-start | bytes 1572872 | tf_op jit(solution)/shard_map/ppermute | solution.py:444
  19.4 46.4 %collective-permute-start.5 = (f32[2,4,128,128]{3,2,1,0:T(8,128)}, f32[2,4,128,128]{3,2,1,0:T(8,128)}, u32[]{:S(2)}, u32[]{:S(2)}) collective-permute-start(f32[2,4,128,128]{3,2,1,0:T(8,128)} %get-tuple-element.67), channel_id=1, source_target_pairs={{0,8},{4,12},{8,0},{12,4},{1,9},{5,13},{9,1},{13,5},{2,10},{6,14},... | collective-permute-start | bytes 1572872 | tf_op jit(solution)/shard_map/ppermute | solution.py:444
  25.8 3.8 %copy-start.7 = (f32[2,4,128,128]{3,2,1,0:T(8,128)}, f32[2,4,128,128]{3,2,1,0:T(8,128)S(1)}, u32[]{:S(2)}) copy-start(f32[2,4,128,128]{3,2,1,0:T(8,128)S(1)} %collective-permute-done.refs_1_) | copy-start | bytes 1572868
  25.8 40.0 %collective-permute-start.6 = (f32[2,4,128,128]{3,2,1,0:T(8,128)}, f32[2,4,128,128]{3,2,1,0:T(8,128)}, u32[]{:S(2)}, u32[]{:S(2)}) collective-permute-start(f32[2,4,128,128]{3,2,1,0:T(8,128)} %get-tuple-element.68), channel_id=1, source_target_pairs={{0,12},{4,0},{8,4},{12,8},{1,13},{5,1},{9,5},{13,9},{2,14},{6,2},{... | collective-permute-start | bytes 1572872 | tf_op jit(solution)/shard_map/ppermute | solution.py:444
  27.5 12.3 %copy-start = (bf16[2,2,2,256,256]{4,3,2,1,0:T(8,128)(2,1)S(1)}, bf16[2,2,2,256,256]{4,3,2,1,0:T(8,128)(2,1)}, u32[]{:S(2)}) copy-start(bf16[2,2,2,256,256]{4,3,2,1,0:T(8,128)(2,1)} %constant.24.clone.refs_4_.table_ref.refs_6_) | copy-start | bytes 3145732
  38.2 0.9 copy-start.8
  39.0 0.8 copy-start.9
  43.3 22.5 %collective-permute-start.8 = (f32[2,1,256,128]{3,2,1,0:T(8,128)}, f32[2,1,256,128]{3,2,1,0:T(8,128)S(1)}, u32[]{:S(2)}, u32[]{:S(2)}) collective-permute-start(f32[2,1,256,128]{3,2,1,0:T(8,128)} %get-tuple-element.69), channel_id=1, source_target_pairs={{0,3},{1,0},{2,1},{3,2},{4,7},{5,4},{6,5},{7,6},{8,11},{9,8},{10,9... | collective-permute-start | bytes 786440 | tf_op jit(solution)/shard_map/ppermute | solution.py:444
  47.2 18.5 %collective-permute-start.7 = (f32[2,1,256,128]{3,2,1,0:T(8,128)}, f32[2,1,256,128]{3,2,1,0:T(8,128)S(1)}, u32[]{:S(2)}, u32[]{:S(2)}) collective-permute-start(f32[2,1,256,128]{3,2,1,0:T(8,128)} %get-tuple-element.60), channel_id=1, source_target_pairs={{0,1},{1,2},{2,3},{3,0},{4,5},{5,6},{6,7},{7,4},{8,9},{9,10},{10,1... | collective-permute-start | bytes 786440 | tf_op jit(solution)/shard_map/ppermute | solution.py:444
  47.2 11.0 %copy-start.1 = (bf16[2,2,2,256,256]{4,3,2,1,0:T(8,128)(2,1)S(1)}, bf16[2,2,2,256,256]{4,3,2,1,0:T(8,128)(2,1)}, u32[]{:S(2)}) copy-start(bf16[2,2,2,256,256]{4,3,2,1,0:T(8,128)(2,1)} %constant.25.clone.table_ref) | copy-start | bytes 3145732
  62.7 3.0 %copy-start.6 = (f32[2,4,128,128]{3,2,1,0:T(8,128)}, f32[2,4,128,128]{3,2,1,0:T(8,128)S(1)}, u32[]{:S(2)}) copy-start(f32[2,4,128,128]{3,2,1,0:T(8,128)S(1)} %collective-permute-done.4.refs_1_) | copy-start | bytes 1572868
  62.8 12.9 %collective-permute-start.3 = (f32[2,2,128,256]{3,2,1,0:T(8,128)}, f32[2,2,128,256]{3,2,1,0:T(8,128)S(1)}, u32[]{:S(2)}, u32[]{:S(2)}) collective-permute-start(f32[2,2,128,256]{3,2,1,0:T(8,128)} %get-tuple-element.64), channel_id=1, source_target_pairs={{0,8},{4,12},{8,0},{12,4},{1,9},{5,13},{9,1},{13,5},{2,10},{6,14},... | collective-permute-start | bytes 1572872 | tf_op jit(solution)/shard_map/ppermute | solution.py:444
  65.8 3.7 %copy-start.12 = (f32[2,2,128,256]{3,2,1,0:T(8,128)S(1)}, f32[2,2,128,256]{3,2,1,0:T(8,128)}, u32[]{:S(2)}) copy-start(f32[2,2,128,256]{3,2,1,0:T(8,128)} %get-tuple-element.77) | copy-start | bytes 1572868
  65.8 4.3 %copy-start.11 = (f32[2,2,128,256]{3,2,1,0:T(8,128)S(1)}, f32[2,2,128,256]{3,2,1,0:T(8,128)}, u32[]{:S(2)}) copy-start(f32[2,2,128,256]{3,2,1,0:T(8,128)} %get-tuple-element.78) | copy-start | bytes 1572868
  65.8 9.8 %copy-start.4 = (f32[2,2,128,256]{3,2,1,0:T(8,128)S(1)}, f32[2,2,128,256]{3,2,1,0:T(8,128)}, u32[]{:S(2)}) copy-start(f32[2,2,128,256]{3,2,1,0:T(8,128)} %get-tuple-element.63.p0) | copy-start | bytes 1572868
  69.4 12.6 %collective-permute-start.9 = (f32[2,2,256,128]{3,2,1,0:T(8,128)}, f32[2,2,256,128]{3,2,1,0:T(8,128)S(1)}, u32[]{:S(2)}, u32[]{:S(2)}) collective-permute-start(f32[2,2,256,128]{3,2,1,0:T(8,128)} %get-tuple-element.75), channel_id=1, source_target_pairs={{0,2},{1,3},{2,0},{3,1},{4,6},{5,7},{6,4},{7,5},{8,10},{9,11},{10,... | collective-permute-start | bytes 1572872 | tf_op jit(solution)/shard_map/ppermute | solution.py:444
  69.5 19.7 %collective-permute-start.10 = (f32[2,2,128,256]{3,2,1,0:T(8,128)S(1)}, f32[2,2,128,256]{3,2,1,0:T(8,128)S(1)}, u32[]{:S(2)}, u32[]{:S(2)}) collective-permute-start(f32[2,2,128,256]{3,2,1,0:T(8,128)S(1)} %copy-done.12), channel_id=1, source_target_pairs={{0,4},{4,8},{8,12},{12,0},{1,5},{5,9},{9,13},{13,1},{2,6},{6,10},{... | collective-permute-start | bytes 1572872 | tf_op jit(solution)/shard_map/ppermute | solution.py:444
  70.1 19.0 %collective-permute-start.11 = (f32[2,2,128,256]{3,2,1,0:T(8,128)S(1)}, f32[2,2,128,256]{3,2,1,0:T(8,128)S(1)}, u32[]{:S(2)}, u32[]{:S(2)}) collective-permute-start(f32[2,2,128,256]{3,2,1,0:T(8,128)S(1)} %copy-done.11), channel_id=1, source_target_pairs={{0,12},{4,0},{8,4},{12,8},{1,13},{5,1},{9,5},{13,9},{2,14},{6,2},{... | collective-permute-start | bytes 1572872 | tf_op jit(solution)/shard_map/ppermute | solution.py:444
  72.2 18.4 %collective-permute-start.12 = (f32[2,1,256,128]{3,2,1,0:T(8,128)}, f32[2,1,256,128]{3,2,1,0:T(8,128)S(1)}, u32[]{:S(2)}, u32[]{:S(2)}) collective-permute-start(f32[2,1,256,128]{3,2,1,0:T(8,128)} %get-tuple-element.80), channel_id=1, source_target_pairs={{0,1},{1,2},{2,3},{3,0},{4,5},{5,6},{6,7},{7,4},{8,9},{9,10},{10,1... | collective-permute-start | bytes 786440 | tf_op jit(solution)/shard_map/ppermute | solution.py:444
  75.6 15.0 %collective-permute-start.13 = (f32[2,1,256,128]{3,2,1,0:T(8,128)}, f32[2,1,256,128]{3,2,1,0:T(8,128)S(1)}, u32[]{:S(2)}, u32[]{:S(2)}) collective-permute-start(f32[2,1,256,128]{3,2,1,0:T(8,128)} %get-tuple-element.81), channel_id=1, source_target_pairs={{0,3},{1,0},{2,1},{3,2},{4,7},{5,4},{6,5},{7,6},{8,11},{9,8},{10,9... | collective-permute-start | bytes 786440 | tf_op jit(solution)/shard_map/ppermute | solution.py:444
  76.6 14.0 %copy-start.2 = (f32[2,2,256,128]{3,2,1,0:T(8,128)S(1)}, f32[2,2,256,128]{3,2,1,0:T(8,128)}, u32[]{:S(2)}) copy-start(f32[2,2,256,128]{3,2,1,0:T(8,128)} %get-tuple-element.83.b0) | copy-start | bytes 1572868
  92.6 36.9 %copy-start.3 = (bf16[2,2,256,512]{3,2,1,0:T(8,128)(2,1)S(1)}, bf16[2,2,256,512]{3,2,1,0:T(8,128)(2,1)}, u32[]{:S(2)}) copy-start(bf16[2,2,256,512]{3,2,1,0:T(8,128)(2,1)} %constant.23.clone.table_ref) | copy-start | bytes 3145732
  92.6 36.9 %copy-start.5 = (bf16[256,256]{1,0:T(8,128)(2,1)S(1)}, bf16[256,256]{1,0:T(8,128)(2,1)}, u32[]{:S(2)}) copy-start(bf16[256,256]{1,0:T(8,128)(2,1)} %constant.26.clone.ordering_ref) | copy-start | bytes 393220
